TPU v7x, 32 devices: a whole 2x2x4 slice. The times are simulated.
32 devices in a mesh: row: 8 (over y, x, core), col: 4 (over z).
Axes of the slice: x: 2, y: 2, z: 4, core: 2. Of those that a mesh axis runs over, the one named last changes fastest.
Arguments:
- source: bfloat16 [8192, 128], P(('row', 'col')), may hold values from -10 to 10
- target: bfloat16 [16384, 128], P(('col', 'row')), may hold values from -80 to 80
- target_potential: bfloat16 [16384], P(('col', 'row')), may hold values from -4 to 4
- prev_moment: float32 [128, 128], replicated, may hold values from -0.1 to 0.5
Outputs:
- moment: float32 [128, 128], replicated
- source_potential: float32 [8192], P('row')
- target_update: float32 [16384], P(('col', 'row'))
All inputs are finite; a program needn't handle non-finite values.
Results may differ from a plain program's by a relative error of at most 0.0059.
Values may be sent and summed in bfloat16 or wider, within the bound.
No kernel may reach another device: no remote copies, remote signals or barrier semaphores. Data moves between devices by JAX's collectives and lax.ppermute only.
A program may use at most 64 MiB of HBM per device.

v0:
```python
import math

import jax
import jax.numpy as jnp
from jax import lax
from jax.sharding import PartitionSpec as P

ITERS = 2


def project(rows_block, matrix):
    return jnp.dot(rows_block.astype(jnp.float32), matrix, precision=lax.Precision.HIGHEST).astype(
        jnp.bfloat16
    )


def tile_costs(projected, cols_block):
    return -4.0 * lax.dot_general(
        projected, cols_block, (((1,), (1,)), ((), ())), preferred_element_type=jnp.float32
    )


def row_totals(scores):
    top_score = lax.pmax(jnp.max(scores, axis=1), "col")
    mass_total = lax.psum(jnp.sum(jnp.exp(scores - top_score[:, None]), axis=1), "col")
    return top_score + jnp.log(mass_total)


def column_totals(scores):
    top_score = lax.pmax(jnp.max(scores, axis=0), "row")
    mass_total = lax.psum(jnp.sum(jnp.exp(scores - top_score[None, :]), axis=0), "row")
    return top_score + jnp.log(mass_total)


def per_device(source, target, target_potential, prev_moment):
    rows_block = lax.all_gather(source, "col", axis=0, tiled=True)
    cols_block, potential = (
        lax.all_gather(target, "row", axis=0, tiled=True),
        lax.all_gather(target_potential, "row", axis=0, tiled=True),
    )
    row_devices = lax.axis_size("row")
    rows_total = rows_block.shape[0] * row_devices
    cols_total = cols_block.shape[0] * lax.axis_size("col")
    share_width = cols_block.shape[0] // row_devices
    position = lax.axis_index("row")
    column = potential.astype(jnp.float32)
    scores = column[None, :] - tile_costs(project(rows_block, prev_moment), cols_block)
    spread = row_totals(scores)
    weights = (jnp.exp(scores - spread[:, None]) / rows_total).astype(jnp.bfloat16)
    carried = jnp.dot(weights, cols_block, preferred_element_type=jnp.float32)
    partial_moment = lax.dot_general(
        rows_block.astype(jnp.float32),
        carried,
        (((0,), (0,)), ((), ())),
        precision=lax.Precision.HIGHEST,
    )
    moment = lax.psum(partial_moment, ("row", "col"))
    cost_tile = tile_costs(project(rows_block, moment), cols_block)
    source_potential = jnp.zeros((rows_block.shape[0],), jnp.float32)
    own_share = jnp.zeros((share_width,), jnp.float32)
    for iteration in range(ITERS):
        source_potential = math.log(cols_total) - row_totals(column[None, :] - cost_tile)
        column_scores = source_potential[:, None] - cost_tile
        column = math.log(rows_total) - column_totals(column_scores)
        own_share = lax.dynamic_slice_in_dim(column, position * share_width, share_width)
    return (moment, source_potential, own_share)


def solution(mesh):
    placed = (P(("row", "col"), None), P(("col", "row"), None), P(("col", "row")), P())
    return jax.shard_map(
        per_device,
        mesh=mesh,
        in_specs=placed,
        out_specs=(P(), P("row"), P(("col", "row"))),
        check_vma=False,
    )
```

profile of v0, /device:TPU:0, one launch (start us, length us, event | category | flops | bytes accessed | tf_op | source)
XLA Modules:
  0.0 396.2 jit_solution(16969298707627419534)
XLA Ops:
  7.2 0.0 copy-start
  7.2 0.0 all-gather.3.cloned.1.call-start
  7.2 0.7 all-gather.3.cloned.1.call-update
  7.9 0.0 all-reduce.2.cloned.1.call-start
  8.0 0.7 reshape.16
  8.6 10.3 %all-gather = bf16[8,1,512]{2,1,0:T(2,128)(2,1)S(1)} all-gather(bf16[1,1,512]{2,1,0:T(2,128)(2,1)S(1)} %reshape.16), channel_id=1, replica_groups=mesh['row'=8,'col'=4] {'row'}, dimensions={0}, use_global_device_ids=true | all-gather | bytes 9216 | tf_op jit(solution)/shard_map/all_gather | solution.py:39
  19.0 14.3 %all_gather.10 = bf16[1024,128]{1,0:T(8,128)(2,1)S(1)} all-gather(bf16[256,128]{1,0:T(8,128)(2,1)} %param.4), channel_id=1, replica_groups=mesh['row'=8,'col'=4] {'col'}, dimensions={0}, use_global_device_ids=true | all-gather | bytes 327680 | tf_op jit(solution)/shard_map/all_gather | solution.py:36
  33.3 0.0 copy-done
  33.3 0.4 convolution_convert_fusion.1
  33.7 2.4 all-gather.3.cloned.1.call-done
  36.1 0.0 copy-start.1
  36.1 8.3 %fusion = (f32[1024]{0:T(1024)S(1)}, f32[1024,4096]{1,0:T(8,128)}) fusion(f32[4096]{0:T(1024)S(1)} %bitcast.14, bf16[1024,128]{1,0:T(8,128)(2,1)S(1)} %convolution_convert_fusion.1, bf16[4096,128]{1,0:T(8,128)(2,1)} %all-gather.3.cloned.1.call-done), kind=kOutput, calls=%fused_computation.11 | convolution fusion | flops 1086323712 | bytes 18108416 | tf_op jit(solution)/shard_map/dot_general | solution.py:18
  44.5 11.7 %pmax.35 = f32[1024]{0:T(1024)S(1)} all-reduce(f32[1024]{0:T(1024)S(1)} %get-tuple-element.9), channel_id=1, replica_groups=mesh['row'=8,'col'=4] {'col'}, use_global_device_ids=true, to_apply=%region_1.0 | all-reduce | flops 1024 | bytes 8192 | tf_op jit(solution)/shard_map/pmax | solution.py:24
  56.1 7.8 %exponential_reduce_fusion.4 = f32[1024]{0:T(1024)S(1)} fusion(f32[1024,4096]{1,0:T(8,128)} %get-tuple-element.10, f32[1024]{0:T(1024)S(1)} %pmax.35, f32[4096]{0:T(1024)S(1)} %bitcast.15), kind=kLoop, calls=%fused_computation.5 | loop fusion | flops 16776192 | bytes 16801792 | tf_op jit(solution)/shard_map/reduce_sum | solution.py:25
  63.9 8.4 %psum.42 = f32[1024]{0:T(1024)S(1)} all-reduce(f32[1024]{0:T(1024)S(1)} %exponential_reduce_fusion.4), channel_id=1, replica_groups=mesh['row'=8,'col'=4] {'col'}, use_global_device_ids=true, to_apply=%region_3.0 | all-reduce | flops 1024 | bytes 8192 | tf_op jit(solution)/shard_map/psum | solution.py:25
  72.3 0.0 copy-done.1
  72.3 7.8 %fusion.1 = f32[1024,128]{1,0:T(8,128)S(1)} fusion(bf16[4096,128]{1,0:T(8,128)(2,1)S(1)} %copy-done.1, f32[1024,4096]{1,0:T(8,128)} %get-tuple-element.10, f32[1024]{0:T(1024)S(1)} %log_add_fusion, f32[4096]{0:T(1024)S(1)} %bitcast.16), kind=kOutput, calls=%fused_computation.12 | convolution fusion | flops 1094713344 | bytes 18370560 | tf_op jit(solution)/shard_map/dot_general | solution.py:50
  80.1 1.2 convolution_bitcast_fusion
  81.3 0.0 all-reduce.2.cloned.1.call-update
  81.4 116.4 %all-reduce.2.cloned.1.call-done = f32[128,128]{0,1:T(8,128)} async-done(((f32[128,128]{0,1:T(8,128)}), f32[128,128]{0,1:T(8,128)}) %all-reduce.2.cloned.1.call-update) | async-done | bytes 65552 | tf_op jit(solution)/shard_map/psum | solution.py:57
  197.8 1.2 convolution_convert_fusion
  199.0 7.0 %subtract_reduce_fusion.3 = (f32[1024]{0:T(1024)S(1)}, f32[1024,4096]{1,0:T(8,128)}) fusion(f32[4096]{0:T(1024)S(1)} %bitcast.17, bf16[128,1024]{1,0:T(8,128)(2,1)S(1)} %convolution_convert_fusion, bf16[4096,128]{1,0:T(8,128)(2,1)S(1)} %copy-done.1), kind=kOutput, calls=%fused_computation.10 | convolution fusion | flops 1086323712 | bytes 18108416 | tf_op jit(solution)/shard_map/dot_general | solution.py:18
  206.0 11.1 %pmax.36 = f32[1024]{0:T(1024)S(1)} all-reduce(f32[1024]{0:T(1024)S(1)} %get-tuple-element.11), channel_id=1, replica_groups=mesh['row'=8,'col'=4] {'col'}, use_global_device_ids=true, to_apply=%region_6.0 | all-reduce | flops 1024 | bytes 8192 | tf_op jit(solution)/shard_map/pmax | solution.py:24
  217.1 7.8 %exponential_reduce_fusion.3 = f32[1024]{0:T(1024)S(1)} fusion(f32[1024,4096]{1,0:T(8,128)} %get-tuple-element.12, f32[1024]{0:T(1024)S(1)} %pmax.36, f32[4096]{0:T(1024)S(1)} %bitcast.18), kind=kLoop, calls=%fused_computation.3 | loop fusion | flops 16776192 | bytes 16801792 | tf_op jit(solution)/shard_map/reduce_sum | solution.py:25
  224.9 8.4 %psum.44 = f32[1024]{0:T(1024)S(1)} all-reduce(f32[1024]{0:T(1024)S(1)} %exponential_reduce_fusion.3), channel_id=1, replica_groups=mesh['row'=8,'col'=4] {'col'}, use_global_device_ids=true, to_apply=%region_8.0 | all-reduce | flops 1024 | bytes 8192 | tf_op jit(solution)/shard_map/psum | solution.py:25
  233.3 7.7 %subtract_reduce_fusion.2 = f32[4096]{0:T(1024)S(1)} fusion(f32[1024,4096]{1,0:T(8,128)} %get-tuple-element.12, f32[1024]{0:T(1024)S(1)} %add_subtract_fusion.2), kind=kLoop, calls=%fused_computation.9 | loop fusion | flops 12578816 | bytes 16797696 | tf_op jit(solution)/shard_map/reduce_max | solution.py:30
  241.1 22.5 %pmax.37 = f32[4096]{0:T(1024)S(1)} all-reduce(f32[4096]{0:T(1024)S(1)} %subtract_reduce_fusion.2), channel_id=1, replica_groups=mesh['row'=8,'col'=4] {'row'}, use_global_device_ids=true, to_apply=%region_10.0 | all-reduce | flops 4096 | bytes 32768 | tf_op jit(solution)/shard_map/pmax | solution.py:30
  263.5 7.7 %exponential_reduce_fusion.2 = f32[4096]{0:T(1024)S(1)} fusion(f32[1024,4096]{1,0:T(8,128)} %get-tuple-element.12, f32[4096]{0:T(1024)S(1)} %pmax.37, f32[1024]{0:T(1024)S(1)} %add_subtract_fusion.2), kind=kLoop, calls=%fused_computation.2 | loop fusion | flops 16773120 | bytes 16814080 | tf_op jit(solution)/shard_map/reduce_sum | solution.py:31
  271.3 22.3 %psum.45 = f32[4096]{0:T(1024)S(1)} all-reduce(f32[4096]{0:T(1024)S(1)} %exponential_reduce_fusion.2), channel_id=1, replica_groups=mesh['row'=8,'col'=4] {'row'}, use_global_device_ids=true, to_apply=%region_12.0 | all-reduce | flops 4096 | bytes 32768 | tf_op jit(solution)/shard_map/psum | solution.py:31
  293.6 7.5 %subtract_reduce_fusion.1 = f32[1024]{0:T(1024)S(1)} fusion(f32[1024,4096]{1,0:T(8,128)} %get-tuple-element.12, f32[4096]{0:T(1024)S(1)} %add_subtract_fusion), kind=kLoop, calls=%fused_computation.8 | loop fusion | flops 12581888 | bytes 16797696 | tf_op jit(solution)/shard_map/reduce_max | solution.py:24
  301.1 10.4 %pmax.38 = f32[1024]{0:T(1024)S(1)} all-reduce(f32[1024]{0:T(1024)S(1)} %subtract_reduce_fusion.1), channel_id=1, replica_groups=mesh['row'=8,'col'=4] {'col'}, use_global_device_ids=true, to_apply=%region_14.0 | all-reduce | flops 1024 | bytes 8192 | tf_op jit(solution)/shard_map/pmax | solution.py:24
  311.5 7.8 %exponential_reduce_fusion.1 = f32[1024]{0:T(1024)S(1)} fusion(f32[1024,4096]{1,0:T(8,128)} %get-tuple-element.12, f32[1024]{0:T(1024)S(1)} %pmax.38, f32[4096]{0:T(1024)S(1)} %add_subtract_fusion), kind=kLoop, calls=%fused_computation.1 | loop fusion | flops 16776192 | bytes 16801792 | tf_op jit(solution)/shard_map/reduce_sum | solution.py:25
  319.3 8.4 %psum.46 = f32[1024]{0:T(1024)S(1)} all-reduce(f32[1024]{0:T(1024)S(1)} %exponential_reduce_fusion.1), channel_id=1, replica_groups=mesh['row'=8,'col'=4] {'col'}, use_global_device_ids=true, to_apply=%region_16.0 | all-reduce | flops 1024 | bytes 8192 | tf_op jit(solution)/shard_map/psum | solution.py:25
  327.7 0.0 copy-start.3
  327.7 0.0 copy-start.2
  327.7 7.8 %subtract_reduce_fusion = f32[4096]{0:T(1024)S(1)} fusion(f32[1024,4096]{1,0:T(8,128)} %get-tuple-element.12, f32[1024]{0:T(1024)S(1)} %add_subtract_fusion.1), kind=kLoop, calls=%fused_computation.7 | loop fusion | flops 12578816 | bytes 16797696 | tf_op jit(solution)/shard_map/reduce_max | solution.py:30
  335.5 22.3 %pmax.39 = f32[4096]{0:T(1024)S(1)} all-reduce(f32[4096]{0:T(1024)S(1)} %subtract_reduce_fusion), channel_id=1, replica_groups=mesh['row'=8,'col'=4] {'row'}, use_global_device_ids=true, to_apply=%region_18.0 | all-reduce | flops 4096 | bytes 32768 | tf_op jit(solution)/shard_map/pmax | solution.py:30
  357.8 7.7 %exponential_reduce_fusion = f32[4096]{0:T(1024)S(1)} fusion(f32[1024,4096]{1,0:T(8,128)} %get-tuple-element.12, f32[4096]{0:T(1024)S(1)} %pmax.39, f32[1024]{0:T(1024)S(1)} %add_subtract_fusion.1), kind=kLoop, calls=%fused_computation | loop fusion | flops 16773120 | bytes 16814080 | tf_op jit(solution)/shard_map/reduce_sum | solution.py:31
  365.6 0.0 copy-done.3
  365.6 22.3 %psum.47 = f32[4096]{0:T(1024)S(1)} all-reduce(f32[4096]{0:T(1024)S(1)} %exponential_reduce_fusion), channel_id=1, replica_groups=mesh['row'=8,'col'=4] {'row'}, use_global_device_ids=true, to_apply=%region_20.0 | all-reduce | flops 4096 | bytes 32768 | tf_op jit(solution)/shard_map/psum | solution.py:31
  388.0 0.7 fusion.2
  388.6 0.0 copy-done.2
  388.6 0.7 copy.8
  (5 shorter events, 0.1 us)
Async XLA Ops:
  7.2 26.1 %copy-start = (f32[128,128]{1,0:T(8,128)S(1)}, f32[128,128]{1,0:T(8,128)}, u32[]{:S(2)}) copy-start(f32[128,128]{1,0:T(8,128)} %param.7) | copy-start | bytes 196612
  7.2 28.9 %all-gather.3.cloned.1.call-start = ((), (), s32[]{:S(2)}) async-start(), calls=%async_computation | async-start | bytes 1179648 | tf_op jit(solution)/shard_map/all_gather | solution.py:38
  7.9 189.8 %all-reduce.2.cloned.1.call-start = ((), (), s32[]{:S(2)}) async-start(), calls=%async_computation.1 | async-start | bytes 131072 | tf_op jit(solution)/shard_map/psum | solution.py:57
  36.1 36.2 %copy-start.1 = (bf16[4096,128]{1,0:T(8,128)(2,1)S(1)}, bf16[4096,128]{1,0:T(8,128)(2,1)}, u32[]{:S(2)}) copy-start(bf16[4096,128]{1,0:T(8,128)(2,1)} %all-gather.3.cloned.1.call-done) | copy-start | bytes 3145732
  327.7 37.9 %copy-start.3 = (f32[1024]{0:T(1024)}, f32[1024]{0:T(1024)S(1)}, u32[]{:S(2)}) copy-start(f32[1024]{0:T(1024)S(1)} %add_subtract_fusion.1) | copy-start | bytes 12292
  327.7 60.9 %copy-start.2 = (f32[128,128]{0,1:T(8,128)S(1)}, f32[128,128]{0,1:T(8,128)}, u32[]{:S(2)}) copy-start(f32[128,128]{0,1:T(8,128)} %all-reduce.2.cloned.1.call-done) | copy-start | bytes 196612
Sparse Core Ops, SparseCore 0:
  9.9 26.1 all-gather.2
  81.5 116.2 all-reduce.1
where the time goes:
time: 397 us; the launch traced here: 396 us
  blocking collectives  172 us (43%)
  waiting for transfers between devices  120 us (30%)
  other arithmetic  62.7 us (16%)
  matrix products  25.9 us (7%)
  between operations  14.1 us (4%)
    psum x1, waiting for transfers between devices, per_device(): moment = lax.psum(partial_moment, ('row', 'col'))  116 us
    pmax x2, blocking collectives, column_totals(): top_score = lax.pmax(jnp.max(scores, axis=0), 'row')  44.8 us
    psum x2, blocking collectives, column_totals(): lax.psum(jnp.sum(jnp.exp(scores - top_score[None, :]), axis=0), 'row')  44.7 us
    pmax x3, blocking collectives, row_totals(): top_score = lax.pmax(jnp.max(scores, axis=1), 'col')  33.2 us
    psum x3, blocking collectives, row_totals(): lax.psum(jnp.sum(jnp.exp(scores - top_score[:, None]), axis=1), 'col')  25.1 us
    reduce_sum x3, other arithmetic, row_totals(): jnp.sum(jnp.exp(scores - top_score[:, None]), axis=1)  23.5 us
    reduce_sum x2, other arithmetic, column_totals(): jnp.sum(jnp.exp(scores - top_score[None, :]), axis=0)  15.5 us
    reduce_max x2, other arithmetic, column_totals(): top_score = lax.pmax(jnp.max(scores, axis=0), 'row')  15.5 us
  transfers between devices with their start and end apart: 2, of which 2 were waited for; matrix products, arithmetic and copies ran while one was open for 0% of the time, Pallas kernels for 0%

commit v1 on v0

v1 whole, which is shorter than its diff:
```python
import functools
import math

import jax
import jax.numpy as jnp
from jax import lax
from jax.experimental import pallas as pl
from jax.experimental.pallas import tpu as pltpu
from jax.sharding import PartitionSpec as P

ITERS = 2
LANES = 128
NT_DIMS = (((1,), (1,)), ((), ()))
TN_DIMS = (((0,), (0,)), ((), ()))


def split3(x):
    high = x.astype(jnp.bfloat16)
    rest = x - high.astype(jnp.float32)
    mid = rest.astype(jnp.bfloat16)
    low = (rest - mid.astype(jnp.float32)).astype(jnp.bfloat16)
    return high, mid, low


def project4(rows, matrix):
    total = None
    for part in reversed(split3(matrix)):
        term = jnp.dot(rows, part, preferred_element_type=jnp.float32)
        total = term if total is None else total + term
    return (total.astype(jnp.bfloat16).astype(jnp.float32) * 4.0).astype(jnp.bfloat16)


def lane_fold(op, x):
    parts = [x[:, i : i + LANES] for i in range(0, x.shape[1], LANES)]
    return functools.reduce(op, parts)


def as_lanes(column):
    return jnp.broadcast_to(column, (LANES, LANES)).T[0:1, :]


def as_rows(lanes):
    return jnp.broadcast_to(lanes, (LANES, LANES)).T


def log_sum(parts):
    top = functools.reduce(jnp.maximum, parts)
    return top + jnp.log(sum(jnp.exp(p - top) for p in parts))


def potential_rows(block_ref, width):
    groups = width // LANES
    tail = block_ref[width:, :].astype(jnp.float32)
    return jnp.concatenate([tail[i : i + 1, :] for i in range(groups)], axis=1)


def row_pass(a, t_refs, column, scores, width, carry_targets):
    top = None
    for g, t_ref in enumerate(t_refs):
        s = column[g] + lax.dot_general(a, t_ref[:width, :], NT_DIMS, preferred_element_type=jnp.float32)
        scores[:, g * width : (g + 1) * width] = s
        m = lane_fold(jnp.maximum, s)
        top = m if top is None else jnp.maximum(top, m)
    top = jnp.max(top, axis=1, keepdims=True)
    mass, carried = None, None
    for g, t_ref in enumerate(t_refs):
        e = jnp.exp(scores[:, g * width : (g + 1) * width] - top)
        m = lane_fold(jnp.add, e)
        mass = m if mass is None else mass + m
        if carry_targets:
            c = jnp.dot(e.astype(jnp.bfloat16), t_ref[:width, :], preferred_element_type=jnp.float32)
            carried = c if carried is None else carried + c
    mass = jnp.sum(mass, axis=1, keepdims=True)
    return top + jnp.log(mass), mass, carried


def couple_kernel(ns, nt, width, *refs):
    s_refs, t_refs, moment_ref = refs[:ns], refs[ns : ns + nt], refs[ns + nt]
    lse_ref, carried_ref, a_ref, scores = refs[ns + nt + 1 :]
    c = lax.axis_index("col")
    piece = s_refs[0].shape[0]
    per = piece // LANES
    for k in range(ns):
        a_ref[k * piece : (k + 1) * piece, :] = project4(s_refs[k][...], moment_ref[...])
    column = [potential_rows(t, width) for t in t_refs]

    @pl.loop(0, ns * per)
    def _(i):
        rows = pl.ds(pl.multiple_of(i * LANES, LANES), LANES)
        lse, mass, carried = row_pass(a_ref[rows, :], t_refs, column, scores, width, True)
        carried_ref[rows, :] = carried / mass
        lse_ref[pl.ds((c ^ (i // per)) * per + i % per, 1), :] = as_lanes(lse)


def moment_kernel(ns, rows_total, pieces, *refs):
    s_refs, l_refs, carried_ref = refs[:ns], refs[ns : 2 * ns], refs[2 * ns]
    out_refs, total_ref = refs[2 * ns + 1 : -1], refs[-1]
    c = lax.axis_index("col")
    piece = s_refs[0].shape[0]
    per = piece // LANES
    scale = jnp.exp(l_refs[0][...] - log_sum([l[...] for l in l_refs])) * (1.0 / rows_total)
    weight, = (scale,)
    total_ref[0 : weight.shape[0], :] = weight
    total = None
    for k in range(ns):
        for j in range(per):
            w = as_rows(total_ref[pl.ds((c ^ k) * per + j, 1), :])
            at = (k * per + j) * LANES
            x = carried_ref[at : at + LANES, :] * w
            s = s_refs[k][j * LANES : (j + 1) * LANES, :]
            for part in reversed(split3(x)):
                term = lax.dot_general(s, part, TN_DIMS, preferred_element_type=jnp.float32)
                total = term if total is None else total + term
    if pieces == 1:
        out_refs[0][...] = total
        return
    r = lax.axis_index("row")
    total_ref[...] = total
    size = total.shape[0] // pieces
    for k in range(pieces):
        out_refs[k][...] = total_ref[pl.ds(pl.multiple_of((r ^ k) * size, size), size), :]


def add_kernel(*refs):
    refs[-1][...] = functools.reduce(jnp.add, [r[...] for r in refs[:-1]])


def first_rows_kernel(ns, nt, width, pieces, *refs):
    s_refs, t_refs, m_refs = refs[:ns], refs[ns : ns + nt], refs[ns + nt : ns + nt + pieces]
    moment_ref, a_ref, lse_ref, scores = refs[ns + nt + pieces :]
    c = lax.axis_index("col")
    piece = s_refs[0].shape[0]
    per = piece // LANES
    if pieces == 1:
        moment_ref[...] = m_refs[0][...]
    else:
        r = lax.axis_index("row")
        size = m_refs[0].shape[0]
        for k in range(pieces):
            moment_ref[pl.ds(pl.multiple_of((r ^ k) * size, size), size), :] = m_refs[k][...]
    for k in range(ns):
        a_ref[k * piece : (k + 1) * piece, :] = project4(s_refs[k][...], moment_ref[...])
    column = [potential_rows(t, width) for t in t_refs]

    @pl.loop(0, ns * per)
    def _(i):
        rows = pl.ds(pl.multiple_of(i * LANES, LANES), LANES)
        lse, _, _ = row_pass(a_ref[rows, :], t_refs, column, scores, width, False)
        lse_ref[pl.ds((c ^ (i // per)) * per + i % per, 1), :] = as_lanes(lse)


def rows_kernel(ns, nt, width, rows_total, *refs):
    a_ref, t_refs, l_refs = refs[0], refs[1 : 1 + nt], refs[1 + nt : 1 + 2 * nt]
    lse_ref, column_ref, scores = refs[1 + 2 * nt :]
    c, r = lax.axis_index("col"), lax.axis_index("row")
    per = a_ref.shape[0] // ns // LANES
    column_ref[...] = math.log(rows_total) - log_sum([l[...] for l in l_refs])
    column = [column_ref[pl.ds(r ^ k, 1), :] for k in range(nt)]

    @pl.loop(0, ns * per)
    def _(i):
        rows = pl.ds(pl.multiple_of(i * LANES, LANES), LANES)
        lse, _, _ = row_pass(a_ref[rows, :], t_refs, column, scores, width, False)
        lse_ref[pl.ds((c ^ (i // per)) * per + i % per, 1), :] = as_lanes(lse)


def columns_kernel(ns, nt, width, cols_total, last, *refs):
    a_ref, t_refs, l_refs = refs[0], refs[1 : 1 + nt], refs[1 + nt : 1 + nt + ns]
    out_refs, (sp_ref, spread_rows, scores) = refs[1 + nt + ns : -3], refs[-3:]
    c, r = lax.axis_index("col"), lax.axis_index("row")
    rows = a_ref.shape[0]
    per = rows // ns // LANES
    sp_ref[...] = math.log(cols_total) - log_sum([l[...] for l in l_refs])
    for k in range(ns):
        for j in range(per):
            at = (k * per + j) * LANES
            spread_rows[at : at + LANES, :] = as_rows(sp_ref[pl.ds((c ^ k) * per + j, 1), :])
    step = 256
    for g, t_ref in enumerate(t_refs):
        top = None
        for at in range(0, rows, step):
            s = lax.dot_general(
                a_ref[at : at + step, :], t_ref[:width, :], NT_DIMS, preferred_element_type=jnp.float32
            )
            s = s + jnp.concatenate([spread_rows[at : at + step, :]] * (width // LANES), axis=1)
            scores[g % 2, at : at + step, :] = s
            m = jnp.max(s.reshape(step // 8, 8, width), axis=0)
            top = m if top is None else jnp.maximum(top, m)
        top = jnp.max(top, axis=0, keepdims=True)
        mass = None
        for at in range(0, rows, step):
            e = jnp.exp(scores[g % 2, at : at + step, :] - top)
            m = jnp.sum(e.reshape(step // 8, 8, width), axis=0)
            mass = m if mass is None else mass + m
        lse = top + jnp.log(jnp.sum(mass, axis=0, keepdims=True))
        if last:
            out_refs[g][...] = lse
        else:
            out_refs[0][pl.ds(r ^ g, 1), :] = lse


def update_kernel(rows_total, *refs):
    refs[-1][...] = math.log(rows_total) - log_sum([r[...] for r in refs[:-1]])


def call(kernel, out, args, scratch=(), flops=0, exps=0):
    vmem = pl.BlockSpec(memory_space=pltpu.VMEM)
    bytes_accessed = sum(x.size * x.dtype.itemsize for x in list(args) + list(out))
    return pl.pallas_call(
        kernel,
        out_shape=list(out),
        in_specs=[vmem] * len(args),
        out_specs=[vmem] * len(out),
        scratch_shapes=list(scratch),
        compiler_params=pltpu.CompilerParams(vmem_limit_bytes=24 << 20),
        cost_estimate=pl.CostEstimate(flops=flops, bytes_accessed=bytes_accessed, transcendentals=exps),
    )(*args)


def swap(x, axis, k):
    return lax.ppermute(x, axis, [(i, i ^ k) for i in range(lax.axis_size(axis))])


def exchange(x, axis):
    return [x] + [swap(x, axis, k) for k in range(1, lax.axis_size(axis))]


def exchange_pairs(x, axis):
    n = lax.axis_size(axis)
    got = {0: x, 1: swap(x, axis, 1)}
    for k in range(2, n, 2):
        got[k] = swap(x, axis, k)
    for k in range(2, n, 2):
        got[k + 1] = swap(got[k], axis, 1)
    return [got[k] for k in range(n)]


def deal(parts, axis):
    return [parts[0]] + [swap(parts[k], axis, k) for k in range(1, len(parts))]


def per_device(source, target, target_potential, prev_moment):
    f32 = jnp.float32
    ns, nt = lax.axis_size("col"), lax.axis_size("row")
    piece, width = source.shape[0], target.shape[0]
    depth = source.shape[1]
    rows, cols = piece * ns, width * nt
    rows_total, cols_total = rows * nt, cols * ns
    groups = width // LANES
    tail = jnp.pad(target_potential.reshape(groups, LANES), ((0, 16 - groups), (0, 0)))
    t_blocks = exchange_pairs(jnp.concatenate([target, tail], axis=0), "row")
    s_pieces = exchange(source, "col")
    tile = jax.ShapeDtypeStruct((rows // LANES, LANES), f32)
    flops, exps = 2 * rows * cols * depth, rows * cols
    row_scores = pltpu.VMEM((LANES, cols), f32)

    lse, carried = call(
        functools.partial(couple_kernel, ns, nt, width),
        [tile, jax.ShapeDtypeStruct((rows, depth), f32)],
        s_pieces + t_blocks + [prev_moment],
        [pltpu.VMEM((rows, depth), jnp.bfloat16), row_scores],
        2 * flops,
        exps,
    )
    pieces = nt if depth % (8 * nt) == 0 else 1
    parts = call(
        functools.partial(moment_kernel, ns, rows_total, pieces),
        [jax.ShapeDtypeStruct((depth // pieces, depth), f32)] * pieces,
        s_pieces + exchange(lse, "col") + [carried],
        [pltpu.VMEM((depth, depth), f32)],
        6 * rows * depth * depth,
    )
    if pieces == 1:
        m_parts = [lax.psum(parts[0], ("row", "col"))]
    else:
        summed, = call(add_kernel, [jax.ShapeDtypeStruct(parts[0].shape, f32)], deal(parts, "row"))
        summed, = call(add_kernel, [jax.ShapeDtypeStruct(parts[0].shape, f32)], exchange(summed, "col"))
        m_parts = exchange(summed, "row")
    moment, a, lse = call(
        functools.partial(first_rows_kernel, ns, nt, width, pieces),
        [jax.ShapeDtypeStruct((depth, depth), f32), jax.ShapeDtypeStruct((rows, depth), jnp.bfloat16), tile],
        s_pieces + t_blocks + m_parts,
        [row_scores],
        flops,
        exps,
    )
    for iteration in range(ITERS):
        last = iteration == ITERS - 1
        if iteration > 0:
            lse, = call(
                functools.partial(rows_kernel, ns, nt, width, rows_total),
                [tile],
                [a] + t_blocks + exchange(column_lse, "row"),
                [pltpu.VMEM((nt, width), f32), row_scores],
                flops,
                exps,
            )
        one = jax.ShapeDtypeStruct((1, width), f32)
        out = [one] * nt if last else [jax.ShapeDtypeStruct((nt, width), f32)]
        *outs, source_potential = call(
            functools.partial(columns_kernel, ns, nt, width, cols_total, last),
            out + [tile],
            [a] + t_blocks + exchange(lse, "col"),
            [pltpu.VMEM((rows, LANES), f32), pltpu.VMEM((2, rows, width), f32)],
            flops,
            exps,
        )
        column_lse = outs[0]
    update, = call(functools.partial(update_kernel, rows_total), [one], deal(outs, "row"))
    return moment, source_potential.reshape(rows), update.reshape(width)


def solution(mesh):
    placed = (P(("row", "col"), None), P(("col", "row"), None), P(("col", "row")), P())
    return jax.shard_map(
        per_device,
        mesh=mesh,
        in_specs=placed,
        out_specs=(P(), P("row"), P(("col", "row"))),
        check_vma=False,
    )
```

time: 397 us -> 122 us (0.31)
  blocking collectives: 172 us -> 0 us
  waiting for transfers between devices: 120 us -> 27.8 us
  other arithmetic: 62.7 us -> 0.95 us
  starting transfers between devices: 0.08 us -> 55.7 us
  Pallas kernels: 0 us -> 36.1 us
  matrix products: 25.9 us -> 0 us
  between operations: 14.1 us -> 0.75 us
    psum x1 -> x0, waiting for transfers between devices: 116 us -> none  [per_device(): moment = lax.psum(partial_moment, ('row', 'col'))]
    pmax x5 -> x0, blocking collectives: 78 us -> none  [the longest x2 44.8 us: column_totals(): top_score = lax.pmax(jnp.max(scores, axis=0), 'row')]
    psum x5 -> x0, blocking collectives: 69.8 us -> none  [the longest x2 44.7 us: column_totals(): lax.psum(jnp.sum(jnp.exp(scores - top_score[None, :]), axis=0), 'row')]
    ppermute x0 -> x50, starting transfers between devices: none -> 55.7 us  [swap(): lax.ppermute(x, axis, [(i, i ^ k) for i in range(lax.axis_size(axis))])]
    reduce_sum x5 -> x0, other arithmetic: 39 us -> none  [the longest x3 23.5 us: row_totals(): jnp.sum(jnp.exp(scores - top_score[:, None]), axis=1)]
    pallas_call x0 -> x9, Pallas kernels: none -> 36.1 us  [call(): pl.pallas_call(kernel, out_shape=list(out), in_specs=[vmem] * len(args),...]
    ppermute x0 -> x50, waiting for transfers between devices: none -> 27.8 us  [swap(): lax.ppermute(x, axis, [(i, i ^ k) for i in range(lax.axis_size(axis))])]
    dot_general x6 -> x0, matrix products: 25.9 us -> none  [the longest x2 15.3 us: tile_costs(): lax.dot_general(projected, cols_block, (((1,), (1,)), ((), ())), preferre...]
  transfers between devices with their start and end apart: 2 -> 50, of which waited for: 2 -> 25; matrix products, arithmetic and copies ran while one was open for 0% -> 0% of each run, Pallas kernels for 0% -> 0%
where the time goes in v1:
time: 122 us
  starting transfers between devices  55.7 us (46%)
  Pallas kernels  36.1 us (30%)
  waiting for transfers between devices  27.8 us (23%)
    ppermute x50, starting transfers between devices, swap(): lax.ppermute(x, axis, [(i, i ^ k) for i in range(lax.axis_size(axis))])  55.7 us
    pallas_call x9, Pallas kernels, call(): pl.pallas_call(kernel, out_shape=list(out), in_specs=[vmem] * len(args),...  36.1 us
    ppermute x50, waiting for transfers between devices, swap(): lax.ppermute(x, axis, [(i, i ^ k) for i in range(lax.axis_size(axis))])  27.8 us
  transfers between devices with their start and end apart: 50, of which 25 were waited for; matrix products, arithmetic and copies ran while one was open for 0% of the time, Pallas kernels for 0%

profile of v1, /device:TPU:0, one launch (start us, length us, event | category | flops | bytes accessed | tf_op | source)
XLA Modules:
  0.0 122.0 jit_solution(9161284344676743501)
XLA Ops:
  0.6 0.7 copy-done.2
  1.3 0.9 fusion.1.refs_4_.refs_1_
  2.3 4.0 %collective-permute-start.8 = (bf16[528,128]{1,0:T(8,128)(2,1)S(1)}, bf16[528,128]{1,0:T(8,128)(2,1)S(1)}, u32[]{:S(2)}, u32[]{:S(2)}) collective-permute-start(bf16[528,128]{1,0:T(8,128)(2,1)S(1)} %fusion.1.refs_4_.refs_1_), channel_id=1, source_target_pairs={{0,24},{4,28},{8,16},{12,20},{16,8},{20,12},{24,0},{28,4},{1,25},{... | collective-permute-start | bytes 405512 | tf_op jit(solution)/shard_map/ppermute | solution.py:221
  6.2 0.5 collective-permute-start.6
  6.9 4.0 %collective-permute-start.2 = (bf16[256,128]{1,0:T(8,128)(2,1)S(1)}, bf16[256,128]{1,0:T(8,128)(2,1)S(1)}, u32[]{:S(2)}, u32[]{:S(2)}) collective-permute-start(bf16[256,128]{1,0:T(8,128)(2,1)S(1)} %copy-done), channel_id=1, source_target_pairs={{0,3},{1,2},{2,1},{3,0},{4,7},{5,6},{6,5},{7,4},{8,11},{9,10},{10,... | collective-permute-start | bytes 196616 | tf_op jit(solution)/shard_map/ppermute | solution.py:221
  10.9 0.5 collective-permute-start.9
  11.4 1.3 %collective-permute-done.6.refs_8_.refs_5_ = bf16[528,128]{1,0:T(8,128)(2,1)S(1)} collective-permute-done((bf16[528,128]{1,0:T(8,128)(2,1)S(1)}, bf16[528,128]{1,0:T(8,128)(2,1)S(1)}, u32[]{:S(2)}, u32[]{:S(2)}) %collective-permute-start.6) | collective-permute-done | bytes 135200 | tf_op jit(solution)/shard_map/ppermute | solution.py:221
  13.2 2.8 %collective-permute-start.1 = (bf16[256,128]{1,0:T(8,128)(2,1)S(1)}, bf16[256,128]{1,0:T(8,128)(2,1)S(1)}, u32[]{:S(2)}, u32[]{:S(2)}) collective-permute-start(bf16[256,128]{1,0:T(8,128)(2,1)S(1)} %copy-done), channel_id=1, source_target_pairs={{0,2},{1,3},{2,0},{3,1},{4,6},{5,7},{6,4},{7,5},{8,10},{9,11},{10,... | collective-permute-start | bytes 196616 | tf_op jit(solution)/shard_map/ppermute | solution.py:221
  16.0 3.8 %collective-permute-done.1.refs_2_ = bf16[256,128]{1,0:T(8,128)(2,1)S(1)} collective-permute-done((bf16[256,128]{1,0:T(8,128)(2,1)S(1)}, bf16[256,128]{1,0:T(8,128)(2,1)S(1)}, u32[]{:S(2)}, u32[]{:S(2)}) %collective-permute-start.1) | collective-permute-done | bytes 65568 | tf_op jit(solution)/shard_map/ppermute | solution.py:221
  19.8 0.7 collective-permute-start
  20.5 3.6 %collective-permute-done.refs_1_ = bf16[256,128]{1,0:T(8,128)(2,1)S(1)} collective-permute-done((bf16[256,128]{1,0:T(8,128)(2,1)S(1)}, bf16[256,128]{1,0:T(8,128)(2,1)S(1)}, u32[]{:S(2)}, u32[]{:S(2)}) %collective-permute-start) | collective-permute-done | bytes 65568 | tf_op jit(solution)/shard_map/ppermute | solution.py:221
  24.1 10.1 %shard_map.67 = (f32[8,128]{1,0:T(8,128)S(1)}, f32[1024,128]{1,0:T(8,128)S(1)}) custom-call(bf16[256,128]{1,0:T(8,128)(2,1)S(1)} %copy-done, bf16[256,128]{1,0:T(8,128)(2,1)S(1)} %collective-permute-done.refs_1_, bf16[256,128]{1,0:T(8,128)(2,1)S(1)} %collective-permute-done.1.refs_2_, bf16[256,128]{1,0:T(8,128)(2,1)S(1)} %collective-permute-done.2.refs_3_, ...), custom_call_target="tpu_custom_call" | custom-call | flops 2147483648 | bytes 1937408 | tf_op jit(solution)/shard_map/pallas_call | solution.py:209
  34.2 3.5 %collective-permute-start.12 = (f32[8,128]{1,0:T(8,128)S(1)}, f32[8,128]{1,0:T(8,128)S(1)}, u32[]{:S(2)}, u32[]{:S(2)}) collective-permute-start(f32[8,128]{1,0:T(8,128)S(1)} %get-tuple-element.26.refs_4_), channel_id=1, source_target_pairs={{0,3},{1,2},{2,1},{3,0},{4,7},{5,6},{6,5},{7,4},{8,11},{9,10},{10,... | collective-permute-start | bytes 12296 | tf_op jit(solution)/shard_map/ppermute | solution.py:221
  37.8 0.9 collective-permute-start.10
  38.7 1.0 collective-permute-done.12.refs_7_
  39.7 2.6 %collective-permute-done.11.refs_6_ = f32[8,128]{1,0:T(8,128)S(1)} collective-permute-done((f32[8,128]{1,0:T(8,128)S(1)}, f32[8,128]{1,0:T(8,128)S(1)}, u32[]{:S(2)}, u32[]{:S(2)}) %collective-permute-start.11) | collective-permute-done | bytes 4128 | tf_op jit(solution)/shard_map/ppermute | solution.py:221
  42.3 0.5 shard_map.68
  42.9 1.6 %collective-permute-start.14 = (f32[16,128]{1,0:T(8,128)S(1)}, f32[16,128]{1,0:T(8,128)S(1)}, u32[]{:S(2)}, u32[]{:S(2)}) collective-permute-start(f32[16,128]{1,0:T(8,128)S(1)} %get-tuple-element.30), channel_id=1, source_target_pairs={{0,8},{4,12},{8,0},{12,4},{16,24},{20,28},{24,16},{28,20},{1,9},{5... | collective-permute-start | bytes 24584 | tf_op jit(solution)/shard_map/ppermute | solution.py:221
  44.7 1.6 %collective-permute-start.16 = (f32[16,128]{1,0:T(8,128)S(1)}, f32[16,128]{1,0:T(8,128)S(1)}, u32[]{:S(2)}, u32[]{:S(2)}) collective-permute-start(f32[16,128]{1,0:T(8,128)S(1)} %get-tuple-element.32), channel_id=1, source_target_pairs={{0,16},{4,20},{8,24},{12,28},{16,0},{20,4},{24,8},{28,12},{1,17},{... | collective-permute-start | bytes 24584 | tf_op jit(solution)/shard_map/ppermute | solution.py:221
  46.4 1.8 %collective-permute-start.18 = (f32[16,128]{1,0:T(8,128)S(1)}, f32[16,128]{1,0:T(8,128)S(1)}, u32[]{:S(2)}, u32[]{:S(2)}) collective-permute-start(f32[16,128]{1,0:T(8,128)S(1)} %get-tuple-element.34), channel_id=1, source_target_pairs={{0,24},{4,28},{8,16},{12,20},{16,8},{20,12},{24,0},{28,4},{1,25},{... | collective-permute-start | bytes 24584 | tf_op jit(solution)/shard_map/ppermute | solution.py:221
  48.2 0.9 collective-permute-start.19
  49.4 1.6 %collective-permute-done.18.refs_6_ = f32[16,128]{1,0:T(8,128)S(1)} collective-permute-done((f32[16,128]{1,0:T(8,128)S(1)}, f32[16,128]{1,0:T(8,128)S(1)}, u32[]{:S(2)}, u32[]{:S(2)}) %collective-permute-start.18) | collective-permute-done | bytes 8224 | tf_op jit(solution)/shard_map/ppermute | solution.py:221
  51.0 1.2 collective-permute-done.19.refs_7_
  52.2 1.5 %collective-permute-start.22 = (f32[16,128]{1,0:T(8,128)S(1)}, f32[16,128]{1,0:T(8,128)S(1)}, u32[]{:S(2)}, u32[]{:S(2)}) collective-permute-start(f32[16,128]{1,0:T(8,128)S(1)} %shard_map.69.refs_0_), channel_id=1, source_target_pairs={{0,3},{1,2},{2,1},{3,0},{4,7},{5,6},{6,5},{7,4},{8,11},{9,10},{10,... | collective-permute-start | bytes 24584 | tf_op jit(solution)/shard_map/ppermute | solution.py:221
  53.7 0.6 collective-permute-start.21
  54.4 2.3 %collective-permute-start.20 = (f32[16,128]{1,0:T(8,128)S(1)}, f32[16,128]{1,0:T(8,128)S(1)}, u32[]{:S(2)}, u32[]{:S(2)}) collective-permute-start(f32[16,128]{1,0:T(8,128)S(1)} %shard_map.69.refs_0_), channel_id=1, source_target_pairs={{0,1},{1,0},{2,3},{3,2},{4,5},{5,4},{6,7},{7,6},{8,9},{9,8},{10,11... | collective-permute-start | bytes 24584 | tf_op jit(solution)/shard_map/ppermute | solution.py:221
  56.7 1.1 collective-permute-done.22.refs_3_
  57.8 0.5 collective-permute-done.21.refs_2_
  58.4 1.6 %collective-permute-start.28 = (f32[16,128]{1,0:T(8,128)S(1)}, f32[16,128]{1,0:T(8,128)S(1)}, u32[]{:S(2)}, u32[]{:S(2)}) collective-permute-start(f32[16,128]{1,0:T(8,128)S(1)} %shard_map.70.refs_12_), channel_id=1, source_target_pairs={{0,24},{4,28},{8,16},{12,20},{16,8},{20,12},{24,0},{28,4},{1,25},{... | collective-permute-start | bytes 24584 | tf_op jit(solution)/shard_map/ppermute | solution.py:221
  60.0 2.0 %collective-permute-start.27 = (f32[16,128]{1,0:T(8,128)S(1)}, f32[16,128]{1,0:T(8,128)S(1)}, u32[]{:S(2)}, u32[]{:S(2)}) collective-permute-start(f32[16,128]{1,0:T(8,128)S(1)} %shard_map.70.refs_12_), channel_id=1, source_target_pairs={{0,20},{4,16},{8,28},{12,24},{16,4},{20,0},{24,12},{28,8},{1,21},{... | collective-permute-start | bytes 24584 | tf_op jit(solution)/shard_map/ppermute | solution.py:221
  62.0 0.8 collective-permute-start.26
  62.8 1.3 %collective-permute-start.24 = (f32[16,128]{1,0:T(8,128)S(1)}, f32[16,128]{1,0:T(8,128)S(1)}, u32[]{:S(2)}, u32[]{:S(2)}) collective-permute-start(f32[16,128]{1,0:T(8,128)S(1)} %shard_map.70.refs_12_), channel_id=1, source_target_pairs={{0,8},{4,12},{8,0},{12,4},{16,24},{20,28},{24,16},{28,20},{1,9},{5... | collective-permute-start | bytes 24584 | tf_op jit(solution)/shard_map/ppermute | solution.py:221
  64.1 0.6 collective-permute-start.23
  64.7 1.0 collective-permute-done.26.refs_16_
  65.9 0.6 collective-permute-done.24.refs_14_
  66.5 7.8 %shard_map.71 = (f32[128,128]{1,0:T(8,128)}, bf16[1024,128]{1,0:T(8,128)(2,1)S(1)}, f32[8,128]{1,0:T(8,128)S(1)}) custom-call(bf16[256,128]{1,0:T(8,128)(2,1)S(1)} %copy-done, bf16[256,128]{1,0:T(8,128)(2,1)S(1)} %collective-permute-done.refs_1_, bf16[256,128]{1,0:T(8,128)(2,1)S(1)} %collective-permute-done.1.refs_2_, ...), custom_call_target="tpu_custom_call" | custom-call | flops 1073741824 | bytes 1740800 | tf_op jit(solution)/shard_map/pallas_call | solution.py:209
  74.3 2.5 %collective-permute-start.32 = (f32[8,128]{1,0:T(8,128)S(1)}, f32[8,128]{1,0:T(8,128)S(1)}, u32[]{:S(2)}, u32[]{:S(2)}) collective-permute-start(f32[8,128]{1,0:T(8,128)S(1)} %get-tuple-element.38.refs_9_), channel_id=1, source_target_pairs={{0,3},{1,2},{2,1},{3,0},{4,7},{5,6},{6,5},{7,4},{8,11},{9,10},{10,... | collective-permute-start | bytes 12296 | tf_op jit(solution)/shard_map/ppermute | solution.py:221
  76.8 0.9 collective-permute-start.31
  77.7 1.0 collective-permute-start.30
  78.7 1.0 collective-permute-done.32.refs_12_
  79.7 1.6 %collective-permute-done.31.refs_11_ = f32[8,128]{1,0:T(8,128)S(1)} collective-permute-done((f32[8,128]{1,0:T(8,128)S(1)}, f32[8,128]{1,0:T(8,128)S(1)}, u32[]{:S(2)}, u32[]{:S(2)}) %collective-permute-start.31) | collective-permute-done | bytes 4128 | tf_op jit(solution)/shard_map/ppermute | solution.py:221
  81.4 4.7 %shard_map.72 = (f32[8,512]{1,0:T(8,128)S(1)}, f32[8,128]{1,0:T(8,128)}) custom-call(bf16[1024,128]{1,0:T(8,128)(2,1)S(1)} %get-tuple-element.37.refs_0_, bf16[528,128]{1,0:T(8,128)(2,1)S(1)} %fusion.1.refs_4_.refs_1_, bf16[528,128]{1,0:T(8,128)(2,1)S(1)} %collective-permute-done.3.refs_5_.refs_2_, ...), custom_call_target="tpu_custom_call" | custom-call | flops 1073741824 | bytes 1380352 | tf_op jit(solution)/shard_map/pallas_call | solution.py:209
  86.1 1.3 %collective-permute-start.38 = (f32[8,512]{1,0:T(8,128)S(1)}, f32[8,512]{1,0:T(8,128)S(1)}, u32[]{:S(2)}, u32[]{:S(2)}) collective-permute-start(f32[8,512]{1,0:T(8,128)S(1)} %get-tuple-element.39.refs_9_), channel_id=1, source_target_pairs={{0,24},{4,28},{8,16},{12,20},{16,8},{20,12},{24,0},{28,4},{1,25},{... | collective-permute-start | bytes 49160 | tf_op jit(solution)/shard_map/ppermute | solution.py:221
  87.4 2.3 %collective-permute-start.37 = (f32[8,512]{1,0:T(8,128)S(1)}, f32[8,512]{1,0:T(8,128)S(1)}, u32[]{:S(2)}, u32[]{:S(2)}) collective-permute-start(f32[8,512]{1,0:T(8,128)S(1)} %get-tuple-element.39.refs_9_), channel_id=1, source_target_pairs={{0,20},{4,16},{8,28},{12,24},{16,4},{20,0},{24,12},{28,8},{1,21},{... | collective-permute-start | bytes 49160 | tf_op jit(solution)/shard_map/ppermute | solution.py:221
  89.6 0.8 collective-permute-start.36
  90.4 1.3 %collective-permute-start.34 = (f32[8,512]{1,0:T(8,128)S(1)}, f32[8,512]{1,0:T(8,128)S(1)}, u32[]{:S(2)}, u32[]{:S(2)}) collective-permute-start(f32[8,512]{1,0:T(8,128)S(1)} %get-tuple-element.39.refs_9_), channel_id=1, source_target_pairs={{0,8},{4,12},{8,0},{12,4},{16,24},{20,28},{24,16},{28,20},{1,9},{5... | collective-permute-start | bytes 49160 | tf_op jit(solution)/shard_map/ppermute | solution.py:221
  91.7 0.6 collective-permute-start.33
  92.3 1.1 collective-permute-done.36.refs_13_
  93.6 0.6 collective-permute-done.34.refs_11_
  94.2 7.7 %shard_map.73.refs_9_ = f32[8,128]{1,0:T(8,128)S(1)} custom-call(bf16[1024,128]{1,0:T(8,128)(2,1)S(1)} %get-tuple-element.37.refs_0_, bf16[528,128]{1,0:T(8,128)(2,1)S(1)} %fusion.1.refs_4_.refs_1_, bf16[528,128]{1,0:T(8,128)(2,1)S(1)} %collective-permute-done.3.refs_5_.refs_2_, bf16[528,128]{1,0:T(8,128)(2,1)S(1)} %collective-permute-done.4.refs_6_.refs_3_, ...), custom_call_target="tpu_custom_call" | custom-call | flops 1073741824 | bytes 1478656 | tf_op jit(solution)/shard_map/pallas_call | solution.py:209
  101.9 1.5 %collective-permute-start.42 = (f32[8,128]{1,0:T(8,128)S(1)}, f32[8,128]{1,0:T(8,128)S(1)}, u32[]{:S(2)}, u32[]{:S(2)}) collective-permute-start(f32[8,128]{1,0:T(8,128)S(1)} %shard_map.73.refs_9_), channel_id=1, source_target_pairs={{0,3},{1,2},{2,1},{3,0},{4,7},{5,6},{6,5},{7,4},{8,11},{9,10},{10,... | collective-permute-start | bytes 12296 | tf_op jit(solution)/shard_map/ppermute | solution.py:221
  103.4 1.0 collective-permute-start.41
  104.4 2.0 %collective-permute-start.40 = (f32[8,128]{1,0:T(8,128)S(1)}, f32[8,128]{1,0:T(8,128)S(1)}, u32[]{:S(2)}, u32[]{:S(2)}) collective-permute-start(f32[8,128]{1,0:T(8,128)S(1)} %shard_map.73.refs_9_), channel_id=1, source_target_pairs={{0,1},{1,0},{2,3},{3,2},{4,5},{5,4},{6,7},{7,6},{8,9},{9,8},{10,11... | collective-permute-start | bytes 12296 | tf_op jit(solution)/shard_map/ppermute | solution.py:221
  106.3 1.0 collective-permute-done.42.refs_12_
  107.4 0.5 collective-permute-done.41.refs_11_
  108.0 4.7 %shard_map.74 = (f32[1,512]{1,0:T(1,128)S(1)}, f32[1,512]{1,0:T(1,128)S(1)}, f32[1,512]{1,0:T(1,128)S(1)}, f32[1,512]{1,0:T(1,128)S(1)}, f32[1,512]{1,0:T(1,128)...) custom-call(bf16[1024,128]{1,0:T(8,128)(2,1)S(1)} %get-tuple-element.37.refs_0_, ...), custom_call_target="tpu_custom_call" | custom-call | flops 1073741824 | bytes 1380352 | tf_op jit(solution)/shard_map/pallas_call | solution.py:209
  112.6 1.3 %collective-permute-start.44 = (f32[1,512]{1,0:T(1,128)S(1)}, f32[1,512]{1,0:T(1,128)S(1)}, u32[]{:S(2)}, u32[]{:S(2)}) collective-permute-start(f32[1,512]{1,0:T(1,128)S(1)} %get-tuple-element.43), channel_id=1, source_target_pairs={{0,8},{4,12},{8,0},{12,4},{16,24},{20,28},{24,16},{28,20},{1,9},{5... | collective-permute-start | bytes 6152 | tf_op jit(solution)/shard_map/ppermute | solution.py:221
  113.9 0.5 collective-permute-start.45
  114.5 1.2 %collective-permute-start.46 = (f32[1,512]{1,0:T(1,128)S(1)}, f32[1,512]{1,0:T(1,128)S(1)}, u32[]{:S(2)}, u32[]{:S(2)}) collective-permute-start(f32[1,512]{1,0:T(1,128)S(1)} %get-tuple-element.45), channel_id=1, source_target_pairs={{0,16},{4,20},{8,24},{12,28},{16,0},{20,4},{24,8},{28,12},{1,17},{... | collective-permute-start | bytes 6152 | tf_op jit(solution)/shard_map/ppermute | solution.py:221
  116.1 1.3 %collective-permute-start.48 = (f32[1,512]{1,0:T(1,128)S(1)}, f32[1,512]{1,0:T(1,128)S(1)}, u32[]{:S(2)}, u32[]{:S(2)}) collective-permute-start(f32[1,512]{1,0:T(1,128)S(1)} %get-tuple-element.47), channel_id=1, source_target_pairs={{0,24},{4,28},{8,16},{12,20},{16,8},{20,12},{24,0},{28,4},{1,25},{... | collective-permute-start | bytes 6152 | tf_op jit(solution)/shard_map/ppermute | solution.py:221
  117.4 1.5 %collective-permute-start.49 = (f32[1,512]{1,0:T(1,128)S(1)}, f32[1,512]{1,0:T(1,128)S(1)}, u32[]{:S(2)}, u32[]{:S(2)}) collective-permute-start(f32[1,512]{1,0:T(1,128)S(1)} %get-tuple-element.48), channel_id=1, source_target_pairs={{0,28},{4,24},{8,20},{12,16},{16,12},{20,8},{24,4},{28,0},{1,29},{... | collective-permute-start | bytes 6152 | tf_op jit(solution)/shard_map/ppermute | solution.py:221
  118.9 1.7 %collective-permute-done.48.refs_6_ = f32[1,512]{1,0:T(1,128)S(1)} collective-permute-done((f32[1,512]{1,0:T(1,128)S(1)}, f32[1,512]{1,0:T(1,128)S(1)}, u32[]{:S(2)}, u32[]{:S(2)}) %collective-permute-start.48) | collective-permute-done | bytes 2080 | tf_op jit(solution)/shard_map/ppermute | solution.py:221
  120.6 0.7 collective-permute-done.49.refs_7_
  121.3 0.6 shard_map.75
  (52 shorter events, 2.5 us)
Async XLA Ops:
  0.6 0.7 copy-start.2
  1.3 5.6 %copy-start = (bf16[256,128]{1,0:T(8,128)(2,1)S(1)}, bf16[256,128]{1,0:T(8,128)(2,1)}, u32[]{:S(2)}) copy-start(bf16[256,128]{1,0:T(8,128)(2,1)} %refs_0_.5) | copy-start | bytes 196612
  1.3 22.8 %copy-start.1 = (f32[128,128]{1,0:T(8,128)S(1)}, f32[128,128]{1,0:T(8,128)}, u32[]{:S(2)}) copy-start(f32[128,128]{1,0:T(8,128)} %refs_12_.1) | copy-start | bytes 196612
  2.3 8.6 %collective-permute-start.8 = (bf16[528,128]{1,0:T(8,128)(2,1)S(1)}, bf16[528,128]{1,0:T(8,128)(2,1)S(1)}, u32[]{:S(2)}, u32[]{:S(2)}) collective-permute-start(bf16[528,128]{1,0:T(8,128)(2,1)S(1)} %fusion.1.refs_4_.refs_1_), channel_id=1, source_target_pairs={{0,24},{4,28},{8,16},{12,20},{16,8},{20,12},{24,0},{28,4},{1,25},{... | collective-permute-start | bytes 405512 | tf_op jit(solution)/shard_map/ppermute | solution.py:221
  6.2 6.5 %collective-permute-start.6 = (bf16[528,128]{1,0:T(8,128)(2,1)S(1)}, bf16[528,128]{1,0:T(8,128)(2,1)S(1)}, u32[]{:S(2)}, u32[]{:S(2)}) collective-permute-start(bf16[528,128]{1,0:T(8,128)(2,1)S(1)} %fusion.1.refs_4_.refs_1_), channel_id=1, source_target_pairs={{0,16},{4,20},{8,24},{12,28},{16,0},{20,4},{24,8},{28,12},{1,17},{... | collective-permute-start | bytes 405512 | tf_op jit(solution)/shard_map/ppermute | solution.py:221
  6.7 6.2 %collective-permute-start.4 = (bf16[528,128]{1,0:T(8,128)(2,1)S(1)}, bf16[528,128]{1,0:T(8,128)(2,1)S(1)}, u32[]{:S(2)}, u32[]{:S(2)}) collective-permute-start(bf16[528,128]{1,0:T(8,128)(2,1)S(1)} %fusion.1.refs_4_.refs_1_), channel_id=1, source_target_pairs={{0,8},{4,12},{8,0},{12,4},{16,24},{20,28},{24,16},{28,20},{1,9},{5... | collective-permute-start | bytes 405512 | tf_op jit(solution)/shard_map/ppermute | solution.py:221
  6.9 6.4 %collective-permute-start.2 = (bf16[256,128]{1,0:T(8,128)(2,1)S(1)}, bf16[256,128]{1,0:T(8,128)(2,1)S(1)}, u32[]{:S(2)}, u32[]{:S(2)}) collective-permute-start(bf16[256,128]{1,0:T(8,128)(2,1)S(1)} %copy-done), channel_id=1, source_target_pairs={{0,3},{1,2},{2,1},{3,0},{4,7},{5,6},{6,5},{7,4},{8,11},{9,10},{10,... | collective-permute-start | bytes 196616 | tf_op jit(solution)/shard_map/ppermute | solution.py:221
  10.9 13.2 %collective-permute-start.3 = (bf16[528,128]{1,0:T(8,128)(2,1)S(1)}, bf16[528,128]{1,0:T(8,128)(2,1)S(1)}, u32[]{:S(2)}, u32[]{:S(2)}) collective-permute-start(bf16[528,128]{1,0:T(8,128)(2,1)S(1)} %fusion.1.refs_4_.refs_1_), channel_id=1, source_target_pairs={{0,4},{4,0},{8,12},{12,8},{16,20},{20,16},{24,28},{28,24},{1,5},{5... | collective-permute-start | bytes 405512 | tf_op jit(solution)/shard_map/ppermute | solution.py:221
  10.9 13.2 %collective-permute-start.9 = (bf16[528,128]{1,0:T(8,128)(2,1)S(1)}, bf16[528,128]{1,0:T(8,128)(2,1)S(1)}, u32[]{:S(2)}, u32[]{:S(2)}) collective-permute-start(bf16[528,128]{1,0:T(8,128)(2,1)S(1)} %collective-permute-done.8.refs_10_.refs_7_), channel_id=1, source_target_pairs={{0,4},{4,0},{8,12},{12,8},{16,20},{20,16},{24,28},{28,24},{1,5},{5... | collective-permute-start | bytes 405512 | tf_op jit(solution)/shard_map/ppermute | solution.py:221
  12.7 11.4 %collective-permute-start.7 = (bf16[528,128]{1,0:T(8,128)(2,1)S(1)}, bf16[528,128]{1,0:T(8,128)(2,1)S(1)}, u32[]{:S(2)}, u32[]{:S(2)}) collective-permute-start(bf16[528,128]{1,0:T(8,128)(2,1)S(1)} %collective-permute-done.6.refs_8_.refs_5_), channel_id=1, source_target_pairs={{0,4},{4,0},{8,12},{12,8},{16,20},{20,16},{24,28},{28,24},{1,5},{5... | collective-permute-start | bytes 405512 | tf_op jit(solution)/shard_map/ppermute | solution.py:221
  13.0 11.1 %collective-permute-start.5 = (bf16[528,128]{1,0:T(8,128)(2,1)S(1)}, bf16[528,128]{1,0:T(8,128)(2,1)S(1)}, u32[]{:S(2)}, u32[]{:S(2)}) collective-permute-start(bf16[528,128]{1,0:T(8,128)(2,1)S(1)} %collective-permute-done.4.refs_6_.refs_3_), channel_id=1, source_target_pairs={{0,4},{4,0},{8,12},{12,8},{16,20},{20,16},{24,28},{28,24},{1,5},{5... | collective-permute-start | bytes 405512 | tf_op jit(solution)/shard_map/ppermute | solution.py:221
  13.2 6.6 %collective-permute-start.1 = (bf16[256,128]{1,0:T(8,128)(2,1)S(1)}, bf16[256,128]{1,0:T(8,128)(2,1)S(1)}, u32[]{:S(2)}, u32[]{:S(2)}) collective-permute-start(bf16[256,128]{1,0:T(8,128)(2,1)S(1)} %copy-done), channel_id=1, source_target_pairs={{0,2},{1,3},{2,0},{3,1},{4,6},{5,7},{6,4},{7,5},{8,10},{9,11},{10,... | collective-permute-start | bytes 196616 | tf_op jit(solution)/shard_map/ppermute | solution.py:221
  19.8 4.3 %collective-permute-start = (bf16[256,128]{1,0:T(8,128)(2,1)S(1)}, bf16[256,128]{1,0:T(8,128)(2,1)S(1)}, u32[]{:S(2)}, u32[]{:S(2)}) collective-permute-start(bf16[256,128]{1,0:T(8,128)(2,1)S(1)} %copy-done), channel_id=1, source_target_pairs={{0,1},{1,0},{2,3},{3,2},{4,5},{5,4},{6,7},{7,6},{8,9},{9,8},{10,11... | collective-permute-start | bytes 196616 | tf_op jit(solution)/shard_map/ppermute | solution.py:221
  34.2 5.5 %collective-permute-start.12 = (f32[8,128]{1,0:T(8,128)S(1)}, f32[8,128]{1,0:T(8,128)S(1)}, u32[]{:S(2)}, u32[]{:S(2)}) collective-permute-start(f32[8,128]{1,0:T(8,128)S(1)} %get-tuple-element.26.refs_4_), channel_id=1, source_target_pairs={{0,3},{1,2},{2,1},{3,0},{4,7},{5,6},{6,5},{7,4},{8,11},{9,10},{10,... | collective-permute-start | bytes 12296 | tf_op jit(solution)/shard_map/ppermute | solution.py:221
  37.8 4.5 %collective-permute-start.11 = (f32[8,128]{1,0:T(8,128)S(1)}, f32[8,128]{1,0:T(8,128)S(1)}, u32[]{:S(2)}, u32[]{:S(2)}) collective-permute-start(f32[8,128]{1,0:T(8,128)S(1)} %get-tuple-element.26.refs_4_), channel_id=1, source_target_pairs={{0,2},{1,3},{2,0},{3,1},{4,6},{5,7},{6,4},{7,5},{8,10},{9,11},{10,... | collective-permute-start | bytes 12296 | tf_op jit(solution)/shard_map/ppermute | solution.py:221
  37.8 4.5 %collective-permute-start.10 = (f32[8,128]{1,0:T(8,128)S(1)}, f32[8,128]{1,0:T(8,128)S(1)}, u32[]{:S(2)}, u32[]{:S(2)}) collective-permute-start(f32[8,128]{1,0:T(8,128)S(1)} %get-tuple-element.26.refs_4_), channel_id=1, source_target_pairs={{0,1},{1,0},{2,3},{3,2},{4,5},{5,4},{6,7},{7,6},{8,9},{9,8},{10,11... | collective-permute-start | bytes 12296 | tf_op jit(solution)/shard_map/ppermute | solution.py:221
  42.8 3.6 %collective-permute-start.13 = (f32[16,128]{1,0:T(8,128)S(1)}, f32[16,128]{1,0:T(8,128)S(1)}, u32[]{:S(2)}, u32[]{:S(2)}) collective-permute-start(f32[16,128]{1,0:T(8,128)S(1)} %get-tuple-element.29), channel_id=1, source_target_pairs={{0,4},{4,0},{8,12},{12,8},{16,20},{20,16},{24,28},{28,24},{1,5},{5... | collective-permute-start | bytes 24584 | tf_op jit(solution)/shard_map/ppermute | solution.py:221
  42.9 5.3 %collective-permute-start.14 = (f32[16,128]{1,0:T(8,128)S(1)}, f32[16,128]{1,0:T(8,128)S(1)}, u32[]{:S(2)}, u32[]{:S(2)}) collective-permute-start(f32[16,128]{1,0:T(8,128)S(1)} %get-tuple-element.30), channel_id=1, source_target_pairs={{0,8},{4,12},{8,0},{12,4},{16,24},{20,28},{24,16},{28,20},{1,9},{5... | collective-permute-start | bytes 24584 | tf_op jit(solution)/shard_map/ppermute | solution.py:221
  44.5 4.6 %collective-permute-start.15 = (f32[16,128]{1,0:T(8,128)S(1)}, f32[16,128]{1,0:T(8,128)S(1)}, u32[]{:S(2)}, u32[]{:S(2)}) collective-permute-start(f32[16,128]{1,0:T(8,128)S(1)} %get-tuple-element.31), channel_id=1, source_target_pairs={{0,12},{4,8},{8,4},{12,0},{16,28},{20,24},{24,20},{28,16},{1,13},{... | collective-permute-start | bytes 24584 | tf_op jit(solution)/shard_map/ppermute | solution.py:221
  44.7 4.4 %collective-permute-start.16 = (f32[16,128]{1,0:T(8,128)S(1)}, f32[16,128]{1,0:T(8,128)S(1)}, u32[]{:S(2)}, u32[]{:S(2)}) collective-permute-start(f32[16,128]{1,0:T(8,128)S(1)} %get-tuple-element.32), channel_id=1, source_target_pairs={{0,16},{4,20},{8,24},{12,28},{16,0},{20,4},{24,8},{28,12},{1,17},{... | collective-permute-start | bytes 24584 | tf_op jit(solution)/shard_map/ppermute | solution.py:221
  46.3 3.1 %collective-permute-start.17 = (f32[16,128]{1,0:T(8,128)S(1)}, f32[16,128]{1,0:T(8,128)S(1)}, u32[]{:S(2)}, u32[]{:S(2)}) collective-permute-start(f32[16,128]{1,0:T(8,128)S(1)} %get-tuple-element.33), channel_id=1, source_target_pairs={{0,20},{4,16},{8,28},{12,24},{16,4},{20,0},{24,12},{28,8},{1,21},{... | collective-permute-start | bytes 24584 | tf_op jit(solution)/shard_map/ppermute | solution.py:221
  46.4 4.6 %collective-permute-start.18 = (f32[16,128]{1,0:T(8,128)S(1)}, f32[16,128]{1,0:T(8,128)S(1)}, u32[]{:S(2)}, u32[]{:S(2)}) collective-permute-start(f32[16,128]{1,0:T(8,128)S(1)} %get-tuple-element.34), channel_id=1, source_target_pairs={{0,24},{4,28},{8,16},{12,20},{16,8},{20,12},{24,0},{28,4},{1,25},{... | collective-permute-start | bytes 24584 | tf_op jit(solution)/shard_map/ppermute | solution.py:221
  48.2 4.0 %collective-permute-start.19 = (f32[16,128]{1,0:T(8,128)S(1)}, f32[16,128]{1,0:T(8,128)S(1)}, u32[]{:S(2)}, u32[]{:S(2)}) collective-permute-start(f32[16,128]{1,0:T(8,128)S(1)} %get-tuple-element.35), channel_id=1, source_target_pairs={{0,28},{4,24},{8,20},{12,16},{16,12},{20,8},{24,4},{28,0},{1,29},{... | collective-permute-start | bytes 24584 | tf_op jit(solution)/shard_map/ppermute | solution.py:221
  52.2 5.6 %collective-permute-start.22 = (f32[16,128]{1,0:T(8,128)S(1)}, f32[16,128]{1,0:T(8,128)S(1)}, u32[]{:S(2)}, u32[]{:S(2)}) collective-permute-start(f32[16,128]{1,0:T(8,128)S(1)} %shard_map.69.refs_0_), channel_id=1, source_target_pairs={{0,3},{1,2},{2,1},{3,0},{4,7},{5,6},{6,5},{7,4},{8,11},{9,10},{10,... | collective-permute-start | bytes 24584 | tf_op jit(solution)/shard_map/ppermute | solution.py:221
  53.7 4.6 %collective-permute-start.21 = (f32[16,128]{1,0:T(8,128)S(1)}, f32[16,128]{1,0:T(8,128)S(1)}, u32[]{:S(2)}, u32[]{:S(2)}) collective-permute-start(f32[16,128]{1,0:T(8,128)S(1)} %shard_map.69.refs_0_), channel_id=1, source_target_pairs={{0,2},{1,3},{2,0},{3,1},{4,6},{5,7},{6,4},{7,5},{8,10},{9,11},{10,... | collective-permute-start | bytes 24584 | tf_op jit(solution)/shard_map/ppermute | solution.py:221
  54.4 4.0 %collective-permute-start.20 = (f32[16,128]{1,0:T(8,128)S(1)}, f32[16,128]{1,0:T(8,128)S(1)}, u32[]{:S(2)}, u32[]{:S(2)}) collective-permute-start(f32[16,128]{1,0:T(8,128)S(1)} %shard_map.69.refs_0_), channel_id=1, source_target_pairs={{0,1},{1,0},{2,3},{3,2},{4,5},{5,4},{6,7},{7,6},{8,9},{9,8},{10,11... | collective-permute-start | bytes 24584 | tf_op jit(solution)/shard_map/ppermute | solution.py:221
  58.4 4.4 %collective-permute-start.29 = (f32[16,128]{1,0:T(8,128)S(1)}, f32[16,128]{1,0:T(8,128)S(1)}, u32[]{:S(2)}, u32[]{:S(2)}) collective-permute-start(f32[16,128]{1,0:T(8,128)S(1)} %shard_map.70.refs_12_), channel_id=1, source_target_pairs={{0,28},{4,24},{8,20},{12,16},{16,12},{20,8},{24,4},{28,0},{1,29},{... | collective-permute-start | bytes 24584 | tf_op jit(solution)/shard_map/ppermute | solution.py:221
  58.4 5.7 %collective-permute-start.28 = (f32[16,128]{1,0:T(8,128)S(1)}, f32[16,128]{1,0:T(8,128)S(1)}, u32[]{:S(2)}, u32[]{:S(2)}) collective-permute-start(f32[16,128]{1,0:T(8,128)S(1)} %shard_map.70.refs_12_), channel_id=1, source_target_pairs={{0,24},{4,28},{8,16},{12,20},{16,8},{20,12},{24,0},{28,4},{1,25},{... | collective-permute-start | bytes 24584 | tf_op jit(solution)/shard_map/ppermute | solution.py:221
  60.0 4.7 %collective-permute-start.27 = (f32[16,128]{1,0:T(8,128)S(1)}, f32[16,128]{1,0:T(8,128)S(1)}, u32[]{:S(2)}, u32[]{:S(2)}) collective-permute-start(f32[16,128]{1,0:T(8,128)S(1)} %shard_map.70.refs_12_), channel_id=1, source_target_pairs={{0,20},{4,16},{8,28},{12,24},{16,4},{20,0},{24,12},{28,8},{1,21},{... | collective-permute-start | bytes 24584 | tf_op jit(solution)/shard_map/ppermute | solution.py:221
  62.0 3.7 %collective-permute-start.26 = (f32[16,128]{1,0:T(8,128)S(1)}, f32[16,128]{1,0:T(8,128)S(1)}, u32[]{:S(2)}, u32[]{:S(2)}) collective-permute-start(f32[16,128]{1,0:T(8,128)S(1)} %shard_map.70.refs_12_), channel_id=1, source_target_pairs={{0,16},{4,20},{8,24},{12,28},{16,0},{20,4},{24,8},{28,12},{1,17},{... | collective-permute-start | bytes 24584 | tf_op jit(solution)/shard_map/ppermute | solution.py:221
  62.8 3.1 %collective-permute-start.25 = (f32[16,128]{1,0:T(8,128)S(1)}, f32[16,128]{1,0:T(8,128)S(1)}, u32[]{:S(2)}, u32[]{:S(2)}) collective-permute-start(f32[16,128]{1,0:T(8,128)S(1)} %shard_map.70.refs_12_), channel_id=1, source_target_pairs={{0,12},{4,8},{8,4},{12,0},{16,28},{20,24},{24,20},{28,16},{1,13},{... | collective-permute-start | bytes 24584 | tf_op jit(solution)/shard_map/ppermute | solution.py:221
  62.8 3.7 %collective-permute-start.24 = (f32[16,128]{1,0:T(8,128)S(1)}, f32[16,128]{1,0:T(8,128)S(1)}, u32[]{:S(2)}, u32[]{:S(2)}) collective-permute-start(f32[16,128]{1,0:T(8,128)S(1)} %shard_map.70.refs_12_), channel_id=1, source_target_pairs={{0,8},{4,12},{8,0},{12,4},{16,24},{20,28},{24,16},{28,20},{1,9},{5... | collective-permute-start | bytes 24584 | tf_op jit(solution)/shard_map/ppermute | solution.py:221
  64.1 2.4 %collective-permute-start.23 = (f32[16,128]{1,0:T(8,128)S(1)}, f32[16,128]{1,0:T(8,128)S(1)}, u32[]{:S(2)}, u32[]{:S(2)}) collective-permute-start(f32[16,128]{1,0:T(8,128)S(1)} %shard_map.70.refs_12_), channel_id=1, source_target_pairs={{0,4},{4,0},{8,12},{12,8},{16,20},{20,16},{24,28},{28,24},{1,5},{5... | collective-permute-start | bytes 24584 | tf_op jit(solution)/shard_map/ppermute | solution.py:221
  74.3 5.4 %collective-permute-start.32 = (f32[8,128]{1,0:T(8,128)S(1)}, f32[8,128]{1,0:T(8,128)S(1)}, u32[]{:S(2)}, u32[]{:S(2)}) collective-permute-start(f32[8,128]{1,0:T(8,128)S(1)} %get-tuple-element.38.refs_9_), channel_id=1, source_target_pairs={{0,3},{1,2},{2,1},{3,0},{4,7},{5,6},{6,5},{7,4},{8,11},{9,10},{10,... | collective-permute-start | bytes 12296 | tf_op jit(solution)/shard_map/ppermute | solution.py:221
  76.8 4.5 %collective-permute-start.31 = (f32[8,128]{1,0:T(8,128)S(1)}, f32[8,128]{1,0:T(8,128)S(1)}, u32[]{:S(2)}, u32[]{:S(2)}) collective-permute-start(f32[8,128]{1,0:T(8,128)S(1)} %get-tuple-element.38.refs_9_), channel_id=1, source_target_pairs={{0,2},{1,3},{2,0},{3,1},{4,6},{5,7},{6,4},{7,5},{8,10},{9,11},{10,... | collective-permute-start | bytes 12296 | tf_op jit(solution)/shard_map/ppermute | solution.py:221
  77.7 3.6 %collective-permute-start.30 = (f32[8,128]{1,0:T(8,128)S(1)}, f32[8,128]{1,0:T(8,128)S(1)}, u32[]{:S(2)}, u32[]{:S(2)}) collective-permute-start(f32[8,128]{1,0:T(8,128)S(1)} %get-tuple-element.38.refs_9_), channel_id=1, source_target_pairs={{0,1},{1,0},{2,3},{3,2},{4,5},{5,4},{6,7},{7,6},{8,9},{9,8},{10,11... | collective-permute-start | bytes 12296 | tf_op jit(solution)/shard_map/ppermute | solution.py:221
  86.0 4.4 %collective-permute-start.39 = (f32[8,512]{1,0:T(8,128)S(1)}, f32[8,512]{1,0:T(8,128)S(1)}, u32[]{:S(2)}, u32[]{:S(2)}) collective-permute-start(f32[8,512]{1,0:T(8,128)S(1)} %get-tuple-element.39.refs_9_), channel_id=1, source_target_pairs={{0,28},{4,24},{8,20},{12,16},{16,12},{20,8},{24,4},{28,0},{1,29},{... | collective-permute-start | bytes 49160 | tf_op jit(solution)/shard_map/ppermute | solution.py:221
  86.1 5.7 %collective-permute-start.38 = (f32[8,512]{1,0:T(8,128)S(1)}, f32[8,512]{1,0:T(8,128)S(1)}, u32[]{:S(2)}, u32[]{:S(2)}) collective-permute-start(f32[8,512]{1,0:T(8,128)S(1)} %get-tuple-element.39.refs_9_), channel_id=1, source_target_pairs={{0,24},{4,28},{8,16},{12,20},{16,8},{20,12},{24,0},{28,4},{1,25},{... | collective-permute-start | bytes 49160 | tf_op jit(solution)/shard_map/ppermute | solution.py:221
  87.4 4.9 %collective-permute-start.37 = (f32[8,512]{1,0:T(8,128)S(1)}, f32[8,512]{1,0:T(8,128)S(1)}, u32[]{:S(2)}, u32[]{:S(2)}) collective-permute-start(f32[8,512]{1,0:T(8,128)S(1)} %get-tuple-element.39.refs_9_), channel_id=1, source_target_pairs={{0,20},{4,16},{8,28},{12,24},{16,4},{20,0},{24,12},{28,8},{1,21},{... | collective-permute-start | bytes 49160 | tf_op jit(solution)/shard_map/ppermute | solution.py:221
  89.6 3.7 %collective-permute-start.36 = (f32[8,512]{1,0:T(8,128)S(1)}, f32[8,512]{1,0:T(8,128)S(1)}, u32[]{:S(2)}, u32[]{:S(2)}) collective-permute-start(f32[8,512]{1,0:T(8,128)S(1)} %get-tuple-element.39.refs_9_), channel_id=1, source_target_pairs={{0,16},{4,20},{8,24},{12,28},{16,0},{20,4},{24,8},{28,12},{1,17},{... | collective-permute-start | bytes 49160 | tf_op jit(solution)/shard_map/ppermute | solution.py:221
  90.4 3.2 %collective-permute-start.35 = (f32[8,512]{1,0:T(8,128)S(1)}, f32[8,512]{1,0:T(8,128)S(1)}, u32[]{:S(2)}, u32[]{:S(2)}) collective-permute-start(f32[8,512]{1,0:T(8,128)S(1)} %get-tuple-element.39.refs_9_), channel_id=1, source_target_pairs={{0,12},{4,8},{8,4},{12,0},{16,28},{20,24},{24,20},{28,16},{1,13},{... | collective-permute-start | bytes 49160 | tf_op jit(solution)/shard_map/ppermute | solution.py:221
  90.4 3.8 %collective-permute-start.34 = (f32[8,512]{1,0:T(8,128)S(1)}, f32[8,512]{1,0:T(8,128)S(1)}, u32[]{:S(2)}, u32[]{:S(2)}) collective-permute-start(f32[8,512]{1,0:T(8,128)S(1)} %get-tuple-element.39.refs_9_), channel_id=1, source_target_pairs={{0,8},{4,12},{8,0},{12,4},{16,24},{20,28},{24,16},{28,20},{1,9},{5... | collective-permute-start | bytes 49160 | tf_op jit(solution)/shard_map/ppermute | solution.py:221
  91.7 2.5 %collective-permute-start.33 = (f32[8,512]{1,0:T(8,128)S(1)}, f32[8,512]{1,0:T(8,128)S(1)}, u32[]{:S(2)}, u32[]{:S(2)}) collective-permute-start(f32[8,512]{1,0:T(8,128)S(1)} %get-tuple-element.39.refs_9_), channel_id=1, source_target_pairs={{0,4},{4,0},{8,12},{12,8},{16,20},{20,16},{24,28},{28,24},{1,5},{5... | collective-permute-start | bytes 49160 | tf_op jit(solution)/shard_map/ppermute | solution.py:221
  101.9 5.5 %collective-permute-start.42 = (f32[8,128]{1,0:T(8,128)S(1)}, f32[8,128]{1,0:T(8,128)S(1)}, u32[]{:S(2)}, u32[]{:S(2)}) collective-permute-start(f32[8,128]{1,0:T(8,128)S(1)} %shard_map.73.refs_9_), channel_id=1, source_target_pairs={{0,3},{1,2},{2,1},{3,0},{4,7},{5,6},{6,5},{7,4},{8,11},{9,10},{10,... | collective-permute-start | bytes 12296 | tf_op jit(solution)/shard_map/ppermute | solution.py:221
  103.4 4.5 %collective-permute-start.41 = (f32[8,128]{1,0:T(8,128)S(1)}, f32[8,128]{1,0:T(8,128)S(1)}, u32[]{:S(2)}, u32[]{:S(2)}) collective-permute-start(f32[8,128]{1,0:T(8,128)S(1)} %shard_map.73.refs_9_), channel_id=1, source_target_pairs={{0,2},{1,3},{2,0},{3,1},{4,6},{5,7},{6,4},{7,5},{8,10},{9,11},{10,... | collective-permute-start | bytes 12296 | tf_op jit(solution)/shard_map/ppermute | solution.py:221
  104.4 3.6 %collective-permute-start.40 = (f32[8,128]{1,0:T(8,128)S(1)}, f32[8,128]{1,0:T(8,128)S(1)}, u32[]{:S(2)}, u32[]{:S(2)}) collective-permute-start(f32[8,128]{1,0:T(8,128)S(1)} %shard_map.73.refs_9_), channel_id=1, source_target_pairs={{0,1},{1,0},{2,3},{3,2},{4,5},{5,4},{6,7},{7,6},{8,9},{9,8},{10,11... | collective-permute-start | bytes 12296 | tf_op jit(solution)/shard_map/ppermute | solution.py:221
  112.6 3.5 %collective-permute-start.43 = (f32[1,512]{1,0:T(1,128)S(1)}, f32[1,512]{1,0:T(1,128)S(1)}, u32[]{:S(2)}, u32[]{:S(2)}) collective-permute-start(f32[1,512]{1,0:T(1,128)S(1)} %get-tuple-element.42), channel_id=1, source_target_pairs={{0,4},{4,0},{8,12},{12,8},{16,20},{20,16},{24,28},{28,24},{1,5},{5... | collective-permute-start | bytes 6152 | tf_op jit(solution)/shard_map/ppermute | solution.py:221
  112.6 4.8 %collective-permute-start.44 = (f32[1,512]{1,0:T(1,128)S(1)}, f32[1,512]{1,0:T(1,128)S(1)}, u32[]{:S(2)}, u32[]{:S(2)}) collective-permute-start(f32[1,512]{1,0:T(1,128)S(1)} %get-tuple-element.43), channel_id=1, source_target_pairs={{0,8},{4,12},{8,0},{12,4},{16,24},{20,28},{24,16},{28,20},{1,9},{5... | collective-permute-start | bytes 6152 | tf_op jit(solution)/shard_map/ppermute | solution.py:221
  113.9 4.9 %collective-permute-start.45 = (f32[1,512]{1,0:T(1,128)S(1)}, f32[1,512]{1,0:T(1,128)S(1)}, u32[]{:S(2)}, u32[]{:S(2)}) collective-permute-start(f32[1,512]{1,0:T(1,128)S(1)} %get-tuple-element.44), channel_id=1, source_target_pairs={{0,12},{4,8},{8,4},{12,0},{16,28},{20,24},{24,20},{28,16},{1,13},{... | collective-permute-start | bytes 6152 | tf_op jit(solution)/shard_map/ppermute | solution.py:221
  114.5 4.4 %collective-permute-start.46 = (f32[1,512]{1,0:T(1,128)S(1)}, f32[1,512]{1,0:T(1,128)S(1)}, u32[]{:S(2)}, u32[]{:S(2)}) collective-permute-start(f32[1,512]{1,0:T(1,128)S(1)} %get-tuple-element.45), channel_id=1, source_target_pairs={{0,16},{4,20},{8,24},{12,28},{16,0},{20,4},{24,8},{28,12},{1,17},{... | collective-permute-start | bytes 6152 | tf_op jit(solution)/shard_map/ppermute | solution.py:221
  115.7 3.2 %collective-permute-start.47 = (f32[1,512]{1,0:T(1,128)S(1)}, f32[1,512]{1,0:T(1,128)S(1)}, u32[]{:S(2)}, u32[]{:S(2)}) collective-permute-start(f32[1,512]{1,0:T(1,128)S(1)} %get-tuple-element.46), channel_id=1, source_target_pairs={{0,20},{4,16},{8,28},{12,24},{16,4},{20,0},{24,12},{28,8},{1,21},{... | collective-permute-start | bytes 6152 | tf_op jit(solution)/shard_map/ppermute | solution.py:221
  116.1 4.5 %collective-permute-start.48 = (f32[1,512]{1,0:T(1,128)S(1)}, f32[1,512]{1,0:T(1,128)S(1)}, u32[]{:S(2)}, u32[]{:S(2)}) collective-permute-start(f32[1,512]{1,0:T(1,128)S(1)} %get-tuple-element.47), channel_id=1, source_target_pairs={{0,24},{4,28},{8,16},{12,20},{16,8},{20,12},{24,0},{28,4},{1,25},{... | collective-permute-start | bytes 6152 | tf_op jit(solution)/shard_map/ppermute | solution.py:221
  117.4 3.9 %collective-permute-start.49 = (f32[1,512]{1,0:T(1,128)S(1)}, f32[1,512]{1,0:T(1,128)S(1)}, u32[]{:S(2)}, u32[]{:S(2)}) collective-permute-start(f32[1,512]{1,0:T(1,128)S(1)} %get-tuple-element.48), channel_id=1, source_target_pairs={{0,28},{4,24},{8,20},{12,16},{16,12},{20,8},{24,4},{28,0},{1,29},{... | collective-permute-start | bytes 6152 | tf_op jit(solution)/shard_map/ppermute | solution.py:221

commit v2 on v1

--- a/solution.py
+++ b/solution.py
@@ -89,88 +89,105 @@
         rows = pl.ds(pl.multiple_of(i * LANES, LANES), LANES)
         lse, mass, carried = row_pass(a_ref[rows, :], t_refs, column, scores, width, True)
         carried_ref[rows, :] = carried / mass
-        lse_ref[pl.ds((c ^ (i // per)) * per + i % per, 1), :] = as_lanes(lse)
-
-
-def moment_kernel(ns, rows_total, pieces, *refs):
-    s_refs, l_refs, carried_ref = refs[:ns], refs[ns : 2 * ns], refs[2 * ns]
-    out_refs, total_ref = refs[2 * ns + 1 : -1], refs[-1]
+        row = as_lanes(lse)
+        for copy in range(ns):
+            lse_ref[copy, pl.ds((c ^ (i // per)) * per + i % per, 1), :] = row
+
+
+def moment_kernel(ns, rows_total, *refs):
+    s_refs, own_ref, l_ref, carried_ref, out_ref, weight_ref = refs[:ns], *refs[ns:]
     c = lax.axis_index("col")
     piece = s_refs[0].shape[0]
     per = piece // LANES
-    scale = jnp.exp(l_refs[0][...] - log_sum([l[...] for l in l_refs])) * (1.0 / rows_total)
-    weight, = (scale,)
-    total_ref[0 : weight.shape[0], :] = weight
+    shift = log_sum([l_ref[k] for k in range(ns)])
+    weight_ref[...] = jnp.exp(own_ref[0] - shift) * (1.0 / rows_total)
     total = None
     for k in range(ns):
         for j in range(per):
-            w = as_rows(total_ref[pl.ds((c ^ k) * per + j, 1), :])
+            w = as_rows(weight_ref[pl.ds((c ^ k) * per + j, 1), :])
             at = (k * per + j) * LANES
             x = carried_ref[at : at + LANES, :] * w
             s = s_refs[k][j * LANES : (j + 1) * LANES, :]
             for part in reversed(split3(x)):
                 term = lax.dot_general(s, part, TN_DIMS, preferred_element_type=jnp.float32)
                 total = term if total is None else total + term
-    if pieces == 1:
-        out_refs[0][...] = total
-        return
-    r = lax.axis_index("row")
-    total_ref[...] = total
-    size = total.shape[0] // pieces
-    for k in range(pieces):
-        out_refs[k][...] = total_ref[pl.ds(pl.multiple_of((r ^ k) * size, size), size), :]
-
-
-def add_kernel(*refs):
-    refs[-1][...] = functools.reduce(jnp.add, [r[...] for r in refs[:-1]])
-
-
-def first_rows_kernel(ns, nt, width, pieces, *refs):
-    s_refs, t_refs, m_refs = refs[:ns], refs[ns : ns + nt], refs[ns + nt : ns + nt + pieces]
-    moment_ref, a_ref, lse_ref, scores = refs[ns + nt + pieces :]
-    c = lax.axis_index("col")
+    write_pieces(out_ref, total)
+
+
+def write_pieces(out_ref, matrix):
+    pieces, _, size = out_ref.shape
+    depth = matrix.shape[1]
+    if size % depth == 0:
+        each = size // depth
+        for i in range(matrix.shape[0]):
+            out_ref[i // each, :, (i % each) * depth : (i % each + 1) * depth] = matrix[i : i + 1, :]
+    else:
+        each = depth // size
+        for i in range(matrix.shape[0]):
+            for j in range(each):
+                out_ref[i * each + j] = matrix[i : i + 1, j * size : (j + 1) * size]
+
+
+def read_pieces(ref, out_ref):
+    pieces, _, size = ref.shape
+    depth = out_ref.shape[1]
+    if size % depth == 0:
+        each = size // depth
+        for i in range(out_ref.shape[0]):
+            out_ref[i : i + 1, :] = ref[i // each, :, (i % each) * depth : (i % each + 1) * depth]
+    else:
+        each = depth // size
+        for i in range(out_ref.shape[0]):
+            for j in range(each):
+                out_ref[i : i + 1, j * size : (j + 1) * size] = ref[i * each + j]
+
+
+def add_kernel(x_ref, out_ref):
+    total = functools.reduce(jnp.add, [x_ref[k] for k in range(x_ref.shape[0])])
+    for k in range(out_ref.shape[0]):
+        out_ref[k] = total
+
+
+def first_rows_kernel(ns, nt, width, *refs):
+    s_refs, t_refs, m_ref = refs[:ns], refs[ns : ns + nt], refs[ns + nt]
+    moment_ref, a_ref, lse_ref, scores = refs[ns + nt + 1 :]
     piece = s_refs[0].shape[0]
-    per = piece // LANES
-    if pieces == 1:
-        moment_ref[...] = m_refs[0][...]
-    else:
-        r = lax.axis_index("row")
-        size = m_refs[0].shape[0]
-        for k in range(pieces):
-            moment_ref[pl.ds(pl.multiple_of((r ^ k) * size, size), size), :] = m_refs[k][...]
+    read_pieces(m_ref, moment_ref)
     for k in range(ns):
         a_ref[k * piece : (k + 1) * piece, :] = project4(s_refs[k][...], moment_ref[...])
     column = [potential_rows(t, width) for t in t_refs]
+    all_rows(ns, a_ref, t_refs, column, scores, width, lse_ref)
+
+
+def all_rows(ns, a_ref, t_refs, column, scores, width, lse_ref):
+    c = lax.axis_index("col")
+    per = a_ref.shape[0] // ns // LANES
 
     @pl.loop(0, ns * per)
     def _(i):
         rows = pl.ds(pl.multiple_of(i * LANES, LANES), LANES)
         lse, _, _ = row_pass(a_ref[rows, :], t_refs, column, scores, width, False)
-        lse_ref[pl.ds((c ^ (i // per)) * per + i % per, 1), :] = as_lanes(lse)
+        row = as_lanes(lse)
+        for copy in range(ns):
+            lse_ref[copy, pl.ds((c ^ (i // per)) * per + i % per, 1), :] = row
 
 
 def rows_kernel(ns, nt, width, rows_total, *refs):
-    a_ref, t_refs, l_refs = refs[0], refs[1 : 1 + nt], refs[1 + nt : 1 + 2 * nt]
-    lse_ref, column_ref, scores = refs[1 + 2 * nt :]
-    c, r = lax.axis_index("col"), lax.axis_index("row")
-    per = a_ref.shape[0] // ns // LANES
-    column_ref[...] = math.log(rows_total) - log_sum([l[...] for l in l_refs])
+    a_ref, t_refs, l_ref = refs[0], refs[1 : 1 + nt], refs[1 + nt]
+    lse_ref, column_ref, scores = refs[2 + nt :]
+    r = lax.axis_index("row")
+    column_ref[...] = math.log(rows_total) - log_sum([l_ref[k] for k in range(nt)])
     column = [column_ref[pl.ds(r ^ k, 1), :] for k in range(nt)]
-
-    @pl.loop(0, ns * per)
-    def _(i):
-        rows = pl.ds(pl.multiple_of(i * LANES, LANES), LANES)
-        lse, _, _ = row_pass(a_ref[rows, :], t_refs, column, scores, width, False)
-        lse_ref[pl.ds((c ^ (i // per)) * per + i % per, 1), :] = as_lanes(lse)
+    all_rows(ns, a_ref, t_refs, column, scores, width, lse_ref)
 
 
 def columns_kernel(ns, nt, width, cols_total, last, *refs):
-    a_ref, t_refs, l_refs = refs[0], refs[1 : 1 + nt], refs[1 + nt : 1 + nt + ns]
-    out_refs, (sp_ref, spread_rows, scores) = refs[1 + nt + ns : -3], refs[-3:]
+    a_ref, t_refs, l_ref = refs[0], refs[1 : 1 + nt], refs[1 + nt]
+    out_ref, sp_ref, spread_rows, scores = refs[2 + nt :]
     c, r = lax.axis_index("col"), lax.axis_index("row")
     rows = a_ref.shape[0]
     per = rows // ns // LANES
-    sp_ref[...] = math.log(cols_total) - log_sum([l[...] for l in l_refs])
+    sp_ref[...] = math.log(cols_total) - log_sum([l_ref[k] for k in range(ns)])
     for k in range(ns):
         for j in range(per):
             at = (k * per + j) * LANES
@@ -194,13 +211,14 @@
             mass = m if mass is None else mass + m
         lse = top + jnp.log(jnp.sum(mass, axis=0, keepdims=True))
         if last:
-            out_refs[g][...] = lse
+            out_ref[pl.ds(r ^ g, 1)] = lse[None]
         else:
-            out_refs[0][pl.ds(r ^ g, 1), :] = lse
-
-
-def update_kernel(rows_total, *refs):
-    refs[-1][...] = math.log(rows_total) - log_sum([r[...] for r in refs[:-1]])
+            for copy in range(nt):
+                out_ref[copy, pl.ds(r ^ g, 1), :] = lse
+
+
+def update_kernel(rows_total, l_ref, out_ref):
+    out_ref[...] = math.log(rows_total) - log_sum([l_ref[k] for k in range(l_ref.shape[0])])
 
 
 def call(kernel, out, args, scratch=(), flops=0, exps=0):
@@ -235,12 +253,12 @@
     return [got[k] for k in range(n)]
 
 
-def deal(parts, axis):
-    return [parts[0]] + [swap(parts[k], axis, k) for k in range(1, len(parts))]
+def deal(x, axis):
+    return lax.all_to_all(x, axis, 0, 0, tiled=True)
 
 
 def per_device(source, target, target_potential, prev_moment):
-    f32 = jnp.float32
+    f32, shape = jnp.float32, jax.ShapeDtypeStruct
     ns, nt = lax.axis_size("col"), lax.axis_size("row")
     piece, width = source.shape[0], target.shape[0]
     depth = source.shape[1]
@@ -250,36 +268,33 @@
     tail = jnp.pad(target_potential.reshape(groups, LANES), ((0, 16 - groups), (0, 0)))
     t_blocks = exchange_pairs(jnp.concatenate([target, tail], axis=0), "row")
     s_pieces = exchange(source, "col")
-    tile = jax.ShapeDtypeStruct((rows // LANES, LANES), f32)
+    tile = shape((rows // LANES, LANES), f32)
+    tiles = shape((ns, rows // LANES, LANES), f32)
     flops, exps = 2 * rows * cols * depth, rows * cols
     row_scores = pltpu.VMEM((LANES, cols), f32)
 
     lse, carried = call(
         functools.partial(couple_kernel, ns, nt, width),
-        [tile, jax.ShapeDtypeStruct((rows, depth), f32)],
+        [tiles, shape((rows, depth), f32)],
         s_pieces + t_blocks + [prev_moment],
         [pltpu.VMEM((rows, depth), jnp.bfloat16), row_scores],
         2 * flops,
         exps,
     )
-    pieces = nt if depth % (8 * nt) == 0 else 1
-    parts = call(
-        functools.partial(moment_kernel, ns, rows_total, pieces),
-        [jax.ShapeDtypeStruct((depth // pieces, depth), f32)] * pieces,
-        s_pieces + exchange(lse, "col") + [carried],
-        [pltpu.VMEM((depth, depth), f32)],
+    devices = ns * nt
+    pieces = shape((devices, 1, depth * depth // devices), f32)
+    parts, = call(
+        functools.partial(moment_kernel, ns, rows_total),
+        [pieces],
+        s_pieces + [lse, deal(lse, "col"), carried],
+        [pltpu.VMEM(tile.shape, f32)],
         6 * rows * depth * depth,
     )
-    if pieces == 1:
-        m_parts = [lax.psum(parts[0], ("row", "col"))]
-    else:
-        summed, = call(add_kernel, [jax.ShapeDtypeStruct(parts[0].shape, f32)], deal(parts, "row"))
-        summed, = call(add_kernel, [jax.ShapeDtypeStruct(parts[0].shape, f32)], exchange(summed, "col"))
-        m_parts = exchange(summed, "row")
+    summed, = call(add_kernel, [pieces], [deal(parts, ("row", "col"))])
     moment, a, lse = call(
-        functools.partial(first_rows_kernel, ns, nt, width, pieces),
-        [jax.ShapeDtypeStruct((depth, depth), f32), jax.ShapeDtypeStruct((rows, depth), jnp.bfloat16), tile],
-        s_pieces + t_blocks + m_parts,
+        functools.partial(first_rows_kernel, ns, nt, width),
+        [shape((depth, depth), f32), shape((rows, depth), jnp.bfloat16), tiles],
+        s_pieces + t_blocks + [deal(summed, ("row", "col"))],
         [row_scores],
         flops,
         exps,
@@ -289,24 +304,21 @@
         if iteration > 0:
             lse, = call(
                 functools.partial(rows_kernel, ns, nt, width, rows_total),
-                [tile],
-                [a] + t_blocks + exchange(column_lse, "row"),
+                [tiles],
+                [a] + t_blocks + [deal(column_lse, "row")],
                 [pltpu.VMEM((nt, width), f32), row_scores],
                 flops,
                 exps,
             )
-        one = jax.ShapeDtypeStruct((1, width), f32)
-        out = [one] * nt if last else [jax.ShapeDtypeStruct((nt, width), f32)]
-        *outs, source_potential = call(
+        column_lse, source_potential = call(
             functools.partial(columns_kernel, ns, nt, width, cols_total, last),
-            out + [tile],
-            [a] + t_blocks + exchange(lse, "col"),
+            [shape((nt, 1, width) if last else (nt, nt, width), f32), tile],
+            [a] + t_blocks + [deal(lse, "col")],
             [pltpu.VMEM((rows, LANES), f32), pltpu.VMEM((2, rows, width), f32)],
             flops,
             exps,
         )
-        column_lse = outs[0]
-    update, = call(functools.partial(update_kernel, rows_total), [one], deal(outs, "row"))
+    update, = call(functools.partial(update_kernel, rows_total), [shape((1, width), f32)], [deal(column_lse, "row")])
     return moment, source_potential.reshape(rows), update.reshape(width)
 
 

time: 122 us -> 120 us (0.984)
  blocking collectives: 0 us -> 59.8 us
  starting transfers between devices: 55.7 us -> 12.8 us
  waiting for transfers between devices: 27.8 us -> 8.96 us
    all_to_all x0 -> x7, blocking collectives: none -> 59.8 us  [deal(): return lax.all_to_all(x, axis, 0, 0, tiled=True)]
    ppermute x50 -> x10, starting transfers between devices: 55.7 us -> 12.8 us  [swap(): lax.ppermute(x, axis, [(i, i ^ k) for i in range(lax.axis_size(axis))])]
    ppermute x50 -> x10, waiting for transfers between devices: 27.8 us -> 8.96 us  [swap(): lax.ppermute(x, axis, [(i, i ^ k) for i in range(lax.axis_size(axis))])]
    pallas_call x9 -> x8, Pallas kernels: 36.1 us -> 36.1 us  [call(): pl.pallas_call(kernel, out_shape=list(out), in_specs=[vmem] * len(args),...]
  transfers between devices with their start and end apart: 50 -> 10, of which waited for: 25 -> 4; matrix products, arithmetic and copies ran while one was open for 0% -> 0% of each run, Pallas kernels for 0% -> 0%
where the time goes in v2:
time: 120 us
  blocking collectives  59.8 us (50%)
  Pallas kernels  36.1 us (30%)
  starting transfers between devices  12.8 us (11%)
  waiting for transfers between devices  8.96 us (7%)
    all_to_all x7, blocking collectives, deal(): return lax.all_to_all(x, axis, 0, 0, tiled=True)  59.8 us
    pallas_call x8, Pallas kernels, call(): pl.pallas_call(kernel, out_shape=list(out), in_specs=[vmem] * len(args),...  36.1 us
    ppermute x10, starting transfers between devices, swap(): lax.ppermute(x, axis, [(i, i ^ k) for i in range(lax.axis_size(axis))])  12.8 us
    ppermute x10, waiting for transfers between devices, swap(): lax.ppermute(x, axis, [(i, i ^ k) for i in range(lax.axis_size(axis))])  8.96 us
  transfers between devices with their start and end apart: 10, of which 4 were waited for; matrix products, arithmetic and copies ran while one was open for 0% of the time, Pallas kernels for 0%

profile of v2, /device:TPU:0, one launch (start us, length us, event | category | flops | bytes accessed | tf_op | source)
XLA Modules:
  0.0 120.0 jit_solution(9379097519112180805)
XLA Ops:
  0.6 0.0 copy-start.2
  0.6 0.7 copy-done.2
  1.3 0.0 copy-start
  1.3 0.0 copy-start.1
  1.3 0.9 fusion.1.refs_4_.refs_1_
  2.3 4.0 %collective-permute-start.8 = (bf16[528,128]{1,0:T(8,128)(2,1)S(1)}, bf16[528,128]{1,0:T(8,128)(2,1)S(1)}, u32[]{:S(2)}, u32[]{:S(2)}) collective-permute-start(bf16[528,128]{1,0:T(8,128)(2,1)S(1)} %fusion.1.refs_4_.refs_1_), channel_id=1, source_target_pairs={{0,24},{4,28},{8,16},{12,20},{16,8},{20,12},{24,0},{28,4},{1,25},{... | collective-permute-start | bytes 405512 | tf_op jit(solution)/shard_map/ppermute | solution.py:239
  6.2 0.5 collective-permute-start.6
  6.7 0.1 collective-permute-start.4
  6.9 0.0 copy-done
  6.9 4.0 %collective-permute-start.2 = (bf16[256,128]{1,0:T(8,128)(2,1)S(1)}, bf16[256,128]{1,0:T(8,128)(2,1)S(1)}, u32[]{:S(2)}, u32[]{:S(2)}) collective-permute-start(bf16[256,128]{1,0:T(8,128)(2,1)S(1)} %copy-done), channel_id=1, source_target_pairs={{0,3},{1,2},{2,1},{3,0},{4,7},{5,6},{6,5},{7,4},{8,11},{9,10},{10,... | collective-permute-start | bytes 196616 | tf_op jit(solution)/shard_map/ppermute | solution.py:239
  10.9 0.0 collective-permute-start.3
  10.9 0.0 collective-permute-done.8.refs_10_.refs_7_
  10.9 0.5 collective-permute-start.9
  11.4 1.3 %collective-permute-done.6.refs_8_.refs_5_ = bf16[528,128]{1,0:T(8,128)(2,1)S(1)} collective-permute-done((bf16[528,128]{1,0:T(8,128)(2,1)S(1)}, bf16[528,128]{1,0:T(8,128)(2,1)S(1)}, u32[]{:S(2)}, u32[]{:S(2)}) %collective-permute-start.6) | collective-permute-done | bytes 135200 | tf_op jit(solution)/shard_map/ppermute | solution.py:239
  12.7 0.0 collective-permute-start.7
  12.7 0.2 collective-permute-done.4.refs_6_.refs_3_
  13.0 0.3 collective-permute-start.5
  13.2 0.0 collective-permute-done.2.refs_3_
  13.2 2.8 %collective-permute-start.1 = (bf16[256,128]{1,0:T(8,128)(2,1)S(1)}, bf16[256,128]{1,0:T(8,128)(2,1)S(1)}, u32[]{:S(2)}, u32[]{:S(2)}) collective-permute-start(bf16[256,128]{1,0:T(8,128)(2,1)S(1)} %copy-done), channel_id=1, source_target_pairs={{0,2},{1,3},{2,0},{3,1},{4,6},{5,7},{6,4},{7,5},{8,10},{9,11},{10,... | collective-permute-start | bytes 196616 | tf_op jit(solution)/shard_map/ppermute | solution.py:239
  16.0 3.8 %collective-permute-done.1.refs_2_ = bf16[256,128]{1,0:T(8,128)(2,1)S(1)} collective-permute-done((bf16[256,128]{1,0:T(8,128)(2,1)S(1)}, bf16[256,128]{1,0:T(8,128)(2,1)S(1)}, u32[]{:S(2)}, u32[]{:S(2)}) %collective-permute-start.1) | collective-permute-done | bytes 65568 | tf_op jit(solution)/shard_map/ppermute | solution.py:239
  19.8 0.7 collective-permute-start
  20.5 3.6 %collective-permute-done.refs_1_ = bf16[256,128]{1,0:T(8,128)(2,1)S(1)} collective-permute-done((bf16[256,128]{1,0:T(8,128)(2,1)S(1)}, bf16[256,128]{1,0:T(8,128)(2,1)S(1)}, u32[]{:S(2)}, u32[]{:S(2)}) %collective-permute-start) | collective-permute-done | bytes 65568 | tf_op jit(solution)/shard_map/ppermute | solution.py:239
  24.1 0.0 collective-permute-done.3.refs_5_.refs_2_
  24.1 0.0 collective-permute-done.9.refs_11_.refs_8_
  24.1 0.0 collective-permute-done.7.refs_9_.refs_6_
  24.1 0.0 collective-permute-done.5.refs_7_.refs_4_
  24.1 0.0 copy-done.1
  24.1 10.1 %shard_map.67 = (f32[4,8,128]{2,1,0:T(8,128)S(1)}, f32[1024,128]{1,0:T(8,128)S(1)}) custom-call(bf16[256,128]{1,0:T(8,128)(2,1)S(1)} %copy-done, bf16[256,128]{1,0:T(8,128)(2,1)S(1)} %collective-permute-done.refs_1_, bf16[256,128]{1,0:T(8,128)(2,1)S(1)} %collective-permute-done.1.refs_2_, bf16[256,128]{1,0:T(8,128)(2,1)S(1)} %collective-permute-done.2.refs_3_, ...), custom_call_target="tpu_custom_call" | custom-call | flops 2147483648 | bytes 1949696 | tf_op jit(solution)/shard_map/pallas_call | solution.py:227
  34.2 10.2 %all_to_all.35.refs_5_ = f32[4,8,128]{2,1,0:T(8,128)S(1)} all-to-all(f32[4,8,128]{2,1,0:T(8,128)S(1)} %get-tuple-element.11.refs_4_), channel_id=1, replica_groups=mesh['row'=8,'col'=4] {'col'}, dimensions={0} | all-to-all | bytes 32768 | tf_op jit(solution)/shard_map/all_to_all | solution.py:257
  44.4 0.6 shard_map.68
  44.9 9.5 %all_to_all.36.x_ref = f32[32,1,512]{2,1,0:T(1,128)S(1)} all-to-all(f32[32,1,512]{2,1,0:T(1,128)S(1)} %shard_map.68), channel_id=1, replica_groups=mesh['row'=8,'col'=4] {'row','col'}, dimensions={0} | all-to-all | bytes 131072 | tf_op jit(solution)/shard_map/all_to_all | solution.py:257
  54.5 9.2 %all_to_all.37.refs_12_ = f32[32,1,512]{2,1,0:T(1,128)S(1)} all-to-all(f32[32,1,512]{2,1,0:T(1,128)S(1)} %shard_map.69), channel_id=1, replica_groups=mesh['row'=8,'col'=4] {'row','col'}, dimensions={0} | all-to-all | bytes 131072 | tf_op jit(solution)/shard_map/all_to_all | solution.py:257
  63.7 7.8 %shard_map.70 = (f32[128,128]{1,0:T(8,128)}, bf16[1024,128]{1,0:T(8,128)(2,1)S(1)}, f32[4,8,128]{2,1,0:T(8,128)S(1)}) custom-call(bf16[256,128]{1,0:T(8,128)(2,1)S(1)} %copy-done, bf16[256,128]{1,0:T(8,128)(2,1)S(1)} %collective-permute-done.refs_1_, bf16[256,128]{1,0:T(8,128)(2,1)S(1)} %collective-permute-done.1.refs_2_, ...), custom_call_target="tpu_custom_call" | custom-call | flops 1073741824 | bytes 1753088 | tf_op jit(solution)/shard_map/pallas_call | solution.py:227
  71.5 8.0 %all_to_all.38.refs_9_ = f32[4,8,128]{2,1,0:T(8,128)S(1)} all-to-all(f32[4,8,128]{2,1,0:T(8,128)S(1)} %get-tuple-element.15), channel_id=1, replica_groups=mesh['row'=8,'col'=4] {'col'}, dimensions={0} | all-to-all | bytes 32768 | tf_op jit(solution)/shard_map/all_to_all | solution.py:257
  79.4 4.8 %shard_map.71 = (f32[8,8,512]{2,1,0:T(8,128)S(1)}, f32[8,128]{1,0:T(8,128)}) custom-call(bf16[1024,128]{1,0:T(8,128)(2,1)S(1)} %get-tuple-element.14.refs_0_, bf16[528,128]{1,0:T(8,128)(2,1)S(1)} %fusion.1.refs_4_.refs_1_, bf16[528,128]{1,0:T(8,128)(2,1)S(1)} %collective-permute-done.3.refs_5_.refs_2_, ...), custom_call_target="tpu_custom_call" | custom-call | flops 1073741824 | bytes 1495040 | tf_op jit(solution)/shard_map/pallas_call | solution.py:227
  84.2 7.9 %all_to_all.39.refs_9_ = f32[8,8,512]{2,1,0:T(8,128)S(1)} all-to-all(f32[8,8,512]{2,1,0:T(8,128)S(1)} %get-tuple-element.16), channel_id=1, replica_groups=mesh['row'=8,'col'=4] {'row'}, dimensions={0} | all-to-all | bytes 262144 | tf_op jit(solution)/shard_map/all_to_all | solution.py:257
  92.1 7.5 %shard_map.72 = f32[4,8,128]{2,1,0:T(8,128)S(1)} custom-call(bf16[1024,128]{1,0:T(8,128)(2,1)S(1)} %get-tuple-element.14.refs_0_, bf16[528,128]{1,0:T(8,128)(2,1)S(1)} %fusion.1.refs_4_.refs_1_, bf16[528,128]{1,0:T(8,128)(2,1)S(1)} %collective-permute-done.3.refs_5_.refs_2_, bf16[528,128]{1,0:T(8,128)(2,1)S(1)} %collective-permute-done.4.refs_6_.refs_3_, ...), custom_call_target="tpu_custom_call" | custom-call | flops 1073741824 | bytes 1490944 | tf_op jit(solution)/shard_map/pallas_call | solution.py:227
  99.6 8.0 %all_to_all.40.refs_9_ = f32[4,8,128]{2,1,0:T(8,128)S(1)} all-to-all(f32[4,8,128]{2,1,0:T(8,128)S(1)} %shard_map.72), channel_id=1, replica_groups=mesh['row'=8,'col'=4] {'col'}, dimensions={0} | all-to-all | bytes 32768 | tf_op jit(solution)/shard_map/all_to_all | solution.py:257
  107.6 4.7 %shard_map.73 = (f32[8,1,512]{2,1,0:T(1,128)S(1)}, f32[8,128]{1,0:T(8,128)}) custom-call(bf16[1024,128]{1,0:T(8,128)(2,1)S(1)} %get-tuple-element.14.refs_0_, bf16[528,128]{1,0:T(8,128)(2,1)S(1)} %fusion.1.refs_4_.refs_1_, bf16[528,128]{1,0:T(8,128)(2,1)S(1)} %collective-permute-done.3.refs_5_.refs_2_, ...), custom_call_target="tpu_custom_call" | custom-call | flops 1073741824 | bytes 1380352 | tf_op jit(solution)/shard_map/pallas_call | solution.py:227
  112.3 7.1 %all_to_all.41.l_ref = f32[8,1,512]{2,1,0:T(1,128)S(1)} all-to-all(f32[8,1,512]{2,1,0:T(1,128)S(1)} %get-tuple-element.18), channel_id=1, replica_groups=mesh['row'=8,'col'=4] {'row'}, dimensions={0} | all-to-all | bytes 32768 | tf_op jit(solution)/shard_map/all_to_all | solution.py:257
  119.4 0.6 shard_map.74
  (1 shorter events, 0.0 us)
Async XLA Ops:
  0.6 0.7 copy-start.2
  1.3 5.6 %copy-start = (bf16[256,128]{1,0:T(8,128)(2,1)S(1)}, bf16[256,128]{1,0:T(8,128)(2,1)}, u32[]{:S(2)}) copy-start(bf16[256,128]{1,0:T(8,128)(2,1)} %refs_0_.5) | copy-start | bytes 196612
  1.3 22.8 %copy-start.1 = (f32[128,128]{1,0:T(8,128)S(1)}, f32[128,128]{1,0:T(8,128)}, u32[]{:S(2)}) copy-start(f32[128,128]{1,0:T(8,128)} %refs_12_.1) | copy-start | bytes 196612
  2.3 8.6 %collective-permute-start.8 = (bf16[528,128]{1,0:T(8,128)(2,1)S(1)}, bf16[528,128]{1,0:T(8,128)(2,1)S(1)}, u32[]{:S(2)}, u32[]{:S(2)}) collective-permute-start(bf16[528,128]{1,0:T(8,128)(2,1)S(1)} %fusion.1.refs_4_.refs_1_), channel_id=1, source_target_pairs={{0,24},{4,28},{8,16},{12,20},{16,8},{20,12},{24,0},{28,4},{1,25},{... | collective-permute-start | bytes 405512 | tf_op jit(solution)/shard_map/ppermute | solution.py:239
  6.2 6.5 %collective-permute-start.6 = (bf16[528,128]{1,0:T(8,128)(2,1)S(1)}, bf16[528,128]{1,0:T(8,128)(2,1)S(1)}, u32[]{:S(2)}, u32[]{:S(2)}) collective-permute-start(bf16[528,128]{1,0:T(8,128)(2,1)S(1)} %fusion.1.refs_4_.refs_1_), channel_id=1, source_target_pairs={{0,16},{4,20},{8,24},{12,28},{16,0},{20,4},{24,8},{28,12},{1,17},{... | collective-permute-start | bytes 405512 | tf_op jit(solution)/shard_map/ppermute | solution.py:239
  6.7 6.2 %collective-permute-start.4 = (bf16[528,128]{1,0:T(8,128)(2,1)S(1)}, bf16[528,128]{1,0:T(8,128)(2,1)S(1)}, u32[]{:S(2)}, u32[]{:S(2)}) collective-permute-start(bf16[528,128]{1,0:T(8,128)(2,1)S(1)} %fusion.1.refs_4_.refs_1_), channel_id=1, source_target_pairs={{0,8},{4,12},{8,0},{12,4},{16,24},{20,28},{24,16},{28,20},{1,9},{5... | collective-permute-start | bytes 405512 | tf_op jit(solution)/shard_map/ppermute | solution.py:239
  6.9 6.4 %collective-permute-start.2 = (bf16[256,128]{1,0:T(8,128)(2,1)S(1)}, bf16[256,128]{1,0:T(8,128)(2,1)S(1)}, u32[]{:S(2)}, u32[]{:S(2)}) collective-permute-start(bf16[256,128]{1,0:T(8,128)(2,1)S(1)} %copy-done), channel_id=1, source_target_pairs={{0,3},{1,2},{2,1},{3,0},{4,7},{5,6},{6,5},{7,4},{8,11},{9,10},{10,... | collective-permute-start | bytes 196616 | tf_op jit(solution)/shard_map/ppermute | solution.py:239
  10.9 13.2 %collective-permute-start.3 = (bf16[528,128]{1,0:T(8,128)(2,1)S(1)}, bf16[528,128]{1,0:T(8,128)(2,1)S(1)}, u32[]{:S(2)}, u32[]{:S(2)}) collective-permute-start(bf16[528,128]{1,0:T(8,128)(2,1)S(1)} %fusion.1.refs_4_.refs_1_), channel_id=1, source_target_pairs={{0,4},{4,0},{8,12},{12,8},{16,20},{20,16},{24,28},{28,24},{1,5},{5... | collective-permute-start | bytes 405512 | tf_op jit(solution)/shard_map/ppermute | solution.py:239
  10.9 13.2 %collective-permute-start.9 = (bf16[528,128]{1,0:T(8,128)(2,1)S(1)}, bf16[528,128]{1,0:T(8,128)(2,1)S(1)}, u32[]{:S(2)}, u32[]{:S(2)}) collective-permute-start(bf16[528,128]{1,0:T(8,128)(2,1)S(1)} %collective-permute-done.8.refs_10_.refs_7_), channel_id=1, source_target_pairs={{0,4},{4,0},{8,12},{12,8},{16,20},{20,16},{24,28},{28,24},{1,5},{5... | collective-permute-start | bytes 405512 | tf_op jit(solution)/shard_map/ppermute | solution.py:239
  12.7 11.4 %collective-permute-start.7 = (bf16[528,128]{1,0:T(8,128)(2,1)S(1)}, bf16[528,128]{1,0:T(8,128)(2,1)S(1)}, u32[]{:S(2)}, u32[]{:S(2)}) collective-permute-start(bf16[528,128]{1,0:T(8,128)(2,1)S(1)} %collective-permute-done.6.refs_8_.refs_5_), channel_id=1, source_target_pairs={{0,4},{4,0},{8,12},{12,8},{16,20},{20,16},{24,28},{28,24},{1,5},{5... | collective-permute-start | bytes 405512 | tf_op jit(solution)/shard_map/ppermute | solution.py:239
  13.0 11.1 %collective-permute-start.5 = (bf16[528,128]{1,0:T(8,128)(2,1)S(1)}, bf16[528,128]{1,0:T(8,128)(2,1)S(1)}, u32[]{:S(2)}, u32[]{:S(2)}) collective-permute-start(bf16[528,128]{1,0:T(8,128)(2,1)S(1)} %collective-permute-done.4.refs_6_.refs_3_), channel_id=1, source_target_pairs={{0,4},{4,0},{8,12},{12,8},{16,20},{20,16},{24,28},{28,24},{1,5},{5... | collective-permute-start | bytes 405512 | tf_op jit(solution)/shard_map/ppermute | solution.py:239
  13.2 6.6 %collective-permute-start.1 = (bf16[256,128]{1,0:T(8,128)(2,1)S(1)}, bf16[256,128]{1,0:T(8,128)(2,1)S(1)}, u32[]{:S(2)}, u32[]{:S(2)}) collective-permute-start(bf16[256,128]{1,0:T(8,128)(2,1)S(1)} %copy-done), channel_id=1, source_target_pairs={{0,2},{1,3},{2,0},{3,1},{4,6},{5,7},{6,4},{7,5},{8,10},{9,11},{10,... | collective-permute-start | bytes 196616 | tf_op jit(solution)/shard_map/ppermute | solution.py:239
  19.8 4.3 %collective-permute-start = (bf16[256,128]{1,0:T(8,128)(2,1)S(1)}, bf16[256,128]{1,0:T(8,128)(2,1)S(1)}, u32[]{:S(2)}, u32[]{:S(2)}) collective-permute-start(bf16[256,128]{1,0:T(8,128)(2,1)S(1)} %copy-done), channel_id=1, source_target_pairs={{0,1},{1,0},{2,3},{3,2},{4,5},{5,4},{6,7},{7,6},{8,9},{9,8},{10,11... | collective-permute-start | bytes 196616 | tf_op jit(solution)/shard_map/ppermute | solution.py:239

commit v3 on v1

v3 whole, which is shorter than its diff:
```python
import functools
import math

import jax
import jax.numpy as jnp
from jax import lax
from jax.experimental import pallas as pl
from jax.experimental.pallas import tpu as pltpu
from jax.sharding import PartitionSpec as P

ITERS = 2
LANES = 128
NT_DIMS = (((1,), (1,)), ((), ()))
TN_DIMS = (((0,), (0,)), ((), ()))


def split3(x):
    high = x.astype(jnp.bfloat16)
    rest = x - high.astype(jnp.float32)
    mid = rest.astype(jnp.bfloat16)
    low = (rest - mid.astype(jnp.float32)).astype(jnp.bfloat16)
    return high, mid, low


def project4(rows, matrix):
    total = None
    for part in reversed(split3(matrix)):
        term = jnp.dot(rows, part, preferred_element_type=jnp.float32)
        total = term if total is None else total + term
    return (total.astype(jnp.bfloat16).astype(jnp.float32) * 4.0).astype(jnp.bfloat16)


def lane_fold(op, x):
    parts = [x[:, i : i + LANES] for i in range(0, x.shape[1], LANES)]
    return functools.reduce(op, parts)


def as_lanes(column):
    return jnp.broadcast_to(column, (LANES, LANES)).T[0:1, :]


def as_rows(lanes):
    return jnp.broadcast_to(lanes, (LANES, LANES)).T


def log_sum(parts):
    top = functools.reduce(jnp.maximum, parts)
    return top + jnp.log(sum(jnp.exp(p - top) for p in parts))


def potential_rows(block_ref, width):
    groups = width // LANES
    tail = block_ref[width:, :].astype(jnp.float32)
    return jnp.concatenate([tail[i : i + 1, :] for i in range(groups)], axis=1)


def row_lse(a_ref, t_refs, column, scores, width, lse_ref, carried_ref=None):
    c = lax.axis_index("col")
    steps = a_ref.shape[0] // LANES
    per = steps // lax.axis_size("col")
    top = None
    for i in range(steps + 1):
        last_top, top, mass, carried = top, None, None, None
        for g, t_ref in enumerate(t_refs):
            at = slice(g * width, (g + 1) * width)
            if i < steps:
                a = a_ref[i * LANES : (i + 1) * LANES, :]
                s = lax.dot_general(a, t_ref[:width, :], NT_DIMS, preferred_element_type=jnp.float32)
                s = s + column[g]
                scores[i % 2, :, at] = s
                m = lane_fold(jnp.maximum, s)
                top = m if top is None else jnp.maximum(top, m)
            if i > 0:
                e = jnp.exp(scores[(i - 1) % 2, :, at] - last_top)
                m = lane_fold(jnp.add, e)
                mass = m if mass is None else mass + m
                if carried_ref is not None:
                    d = jnp.dot(e.astype(jnp.bfloat16), t_ref[:width, :], preferred_element_type=jnp.float32)
                    carried = d if carried is None else carried + d
        if i < steps:
            top = jnp.max(top, axis=1, keepdims=True)
        if i > 0:
            mass = jnp.sum(mass, axis=1, keepdims=True)
            if carried_ref is not None:
                carried_ref[(i - 1) * LANES : i * LANES, :] = carried / mass
            row = (c ^ ((i - 1) // per)) * per + (i - 1) % per
            lse_ref[pl.ds(row, 1), :] = as_lanes(last_top + jnp.log(mass))


def couple_kernel(ns, nt, width, *refs):
    s_refs, t_refs, moment_ref = refs[:ns], refs[ns : ns + nt], refs[ns + nt]
    lse_ref, carried_ref, a_ref, scores = refs[ns + nt + 1 :]
    piece = s_refs[0].shape[0]
    for k in range(ns):
        a_ref[k * piece : (k + 1) * piece, :] = project4(s_refs[k][...], moment_ref[...])
    column = [potential_rows(t, width) for t in t_refs]
    row_lse(a_ref, t_refs, column, scores, width, lse_ref, carried_ref)


def moment_kernel(ns, rows_total, *refs):
    s_refs, own_ref, l_refs, carried_ref = refs[:ns], refs[ns], refs[ns + 1 : ns + 3], refs[ns + 3]
    keep_ref, send_ref, weight_ref, total_ref = refs[ns + 4 :]
    c, r = lax.axis_index("col"), lax.axis_index("row")
    piece = s_refs[0].shape[0]
    per = piece // LANES
    shift = log_sum([l[...] for l in l_refs])
    weight_ref[...] = jnp.exp(own_ref[...] - shift) * (1.0 / rows_total)
    total = None
    for k in range(ns):
        for j in range(per):
            w = as_rows(weight_ref[pl.ds((c ^ k) * per + j, 1), :])
            at = (k * per + j) * LANES
            x = carried_ref[at : at + LANES, :] * w
            s = s_refs[k][j * LANES : (j + 1) * LANES, :]
            for part in reversed(split3(x)):
                term = lax.dot_general(s, part, TN_DIMS, preferred_element_type=jnp.float32)
                total = term if total is None else total + term
    total_ref[...] = total
    half = keep_ref.shape[0]
    keep_ref[...] = total_ref[pl.ds(pl.multiple_of((r & 1) * half, half), half), :]
    send_ref[...] = total_ref[pl.ds(pl.multiple_of((1 - (r & 1)) * half, half), half), :]


def add_kernel(x_ref, y_ref, out_ref):
    out_ref[...] = x_ref[...] + y_ref[...]


def log_sum_kernel(x_ref, y_ref, out_ref):
    out_ref[...] = log_sum([x_ref[...], y_ref[...]])


def first_rows_kernel(ns, nt, width, *refs):
    s_refs, t_refs, m_refs = refs[:ns], refs[ns : ns + nt], refs[ns + nt : ns + nt + 2]
    moment_ref, a_ref, lse_ref, scores = refs[ns + nt + 2 :]
    r = lax.axis_index("row")
    piece, half = s_refs[0].shape[0], m_refs[0].shape[0]
    for k in range(2):
        moment_ref[pl.ds(pl.multiple_of((k ^ (r & 1)) * half, half), half), :] = m_refs[k][...]
    for k in range(ns):
        a_ref[k * piece : (k + 1) * piece, :] = project4(s_refs[k][...], moment_ref[...])
    column = [potential_rows(t, width) for t in t_refs]
    row_lse(a_ref, t_refs, column, scores, width, lse_ref)


def rows_kernel(nt, width, rows_total, *refs):
    a_ref, t_refs, l_refs = refs[0], refs[1 : 1 + nt], refs[1 + nt : 3 + nt]
    lse_ref, column_ref, scores = refs[3 + nt :]
    r = lax.axis_index("row")
    column_ref[...] = math.log(rows_total) - log_sum([l[...] for l in l_refs])
    column = [column_ref[pl.ds(r ^ k, 1), :] for k in range(nt)]
    row_lse(a_ref, t_refs, column, scores, width, lse_ref)


def columns_kernel(ns, nt, width, cols_total, last, *refs):
    a_ref, t_refs, l_refs = refs[0], refs[1 : 1 + nt], refs[1 + nt : 3 + nt]
    out_refs, (sp_ref, spread_rows, scores) = refs[3 + nt : -3], refs[-3:]
    c, r = lax.axis_index("col"), lax.axis_index("row")
    rows = a_ref.shape[0]
    per = rows // ns // LANES
    sp_ref[...] = math.log(cols_total) - log_sum([l[...] for l in l_refs])
    for k in range(ns):
        for j in range(per):
            at = (k * per + j) * LANES
            spread_rows[at : at + LANES, :] = as_rows(sp_ref[pl.ds((c ^ k) * per + j, 1), :])
    step = LANES
    top = None
    for g in range(nt + 1):
        last_top, top, mass = top, None, None
        for at in range(0, rows, step):
            if g < nt:
                s = lax.dot_general(
                    a_ref[at : at + step, :], t_refs[g][:width, :], NT_DIMS, preferred_element_type=jnp.float32
                )
                s = s + jnp.concatenate([spread_rows[at : at + step, :]] * (width // LANES), axis=1)
                scores[g % 2, at : at + step, :] = s
                m = jnp.max(s.reshape(step // 8, 8, width), axis=0)
                top = m if top is None else jnp.maximum(top, m)
            if g > 0:
                e = jnp.exp(scores[(g - 1) % 2, at : at + step, :] - last_top)
                m = jnp.sum(e.reshape(step // 8, 8, width), axis=0)
                mass = m if mass is None else mass + m
        if g < nt:
            top = jnp.max(top, axis=0, keepdims=True)
        if g > 0:
            lse = last_top + jnp.log(jnp.sum(mass, axis=0, keepdims=True))
            if last:
                out_refs[(g - 1) % 2][(g - 1) // 2] = lse
            else:
                out_refs[0][pl.ds(r ^ (g - 1), 1), :] = lse


def halve_kernel(x_ref, y_ref, keep_ref, send_ref):
    for k in range(x_ref.shape[0]):
        (send_ref if k % 2 else keep_ref)[k // 2] = log_sum([x_ref[k], y_ref[k]])


def update_kernel(rows_total, x_ref, y_ref, out_ref):
    out_ref[...] = math.log(rows_total) - log_sum([x_ref[0], y_ref[0]])


def call(kernel, out, args, scratch=(), flops=0, exps=0):
    vmem = pl.BlockSpec(memory_space=pltpu.VMEM)
    bytes_accessed = sum(x.size * x.dtype.itemsize for x in list(args) + list(out))
    return pl.pallas_call(
        kernel,
        out_shape=list(out),
        in_specs=[vmem] * len(args),
        out_specs=[vmem] * len(out),
        scratch_shapes=list(scratch),
        compiler_params=pltpu.CompilerParams(vmem_limit_bytes=24 << 20),
        cost_estimate=pl.CostEstimate(flops=flops, bytes_accessed=bytes_accessed, transcendentals=exps),
    )(*args)


def swap(x, axis, k):
    return lax.ppermute(x, axis, [(i, i ^ k) for i in range(lax.axis_size(axis))])


def exchange(x, axis):
    return [x] + [swap(x, axis, k) for k in range(1, lax.axis_size(axis))]


def exchange_pairs(x, axis):
    n = lax.axis_size(axis)
    got = {0: x, 1: swap(x, axis, 1)}
    for k in range(2, n, 2):
        got[k] = swap(x, axis, k)
    for k in range(2, n, 2):
        got[k + 1] = swap(got[k], axis, 1)
    return [got[k] for k in range(n)]


def all_but_last(kernel, x, axis, first=1):
    k, n = first, lax.axis_size(axis)
    while 2 * k < n:
        x, = call(kernel, [jax.ShapeDtypeStruct(x.shape, x.dtype)], [x, swap(x, axis, k)])
        k *= 2
    return [x, swap(x, axis, k)]


def per_device(source, target, target_potential, prev_moment):
    f32, shape = jnp.float32, jax.ShapeDtypeStruct
    ns, nt = lax.axis_size("col"), lax.axis_size("row")
    piece, width = source.shape[0], target.shape[0]
    depth = source.shape[1]
    rows, cols = piece * ns, width * nt
    rows_total, cols_total = rows * nt, cols * ns
    groups = width // LANES
    tail = jnp.pad(target_potential.reshape(groups, LANES), ((0, 16 - groups), (0, 0)))
    t_blocks = exchange_pairs(jnp.concatenate([target, tail], axis=0), "row")
    s_pieces = exchange(source, "col")
    tile = shape((rows // LANES, LANES), f32)
    flops, exps = 2 * rows * cols * depth, rows * cols
    row_scores = pltpu.VMEM((2, LANES, cols), f32)

    lse, carried = call(
        functools.partial(couple_kernel, ns, nt, width),
        [tile, shape((rows, depth), f32)],
        s_pieces + t_blocks + [prev_moment],
        [pltpu.VMEM((rows, depth), jnp.bfloat16), row_scores],
        2 * flops,
        exps,
    )
    half = shape((depth // 2, depth), f32)
    keep, send = call(
        functools.partial(moment_kernel, ns, rows_total),
        [half, half],
        s_pieces + [lse] + all_but_last(log_sum_kernel, lse, "col") + [carried],
        [pltpu.VMEM(tile.shape, f32), pltpu.VMEM((depth, depth), f32)],
        6 * rows * depth * depth,
    )
    part, = call(add_kernel, [half], [keep, swap(send, "row", 1)])
    part, = call(add_kernel, [half], all_but_last(add_kernel, part, "row", 2))
    part, = call(add_kernel, [half], all_but_last(add_kernel, part, "col"))
    moment, a, lse = call(
        functools.partial(first_rows_kernel, ns, nt, width),
        [shape((depth, depth), f32), shape((rows, depth), jnp.bfloat16), tile],
        s_pieces + t_blocks + [part, swap(part, "row", 1)],
        [row_scores],
        flops,
        exps,
    )
    for iteration in range(ITERS):
        last = iteration == ITERS - 1
        if iteration > 0:
            lse, = call(
                functools.partial(rows_kernel, nt, width, rows_total),
                [tile],
                [a] + t_blocks + all_but_last(log_sum_kernel, column_lse, "row"),
                [pltpu.VMEM((nt, width), f32), row_scores],
                flops,
                exps,
            )
        blocks = shape((nt // 2, 1, width), f32)
        *outs, source_potential = call(
            functools.partial(columns_kernel, ns, nt, width, cols_total, last),
            ([blocks, blocks] if last else [shape((nt, width), f32)]) + [tile],
            [a] + t_blocks + all_but_last(log_sum_kernel, lse, "col"),
            [pltpu.VMEM((rows, LANES), f32), pltpu.VMEM((2, rows, width), f32)],
            flops,
            exps,
        )
        column_lse = outs[0]
    keep, send = outs
    k = 1
    while keep.shape[0] > 1:
        blocks = shape((keep.shape[0] // 2, 1, width), f32)
        keep, send = call(halve_kernel, [blocks, blocks], [keep, swap(send, "row", k)])
        k *= 2
    update, = call(
        functools.partial(update_kernel, rows_total), [shape((1, width), f32)], [keep, swap(send, "row", k)]
    )
    return moment, source_potential.reshape(rows), update.reshape(width)


def solution(mesh):
    placed = (P(("row", "col"), None), P(("col", "row"), None), P(("col", "row")), P())
    return jax.shard_map(
        per_device,
        mesh=mesh,
        in_specs=placed,
        out_specs=(P(), P("row"), P(("col", "row"))),
        check_vma=False,
    )
```

time: 122 us -> 114 us (0.934)
  starting transfers between devices: 55.7 us -> 36.7 us
  waiting for transfers between devices: 27.8 us -> 46 us
  Pallas kernels: 36.1 us -> 29.1 us
    ppermute x50 -> x28, starting transfers between devices: 55.7 us -> 36.7 us  [swap(): lax.ppermute(x, axis, [(i, i ^ k) for i in range(lax.axis_size(axis))])]
    ppermute x50 -> x28, waiting for transfers between devices: 27.8 us -> 46 us  [swap(): lax.ppermute(x, axis, [(i, i ^ k) for i in range(lax.axis_size(axis))])]
    pallas_call x9 -> x19, Pallas kernels: 36.1 us -> 29.1 us  [call(): pl.pallas_call(kernel, out_shape=list(out), in_specs=[vmem] * len(args),...]
  transfers between devices with their start and end apart: 50 -> 28, of which waited for: 25 -> 22; matrix products, arithmetic and copies ran while one was open for 0% -> 0% of each run, Pallas kernels for 0% -> 0%
where the time goes in v3:
time: 114 us
  waiting for transfers between devices  46 us (40%)
  starting transfers between devices  36.7 us (32%)
  Pallas kernels  29.1 us (26%)
    ppermute x28, waiting for transfers between devices, swap(): lax.ppermute(x, axis, [(i, i ^ k) for i in range(lax.axis_size(axis))])  46 us
    ppermute x28, starting transfers between devices, swap(): lax.ppermute(x, axis, [(i, i ^ k) for i in range(lax.axis_size(axis))])  36.7 us
    pallas_call x19, Pallas kernels, call(): pl.pallas_call(kernel, out_shape=list(out), in_specs=[vmem] * len(args),...  29.1 us
  transfers between devices with their start and end apart: 28, of which 22 were waited for; matrix products, arithmetic and copies ran while one was open for 0% of the time, Pallas kernels for 0%

profile of v3, /device:TPU:0, one launch (start us, length us, event | category | flops | bytes accessed | tf_op | source)
XLA Modules:
  0.0 114.2 jit_solution(1391899456924303406)
XLA Ops:
  0.6 0.7 copy-done.2
  1.3 0.9 fusion.1.refs_4_.refs_1_
  2.3 4.0 %collective-permute-start.8 = (bf16[528,128]{1,0:T(8,128)(2,1)S(1)}, bf16[528,128]{1,0:T(8,128)(2,1)S(1)}, u32[]{:S(2)}, u32[]{:S(2)}) collective-permute-start(bf16[528,128]{1,0:T(8,128)(2,1)S(1)} %fusion.1.refs_4_.refs_1_), channel_id=1, source_target_pairs={{0,24},{4,28},{8,16},{12,20},{16,8},{20,12},{24,0},{28,4},{1,25},{... | collective-permute-start | bytes 405512 | tf_op jit(solution)/shard_map/ppermute | solution.py:216
  6.2 0.5 collective-permute-start.6
  6.7 0.1 collective-permute-start.4
  6.9 4.0 %collective-permute-start.2 = (bf16[256,128]{1,0:T(8,128)(2,1)S(1)}, bf16[256,128]{1,0:T(8,128)(2,1)S(1)}, u32[]{:S(2)}, u32[]{:S(2)}) collective-permute-start(bf16[256,128]{1,0:T(8,128)(2,1)S(1)} %copy-done), channel_id=1, source_target_pairs={{0,3},{1,2},{2,1},{3,0},{4,7},{5,6},{6,5},{7,4},{8,11},{9,10},{10,... | collective-permute-start | bytes 196616 | tf_op jit(solution)/shard_map/ppermute | solution.py:216
  10.9 0.0 collective-permute-start.3
  10.9 0.0 collective-permute-done.8.refs_10_.refs_7_
  10.9 0.5 collective-permute-start.9
  11.4 1.3 %collective-permute-done.6.refs_8_.refs_5_ = bf16[528,128]{1,0:T(8,128)(2,1)S(1)} collective-permute-done((bf16[528,128]{1,0:T(8,128)(2,1)S(1)}, bf16[528,128]{1,0:T(8,128)(2,1)S(1)}, u32[]{:S(2)}, u32[]{:S(2)}) %collective-permute-start.6) | collective-permute-done | bytes 135200 | tf_op jit(solution)/shard_map/ppermute | solution.py:216
  12.7 0.0 collective-permute-start.7
  12.7 0.2 collective-permute-done.4.refs_6_.refs_3_
  13.0 0.3 collective-permute-start.5
  13.2 0.0 collective-permute-done.2.refs_3_
  13.2 2.8 %collective-permute-start.1 = (bf16[256,128]{1,0:T(8,128)(2,1)S(1)}, bf16[256,128]{1,0:T(8,128)(2,1)S(1)}, u32[]{:S(2)}, u32[]{:S(2)}) collective-permute-start(bf16[256,128]{1,0:T(8,128)(2,1)S(1)} %copy-done), channel_id=1, source_target_pairs={{0,2},{1,3},{2,0},{3,1},{4,6},{5,7},{6,4},{7,5},{8,10},{9,11},{10,... | collective-permute-start | bytes 196616 | tf_op jit(solution)/shard_map/ppermute | solution.py:216
  16.0 3.8 %collective-permute-done.1.refs_2_ = bf16[256,128]{1,0:T(8,128)(2,1)S(1)} collective-permute-done((bf16[256,128]{1,0:T(8,128)(2,1)S(1)}, bf16[256,128]{1,0:T(8,128)(2,1)S(1)}, u32[]{:S(2)}, u32[]{:S(2)}) %collective-permute-start.1) | collective-permute-done | bytes 65568 | tf_op jit(solution)/shard_map/ppermute | solution.py:216
  19.8 0.7 collective-permute-start
  20.5 3.6 %collective-permute-done.refs_1_ = bf16[256,128]{1,0:T(8,128)(2,1)S(1)} collective-permute-done((bf16[256,128]{1,0:T(8,128)(2,1)S(1)}, bf16[256,128]{1,0:T(8,128)(2,1)S(1)}, u32[]{:S(2)}, u32[]{:S(2)}) %collective-permute-start) | collective-permute-done | bytes 65568 | tf_op jit(solution)/shard_map/ppermute | solution.py:216
  24.1 0.0 collective-permute-done.3.refs_5_.refs_2_
  24.1 0.0 collective-permute-done.9.refs_11_.refs_8_
  24.1 0.0 collective-permute-done.7.refs_9_.refs_6_
  24.1 0.0 collective-permute-done.5.refs_7_.refs_4_
  24.1 7.0 %shard_map.67 = (f32[8,128]{1,0:T(8,128)S(1)}, f32[1024,128]{1,0:T(8,128)S(1)}) custom-call(bf16[256,128]{1,0:T(8,128)(2,1)S(1)} %copy-done, bf16[256,128]{1,0:T(8,128)(2,1)S(1)} %collective-permute-done.refs_1_, bf16[256,128]{1,0:T(8,128)(2,1)S(1)} %collective-permute-done.1.refs_2_, bf16[256,128]{1,0:T(8,128)(2,1)S(1)} %collective-permute-done.2.refs_3_, ...), custom_call_target="tpu_custom_call" | custom-call | flops 2147483648 | bytes 1937408 | tf_op jit(solution)/shard_map/pallas_call | solution.py:204
  31.2 0.7 collective-permute-start.10
  31.9 2.9 %collective-permute-done.10.y_ref = f32[8,128]{1,0:T(8,128)S(1)} collective-permute-done((f32[8,128]{1,0:T(8,128)S(1)}, f32[8,128]{1,0:T(8,128)S(1)}, u32[]{:S(2)}, u32[]{:S(2)}) %collective-permute-start.10) | collective-permute-done | bytes 4128 | tf_op jit(solution)/shard_map/ppermute | solution.py:216
  34.8 2.1 %collective-permute-start.11 = (f32[8,128]{1,0:T(8,128)S(1)}, f32[8,128]{1,0:T(8,128)S(1)}, u32[]{:S(2)}, u32[]{:S(2)}) collective-permute-start(f32[8,128]{1,0:T(8,128)S(1)} %shard_map.68.refs_5_), channel_id=1, source_target_pairs={{0,2},{1,3},{2,0},{3,1},{4,6},{5,7},{6,4},{7,5},{8,10},{9,11},{10,... | collective-permute-start | bytes 12296 | tf_op jit(solution)/shard_map/ppermute | solution.py:216
  36.9 2.5 %collective-permute-done.11.refs_6_ = f32[8,128]{1,0:T(8,128)S(1)} collective-permute-done((f32[8,128]{1,0:T(8,128)S(1)}, f32[8,128]{1,0:T(8,128)S(1)}, u32[]{:S(2)}, u32[]{:S(2)}) %collective-permute-start.11) | collective-permute-done | bytes 4128 | tf_op jit(solution)/shard_map/ppermute | solution.py:216
  39.4 0.6 shard_map.69
  40.0 0.1 collective-permute-start.12
  40.1 1.2 %collective-permute-done.12.y_ref = f32[64,128]{1,0:T(8,128)S(1)} collective-permute-done((f32[64,128]{1,0:T(8,128)S(1)}, f32[64,128]{1,0:T(8,128)S(1)}, u32[]{:S(2)}, u32[]{:S(2)}) %collective-permute-start.12) | collective-permute-done | bytes 32800 | tf_op jit(solution)/shard_map/ppermute | solution.py:216
  41.3 1.7 %collective-permute-start.13 = (f32[64,128]{1,0:T(8,128)S(1)}, f32[64,128]{1,0:T(8,128)S(1)}, u32[]{:S(2)}, u32[]{:S(2)}) collective-permute-start(f32[64,128]{1,0:T(8,128)S(1)} %shard_map.70.x_ref), channel_id=1, source_target_pairs={{0,8},{4,12},{8,0},{12,4},{16,24},{20,28},{24,16},{28,20},{1,9},{5... | collective-permute-start | bytes 98312 | tf_op jit(solution)/shard_map/ppermute | solution.py:216
  43.0 2.2 %collective-permute-done.13.y_ref = f32[64,128]{1,0:T(8,128)S(1)} collective-permute-done((f32[64,128]{1,0:T(8,128)S(1)}, f32[64,128]{1,0:T(8,128)S(1)}, u32[]{:S(2)}, u32[]{:S(2)}) %collective-permute-start.13) | collective-permute-done | bytes 32800 | tf_op jit(solution)/shard_map/ppermute | solution.py:216
  45.2 1.7 %collective-permute-start.14 = (f32[64,128]{1,0:T(8,128)S(1)}, f32[64,128]{1,0:T(8,128)S(1)}, u32[]{:S(2)}, u32[]{:S(2)}) collective-permute-start(f32[64,128]{1,0:T(8,128)S(1)} %shard_map.71.x_ref), channel_id=1, source_target_pairs={{0,16},{4,20},{8,24},{12,28},{16,0},{20,4},{24,8},{28,12},{1,17},{... | collective-permute-start | bytes 98312 | tf_op jit(solution)/shard_map/ppermute | solution.py:216
  46.9 2.2 %collective-permute-done.14.y_ref = f32[64,128]{1,0:T(8,128)S(1)} collective-permute-done((f32[64,128]{1,0:T(8,128)S(1)}, f32[64,128]{1,0:T(8,128)S(1)}, u32[]{:S(2)}, u32[]{:S(2)}) %collective-permute-start.14) | collective-permute-done | bytes 32800 | tf_op jit(solution)/shard_map/ppermute | solution.py:216
  49.1 1.1 collective-permute-start.15
  50.2 2.8 %collective-permute-done.15.y_ref = f32[64,128]{1,0:T(8,128)S(1)} collective-permute-done((f32[64,128]{1,0:T(8,128)S(1)}, f32[64,128]{1,0:T(8,128)S(1)}, u32[]{:S(2)}, u32[]{:S(2)}) %collective-permute-start.15) | collective-permute-done | bytes 32800 | tf_op jit(solution)/shard_map/ppermute | solution.py:216
  53.0 2.3 %collective-permute-start.16 = (f32[64,128]{1,0:T(8,128)S(1)}, f32[64,128]{1,0:T(8,128)S(1)}, u32[]{:S(2)}, u32[]{:S(2)}) collective-permute-start(f32[64,128]{1,0:T(8,128)S(1)} %shard_map.73.x_ref), channel_id=1, source_target_pairs={{0,2},{1,3},{2,0},{3,1},{4,6},{5,7},{6,4},{7,5},{8,10},{9,11},{10,... | collective-permute-start | bytes 98312 | tf_op jit(solution)/shard_map/ppermute | solution.py:216
  55.4 2.5 %collective-permute-done.16.y_ref = f32[64,128]{1,0:T(8,128)S(1)} collective-permute-done((f32[64,128]{1,0:T(8,128)S(1)}, f32[64,128]{1,0:T(8,128)S(1)}, u32[]{:S(2)}, u32[]{:S(2)}) %collective-permute-start.16) | collective-permute-done | bytes 32800 | tf_op jit(solution)/shard_map/ppermute | solution.py:216
  57.9 0.0 collective-permute-start.17
  57.9 1.2 %collective-permute-done.17.refs_13_ = f32[64,128]{1,0:T(8,128)S(1)} collective-permute-done((f32[64,128]{1,0:T(8,128)S(1)}, f32[64,128]{1,0:T(8,128)S(1)}, u32[]{:S(2)}, u32[]{:S(2)}) %collective-permute-start.17) | collective-permute-done | bytes 32800 | tf_op jit(solution)/shard_map/ppermute | solution.py:216
  59.1 6.0 %shard_map.75 = (f32[128,128]{1,0:T(8,128)}, bf16[1024,128]{1,0:T(8,128)(2,1)S(1)}, f32[8,128]{1,0:T(8,128)S(1)}) custom-call(bf16[256,128]{1,0:T(8,128)(2,1)S(1)} %copy-done, bf16[256,128]{1,0:T(8,128)(2,1)S(1)} %collective-permute-done.refs_1_, bf16[256,128]{1,0:T(8,128)(2,1)S(1)} %collective-permute-done.1.refs_2_, ...), custom_call_target="tpu_custom_call" | custom-call | flops 1073741824 | bytes 1740800 | tf_op jit(solution)/shard_map/pallas_call | solution.py:204
  65.1 1.1 collective-permute-start.18
  66.2 2.5 %collective-permute-done.18.y_ref = f32[8,128]{1,0:T(8,128)S(1)} collective-permute-done((f32[8,128]{1,0:T(8,128)S(1)}, f32[8,128]{1,0:T(8,128)S(1)}, u32[]{:S(2)}, u32[]{:S(2)}) %collective-permute-start.18) | collective-permute-done | bytes 4128 | tf_op jit(solution)/shard_map/ppermute | solution.py:216
  68.7 2.4 %collective-permute-start.19 = (f32[8,128]{1,0:T(8,128)S(1)}, f32[8,128]{1,0:T(8,128)S(1)}, u32[]{:S(2)}, u32[]{:S(2)}) collective-permute-start(f32[8,128]{1,0:T(8,128)S(1)} %shard_map.76.refs_9_), channel_id=1, source_target_pairs={{0,2},{1,3},{2,0},{3,1},{4,6},{5,7},{6,4},{7,5},{8,10},{9,11},{10,... | collective-permute-start | bytes 12296 | tf_op jit(solution)/shard_map/ppermute | solution.py:216
  71.1 2.2 %collective-permute-done.19.refs_10_ = f32[8,128]{1,0:T(8,128)S(1)} collective-permute-done((f32[8,128]{1,0:T(8,128)S(1)}, f32[8,128]{1,0:T(8,128)S(1)}, u32[]{:S(2)}, u32[]{:S(2)}) %collective-permute-start.19) | collective-permute-done | bytes 4128 | tf_op jit(solution)/shard_map/ppermute | solution.py:216
  73.3 4.8 %shard_map.77 = (f32[8,512]{1,0:T(8,128)S(1)}, f32[8,128]{1,0:T(8,128)}) custom-call(bf16[1024,128]{1,0:T(8,128)(2,1)S(1)} %get-tuple-element.23.refs_0_, bf16[528,128]{1,0:T(8,128)(2,1)S(1)} %fusion.1.refs_4_.refs_1_, bf16[528,128]{1,0:T(8,128)(2,1)S(1)} %collective-permute-done.3.refs_5_.refs_2_, ...), custom_call_target="tpu_custom_call" | custom-call | flops 1073741824 | bytes 1372160 | tf_op jit(solution)/shard_map/pallas_call | solution.py:204
  78.1 1.2 %collective-permute-done.20.y_ref = f32[8,512]{1,0:T(8,128)S(1)} collective-permute-done((f32[8,512]{1,0:T(8,128)S(1)}, f32[8,512]{1,0:T(8,128)S(1)}, u32[]{:S(2)}, u32[]{:S(2)}) %collective-permute-start.20) | collective-permute-done | bytes 16416 | tf_op jit(solution)/shard_map/ppermute | solution.py:216
  79.3 1.7 %collective-permute-start.21 = (f32[8,512]{1,0:T(8,128)S(1)}, f32[8,512]{1,0:T(8,128)S(1)}, u32[]{:S(2)}, u32[]{:S(2)}) collective-permute-start(f32[8,512]{1,0:T(8,128)S(1)} %shard_map.78.x_ref), channel_id=1, source_target_pairs={{0,8},{4,12},{8,0},{12,4},{16,24},{20,28},{24,16},{28,20},{1,9},{5... | collective-permute-start | bytes 49160 | tf_op jit(solution)/shard_map/ppermute | solution.py:216
  81.0 2.1 %collective-permute-done.21.y_ref = f32[8,512]{1,0:T(8,128)S(1)} collective-permute-done((f32[8,512]{1,0:T(8,128)S(1)}, f32[8,512]{1,0:T(8,128)S(1)}, u32[]{:S(2)}, u32[]{:S(2)}) %collective-permute-start.21) | collective-permute-done | bytes 16416 | tf_op jit(solution)/shard_map/ppermute | solution.py:216
  83.1 1.8 %collective-permute-start.22 = (f32[8,512]{1,0:T(8,128)S(1)}, f32[8,512]{1,0:T(8,128)S(1)}, u32[]{:S(2)}, u32[]{:S(2)}) collective-permute-start(f32[8,512]{1,0:T(8,128)S(1)} %shard_map.79.refs_9_), channel_id=1, source_target_pairs={{0,16},{4,20},{8,24},{12,28},{16,0},{20,4},{24,8},{28,12},{1,17},{... | collective-permute-start | bytes 49160 | tf_op jit(solution)/shard_map/ppermute | solution.py:216
  84.9 2.0 %collective-permute-done.22.refs_10_ = f32[8,512]{1,0:T(8,128)S(1)} collective-permute-done((f32[8,512]{1,0:T(8,128)S(1)}, f32[8,512]{1,0:T(8,128)S(1)}, u32[]{:S(2)}, u32[]{:S(2)}) %collective-permute-start.22) | collective-permute-done | bytes 16416 | tf_op jit(solution)/shard_map/ppermute | solution.py:216
  86.9 4.9 %shard_map.80.x_ref = f32[8,128]{1,0:T(8,128)S(1)} custom-call(bf16[1024,128]{1,0:T(8,128)(2,1)S(1)} %get-tuple-element.23.refs_0_, bf16[528,128]{1,0:T(8,128)(2,1)S(1)} %fusion.1.refs_4_.refs_1_, bf16[528,128]{1,0:T(8,128)(2,1)S(1)} %collective-permute-done.3.refs_5_.refs_2_, bf16[528,128]{1,0:T(8,128)(2,1)S(1)} %collective-permute-done.4.refs_6_.refs_3_, ...), custom_call_target="tpu_custom_call" | custom-call | flops 1073741824 | bytes 1380352 | tf_op jit(solution)/shard_map/pallas_call | solution.py:204
  91.9 1.2 %collective-permute-start.23 = (f32[8,128]{1,0:T(8,128)S(1)}, f32[8,128]{1,0:T(8,128)S(1)}, u32[]{:S(2)}, u32[]{:S(2)}) collective-permute-start(f32[8,128]{1,0:T(8,128)S(1)} %shard_map.80.x_ref), channel_id=1, source_target_pairs={{0,1},{1,0},{2,3},{3,2},{4,5},{5,4},{6,7},{7,6},{8,9},{9,8},{10,11... | collective-permute-start | bytes 12296 | tf_op jit(solution)/shard_map/ppermute | solution.py:216
  93.1 2.4 %collective-permute-done.23.y_ref = f32[8,128]{1,0:T(8,128)S(1)} collective-permute-done((f32[8,128]{1,0:T(8,128)S(1)}, f32[8,128]{1,0:T(8,128)S(1)}, u32[]{:S(2)}, u32[]{:S(2)}) %collective-permute-start.23) | collective-permute-done | bytes 4128 | tf_op jit(solution)/shard_map/ppermute | solution.py:216
  95.5 2.4 %collective-permute-start.24 = (f32[8,128]{1,0:T(8,128)S(1)}, f32[8,128]{1,0:T(8,128)S(1)}, u32[]{:S(2)}, u32[]{:S(2)}) collective-permute-start(f32[8,128]{1,0:T(8,128)S(1)} %shard_map.81.refs_9_), channel_id=1, source_target_pairs={{0,2},{1,3},{2,0},{3,1},{4,6},{5,7},{6,4},{7,5},{8,10},{9,11},{10,... | collective-permute-start | bytes 12296 | tf_op jit(solution)/shard_map/ppermute | solution.py:216
  97.9 2.2 %collective-permute-done.24.refs_10_ = f32[8,128]{1,0:T(8,128)S(1)} collective-permute-done((f32[8,128]{1,0:T(8,128)S(1)}, f32[8,128]{1,0:T(8,128)S(1)}, u32[]{:S(2)}, u32[]{:S(2)}) %collective-permute-start.24) | collective-permute-done | bytes 4128 | tf_op jit(solution)/shard_map/ppermute | solution.py:216
  100.1 5.0 %shard_map.82 = (f32[4,1,512]{2,1,0:T(1,128)S(1)}, f32[4,1,512]{2,1,0:T(1,128)S(1)}, f32[8,128]{1,0:T(8,128)}) custom-call(bf16[1024,128]{1,0:T(8,128)(2,1)S(1)} %get-tuple-element.23.refs_0_, bf16[528,128]{1,0:T(8,128)(2,1)S(1)} %fusion.1.refs_4_.refs_1_, bf16[528,128]{1,0:T(8,128)(2,1)S(1)} %collective-permute-done.3.refs_5_.refs_2_, ...), custom_call_target="tpu_custom_call" | custom-call | flops 1073741824 | bytes 1372160 | tf_op jit(solution)/shard_map/pallas_call | solution.py:204
  105.1 0.0 collective-permute-start.25
  105.1 1.2 %collective-permute-done.25.y_ref = f32[4,1,512]{2,1,0:T(1,128)S(1)} collective-permute-done((f32[4,1,512]{2,1,0:T(1,128)S(1)}, f32[4,1,512]{2,1,0:T(1,128)S(1)}, u32[]{:S(2)}, u32[]{:S(2)}) %collective-permute-start.25) | collective-permute-done | bytes 8224 | tf_op jit(solution)/shard_map/ppermute | solution.py:216
  106.3 1.7 %collective-permute-start.26 = (f32[2,1,512]{2,1,0:T(1,128)S(1)}, f32[2,1,512]{2,1,0:T(1,128)S(1)}, u32[]{:S(2)}, u32[]{:S(2)}) collective-permute-start(f32[2,1,512]{2,1,0:T(1,128)S(1)} %get-tuple-element.30), channel_id=1, source_target_pairs={{0,8},{4,12},{8,0},{12,4},{16,24},{20,28},{24,16},{28,20},{1,9},{5... | collective-permute-start | bytes 12296 | tf_op jit(solution)/shard_map/ppermute | solution.py:216
  108.0 1.9 %collective-permute-done.26.y_ref = f32[2,1,512]{2,1,0:T(1,128)S(1)} collective-permute-done((f32[2,1,512]{2,1,0:T(1,128)S(1)}, f32[2,1,512]{2,1,0:T(1,128)S(1)}, u32[]{:S(2)}, u32[]{:S(2)}) %collective-permute-start.26) | collective-permute-done | bytes 4128 | tf_op jit(solution)/shard_map/ppermute | solution.py:216
  110.0 1.8 %collective-permute-start.27 = (f32[1,1,512]{2,1,0:T(1,128)S(1)}, f32[1,1,512]{2,1,0:T(1,128)S(1)}, u32[]{:S(2)}, u32[]{:S(2)}) collective-permute-start(f32[1,1,512]{2,1,0:T(1,128)S(1)} %get-tuple-element.32), channel_id=1, source_target_pairs={{0,16},{4,20},{8,24},{12,28},{16,0},{20,4},{24,8},{28,12},{1,17},{... | collective-permute-start | bytes 6152 | tf_op jit(solution)/shard_map/ppermute | solution.py:216
  111.8 1.9 %collective-permute-done.27.y_ref = f32[1,1,512]{2,1,0:T(1,128)S(1)} collective-permute-done((f32[1,1,512]{2,1,0:T(1,128)S(1)}, f32[1,1,512]{2,1,0:T(1,128)S(1)}, u32[]{:S(2)}, u32[]{:S(2)}) %collective-permute-start.27) | collective-permute-done | bytes 2080 | tf_op jit(solution)/shard_map/ppermute | solution.py:216
  113.6 0.6 shard_map.85
  (18 shorter events, 0.2 us)
Async XLA Ops:
  0.6 0.7 copy-start.2
  1.3 5.6 %copy-start = (bf16[256,128]{1,0:T(8,128)(2,1)S(1)}, bf16[256,128]{1,0:T(8,128)(2,1)}, u32[]{:S(2)}) copy-start(bf16[256,128]{1,0:T(8,128)(2,1)} %refs_0_.5) | copy-start | bytes 196612
  1.3 22.8 %copy-start.1 = (f32[128,128]{1,0:T(8,128)S(1)}, f32[128,128]{1,0:T(8,128)}, u32[]{:S(2)}) copy-start(f32[128,128]{1,0:T(8,128)} %refs_12_.1) | copy-start | bytes 196612
  2.3 8.6 %collective-permute-start.8 = (bf16[528,128]{1,0:T(8,128)(2,1)S(1)}, bf16[528,128]{1,0:T(8,128)(2,1)S(1)}, u32[]{:S(2)}, u32[]{:S(2)}) collective-permute-start(bf16[528,128]{1,0:T(8,128)(2,1)S(1)} %fusion.1.refs_4_.refs_1_), channel_id=1, source_target_pairs={{0,24},{4,28},{8,16},{12,20},{16,8},{20,12},{24,0},{28,4},{1,25},{... | collective-permute-start | bytes 405512 | tf_op jit(solution)/shard_map/ppermute | solution.py:216
  6.2 6.5 %collective-permute-start.6 = (bf16[528,128]{1,0:T(8,128)(2,1)S(1)}, bf16[528,128]{1,0:T(8,128)(2,1)S(1)}, u32[]{:S(2)}, u32[]{:S(2)}) collective-permute-start(bf16[528,128]{1,0:T(8,128)(2,1)S(1)} %fusion.1.refs_4_.refs_1_), channel_id=1, source_target_pairs={{0,16},{4,20},{8,24},{12,28},{16,0},{20,4},{24,8},{28,12},{1,17},{... | collective-permute-start | bytes 405512 | tf_op jit(solution)/shard_map/ppermute | solution.py:216
  6.7 6.2 %collective-permute-start.4 = (bf16[528,128]{1,0:T(8,128)(2,1)S(1)}, bf16[528,128]{1,0:T(8,128)(2,1)S(1)}, u32[]{:S(2)}, u32[]{:S(2)}) collective-permute-start(bf16[528,128]{1,0:T(8,128)(2,1)S(1)} %fusion.1.refs_4_.refs_1_), channel_id=1, source_target_pairs={{0,8},{4,12},{8,0},{12,4},{16,24},{20,28},{24,16},{28,20},{1,9},{5... | collective-permute-start | bytes 405512 | tf_op jit(solution)/shard_map/ppermute | solution.py:216
  6.9 6.4 %collective-permute-start.2 = (bf16[256,128]{1,0:T(8,128)(2,1)S(1)}, bf16[256,128]{1,0:T(8,128)(2,1)S(1)}, u32[]{:S(2)}, u32[]{:S(2)}) collective-permute-start(bf16[256,128]{1,0:T(8,128)(2,1)S(1)} %copy-done), channel_id=1, source_target_pairs={{0,3},{1,2},{2,1},{3,0},{4,7},{5,6},{6,5},{7,4},{8,11},{9,10},{10,... | collective-permute-start | bytes 196616 | tf_op jit(solution)/shard_map/ppermute | solution.py:216
  10.9 13.2 %collective-permute-start.3 = (bf16[528,128]{1,0:T(8,128)(2,1)S(1)}, bf16[528,128]{1,0:T(8,128)(2,1)S(1)}, u32[]{:S(2)}, u32[]{:S(2)}) collective-permute-start(bf16[528,128]{1,0:T(8,128)(2,1)S(1)} %fusion.1.refs_4_.refs_1_), channel_id=1, source_target_pairs={{0,4},{4,0},{8,12},{12,8},{16,20},{20,16},{24,28},{28,24},{1,5},{5... | collective-permute-start | bytes 405512 | tf_op jit(solution)/shard_map/ppermute | solution.py:216
  10.9 13.2 %collective-permute-start.9 = (bf16[528,128]{1,0:T(8,128)(2,1)S(1)}, bf16[528,128]{1,0:T(8,128)(2,1)S(1)}, u32[]{:S(2)}, u32[]{:S(2)}) collective-permute-start(bf16[528,128]{1,0:T(8,128)(2,1)S(1)} %collective-permute-done.8.refs_10_.refs_7_), channel_id=1, source_target_pairs={{0,4},{4,0},{8,12},{12,8},{16,20},{20,16},{24,28},{28,24},{1,5},{5... | collective-permute-start | bytes 405512 | tf_op jit(solution)/shard_map/ppermute | solution.py:216
  12.7 11.4 %collective-permute-start.7 = (bf16[528,128]{1,0:T(8,128)(2,1)S(1)}, bf16[528,128]{1,0:T(8,128)(2,1)S(1)}, u32[]{:S(2)}, u32[]{:S(2)}) collective-permute-start(bf16[528,128]{1,0:T(8,128)(2,1)S(1)} %collective-permute-done.6.refs_8_.refs_5_), channel_id=1, source_target_pairs={{0,4},{4,0},{8,12},{12,8},{16,20},{20,16},{24,28},{28,24},{1,5},{5... | collective-permute-start | bytes 405512 | tf_op jit(solution)/shard_map/ppermute | solution.py:216
  13.0 11.1 %collective-permute-start.5 = (bf16[528,128]{1,0:T(8,128)(2,1)S(1)}, bf16[528,128]{1,0:T(8,128)(2,1)S(1)}, u32[]{:S(2)}, u32[]{:S(2)}) collective-permute-start(bf16[528,128]{1,0:T(8,128)(2,1)S(1)} %collective-permute-done.4.refs_6_.refs_3_), channel_id=1, source_target_pairs={{0,4},{4,0},{8,12},{12,8},{16,20},{20,16},{24,28},{28,24},{1,5},{5... | collective-permute-start | bytes 405512 | tf_op jit(solution)/shard_map/ppermute | solution.py:216
  13.2 6.6 %collective-permute-start.1 = (bf16[256,128]{1,0:T(8,128)(2,1)S(1)}, bf16[256,128]{1,0:T(8,128)(2,1)S(1)}, u32[]{:S(2)}, u32[]{:S(2)}) collective-permute-start(bf16[256,128]{1,0:T(8,128)(2,1)S(1)} %copy-done), channel_id=1, source_target_pairs={{0,2},{1,3},{2,0},{3,1},{4,6},{5,7},{6,4},{7,5},{8,10},{9,11},{10,... | collective-permute-start | bytes 196616 | tf_op jit(solution)/shard_map/ppermute | solution.py:216
  19.8 4.3 %collective-permute-start = (bf16[256,128]{1,0:T(8,128)(2,1)S(1)}, bf16[256,128]{1,0:T(8,128)(2,1)S(1)}, u32[]{:S(2)}, u32[]{:S(2)}) collective-permute-start(bf16[256,128]{1,0:T(8,128)(2,1)S(1)} %copy-done), channel_id=1, source_target_pairs={{0,1},{1,0},{2,3},{3,2},{4,5},{5,4},{6,7},{7,6},{8,9},{9,8},{10,11... | collective-permute-start | bytes 196616 | tf_op jit(solution)/shard_map/ppermute | solution.py:216
  31.2 3.7 %collective-permute-start.10 = (f32[8,128]{1,0:T(8,128)S(1)}, f32[8,128]{1,0:T(8,128)S(1)}, u32[]{:S(2)}, u32[]{:S(2)}) collective-permute-start(f32[8,128]{1,0:T(8,128)S(1)} %get-tuple-element.18.x_ref.refs_4_), channel_id=1, source_target_pairs={{0,1},{1,0},{2,3},{3,2},{4,5},{5,4},{6,7},{7,6},{8,9},{9,8},{10,11... | collective-permute-start | bytes 12296 | tf_op jit(solution)/shard_map/ppermute | solution.py:216
  34.8 4.6 %collective-permute-start.11 = (f32[8,128]{1,0:T(8,128)S(1)}, f32[8,128]{1,0:T(8,128)S(1)}, u32[]{:S(2)}, u32[]{:S(2)}) collective-permute-start(f32[8,128]{1,0:T(8,128)S(1)} %shard_map.68.refs_5_), channel_id=1, source_target_pairs={{0,2},{1,3},{2,0},{3,1},{4,6},{5,7},{6,4},{7,5},{8,10},{9,11},{10,... | collective-permute-start | bytes 12296 | tf_op jit(solution)/shard_map/ppermute | solution.py:216
  40.0 1.3 %collective-permute-start.12 = (f32[64,128]{1,0:T(8,128)S(1)}, f32[64,128]{1,0:T(8,128)S(1)}, u32[]{:S(2)}, u32[]{:S(2)}) collective-permute-start(f32[64,128]{1,0:T(8,128)S(1)} %get-tuple-element.21), channel_id=1, source_target_pairs={{0,4},{4,0},{8,12},{12,8},{16,20},{20,16},{24,28},{28,24},{1,5},{5... | collective-permute-start | bytes 98312 | tf_op jit(solution)/shard_map/ppermute | solution.py:216
  41.3 3.9 %collective-permute-start.13 = (f32[64,128]{1,0:T(8,128)S(1)}, f32[64,128]{1,0:T(8,128)S(1)}, u32[]{:S(2)}, u32[]{:S(2)}) collective-permute-start(f32[64,128]{1,0:T(8,128)S(1)} %shard_map.70.x_ref), channel_id=1, source_target_pairs={{0,8},{4,12},{8,0},{12,4},{16,24},{20,28},{24,16},{28,20},{1,9},{5... | collective-permute-start | bytes 98312 | tf_op jit(solution)/shard_map/ppermute | solution.py:216
  45.2 3.9 %collective-permute-start.14 = (f32[64,128]{1,0:T(8,128)S(1)}, f32[64,128]{1,0:T(8,128)S(1)}, u32[]{:S(2)}, u32[]{:S(2)}) collective-permute-start(f32[64,128]{1,0:T(8,128)S(1)} %shard_map.71.x_ref), channel_id=1, source_target_pairs={{0,16},{4,20},{8,24},{12,28},{16,0},{20,4},{24,8},{28,12},{1,17},{... | collective-permute-start | bytes 98312 | tf_op jit(solution)/shard_map/ppermute | solution.py:216
  49.1 3.9 %collective-permute-start.15 = (f32[64,128]{1,0:T(8,128)S(1)}, f32[64,128]{1,0:T(8,128)S(1)}, u32[]{:S(2)}, u32[]{:S(2)}) collective-permute-start(f32[64,128]{1,0:T(8,128)S(1)} %shard_map.72.x_ref), channel_id=1, source_target_pairs={{0,1},{1,0},{2,3},{3,2},{4,5},{5,4},{6,7},{7,6},{8,9},{9,8},{10,11... | collective-permute-start | bytes 98312 | tf_op jit(solution)/shard_map/ppermute | solution.py:216
  53.0 4.8 %collective-permute-start.16 = (f32[64,128]{1,0:T(8,128)S(1)}, f32[64,128]{1,0:T(8,128)S(1)}, u32[]{:S(2)}, u32[]{:S(2)}) collective-permute-start(f32[64,128]{1,0:T(8,128)S(1)} %shard_map.73.x_ref), channel_id=1, source_target_pairs={{0,2},{1,3},{2,0},{3,1},{4,6},{5,7},{6,4},{7,5},{8,10},{9,11},{10,... | collective-permute-start | bytes 98312 | tf_op jit(solution)/shard_map/ppermute | solution.py:216
  57.9 1.2 %collective-permute-start.17 = (f32[64,128]{1,0:T(8,128)S(1)}, f32[64,128]{1,0:T(8,128)S(1)}, u32[]{:S(2)}, u32[]{:S(2)}) collective-permute-start(f32[64,128]{1,0:T(8,128)S(1)} %shard_map.74.refs_12_), channel_id=1, source_target_pairs={{0,4},{4,0},{8,12},{12,8},{16,20},{20,16},{24,28},{28,24},{1,5},{5... | collective-permute-start | bytes 98312 | tf_op jit(solution)/shard_map/ppermute | solution.py:216
  65.1 3.6 %collective-permute-start.18 = (f32[8,128]{1,0:T(8,128)S(1)}, f32[8,128]{1,0:T(8,128)S(1)}, u32[]{:S(2)}, u32[]{:S(2)}) collective-permute-start(f32[8,128]{1,0:T(8,128)S(1)} %get-tuple-element.24.x_ref), channel_id=1, source_target_pairs={{0,1},{1,0},{2,3},{3,2},{4,5},{5,4},{6,7},{7,6},{8,9},{9,8},{10,11... | collective-permute-start | bytes 12296 | tf_op jit(solution)/shard_map/ppermute | solution.py:216
  68.7 4.6 %collective-permute-start.19 = (f32[8,128]{1,0:T(8,128)S(1)}, f32[8,128]{1,0:T(8,128)S(1)}, u32[]{:S(2)}, u32[]{:S(2)}) collective-permute-start(f32[8,128]{1,0:T(8,128)S(1)} %shard_map.76.refs_9_), channel_id=1, source_target_pairs={{0,2},{1,3},{2,0},{3,1},{4,6},{5,7},{6,4},{7,5},{8,10},{9,11},{10,... | collective-permute-start | bytes 12296 | tf_op jit(solution)/shard_map/ppermute | solution.py:216
  78.1 1.2 %collective-permute-start.20 = (f32[8,512]{1,0:T(8,128)S(1)}, f32[8,512]{1,0:T(8,128)S(1)}, u32[]{:S(2)}, u32[]{:S(2)}) collective-permute-start(f32[8,512]{1,0:T(8,128)S(1)} %get-tuple-element.25.x_ref), channel_id=1, source_target_pairs={{0,4},{4,0},{8,12},{12,8},{16,20},{20,16},{24,28},{28,24},{1,5},{5... | collective-permute-start | bytes 49160 | tf_op jit(solution)/shard_map/ppermute | solution.py:216
  79.3 3.8 %collective-permute-start.21 = (f32[8,512]{1,0:T(8,128)S(1)}, f32[8,512]{1,0:T(8,128)S(1)}, u32[]{:S(2)}, u32[]{:S(2)}) collective-permute-start(f32[8,512]{1,0:T(8,128)S(1)} %shard_map.78.x_ref), channel_id=1, source_target_pairs={{0,8},{4,12},{8,0},{12,4},{16,24},{20,28},{24,16},{28,20},{1,9},{5... | collective-permute-start | bytes 49160 | tf_op jit(solution)/shard_map/ppermute | solution.py:216
  83.1 3.8 %collective-permute-start.22 = (f32[8,512]{1,0:T(8,128)S(1)}, f32[8,512]{1,0:T(8,128)S(1)}, u32[]{:S(2)}, u32[]{:S(2)}) collective-permute-start(f32[8,512]{1,0:T(8,128)S(1)} %shard_map.79.refs_9_), channel_id=1, source_target_pairs={{0,16},{4,20},{8,24},{12,28},{16,0},{20,4},{24,8},{28,12},{1,17},{... | collective-permute-start | bytes 49160 | tf_op jit(solution)/shard_map/ppermute | solution.py:216
  91.9 3.6 %collective-permute-start.23 = (f32[8,128]{1,0:T(8,128)S(1)}, f32[8,128]{1,0:T(8,128)S(1)}, u32[]{:S(2)}, u32[]{:S(2)}) collective-permute-start(f32[8,128]{1,0:T(8,128)S(1)} %shard_map.80.x_ref), channel_id=1, source_target_pairs={{0,1},{1,0},{2,3},{3,2},{4,5},{5,4},{6,7},{7,6},{8,9},{9,8},{10,11... | collective-permute-start | bytes 12296 | tf_op jit(solution)/shard_map/ppermute | solution.py:216
  95.5 4.6 %collective-permute-start.24 = (f32[8,128]{1,0:T(8,128)S(1)}, f32[8,128]{1,0:T(8,128)S(1)}, u32[]{:S(2)}, u32[]{:S(2)}) collective-permute-start(f32[8,128]{1,0:T(8,128)S(1)} %shard_map.81.refs_9_), channel_id=1, source_target_pairs={{0,2},{1,3},{2,0},{3,1},{4,6},{5,7},{6,4},{7,5},{8,10},{9,11},{10,... | collective-permute-start | bytes 12296 | tf_op jit(solution)/shard_map/ppermute | solution.py:216
  105.1 1.2 %collective-permute-start.25 = (f32[4,1,512]{2,1,0:T(1,128)S(1)}, f32[4,1,512]{2,1,0:T(1,128)S(1)}, u32[]{:S(2)}, u32[]{:S(2)}) collective-permute-start(f32[4,1,512]{2,1,0:T(1,128)S(1)} %get-tuple-element.28), channel_id=1, source_target_pairs={{0,4},{4,0},{8,12},{12,8},{16,20},{20,16},{24,28},{28,24},{1,5},{5... | collective-permute-start | bytes 24584 | tf_op jit(solution)/shard_map/ppermute | solution.py:216
  106.3 3.7 %collective-permute-start.26 = (f32[2,1,512]{2,1,0:T(1,128)S(1)}, f32[2,1,512]{2,1,0:T(1,128)S(1)}, u32[]{:S(2)}, u32[]{:S(2)}) collective-permute-start(f32[2,1,512]{2,1,0:T(1,128)S(1)} %get-tuple-element.30), channel_id=1, source_target_pairs={{0,8},{4,12},{8,0},{12,4},{16,24},{20,28},{24,16},{28,20},{1,9},{5... | collective-permute-start | bytes 12296 | tf_op jit(solution)/shard_map/ppermute | solution.py:216
  110.0 3.7 %collective-permute-start.27 = (f32[1,1,512]{2,1,0:T(1,128)S(1)}, f32[1,1,512]{2,1,0:T(1,128)S(1)}, u32[]{:S(2)}, u32[]{:S(2)}) collective-permute-start(f32[1,1,512]{2,1,0:T(1,128)S(1)} %get-tuple-element.32), channel_id=1, source_target_pairs={{0,16},{4,20},{8,24},{12,28},{16,0},{20,4},{24,8},{28,12},{1,17},{... | collective-permute-start | bytes 6152 | tf_op jit(solution)/shard_map/ppermute | solution.py:216

commit v4 on v3

--- a/solution.py
+++ b/solution.py
@@ -43,9 +43,15 @@
     return jnp.broadcast_to(lanes, (LANES, LANES)).T
 
 
+def tree(op, parts):
+    while len(parts) > 1:
+        parts = [op(parts[i], parts[i + 1]) for i in range(0, len(parts), 2)]
+    return parts[0]
+
+
 def log_sum(parts):
     top = functools.reduce(jnp.maximum, parts)
-    return top + jnp.log(sum(jnp.exp(p - top) for p in parts))
+    return top + jnp.log(tree(jnp.add, [jnp.exp(p - top) for p in parts]))
 
 
 def potential_rows(block_ref, width):
@@ -98,13 +104,13 @@
 
 
 def moment_kernel(ns, rows_total, *refs):
-    s_refs, own_ref, l_refs, carried_ref = refs[:ns], refs[ns], refs[ns + 1 : ns + 3], refs[ns + 3]
-    keep_ref, send_ref, weight_ref, total_ref = refs[ns + 4 :]
-    c, r = lax.axis_index("col"), lax.axis_index("row")
+    s_refs, l_refs, carried_ref = refs[:ns], refs[ns : 2 * ns], refs[2 * ns]
+    out_ref, weight_ref = refs[2 * ns + 1 :]
+    c = lax.axis_index("col")
     piece = s_refs[0].shape[0]
     per = piece // LANES
     shift = log_sum([l[...] for l in l_refs])
-    weight_ref[...] = jnp.exp(own_ref[...] - shift) * (1.0 / rows_total)
+    weight_ref[...] = jnp.exp(l_refs[0][...] - shift) * (1.0 / rows_total)
     total = None
     for k in range(ns):
         for j in range(per):
@@ -115,27 +121,26 @@
             for part in reversed(split3(x)):
                 term = lax.dot_general(s, part, TN_DIMS, preferred_element_type=jnp.float32)
                 total = term if total is None else total + term
-    total_ref[...] = total
-    half = keep_ref.shape[0]
-    keep_ref[...] = total_ref[pl.ds(pl.multiple_of((r & 1) * half, half), half), :]
-    send_ref[...] = total_ref[pl.ds(pl.multiple_of((1 - (r & 1)) * half, half), half), :]
-
-
-def add_kernel(x_ref, y_ref, out_ref):
-    out_ref[...] = x_ref[...] + y_ref[...]
-
-
-def log_sum_kernel(x_ref, y_ref, out_ref):
-    out_ref[...] = log_sum([x_ref[...], y_ref[...]])
+    out_ref[...] = total
+
+
+def add_kernel(*refs):
+    refs[-1][...] = tree(jnp.add, [r[...] for r in refs[:-1]])
+
+
+def log_sum_kernel(*refs):
+    refs[-1][...] = log_sum([r[...] for r in refs[:-1]])
+
+
+def on_core(core, here, passed):
+    return jnp.where(lax.axis_index("row") % 2 == core, here, passed)
 
 
 def first_rows_kernel(ns, nt, width, *refs):
     s_refs, t_refs, m_refs = refs[:ns], refs[ns : ns + nt], refs[ns + nt : ns + nt + 2]
     moment_ref, a_ref, lse_ref, scores = refs[ns + nt + 2 :]
-    r = lax.axis_index("row")
-    piece, half = s_refs[0].shape[0], m_refs[0].shape[0]
-    for k in range(2):
-        moment_ref[pl.ds(pl.multiple_of((k ^ (r & 1)) * half, half), half), :] = m_refs[k][...]
+    piece = s_refs[0].shape[0]
+    moment_ref[...] = on_core(1, m_refs[0][...], m_refs[1][...])
     for k in range(ns):
         a_ref[k * piece : (k + 1) * piece, :] = project4(s_refs[k][...], moment_ref[...])
     column = [potential_rows(t, width) for t in t_refs]
@@ -146,14 +151,14 @@
     a_ref, t_refs, l_refs = refs[0], refs[1 : 1 + nt], refs[1 + nt : 3 + nt]
     lse_ref, column_ref, scores = refs[3 + nt :]
     r = lax.axis_index("row")
-    column_ref[...] = math.log(rows_total) - log_sum([l[...] for l in l_refs])
+    column_ref[...] = math.log(rows_total) - on_core(0, l_refs[0][...], l_refs[1][...])
     column = [column_ref[pl.ds(r ^ k, 1), :] for k in range(nt)]
     row_lse(a_ref, t_refs, column, scores, width, lse_ref)
 
 
 def columns_kernel(ns, nt, width, cols_total, last, *refs):
-    a_ref, t_refs, l_refs = refs[0], refs[1 : 1 + nt], refs[1 + nt : 3 + nt]
-    out_refs, (sp_ref, spread_rows, scores) = refs[3 + nt : -3], refs[-3:]
+    a_ref, t_refs, l_refs = refs[0], refs[1 : 1 + nt], refs[1 + nt : 1 + nt + ns]
+    out_ref, sp_ref, spread_rows, scores = refs[1 + nt + ns :]
     c, r = lax.axis_index("col"), lax.axis_index("row")
     rows = a_ref.shape[0]
     per = rows // ns // LANES
@@ -184,18 +189,20 @@
         if g > 0:
             lse = last_top + jnp.log(jnp.sum(mass, axis=0, keepdims=True))
             if last:
-                out_refs[(g - 1) % 2][(g - 1) // 2] = lse
+                out_ref[g - 1] = lse
             else:
-                out_refs[0][pl.ds(r ^ (g - 1), 1), :] = lse
-
-
-def halve_kernel(x_ref, y_ref, keep_ref, send_ref):
-    for k in range(x_ref.shape[0]):
-        (send_ref if k % 2 else keep_ref)[k // 2] = log_sum([x_ref[k], y_ref[k]])
+                out_ref[pl.ds(r ^ (g - 1), 1), :] = lse
+
+
+def pairs_kernel(x_ref, y_ref, *out_refs):
+    for k, out_ref in enumerate(out_refs):
+        for i in range(2):
+            g = 2 * k + (i if k == 0 else 1 - i)
+            out_ref[i] = log_sum([x_ref[g], y_ref[g ^ 1]])
 
 
 def update_kernel(rows_total, x_ref, y_ref, out_ref):
-    out_ref[...] = math.log(rows_total) - log_sum([x_ref[0], y_ref[0]])
+    out_ref[...] = math.log(rows_total) - on_core(0, x_ref[0], y_ref[1])
 
 
 def call(kernel, out, args, scratch=(), flops=0, exps=0):
@@ -220,22 +227,34 @@
     return [x] + [swap(x, axis, k) for k in range(1, lax.axis_size(axis))]
 
 
-def exchange_pairs(x, axis):
-    n = lax.axis_size(axis)
-    got = {0: x, 1: swap(x, axis, 1)}
-    for k in range(2, n, 2):
-        got[k] = swap(x, axis, k)
-    for k in range(2, n, 2):
-        got[k + 1] = swap(got[k], axis, 1)
-    return [got[k] for k in range(n)]
-
-
-def all_but_last(kernel, x, axis, first=1):
-    k, n = first, lax.axis_size(axis)
-    while 2 * k < n:
-        x, = call(kernel, [jax.ShapeDtypeStruct(x.shape, x.dtype)], [x, swap(x, axis, k)])
-        k *= 2
-    return [x, swap(x, axis, k)]
+def one_way(x, k, core):
+    return lax.ppermute(x, "row", [(i, i ^ k ^ 1) for i in range(lax.axis_size("row")) if i % 2 == core])
+
+
+def one_way_col(x, k, core):
+    n = lax.axis_size("col")
+    pairs = [
+        (i * n + j, (i ^ 1) * n + (j ^ k)) for i in range(lax.axis_size("row")) if i % 2 == core for j in range(n)
+    ]
+    return lax.ppermute(x, ("row", "col"), pairs)
+
+
+def combine(kernel, parts):
+    return call(kernel, [jax.ShapeDtypeStruct(parts[0].shape, parts[0].dtype)], parts)[0]
+
+
+def gather(block, piece):
+    ns, nt = lax.axis_size("col"), lax.axis_size("row")
+    blocks, pieces = {0: block}, {0: piece}
+    for k in range(2, nt, 2):
+        blocks[k] = swap(block, "row", k)
+    for k in range(1, ns):
+        pieces[k] = swap(piece, "col", k)
+    far = {**blocks, **{nt + k: pieces[k] for k in range(1, ns)}}
+    far = lax.optimization_barrier(far)
+    for k in range(0, nt, 2):
+        blocks[k + 1] = swap(far[k], "row", 1)
+    return [blocks[k] for k in range(nt)], [pieces[k] for k in range(ns)]
 
 
 def per_device(source, target, target_potential, prev_moment):
@@ -247,8 +266,7 @@
     rows_total, cols_total = rows * nt, cols * ns
     groups = width // LANES
     tail = jnp.pad(target_potential.reshape(groups, LANES), ((0, 16 - groups), (0, 0)))
-    t_blocks = exchange_pairs(jnp.concatenate([target, tail], axis=0), "row")
-    s_pieces = exchange(source, "col")
+    t_blocks, s_pieces = gather(jnp.concatenate([target, tail], axis=0), source)
     tile = shape((rows // LANES, LANES), f32)
     flops, exps = 2 * rows * cols * depth, rows * cols
     row_scores = pltpu.VMEM((2, LANES, cols), f32)
@@ -261,21 +279,20 @@
         2 * flops,
         exps,
     )
-    half = shape((depth // 2, depth), f32)
-    keep, send = call(
+    part, = call(
         functools.partial(moment_kernel, ns, rows_total),
-        [half, half],
-        s_pieces + [lse] + all_but_last(log_sum_kernel, lse, "col") + [carried],
-        [pltpu.VMEM(tile.shape, f32), pltpu.VMEM((depth, depth), f32)],
+        [shape((depth, depth), f32)],
+        s_pieces + exchange(lse, "col") + [carried],
+        [pltpu.VMEM(tile.shape, f32)],
         6 * rows * depth * depth,
     )
-    part, = call(add_kernel, [half], [keep, swap(send, "row", 1)])
-    part, = call(add_kernel, [half], all_but_last(add_kernel, part, "row", 2))
-    part, = call(add_kernel, [half], all_but_last(add_kernel, part, "col"))
+    part = combine(add_kernel, [part, swap(part, "row", 1)])
+    part = combine(add_kernel, [part] + [one_way(part, k, 1) for k in range(2, nt, 2)])
+    part = combine(add_kernel, [one_way_col(part, k, 0) for k in range(ns)])
     moment, a, lse = call(
         functools.partial(first_rows_kernel, ns, nt, width),
         [shape((depth, depth), f32), shape((rows, depth), jnp.bfloat16), tile],
-        s_pieces + t_blocks + [part, swap(part, "row", 1)],
+        s_pieces + t_blocks + [part, one_way(part, 0, 1)],
         [row_scores],
         flops,
         exps,
@@ -283,32 +300,29 @@
     for iteration in range(ITERS):
         last = iteration == ITERS - 1
         if iteration > 0:
+            both = combine(log_sum_kernel, [column_lse, swap(column_lse, "row", 1)])
+            here = combine(log_sum_kernel, [both] + [one_way(both, k, 1) for k in range(2, nt, 2)])
             lse, = call(
                 functools.partial(rows_kernel, nt, width, rows_total),
                 [tile],
-                [a] + t_blocks + all_but_last(log_sum_kernel, column_lse, "row"),
+                [a] + t_blocks + [here, one_way(here, 0, 0)],
                 [pltpu.VMEM((nt, width), f32), row_scores],
                 flops,
                 exps,
             )
-        blocks = shape((nt // 2, 1, width), f32)
-        *outs, source_potential = call(
+        column_lse, source_potential = call(
             functools.partial(columns_kernel, ns, nt, width, cols_total, last),
-            ([blocks, blocks] if last else [shape((nt, width), f32)]) + [tile],
-            [a] + t_blocks + all_but_last(log_sum_kernel, lse, "col"),
+            [shape((nt, 1, width) if last else (nt, width), f32), tile],
+            [a] + t_blocks + exchange(lse, "col"),
             [pltpu.VMEM((rows, LANES), f32), pltpu.VMEM((2, rows, width), f32)],
             flops,
             exps,
         )
-        column_lse = outs[0]
-    keep, send = outs
-    k = 1
-    while keep.shape[0] > 1:
-        blocks = shape((keep.shape[0] // 2, 1, width), f32)
-        keep, send = call(halve_kernel, [blocks, blocks], [keep, swap(send, "row", k)])
-        k *= 2
+    pair = shape((2, 1, width), f32)
+    own, *sent = call(pairs_kernel, [pair] * (nt // 2), [column_lse, swap(column_lse, "row", 1)])
+    here = combine(log_sum_kernel, [own] + [one_way(x, 2 * k + 2, 1) for k, x in enumerate(sent)])
     update, = call(
-        functools.partial(update_kernel, rows_total), [shape((1, width), f32)], [keep, swap(send, "row", k)]
+        functools.partial(update_kernel, rows_total), [shape((1, width), f32)], [here, one_way(here, 0, 0)]
     )
     return moment, source_potential.reshape(rows), update.reshape(width)
 

time: 114 us -> 114 us (level)
  starting transfers between devices: 36.7 us -> 47 us
  waiting for transfers between devices: 46 us -> 35.9 us
    ppermute x28 -> x22, waiting for transfers between devices: 46 us -> 18.4 us  [swap(): lax.ppermute(x, axis, [(i, i ^ k) for i in range(lax.axis_size(axis))])]
    ppermute x0 -> x16, starting transfers between devices: none -> 22.5 us  [the longest x12 15.9 us: one_way(): lax.ppermute(x, 'row', [(i, i ^ k ^ 1) for i in range(lax.axis_size('row'...]
    ppermute x0 -> x16, waiting for transfers between devices: none -> 17.5 us  [the longest x12 16.6 us: one_way(): lax.ppermute(x, 'row', [(i, i ^ k ^ 1) for i in range(lax.axis_size('row'...]
    ppermute x28 -> x22, starting transfers between devices: 36.7 us -> 24.5 us  [swap(): lax.ppermute(x, axis, [(i, i ^ k) for i in range(lax.axis_size(axis))])]
    pallas_call x19 -> x14, Pallas kernels: 29.1 us -> 28.5 us  [call(): pl.pallas_call(kernel, out_shape=list(out), in_specs=[vmem] * len(args),...]
  transfers between devices with their start and end apart: 28 -> 38, of which waited for: 22 -> 31; matrix products, arithmetic and copies ran while one was open for 0% -> 0% of each run, Pallas kernels for 0% -> 0%
where the time goes in v4:
time: 114 us
  starting transfers between devices  47 us (41%)
  waiting for transfers between devices  35.9 us (31%)
  Pallas kernels  28.5 us (25%)
    pallas_call x14, Pallas kernels, call(): pl.pallas_call(kernel, out_shape=list(out), in_specs=[vmem] * len(args),...  28.5 us
    ppermute x22, starting transfers between devices, swap(): lax.ppermute(x, axis, [(i, i ^ k) for i in range(lax.axis_size(axis))])  24.5 us
    ppermute x22, waiting for transfers between devices, swap(): lax.ppermute(x, axis, [(i, i ^ k) for i in range(lax.axis_size(axis))])  18.4 us
    ppermute x12, waiting for transfers between devices, one_way(): lax.ppermute(x, 'row', [(i, i ^ k ^ 1) for i in range(lax.axis_size('row'...  16.6 us
    ppermute x12, starting transfers between devices, one_way(): lax.ppermute(x, 'row', [(i, i ^ k ^ 1) for i in range(lax.axis_size('row'...  15.9 us
    ppermute x4, starting transfers between devices, one_way_col(): return lax.ppermute(x, ('row', 'col'), pairs)  6.64 us
  transfers between devices with their start and end apart: 38, of which 31 were waited for; matrix products, arithmetic and copies ran while one was open for 0% of the time, Pallas kernels for 0%

profile of v4, /device:TPU:0, one launch (start us, length us, event | category | flops | bytes accessed | tf_op | source)
XLA Modules:
  0.0 113.9 jit_solution(14301224233369331466)
XLA Ops:
  0.6 0.7 copy-done.2
  1.3 0.9 fusion.1.refs_4_.refs_1_
  2.3 4.0 %collective-permute-start.5 = (bf16[528,128]{1,0:T(8,128)(2,1)S(1)}, bf16[528,128]{1,0:T(8,128)(2,1)S(1)}, u32[]{:S(2)}, u32[]{:S(2)}) collective-permute-start(bf16[528,128]{1,0:T(8,128)(2,1)S(1)} %fusion.1.refs_4_.refs_1_), channel_id=1, source_target_pairs={{0,24},{4,28},{8,16},{12,20},{16,8},{20,12},{24,0},{28,4},{1,25},{... | collective-permute-start | bytes 405512 | tf_op jit(solution)/shard_map/ppermute | solution.py:223
  6.2 0.5 collective-permute-start.4
  6.9 4.0 %collective-permute-start.2 = (bf16[256,128]{1,0:T(8,128)(2,1)S(1)}, bf16[256,128]{1,0:T(8,128)(2,1)S(1)}, u32[]{:S(2)}, u32[]{:S(2)}) collective-permute-start(bf16[256,128]{1,0:T(8,128)(2,1)S(1)} %copy-done), channel_id=1, source_target_pairs={{0,3},{1,2},{2,1},{3,0},{4,7},{5,6},{6,5},{7,4},{8,11},{9,10},{10,... | collective-permute-start | bytes 196616 | tf_op jit(solution)/shard_map/ppermute | solution.py:223
  10.9 2.7 %collective-permute-done.2.refs_3_ = bf16[256,128]{1,0:T(8,128)(2,1)S(1)} collective-permute-done((bf16[256,128]{1,0:T(8,128)(2,1)S(1)}, bf16[256,128]{1,0:T(8,128)(2,1)S(1)}, u32[]{:S(2)}, u32[]{:S(2)}) %collective-permute-start.2) | collective-permute-done | bytes 65568 | tf_op jit(solution)/shard_map/ppermute | solution.py:223
  13.6 1.3 %collective-permute-start = (bf16[256,128]{1,0:T(8,128)(2,1)S(1)}, bf16[256,128]{1,0:T(8,128)(2,1)S(1)}, u32[]{:S(2)}, u32[]{:S(2)}) collective-permute-start(bf16[256,128]{1,0:T(8,128)(2,1)S(1)} %copy-done), channel_id=1, source_target_pairs={{0,1},{1,0},{2,3},{3,2},{4,5},{5,4},{6,7},{7,6},{8,9},{9,8},{10,11... | collective-permute-start | bytes 196616 | tf_op jit(solution)/shard_map/ppermute | solution.py:223
  14.9 1.2 %collective-permute-done.1.refs_2_ = bf16[256,128]{1,0:T(8,128)(2,1)S(1)} collective-permute-done((bf16[256,128]{1,0:T(8,128)(2,1)S(1)}, bf16[256,128]{1,0:T(8,128)(2,1)S(1)}, u32[]{:S(2)}, u32[]{:S(2)}) %collective-permute-start.1) | collective-permute-done | bytes 65568 | tf_op jit(solution)/shard_map/ppermute | solution.py:223
  16.1 1.8 %collective-permute-done.refs_1_ = bf16[256,128]{1,0:T(8,128)(2,1)S(1)} collective-permute-done((bf16[256,128]{1,0:T(8,128)(2,1)S(1)}, bf16[256,128]{1,0:T(8,128)(2,1)S(1)}, u32[]{:S(2)}, u32[]{:S(2)}) %collective-permute-start) | collective-permute-done | bytes 65568 | tf_op jit(solution)/shard_map/ppermute | solution.py:223
  17.9 0.5 collective-permute-start.7
  18.5 0.4 collective-permute-start.9
  20.0 7.0 %shard_map.67 = (f32[8,128]{1,0:T(8,128)S(1)}, f32[1024,128]{1,0:T(8,128)S(1)}) custom-call(bf16[256,128]{1,0:T(8,128)(2,1)S(1)} %copy-done, bf16[256,128]{1,0:T(8,128)(2,1)S(1)} %collective-permute-done.refs_1_, bf16[256,128]{1,0:T(8,128)(2,1)S(1)} %collective-permute-done.1.refs_2_, bf16[256,128]{1,0:T(8,128)(2,1)S(1)} %collective-permute-done.2.refs_3_, ...), custom_call_target="tpu_custom_call" | custom-call | flops 2147483648 | bytes 1937408 | tf_op jit(solution)/shard_map/pallas_call | solution.py:211
  27.0 3.9 %collective-permute-start.12 = (f32[8,128]{1,0:T(8,128)S(1)}, f32[8,128]{1,0:T(8,128)S(1)}, u32[]{:S(2)}, u32[]{:S(2)}) collective-permute-start(f32[8,128]{1,0:T(8,128)S(1)} %get-tuple-element.23.refs_4_), channel_id=1, source_target_pairs={{0,3},{1,2},{2,1},{3,0},{4,7},{5,6},{6,5},{7,4},{8,11},{9,10},{10,... | collective-permute-start | bytes 12296 | tf_op jit(solution)/shard_map/ppermute | solution.py:223
  30.9 0.6 collective-permute-start.10
  31.5 0.9 collective-permute-done.12.refs_7_
  32.5 2.9 %collective-permute-done.11.refs_6_ = f32[8,128]{1,0:T(8,128)S(1)} collective-permute-done((f32[8,128]{1,0:T(8,128)S(1)}, f32[8,128]{1,0:T(8,128)S(1)}, u32[]{:S(2)}, u32[]{:S(2)}) %collective-permute-start.11) | collective-permute-done | bytes 4128 | tf_op jit(solution)/shard_map/ppermute | solution.py:223
  35.4 0.5 shard_map.68.refs_0_
  36.0 1.2 %collective-permute-done.13.refs_1_ = f32[128,128]{1,0:T(8,128)S(1)} collective-permute-done((f32[128,128]{1,0:T(8,128)S(1)}, f32[128,128]{1,0:T(8,128)S(1)}, u32[]{:S(2)}, u32[]{:S(2)}) %collective-permute-start.13) | collective-permute-done | bytes 65568 | tf_op jit(solution)/shard_map/ppermute | solution.py:223
  37.3 1.3 %collective-permute-start.16 = (f32[128,128]{1,0:T(8,128)S(1)}, f32[128,128]{1,0:T(8,128)S(1)}, u32[]{:S(2)}, u32[]{:S(2)}) collective-permute-start(f32[128,128]{1,0:T(8,128)S(1)} %shard_map.69.refs_0_), channel_id=1, source_target_pairs={{4,24},{12,16},{20,8},{28,0},{5,25},{13,17},{21,9},{29,1},{6,26},{... | collective-permute-start | bytes 196616 | tf_op jit(solution)/shard_map/ppermute | solution.py:231
  38.6 1.3 %collective-permute-start.15 = (f32[128,128]{1,0:T(8,128)S(1)}, f32[128,128]{1,0:T(8,128)S(1)}, u32[]{:S(2)}, u32[]{:S(2)}) collective-permute-start(f32[128,128]{1,0:T(8,128)S(1)} %shard_map.69.refs_0_), channel_id=1, source_target_pairs={{4,16},{12,24},{20,0},{28,8},{5,17},{13,25},{21,1},{29,9},{6,18},{... | collective-permute-start | bytes 196616 | tf_op jit(solution)/shard_map/ppermute | solution.py:231
  39.9 1.3 %collective-permute-start.14 = (f32[128,128]{1,0:T(8,128)S(1)}, f32[128,128]{1,0:T(8,128)S(1)}, u32[]{:S(2)}, u32[]{:S(2)}) collective-permute-start(f32[128,128]{1,0:T(8,128)S(1)} %shard_map.69.refs_0_), channel_id=1, source_target_pairs={{4,8},{12,0},{20,24},{28,16},{5,9},{13,1},{21,25},{29,17},{6,10},{... | collective-permute-start | bytes 196616 | tf_op jit(solution)/shard_map/ppermute | solution.py:231
  41.2 2.6 %collective-permute-done.16.refs_3_ = f32[128,128]{1,0:T(8,128)S(1)} collective-permute-done((f32[128,128]{1,0:T(8,128)S(1)}, f32[128,128]{1,0:T(8,128)S(1)}, u32[]{:S(2)}, u32[]{:S(2)}) %collective-permute-start.16) | collective-permute-done | bytes 65568 | tf_op jit(solution)/shard_map/ppermute | solution.py:231
  43.8 1.3 %collective-permute-done.15.refs_2_ = f32[128,128]{1,0:T(8,128)S(1)} collective-permute-done((f32[128,128]{1,0:T(8,128)S(1)}, f32[128,128]{1,0:T(8,128)S(1)}, u32[]{:S(2)}, u32[]{:S(2)}) %collective-permute-start.15) | collective-permute-done | bytes 65568 | tf_op jit(solution)/shard_map/ppermute | solution.py:231
  45.1 1.4 %collective-permute-done.14.refs_1_ = f32[128,128]{1,0:T(8,128)S(1)} collective-permute-done((f32[128,128]{1,0:T(8,128)S(1)}, f32[128,128]{1,0:T(8,128)S(1)}, u32[]{:S(2)}, u32[]{:S(2)}) %collective-permute-start.14) | collective-permute-done | bytes 65568 | tf_op jit(solution)/shard_map/ppermute | solution.py:231
  46.5 2.2 %collective-permute-start.20 = (f32[128,128]{1,0:T(8,128)S(1)}, f32[128,128]{1,0:T(8,128)S(1)}, u32[]{:S(2)}, u32[]{:S(2)}) collective-permute-start(f32[128,128]{1,0:T(8,128)S(1)} %shard_map.70), channel_id=1, source_target_pairs={{0,7},{1,6},{2,5},{3,4},{8,15},{9,14},{10,13},{11,12},{16,23},{17,... | collective-permute-start | bytes 196616 | tf_op jit(solution)/shard_map/ppermute | solution.py:239
  48.7 1.9 %collective-permute-start.19 = (f32[128,128]{1,0:T(8,128)S(1)}, f32[128,128]{1,0:T(8,128)S(1)}, u32[]{:S(2)}, u32[]{:S(2)}) collective-permute-start(f32[128,128]{1,0:T(8,128)S(1)} %shard_map.70), channel_id=1, source_target_pairs={{0,6},{1,7},{2,4},{3,5},{8,14},{9,15},{10,12},{11,13},{16,22},{17,... | collective-permute-start | bytes 196616 | tf_op jit(solution)/shard_map/ppermute | solution.py:239
  50.5 1.3 %collective-permute-start.18 = (f32[128,128]{1,0:T(8,128)S(1)}, f32[128,128]{1,0:T(8,128)S(1)}, u32[]{:S(2)}, u32[]{:S(2)}) collective-permute-start(f32[128,128]{1,0:T(8,128)S(1)} %shard_map.70), channel_id=1, source_target_pairs={{0,5},{1,4},{2,7},{3,6},{8,13},{9,12},{10,15},{11,14},{16,21},{17,... | collective-permute-start | bytes 196616 | tf_op jit(solution)/shard_map/ppermute | solution.py:239
  51.8 1.3 %collective-permute-start.17 = (f32[128,128]{1,0:T(8,128)S(1)}, f32[128,128]{1,0:T(8,128)S(1)}, u32[]{:S(2)}, u32[]{:S(2)}) collective-permute-start(f32[128,128]{1,0:T(8,128)S(1)} %shard_map.70), channel_id=1, source_target_pairs={{0,4},{1,5},{2,6},{3,7},{8,12},{9,13},{10,14},{11,15},{16,20},{17,... | collective-permute-start | bytes 196616 | tf_op jit(solution)/shard_map/ppermute | solution.py:239
  53.2 0.6 collective-permute-done.18.refs_1_
  54.0 1.5 %collective-permute-start.21 = (f32[128,128]{1,0:T(8,128)S(1)}, f32[128,128]{1,0:T(8,128)S(1)}, u32[]{:S(2)}, u32[]{:S(2)}) collective-permute-start(f32[128,128]{1,0:T(8,128)S(1)} %shard_map.71.refs_12_), channel_id=1, source_target_pairs={{4,0},{12,8},{20,16},{28,24},{5,1},{13,9},{21,17},{29,25},{6,2},{1... | collective-permute-start | bytes 196616 | tf_op jit(solution)/shard_map/ppermute | solution.py:231
  55.5 1.7 %collective-permute-done.21.refs_13_ = f32[128,128]{1,0:T(8,128)S(1)} collective-permute-done((f32[128,128]{1,0:T(8,128)S(1)}, f32[128,128]{1,0:T(8,128)S(1)}, u32[]{:S(2)}, u32[]{:S(2)}) %collective-permute-start.21) | collective-permute-done | bytes 65568 | tf_op jit(solution)/shard_map/ppermute | solution.py:231
  57.2 5.8 %shard_map.72 = (f32[128,128]{1,0:T(8,128)}, bf16[1024,128]{1,0:T(8,128)(2,1)S(1)}, f32[8,128]{1,0:T(8,128)S(1)}) custom-call(bf16[256,128]{1,0:T(8,128)(2,1)S(1)} %copy-done, bf16[256,128]{1,0:T(8,128)(2,1)S(1)} %collective-permute-done.refs_1_, bf16[256,128]{1,0:T(8,128)(2,1)S(1)} %collective-permute-done.1.refs_2_, ...), custom_call_target="tpu_custom_call" | custom-call | flops 1073741824 | bytes 1806336 | tf_op jit(solution)/shard_map/pallas_call | solution.py:211
  63.0 1.8 %collective-permute-start.24 = (f32[8,128]{1,0:T(8,128)S(1)}, f32[8,128]{1,0:T(8,128)S(1)}, u32[]{:S(2)}, u32[]{:S(2)}) collective-permute-start(f32[8,128]{1,0:T(8,128)S(1)} %get-tuple-element.27.refs_9_), channel_id=1, source_target_pairs={{0,3},{1,2},{2,1},{3,0},{4,7},{5,6},{6,5},{7,4},{8,11},{9,10},{10,... | collective-permute-start | bytes 12296 | tf_op jit(solution)/shard_map/ppermute | solution.py:223
  64.8 0.4 collective-permute-start.23
  65.2 2.2 %collective-permute-start.22 = (f32[8,128]{1,0:T(8,128)S(1)}, f32[8,128]{1,0:T(8,128)S(1)}, u32[]{:S(2)}, u32[]{:S(2)}) collective-permute-start(f32[8,128]{1,0:T(8,128)S(1)} %get-tuple-element.27.refs_9_), channel_id=1, source_target_pairs={{0,1},{1,0},{2,3},{3,2},{4,5},{5,4},{6,7},{7,6},{8,9},{9,8},{10,11... | collective-permute-start | bytes 12296 | tf_op jit(solution)/shard_map/ppermute | solution.py:223
  67.4 1.0 collective-permute-done.24.refs_12_
  68.4 0.9 collective-permute-done.23.refs_11_
  69.3 4.8 %shard_map.73 = (f32[8,512]{1,0:T(8,128)S(1)}, f32[8,128]{1,0:T(8,128)}) custom-call(bf16[1024,128]{1,0:T(8,128)(2,1)S(1)} %get-tuple-element.26.refs_0_, bf16[528,128]{1,0:T(8,128)(2,1)S(1)} %fusion.1.refs_4_.refs_1_, bf16[528,128]{1,0:T(8,128)(2,1)S(1)} %collective-permute-done.6.refs_5_.refs_2_, ...), custom_call_target="tpu_custom_call" | custom-call | flops 1073741824 | bytes 1380352 | tf_op jit(solution)/shard_map/pallas_call | solution.py:211
  74.1 1.2 %collective-permute-done.25.refs_1_ = f32[8,512]{1,0:T(8,128)S(1)} collective-permute-done((f32[8,512]{1,0:T(8,128)S(1)}, f32[8,512]{1,0:T(8,128)S(1)}, u32[]{:S(2)}, u32[]{:S(2)}) %collective-permute-start.25) | collective-permute-done | bytes 16416 | tf_op jit(solution)/shard_map/ppermute | solution.py:223
  75.3 1.3 %collective-permute-start.28 = (f32[8,512]{1,0:T(8,128)S(1)}, f32[8,512]{1,0:T(8,128)S(1)}, u32[]{:S(2)}, u32[]{:S(2)}) collective-permute-start(f32[8,512]{1,0:T(8,128)S(1)} %shard_map.74.refs_0_), channel_id=1, source_target_pairs={{4,24},{12,16},{20,8},{28,0},{5,25},{13,17},{21,9},{29,1},{6,26},{... | collective-permute-start | bytes 49160 | tf_op jit(solution)/shard_map/ppermute | solution.py:231
  76.6 1.3 %collective-permute-start.27 = (f32[8,512]{1,0:T(8,128)S(1)}, f32[8,512]{1,0:T(8,128)S(1)}, u32[]{:S(2)}, u32[]{:S(2)}) collective-permute-start(f32[8,512]{1,0:T(8,128)S(1)} %shard_map.74.refs_0_), channel_id=1, source_target_pairs={{4,16},{12,24},{20,0},{28,8},{5,17},{13,25},{21,1},{29,9},{6,18},{... | collective-permute-start | bytes 49160 | tf_op jit(solution)/shard_map/ppermute | solution.py:231
  77.9 1.3 %collective-permute-start.26 = (f32[8,512]{1,0:T(8,128)S(1)}, f32[8,512]{1,0:T(8,128)S(1)}, u32[]{:S(2)}, u32[]{:S(2)}) collective-permute-start(f32[8,512]{1,0:T(8,128)S(1)} %shard_map.74.refs_0_), channel_id=1, source_target_pairs={{4,8},{12,0},{20,24},{28,16},{5,9},{13,1},{21,25},{29,17},{6,10},{... | collective-permute-start | bytes 49160 | tf_op jit(solution)/shard_map/ppermute | solution.py:231
  79.2 2.1 %collective-permute-done.28.refs_3_ = f32[8,512]{1,0:T(8,128)S(1)} collective-permute-done((f32[8,512]{1,0:T(8,128)S(1)}, f32[8,512]{1,0:T(8,128)S(1)}, u32[]{:S(2)}, u32[]{:S(2)}) %collective-permute-start.28) | collective-permute-done | bytes 16416 | tf_op jit(solution)/shard_map/ppermute | solution.py:231
  81.2 0.4 collective-permute-done.27.refs_2_
  81.6 1.3 %collective-permute-done.26.refs_1_ = f32[8,512]{1,0:T(8,128)S(1)} collective-permute-done((f32[8,512]{1,0:T(8,128)S(1)}, f32[8,512]{1,0:T(8,128)S(1)}, u32[]{:S(2)}, u32[]{:S(2)}) %collective-permute-start.26) | collective-permute-done | bytes 16416 | tf_op jit(solution)/shard_map/ppermute | solution.py:231
  83.0 1.5 %collective-permute-start.29 = (f32[8,512]{1,0:T(8,128)S(1)}, f32[8,512]{1,0:T(8,128)S(1)}, u32[]{:S(2)}, u32[]{:S(2)}) collective-permute-start(f32[8,512]{1,0:T(8,128)S(1)} %shard_map.75.refs_9_), channel_id=1, source_target_pairs={{0,4},{8,12},{16,20},{24,28},{1,5},{9,13},{17,21},{25,29},{2,6},{1... | collective-permute-start | bytes 49160 | tf_op jit(solution)/shard_map/ppermute | solution.py:231
  84.5 0.6 collective-permute-done.29.refs_10_
  85.1 4.9 %shard_map.76.refs_9_ = f32[8,128]{1,0:T(8,128)S(1)} custom-call(bf16[1024,128]{1,0:T(8,128)(2,1)S(1)} %get-tuple-element.26.refs_0_, bf16[528,128]{1,0:T(8,128)(2,1)S(1)} %fusion.1.refs_4_.refs_1_, bf16[528,128]{1,0:T(8,128)(2,1)S(1)} %collective-permute-done.6.refs_5_.refs_2_, bf16[528,128]{1,0:T(8,128)(2,1)S(1)} %collective-permute-done.3.refs_6_.refs_3_, ...), custom_call_target="tpu_custom_call" | custom-call | flops 1073741824 | bytes 1380352 | tf_op jit(solution)/shard_map/pallas_call | solution.py:211
  90.0 2.0 %collective-permute-start.32 = (f32[8,128]{1,0:T(8,128)S(1)}, f32[8,128]{1,0:T(8,128)S(1)}, u32[]{:S(2)}, u32[]{:S(2)}) collective-permute-start(f32[8,128]{1,0:T(8,128)S(1)} %shard_map.76.refs_9_), channel_id=1, source_target_pairs={{0,3},{1,2},{2,1},{3,0},{4,7},{5,6},{6,5},{7,4},{8,11},{9,10},{10,... | collective-permute-start | bytes 12296 | tf_op jit(solution)/shard_map/ppermute | solution.py:223
  92.1 1.1 collective-permute-start.31
  93.2 1.2 %collective-permute-start.30 = (f32[8,128]{1,0:T(8,128)S(1)}, f32[8,128]{1,0:T(8,128)S(1)}, u32[]{:S(2)}, u32[]{:S(2)}) collective-permute-start(f32[8,128]{1,0:T(8,128)S(1)} %shard_map.76.refs_9_), channel_id=1, source_target_pairs={{0,1},{1,0},{2,3},{3,2},{4,5},{5,4},{6,7},{7,6},{8,9},{9,8},{10,11... | collective-permute-start | bytes 12296 | tf_op jit(solution)/shard_map/ppermute | solution.py:223
  94.4 1.0 collective-permute-done.32.refs_12_
  95.4 1.1 collective-permute-done.31.refs_11_
  96.8 4.8 %shard_map.77 = (f32[8,1,512]{2,1,0:T(1,128)S(1)}, f32[8,128]{1,0:T(8,128)}) custom-call(bf16[1024,128]{1,0:T(8,128)(2,1)S(1)} %get-tuple-element.26.refs_0_, bf16[528,128]{1,0:T(8,128)(2,1)S(1)} %fusion.1.refs_4_.refs_1_, bf16[528,128]{1,0:T(8,128)(2,1)S(1)} %collective-permute-done.6.refs_5_.refs_2_, ...), custom_call_target="tpu_custom_call" | custom-call | flops 1073741824 | bytes 1380352 | tf_op jit(solution)/shard_map/pallas_call | solution.py:211
  101.6 1.2 %collective-permute-done.33.y_ref = f32[8,1,512]{2,1,0:T(1,128)S(1)} collective-permute-done((f32[8,1,512]{2,1,0:T(1,128)S(1)}, f32[8,1,512]{2,1,0:T(1,128)S(1)}, u32[]{:S(2)}, u32[]{:S(2)}) %collective-permute-start.33) | collective-permute-done | bytes 16416 | tf_op jit(solution)/shard_map/ppermute | solution.py:223
  102.8 1.3 %collective-permute-start.34 = (f32[2,1,512]{2,1,0:T(1,128)S(1)}, f32[2,1,512]{2,1,0:T(1,128)S(1)}, u32[]{:S(2)}, u32[]{:S(2)}) collective-permute-start(f32[2,1,512]{2,1,0:T(1,128)S(1)} %get-tuple-element.32), channel_id=1, source_target_pairs={{4,8},{12,0},{20,24},{28,16},{5,9},{13,1},{21,25},{29,17},{6,10},{... | collective-permute-start | bytes 12296 | tf_op jit(solution)/shard_map/ppermute | solution.py:231
  104.1 1.3 %collective-permute-start.35 = (f32[2,1,512]{2,1,0:T(1,128)S(1)}, f32[2,1,512]{2,1,0:T(1,128)S(1)}, u32[]{:S(2)}, u32[]{:S(2)}) collective-permute-start(f32[2,1,512]{2,1,0:T(1,128)S(1)} %get-tuple-element.33), channel_id=1, source_target_pairs={{4,16},{12,24},{20,0},{28,8},{5,17},{13,25},{21,1},{29,9},{6,18},{... | collective-permute-start | bytes 12296 | tf_op jit(solution)/shard_map/ppermute | solution.py:231
  105.4 1.3 %collective-permute-start.36 = (f32[2,1,512]{2,1,0:T(1,128)S(1)}, f32[2,1,512]{2,1,0:T(1,128)S(1)}, u32[]{:S(2)}, u32[]{:S(2)}) collective-permute-start(f32[2,1,512]{2,1,0:T(1,128)S(1)} %get-tuple-element.34), channel_id=1, source_target_pairs={{4,24},{12,16},{20,8},{28,0},{5,25},{13,17},{21,9},{29,1},{6,26},{... | collective-permute-start | bytes 12296 | tf_op jit(solution)/shard_map/ppermute | solution.py:231
  106.7 1.0 collective-permute-done.34.refs_1_
  107.7 1.3 %collective-permute-done.35.refs_2_ = f32[2,1,512]{2,1,0:T(1,128)S(1)} collective-permute-done((f32[2,1,512]{2,1,0:T(1,128)S(1)}, f32[2,1,512]{2,1,0:T(1,128)S(1)}, u32[]{:S(2)}, u32[]{:S(2)}) %collective-permute-start.35) | collective-permute-done | bytes 4128 | tf_op jit(solution)/shard_map/ppermute | solution.py:231
  109.0 2.2 %collective-permute-done.36.refs_3_ = f32[2,1,512]{2,1,0:T(1,128)S(1)} collective-permute-done((f32[2,1,512]{2,1,0:T(1,128)S(1)}, f32[2,1,512]{2,1,0:T(1,128)S(1)}, u32[]{:S(2)}, u32[]{:S(2)}) %collective-permute-start.36) | collective-permute-done | bytes 4128 | tf_op jit(solution)/shard_map/ppermute | solution.py:231
  111.2 1.3 %collective-permute-start.37 = (f32[2,1,512]{2,1,0:T(1,128)S(1)}, f32[2,1,512]{2,1,0:T(1,128)S(1)}, u32[]{:S(2)}, u32[]{:S(2)}) collective-permute-start(f32[2,1,512]{2,1,0:T(1,128)S(1)} %shard_map.79.x_ref), channel_id=1, source_target_pairs={{0,4},{8,12},{16,20},{24,28},{1,5},{9,13},{17,21},{25,29},{2,6},{1... | collective-permute-start | bytes 12296 | tf_op jit(solution)/shard_map/ppermute | solution.py:231
  112.5 0.8 collective-permute-done.37.y_ref
  113.3 0.6 shard_map.80
  (33 shorter events, 2.1 us)
Async XLA Ops:
  0.6 0.7 copy-start.2
  1.3 5.6 %copy-start = (bf16[256,128]{1,0:T(8,128)(2,1)S(1)}, bf16[256,128]{1,0:T(8,128)(2,1)}, u32[]{:S(2)}) copy-start(bf16[256,128]{1,0:T(8,128)(2,1)} %refs_0_.5) | copy-start | bytes 196612
  1.3 18.7 %copy-start.1 = (f32[128,128]{1,0:T(8,128)S(1)}, f32[128,128]{1,0:T(8,128)}, u32[]{:S(2)}) copy-start(f32[128,128]{1,0:T(8,128)} %refs_12_.1) | copy-start | bytes 196612
  2.3 15.6 %collective-permute-start.5 = (bf16[528,128]{1,0:T(8,128)(2,1)S(1)}, bf16[528,128]{1,0:T(8,128)(2,1)S(1)}, u32[]{:S(2)}, u32[]{:S(2)}) collective-permute-start(bf16[528,128]{1,0:T(8,128)(2,1)S(1)} %fusion.1.refs_4_.refs_1_), channel_id=1, source_target_pairs={{0,24},{4,28},{8,16},{12,20},{16,8},{20,12},{24,0},{28,4},{1,25},{... | collective-permute-start | bytes 405512 | tf_op jit(solution)/shard_map/ppermute | solution.py:223
  6.2 11.6 %collective-permute-start.4 = (bf16[528,128]{1,0:T(8,128)(2,1)S(1)}, bf16[528,128]{1,0:T(8,128)(2,1)S(1)}, u32[]{:S(2)}, u32[]{:S(2)}) collective-permute-start(bf16[528,128]{1,0:T(8,128)(2,1)S(1)} %fusion.1.refs_4_.refs_1_), channel_id=1, source_target_pairs={{0,16},{4,20},{8,24},{12,28},{16,0},{20,4},{24,8},{28,12},{1,17},{... | collective-permute-start | bytes 405512 | tf_op jit(solution)/shard_map/ppermute | solution.py:223
  6.7 11.1 %collective-permute-start.3 = (bf16[528,128]{1,0:T(8,128)(2,1)S(1)}, bf16[528,128]{1,0:T(8,128)(2,1)S(1)}, u32[]{:S(2)}, u32[]{:S(2)}) collective-permute-start(bf16[528,128]{1,0:T(8,128)(2,1)S(1)} %fusion.1.refs_4_.refs_1_), channel_id=1, source_target_pairs={{0,8},{4,12},{8,0},{12,4},{16,24},{20,28},{24,16},{28,20},{1,9},{5... | collective-permute-start | bytes 405512 | tf_op jit(solution)/shard_map/ppermute | solution.py:223
  6.9 6.7 %collective-permute-start.2 = (bf16[256,128]{1,0:T(8,128)(2,1)S(1)}, bf16[256,128]{1,0:T(8,128)(2,1)S(1)}, u32[]{:S(2)}, u32[]{:S(2)}) collective-permute-start(bf16[256,128]{1,0:T(8,128)(2,1)S(1)} %copy-done), channel_id=1, source_target_pairs={{0,3},{1,2},{2,1},{3,0},{4,7},{5,6},{6,5},{7,4},{8,11},{9,10},{10,... | collective-permute-start | bytes 196616 | tf_op jit(solution)/shard_map/ppermute | solution.py:223
  10.9 5.2 %collective-permute-start.1 = (bf16[256,128]{1,0:T(8,128)(2,1)S(1)}, bf16[256,128]{1,0:T(8,128)(2,1)S(1)}, u32[]{:S(2)}, u32[]{:S(2)}) collective-permute-start(bf16[256,128]{1,0:T(8,128)(2,1)S(1)} %copy-done), channel_id=1, source_target_pairs={{0,2},{1,3},{2,0},{3,1},{4,6},{5,7},{6,4},{7,5},{8,10},{9,11},{10,... | collective-permute-start | bytes 196616 | tf_op jit(solution)/shard_map/ppermute | solution.py:223
  13.6 4.3 %collective-permute-start = (bf16[256,128]{1,0:T(8,128)(2,1)S(1)}, bf16[256,128]{1,0:T(8,128)(2,1)S(1)}, u32[]{:S(2)}, u32[]{:S(2)}) collective-permute-start(bf16[256,128]{1,0:T(8,128)(2,1)S(1)} %copy-done), channel_id=1, source_target_pairs={{0,1},{1,0},{2,3},{3,2},{4,5},{5,4},{6,7},{7,6},{8,9},{9,8},{10,11... | collective-permute-start | bytes 196616 | tf_op jit(solution)/shard_map/ppermute | solution.py:223
  17.9 1.4 %collective-permute-start.6 = (bf16[528,128]{1,0:T(8,128)(2,1)S(1)}, bf16[528,128]{1,0:T(8,128)(2,1)S(1)}, u32[]{:S(2)}, u32[]{:S(2)}) collective-permute-start(bf16[528,128]{1,0:T(8,128)(2,1)S(1)} %fusion.1.refs_4_.refs_1_), channel_id=1, source_target_pairs={{0,4},{4,0},{8,12},{12,8},{16,20},{20,16},{24,28},{28,24},{1,5},{5... | collective-permute-start | bytes 405512 | tf_op jit(solution)/shard_map/ppermute | solution.py:223
  17.9 1.5 %collective-permute-start.7 = (bf16[528,128]{1,0:T(8,128)(2,1)S(1)}, bf16[528,128]{1,0:T(8,128)(2,1)S(1)}, u32[]{:S(2)}, u32[]{:S(2)}) collective-permute-start(bf16[528,128]{1,0:T(8,128)(2,1)S(1)} %collective-permute-done.3.refs_6_.refs_3_), channel_id=1, source_target_pairs={{0,4},{4,0},{8,12},{12,8},{16,20},{20,16},{24,28},{28,24},{1,5},{5... | collective-permute-start | bytes 405512 | tf_op jit(solution)/shard_map/ppermute | solution.py:223
  18.4 1.4 %collective-permute-start.8 = (bf16[528,128]{1,0:T(8,128)(2,1)S(1)}, bf16[528,128]{1,0:T(8,128)(2,1)S(1)}, u32[]{:S(2)}, u32[]{:S(2)}) collective-permute-start(bf16[528,128]{1,0:T(8,128)(2,1)S(1)} %collective-permute-done.4.refs_8_.refs_5_), channel_id=1, source_target_pairs={{0,4},{4,0},{8,12},{12,8},{16,20},{20,16},{24,28},{28,24},{1,5},{5... | collective-permute-start | bytes 405512 | tf_op jit(solution)/shard_map/ppermute | solution.py:223
  18.5 1.5 %collective-permute-start.9 = (bf16[528,128]{1,0:T(8,128)(2,1)S(1)}, bf16[528,128]{1,0:T(8,128)(2,1)S(1)}, u32[]{:S(2)}, u32[]{:S(2)}) collective-permute-start(bf16[528,128]{1,0:T(8,128)(2,1)S(1)} %collective-permute-done.5.refs_10_.refs_7_), channel_id=1, source_target_pairs={{0,4},{4,0},{8,12},{12,8},{16,20},{20,16},{24,28},{28,24},{1,5},{5... | collective-permute-start | bytes 405512 | tf_op jit(solution)/shard_map/ppermute | solution.py:223
  27.0 5.5 %collective-permute-start.12 = (f32[8,128]{1,0:T(8,128)S(1)}, f32[8,128]{1,0:T(8,128)S(1)}, u32[]{:S(2)}, u32[]{:S(2)}) collective-permute-start(f32[8,128]{1,0:T(8,128)S(1)} %get-tuple-element.23.refs_4_), channel_id=1, source_target_pairs={{0,3},{1,2},{2,1},{3,0},{4,7},{5,6},{6,5},{7,4},{8,11},{9,10},{10,... | collective-permute-start | bytes 12296 | tf_op jit(solution)/shard_map/ppermute | solution.py:223
  30.9 4.5 %collective-permute-start.11 = (f32[8,128]{1,0:T(8,128)S(1)}, f32[8,128]{1,0:T(8,128)S(1)}, u32[]{:S(2)}, u32[]{:S(2)}) collective-permute-start(f32[8,128]{1,0:T(8,128)S(1)} %get-tuple-element.23.refs_4_), channel_id=1, source_target_pairs={{0,2},{1,3},{2,0},{3,1},{4,6},{5,7},{6,4},{7,5},{8,10},{9,11},{10,... | collective-permute-start | bytes 12296 | tf_op jit(solution)/shard_map/ppermute | solution.py:223
  30.9 4.5 %collective-permute-start.10 = (f32[8,128]{1,0:T(8,128)S(1)}, f32[8,128]{1,0:T(8,128)S(1)}, u32[]{:S(2)}, u32[]{:S(2)}) collective-permute-start(f32[8,128]{1,0:T(8,128)S(1)} %get-tuple-element.23.refs_4_), channel_id=1, source_target_pairs={{0,1},{1,0},{2,3},{3,2},{4,5},{5,4},{6,7},{7,6},{8,9},{9,8},{10,11... | collective-permute-start | bytes 12296 | tf_op jit(solution)/shard_map/ppermute | solution.py:223
  36.0 1.3 %collective-permute-start.13 = (f32[128,128]{1,0:T(8,128)S(1)}, f32[128,128]{1,0:T(8,128)S(1)}, u32[]{:S(2)}, u32[]{:S(2)}) collective-permute-start(f32[128,128]{1,0:T(8,128)S(1)} %shard_map.68.refs_0_), channel_id=1, source_target_pairs={{0,4},{4,0},{8,12},{12,8},{16,20},{20,16},{24,28},{28,24},{1,5},{5... | collective-permute-start | bytes 196616 | tf_op jit(solution)/shard_map/ppermute | solution.py:223
  37.3 6.5 %collective-permute-start.16 = (f32[128,128]{1,0:T(8,128)S(1)}, f32[128,128]{1,0:T(8,128)S(1)}, u32[]{:S(2)}, u32[]{:S(2)}) collective-permute-start(f32[128,128]{1,0:T(8,128)S(1)} %shard_map.69.refs_0_), channel_id=1, source_target_pairs={{4,24},{12,16},{20,8},{28,0},{5,25},{13,17},{21,9},{29,1},{6,26},{... | collective-permute-start | bytes 196616 | tf_op jit(solution)/shard_map/ppermute | solution.py:231
  38.6 6.5 %collective-permute-start.15 = (f32[128,128]{1,0:T(8,128)S(1)}, f32[128,128]{1,0:T(8,128)S(1)}, u32[]{:S(2)}, u32[]{:S(2)}) collective-permute-start(f32[128,128]{1,0:T(8,128)S(1)} %shard_map.69.refs_0_), channel_id=1, source_target_pairs={{4,16},{12,24},{20,0},{28,8},{5,17},{13,25},{21,1},{29,9},{6,18},{... | collective-permute-start | bytes 196616 | tf_op jit(solution)/shard_map/ppermute | solution.py:231
  39.9 6.6 %collective-permute-start.14 = (f32[128,128]{1,0:T(8,128)S(1)}, f32[128,128]{1,0:T(8,128)S(1)}, u32[]{:S(2)}, u32[]{:S(2)}) collective-permute-start(f32[128,128]{1,0:T(8,128)S(1)} %shard_map.69.refs_0_), channel_id=1, source_target_pairs={{4,8},{12,0},{20,24},{28,16},{5,9},{13,1},{21,25},{29,17},{6,10},{... | collective-permute-start | bytes 196616 | tf_op jit(solution)/shard_map/ppermute | solution.py:231
  46.5 6.7 %collective-permute-start.20 = (f32[128,128]{1,0:T(8,128)S(1)}, f32[128,128]{1,0:T(8,128)S(1)}, u32[]{:S(2)}, u32[]{:S(2)}) collective-permute-start(f32[128,128]{1,0:T(8,128)S(1)} %shard_map.70), channel_id=1, source_target_pairs={{0,7},{1,6},{2,5},{3,4},{8,15},{9,14},{10,13},{11,12},{16,23},{17,... | collective-permute-start | bytes 196616 | tf_op jit(solution)/shard_map/ppermute | solution.py:239
  48.7 4.5 %collective-permute-start.19 = (f32[128,128]{1,0:T(8,128)S(1)}, f32[128,128]{1,0:T(8,128)S(1)}, u32[]{:S(2)}, u32[]{:S(2)}) collective-permute-start(f32[128,128]{1,0:T(8,128)S(1)} %shard_map.70), channel_id=1, source_target_pairs={{0,6},{1,7},{2,4},{3,5},{8,14},{9,15},{10,12},{11,13},{16,22},{17,... | collective-permute-start | bytes 196616 | tf_op jit(solution)/shard_map/ppermute | solution.py:239
  50.5 3.2 %collective-permute-start.18 = (f32[128,128]{1,0:T(8,128)S(1)}, f32[128,128]{1,0:T(8,128)S(1)}, u32[]{:S(2)}, u32[]{:S(2)}) collective-permute-start(f32[128,128]{1,0:T(8,128)S(1)} %shard_map.70), channel_id=1, source_target_pairs={{0,5},{1,4},{2,7},{3,6},{8,13},{9,12},{10,15},{11,14},{16,21},{17,... | collective-permute-start | bytes 196616 | tf_op jit(solution)/shard_map/ppermute | solution.py:239
  51.8 2.2 %collective-permute-start.17 = (f32[128,128]{1,0:T(8,128)S(1)}, f32[128,128]{1,0:T(8,128)S(1)}, u32[]{:S(2)}, u32[]{:S(2)}) collective-permute-start(f32[128,128]{1,0:T(8,128)S(1)} %shard_map.70), channel_id=1, source_target_pairs={{0,4},{1,5},{2,6},{3,7},{8,12},{9,13},{10,14},{11,15},{16,20},{17,... | collective-permute-start | bytes 196616 | tf_op jit(solution)/shard_map/ppermute | solution.py:239
  54.0 3.1 %collective-permute-start.21 = (f32[128,128]{1,0:T(8,128)S(1)}, f32[128,128]{1,0:T(8,128)S(1)}, u32[]{:S(2)}, u32[]{:S(2)}) collective-permute-start(f32[128,128]{1,0:T(8,128)S(1)} %shard_map.71.refs_12_), channel_id=1, source_target_pairs={{4,0},{12,8},{20,16},{28,24},{5,1},{13,9},{21,17},{29,25},{6,2},{1... | collective-permute-start | bytes 196616 | tf_op jit(solution)/shard_map/ppermute | solution.py:231
  63.0 5.4 %collective-permute-start.24 = (f32[8,128]{1,0:T(8,128)S(1)}, f32[8,128]{1,0:T(8,128)S(1)}, u32[]{:S(2)}, u32[]{:S(2)}) collective-permute-start(f32[8,128]{1,0:T(8,128)S(1)} %get-tuple-element.27.refs_9_), channel_id=1, source_target_pairs={{0,3},{1,2},{2,1},{3,0},{4,7},{5,6},{6,5},{7,4},{8,11},{9,10},{10,... | collective-permute-start | bytes 12296 | tf_op jit(solution)/shard_map/ppermute | solution.py:223
  64.8 4.5 %collective-permute-start.23 = (f32[8,128]{1,0:T(8,128)S(1)}, f32[8,128]{1,0:T(8,128)S(1)}, u32[]{:S(2)}, u32[]{:S(2)}) collective-permute-start(f32[8,128]{1,0:T(8,128)S(1)} %get-tuple-element.27.refs_9_), channel_id=1, source_target_pairs={{0,2},{1,3},{2,0},{3,1},{4,6},{5,7},{6,4},{7,5},{8,10},{9,11},{10,... | collective-permute-start | bytes 12296 | tf_op jit(solution)/shard_map/ppermute | solution.py:223
  65.2 4.1 %collective-permute-start.22 = (f32[8,128]{1,0:T(8,128)S(1)}, f32[8,128]{1,0:T(8,128)S(1)}, u32[]{:S(2)}, u32[]{:S(2)}) collective-permute-start(f32[8,128]{1,0:T(8,128)S(1)} %get-tuple-element.27.refs_9_), channel_id=1, source_target_pairs={{0,1},{1,0},{2,3},{3,2},{4,5},{5,4},{6,7},{7,6},{8,9},{9,8},{10,11... | collective-permute-start | bytes 12296 | tf_op jit(solution)/shard_map/ppermute | solution.py:223
  74.1 1.2 %collective-permute-start.25 = (f32[8,512]{1,0:T(8,128)S(1)}, f32[8,512]{1,0:T(8,128)S(1)}, u32[]{:S(2)}, u32[]{:S(2)}) collective-permute-start(f32[8,512]{1,0:T(8,128)S(1)} %get-tuple-element.28.refs_0_), channel_id=1, source_target_pairs={{0,4},{4,0},{8,12},{12,8},{16,20},{20,16},{24,28},{28,24},{1,5},{5... | collective-permute-start | bytes 49160 | tf_op jit(solution)/shard_map/ppermute | solution.py:223
  75.3 6.0 %collective-permute-start.28 = (f32[8,512]{1,0:T(8,128)S(1)}, f32[8,512]{1,0:T(8,128)S(1)}, u32[]{:S(2)}, u32[]{:S(2)}) collective-permute-start(f32[8,512]{1,0:T(8,128)S(1)} %shard_map.74.refs_0_), channel_id=1, source_target_pairs={{4,24},{12,16},{20,8},{28,0},{5,25},{13,17},{21,9},{29,1},{6,26},{... | collective-permute-start | bytes 49160 | tf_op jit(solution)/shard_map/ppermute | solution.py:231
  76.6 5.1 %collective-permute-start.27 = (f32[8,512]{1,0:T(8,128)S(1)}, f32[8,512]{1,0:T(8,128)S(1)}, u32[]{:S(2)}, u32[]{:S(2)}) collective-permute-start(f32[8,512]{1,0:T(8,128)S(1)} %shard_map.74.refs_0_), channel_id=1, source_target_pairs={{4,16},{12,24},{20,0},{28,8},{5,17},{13,25},{21,1},{29,9},{6,18},{... | collective-permute-start | bytes 49160 | tf_op jit(solution)/shard_map/ppermute | solution.py:231
  77.9 5.1 %collective-permute-start.26 = (f32[8,512]{1,0:T(8,128)S(1)}, f32[8,512]{1,0:T(8,128)S(1)}, u32[]{:S(2)}, u32[]{:S(2)}) collective-permute-start(f32[8,512]{1,0:T(8,128)S(1)} %shard_map.74.refs_0_), channel_id=1, source_target_pairs={{4,8},{12,0},{20,24},{28,16},{5,9},{13,1},{21,25},{29,17},{6,10},{... | collective-permute-start | bytes 49160 | tf_op jit(solution)/shard_map/ppermute | solution.py:231
  83.0 2.1 %collective-permute-start.29 = (f32[8,512]{1,0:T(8,128)S(1)}, f32[8,512]{1,0:T(8,128)S(1)}, u32[]{:S(2)}, u32[]{:S(2)}) collective-permute-start(f32[8,512]{1,0:T(8,128)S(1)} %shard_map.75.refs_9_), channel_id=1, source_target_pairs={{0,4},{8,12},{16,20},{24,28},{1,5},{9,13},{17,21},{25,29},{2,6},{1... | collective-permute-start | bytes 49160 | tf_op jit(solution)/shard_map/ppermute | solution.py:231
  90.0 5.4 %collective-permute-start.32 = (f32[8,128]{1,0:T(8,128)S(1)}, f32[8,128]{1,0:T(8,128)S(1)}, u32[]{:S(2)}, u32[]{:S(2)}) collective-permute-start(f32[8,128]{1,0:T(8,128)S(1)} %shard_map.76.refs_9_), channel_id=1, source_target_pairs={{0,3},{1,2},{2,1},{3,0},{4,7},{5,6},{6,5},{7,4},{8,11},{9,10},{10,... | collective-permute-start | bytes 12296 | tf_op jit(solution)/shard_map/ppermute | solution.py:223
  92.1 4.5 %collective-permute-start.31 = (f32[8,128]{1,0:T(8,128)S(1)}, f32[8,128]{1,0:T(8,128)S(1)}, u32[]{:S(2)}, u32[]{:S(2)}) collective-permute-start(f32[8,128]{1,0:T(8,128)S(1)} %shard_map.76.refs_9_), channel_id=1, source_target_pairs={{0,2},{1,3},{2,0},{3,1},{4,6},{5,7},{6,4},{7,5},{8,10},{9,11},{10,... | collective-permute-start | bytes 12296 | tf_op jit(solution)/shard_map/ppermute | solution.py:223
  93.2 3.6 %collective-permute-start.30 = (f32[8,128]{1,0:T(8,128)S(1)}, f32[8,128]{1,0:T(8,128)S(1)}, u32[]{:S(2)}, u32[]{:S(2)}) collective-permute-start(f32[8,128]{1,0:T(8,128)S(1)} %shard_map.76.refs_9_), channel_id=1, source_target_pairs={{0,1},{1,0},{2,3},{3,2},{4,5},{5,4},{6,7},{7,6},{8,9},{9,8},{10,11... | collective-permute-start | bytes 12296 | tf_op jit(solution)/shard_map/ppermute | solution.py:223
  101.6 1.2 %collective-permute-start.33 = (f32[8,1,512]{2,1,0:T(1,128)S(1)}, f32[8,1,512]{2,1,0:T(1,128)S(1)}, u32[]{:S(2)}, u32[]{:S(2)}) collective-permute-start(f32[8,1,512]{2,1,0:T(1,128)S(1)} %get-tuple-element.30.x_ref), channel_id=1, source_target_pairs={{0,4},{4,0},{8,12},{12,8},{16,20},{20,16},{24,28},{28,24},{1,5},{5... | collective-permute-start | bytes 49160 | tf_op jit(solution)/shard_map/ppermute | solution.py:223
  102.8 4.9 %collective-permute-start.34 = (f32[2,1,512]{2,1,0:T(1,128)S(1)}, f32[2,1,512]{2,1,0:T(1,128)S(1)}, u32[]{:S(2)}, u32[]{:S(2)}) collective-permute-start(f32[2,1,512]{2,1,0:T(1,128)S(1)} %get-tuple-element.32), channel_id=1, source_target_pairs={{4,8},{12,0},{20,24},{28,16},{5,9},{13,1},{21,25},{29,17},{6,10},{... | collective-permute-start | bytes 12296 | tf_op jit(solution)/shard_map/ppermute | solution.py:231
  104.1 4.9 %collective-permute-start.35 = (f32[2,1,512]{2,1,0:T(1,128)S(1)}, f32[2,1,512]{2,1,0:T(1,128)S(1)}, u32[]{:S(2)}, u32[]{:S(2)}) collective-permute-start(f32[2,1,512]{2,1,0:T(1,128)S(1)} %get-tuple-element.33), channel_id=1, source_target_pairs={{4,16},{12,24},{20,0},{28,8},{5,17},{13,25},{21,1},{29,9},{6,18},{... | collective-permute-start | bytes 12296 | tf_op jit(solution)/shard_map/ppermute | solution.py:231
  105.4 5.8 %collective-permute-start.36 = (f32[2,1,512]{2,1,0:T(1,128)S(1)}, f32[2,1,512]{2,1,0:T(1,128)S(1)}, u32[]{:S(2)}, u32[]{:S(2)}) collective-permute-start(f32[2,1,512]{2,1,0:T(1,128)S(1)} %get-tuple-element.34), channel_id=1, source_target_pairs={{4,24},{12,16},{20,8},{28,0},{5,25},{13,17},{21,9},{29,1},{6,26},{... | collective-permute-start | bytes 12296 | tf_op jit(solution)/shard_map/ppermute | solution.py:231
  111.2 2.1 %collective-permute-start.37 = (f32[2,1,512]{2,1,0:T(1,128)S(1)}, f32[2,1,512]{2,1,0:T(1,128)S(1)}, u32[]{:S(2)}, u32[]{:S(2)}) collective-permute-start(f32[2,1,512]{2,1,0:T(1,128)S(1)} %shard_map.79.x_ref), channel_id=1, source_target_pairs={{0,4},{8,12},{16,20},{24,28},{1,5},{9,13},{17,21},{25,29},{2,6},{1... | collective-permute-start | bytes 12296 | tf_op jit(solution)/shard_map/ppermute | solution.py:231

commit v5 on v4

v5 whole, which is shorter than its diff:
```python
import functools
import math

import jax
import jax.numpy as jnp
from jax import lax
from jax.experimental import pallas as pl
from jax.experimental.pallas import tpu as pltpu
from jax.sharding import PartitionSpec as P

ITERS = 2
LANES = 128
SUB = 16
SMALLEST = 1e-25
NT_DIMS = (((1,), (1,)), ((), ()))
TN_DIMS = (((0,), (0,)), ((), ()))


def split3(x):
    high = x.astype(jnp.bfloat16)
    rest = x - high.astype(jnp.float32)
    mid = rest.astype(jnp.bfloat16)
    low = (rest - mid.astype(jnp.float32)).astype(jnp.bfloat16)
    return high, mid, low


def project4(rows, matrix):
    total = None
    for part in reversed(split3(matrix)):
        term = jnp.dot(rows, part, preferred_element_type=jnp.float32)
        total = term if total is None else total + term
    return (total.astype(jnp.bfloat16).astype(jnp.float32) * 4.0).astype(jnp.bfloat16)


def lane_fold(op, x):
    parts = [x[:, i : i + LANES] for i in range(0, x.shape[1], LANES)]
    return functools.reduce(op, parts)


def as_lanes(column):
    return jnp.broadcast_to(column, (LANES, LANES)).T[0:1, :]


def as_rows(lanes):
    return jnp.broadcast_to(lanes, (LANES, LANES)).T


def tree(op, parts):
    while len(parts) > 1:
        parts = [op(parts[i], parts[i + 1]) for i in range(0, len(parts), 2)]
    return parts[0]


def log_sum(parts):
    top = functools.reduce(jnp.maximum, parts)
    return top + jnp.log(tree(jnp.add, [jnp.exp(p - top) for p in parts]))


def potential_rows(block_ref, width):
    groups = width // LANES
    tail = block_ref[width:, :].astype(jnp.float32)
    return jnp.concatenate([tail[i : i + 1, :] for i in range(groups)], axis=1)


def row_lse(a_ref, t_refs, column, scores, width, lse_ref, carried_ref=None, e_ref=None, top_ref=None):
    c = lax.axis_index("col")
    steps = a_ref.shape[0] // LANES
    per = steps // lax.axis_size("col")
    top = None
    for i in range(steps + 1):
        last_top, top, mass, carried = top, None, None, None
        for g, t_ref in enumerate(t_refs):
            at = slice(g * width, (g + 1) * width)
            if i < steps:
                a = a_ref[i * LANES : (i + 1) * LANES, :]
                s = lax.dot_general(a, t_ref[:width, :], NT_DIMS, preferred_element_type=jnp.float32)
                s = s + column[g]
                scores[i % 2, :, at] = s
                m = lane_fold(jnp.maximum, s)
                top = m if top is None else jnp.maximum(top, m)
            if i > 0:
                e = jnp.exp(scores[(i - 1) % 2, :, at] - last_top)
                m = lane_fold(jnp.add, e)
                mass = m if mass is None else mass + m
                if e_ref is not None:
                    e_ref[(i - 1) * LANES : i * LANES, at] = e.astype(jnp.bfloat16)
                if carried_ref is not None:
                    d = jnp.dot(e.astype(jnp.bfloat16), t_ref[:width, :], preferred_element_type=jnp.float32)
                    carried = d if carried is None else carried + d
        if i < steps:
            top = jnp.max(top, axis=1, keepdims=True)
        if i > 0:
            mass = jnp.sum(mass, axis=1, keepdims=True)
            if carried_ref is not None:
                carried_ref[(i - 1) * LANES : i * LANES, :] = carried / mass
            row = (c ^ ((i - 1) // per)) * per + (i - 1) % per
            lse_ref[pl.ds(row, 1), :] = as_lanes(last_top + jnp.log(mass))
            if top_ref is not None:
                top_ref[pl.ds(row, 1), :] = as_lanes(last_top)


def couple_kernel(ns, nt, width, *refs):
    s_refs, t_refs, moment_ref = refs[:ns], refs[ns : ns + nt], refs[ns + nt]
    lse_ref, carried_ref, a_ref, scores = refs[ns + nt + 1 :]
    piece = s_refs[0].shape[0]
    for k in range(ns):
        a_ref[k * piece : (k + 1) * piece, :] = project4(s_refs[k][...], moment_ref[...])
    column = [potential_rows(t, width) for t in t_refs]
    row_lse(a_ref, t_refs, column, scores, width, lse_ref, carried_ref)


def moment_kernel(ns, rows_total, *refs):
    s_refs, l_refs, carried_ref = refs[:ns], refs[ns : 2 * ns], refs[2 * ns]
    keep_ref, send_ref, weight_ref, total_ref = refs[2 * ns + 1 :]
    c, r = lax.axis_index("col"), lax.axis_index("row")
    piece = s_refs[0].shape[0]
    per = piece // LANES
    shift = log_sum([l[...] for l in l_refs])
    weight_ref[...] = jnp.exp(l_refs[0][...] - shift) * (1.0 / rows_total)
    total = None
    for k in range(ns):
        for j in range(per):
            w = as_rows(weight_ref[pl.ds((c ^ k) * per + j, 1), :])
            at = (k * per + j) * LANES
            x = carried_ref[at : at + LANES, :] * w
            s = s_refs[k][j * LANES : (j + 1) * LANES, :]
            for part in reversed(split3(x)):
                term = lax.dot_general(s, part, TN_DIMS, preferred_element_type=jnp.float32)
                total = term if total is None else total + term
    total_ref[...] = total
    half = keep_ref.shape[0]
    keep_ref[...] = total_ref[pl.ds(pl.multiple_of((r % 2) * half, half), half), :]
    send_ref[...] = total_ref[pl.ds(pl.multiple_of((1 - r % 2) * half, half), half), :]


def add_kernel(*refs):
    refs[-1][...] = tree(jnp.add, [r[...] for r in refs[:-1]])


def log_sum_kernel(*refs):
    refs[-1][...] = log_sum([r[...] for r in refs[:-1]])


def first_rows_kernel(ns, nt, width, *refs):
    s_refs, t_refs, m_refs = refs[:ns], refs[ns : ns + nt], refs[ns + nt : ns + nt + 2]
    moment_ref, a_ref, lse_ref, top_ref, e_ref, scores = refs[ns + nt + 2 :]
    r = lax.axis_index("row")
    piece, half = s_refs[0].shape[0], m_refs[0].shape[0]
    for k in range(2):
        moment_ref[pl.ds(pl.multiple_of((k ^ (r % 2)) * half, half), half), :] = m_refs[k][...]
    for k in range(ns):
        a_ref[k * piece : (k + 1) * piece, :] = project4(s_refs[k][...], moment_ref[...])
    column = [potential_rows(t, width) for t in t_refs]
    row_lse(a_ref, t_refs, column, scores, width, lse_ref, None, e_ref, top_ref)


def high_low(x):
    high = x.astype(jnp.bfloat16).astype(jnp.float32)
    at = lax.broadcasted_iota(jnp.int32, (SUB, x.shape[1]), 0)
    return jnp.where(at == 0, high, jnp.where(at == 1, x - high, 0.0)).astype(jnp.bfloat16)


def rows_kernel(nt, width, rows_total, *refs):
    a_ref, e_ref, top_ref, t_refs = refs[0], refs[1], refs[2], refs[3 : 3 + nt]
    l_refs = refs[3 + nt : 3 + nt + nt // 2]
    lse_ref, column_ref, weights, scores = refs[3 + nt + nt // 2 :]
    c, r = lax.axis_index("col"), lax.axis_index("row")
    column_ref[...] = math.log(rows_total) - log_sum([l[...] for l in l_refs])
    column = [column_ref[pl.ds(r ^ k, 1), :] for k in range(nt)]
    change = [column[k] - potential_rows(t_refs[k], width) for k in range(nt)]
    top = jnp.max(functools.reduce(jnp.maximum, change), axis=1, keepdims=True)
    for k in range(nt):
        weights[:, k * width : (k + 1) * width] = high_low(jnp.exp(change[k] - top))
    steps = a_ref.shape[0] // LANES
    per = steps // lax.axis_size("col")
    least = None
    for i in range(steps):
        e = e_ref[i * LANES : (i + 1) * LANES, :]
        sums = lax.dot_general(weights[...], e, NT_DIMS, preferred_element_type=jnp.float32)
        mass = sums[0:1, :] + sums[1:2, :]
        least = mass if least is None else jnp.minimum(least, mass)
        row = pl.ds((c ^ (i // per)) * per + i % per, 1)
        lse_ref[row, :] = top + top_ref[row, :] + jnp.log(mass)

    @pl.when(jnp.logical_not(jnp.min(least) > SMALLEST))
    def _():
        row_lse(a_ref, t_refs, column, scores, width, lse_ref)


def columns_kernel(ns, nt, width, cols_total, last, *refs):
    a_ref, e_ref, top_ref, t_refs, l_refs = refs[0], refs[1], refs[2], refs[3 : 3 + nt], refs[3 + nt : 3 + nt + ns]
    out_refs, (sp_ref, weight_rows, weights, spread_rows, scores) = refs[3 + nt + ns : -5], refs[-5:]
    c, r = lax.axis_index("col"), lax.axis_index("row")
    rows = a_ref.shape[0]
    per = rows // ns // LANES
    potential = math.log(cols_total) - log_sum([l[...] for l in l_refs])
    sp_ref[...] = potential
    shift = potential + top_ref[...]
    top = jnp.max(jnp.max(shift, axis=1, keepdims=True), axis=0, keepdims=True)
    weight_rows[...] = jnp.exp(shift - top)
    for k in range(ns):
        for j in range(per):
            at = (k * per + j) * LANES
            weights[:, at : at + LANES] = high_low(weight_rows[pl.ds((c ^ k) * per + j, 1), :])

    def store(g, lse):
        if last:
            out_refs[g % 2][g // 2] = lse
        else:
            out_refs[0][pl.ds(r ^ g, 1), :] = lse

    least = None
    for g in range(nt):
        e = e_ref[:, g * width : (g + 1) * width]
        sums = jnp.dot(weights[...], e, preferred_element_type=jnp.float32)
        mass = sums[0:1, :] + sums[1:2, :]
        least = mass if least is None else jnp.minimum(least, mass)
        store(g, top - potential_rows(t_refs[g], width) + jnp.log(mass))

    @pl.when(jnp.logical_not(jnp.min(least) > SMALLEST))
    def _():
        column_lse(ns, a_ref, t_refs, sp_ref, spread_rows, scores, width, store)


def column_lse(ns, a_ref, t_refs, sp_ref, spread_rows, scores, width, store):
    c = lax.axis_index("col")
    rows = a_ref.shape[0]
    per = rows // ns // LANES
    for k in range(ns):
        for j in range(per):
            at = (k * per + j) * LANES
            spread_rows[at : at + LANES, :] = as_rows(sp_ref[pl.ds((c ^ k) * per + j, 1), :])
    for g, t_ref in enumerate(t_refs):
        top = None
        for at in range(0, rows, LANES):
            a = a_ref[at : at + LANES, :]
            s = lax.dot_general(a, t_ref[:width, :], NT_DIMS, preferred_element_type=jnp.float32)
            s = s + jnp.concatenate([spread_rows[at : at + LANES, :]] * (width // LANES), axis=1)
            scores[at : at + LANES, :] = s
            m = jnp.max(s.reshape(LANES // 8, 8, width), axis=0)
            top = m if top is None else jnp.maximum(top, m)
        top = jnp.max(top, axis=0, keepdims=True)
        mass = None
        for at in range(0, rows, LANES):
            e = jnp.exp(scores[at : at + LANES, :] - top)
            m = jnp.sum(e.reshape(LANES // 8, 8, width), axis=0)
            mass = m if mass is None else mass + m
        store(g, top + jnp.log(jnp.sum(mass, axis=0, keepdims=True)))


def split_kernel(x_ref, y_ref, *out_refs):
    for k, out_ref in enumerate(out_refs):
        out_ref[...] = log_sum([x_ref[k], y_ref[k]])


def update_kernel(rows_total, *refs):
    refs[-1][...] = math.log(rows_total) - log_sum([l[...] for l in refs[:-1]])


def call(kernel, out, args, scratch=(), flops=0, exps=0):
    vmem = pl.BlockSpec(memory_space=pltpu.VMEM)
    bytes_accessed = sum(x.size * x.dtype.itemsize for x in list(args) + list(out))
    return pl.pallas_call(
        kernel,
        out_shape=list(out),
        in_specs=[vmem] * len(args),
        out_specs=[vmem] * len(out),
        scratch_shapes=list(scratch),
        compiler_params=pltpu.CompilerParams(vmem_limit_bytes=24 << 20),
        cost_estimate=pl.CostEstimate(flops=flops, bytes_accessed=bytes_accessed, transcendentals=exps),
    )(*args)


def swap(x, axis, k):
    return lax.ppermute(x, axis, [(i, i ^ k) for i in range(lax.axis_size(axis))])


def exchange(x, axis):
    return [x] + [swap(x, axis, k) for k in range(1, lax.axis_size(axis))]


def exchange_chips(x):
    return [x] + [swap(x, "row", k) for k in range(2, lax.axis_size("row"), 2)]


def combine(kernel, parts):
    return call(kernel, [jax.ShapeDtypeStruct(parts[0].shape, parts[0].dtype)], parts)[0]


def gather(block, piece):
    ns, nt = lax.axis_size("col"), lax.axis_size("row")
    blocks, pieces = {0: block}, {0: piece}
    for k in range(2, nt, 2):
        blocks[k] = swap(block, "row", k)
    for k in range(1, ns):
        pieces[k] = swap(piece, "col", k)
    near = {k: blocks[k] for k in range(0, nt, 2)}
    near, _ = lax.optimization_barrier((near, pieces))
    for k in range(0, nt, 2):
        blocks[k + 1] = swap(near[k], "row", 1)
    return [blocks[k] for k in range(nt)], [pieces[k] for k in range(ns)]


def per_device(source, target, target_potential, prev_moment):
    f32, shape = jnp.float32, jax.ShapeDtypeStruct
    ns, nt = lax.axis_size("col"), lax.axis_size("row")
    piece, width = source.shape[0], target.shape[0]
    depth = source.shape[1]
    rows, cols = piece * ns, width * nt
    rows_total, cols_total = rows * nt, cols * ns
    groups = width // LANES
    tail = jnp.pad(target_potential.reshape(groups, LANES), ((0, SUB - groups), (0, 0)))
    block = jnp.concatenate([target, tail], axis=0)
    t_blocks, s_pieces = gather(block, source)
    tile = shape((rows // LANES, LANES), f32)
    flops, exps = 2 * rows * cols * depth, rows * cols
    row_scores = pltpu.VMEM((2, LANES, cols), f32)

    lse, carried = call(
        functools.partial(couple_kernel, ns, nt, width),
        [tile, shape((rows, depth), f32)],
        s_pieces + t_blocks + [prev_moment],
        [pltpu.VMEM((rows, depth), jnp.bfloat16), row_scores],
        2 * flops,
        exps,
    )
    half = shape((depth // 2, depth), f32)
    keep, send = call(
        functools.partial(moment_kernel, ns, rows_total),
        [half, half],
        s_pieces + exchange(lse, "col") + [carried],
        [pltpu.VMEM(tile.shape, f32), pltpu.VMEM((depth, depth), f32)],
        6 * rows * depth * depth,
    )
    part = combine(add_kernel, [keep, swap(send, "row", 1)])
    part = combine(add_kernel, exchange(part, "col"))
    part = combine(add_kernel, exchange_chips(part))
    moment, a, lse, top, e = call(
        functools.partial(first_rows_kernel, ns, nt, width),
        [shape((depth, depth), f32), shape((rows, depth), jnp.bfloat16), tile, tile, shape((rows, cols), jnp.bfloat16)],
        s_pieces + t_blocks + [part, swap(part, "row", 1)],
        [row_scores],
        flops,
        exps,
    )
    for iteration in range(ITERS):
        last = iteration == ITERS - 1
        if iteration > 0:
            both = combine(log_sum_kernel, [column, swap(column, "row", 1)])
            lse, = call(
                functools.partial(rows_kernel, nt, width, rows_total),
                [tile],
                [a, e, top] + t_blocks + exchange_chips(both),
                [pltpu.VMEM((nt, width), f32), pltpu.VMEM((SUB, cols), jnp.bfloat16), row_scores],
                16 * rows * cols,
            )
        blocks = shape((nt // 2, 1, width), f32)
        column, *sent, source_potential = call(
            functools.partial(columns_kernel, ns, nt, width, cols_total, last),
            ([blocks, blocks] if last else [shape((nt, width), f32)]) + [tile],
            [a, e, top] + t_blocks + exchange(lse, "col"),
            [
                pltpu.VMEM(tile.shape, f32),
                pltpu.VMEM((SUB, rows), jnp.bfloat16),
                pltpu.VMEM((rows, LANES), f32),
                pltpu.VMEM((rows, width), f32),
            ],
            16 * rows * cols,
        )
    one = shape((1, width), f32)
    parts = call(split_kernel, [one] * (nt // 2), [column, swap(sent[0], "row", 1)])
    parts = [parts[0]] + [swap(x, "row", 2 * k) for k, x in enumerate(parts) if k > 0]
    update, = call(functools.partial(update_kernel, rows_total), [one], parts)
    return moment, source_potential.reshape(rows), update.reshape(width)


def solution(mesh):
    placed = (P(("row", "col"), None), P(("col", "row"), None), P(("col", "row")), P())
    return jax.shard_map(
        per_device,
        mesh=mesh,
        in_specs=placed,
        out_specs=(P(), P("row"), P(("col", "row"))),
        check_vma=False,
    )
```

time: 114 us -> 111 us (0.974)
  starting transfers between devices: 47 us -> 39.8 us
  Pallas kernels: 28.5 us -> 35.3 us
  waiting for transfers between devices: 35.9 us -> 31.9 us
    ppermute x16 -> x0, starting transfers between devices: 22.5 us -> none  [the longest x12 15.9 us: one_way(): lax.ppermute(x, 'row', [(i, i ^ k ^ 1) for i in range(lax.axis_size('row'...]
    ppermute x16 -> x0, waiting for transfers between devices: 17.5 us -> none  [the longest x12 16.6 us: one_way(): lax.ppermute(x, 'row', [(i, i ^ k ^ 1) for i in range(lax.axis_size('row'...]
    ppermute x22 -> x35, starting transfers between devices: 24.5 us -> 39.8 us  [swap(): lax.ppermute(x, axis, [(i, i ^ k) for i in range(lax.axis_size(axis))])]
    ppermute x22 -> x35, waiting for transfers between devices: 18.4 us -> 31.9 us  [swap(): lax.ppermute(x, axis, [(i, i ^ k) for i in range(lax.axis_size(axis))])]
    pallas_call x14 -> x12, Pallas kernels: 28.5 us -> 35.3 us  [call(): pl.pallas_call(kernel, out_shape=list(out), in_specs=[vmem] * len(args),...]
  transfers between devices with their start and end apart: 38 -> 35, of which waited for: 31 -> 30; matrix products, arithmetic and copies ran while one was open for 0% -> 0% of each run, Pallas kernels for 0% -> 0%
where the time goes in v5:
time: 111 us; the launch traced here: 110 us
  starting transfers between devices  39.8 us (36%)
  Pallas kernels  35.3 us (32%)
  waiting for transfers between devices  31.9 us (29%)
  local copies, waits for them, and re-layouts  1.68 us (2%)
    ppermute x35, starting transfers between devices, swap(): lax.ppermute(x, axis, [(i, i ^ k) for i in range(lax.axis_size(axis))])  39.8 us
    pallas_call x12, Pallas kernels, call(): pl.pallas_call(kernel, out_shape=list(out), in_specs=[vmem] * len(args),...  35.3 us
    ppermute x35, waiting for transfers between devices, swap(): lax.ppermute(x, axis, [(i, i ^ k) for i in range(lax.axis_size(axis))])  31.9 us
  transfers between devices with their start and end apart: 35, of which 30 were waited for; matrix products, arithmetic and copies ran while one was open for 0% of the time, Pallas kernels for 0%

profile of v5, /device:TPU:0, one launch (start us, length us, event | category | flops | bytes accessed | tf_op | source)
XLA Modules:
  0.0 110.4 jit_solution(16795728372657846562)
XLA Ops:
  0.6 1.0 fusion.1.refs_4_.refs_3_
  1.6 4.0 %collective-permute-start.5 = (bf16[528,128]{1,0:T(8,128)(2,1)S(1)}, bf16[528,128]{1,0:T(8,128)(2,1)S(1)}, u32[]{:S(2)}, u32[]{:S(2)}) collective-permute-start(bf16[528,128]{1,0:T(8,128)(2,1)S(1)} %fusion.1.refs_4_.refs_3_), channel_id=1, source_target_pairs={{0,24},{4,28},{8,16},{12,20},{16,8},{20,12},{24,0},{28,4},{1,25},{... | collective-permute-start | bytes 405512 | tf_op jit(solution)/shard_map/ppermute | solution.py:275
  5.6 0.5 collective-permute-start.4
  6.2 4.0 %collective-permute-start.2 = (bf16[256,128]{1,0:T(8,128)(2,1)}, bf16[256,128]{1,0:T(8,128)(2,1)S(1)}, u32[]{:S(2)}, u32[]{:S(2)}) collective-permute-start(bf16[256,128]{1,0:T(8,128)(2,1)} %refs_0_.5), channel_id=1, source_target_pairs={{0,3},{1,2},{2,1},{3,0},{4,7},{5,6},{6,5},{7,4},{8,11},{9,10},{10,... | collective-permute-start | bytes 196616 | tf_op jit(solution)/shard_map/ppermute | solution.py:275
  10.2 2.9 %collective-permute-done.2.refs_3_ = bf16[256,128]{1,0:T(8,128)(2,1)S(1)} collective-permute-done((bf16[256,128]{1,0:T(8,128)(2,1)}, bf16[256,128]{1,0:T(8,128)(2,1)S(1)}, u32[]{:S(2)}, u32[]{:S(2)}) %collective-permute-start.2) | collective-permute-done | bytes 65568 | tf_op jit(solution)/shard_map/ppermute | solution.py:275
  13.1 1.3 %collective-permute-start = (bf16[256,128]{1,0:T(8,128)(2,1)}, bf16[256,128]{1,0:T(8,128)(2,1)S(1)}, u32[]{:S(2)}, u32[]{:S(2)}) collective-permute-start(bf16[256,128]{1,0:T(8,128)(2,1)} %refs_0_.5), channel_id=1, source_target_pairs={{0,1},{1,0},{2,3},{3,2},{4,5},{5,4},{6,7},{7,6},{8,9},{9,8},{10,11... | collective-permute-start | bytes 196616 | tf_op jit(solution)/shard_map/ppermute | solution.py:275
  14.5 1.2 %collective-permute-done.1.refs_2_ = bf16[256,128]{1,0:T(8,128)(2,1)S(1)} collective-permute-done((bf16[256,128]{1,0:T(8,128)(2,1)}, bf16[256,128]{1,0:T(8,128)(2,1)S(1)}, u32[]{:S(2)}, u32[]{:S(2)}) %collective-permute-start.1) | collective-permute-done | bytes 65568 | tf_op jit(solution)/shard_map/ppermute | solution.py:275
  15.6 2.0 %collective-permute-done.refs_1_ = bf16[256,128]{1,0:T(8,128)(2,1)S(1)} collective-permute-done((bf16[256,128]{1,0:T(8,128)(2,1)}, bf16[256,128]{1,0:T(8,128)(2,1)S(1)}, u32[]{:S(2)}, u32[]{:S(2)}) %collective-permute-start) | collective-permute-done | bytes 65568 | tf_op jit(solution)/shard_map/ppermute | solution.py:275
  17.7 0.5 collective-permute-start.7
  18.3 0.4 collective-permute-start.9
  18.7 0.3 collective-permute-done.6.refs_5_.refs_4_
  19.0 0.2 collective-permute-done.7.refs_7_.refs_6_
  19.2 0.3 collective-permute-done.8.refs_9_.refs_8_
  19.7 0.8 copy-done
  20.6 0.8 copy-done.2
  21.4 7.0 %shard_map.67 = (f32[8,128]{1,0:T(8,128)S(1)}, f32[1024,128]{1,0:T(8,128)S(1)}) custom-call(bf16[256,128]{1,0:T(8,128)(2,1)S(1)} %copy-done, bf16[256,128]{1,0:T(8,128)(2,1)S(1)} %collective-permute-done.refs_1_, bf16[256,128]{1,0:T(8,128)(2,1)S(1)} %collective-permute-done.1.refs_2_, bf16[256,128]{1,0:T(8,128)(2,1)S(1)} %collective-permute-done.2.refs_3_, ...), custom_call_target="tpu_custom_call" | custom-call | flops 2147483648 | bytes 1937408 | tf_op jit(solution)/shard_map/pallas_call | solution.py:263
  28.4 4.1 %collective-permute-start.12 = (f32[8,128]{1,0:T(8,128)S(1)}, f32[8,128]{1,0:T(8,128)S(1)}, u32[]{:S(2)}, u32[]{:S(2)}) collective-permute-start(f32[8,128]{1,0:T(8,128)S(1)} %get-tuple-element.28.refs_4_), channel_id=1, source_target_pairs={{0,3},{1,2},{2,1},{3,0},{4,7},{5,6},{6,5},{7,4},{8,11},{9,10},{10,... | collective-permute-start | bytes 12296 | tf_op jit(solution)/shard_map/ppermute | solution.py:275
  32.5 0.6 collective-permute-start.10
  33.2 0.9 collective-permute-done.12.refs_7_
  34.1 2.9 %collective-permute-done.11.refs_6_ = f32[8,128]{1,0:T(8,128)S(1)} collective-permute-done((f32[8,128]{1,0:T(8,128)S(1)}, f32[8,128]{1,0:T(8,128)S(1)}, u32[]{:S(2)}, u32[]{:S(2)}) %collective-permute-start.11) | collective-permute-done | bytes 4128 | tf_op jit(solution)/shard_map/ppermute | solution.py:275
  37.1 0.5 shard_map.68
  37.7 1.2 %collective-permute-done.13.refs_1_ = f32[64,128]{1,0:T(8,128)S(1)} collective-permute-done((f32[64,128]{1,0:T(8,128)S(1)}, f32[64,128]{1,0:T(8,128)S(1)}, u32[]{:S(2)}, u32[]{:S(2)}) %collective-permute-start.13) | collective-permute-done | bytes 32800 | tf_op jit(solution)/shard_map/ppermute | solution.py:275
  38.9 1.5 %collective-permute-start.16 = (f32[64,128]{1,0:T(8,128)S(1)}, f32[64,128]{1,0:T(8,128)S(1)}, u32[]{:S(2)}, u32[]{:S(2)}) collective-permute-start(f32[64,128]{1,0:T(8,128)S(1)} %shard_map.69.refs_0_), channel_id=1, source_target_pairs={{0,3},{1,2},{2,1},{3,0},{4,7},{5,6},{6,5},{7,4},{8,11},{9,10},{10,... | collective-permute-start | bytes 98312 | tf_op jit(solution)/shard_map/ppermute | solution.py:275
  40.3 0.6 collective-permute-start.15
  41.0 2.3 %collective-permute-start.14 = (f32[64,128]{1,0:T(8,128)S(1)}, f32[64,128]{1,0:T(8,128)S(1)}, u32[]{:S(2)}, u32[]{:S(2)}) collective-permute-start(f32[64,128]{1,0:T(8,128)S(1)} %shard_map.69.refs_0_), channel_id=1, source_target_pairs={{0,1},{1,0},{2,3},{3,2},{4,5},{5,4},{6,7},{7,6},{8,9},{9,8},{10,11... | collective-permute-start | bytes 98312 | tf_op jit(solution)/shard_map/ppermute | solution.py:275
  43.3 1.6 %collective-permute-done.16.refs_3_ = f32[64,128]{1,0:T(8,128)S(1)} collective-permute-done((f32[64,128]{1,0:T(8,128)S(1)}, f32[64,128]{1,0:T(8,128)S(1)}, u32[]{:S(2)}, u32[]{:S(2)}) %collective-permute-start.16) | collective-permute-done | bytes 32800 | tf_op jit(solution)/shard_map/ppermute | solution.py:275
  44.9 0.4 collective-permute-done.15.refs_2_
  45.3 0.2 collective-permute-done.14.refs_1_
  45.6 2.5 %collective-permute-start.19 = (f32[64,128]{1,0:T(8,128)S(1)}, f32[64,128]{1,0:T(8,128)S(1)}, u32[]{:S(2)}, u32[]{:S(2)}) collective-permute-start(f32[64,128]{1,0:T(8,128)S(1)} %shard_map.70.refs_0_), channel_id=1, source_target_pairs={{0,24},{4,28},{8,16},{12,20},{16,8},{20,12},{24,0},{28,4},{1,25},{... | collective-permute-start | bytes 98312 | tf_op jit(solution)/shard_map/ppermute | solution.py:275
  48.1 0.5 collective-permute-start.18
  48.6 0.5 collective-permute-start.17
  49.1 1.3 %collective-permute-done.19.refs_3_ = f32[64,128]{1,0:T(8,128)S(1)} collective-permute-done((f32[64,128]{1,0:T(8,128)S(1)}, f32[64,128]{1,0:T(8,128)S(1)}, u32[]{:S(2)}, u32[]{:S(2)}) %collective-permute-start.19) | collective-permute-done | bytes 32800 | tf_op jit(solution)/shard_map/ppermute | solution.py:275
  50.5 1.5 %collective-permute-done.18.refs_2_ = f32[64,128]{1,0:T(8,128)S(1)} collective-permute-done((f32[64,128]{1,0:T(8,128)S(1)}, f32[64,128]{1,0:T(8,128)S(1)}, u32[]{:S(2)}, u32[]{:S(2)}) %collective-permute-start.18) | collective-permute-done | bytes 32800 | tf_op jit(solution)/shard_map/ppermute | solution.py:275
  52.0 0.5 collective-permute-done.17.refs_1_
  52.6 1.2 %collective-permute-done.20.refs_13_ = f32[64,128]{1,0:T(8,128)S(1)} collective-permute-done((f32[64,128]{1,0:T(8,128)S(1)}, f32[64,128]{1,0:T(8,128)S(1)}, u32[]{:S(2)}, u32[]{:S(2)}) %collective-permute-start.20) | collective-permute-done | bytes 32800 | tf_op jit(solution)/shard_map/ppermute | solution.py:275
  53.8 6.2 %shard_map.72 = (f32[128,128]{1,0:T(8,128)}, bf16[1024,128]{1,0:T(8,128)(2,1)S(1)}, f32[8,128]{1,0:T(8,128)S(1)}, f32[8,128]{1,0:T(8,128)S(1)}, bf16[1024,4096]{1,0:T(8,128)(2,1)S(1)}) custom-call(bf16[256,128]{1,0:T(8,128)(2,1)S(1)} %copy-done.1, bf16[256,128]{1,0:T(8,128)(2,1)S(1)} %collective-permute-done.refs_1_, ...), custom_call_target="tpu_custom_call" | custom-call | flops 1073741824 | bytes 10133504 | tf_op jit(solution)/shard_map/pallas_call | solution.py:263
  60.0 2.3 %collective-permute-start.23 = (f32[8,128]{1,0:T(8,128)S(1)}, f32[8,128]{1,0:T(8,128)S(1)}, u32[]{:S(2)}, u32[]{:S(2)}) collective-permute-start(f32[8,128]{1,0:T(8,128)S(1)} %get-tuple-element.36.refs_11_), channel_id=1, source_target_pairs={{0,3},{1,2},{2,1},{3,0},{4,7},{5,6},{6,5},{7,4},{8,11},{9,10},{10,... | collective-permute-start | bytes 12296 | tf_op jit(solution)/shard_map/ppermute | solution.py:275
  62.3 0.8 collective-permute-start.22
  63.1 1.3 %collective-permute-start.21 = (f32[8,128]{1,0:T(8,128)S(1)}, f32[8,128]{1,0:T(8,128)S(1)}, u32[]{:S(2)}, u32[]{:S(2)}) collective-permute-start(f32[8,128]{1,0:T(8,128)S(1)} %get-tuple-element.36.refs_11_), channel_id=1, source_target_pairs={{0,1},{1,0},{2,3},{3,2},{4,5},{5,4},{6,7},{7,6},{8,9},{9,8},{10,11... | collective-permute-start | bytes 12296 | tf_op jit(solution)/shard_map/ppermute | solution.py:275
  64.4 1.0 collective-permute-done.23.refs_14_
  65.4 1.4 %collective-permute-done.22.refs_13_ = f32[8,128]{1,0:T(8,128)S(1)} collective-permute-done((f32[8,128]{1,0:T(8,128)S(1)}, f32[8,128]{1,0:T(8,128)S(1)}, u32[]{:S(2)}, u32[]{:S(2)}) %collective-permute-start.22) | collective-permute-done | bytes 4128 | tf_op jit(solution)/shard_map/ppermute | solution.py:275
  66.8 6.6 %shard_map.73 = (f32[8,512]{1,0:T(8,128)S(1)}, f32[8,128]{1,0:T(8,128)}) custom-call(bf16[1024,128]{1,0:T(8,128)(2,1)S(1)} %get-tuple-element.33.refs_0_, bf16[1024,4096]{1,0:T(8,128)(2,1)S(1)} %get-tuple-element.34.refs_1_, f32[8,128]{1,0:T(8,128)S(1)} %get-tuple-element.35.refs_2_, bf16[528,128]{1,0:T(8,128)(2,1)S(1)} %fusion.1.refs_4_.refs_3_, ...), custom_call_target="tpu_custom_call" | custom-call | flops 67108864 | bytes 9773056 | tf_op jit(solution)/shard_map/pallas_call | solution.py:263
  73.5 1.2 %collective-permute-done.24.refs_1_ = f32[8,512]{1,0:T(8,128)S(1)} collective-permute-done((f32[8,512]{1,0:T(8,128)S(1)}, f32[8,512]{1,0:T(8,128)S(1)}, u32[]{:S(2)}, u32[]{:S(2)}) %collective-permute-start.24) | collective-permute-done | bytes 16416 | tf_op jit(solution)/shard_map/ppermute | solution.py:275
  74.7 1.6 %collective-permute-start.27 = (f32[8,512]{1,0:T(8,128)S(1)}, f32[8,512]{1,0:T(8,128)S(1)}, u32[]{:S(2)}, u32[]{:S(2)}) collective-permute-start(f32[8,512]{1,0:T(8,128)S(1)} %shard_map.74.refs_11_), channel_id=1, source_target_pairs={{0,24},{4,28},{8,16},{12,20},{16,8},{20,12},{24,0},{28,4},{1,25},{... | collective-permute-start | bytes 49160 | tf_op jit(solution)/shard_map/ppermute | solution.py:275
  76.2 0.5 collective-permute-start.26
  76.7 1.5 %collective-permute-start.25 = (f32[8,512]{1,0:T(8,128)S(1)}, f32[8,512]{1,0:T(8,128)S(1)}, u32[]{:S(2)}, u32[]{:S(2)}) collective-permute-start(f32[8,512]{1,0:T(8,128)S(1)} %shard_map.74.refs_11_), channel_id=1, source_target_pairs={{0,8},{4,12},{8,0},{12,4},{16,24},{20,28},{24,16},{28,20},{1,9},{5... | collective-permute-start | bytes 49160 | tf_op jit(solution)/shard_map/ppermute | solution.py:275
  78.2 1.1 %collective-permute-done.27.refs_14_ = f32[8,512]{1,0:T(8,128)S(1)} collective-permute-done((f32[8,512]{1,0:T(8,128)S(1)}, f32[8,512]{1,0:T(8,128)S(1)}, u32[]{:S(2)}, u32[]{:S(2)}) %collective-permute-start.27) | collective-permute-done | bytes 16416 | tf_op jit(solution)/shard_map/ppermute | solution.py:275
  79.4 0.6 collective-permute-done.26.refs_13_
  80.0 0.5 collective-permute-done.25.refs_12_
  80.5 7.7 %shard_map.75.refs_11_ = f32[8,128]{1,0:T(8,128)S(1)} custom-call(bf16[1024,128]{1,0:T(8,128)(2,1)S(1)} %get-tuple-element.33.refs_0_, bf16[1024,4096]{1,0:T(8,128)(2,1)S(1)} %get-tuple-element.34.refs_1_, f32[8,128]{1,0:T(8,128)S(1)} %get-tuple-element.35.refs_2_, bf16[528,128]{1,0:T(8,128)(2,1)S(1)} %fusion.1.refs_4_.refs_3_, ...), custom_call_target="tpu_custom_call" | custom-call | flops 67108864 | bytes 9805824 | tf_op jit(solution)/shard_map/pallas_call | solution.py:263
  88.1 1.5 %collective-permute-start.30 = (f32[8,128]{1,0:T(8,128)S(1)}, f32[8,128]{1,0:T(8,128)S(1)}, u32[]{:S(2)}, u32[]{:S(2)}) collective-permute-start(f32[8,128]{1,0:T(8,128)S(1)} %shard_map.75.refs_11_), channel_id=1, source_target_pairs={{0,3},{1,2},{2,1},{3,0},{4,7},{5,6},{6,5},{7,4},{8,11},{9,10},{10,... | collective-permute-start | bytes 12296 | tf_op jit(solution)/shard_map/ppermute | solution.py:275
  89.7 1.1 %collective-permute-start.29 = (f32[8,128]{1,0:T(8,128)S(1)}, f32[8,128]{1,0:T(8,128)S(1)}, u32[]{:S(2)}, u32[]{:S(2)}) collective-permute-start(f32[8,128]{1,0:T(8,128)S(1)} %shard_map.75.refs_11_), channel_id=1, source_target_pairs={{0,2},{1,3},{2,0},{3,1},{4,6},{5,7},{6,4},{7,5},{8,10},{9,11},{10,... | collective-permute-start | bytes 12296 | tf_op jit(solution)/shard_map/ppermute | solution.py:275
  90.8 1.8 %collective-permute-start.28 = (f32[8,128]{1,0:T(8,128)S(1)}, f32[8,128]{1,0:T(8,128)S(1)}, u32[]{:S(2)}, u32[]{:S(2)}) collective-permute-start(f32[8,128]{1,0:T(8,128)S(1)} %shard_map.75.refs_11_), channel_id=1, source_target_pairs={{0,1},{1,0},{2,3},{3,2},{4,5},{5,4},{6,7},{7,6},{8,9},{9,8},{10,11... | collective-permute-start | bytes 12296 | tf_op jit(solution)/shard_map/ppermute | solution.py:275
  92.6 1.0 collective-permute-done.30.refs_14_
  93.6 0.6 collective-permute-done.29.refs_13_
  94.2 0.2 collective-permute-done.28.refs_12_
  94.4 6.6 %shard_map.76 = (f32[4,1,512]{2,1,0:T(1,128)S(1)}, f32[4,1,512]{2,1,0:T(1,128)S(1)}, f32[8,128]{1,0:T(8,128)}) custom-call(bf16[1024,128]{1,0:T(8,128)(2,1)S(1)} %get-tuple-element.33.refs_0_, bf16[1024,4096]{1,0:T(8,128)(2,1)S(1)} %get-tuple-element.34.refs_1_, f32[8,128]{1,0:T(8,128)S(1)} %get-tuple-element.35.refs_2_, ...), custom_call_target="tpu_custom_call" | custom-call | flops 67108864 | bytes 9773056 | tf_op jit(solution)/shard_map/pallas_call | solution.py:263
  101.0 1.2 %collective-permute-done.31.y_ref = f32[4,1,512]{2,1,0:T(1,128)S(1)} collective-permute-done((f32[4,1,512]{2,1,0:T(1,128)S(1)}, f32[4,1,512]{2,1,0:T(1,128)S(1)}, u32[]{:S(2)}, u32[]{:S(2)}) %collective-permute-start.31) | collective-permute-done | bytes 8224 | tf_op jit(solution)/shard_map/ppermute | solution.py:275
  102.2 1.6 %collective-permute-start.32 = (f32[1,512]{1,0:T(1,128)S(1)}, f32[1,512]{1,0:T(1,128)S(1)}, u32[]{:S(2)}, u32[]{:S(2)}) collective-permute-start(f32[1,512]{1,0:T(1,128)S(1)} %get-tuple-element.42), channel_id=1, source_target_pairs={{0,8},{4,12},{8,0},{12,4},{16,24},{20,28},{24,16},{28,20},{1,9},{5... | collective-permute-start | bytes 6152 | tf_op jit(solution)/shard_map/ppermute | solution.py:275
  103.8 1.5 %collective-permute-start.33 = (f32[1,512]{1,0:T(1,128)S(1)}, f32[1,512]{1,0:T(1,128)S(1)}, u32[]{:S(2)}, u32[]{:S(2)}) collective-permute-start(f32[1,512]{1,0:T(1,128)S(1)} %get-tuple-element.43), channel_id=1, source_target_pairs={{0,16},{4,20},{8,24},{12,28},{16,0},{20,4},{24,8},{28,12},{1,17},{... | collective-permute-start | bytes 6152 | tf_op jit(solution)/shard_map/ppermute | solution.py:275
  105.3 0.5 collective-permute-start.34
  105.9 1.5 %collective-permute-done.33.refs_2_ = f32[1,512]{1,0:T(1,128)S(1)} collective-permute-done((f32[1,512]{1,0:T(1,128)S(1)}, f32[1,512]{1,0:T(1,128)S(1)}, u32[]{:S(2)}, u32[]{:S(2)}) %collective-permute-start.33) | collective-permute-done | bytes 2080 | tf_op jit(solution)/shard_map/ppermute | solution.py:275
  107.4 2.4 %collective-permute-done.34.refs_3_ = f32[1,512]{1,0:T(1,128)S(1)} collective-permute-done((f32[1,512]{1,0:T(1,128)S(1)}, f32[1,512]{1,0:T(1,128)S(1)}, u32[]{:S(2)}, u32[]{:S(2)}) %collective-permute-start.34) | collective-permute-done | bytes 2080 | tf_op jit(solution)/shard_map/ppermute | solution.py:275
  109.8 0.6 shard_map.78
  (25 shorter events, 0.8 us)
Async XLA Ops:
  0.6 53.2 %copy-start.1 = (bf16[256,128]{1,0:T(8,128)(2,1)S(1)}, bf16[256,128]{1,0:T(8,128)(2,1)}, u32[]{:S(2)}) copy-start(bf16[256,128]{1,0:T(8,128)(2,1)} %refs_0_.5) | copy-start | bytes 196612
  1.6 16.0 %collective-permute-start.5 = (bf16[528,128]{1,0:T(8,128)(2,1)S(1)}, bf16[528,128]{1,0:T(8,128)(2,1)S(1)}, u32[]{:S(2)}, u32[]{:S(2)}) collective-permute-start(bf16[528,128]{1,0:T(8,128)(2,1)S(1)} %fusion.1.refs_4_.refs_3_), channel_id=1, source_target_pairs={{0,24},{4,28},{8,16},{12,20},{16,8},{20,12},{24,0},{28,4},{1,25},{... | collective-permute-start | bytes 405512 | tf_op jit(solution)/shard_map/ppermute | solution.py:275
  5.6 12.0 %collective-permute-start.4 = (bf16[528,128]{1,0:T(8,128)(2,1)S(1)}, bf16[528,128]{1,0:T(8,128)(2,1)S(1)}, u32[]{:S(2)}, u32[]{:S(2)}) collective-permute-start(bf16[528,128]{1,0:T(8,128)(2,1)S(1)} %fusion.1.refs_4_.refs_3_), channel_id=1, source_target_pairs={{0,16},{4,20},{8,24},{12,28},{16,0},{20,4},{24,8},{28,12},{1,17},{... | collective-permute-start | bytes 405512 | tf_op jit(solution)/shard_map/ppermute | solution.py:275
  6.1 11.5 %collective-permute-start.3 = (bf16[528,128]{1,0:T(8,128)(2,1)S(1)}, bf16[528,128]{1,0:T(8,128)(2,1)S(1)}, u32[]{:S(2)}, u32[]{:S(2)}) collective-permute-start(bf16[528,128]{1,0:T(8,128)(2,1)S(1)} %fusion.1.refs_4_.refs_3_), channel_id=1, source_target_pairs={{0,8},{4,12},{8,0},{12,4},{16,24},{20,28},{24,16},{28,20},{1,9},{5... | collective-permute-start | bytes 405512 | tf_op jit(solution)/shard_map/ppermute | solution.py:275
  6.2 6.9 %collective-permute-start.2 = (bf16[256,128]{1,0:T(8,128)(2,1)}, bf16[256,128]{1,0:T(8,128)(2,1)S(1)}, u32[]{:S(2)}, u32[]{:S(2)}) collective-permute-start(bf16[256,128]{1,0:T(8,128)(2,1)} %refs_0_.5), channel_id=1, source_target_pairs={{0,3},{1,2},{2,1},{3,0},{4,7},{5,6},{6,5},{7,4},{8,11},{9,10},{10,... | collective-permute-start | bytes 196616 | tf_op jit(solution)/shard_map/ppermute | solution.py:275
  10.2 5.4 %collective-permute-start.1 = (bf16[256,128]{1,0:T(8,128)(2,1)}, bf16[256,128]{1,0:T(8,128)(2,1)S(1)}, u32[]{:S(2)}, u32[]{:S(2)}) collective-permute-start(bf16[256,128]{1,0:T(8,128)(2,1)} %refs_0_.5), channel_id=1, source_target_pairs={{0,2},{1,3},{2,0},{3,1},{4,6},{5,7},{6,4},{7,5},{8,10},{9,11},{10,... | collective-permute-start | bytes 196616 | tf_op jit(solution)/shard_map/ppermute | solution.py:275
  13.1 4.5 %collective-permute-start = (bf16[256,128]{1,0:T(8,128)(2,1)}, bf16[256,128]{1,0:T(8,128)(2,1)S(1)}, u32[]{:S(2)}, u32[]{:S(2)}) collective-permute-start(bf16[256,128]{1,0:T(8,128)(2,1)} %refs_0_.5), channel_id=1, source_target_pairs={{0,1},{1,0},{2,3},{3,2},{4,5},{5,4},{6,7},{7,6},{8,9},{9,8},{10,11... | collective-permute-start | bytes 196616 | tf_op jit(solution)/shard_map/ppermute | solution.py:275
  17.6 1.4 %collective-permute-start.6 = (bf16[528,128]{1,0:T(8,128)(2,1)S(1)}, bf16[528,128]{1,0:T(8,128)(2,1)S(1)}, u32[]{:S(2)}, u32[]{:S(2)}) collective-permute-start(bf16[528,128]{1,0:T(8,128)(2,1)S(1)} %fusion.1.refs_4_.refs_3_), channel_id=1, source_target_pairs={{0,4},{4,0},{8,12},{12,8},{16,20},{20,16},{24,28},{28,24},{1,5},{5... | collective-permute-start | bytes 405512 | tf_op jit(solution)/shard_map/ppermute | solution.py:275
  17.7 1.5 %collective-permute-start.7 = (bf16[528,128]{1,0:T(8,128)(2,1)S(1)}, bf16[528,128]{1,0:T(8,128)(2,1)S(1)}, u32[]{:S(2)}, u32[]{:S(2)}) collective-permute-start(bf16[528,128]{1,0:T(8,128)(2,1)S(1)} %collective-permute-done.3.refs_6_.refs_5_), channel_id=1, source_target_pairs={{0,4},{4,0},{8,12},{12,8},{16,20},{20,16},{24,28},{28,24},{1,5},{5... | collective-permute-start | bytes 405512 | tf_op jit(solution)/shard_map/ppermute | solution.py:275
  18.2 1.4 %collective-permute-start.8 = (bf16[528,128]{1,0:T(8,128)(2,1)S(1)}, bf16[528,128]{1,0:T(8,128)(2,1)S(1)}, u32[]{:S(2)}, u32[]{:S(2)}) collective-permute-start(bf16[528,128]{1,0:T(8,128)(2,1)S(1)} %collective-permute-done.4.refs_8_.refs_7_), channel_id=1, source_target_pairs={{0,4},{4,0},{8,12},{12,8},{16,20},{20,16},{24,28},{28,24},{1,5},{5... | collective-permute-start | bytes 405512 | tf_op jit(solution)/shard_map/ppermute | solution.py:275
  18.3 1.5 %collective-permute-start.9 = (bf16[528,128]{1,0:T(8,128)(2,1)S(1)}, bf16[528,128]{1,0:T(8,128)(2,1)S(1)}, u32[]{:S(2)}, u32[]{:S(2)}) collective-permute-start(bf16[528,128]{1,0:T(8,128)(2,1)S(1)} %collective-permute-done.5.refs_10_.refs_9_), channel_id=1, source_target_pairs={{0,4},{4,0},{8,12},{12,8},{16,20},{20,16},{24,28},{28,24},{1,5},{5... | collective-permute-start | bytes 405512 | tf_op jit(solution)/shard_map/ppermute | solution.py:275
  19.7 0.8 copy-start
  20.6 0.8 copy-start.2
  28.4 5.7 %collective-permute-start.12 = (f32[8,128]{1,0:T(8,128)S(1)}, f32[8,128]{1,0:T(8,128)S(1)}, u32[]{:S(2)}, u32[]{:S(2)}) collective-permute-start(f32[8,128]{1,0:T(8,128)S(1)} %get-tuple-element.28.refs_4_), channel_id=1, source_target_pairs={{0,3},{1,2},{2,1},{3,0},{4,7},{5,6},{6,5},{7,4},{8,11},{9,10},{10,... | collective-permute-start | bytes 12296 | tf_op jit(solution)/shard_map/ppermute | solution.py:275
  32.5 4.5 %collective-permute-start.11 = (f32[8,128]{1,0:T(8,128)S(1)}, f32[8,128]{1,0:T(8,128)S(1)}, u32[]{:S(2)}, u32[]{:S(2)}) collective-permute-start(f32[8,128]{1,0:T(8,128)S(1)} %get-tuple-element.28.refs_4_), channel_id=1, source_target_pairs={{0,2},{1,3},{2,0},{3,1},{4,6},{5,7},{6,4},{7,5},{8,10},{9,11},{10,... | collective-permute-start | bytes 12296 | tf_op jit(solution)/shard_map/ppermute | solution.py:275
  32.5 4.5 %collective-permute-start.10 = (f32[8,128]{1,0:T(8,128)S(1)}, f32[8,128]{1,0:T(8,128)S(1)}, u32[]{:S(2)}, u32[]{:S(2)}) collective-permute-start(f32[8,128]{1,0:T(8,128)S(1)} %get-tuple-element.28.refs_4_), channel_id=1, source_target_pairs={{0,1},{1,0},{2,3},{3,2},{4,5},{5,4},{6,7},{7,6},{8,9},{9,8},{10,11... | collective-permute-start | bytes 12296 | tf_op jit(solution)/shard_map/ppermute | solution.py:275
  37.6 1.3 %collective-permute-start.13 = (f32[64,128]{1,0:T(8,128)S(1)}, f32[64,128]{1,0:T(8,128)S(1)}, u32[]{:S(2)}, u32[]{:S(2)}) collective-permute-start(f32[64,128]{1,0:T(8,128)S(1)} %get-tuple-element.31), channel_id=1, source_target_pairs={{0,4},{4,0},{8,12},{12,8},{16,20},{20,16},{24,28},{28,24},{1,5},{5... | collective-permute-start | bytes 98312 | tf_op jit(solution)/shard_map/ppermute | solution.py:275
  38.9 6.0 %collective-permute-start.16 = (f32[64,128]{1,0:T(8,128)S(1)}, f32[64,128]{1,0:T(8,128)S(1)}, u32[]{:S(2)}, u32[]{:S(2)}) collective-permute-start(f32[64,128]{1,0:T(8,128)S(1)} %shard_map.69.refs_0_), channel_id=1, source_target_pairs={{0,3},{1,2},{2,1},{3,0},{4,7},{5,6},{6,5},{7,4},{8,11},{9,10},{10,... | collective-permute-start | bytes 98312 | tf_op jit(solution)/shard_map/ppermute | solution.py:275
  40.3 5.0 %collective-permute-start.15 = (f32[64,128]{1,0:T(8,128)S(1)}, f32[64,128]{1,0:T(8,128)S(1)}, u32[]{:S(2)}, u32[]{:S(2)}) collective-permute-start(f32[64,128]{1,0:T(8,128)S(1)} %shard_map.69.refs_0_), channel_id=1, source_target_pairs={{0,2},{1,3},{2,0},{3,1},{4,6},{5,7},{6,4},{7,5},{8,10},{9,11},{10,... | collective-permute-start | bytes 98312 | tf_op jit(solution)/shard_map/ppermute | solution.py:275
  41.0 4.6 %collective-permute-start.14 = (f32[64,128]{1,0:T(8,128)S(1)}, f32[64,128]{1,0:T(8,128)S(1)}, u32[]{:S(2)}, u32[]{:S(2)}) collective-permute-start(f32[64,128]{1,0:T(8,128)S(1)} %shard_map.69.refs_0_), channel_id=1, source_target_pairs={{0,1},{1,0},{2,3},{3,2},{4,5},{5,4},{6,7},{7,6},{8,9},{9,8},{10,11... | collective-permute-start | bytes 98312 | tf_op jit(solution)/shard_map/ppermute | solution.py:275
  45.6 4.9 %collective-permute-start.19 = (f32[64,128]{1,0:T(8,128)S(1)}, f32[64,128]{1,0:T(8,128)S(1)}, u32[]{:S(2)}, u32[]{:S(2)}) collective-permute-start(f32[64,128]{1,0:T(8,128)S(1)} %shard_map.70.refs_0_), channel_id=1, source_target_pairs={{0,24},{4,28},{8,16},{12,20},{16,8},{20,12},{24,0},{28,4},{1,25},{... | collective-permute-start | bytes 98312 | tf_op jit(solution)/shard_map/ppermute | solution.py:275
  48.1 3.9 %collective-permute-start.18 = (f32[64,128]{1,0:T(8,128)S(1)}, f32[64,128]{1,0:T(8,128)S(1)}, u32[]{:S(2)}, u32[]{:S(2)}) collective-permute-start(f32[64,128]{1,0:T(8,128)S(1)} %shard_map.70.refs_0_), channel_id=1, source_target_pairs={{0,16},{4,20},{8,24},{12,28},{16,0},{20,4},{24,8},{28,12},{1,17},{... | collective-permute-start | bytes 98312 | tf_op jit(solution)/shard_map/ppermute | solution.py:275
  48.6 3.9 %collective-permute-start.17 = (f32[64,128]{1,0:T(8,128)S(1)}, f32[64,128]{1,0:T(8,128)S(1)}, u32[]{:S(2)}, u32[]{:S(2)}) collective-permute-start(f32[64,128]{1,0:T(8,128)S(1)} %shard_map.70.refs_0_), channel_id=1, source_target_pairs={{0,8},{4,12},{8,0},{12,4},{16,24},{20,28},{24,16},{28,20},{1,9},{5... | collective-permute-start | bytes 98312 | tf_op jit(solution)/shard_map/ppermute | solution.py:275
  52.5 1.3 %collective-permute-start.20 = (f32[64,128]{1,0:T(8,128)S(1)}, f32[64,128]{1,0:T(8,128)S(1)}, u32[]{:S(2)}, u32[]{:S(2)}) collective-permute-start(f32[64,128]{1,0:T(8,128)S(1)} %shard_map.71.refs_12_), channel_id=1, source_target_pairs={{0,4},{4,0},{8,12},{12,8},{16,20},{20,16},{24,28},{28,24},{1,5},{5... | collective-permute-start | bytes 98312 | tf_op jit(solution)/shard_map/ppermute | solution.py:275
  60.0 5.4 %collective-permute-start.23 = (f32[8,128]{1,0:T(8,128)S(1)}, f32[8,128]{1,0:T(8,128)S(1)}, u32[]{:S(2)}, u32[]{:S(2)}) collective-permute-start(f32[8,128]{1,0:T(8,128)S(1)} %get-tuple-element.36.refs_11_), channel_id=1, source_target_pairs={{0,3},{1,2},{2,1},{3,0},{4,7},{5,6},{6,5},{7,4},{8,11},{9,10},{10,... | collective-permute-start | bytes 12296 | tf_op jit(solution)/shard_map/ppermute | solution.py:275
  62.3 4.5 %collective-permute-start.22 = (f32[8,128]{1,0:T(8,128)S(1)}, f32[8,128]{1,0:T(8,128)S(1)}, u32[]{:S(2)}, u32[]{:S(2)}) collective-permute-start(f32[8,128]{1,0:T(8,128)S(1)} %get-tuple-element.36.refs_11_), channel_id=1, source_target_pairs={{0,2},{1,3},{2,0},{3,1},{4,6},{5,7},{6,4},{7,5},{8,10},{9,11},{10,... | collective-permute-start | bytes 12296 | tf_op jit(solution)/shard_map/ppermute | solution.py:275
  63.1 3.7 %collective-permute-start.21 = (f32[8,128]{1,0:T(8,128)S(1)}, f32[8,128]{1,0:T(8,128)S(1)}, u32[]{:S(2)}, u32[]{:S(2)}) collective-permute-start(f32[8,128]{1,0:T(8,128)S(1)} %get-tuple-element.36.refs_11_), channel_id=1, source_target_pairs={{0,1},{1,0},{2,3},{3,2},{4,5},{5,4},{6,7},{7,6},{8,9},{9,8},{10,11... | collective-permute-start | bytes 12296 | tf_op jit(solution)/shard_map/ppermute | solution.py:275
  73.5 1.2 %collective-permute-start.24 = (f32[8,512]{1,0:T(8,128)S(1)}, f32[8,512]{1,0:T(8,128)S(1)}, u32[]{:S(2)}, u32[]{:S(2)}) collective-permute-start(f32[8,512]{1,0:T(8,128)S(1)} %get-tuple-element.37.refs_0_), channel_id=1, source_target_pairs={{0,4},{4,0},{8,12},{12,8},{16,20},{20,16},{24,28},{28,24},{1,5},{5... | collective-permute-start | bytes 49160 | tf_op jit(solution)/shard_map/ppermute | solution.py:275
  74.7 4.7 %collective-permute-start.27 = (f32[8,512]{1,0:T(8,128)S(1)}, f32[8,512]{1,0:T(8,128)S(1)}, u32[]{:S(2)}, u32[]{:S(2)}) collective-permute-start(f32[8,512]{1,0:T(8,128)S(1)} %shard_map.74.refs_11_), channel_id=1, source_target_pairs={{0,24},{4,28},{8,16},{12,20},{16,8},{20,12},{24,0},{28,4},{1,25},{... | collective-permute-start | bytes 49160 | tf_op jit(solution)/shard_map/ppermute | solution.py:275
  76.2 3.7 %collective-permute-start.26 = (f32[8,512]{1,0:T(8,128)S(1)}, f32[8,512]{1,0:T(8,128)S(1)}, u32[]{:S(2)}, u32[]{:S(2)}) collective-permute-start(f32[8,512]{1,0:T(8,128)S(1)} %shard_map.74.refs_11_), channel_id=1, source_target_pairs={{0,16},{4,20},{8,24},{12,28},{16,0},{20,4},{24,8},{28,12},{1,17},{... | collective-permute-start | bytes 49160 | tf_op jit(solution)/shard_map/ppermute | solution.py:275
  76.7 3.7 %collective-permute-start.25 = (f32[8,512]{1,0:T(8,128)S(1)}, f32[8,512]{1,0:T(8,128)S(1)}, u32[]{:S(2)}, u32[]{:S(2)}) collective-permute-start(f32[8,512]{1,0:T(8,128)S(1)} %shard_map.74.refs_11_), channel_id=1, source_target_pairs={{0,8},{4,12},{8,0},{12,4},{16,24},{20,28},{24,16},{28,20},{1,9},{5... | collective-permute-start | bytes 49160 | tf_op jit(solution)/shard_map/ppermute | solution.py:275
  88.1 5.4 %collective-permute-start.30 = (f32[8,128]{1,0:T(8,128)S(1)}, f32[8,128]{1,0:T(8,128)S(1)}, u32[]{:S(2)}, u32[]{:S(2)}) collective-permute-start(f32[8,128]{1,0:T(8,128)S(1)} %shard_map.75.refs_11_), channel_id=1, source_target_pairs={{0,3},{1,2},{2,1},{3,0},{4,7},{5,6},{6,5},{7,4},{8,11},{9,10},{10,... | collective-permute-start | bytes 12296 | tf_op jit(solution)/shard_map/ppermute | solution.py:275
  89.7 4.5 %collective-permute-start.29 = (f32[8,128]{1,0:T(8,128)S(1)}, f32[8,128]{1,0:T(8,128)S(1)}, u32[]{:S(2)}, u32[]{:S(2)}) collective-permute-start(f32[8,128]{1,0:T(8,128)S(1)} %shard_map.75.refs_11_), channel_id=1, source_target_pairs={{0,2},{1,3},{2,0},{3,1},{4,6},{5,7},{6,4},{7,5},{8,10},{9,11},{10,... | collective-permute-start | bytes 12296 | tf_op jit(solution)/shard_map/ppermute | solution.py:275
  90.8 3.6 %collective-permute-start.28 = (f32[8,128]{1,0:T(8,128)S(1)}, f32[8,128]{1,0:T(8,128)S(1)}, u32[]{:S(2)}, u32[]{:S(2)}) collective-permute-start(f32[8,128]{1,0:T(8,128)S(1)} %shard_map.75.refs_11_), channel_id=1, source_target_pairs={{0,1},{1,0},{2,3},{3,2},{4,5},{5,4},{6,7},{7,6},{8,9},{9,8},{10,11... | collective-permute-start | bytes 12296 | tf_op jit(solution)/shard_map/ppermute | solution.py:275
  101.0 1.2 %collective-permute-start.31 = (f32[4,1,512]{2,1,0:T(1,128)S(1)}, f32[4,1,512]{2,1,0:T(1,128)S(1)}, u32[]{:S(2)}, u32[]{:S(2)}) collective-permute-start(f32[4,1,512]{2,1,0:T(1,128)S(1)} %get-tuple-element.40), channel_id=1, source_target_pairs={{0,4},{4,0},{8,12},{12,8},{16,20},{20,16},{24,28},{28,24},{1,5},{5... | collective-permute-start | bytes 24584 | tf_op jit(solution)/shard_map/ppermute | solution.py:275
  102.2 3.7 %collective-permute-start.32 = (f32[1,512]{1,0:T(1,128)S(1)}, f32[1,512]{1,0:T(1,128)S(1)}, u32[]{:S(2)}, u32[]{:S(2)}) collective-permute-start(f32[1,512]{1,0:T(1,128)S(1)} %get-tuple-element.42), channel_id=1, source_target_pairs={{0,8},{4,12},{8,0},{12,4},{16,24},{20,28},{24,16},{28,20},{1,9},{5... | collective-permute-start | bytes 6152 | tf_op jit(solution)/shard_map/ppermute | solution.py:275
  103.8 3.6 %collective-permute-start.33 = (f32[1,512]{1,0:T(1,128)S(1)}, f32[1,512]{1,0:T(1,128)S(1)}, u32[]{:S(2)}, u32[]{:S(2)}) collective-permute-start(f32[1,512]{1,0:T(1,128)S(1)} %get-tuple-element.43), channel_id=1, source_target_pairs={{0,16},{4,20},{8,24},{12,28},{16,0},{20,4},{24,8},{28,12},{1,17},{... | collective-permute-start | bytes 6152 | tf_op jit(solution)/shard_map/ppermute | solution.py:275
  105.3 4.5 %collective-permute-start.34 = (f32[1,512]{1,0:T(1,128)S(1)}, f32[1,512]{1,0:T(1,128)S(1)}, u32[]{:S(2)}, u32[]{:S(2)}) collective-permute-start(f32[1,512]{1,0:T(1,128)S(1)} %get-tuple-element.44), channel_id=1, source_target_pairs={{0,24},{4,28},{8,16},{12,20},{16,8},{20,12},{24,0},{28,4},{1,25},{... | collective-permute-start | bytes 6152 | tf_op jit(solution)/shard_map/ppermute | solution.py:275

commit v6 on v5

v6 whole, which is shorter than its diff:
```python
import functools
import math

import jax
import jax.numpy as jnp
from jax import lax
from jax.experimental import pallas as pl
from jax.experimental.pallas import tpu as pltpu
from jax.sharding import PartitionSpec as P

ITERS = 2
LANES = 128
SUB = 16
SMALLEST = 1e-16
LARGEST = 1e12
NT_DIMS = (((1,), (1,)), ((), ()))
TN_DIMS = (((0,), (0,)), ((), ()))


def split3(x):
    high = x.astype(jnp.bfloat16)
    rest = x - high.astype(jnp.float32)
    mid = rest.astype(jnp.bfloat16)
    low = (rest - mid.astype(jnp.float32)).astype(jnp.bfloat16)
    return high, mid, low


def project4(rows, matrix):
    total = None
    for part in reversed(split3(matrix)):
        term = jnp.dot(rows, part, preferred_element_type=jnp.float32)
        total = term if total is None else total + term
    return (total.astype(jnp.bfloat16).astype(jnp.float32) * 4.0).astype(jnp.bfloat16)


def lane_fold(op, x):
    parts = [x[:, i : i + LANES] for i in range(0, x.shape[1], LANES)]
    return functools.reduce(op, parts)


def as_lanes(column):
    return jnp.broadcast_to(column, (LANES, LANES)).T[0:1, :]


def as_rows(lanes):
    return jnp.broadcast_to(lanes, (LANES, LANES)).T


def tree(op, parts):
    while len(parts) > 1:
        parts = [op(parts[i], parts[i + 1]) for i in range(0, len(parts), 2)]
    return parts[0]


def log_sum(parts):
    top = functools.reduce(jnp.maximum, parts)
    return top + jnp.log(tree(jnp.add, [jnp.exp(p - top) for p in parts]))


def within(masses):
    low = jnp.min(functools.reduce(jnp.minimum, masses))
    high = jnp.max(functools.reduce(jnp.maximum, masses))
    return jnp.logical_and(low > SMALLEST, high < LARGEST)


def block_of(t_ref, g, width):
    return t_ref[g * width : (g + 1) * width, :LANES]


def shifted_rows(a_ref, t_ref, pot_ref, aug_ref, lse_ref, top_ref, mass_ref, e_ref, carried_ref=None):
    c = lax.axis_index("col")
    width = pot_ref.shape[1]
    blocks = pot_ref.shape[0]
    steps = a_ref.shape[0] // LANES
    per = steps // lax.axis_size("col")
    lane = lax.broadcasted_iota(jnp.int32, (LANES, LANES), 1)

    def row(i):
        return pl.ds((c ^ (i // per)) * per + i % per, 1)

    for i in range(steps):
        at = slice(i * LANES, (i + 1) * LANES)
        a = a_ref[at, :]
        s = lax.dot_general(a, block_of(t_ref, 0, width), NT_DIMS, preferred_element_type=jnp.float32)
        top = jnp.max(lane_fold(jnp.maximum, s + pot_ref[0:1, :]), axis=1, keepdims=True)
        top = top.astype(jnp.bfloat16).astype(jnp.float32)
        aug_ref[at, :LANES] = a
        aug_ref[at, LANES:] = jnp.where(lane == 0, 1.0, jnp.where(lane == 1, -top, 0.0)).astype(jnp.bfloat16)
        top_ref[row(i), :] = as_lanes(top)
    for i in range(steps + 1):
        mass, carried = None, None
        for g in range(blocks):
            cols = slice(g * width, (g + 1) * width)
            if i < steps:
                at = slice(i * LANES, (i + 1) * LANES)
                s = lax.dot_general(aug_ref[at, :], t_ref[cols, :], NT_DIMS, preferred_element_type=jnp.float32)
                e = jnp.exp(s)
                m = lane_fold(jnp.add, e)
                mass = m if mass is None else mass + m
                e_ref[at, cols] = e.astype(jnp.bfloat16)
            if i > 0 and carried_ref is not None:
                before = slice((i - 1) * LANES, i * LANES)
                d = jnp.dot(e_ref[before, cols], block_of(t_ref, g, width), preferred_element_type=jnp.float32)
                carried = d if carried is None else carried + d
        if i > 0 and carried_ref is not None:
            carried_ref[before, :] = carried / last_mass
        if i < steps:
            last_mass = jnp.sum(mass, axis=1, keepdims=True)
            mass_ref[row(i), :] = as_lanes(last_mass)
    lse_ref[...] = top_ref[...] + jnp.log(mass_ref[...])
    return within([mass_ref[...]])


def exact_rows(a_ref, t_ref, column, scores, lse_ref, top_ref=None, e_ref=None, carried_ref=None):
    c = lax.axis_index("col")
    steps = a_ref.shape[0] // LANES
    per = steps // lax.axis_size("col")
    width = column[0].shape[1]

    @pl.loop(0, steps)
    def _(i):
        rows = pl.ds(pl.multiple_of(i * LANES, LANES), LANES)
        top = None
        for g in range(len(column)):
            t = block_of(t_ref, g, width)
            s = column[g] + lax.dot_general(a_ref[rows, :], t, NT_DIMS, preferred_element_type=jnp.float32)
            scores[:, g * width : (g + 1) * width] = s
            m = lane_fold(jnp.maximum, s)
            top = m if top is None else jnp.maximum(top, m)
        top = jnp.max(top, axis=1, keepdims=True)
        mass, carried = None, None
        for g in range(len(column)):
            cols = slice(g * width, (g + 1) * width)
            e = jnp.exp(scores[:, cols] - top)
            m = lane_fold(jnp.add, e)
            mass = m if mass is None else mass + m
            if e_ref is not None:
                e_ref[rows, cols] = e.astype(jnp.bfloat16)
            if carried_ref is not None:
                t = block_of(t_ref, g, width)
                d = jnp.dot(e.astype(jnp.bfloat16), t, preferred_element_type=jnp.float32)
                carried = d if carried is None else carried + d
        mass = jnp.sum(mass, axis=1, keepdims=True)
        row = pl.ds((c ^ (i // per)) * per + i % per, 1)
        lse_ref[row, :] = as_lanes(top + jnp.log(mass))
        if top_ref is not None:
            top_ref[row, :] = as_lanes(top)
        if carried_ref is not None:
            carried_ref[rows, :] = carried / mass


def project_kernel(ns, *refs):
    s_refs, moment_ref, a_ref = refs[:ns], refs[ns], refs[ns + 1]
    piece = s_refs[0].shape[0]
    for k in range(ns):
        a_ref[k * piece : (k + 1) * piece, :] = project4(s_refs[k][...], moment_ref[...])


def couple_kernel(nt, width, *refs):
    a_ref, t_refs = refs[0], refs[1 : 1 + nt]
    lse_ref, carried_ref, t_ref, pot_ref, top_ref, mass_ref, e_ref, aug_ref, scores = refs[1 + nt :]
    lane = lax.broadcasted_iota(jnp.int32, (LANES, LANES), 1)
    for g in range(nt):
        t_ref[g * width : (g + 1) * width, :LANES] = t_refs[g][:width, :]
        potential = t_refs[g][width:, :].astype(jnp.float32)
        for j in range(width // LANES):
            row = potential[j : j + 1, :]
            at = g * width + j * LANES
            added = jnp.where(lane == 0, as_rows(row), jnp.where(lane == 1, 1.0, 0.0))
            t_ref[at : at + LANES, LANES:] = added.astype(jnp.bfloat16)
            pot_ref[g : g + 1, j * LANES : (j + 1) * LANES] = row
    fine = shifted_rows(a_ref, t_ref, pot_ref, aug_ref, lse_ref, top_ref, mass_ref, e_ref, carried_ref)

    @pl.when(jnp.logical_not(fine))
    def _():
        column = [pot_ref[g : g + 1, :] for g in range(nt)]
        exact_rows(a_ref, t_ref, column, scores, lse_ref, None, None, carried_ref)


def moment_kernel(ns, rows_total, *refs):
    s_refs, l_refs, carried_ref = refs[:ns], refs[ns : 2 * ns], refs[2 * ns]
    keep_ref, send_ref, weight_ref, total_ref = refs[2 * ns + 1 :]
    c, r = lax.axis_index("col"), lax.axis_index("row")
    piece = s_refs[0].shape[0]
    per = piece // LANES
    shift = log_sum([l[...] for l in l_refs])
    weight_ref[...] = jnp.exp(l_refs[0][...] - shift) * (1.0 / rows_total)
    total = None
    for k in range(ns):
        for j in range(per):
            w = as_rows(weight_ref[pl.ds((c ^ k) * per + j, 1), :])
            at = (k * per + j) * LANES
            x = carried_ref[at : at + LANES, :] * w
            s = s_refs[k][j * LANES : (j + 1) * LANES, :]
            for part in reversed(split3(x)):
                term = lax.dot_general(s, part, TN_DIMS, preferred_element_type=jnp.float32)
                total = term if total is None else total + term
    total_ref[...] = total
    half = keep_ref.shape[0]
    keep_ref[...] = total_ref[pl.ds(pl.multiple_of((r % 2) * half, half), half), :]
    send_ref[...] = total_ref[pl.ds(pl.multiple_of((1 - r % 2) * half, half), half), :]


def add_kernel(*refs):
    refs[-1][...] = tree(jnp.add, [r[...] for r in refs[:-1]])


def log_sum_kernel(*refs):
    refs[-1][...] = log_sum([r[...] for r in refs[:-1]])


def first_rows_kernel(ns, *refs):
    s_refs, t_ref, pot_ref, m_refs = refs[:ns], refs[ns], refs[ns + 1], refs[ns + 2 : ns + 4]
    moment_ref, a_ref, lse_ref, top_ref, e_ref, mass_ref, aug_ref, scores = refs[ns + 4 :]
    r = lax.axis_index("row")
    piece, half = s_refs[0].shape[0], m_refs[0].shape[0]
    for k in range(2):
        moment_ref[pl.ds(pl.multiple_of((k ^ (r % 2)) * half, half), half), :] = m_refs[k][...]
    for k in range(ns):
        a_ref[k * piece : (k + 1) * piece, :] = project4(s_refs[k][...], moment_ref[...])
    fine = shifted_rows(a_ref, t_ref, pot_ref, aug_ref, lse_ref, top_ref, mass_ref, e_ref)

    @pl.when(jnp.logical_not(fine))
    def _():
        column = [pot_ref[g : g + 1, :] for g in range(pot_ref.shape[0])]
        exact_rows(a_ref, t_ref, column, scores, lse_ref, top_ref, e_ref)


def high_low(x):
    high = x.astype(jnp.bfloat16).astype(jnp.float32)
    at = lax.broadcasted_iota(jnp.int32, (SUB, x.shape[1]), 0)
    return jnp.where(at == 0, high, jnp.where(at == 1, x - high, 0.0)).astype(jnp.bfloat16)


def rows_kernel(rows_total, *refs):
    a_ref, e_ref, top_ref, t_ref, pot_ref = refs[:5]
    l_refs, (lse_ref, column_ref, weights, scores) = refs[5:-4], refs[-4:]
    c, r = lax.axis_index("col"), lax.axis_index("row")
    nt, width = pot_ref.shape
    column_ref[...] = math.log(rows_total) - log_sum([l[...] for l in l_refs])
    column = [column_ref[pl.ds(r ^ k, 1), :] for k in range(nt)]
    change = [column[k] - pot_ref[k : k + 1, :] for k in range(nt)]
    top = jnp.max(functools.reduce(jnp.maximum, change), axis=1, keepdims=True)
    for k in range(nt):
        weights[:, k * width : (k + 1) * width] = high_low(jnp.exp(change[k] - top))
    steps = a_ref.shape[0] // LANES
    per = steps // lax.axis_size("col")
    masses = []
    for i in range(steps):
        e = e_ref[i * LANES : (i + 1) * LANES, :]
        sums = lax.dot_general(weights[...], e, NT_DIMS, preferred_element_type=jnp.float32)
        masses.append(sums[0:1, :] + sums[1:2, :])
        row = pl.ds((c ^ (i // per)) * per + i % per, 1)
        lse_ref[row, :] = top + top_ref[row, :] + jnp.log(masses[i])

    @pl.when(jnp.logical_not(within(masses)))
    def _():
        exact_rows(a_ref, t_ref, column, scores, lse_ref)


def columns_kernel(ns, cols_total, last, *refs):
    a_ref, e_ref, top_ref, t_ref, pot_ref, l_refs = *refs[:5], refs[5 : 5 + ns]
    out_refs, (sp_ref, weight_rows, weights, spread_rows, scores) = refs[5 + ns : -5], refs[-5:]
    c, r = lax.axis_index("col"), lax.axis_index("row")
    nt, width = pot_ref.shape
    rows = a_ref.shape[0]
    per = rows // ns // LANES
    potential = math.log(cols_total) - log_sum([l[...] for l in l_refs])
    sp_ref[...] = potential
    shift = potential + top_ref[...]
    top = jnp.max(jnp.max(shift, axis=1, keepdims=True), axis=0, keepdims=True)
    weight_rows[...] = jnp.exp(shift - top)
    for k in range(ns):
        for j in range(per):
            at = (k * per + j) * LANES
            weights[:, at : at + LANES] = high_low(weight_rows[pl.ds((c ^ k) * per + j, 1), :])

    def store(g, lse):
        if last:
            out_refs[g % 2][g // 2] = lse
        else:
            out_refs[0][pl.ds(r ^ g, 1), :] = lse

    masses = []
    for g in range(nt):
        e = e_ref[:, g * width : (g + 1) * width]
        sums = jnp.dot(weights[...], e, preferred_element_type=jnp.float32)
        masses.append(sums[0:1, :] + sums[1:2, :])
        store(g, top - pot_ref[g : g + 1, :] + jnp.log(masses[g]))

    @pl.when(jnp.logical_not(within(masses)))
    def _():
        exact_columns(ns, a_ref, t_ref, sp_ref, spread_rows, scores, store)


def exact_columns(ns, a_ref, t_ref, sp_ref, spread_rows, scores, store):
    c = lax.axis_index("col")
    rows, width = scores.shape
    per = rows // ns // LANES
    for k in range(ns):
        for j in range(per):
            at = (k * per + j) * LANES
            spread_rows[at : at + LANES, :] = as_rows(sp_ref[pl.ds((c ^ k) * per + j, 1), :])
    for g in range(t_ref.shape[0] // width):
        top = None
        for at in range(0, rows, LANES):
            a = a_ref[at : at + LANES, :]
            s = lax.dot_general(a, block_of(t_ref, g, width), NT_DIMS, preferred_element_type=jnp.float32)
            s = s + jnp.concatenate([spread_rows[at : at + LANES, :]] * (width // LANES), axis=1)
            scores[at : at + LANES, :] = s
            m = jnp.max(s.reshape(LANES // 8, 8, width), axis=0)
            top = m if top is None else jnp.maximum(top, m)
        top = jnp.max(top, axis=0, keepdims=True)
        mass = None
        for at in range(0, rows, LANES):
            e = jnp.exp(scores[at : at + LANES, :] - top)
            m = jnp.sum(e.reshape(LANES // 8, 8, width), axis=0)
            mass = m if mass is None else mass + m
        store(g, top + jnp.log(jnp.sum(mass, axis=0, keepdims=True)))


def split_kernel(x_ref, y_ref, *out_refs):
    for k, out_ref in enumerate(out_refs):
        out_ref[...] = log_sum([x_ref[k], y_ref[k]])


def update_kernel(rows_total, *refs):
    refs[-1][...] = math.log(rows_total) - log_sum([l[...] for l in refs[:-1]])


def call(kernel, out, args, scratch=(), flops=0, exps=0):
    vmem = pl.BlockSpec(memory_space=pltpu.VMEM)
    bytes_accessed = sum(x.size * x.dtype.itemsize for x in list(args) + list(out))
    return pl.pallas_call(
        kernel,
        out_shape=list(out),
        in_specs=[vmem] * len(args),
        out_specs=[vmem] * len(out),
        scratch_shapes=list(scratch),
        compiler_params=pltpu.CompilerParams(vmem_limit_bytes=24 << 20),
        cost_estimate=pl.CostEstimate(flops=flops, bytes_accessed=bytes_accessed, transcendentals=exps),
    )(*args)


def swap(x, axis, k):
    return lax.ppermute(x, axis, [(i, i ^ k) for i in range(lax.axis_size(axis))])


def exchange(x, axis):
    return [x] + [swap(x, axis, k) for k in range(1, lax.axis_size(axis))]


def exchange_chips(x):
    return [x] + [swap(x, "row", k) for k in range(2, lax.axis_size("row"), 2)]


def combine(kernel, parts):
    return call(kernel, [jax.ShapeDtypeStruct(parts[0].shape, parts[0].dtype)], parts)[0]


def per_device(source, target, target_potential, prev_moment):
    f32, bf16, shape = jnp.float32, jnp.bfloat16, jax.ShapeDtypeStruct
    ns, nt = lax.axis_size("col"), lax.axis_size("row")
    piece, width = source.shape[0], target.shape[0]
    depth = source.shape[1]
    rows, cols = piece * ns, width * nt
    rows_total, cols_total = rows * nt, cols * ns
    tile = shape((rows // LANES, LANES), f32)
    projected = shape((rows, depth), bf16)
    flops, exps = 2 * rows * cols * depth, rows * cols
    row_scores = pltpu.VMEM((LANES, cols), f32)
    small = pltpu.VMEM(tile.shape, f32)
    augmented = pltpu.VMEM((rows, 2 * depth), bf16)

    groups = width // LANES
    tail = jnp.pad(target_potential.reshape(groups, LANES), ((0, SUB - groups), (0, 0)))
    block = jnp.concatenate([target, tail], axis=0)
    far = exchange_chips(block)
    pieces = exchange(source, "col")
    a, = call(functools.partial(project_kernel, ns), [projected], pieces + [prev_moment], flops=6 * rows * depth * depth)
    far, a = lax.optimization_barrier((far, a))
    blocks = [x for pair in zip(far, [swap(x, "row", 1) for x in far]) for x in pair]
    lse, carried, t, pot = call(
        functools.partial(couple_kernel, nt, width),
        [tile, shape((rows, depth), f32), shape((cols, 2 * depth), bf16), shape((nt, width), f32)],
        [a] + blocks,
        [small, small, pltpu.VMEM((rows, cols), bf16), augmented, row_scores],
        2 * flops,
        exps,
    )
    half = shape((depth // 2, depth), f32)
    keep, send = call(
        functools.partial(moment_kernel, ns, rows_total),
        [half, half],
        pieces + exchange(lse, "col") + [carried],
        [small, pltpu.VMEM((depth, depth), f32)],
        6 * rows * depth * depth,
    )
    part = combine(add_kernel, [keep, swap(send, "row", 1)])
    part = combine(add_kernel, exchange(part, "col"))
    part = combine(add_kernel, exchange_chips(part))
    moment, a, lse, top, e = call(
        functools.partial(first_rows_kernel, ns),
        [shape((depth, depth), f32), projected, tile, tile, shape((rows, cols), bf16)],
        pieces + [t, pot, part, swap(part, "row", 1)],
        [small, augmented, row_scores],
        flops,
        exps,
    )
    for iteration in range(ITERS):
        last = iteration == ITERS - 1
        if iteration > 0:
            both = combine(log_sum_kernel, [column, swap(column, "row", 1)])
            lse, = call(
                functools.partial(rows_kernel, rows_total),
                [tile],
                [a, e, top, t, pot] + exchange_chips(both),
                [pltpu.VMEM((nt, width), f32), pltpu.VMEM((SUB, cols), bf16), row_scores],
                16 * rows * cols,
            )
        halves = shape((nt // 2, 1, width), f32)
        column, *sent, source_potential = call(
            functools.partial(columns_kernel, ns, cols_total, last),
            ([halves, halves] if last else [shape((nt, width), f32)]) + [tile],
            [a, e, top, t, pot] + exchange(lse, "col"),
            [
                small,
                pltpu.VMEM((SUB, rows), bf16),
                pltpu.VMEM((rows, LANES), f32),
                pltpu.VMEM((rows, width), f32),
            ],
            16 * rows * cols,
        )
    one = shape((1, width), f32)
    parts = call(split_kernel, [one] * (nt // 2), [column, swap(sent[0], "row", 1)])
    parts = [parts[0]] + [swap(x, "row", 2 * k) for k, x in enumerate(parts) if k > 0]
    update, = call(functools.partial(update_kernel, rows_total), [one], parts)
    return moment, source_potential.reshape(rows), update.reshape(width)


def solution(mesh):
    placed = (P(("row", "col"), None), P(("col", "row"), None), P(("col", "row")), P())
    return jax.shard_map(
        per_device,
        mesh=mesh,
        in_specs=placed,
        out_specs=(P(), P("row"), P(("col", "row"))),
        check_vma=False,
    )
```

time: 111 us -> 131 us (1.18)
  Pallas kernels: 35.3 us -> 59.4 us
  waiting for transfers between devices: 31.9 us -> 29.4 us
    pallas_call x12 -> x13, Pallas kernels: 35.3 us -> 59.4 us  [call(): pl.pallas_call(kernel, out_shape=list(out), in_specs=[vmem] * len(args),...]
    ppermute x35, waiting for transfers between devices: 31.9 us -> 29.4 us  [swap(): lax.ppermute(x, axis, [(i, i ^ k) for i in range(lax.axis_size(axis))])]
  transfers between devices with their start and end apart: 35 -> 35, of which waited for: 30 -> 29; matrix products, arithmetic and copies ran while one was open for 0% -> 1% of each run, Pallas kernels for 0% -> 0%
where the time goes in v6:
time: 131 us
  Pallas kernels  59.4 us (45%)
  starting transfers between devices  38.8 us (30%)
  waiting for transfers between devices  29.4 us (22%)
  local copies, waits for them, and re-layouts  1.69 us (1%)
    pallas_call x13, Pallas kernels, call(): pl.pallas_call(kernel, out_shape=list(out), in_specs=[vmem] * len(args),...  59.4 us
    ppermute x35, starting transfers between devices, swap(): lax.ppermute(x, axis, [(i, i ^ k) for i in range(lax.axis_size(axis))])  38.8 us
    ppermute x35, waiting for transfers between devices, swap(): lax.ppermute(x, axis, [(i, i ^ k) for i in range(lax.axis_size(axis))])  29.4 us
  transfers between devices with their start and end apart: 35, of which 29 were waited for; matrix products, arithmetic and copies ran while one was open for 1% of the time, Pallas kernels for 0%

profile of v6, /device:TPU:0, one launch (start us, length us, event | category | flops | bytes accessed | tf_op | source)
XLA Modules:
  0.0 131.0 jit_solution(13872139319277765262)
XLA Ops:
  0.6 5.1 %collective-permute-start.2 = (bf16[256,128]{1,0:T(8,128)(2,1)}, bf16[256,128]{1,0:T(8,128)(2,1)S(1)}, u32[]{:S(2)}, u32[]{:S(2)}) collective-permute-start(bf16[256,128]{1,0:T(8,128)(2,1)} %refs_0_.5), channel_id=1, source_target_pairs={{0,3},{1,2},{2,1},{3,0},{4,7},{5,6},{6,5},{7,4},{8,11},{9,10},{10,... | collective-permute-start | bytes 196616 | tf_op jit(solution)/shard_map/ppermute | solution.py:346
  5.8 0.9 fusion.1.refs_1_
  6.7 2.5 %collective-permute-start.5 = (bf16[528,128]{1,0:T(8,128)(2,1)S(1)}, bf16[528,128]{1,0:T(8,128)(2,1)S(1)}, u32[]{:S(2)}, u32[]{:S(2)}) collective-permute-start(bf16[528,128]{1,0:T(8,128)(2,1)S(1)} %fusion.1.refs_1_), channel_id=1, source_target_pairs={{0,24},{4,28},{8,16},{12,20},{16,8},{20,12},{24,0},{28,4},{1,25},{... | collective-permute-start | bytes 405512 | tf_op jit(solution)/shard_map/ppermute | solution.py:346
  9.2 0.5 collective-permute-start.4
  9.7 0.5 collective-permute-start.3
  10.3 0.6 collective-permute-start
  10.8 5.0 %collective-permute-done.1.refs_2_ = bf16[256,128]{1,0:T(8,128)(2,1)S(1)} collective-permute-done((bf16[256,128]{1,0:T(8,128)(2,1)}, bf16[256,128]{1,0:T(8,128)(2,1)S(1)}, u32[]{:S(2)}, u32[]{:S(2)}) %collective-permute-start.1) | collective-permute-done | bytes 65568 | tf_op jit(solution)/shard_map/ppermute | solution.py:346
  15.8 0.8 copy-done
  16.7 0.8 copy-done.2
  17.5 0.4 shard_map.67.refs_0_
  18.0 0.5 collective-permute-start.7
  18.6 0.4 collective-permute-start.9
  19.0 0.3 collective-permute-done.6.refs_2_
  19.5 0.3 collective-permute-done.8.refs_6_
  20.0 19.3 %shard_map.68 = (f32[8,128]{1,0:T(8,128)S(1)}, f32[1024,128]{1,0:T(8,128)S(1)}, bf16[4096,256]{1,0:T(8,128)(2,1)S(1)}, f32[8,512]{1,0:T(8,128)S(1)}) custom-call(bf16[1024,128]{1,0:T(8,128)(2,1)S(1)} %shard_map.67.refs_0_, bf16[528,128]{1,0:T(8,128)(2,1)S(1)} %fusion.1.refs_1_, bf16[528,128]{1,0:T(8,128)(2,1)S(1)} %collective-permute-done.6.refs_2_, ...), custom_call_target="tpu_custom_call" | custom-call | flops 2147483648 | bytes 3985408 | tf_op jit(solution)/shard_map/pallas_call | solution.py:334
  39.3 1.4 %collective-permute-start.12 = (f32[8,128]{1,0:T(8,128)S(1)}, f32[8,128]{1,0:T(8,128)S(1)}, u32[]{:S(2)}, u32[]{:S(2)}) collective-permute-start(f32[8,128]{1,0:T(8,128)S(1)} %get-tuple-element.34.refs_4_), channel_id=1, source_target_pairs={{0,3},{1,2},{2,1},{3,0},{4,7},{5,6},{6,5},{7,4},{8,11},{9,10},{10,... | collective-permute-start | bytes 12296 | tf_op jit(solution)/shard_map/ppermute | solution.py:346
  40.7 0.6 collective-permute-start.11
  41.3 2.5 %collective-permute-start.10 = (f32[8,128]{1,0:T(8,128)S(1)}, f32[8,128]{1,0:T(8,128)S(1)}, u32[]{:S(2)}, u32[]{:S(2)}) collective-permute-start(f32[8,128]{1,0:T(8,128)S(1)} %get-tuple-element.34.refs_4_), channel_id=1, source_target_pairs={{0,1},{1,0},{2,3},{3,2},{4,5},{5,4},{6,7},{7,6},{8,9},{9,8},{10,11... | collective-permute-start | bytes 12296 | tf_op jit(solution)/shard_map/ppermute | solution.py:346
  43.7 1.1 collective-permute-done.12.refs_7_
  44.8 0.4 collective-permute-done.11.refs_6_
  45.3 0.5 shard_map.69
  45.9 1.2 collective-permute-done.13.refs_1_
  47.1 2.4 %collective-permute-start.16 = (f32[64,128]{1,0:T(8,128)S(1)}, f32[64,128]{1,0:T(8,128)S(1)}, u32[]{:S(2)}, u32[]{:S(2)}) collective-permute-start(f32[64,128]{1,0:T(8,128)S(1)} %shard_map.70.refs_0_), channel_id=1, source_target_pairs={{0,3},{1,2},{2,1},{3,0},{4,7},{5,6},{6,5},{7,4},{8,11},{9,10},{10,... | collective-permute-start | bytes 98312 | tf_op jit(solution)/shard_map/ppermute | solution.py:346
  49.6 1.1 collective-permute-start.15
  50.6 0.9 collective-permute-start.14
  51.5 1.7 %collective-permute-done.16.refs_3_ = f32[64,128]{1,0:T(8,128)S(1)} collective-permute-done((f32[64,128]{1,0:T(8,128)S(1)}, f32[64,128]{1,0:T(8,128)S(1)}, u32[]{:S(2)}, u32[]{:S(2)}) %collective-permute-start.16) | collective-permute-done | bytes 32800 | tf_op jit(solution)/shard_map/ppermute | solution.py:346
  53.2 1.1 collective-permute-done.15.refs_2_
  54.4 0.3 collective-permute-done.14.refs_1_
  54.7 2.5 %collective-permute-start.19 = (f32[64,128]{1,0:T(8,128)S(1)}, f32[64,128]{1,0:T(8,128)S(1)}, u32[]{:S(2)}, u32[]{:S(2)}) collective-permute-start(f32[64,128]{1,0:T(8,128)S(1)} %shard_map.71.refs_0_), channel_id=1, source_target_pairs={{0,24},{4,28},{8,16},{12,20},{16,8},{20,12},{24,0},{28,4},{1,25},{... | collective-permute-start | bytes 98312 | tf_op jit(solution)/shard_map/ppermute | solution.py:346
  57.2 0.5 collective-permute-start.18
  57.7 0.5 collective-permute-start.17
  58.3 1.3 %collective-permute-done.19.refs_3_ = f32[64,128]{1,0:T(8,128)S(1)} collective-permute-done((f32[64,128]{1,0:T(8,128)S(1)}, f32[64,128]{1,0:T(8,128)S(1)}, u32[]{:S(2)}, u32[]{:S(2)}) %collective-permute-start.19) | collective-permute-done | bytes 32800 | tf_op jit(solution)/shard_map/ppermute | solution.py:346
  59.6 1.5 %collective-permute-done.18.refs_2_ = f32[64,128]{1,0:T(8,128)S(1)} collective-permute-done((f32[64,128]{1,0:T(8,128)S(1)}, f32[64,128]{1,0:T(8,128)S(1)}, u32[]{:S(2)}, u32[]{:S(2)}) %collective-permute-start.18) | collective-permute-done | bytes 32800 | tf_op jit(solution)/shard_map/ppermute | solution.py:346
  61.2 0.5 collective-permute-done.17.refs_1_
  61.8 1.2 collective-permute-done.20.refs_7_
  62.9 14.8 %shard_map.73 = (f32[128,128]{1,0:T(8,128)}, bf16[1024,128]{1,0:T(8,128)(2,1)S(1)}, f32[8,128]{1,0:T(8,128)S(1)}, f32[8,128]{1,0:T(8,128)S(1)}, bf16[1024,4096]{1,0:T(8,128)(2,1)S(1)}) custom-call(bf16[256,128]{1,0:T(8,128)(2,1)S(1)} %copy-done.1, bf16[256,128]{1,0:T(8,128)(2,1)S(1)} %collective-permute-done.refs_1_, ...), custom_call_target="tpu_custom_call" | custom-call | flops 1073741824 | bytes 11165696 | tf_op jit(solution)/shard_map/pallas_call | solution.py:334
  77.7 1.5 %collective-permute-start.23 = (f32[8,128]{1,0:T(8,128)S(1)}, f32[8,128]{1,0:T(8,128)S(1)}, u32[]{:S(2)}, u32[]{:S(2)}) collective-permute-start(f32[8,128]{1,0:T(8,128)S(1)} %get-tuple-element.42.refs_5_), channel_id=1, source_target_pairs={{0,3},{1,2},{2,1},{3,0},{4,7},{5,6},{6,5},{7,4},{8,11},{9,10},{10,... | collective-permute-start | bytes 12296 | tf_op jit(solution)/shard_map/ppermute | solution.py:346
  79.3 0.7 collective-permute-start.22
  79.9 2.2 %collective-permute-start.21 = (f32[8,128]{1,0:T(8,128)S(1)}, f32[8,128]{1,0:T(8,128)S(1)}, u32[]{:S(2)}, u32[]{:S(2)}) collective-permute-start(f32[8,128]{1,0:T(8,128)S(1)} %get-tuple-element.42.refs_5_), channel_id=1, source_target_pairs={{0,1},{1,0},{2,3},{3,2},{4,5},{5,4},{6,7},{7,6},{8,9},{9,8},{10,11... | collective-permute-start | bytes 12296 | tf_op jit(solution)/shard_map/ppermute | solution.py:346
  82.1 1.0 collective-permute-done.23.refs_8_
  83.1 0.6 collective-permute-done.22.refs_7_
  83.8 6.9 %shard_map.74 = (f32[8,512]{1,0:T(8,128)S(1)}, f32[8,128]{1,0:T(8,128)}) custom-call(bf16[1024,128]{1,0:T(8,128)(2,1)S(1)} %get-tuple-element.39.refs_0_, bf16[1024,4096]{1,0:T(8,128)(2,1)S(1)} %get-tuple-element.40.refs_1_, f32[8,128]{1,0:T(8,128)S(1)} %get-tuple-element.41.refs_2_, bf16[4096,256]{1,0:T(8,128)(2,1)S(1)} %get-tuple-element.32.refs_4_.refs_3_, ...), custom_call_target="tpu_custom_call" | custom-call | flops 67108864 | bytes 10805248 | tf_op jit(solution)/shard_map/pallas_call | solution.py:334
  90.7 1.2 collective-permute-done.24.refs_1_
  91.9 1.6 %collective-permute-start.27 = (f32[8,512]{1,0:T(8,128)S(1)}, f32[8,512]{1,0:T(8,128)S(1)}, u32[]{:S(2)}, u32[]{:S(2)}) collective-permute-start(f32[8,512]{1,0:T(8,128)S(1)} %shard_map.75.refs_5_), channel_id=1, source_target_pairs={{0,24},{4,28},{8,16},{12,20},{16,8},{20,12},{24,0},{28,4},{1,25},{... | collective-permute-start | bytes 49160 | tf_op jit(solution)/shard_map/ppermute | solution.py:346
  93.5 0.5 collective-permute-start.26
  94.0 1.5 %collective-permute-start.25 = (f32[8,512]{1,0:T(8,128)S(1)}, f32[8,512]{1,0:T(8,128)S(1)}, u32[]{:S(2)}, u32[]{:S(2)}) collective-permute-start(f32[8,512]{1,0:T(8,128)S(1)} %shard_map.75.refs_5_), channel_id=1, source_target_pairs={{0,8},{4,12},{8,0},{12,4},{16,24},{20,28},{24,16},{28,20},{1,9},{5... | collective-permute-start | bytes 49160 | tf_op jit(solution)/shard_map/ppermute | solution.py:346
  95.5 1.1 collective-permute-done.27.refs_8_
  96.6 0.6 collective-permute-done.26.refs_7_
  97.2 0.5 collective-permute-done.25.refs_6_
  97.7 10.0 %shard_map.76.refs_5_ = f32[8,128]{1,0:T(8,128)S(1)} custom-call(bf16[1024,128]{1,0:T(8,128)(2,1)S(1)} %get-tuple-element.39.refs_0_, bf16[1024,4096]{1,0:T(8,128)(2,1)S(1)} %get-tuple-element.40.refs_1_, f32[8,128]{1,0:T(8,128)S(1)} %get-tuple-element.41.refs_2_, bf16[4096,256]{1,0:T(8,128)(2,1)S(1)} %get-tuple-element.32.refs_4_.refs_3_, ...), custom_call_target="tpu_custom_call" | custom-call | flops 67108864 | bytes 10838016 | tf_op jit(solution)/shard_map/pallas_call | solution.py:334
  107.7 2.3 %collective-permute-start.30 = (f32[8,128]{1,0:T(8,128)S(1)}, f32[8,128]{1,0:T(8,128)S(1)}, u32[]{:S(2)}, u32[]{:S(2)}) collective-permute-start(f32[8,128]{1,0:T(8,128)S(1)} %shard_map.76.refs_5_), channel_id=1, source_target_pairs={{0,3},{1,2},{2,1},{3,0},{4,7},{5,6},{6,5},{7,4},{8,11},{9,10},{10,... | collective-permute-start | bytes 12296 | tf_op jit(solution)/shard_map/ppermute | solution.py:346
  110.0 1.1 collective-permute-start.29
  111.1 1.0 collective-permute-start.28
  112.1 1.0 collective-permute-done.30.refs_8_
  113.1 1.4 %collective-permute-done.29.refs_7_ = f32[8,128]{1,0:T(8,128)S(1)} collective-permute-done((f32[8,128]{1,0:T(8,128)S(1)}, f32[8,128]{1,0:T(8,128)S(1)}, u32[]{:S(2)}, u32[]{:S(2)}) %collective-permute-start.29) | collective-permute-done | bytes 4128 | tf_op jit(solution)/shard_map/ppermute | solution.py:346
  114.5 0.2 collective-permute-done.28.refs_6_
  114.7 6.9 %shard_map.77 = (f32[4,1,512]{2,1,0:T(1,128)S(1)}, f32[4,1,512]{2,1,0:T(1,128)S(1)}, f32[8,128]{1,0:T(8,128)}) custom-call(bf16[1024,128]{1,0:T(8,128)(2,1)S(1)} %get-tuple-element.39.refs_0_, bf16[1024,4096]{1,0:T(8,128)(2,1)S(1)} %get-tuple-element.40.refs_1_, f32[8,128]{1,0:T(8,128)S(1)} %get-tuple-element.41.refs_2_, ...), custom_call_target="tpu_custom_call" | custom-call | flops 67108864 | bytes 10805248 | tf_op jit(solution)/shard_map/pallas_call | solution.py:334
  121.7 1.2 collective-permute-done.31.y_ref
  122.9 1.6 %collective-permute-start.32 = (f32[1,512]{1,0:T(1,128)S(1)}, f32[1,512]{1,0:T(1,128)S(1)}, u32[]{:S(2)}, u32[]{:S(2)}) collective-permute-start(f32[1,512]{1,0:T(1,128)S(1)} %get-tuple-element.48), channel_id=1, source_target_pairs={{0,8},{4,12},{8,0},{12,4},{16,24},{20,28},{24,16},{28,20},{1,9},{5... | collective-permute-start | bytes 6152 | tf_op jit(solution)/shard_map/ppermute | solution.py:346
  124.4 1.5 %collective-permute-start.33 = (f32[1,512]{1,0:T(1,128)S(1)}, f32[1,512]{1,0:T(1,128)S(1)}, u32[]{:S(2)}, u32[]{:S(2)}) collective-permute-start(f32[1,512]{1,0:T(1,128)S(1)} %get-tuple-element.49), channel_id=1, source_target_pairs={{0,16},{4,20},{8,24},{12,28},{16,0},{20,4},{24,8},{28,12},{1,17},{... | collective-permute-start | bytes 6152 | tf_op jit(solution)/shard_map/ppermute | solution.py:346
  125.9 0.5 collective-permute-start.34
  126.5 1.5 %collective-permute-done.33.refs_2_ = f32[1,512]{1,0:T(1,128)S(1)} collective-permute-done((f32[1,512]{1,0:T(1,128)S(1)}, f32[1,512]{1,0:T(1,128)S(1)}, u32[]{:S(2)}, u32[]{:S(2)}) %collective-permute-start.33) | collective-permute-done | bytes 2080 | tf_op jit(solution)/shard_map/ppermute | solution.py:346
  128.0 2.4 %collective-permute-done.34.refs_3_ = f32[1,512]{1,0:T(1,128)S(1)} collective-permute-done((f32[1,512]{1,0:T(1,128)S(1)}, f32[1,512]{1,0:T(1,128)S(1)}, u32[]{:S(2)}, u32[]{:S(2)}) %collective-permute-start.34) | collective-permute-done | bytes 2080 | tf_op jit(solution)/shard_map/ppermute | solution.py:346
  130.4 0.6 shard_map.79
  (26 shorter events, 1.0 us)
Async XLA Ops:
  0.6 44.7 %copy-start.1 = (bf16[256,128]{1,0:T(8,128)(2,1)S(1)}, bf16[256,128]{1,0:T(8,128)(2,1)}, u32[]{:S(2)}) copy-start(bf16[256,128]{1,0:T(8,128)(2,1)} %refs_0_.5) | copy-start | bytes 196612
  0.6 9.6 %collective-permute-start.2 = (bf16[256,128]{1,0:T(8,128)(2,1)}, bf16[256,128]{1,0:T(8,128)(2,1)S(1)}, u32[]{:S(2)}, u32[]{:S(2)}) collective-permute-start(bf16[256,128]{1,0:T(8,128)(2,1)} %refs_0_.5), channel_id=1, source_target_pairs={{0,3},{1,2},{2,1},{3,0},{4,7},{5,6},{6,5},{7,4},{8,11},{9,10},{10,... | collective-permute-start | bytes 196616 | tf_op jit(solution)/shard_map/ppermute | solution.py:346
  6.7 11.2 %collective-permute-start.5 = (bf16[528,128]{1,0:T(8,128)(2,1)S(1)}, bf16[528,128]{1,0:T(8,128)(2,1)S(1)}, u32[]{:S(2)}, u32[]{:S(2)}) collective-permute-start(bf16[528,128]{1,0:T(8,128)(2,1)S(1)} %fusion.1.refs_1_), channel_id=1, source_target_pairs={{0,24},{4,28},{8,16},{12,20},{16,8},{20,12},{24,0},{28,4},{1,25},{... | collective-permute-start | bytes 405512 | tf_op jit(solution)/shard_map/ppermute | solution.py:346
  9.2 8.7 %collective-permute-start.4 = (bf16[528,128]{1,0:T(8,128)(2,1)S(1)}, bf16[528,128]{1,0:T(8,128)(2,1)S(1)}, u32[]{:S(2)}, u32[]{:S(2)}) collective-permute-start(bf16[528,128]{1,0:T(8,128)(2,1)S(1)} %fusion.1.refs_1_), channel_id=1, source_target_pairs={{0,16},{4,20},{8,24},{12,28},{16,0},{20,4},{24,8},{28,12},{1,17},{... | collective-permute-start | bytes 405512 | tf_op jit(solution)/shard_map/ppermute | solution.py:346
  9.7 8.2 %collective-permute-start.3 = (bf16[528,128]{1,0:T(8,128)(2,1)S(1)}, bf16[528,128]{1,0:T(8,128)(2,1)S(1)}, u32[]{:S(2)}, u32[]{:S(2)}) collective-permute-start(bf16[528,128]{1,0:T(8,128)(2,1)S(1)} %fusion.1.refs_1_), channel_id=1, source_target_pairs={{0,8},{4,12},{8,0},{12,4},{16,24},{20,28},{24,16},{28,20},{1,9},{5... | collective-permute-start | bytes 405512 | tf_op jit(solution)/shard_map/ppermute | solution.py:346
  10.2 5.6 %collective-permute-start.1 = (bf16[256,128]{1,0:T(8,128)(2,1)}, bf16[256,128]{1,0:T(8,128)(2,1)S(1)}, u32[]{:S(2)}, u32[]{:S(2)}) collective-permute-start(bf16[256,128]{1,0:T(8,128)(2,1)} %refs_0_.5), channel_id=1, source_target_pairs={{0,2},{1,3},{2,0},{3,1},{4,6},{5,7},{6,4},{7,5},{8,10},{9,11},{10,... | collective-permute-start | bytes 196616 | tf_op jit(solution)/shard_map/ppermute | solution.py:346
  10.3 5.6 %collective-permute-start = (bf16[256,128]{1,0:T(8,128)(2,1)}, bf16[256,128]{1,0:T(8,128)(2,1)S(1)}, u32[]{:S(2)}, u32[]{:S(2)}) collective-permute-start(bf16[256,128]{1,0:T(8,128)(2,1)} %refs_0_.5), channel_id=1, source_target_pairs={{0,1},{1,0},{2,3},{3,2},{4,5},{5,4},{6,7},{7,6},{8,9},{9,8},{10,11... | collective-permute-start | bytes 196616 | tf_op jit(solution)/shard_map/ppermute | solution.py:346
  15.8 0.8 copy-start
  16.7 0.8 copy-start.2
  17.9 1.4 %collective-permute-start.6 = (bf16[528,128]{1,0:T(8,128)(2,1)S(1)}, bf16[528,128]{1,0:T(8,128)(2,1)S(1)}, u32[]{:S(2)}, u32[]{:S(2)}) collective-permute-start(bf16[528,128]{1,0:T(8,128)(2,1)S(1)} %fusion.1.refs_1_), channel_id=1, source_target_pairs={{0,4},{4,0},{8,12},{12,8},{16,20},{20,16},{24,28},{28,24},{1,5},{5... | collective-permute-start | bytes 405512 | tf_op jit(solution)/shard_map/ppermute | solution.py:346
  18.0 1.5 %collective-permute-start.7 = (bf16[528,128]{1,0:T(8,128)(2,1)S(1)}, bf16[528,128]{1,0:T(8,128)(2,1)S(1)}, u32[]{:S(2)}, u32[]{:S(2)}) collective-permute-start(bf16[528,128]{1,0:T(8,128)(2,1)S(1)} %collective-permute-done.3.refs_3_), channel_id=1, source_target_pairs={{0,4},{4,0},{8,12},{12,8},{16,20},{20,16},{24,28},{28,24},{1,5},{5... | collective-permute-start | bytes 405512 | tf_op jit(solution)/shard_map/ppermute | solution.py:346
  18.5 1.4 %collective-permute-start.8 = (bf16[528,128]{1,0:T(8,128)(2,1)S(1)}, bf16[528,128]{1,0:T(8,128)(2,1)S(1)}, u32[]{:S(2)}, u32[]{:S(2)}) collective-permute-start(bf16[528,128]{1,0:T(8,128)(2,1)S(1)} %collective-permute-done.4.refs_5_), channel_id=1, source_target_pairs={{0,4},{4,0},{8,12},{12,8},{16,20},{20,16},{24,28},{28,24},{1,5},{5... | collective-permute-start | bytes 405512 | tf_op jit(solution)/shard_map/ppermute | solution.py:346
  18.6 1.5 %collective-permute-start.9 = (bf16[528,128]{1,0:T(8,128)(2,1)S(1)}, bf16[528,128]{1,0:T(8,128)(2,1)S(1)}, u32[]{:S(2)}, u32[]{:S(2)}) collective-permute-start(bf16[528,128]{1,0:T(8,128)(2,1)S(1)} %collective-permute-done.5.refs_7_), channel_id=1, source_target_pairs={{0,4},{4,0},{8,12},{12,8},{16,20},{20,16},{24,28},{28,24},{1,5},{5... | collective-permute-start | bytes 405512 | tf_op jit(solution)/shard_map/ppermute | solution.py:346
  39.3 5.5 %collective-permute-start.12 = (f32[8,128]{1,0:T(8,128)S(1)}, f32[8,128]{1,0:T(8,128)S(1)}, u32[]{:S(2)}, u32[]{:S(2)}) collective-permute-start(f32[8,128]{1,0:T(8,128)S(1)} %get-tuple-element.34.refs_4_), channel_id=1, source_target_pairs={{0,3},{1,2},{2,1},{3,0},{4,7},{5,6},{6,5},{7,4},{8,11},{9,10},{10,... | collective-permute-start | bytes 12296 | tf_op jit(solution)/shard_map/ppermute | solution.py:346
  40.7 4.5 %collective-permute-start.11 = (f32[8,128]{1,0:T(8,128)S(1)}, f32[8,128]{1,0:T(8,128)S(1)}, u32[]{:S(2)}, u32[]{:S(2)}) collective-permute-start(f32[8,128]{1,0:T(8,128)S(1)} %get-tuple-element.34.refs_4_), channel_id=1, source_target_pairs={{0,2},{1,3},{2,0},{3,1},{4,6},{5,7},{6,4},{7,5},{8,10},{9,11},{10,... | collective-permute-start | bytes 12296 | tf_op jit(solution)/shard_map/ppermute | solution.py:346
  41.3 4.1 %collective-permute-start.10 = (f32[8,128]{1,0:T(8,128)S(1)}, f32[8,128]{1,0:T(8,128)S(1)}, u32[]{:S(2)}, u32[]{:S(2)}) collective-permute-start(f32[8,128]{1,0:T(8,128)S(1)} %get-tuple-element.34.refs_4_), channel_id=1, source_target_pairs={{0,1},{1,0},{2,3},{3,2},{4,5},{5,4},{6,7},{7,6},{8,9},{9,8},{10,11... | collective-permute-start | bytes 12296 | tf_op jit(solution)/shard_map/ppermute | solution.py:346
  45.9 1.3 collective-permute-start.13
  47.1 6.1 %collective-permute-start.16 = (f32[64,128]{1,0:T(8,128)S(1)}, f32[64,128]{1,0:T(8,128)S(1)}, u32[]{:S(2)}, u32[]{:S(2)}) collective-permute-start(f32[64,128]{1,0:T(8,128)S(1)} %shard_map.70.refs_0_), channel_id=1, source_target_pairs={{0,3},{1,2},{2,1},{3,0},{4,7},{5,6},{6,5},{7,4},{8,11},{9,10},{10,... | collective-permute-start | bytes 98312 | tf_op jit(solution)/shard_map/ppermute | solution.py:346
  49.6 4.8 %collective-permute-start.15 = (f32[64,128]{1,0:T(8,128)S(1)}, f32[64,128]{1,0:T(8,128)S(1)}, u32[]{:S(2)}, u32[]{:S(2)}) collective-permute-start(f32[64,128]{1,0:T(8,128)S(1)} %shard_map.70.refs_0_), channel_id=1, source_target_pairs={{0,2},{1,3},{2,0},{3,1},{4,6},{5,7},{6,4},{7,5},{8,10},{9,11},{10,... | collective-permute-start | bytes 98312 | tf_op jit(solution)/shard_map/ppermute | solution.py:346
  50.6 4.1 %collective-permute-start.14 = (f32[64,128]{1,0:T(8,128)S(1)}, f32[64,128]{1,0:T(8,128)S(1)}, u32[]{:S(2)}, u32[]{:S(2)}) collective-permute-start(f32[64,128]{1,0:T(8,128)S(1)} %shard_map.70.refs_0_), channel_id=1, source_target_pairs={{0,1},{1,0},{2,3},{3,2},{4,5},{5,4},{6,7},{7,6},{8,9},{9,8},{10,11... | collective-permute-start | bytes 98312 | tf_op jit(solution)/shard_map/ppermute | solution.py:346
  54.7 4.9 %collective-permute-start.19 = (f32[64,128]{1,0:T(8,128)S(1)}, f32[64,128]{1,0:T(8,128)S(1)}, u32[]{:S(2)}, u32[]{:S(2)}) collective-permute-start(f32[64,128]{1,0:T(8,128)S(1)} %shard_map.71.refs_0_), channel_id=1, source_target_pairs={{0,24},{4,28},{8,16},{12,20},{16,8},{20,12},{24,0},{28,4},{1,25},{... | collective-permute-start | bytes 98312 | tf_op jit(solution)/shard_map/ppermute | solution.py:346
  57.2 3.9 %collective-permute-start.18 = (f32[64,128]{1,0:T(8,128)S(1)}, f32[64,128]{1,0:T(8,128)S(1)}, u32[]{:S(2)}, u32[]{:S(2)}) collective-permute-start(f32[64,128]{1,0:T(8,128)S(1)} %shard_map.71.refs_0_), channel_id=1, source_target_pairs={{0,16},{4,20},{8,24},{12,28},{16,0},{20,4},{24,8},{28,12},{1,17},{... | collective-permute-start | bytes 98312 | tf_op jit(solution)/shard_map/ppermute | solution.py:346
  57.7 3.9 %collective-permute-start.17 = (f32[64,128]{1,0:T(8,128)S(1)}, f32[64,128]{1,0:T(8,128)S(1)}, u32[]{:S(2)}, u32[]{:S(2)}) collective-permute-start(f32[64,128]{1,0:T(8,128)S(1)} %shard_map.71.refs_0_), channel_id=1, source_target_pairs={{0,8},{4,12},{8,0},{12,4},{16,24},{20,28},{24,16},{28,20},{1,9},{5... | collective-permute-start | bytes 98312 | tf_op jit(solution)/shard_map/ppermute | solution.py:346
  61.7 1.3 collective-permute-start.20
  77.7 5.4 %collective-permute-start.23 = (f32[8,128]{1,0:T(8,128)S(1)}, f32[8,128]{1,0:T(8,128)S(1)}, u32[]{:S(2)}, u32[]{:S(2)}) collective-permute-start(f32[8,128]{1,0:T(8,128)S(1)} %get-tuple-element.42.refs_5_), channel_id=1, source_target_pairs={{0,3},{1,2},{2,1},{3,0},{4,7},{5,6},{6,5},{7,4},{8,11},{9,10},{10,... | collective-permute-start | bytes 12296 | tf_op jit(solution)/shard_map/ppermute | solution.py:346
  79.3 4.5 %collective-permute-start.22 = (f32[8,128]{1,0:T(8,128)S(1)}, f32[8,128]{1,0:T(8,128)S(1)}, u32[]{:S(2)}, u32[]{:S(2)}) collective-permute-start(f32[8,128]{1,0:T(8,128)S(1)} %get-tuple-element.42.refs_5_), channel_id=1, source_target_pairs={{0,2},{1,3},{2,0},{3,1},{4,6},{5,7},{6,4},{7,5},{8,10},{9,11},{10,... | collective-permute-start | bytes 12296 | tf_op jit(solution)/shard_map/ppermute | solution.py:346
  79.9 3.8 %collective-permute-start.21 = (f32[8,128]{1,0:T(8,128)S(1)}, f32[8,128]{1,0:T(8,128)S(1)}, u32[]{:S(2)}, u32[]{:S(2)}) collective-permute-start(f32[8,128]{1,0:T(8,128)S(1)} %get-tuple-element.42.refs_5_), channel_id=1, source_target_pairs={{0,1},{1,0},{2,3},{3,2},{4,5},{5,4},{6,7},{7,6},{8,9},{9,8},{10,11... | collective-permute-start | bytes 12296 | tf_op jit(solution)/shard_map/ppermute | solution.py:346
  90.7 1.2 collective-permute-start.24
  91.9 4.7 %collective-permute-start.27 = (f32[8,512]{1,0:T(8,128)S(1)}, f32[8,512]{1,0:T(8,128)S(1)}, u32[]{:S(2)}, u32[]{:S(2)}) collective-permute-start(f32[8,512]{1,0:T(8,128)S(1)} %shard_map.75.refs_5_), channel_id=1, source_target_pairs={{0,24},{4,28},{8,16},{12,20},{16,8},{20,12},{24,0},{28,4},{1,25},{... | collective-permute-start | bytes 49160 | tf_op jit(solution)/shard_map/ppermute | solution.py:346
  93.5 3.7 %collective-permute-start.26 = (f32[8,512]{1,0:T(8,128)S(1)}, f32[8,512]{1,0:T(8,128)S(1)}, u32[]{:S(2)}, u32[]{:S(2)}) collective-permute-start(f32[8,512]{1,0:T(8,128)S(1)} %shard_map.75.refs_5_), channel_id=1, source_target_pairs={{0,16},{4,20},{8,24},{12,28},{16,0},{20,4},{24,8},{28,12},{1,17},{... | collective-permute-start | bytes 49160 | tf_op jit(solution)/shard_map/ppermute | solution.py:346
  94.0 3.7 %collective-permute-start.25 = (f32[8,512]{1,0:T(8,128)S(1)}, f32[8,512]{1,0:T(8,128)S(1)}, u32[]{:S(2)}, u32[]{:S(2)}) collective-permute-start(f32[8,512]{1,0:T(8,128)S(1)} %shard_map.75.refs_5_), channel_id=1, source_target_pairs={{0,8},{4,12},{8,0},{12,4},{16,24},{20,28},{24,16},{28,20},{1,9},{5... | collective-permute-start | bytes 49160 | tf_op jit(solution)/shard_map/ppermute | solution.py:346
  107.7 5.4 %collective-permute-start.30 = (f32[8,128]{1,0:T(8,128)S(1)}, f32[8,128]{1,0:T(8,128)S(1)}, u32[]{:S(2)}, u32[]{:S(2)}) collective-permute-start(f32[8,128]{1,0:T(8,128)S(1)} %shard_map.76.refs_5_), channel_id=1, source_target_pairs={{0,3},{1,2},{2,1},{3,0},{4,7},{5,6},{6,5},{7,4},{8,11},{9,10},{10,... | collective-permute-start | bytes 12296 | tf_op jit(solution)/shard_map/ppermute | solution.py:346
  110.0 4.5 %collective-permute-start.29 = (f32[8,128]{1,0:T(8,128)S(1)}, f32[8,128]{1,0:T(8,128)S(1)}, u32[]{:S(2)}, u32[]{:S(2)}) collective-permute-start(f32[8,128]{1,0:T(8,128)S(1)} %shard_map.76.refs_5_), channel_id=1, source_target_pairs={{0,2},{1,3},{2,0},{3,1},{4,6},{5,7},{6,4},{7,5},{8,10},{9,11},{10,... | collective-permute-start | bytes 12296 | tf_op jit(solution)/shard_map/ppermute | solution.py:346
  111.1 3.6 %collective-permute-start.28 = (f32[8,128]{1,0:T(8,128)S(1)}, f32[8,128]{1,0:T(8,128)S(1)}, u32[]{:S(2)}, u32[]{:S(2)}) collective-permute-start(f32[8,128]{1,0:T(8,128)S(1)} %shard_map.76.refs_5_), channel_id=1, source_target_pairs={{0,1},{1,0},{2,3},{3,2},{4,5},{5,4},{6,7},{7,6},{8,9},{9,8},{10,11... | collective-permute-start | bytes 12296 | tf_op jit(solution)/shard_map/ppermute | solution.py:346
  121.7 1.2 collective-permute-start.31
  122.9 3.7 %collective-permute-start.32 = (f32[1,512]{1,0:T(1,128)S(1)}, f32[1,512]{1,0:T(1,128)S(1)}, u32[]{:S(2)}, u32[]{:S(2)}) collective-permute-start(f32[1,512]{1,0:T(1,128)S(1)} %get-tuple-element.48), channel_id=1, source_target_pairs={{0,8},{4,12},{8,0},{12,4},{16,24},{20,28},{24,16},{28,20},{1,9},{5... | collective-permute-start | bytes 6152 | tf_op jit(solution)/shard_map/ppermute | solution.py:346
  124.4 3.6 %collective-permute-start.33 = (f32[1,512]{1,0:T(1,128)S(1)}, f32[1,512]{1,0:T(1,128)S(1)}, u32[]{:S(2)}, u32[]{:S(2)}) collective-permute-start(f32[1,512]{1,0:T(1,128)S(1)} %get-tuple-element.49), channel_id=1, source_target_pairs={{0,16},{4,20},{8,24},{12,28},{16,0},{20,4},{24,8},{28,12},{1,17},{... | collective-permute-start | bytes 6152 | tf_op jit(solution)/shard_map/ppermute | solution.py:346
  125.9 4.5 %collective-permute-start.34 = (f32[1,512]{1,0:T(1,128)S(1)}, f32[1,512]{1,0:T(1,128)S(1)}, u32[]{:S(2)}, u32[]{:S(2)}) collective-permute-start(f32[1,512]{1,0:T(1,128)S(1)} %get-tuple-element.50), channel_id=1, source_target_pairs={{0,24},{4,28},{8,16},{12,20},{16,8},{20,12},{24,0},{28,4},{1,25},{... | collective-permute-start | bytes 6152 | tf_op jit(solution)/shard_map/ppermute | solution.py:346

commit v7 on v6

--- a/solution.py
+++ b/solution.py
@@ -25,9 +25,9 @@
     return high, mid, low
 
 
-def project4(rows, matrix):
+def project4(rows, matrix_parts):
     total = None
-    for part in reversed(split3(matrix)):
+    for part in reversed(matrix_parts):
         term = jnp.dot(rows, part, preferred_element_type=jnp.float32)
         total = term if total is None else total + term
     return (total.astype(jnp.bfloat16).astype(jnp.float32) * 4.0).astype(jnp.bfloat16)
@@ -67,7 +67,7 @@
     return t_ref[g * width : (g + 1) * width, :LANES]
 
 
-def shifted_rows(a_ref, t_ref, pot_ref, aug_ref, lse_ref, top_ref, mass_ref, e_ref, carried_ref=None):
+def shifted_rows(a_ref, t_ref, pot_ref, aug_ref, lse_ref, top_ref, mass_ref, scores, e_ref=None, carried_ref=None):
     c = lax.axis_index("col")
     width = pot_ref.shape[1]
     blocks = pot_ref.shape[0]
@@ -87,28 +87,33 @@
         aug_ref[at, :LANES] = a
         aug_ref[at, LANES:] = jnp.where(lane == 0, 1.0, jnp.where(lane == 1, -top, 0.0)).astype(jnp.bfloat16)
         top_ref[row(i), :] = as_lanes(top)
-    for i in range(steps + 1):
-        mass, carried = None, None
-        for g in range(blocks):
-            cols = slice(g * width, (g + 1) * width)
-            if i < steps:
-                at = slice(i * LANES, (i + 1) * LANES)
-                s = lax.dot_general(aug_ref[at, :], t_ref[cols, :], NT_DIMS, preferred_element_type=jnp.float32)
-                e = jnp.exp(s)
+    rows = a_ref.shape[0]
+    half = rows // 2
+    for g in range(blocks + 1):
+        for h in range(0, rows, half):
+            at = slice(h, h + half)
+            if g < blocks:
+                t = t_ref[g * width : (g + 1) * width, :]
+                scores[g % 2, at, :] = lax.dot_general(aug_ref[at, :], t, NT_DIMS, preferred_element_type=jnp.float32)
+            if g > 0:
+                e = jnp.exp(scores[(g - 1) % 2, at, :])
                 m = lane_fold(jnp.add, e)
-                mass = m if mass is None else mass + m
-                e_ref[at, cols] = e.astype(jnp.bfloat16)
-            if i > 0 and carried_ref is not None:
-                before = slice((i - 1) * LANES, i * LANES)
-                d = jnp.dot(e_ref[before, cols], block_of(t_ref, g, width), preferred_element_type=jnp.float32)
-                carried = d if carried is None else carried + d
-        if i > 0 and carried_ref is not None:
-            carried_ref[before, :] = carried / last_mass
-        if i < steps:
-            last_mass = jnp.sum(mass, axis=1, keepdims=True)
-            mass_ref[row(i), :] = as_lanes(last_mass)
-    lse_ref[...] = top_ref[...] + jnp.log(mass_ref[...])
-    return within([mass_ref[...]])
+                mass_ref[at, :] = m if g == 1 else mass_ref[at, :] + m
+                e = e.astype(jnp.bfloat16)
+                if e_ref is not None:
+                    e_ref[at, (g - 1) * width : g * width] = e
+                if carried_ref is not None:
+                    d = jnp.dot(e, block_of(t_ref, g - 1, width), preferred_element_type=jnp.float32)
+                    carried_ref[at, :] = d if g == 1 else carried_ref[at, :] + d
+    masses = []
+    for i in range(steps):
+        at = slice(i * LANES, (i + 1) * LANES)
+        mass = jnp.sum(mass_ref[at, :], axis=1, keepdims=True)
+        masses.append(as_lanes(mass))
+        lse_ref[row(i), :] = top_ref[row(i), :] + jnp.log(masses[i])
+        if carried_ref is not None:
+            carried_ref[at, :] = carried_ref[at, :] / mass
+    return within(masses)
 
 
 def exact_rows(a_ref, t_ref, column, scores, lse_ref, top_ref=None, e_ref=None, carried_ref=None):
@@ -149,16 +154,27 @@
             carried_ref[rows, :] = carried / mass
 
 
+def own_kernel(own_ref, moment_ref, s_ref, a_ref, parts_ref):
+    s_ref[...] = own_ref[...]
+    for k, part in enumerate(split3(moment_ref[...])):
+        parts_ref[k] = part
+    a_ref[...] = project4(own_ref[...], split3(moment_ref[...]))
+
+
 def project_kernel(ns, *refs):
-    s_refs, moment_ref, a_ref = refs[:ns], refs[ns], refs[ns + 1]
-    piece = s_refs[0].shape[0]
+    s_refs, a_own_ref, parts_ref, s_ref, a_ref = refs[:ns], *refs[ns:]
+    piece = a_own_ref.shape[0]
+    a_ref[:piece, :] = a_own_ref[...]
     for k in range(ns):
-        a_ref[k * piece : (k + 1) * piece, :] = project4(s_refs[k][...], moment_ref[...])
+        at = slice(k * piece, (k + 1) * piece)
+        s_ref[at, :] = s_refs[k][...]
+        if k > 0:
+            a_ref[at, :] = project4(s_refs[k][...], [parts_ref[i] for i in range(3)])
 
 
 def couple_kernel(nt, width, *refs):
     a_ref, t_refs = refs[0], refs[1 : 1 + nt]
-    lse_ref, carried_ref, t_ref, pot_ref, top_ref, mass_ref, e_ref, aug_ref, scores = refs[1 + nt :]
+    lse_ref, carried_ref, t_ref, pot_ref, top_ref, mass_ref, aug_ref, ahead, scores = refs[1 + nt :]
     lane = lax.broadcasted_iota(jnp.int32, (LANES, LANES), 1)
     for g in range(nt):
         t_ref[g * width : (g + 1) * width, :LANES] = t_refs[g][:width, :]
@@ -169,7 +185,7 @@
             added = jnp.where(lane == 0, as_rows(row), jnp.where(lane == 1, 1.0, 0.0))
             t_ref[at : at + LANES, LANES:] = added.astype(jnp.bfloat16)
             pot_ref[g : g + 1, j * LANES : (j + 1) * LANES] = row
-    fine = shifted_rows(a_ref, t_ref, pot_ref, aug_ref, lse_ref, top_ref, mass_ref, e_ref, carried_ref)
+    fine = shifted_rows(a_ref, t_ref, pot_ref, aug_ref, lse_ref, top_ref, mass_ref, ahead, None, carried_ref)
 
     @pl.when(jnp.logical_not(fine))
     def _():
@@ -178,11 +194,10 @@
 
 
 def moment_kernel(ns, rows_total, *refs):
-    s_refs, l_refs, carried_ref = refs[:ns], refs[ns : 2 * ns], refs[2 * ns]
-    keep_ref, send_ref, weight_ref, total_ref = refs[2 * ns + 1 :]
+    s_ref, l_refs, carried_ref = refs[0], refs[1 : 1 + ns], refs[1 + ns]
+    keep_ref, send_ref, weight_ref, total_ref = refs[2 + ns :]
     c, r = lax.axis_index("col"), lax.axis_index("row")
-    piece = s_refs[0].shape[0]
-    per = piece // LANES
+    per = s_ref.shape[0] // ns // LANES
     shift = log_sum([l[...] for l in l_refs])
     weight_ref[...] = jnp.exp(l_refs[0][...] - shift) * (1.0 / rows_total)
     total = None
@@ -191,7 +206,7 @@
             w = as_rows(weight_ref[pl.ds((c ^ k) * per + j, 1), :])
             at = (k * per + j) * LANES
             x = carried_ref[at : at + LANES, :] * w
-            s = s_refs[k][j * LANES : (j + 1) * LANES, :]
+            s = s_ref[at : at + LANES, :]
             for part in reversed(split3(x)):
                 term = lax.dot_general(s, part, TN_DIMS, preferred_element_type=jnp.float32)
                 total = term if total is None else total + term
@@ -209,16 +224,15 @@
     refs[-1][...] = log_sum([r[...] for r in refs[:-1]])
 
 
-def first_rows_kernel(ns, *refs):
-    s_refs, t_ref, pot_ref, m_refs = refs[:ns], refs[ns], refs[ns + 1], refs[ns + 2 : ns + 4]
-    moment_ref, a_ref, lse_ref, top_ref, e_ref, mass_ref, aug_ref, scores = refs[ns + 4 :]
+def first_rows_kernel(*refs):
+    s_ref, t_ref, pot_ref, m_refs = refs[0], refs[1], refs[2], refs[3:5]
+    moment_ref, a_ref, lse_ref, top_ref, e_ref, mass_ref, aug_ref, ahead, scores = refs[5:]
     r = lax.axis_index("row")
-    piece, half = s_refs[0].shape[0], m_refs[0].shape[0]
+    half = m_refs[0].shape[0]
     for k in range(2):
         moment_ref[pl.ds(pl.multiple_of((k ^ (r % 2)) * half, half), half), :] = m_refs[k][...]
-    for k in range(ns):
-        a_ref[k * piece : (k + 1) * piece, :] = project4(s_refs[k][...], moment_ref[...])
-    fine = shifted_rows(a_ref, t_ref, pot_ref, aug_ref, lse_ref, top_ref, mass_ref, e_ref)
+    a_ref[...] = project4(s_ref[...], split3(moment_ref[...]))
+    fine = shifted_rows(a_ref, t_ref, pot_ref, aug_ref, lse_ref, top_ref, mass_ref, ahead, e_ref)
 
     @pl.when(jnp.logical_not(fine))
     def _():
@@ -370,6 +384,8 @@
     flops, exps = 2 * rows * cols * depth, rows * cols
     row_scores = pltpu.VMEM((LANES, cols), f32)
     small = pltpu.VMEM(tile.shape, f32)
+    sums = pltpu.VMEM((rows, LANES), f32)
+    ahead = pltpu.VMEM((2, rows, width), f32)
     augmented = pltpu.VMEM((rows, 2 * depth), bf16)
 
     groups = width // LANES
@@ -377,14 +393,23 @@
     block = jnp.concatenate([target, tail], axis=0)
     far = exchange_chips(block)
     pieces = exchange(source, "col")
-    a, = call(functools.partial(project_kernel, ns), [projected], pieces + [prev_moment], flops=6 * rows * depth * depth)
+    own = shape((piece, depth), bf16)
+    s_own, a_own, moment_parts = call(
+        own_kernel, [own, own, shape((3, depth, depth), bf16)], [source, prev_moment], flops=6 * piece * depth * depth
+    )
+    s, a = call(
+        functools.partial(project_kernel, ns),
+        [projected, projected],
+        [s_own] + pieces[1:] + [a_own, moment_parts],
+        flops=6 * rows * depth * depth,
+    )
     far, a = lax.optimization_barrier((far, a))
     blocks = [x for pair in zip(far, [swap(x, "row", 1) for x in far]) for x in pair]
     lse, carried, t, pot = call(
         functools.partial(couple_kernel, nt, width),
         [tile, shape((rows, depth), f32), shape((cols, 2 * depth), bf16), shape((nt, width), f32)],
         [a] + blocks,
-        [small, small, pltpu.VMEM((rows, cols), bf16), augmented, row_scores],
+        [small, sums, augmented, ahead, row_scores],
         2 * flops,
         exps,
     )
@@ -392,7 +417,7 @@
     keep, send = call(
         functools.partial(moment_kernel, ns, rows_total),
         [half, half],
-        pieces + exchange(lse, "col") + [carried],
+        [s] + exchange(lse, "col") + [carried],
         [small, pltpu.VMEM((depth, depth), f32)],
         6 * rows * depth * depth,
     )
@@ -400,10 +425,10 @@
     part = combine(add_kernel, exchange(part, "col"))
     part = combine(add_kernel, exchange_chips(part))
     moment, a, lse, top, e = call(
-        functools.partial(first_rows_kernel, ns),
+        first_rows_kernel,
         [shape((depth, depth), f32), projected, tile, tile, shape((rows, cols), bf16)],
-        pieces + [t, pot, part, swap(part, "row", 1)],
-        [small, augmented, row_scores],
+        [s, t, pot, part, swap(part, "row", 1)],
+        [sums, augmented, ahead, row_scores],
         flops,
         exps,
     )

time: 131 us -> 124 us (0.947)
  Pallas kernels: 59.4 us -> 52.8 us
    pallas_call x13 -> x14, Pallas kernels: 59.4 us -> 52.8 us  [call(): pl.pallas_call(kernel, out_shape=list(out), in_specs=[vmem] * len(args),...]
where the time goes in v7:
time: 124 us; the launch traced here: 123 us
  Pallas kernels  52.8 us (43%)
  starting transfers between devices  38.8 us (31%)
  waiting for transfers between devices  28.5 us (23%)
  local copies, waits for them, and re-layouts  1.68 us (1%)
    pallas_call x14, Pallas kernels, call(): pl.pallas_call(kernel, out_shape=list(out), in_specs=[vmem] * len(args),...  52.8 us
    ppermute x35, starting transfers between devices, swap(): lax.ppermute(x, axis, [(i, i ^ k) for i in range(lax.axis_size(axis))])  38.8 us
    ppermute x35, waiting for transfers between devices, swap(): lax.ppermute(x, axis, [(i, i ^ k) for i in range(lax.axis_size(axis))])  28.5 us
  transfers between devices with their start and end apart: 35, of which 29 were waited for; matrix products, arithmetic and copies ran while one was open for 1% of the time, Pallas kernels for 0%

profile of v7, /device:TPU:0, one launch (start us, length us, event | category | flops | bytes accessed | tf_op | source)
XLA Modules:
  0.0 123.4 jit_solution(4357186122541709614)
XLA Ops:
  0.6 3.1 %collective-permute-start = (bf16[256,128]{1,0:T(8,128)(2,1)}, bf16[256,128]{1,0:T(8,128)(2,1)S(1)}, u32[]{:S(2)}, u32[]{:S(2)}) collective-permute-start(bf16[256,128]{1,0:T(8,128)(2,1)} %own_ref.1), channel_id=1, source_target_pairs={{0,1},{1,0},{2,3},{3,2},{4,5},{5,4},{6,7},{7,6},{8,9},{9,8},{10,11... | collective-permute-start | bytes 196616 | tf_op jit(solution)/shard_map/ppermute | solution.py:360
  3.7 0.9 fusion.1.refs_1_
  4.7 2.5 %collective-permute-start.5 = (bf16[528,128]{1,0:T(8,128)(2,1)S(1)}, bf16[528,128]{1,0:T(8,128)(2,1)S(1)}, u32[]{:S(2)}, u32[]{:S(2)}) collective-permute-start(bf16[528,128]{1,0:T(8,128)(2,1)S(1)} %fusion.1.refs_1_), channel_id=1, source_target_pairs={{0,24},{4,28},{8,16},{12,20},{16,8},{20,12},{24,0},{28,4},{1,25},{... | collective-permute-start | bytes 405512 | tf_op jit(solution)/shard_map/ppermute | solution.py:360
  7.2 0.5 collective-permute-start.4
  7.7 0.5 collective-permute-start.3
  8.2 2.5 %collective-permute-start.2 = (bf16[256,128]{1,0:T(8,128)(2,1)}, bf16[256,128]{1,0:T(8,128)(2,1)S(1)}, u32[]{:S(2)}, u32[]{:S(2)}) collective-permute-start(bf16[256,128]{1,0:T(8,128)(2,1)} %own_ref.1), channel_id=1, source_target_pairs={{0,3},{1,2},{2,1},{3,0},{4,7},{5,6},{6,5},{7,4},{8,11},{9,10},{10,... | collective-permute-start | bytes 196616 | tf_op jit(solution)/shard_map/ppermute | solution.py:360
  10.8 0.8 copy-done
  11.6 0.8 copy-done.1
  12.7 1.8 %collective-permute-done.2.refs_3_ = bf16[256,128]{1,0:T(8,128)(2,1)S(1)} collective-permute-done((bf16[256,128]{1,0:T(8,128)(2,1)}, bf16[256,128]{1,0:T(8,128)(2,1)S(1)}, u32[]{:S(2)}, u32[]{:S(2)}) %collective-permute-start.2) | collective-permute-done | bytes 65568 | tf_op jit(solution)/shard_map/ppermute | solution.py:360
  14.5 2.3 %collective-permute-done.1.refs_2_ = bf16[256,128]{1,0:T(8,128)(2,1)S(1)} collective-permute-done((bf16[256,128]{1,0:T(8,128)(2,1)}, bf16[256,128]{1,0:T(8,128)(2,1)S(1)}, u32[]{:S(2)}, u32[]{:S(2)}) %collective-permute-start.1) | collective-permute-done | bytes 65568 | tf_op jit(solution)/shard_map/ppermute | solution.py:360
  16.8 0.3 shard_map.68
  17.2 0.5 collective-permute-start.7
  17.8 0.4 collective-permute-start.9
  18.2 0.3 collective-permute-done.6.refs_2_
  18.7 0.3 collective-permute-done.8.refs_6_
  19.2 15.2 %shard_map.69 = (f32[8,128]{1,0:T(8,128)S(1)}, f32[1024,128]{1,0:T(8,128)S(1)}, bf16[4096,256]{1,0:T(8,128)(2,1)S(1)}, f32[8,512]{1,0:T(8,128)S(1)}) custom-call(bf16[1024,128]{1,0:T(8,128)(2,1)S(1)} %get-tuple-element.37.refs_0_, bf16[528,128]{1,0:T(8,128)(2,1)S(1)} %fusion.1.refs_1_, bf16[528,128]{1,0:T(8,128)(2,1)S(1)} %collective-permute-done.6.refs_2_, ...), custom_call_target="tpu_custom_call" | custom-call | flops 2147483648 | bytes 3985408 | tf_op jit(solution)/shard_map/pallas_call | solution.py:348
  34.4 2.2 %collective-permute-start.12 = (f32[8,128]{1,0:T(8,128)S(1)}, f32[8,128]{1,0:T(8,128)S(1)}, u32[]{:S(2)}, u32[]{:S(2)}) collective-permute-start(f32[8,128]{1,0:T(8,128)S(1)} %get-tuple-element.44.refs_1_), channel_id=1, source_target_pairs={{0,3},{1,2},{2,1},{3,0},{4,7},{5,6},{6,5},{7,4},{8,11},{9,10},{10,... | collective-permute-start | bytes 12296 | tf_op jit(solution)/shard_map/ppermute | solution.py:360
  36.6 2.2 %collective-permute-start.10 = (f32[8,128]{1,0:T(8,128)S(1)}, f32[8,128]{1,0:T(8,128)S(1)}, u32[]{:S(2)}, u32[]{:S(2)}) collective-permute-start(f32[8,128]{1,0:T(8,128)S(1)} %get-tuple-element.44.refs_1_), channel_id=1, source_target_pairs={{0,1},{1,0},{2,3},{3,2},{4,5},{5,4},{6,7},{7,6},{8,9},{9,8},{10,11... | collective-permute-start | bytes 12296 | tf_op jit(solution)/shard_map/ppermute | solution.py:360
  38.9 1.0 collective-permute-done.12.refs_4_
  39.9 1.2 %collective-permute-done.11.refs_3_ = f32[8,128]{1,0:T(8,128)S(1)} collective-permute-done((f32[8,128]{1,0:T(8,128)S(1)}, f32[8,128]{1,0:T(8,128)S(1)}, u32[]{:S(2)}, u32[]{:S(2)}) %collective-permute-start.11) | collective-permute-done | bytes 4128 | tf_op jit(solution)/shard_map/ppermute | solution.py:360
  41.2 0.5 shard_map.70
  41.8 1.2 collective-permute-done.13.refs_1_
  43.0 1.7 %collective-permute-start.16 = (f32[64,128]{1,0:T(8,128)S(1)}, f32[64,128]{1,0:T(8,128)S(1)}, u32[]{:S(2)}, u32[]{:S(2)}) collective-permute-start(f32[64,128]{1,0:T(8,128)S(1)} %shard_map.71.refs_0_), channel_id=1, source_target_pairs={{0,3},{1,2},{2,1},{3,0},{4,7},{5,6},{6,5},{7,4},{8,11},{9,10},{10,... | collective-permute-start | bytes 98312 | tf_op jit(solution)/shard_map/ppermute | solution.py:360
  44.7 1.1 collective-permute-start.15
  45.8 1.6 %collective-permute-start.14 = (f32[64,128]{1,0:T(8,128)S(1)}, f32[64,128]{1,0:T(8,128)S(1)}, u32[]{:S(2)}, u32[]{:S(2)}) collective-permute-start(f32[64,128]{1,0:T(8,128)S(1)} %shard_map.71.refs_0_), channel_id=1, source_target_pairs={{0,1},{1,0},{2,3},{3,2},{4,5},{5,4},{6,7},{7,6},{8,9},{9,8},{10,11... | collective-permute-start | bytes 98312 | tf_op jit(solution)/shard_map/ppermute | solution.py:360
  47.4 1.6 %collective-permute-done.16.refs_3_ = f32[64,128]{1,0:T(8,128)S(1)} collective-permute-done((f32[64,128]{1,0:T(8,128)S(1)}, f32[64,128]{1,0:T(8,128)S(1)}, u32[]{:S(2)}, u32[]{:S(2)}) %collective-permute-start.16) | collective-permute-done | bytes 32800 | tf_op jit(solution)/shard_map/ppermute | solution.py:360
  49.0 0.5 collective-permute-done.15.refs_2_
  49.5 0.3 collective-permute-done.14.refs_1_
  49.8 2.5 %collective-permute-start.19 = (f32[64,128]{1,0:T(8,128)S(1)}, f32[64,128]{1,0:T(8,128)S(1)}, u32[]{:S(2)}, u32[]{:S(2)}) collective-permute-start(f32[64,128]{1,0:T(8,128)S(1)} %shard_map.72.refs_0_), channel_id=1, source_target_pairs={{0,24},{4,28},{8,16},{12,20},{16,8},{20,12},{24,0},{28,4},{1,25},{... | collective-permute-start | bytes 98312 | tf_op jit(solution)/shard_map/ppermute | solution.py:360
  52.3 0.5 collective-permute-start.18
  52.8 0.5 collective-permute-start.17
  53.4 1.3 %collective-permute-done.19.refs_3_ = f32[64,128]{1,0:T(8,128)S(1)} collective-permute-done((f32[64,128]{1,0:T(8,128)S(1)}, f32[64,128]{1,0:T(8,128)S(1)}, u32[]{:S(2)}, u32[]{:S(2)}) %collective-permute-start.19) | collective-permute-done | bytes 32800 | tf_op jit(solution)/shard_map/ppermute | solution.py:360
  54.7 1.5 %collective-permute-done.18.refs_2_ = f32[64,128]{1,0:T(8,128)S(1)} collective-permute-done((f32[64,128]{1,0:T(8,128)S(1)}, f32[64,128]{1,0:T(8,128)S(1)}, u32[]{:S(2)}, u32[]{:S(2)}) %collective-permute-start.18) | collective-permute-done | bytes 32800 | tf_op jit(solution)/shard_map/ppermute | solution.py:360
  56.3 0.5 collective-permute-done.17.refs_1_
  56.9 1.2 collective-permute-done.20.refs_4_
  58.0 12.3 %shard_map.74 = (f32[128,128]{1,0:T(8,128)}, bf16[1024,128]{1,0:T(8,128)(2,1)S(1)}, f32[8,128]{1,0:T(8,128)S(1)}, f32[8,128]{1,0:T(8,128)S(1)}, bf16[1024,4096]{1,0:T(8,128)(2,1)S(1)}) custom-call(bf16[1024,128]{1,0:T(8,128)(2,1)S(1)} %get-tuple-element.35.refs_0_, bf16[4096,256]{1,0:T(8,128)(2,1)S(1)} %get-tuple-element.42.refs_1_.refs_3_, ...), custom_call_target="tpu_custom_call" | custom-call | flops 1073741824 | bytes 11165696 | tf_op jit(solution)/shard_map/pallas_call | solution.py:348
  70.4 2.3 %collective-permute-start.23 = (f32[8,128]{1,0:T(8,128)S(1)}, f32[8,128]{1,0:T(8,128)S(1)}, u32[]{:S(2)}, u32[]{:S(2)}) collective-permute-start(f32[8,128]{1,0:T(8,128)S(1)} %get-tuple-element.52.refs_5_), channel_id=1, source_target_pairs={{0,3},{1,2},{2,1},{3,0},{4,7},{5,6},{6,5},{7,4},{8,11},{9,10},{10,... | collective-permute-start | bytes 12296 | tf_op jit(solution)/shard_map/ppermute | solution.py:360
  72.7 0.6 collective-permute-start.22
  73.3 1.5 %collective-permute-start.21 = (f32[8,128]{1,0:T(8,128)S(1)}, f32[8,128]{1,0:T(8,128)S(1)}, u32[]{:S(2)}, u32[]{:S(2)}) collective-permute-start(f32[8,128]{1,0:T(8,128)S(1)} %get-tuple-element.52.refs_5_), channel_id=1, source_target_pairs={{0,1},{1,0},{2,3},{3,2},{4,5},{5,4},{6,7},{7,6},{8,9},{9,8},{10,11... | collective-permute-start | bytes 12296 | tf_op jit(solution)/shard_map/ppermute | solution.py:360
  74.8 1.0 collective-permute-done.23.refs_8_
  75.8 1.4 %collective-permute-done.22.refs_7_ = f32[8,128]{1,0:T(8,128)S(1)} collective-permute-done((f32[8,128]{1,0:T(8,128)S(1)}, f32[8,128]{1,0:T(8,128)S(1)}, u32[]{:S(2)}, u32[]{:S(2)}) %collective-permute-start.22) | collective-permute-done | bytes 4128 | tf_op jit(solution)/shard_map/ppermute | solution.py:360
  77.2 6.9 %shard_map.75 = (f32[8,512]{1,0:T(8,128)S(1)}, f32[8,128]{1,0:T(8,128)}) custom-call(bf16[1024,128]{1,0:T(8,128)(2,1)S(1)} %get-tuple-element.49.refs_0_, bf16[1024,4096]{1,0:T(8,128)(2,1)S(1)} %get-tuple-element.50.refs_1_, f32[8,128]{1,0:T(8,128)S(1)} %get-tuple-element.51.refs_2_, bf16[4096,256]{1,0:T(8,128)(2,1)S(1)} %get-tuple-element.42.refs_1_.refs_3_, ...), custom_call_target="tpu_custom_call" | custom-call | flops 67108864 | bytes 10805248 | tf_op jit(solution)/shard_map/pallas_call | solution.py:348
  84.1 1.2 collective-permute-done.24.refs_1_
  85.3 1.6 %collective-permute-start.27 = (f32[8,512]{1,0:T(8,128)S(1)}, f32[8,512]{1,0:T(8,128)S(1)}, u32[]{:S(2)}, u32[]{:S(2)}) collective-permute-start(f32[8,512]{1,0:T(8,128)S(1)} %shard_map.76.refs_5_), channel_id=1, source_target_pairs={{0,24},{4,28},{8,16},{12,20},{16,8},{20,12},{24,0},{28,4},{1,25},{... | collective-permute-start | bytes 49160 | tf_op jit(solution)/shard_map/ppermute | solution.py:360
  86.9 0.5 collective-permute-start.26
  87.4 1.5 %collective-permute-start.25 = (f32[8,512]{1,0:T(8,128)S(1)}, f32[8,512]{1,0:T(8,128)S(1)}, u32[]{:S(2)}, u32[]{:S(2)}) collective-permute-start(f32[8,512]{1,0:T(8,128)S(1)} %shard_map.76.refs_5_), channel_id=1, source_target_pairs={{0,8},{4,12},{8,0},{12,4},{16,24},{20,28},{24,16},{28,20},{1,9},{5... | collective-permute-start | bytes 49160 | tf_op jit(solution)/shard_map/ppermute | solution.py:360
  88.9 1.1 collective-permute-done.27.refs_8_
  90.0 0.6 collective-permute-done.26.refs_7_
  90.6 0.5 collective-permute-done.25.refs_6_
  91.1 10.0 %shard_map.77.refs_5_ = f32[8,128]{1,0:T(8,128)S(1)} custom-call(bf16[1024,128]{1,0:T(8,128)(2,1)S(1)} %get-tuple-element.49.refs_0_, bf16[1024,4096]{1,0:T(8,128)(2,1)S(1)} %get-tuple-element.50.refs_1_, f32[8,128]{1,0:T(8,128)S(1)} %get-tuple-element.51.refs_2_, bf16[4096,256]{1,0:T(8,128)(2,1)S(1)} %get-tuple-element.42.refs_1_.refs_3_, ...), custom_call_target="tpu_custom_call" | custom-call | flops 67108864 | bytes 10838016 | tf_op jit(solution)/shard_map/pallas_call | solution.py:348
  101.1 1.6 %collective-permute-start.30 = (f32[8,128]{1,0:T(8,128)S(1)}, f32[8,128]{1,0:T(8,128)S(1)}, u32[]{:S(2)}, u32[]{:S(2)}) collective-permute-start(f32[8,128]{1,0:T(8,128)S(1)} %shard_map.77.refs_5_), channel_id=1, source_target_pairs={{0,3},{1,2},{2,1},{3,0},{4,7},{5,6},{6,5},{7,4},{8,11},{9,10},{10,... | collective-permute-start | bytes 12296 | tf_op jit(solution)/shard_map/ppermute | solution.py:360
  102.6 1.1 collective-permute-start.29
  103.8 1.7 %collective-permute-start.28 = (f32[8,128]{1,0:T(8,128)S(1)}, f32[8,128]{1,0:T(8,128)S(1)}, u32[]{:S(2)}, u32[]{:S(2)}) collective-permute-start(f32[8,128]{1,0:T(8,128)S(1)} %shard_map.77.refs_5_), channel_id=1, source_target_pairs={{0,1},{1,0},{2,3},{3,2},{4,5},{5,4},{6,7},{7,6},{8,9},{9,8},{10,11... | collective-permute-start | bytes 12296 | tf_op jit(solution)/shard_map/ppermute | solution.py:360
  105.5 1.0 collective-permute-done.30.refs_8_
  106.5 0.6 collective-permute-done.29.refs_7_
  107.1 0.2 collective-permute-done.28.refs_6_
  107.4 6.7 %shard_map.78 = (f32[4,1,512]{2,1,0:T(1,128)S(1)}, f32[4,1,512]{2,1,0:T(1,128)S(1)}, f32[8,128]{1,0:T(8,128)}) custom-call(bf16[1024,128]{1,0:T(8,128)(2,1)S(1)} %get-tuple-element.49.refs_0_, bf16[1024,4096]{1,0:T(8,128)(2,1)S(1)} %get-tuple-element.50.refs_1_, f32[8,128]{1,0:T(8,128)S(1)} %get-tuple-element.51.refs_2_, ...), custom_call_target="tpu_custom_call" | custom-call | flops 67108864 | bytes 10805248 | tf_op jit(solution)/shard_map/pallas_call | solution.py:348
  114.1 1.2 collective-permute-done.31.y_ref
  115.2 1.6 %collective-permute-start.32 = (f32[1,512]{1,0:T(1,128)S(1)}, f32[1,512]{1,0:T(1,128)S(1)}, u32[]{:S(2)}, u32[]{:S(2)}) collective-permute-start(f32[1,512]{1,0:T(1,128)S(1)} %get-tuple-element.58), channel_id=1, source_target_pairs={{0,8},{4,12},{8,0},{12,4},{16,24},{20,28},{24,16},{28,20},{1,9},{5... | collective-permute-start | bytes 6152 | tf_op jit(solution)/shard_map/ppermute | solution.py:360
  116.8 1.5 %collective-permute-start.33 = (f32[1,512]{1,0:T(1,128)S(1)}, f32[1,512]{1,0:T(1,128)S(1)}, u32[]{:S(2)}, u32[]{:S(2)}) collective-permute-start(f32[1,512]{1,0:T(1,128)S(1)} %get-tuple-element.59), channel_id=1, source_target_pairs={{0,16},{4,20},{8,24},{12,28},{16,0},{20,4},{24,8},{28,12},{1,17},{... | collective-permute-start | bytes 6152 | tf_op jit(solution)/shard_map/ppermute | solution.py:360
  118.3 0.5 collective-permute-start.34
  118.9 1.5 %collective-permute-done.33.refs_2_ = f32[1,512]{1,0:T(1,128)S(1)} collective-permute-done((f32[1,512]{1,0:T(1,128)S(1)}, f32[1,512]{1,0:T(1,128)S(1)}, u32[]{:S(2)}, u32[]{:S(2)}) %collective-permute-start.33) | collective-permute-done | bytes 2080 | tf_op jit(solution)/shard_map/ppermute | solution.py:360
  120.4 2.4 %collective-permute-done.34.refs_3_ = f32[1,512]{1,0:T(1,128)S(1)} collective-permute-done((f32[1,512]{1,0:T(1,128)S(1)}, f32[1,512]{1,0:T(1,128)S(1)}, u32[]{:S(2)}, u32[]{:S(2)}) %collective-permute-start.34) | collective-permute-done | bytes 2080 | tf_op jit(solution)/shard_map/ppermute | solution.py:360
  122.8 0.6 shard_map.80
  (25 shorter events, 1.2 us)
Async XLA Ops:
  0.6 10.1 %collective-permute-start = (bf16[256,128]{1,0:T(8,128)(2,1)}, bf16[256,128]{1,0:T(8,128)(2,1)S(1)}, u32[]{:S(2)}, u32[]{:S(2)}) collective-permute-start(bf16[256,128]{1,0:T(8,128)(2,1)} %own_ref.1), channel_id=1, source_target_pairs={{0,1},{1,0},{2,3},{3,2},{4,5},{5,4},{6,7},{7,6},{8,9},{9,8},{10,11... | collective-permute-start | bytes 196616 | tf_op jit(solution)/shard_map/ppermute | solution.py:360
  4.7 12.4 %collective-permute-start.5 = (bf16[528,128]{1,0:T(8,128)(2,1)S(1)}, bf16[528,128]{1,0:T(8,128)(2,1)S(1)}, u32[]{:S(2)}, u32[]{:S(2)}) collective-permute-start(bf16[528,128]{1,0:T(8,128)(2,1)S(1)} %fusion.1.refs_1_), channel_id=1, source_target_pairs={{0,24},{4,28},{8,16},{12,20},{16,8},{20,12},{24,0},{28,4},{1,25},{... | collective-permute-start | bytes 405512 | tf_op jit(solution)/shard_map/ppermute | solution.py:360
  7.2 9.9 %collective-permute-start.4 = (bf16[528,128]{1,0:T(8,128)(2,1)S(1)}, bf16[528,128]{1,0:T(8,128)(2,1)S(1)}, u32[]{:S(2)}, u32[]{:S(2)}) collective-permute-start(bf16[528,128]{1,0:T(8,128)(2,1)S(1)} %fusion.1.refs_1_), channel_id=1, source_target_pairs={{0,16},{4,20},{8,24},{12,28},{16,0},{20,4},{24,8},{28,12},{1,17},{... | collective-permute-start | bytes 405512 | tf_op jit(solution)/shard_map/ppermute | solution.py:360
  7.7 9.4 %collective-permute-start.3 = (bf16[528,128]{1,0:T(8,128)(2,1)S(1)}, bf16[528,128]{1,0:T(8,128)(2,1)S(1)}, u32[]{:S(2)}, u32[]{:S(2)}) collective-permute-start(bf16[528,128]{1,0:T(8,128)(2,1)S(1)} %fusion.1.refs_1_), channel_id=1, source_target_pairs={{0,8},{4,12},{8,0},{12,4},{16,24},{20,28},{24,16},{28,20},{1,9},{5... | collective-permute-start | bytes 405512 | tf_op jit(solution)/shard_map/ppermute | solution.py:360
  8.2 6.3 %collective-permute-start.2 = (bf16[256,128]{1,0:T(8,128)(2,1)}, bf16[256,128]{1,0:T(8,128)(2,1)S(1)}, u32[]{:S(2)}, u32[]{:S(2)}) collective-permute-start(bf16[256,128]{1,0:T(8,128)(2,1)} %own_ref.1), channel_id=1, source_target_pairs={{0,3},{1,2},{2,1},{3,0},{4,7},{5,6},{6,5},{7,4},{8,11},{9,10},{10,... | collective-permute-start | bytes 196616 | tf_op jit(solution)/shard_map/ppermute | solution.py:360
  10.7 6.1 %collective-permute-start.1 = (bf16[256,128]{1,0:T(8,128)(2,1)}, bf16[256,128]{1,0:T(8,128)(2,1)S(1)}, u32[]{:S(2)}, u32[]{:S(2)}) collective-permute-start(bf16[256,128]{1,0:T(8,128)(2,1)} %own_ref.1), channel_id=1, source_target_pairs={{0,2},{1,3},{2,0},{3,1},{4,6},{5,7},{6,4},{7,5},{8,10},{9,11},{10,... | collective-permute-start | bytes 196616 | tf_op jit(solution)/shard_map/ppermute | solution.py:360
  10.8 0.8 copy-start
  11.6 0.8 copy-start.1
  17.1 1.4 %collective-permute-start.6 = (bf16[528,128]{1,0:T(8,128)(2,1)S(1)}, bf16[528,128]{1,0:T(8,128)(2,1)S(1)}, u32[]{:S(2)}, u32[]{:S(2)}) collective-permute-start(bf16[528,128]{1,0:T(8,128)(2,1)S(1)} %fusion.1.refs_1_), channel_id=1, source_target_pairs={{0,4},{4,0},{8,12},{12,8},{16,20},{20,16},{24,28},{28,24},{1,5},{5... | collective-permute-start | bytes 405512 | tf_op jit(solution)/shard_map/ppermute | solution.py:360
  17.2 1.5 %collective-permute-start.7 = (bf16[528,128]{1,0:T(8,128)(2,1)S(1)}, bf16[528,128]{1,0:T(8,128)(2,1)S(1)}, u32[]{:S(2)}, u32[]{:S(2)}) collective-permute-start(bf16[528,128]{1,0:T(8,128)(2,1)S(1)} %collective-permute-done.3.refs_3_), channel_id=1, source_target_pairs={{0,4},{4,0},{8,12},{12,8},{16,20},{20,16},{24,28},{28,24},{1,5},{5... | collective-permute-start | bytes 405512 | tf_op jit(solution)/shard_map/ppermute | solution.py:360
  17.7 1.4 %collective-permute-start.8 = (bf16[528,128]{1,0:T(8,128)(2,1)S(1)}, bf16[528,128]{1,0:T(8,128)(2,1)S(1)}, u32[]{:S(2)}, u32[]{:S(2)}) collective-permute-start(bf16[528,128]{1,0:T(8,128)(2,1)S(1)} %collective-permute-done.4.refs_5_), channel_id=1, source_target_pairs={{0,4},{4,0},{8,12},{12,8},{16,20},{20,16},{24,28},{28,24},{1,5},{5... | collective-permute-start | bytes 405512 | tf_op jit(solution)/shard_map/ppermute | solution.py:360
  17.8 1.5 %collective-permute-start.9 = (bf16[528,128]{1,0:T(8,128)(2,1)S(1)}, bf16[528,128]{1,0:T(8,128)(2,1)S(1)}, u32[]{:S(2)}, u32[]{:S(2)}) collective-permute-start(bf16[528,128]{1,0:T(8,128)(2,1)S(1)} %collective-permute-done.5.refs_7_), channel_id=1, source_target_pairs={{0,4},{4,0},{8,12},{12,8},{16,20},{20,16},{24,28},{28,24},{1,5},{5... | collective-permute-start | bytes 405512 | tf_op jit(solution)/shard_map/ppermute | solution.py:360
  34.4 5.5 %collective-permute-start.12 = (f32[8,128]{1,0:T(8,128)S(1)}, f32[8,128]{1,0:T(8,128)S(1)}, u32[]{:S(2)}, u32[]{:S(2)}) collective-permute-start(f32[8,128]{1,0:T(8,128)S(1)} %get-tuple-element.44.refs_1_), channel_id=1, source_target_pairs={{0,3},{1,2},{2,1},{3,0},{4,7},{5,6},{6,5},{7,4},{8,11},{9,10},{10,... | collective-permute-start | bytes 12296 | tf_op jit(solution)/shard_map/ppermute | solution.py:360
  36.6 4.5 %collective-permute-start.11 = (f32[8,128]{1,0:T(8,128)S(1)}, f32[8,128]{1,0:T(8,128)S(1)}, u32[]{:S(2)}, u32[]{:S(2)}) collective-permute-start(f32[8,128]{1,0:T(8,128)S(1)} %get-tuple-element.44.refs_1_), channel_id=1, source_target_pairs={{0,2},{1,3},{2,0},{3,1},{4,6},{5,7},{6,4},{7,5},{8,10},{9,11},{10,... | collective-permute-start | bytes 12296 | tf_op jit(solution)/shard_map/ppermute | solution.py:360
  36.6 4.5 %collective-permute-start.10 = (f32[8,128]{1,0:T(8,128)S(1)}, f32[8,128]{1,0:T(8,128)S(1)}, u32[]{:S(2)}, u32[]{:S(2)}) collective-permute-start(f32[8,128]{1,0:T(8,128)S(1)} %get-tuple-element.44.refs_1_), channel_id=1, source_target_pairs={{0,1},{1,0},{2,3},{3,2},{4,5},{5,4},{6,7},{7,6},{8,9},{9,8},{10,11... | collective-permute-start | bytes 12296 | tf_op jit(solution)/shard_map/ppermute | solution.py:360
  41.7 1.3 %collective-permute-start.13 = (f32[64,128]{1,0:T(8,128)S(1)}, f32[64,128]{1,0:T(8,128)S(1)}, u32[]{:S(2)}, u32[]{:S(2)}) collective-permute-start(f32[64,128]{1,0:T(8,128)S(1)} %get-tuple-element.47), channel_id=1, source_target_pairs={{0,4},{4,0},{8,12},{12,8},{16,20},{20,16},{24,28},{28,24},{1,5},{5... | collective-permute-start | bytes 98312 | tf_op jit(solution)/shard_map/ppermute | solution.py:360
  43.0 6.0 %collective-permute-start.16 = (f32[64,128]{1,0:T(8,128)S(1)}, f32[64,128]{1,0:T(8,128)S(1)}, u32[]{:S(2)}, u32[]{:S(2)}) collective-permute-start(f32[64,128]{1,0:T(8,128)S(1)} %shard_map.71.refs_0_), channel_id=1, source_target_pairs={{0,3},{1,2},{2,1},{3,0},{4,7},{5,6},{6,5},{7,4},{8,11},{9,10},{10,... | collective-permute-start | bytes 98312 | tf_op jit(solution)/shard_map/ppermute | solution.py:360
  44.7 4.8 %collective-permute-start.15 = (f32[64,128]{1,0:T(8,128)S(1)}, f32[64,128]{1,0:T(8,128)S(1)}, u32[]{:S(2)}, u32[]{:S(2)}) collective-permute-start(f32[64,128]{1,0:T(8,128)S(1)} %shard_map.71.refs_0_), channel_id=1, source_target_pairs={{0,2},{1,3},{2,0},{3,1},{4,6},{5,7},{6,4},{7,5},{8,10},{9,11},{10,... | collective-permute-start | bytes 98312 | tf_op jit(solution)/shard_map/ppermute | solution.py:360
  45.8 4.0 %collective-permute-start.14 = (f32[64,128]{1,0:T(8,128)S(1)}, f32[64,128]{1,0:T(8,128)S(1)}, u32[]{:S(2)}, u32[]{:S(2)}) collective-permute-start(f32[64,128]{1,0:T(8,128)S(1)} %shard_map.71.refs_0_), channel_id=1, source_target_pairs={{0,1},{1,0},{2,3},{3,2},{4,5},{5,4},{6,7},{7,6},{8,9},{9,8},{10,11... | collective-permute-start | bytes 98312 | tf_op jit(solution)/shard_map/ppermute | solution.py:360
  49.8 4.9 %collective-permute-start.19 = (f32[64,128]{1,0:T(8,128)S(1)}, f32[64,128]{1,0:T(8,128)S(1)}, u32[]{:S(2)}, u32[]{:S(2)}) collective-permute-start(f32[64,128]{1,0:T(8,128)S(1)} %shard_map.72.refs_0_), channel_id=1, source_target_pairs={{0,24},{4,28},{8,16},{12,20},{16,8},{20,12},{24,0},{28,4},{1,25},{... | collective-permute-start | bytes 98312 | tf_op jit(solution)/shard_map/ppermute | solution.py:360
  52.3 3.9 %collective-permute-start.18 = (f32[64,128]{1,0:T(8,128)S(1)}, f32[64,128]{1,0:T(8,128)S(1)}, u32[]{:S(2)}, u32[]{:S(2)}) collective-permute-start(f32[64,128]{1,0:T(8,128)S(1)} %shard_map.72.refs_0_), channel_id=1, source_target_pairs={{0,16},{4,20},{8,24},{12,28},{16,0},{20,4},{24,8},{28,12},{1,17},{... | collective-permute-start | bytes 98312 | tf_op jit(solution)/shard_map/ppermute | solution.py:360
  52.8 3.9 %collective-permute-start.17 = (f32[64,128]{1,0:T(8,128)S(1)}, f32[64,128]{1,0:T(8,128)S(1)}, u32[]{:S(2)}, u32[]{:S(2)}) collective-permute-start(f32[64,128]{1,0:T(8,128)S(1)} %shard_map.72.refs_0_), channel_id=1, source_target_pairs={{0,8},{4,12},{8,0},{12,4},{16,24},{20,28},{24,16},{28,20},{1,9},{5... | collective-permute-start | bytes 98312 | tf_op jit(solution)/shard_map/ppermute | solution.py:360
  56.8 1.3 %collective-permute-start.20 = (f32[64,128]{1,0:T(8,128)S(1)}, f32[64,128]{1,0:T(8,128)S(1)}, u32[]{:S(2)}, u32[]{:S(2)}) collective-permute-start(f32[64,128]{1,0:T(8,128)S(1)} %shard_map.73.refs_3_), channel_id=1, source_target_pairs={{0,4},{4,0},{8,12},{12,8},{16,20},{20,16},{24,28},{28,24},{1,5},{5... | collective-permute-start | bytes 98312 | tf_op jit(solution)/shard_map/ppermute | solution.py:360
  70.4 5.4 %collective-permute-start.23 = (f32[8,128]{1,0:T(8,128)S(1)}, f32[8,128]{1,0:T(8,128)S(1)}, u32[]{:S(2)}, u32[]{:S(2)}) collective-permute-start(f32[8,128]{1,0:T(8,128)S(1)} %get-tuple-element.52.refs_5_), channel_id=1, source_target_pairs={{0,3},{1,2},{2,1},{3,0},{4,7},{5,6},{6,5},{7,4},{8,11},{9,10},{10,... | collective-permute-start | bytes 12296 | tf_op jit(solution)/shard_map/ppermute | solution.py:360
  72.7 4.5 %collective-permute-start.22 = (f32[8,128]{1,0:T(8,128)S(1)}, f32[8,128]{1,0:T(8,128)S(1)}, u32[]{:S(2)}, u32[]{:S(2)}) collective-permute-start(f32[8,128]{1,0:T(8,128)S(1)} %get-tuple-element.52.refs_5_), channel_id=1, source_target_pairs={{0,2},{1,3},{2,0},{3,1},{4,6},{5,7},{6,4},{7,5},{8,10},{9,11},{10,... | collective-permute-start | bytes 12296 | tf_op jit(solution)/shard_map/ppermute | solution.py:360
  73.3 3.9 %collective-permute-start.21 = (f32[8,128]{1,0:T(8,128)S(1)}, f32[8,128]{1,0:T(8,128)S(1)}, u32[]{:S(2)}, u32[]{:S(2)}) collective-permute-start(f32[8,128]{1,0:T(8,128)S(1)} %get-tuple-element.52.refs_5_), channel_id=1, source_target_pairs={{0,1},{1,0},{2,3},{3,2},{4,5},{5,4},{6,7},{7,6},{8,9},{9,8},{10,11... | collective-permute-start | bytes 12296 | tf_op jit(solution)/shard_map/ppermute | solution.py:360
  84.1 1.2 collective-permute-start.24
  85.3 4.7 %collective-permute-start.27 = (f32[8,512]{1,0:T(8,128)S(1)}, f32[8,512]{1,0:T(8,128)S(1)}, u32[]{:S(2)}, u32[]{:S(2)}) collective-permute-start(f32[8,512]{1,0:T(8,128)S(1)} %shard_map.76.refs_5_), channel_id=1, source_target_pairs={{0,24},{4,28},{8,16},{12,20},{16,8},{20,12},{24,0},{28,4},{1,25},{... | collective-permute-start | bytes 49160 | tf_op jit(solution)/shard_map/ppermute | solution.py:360
  86.9 3.7 %collective-permute-start.26 = (f32[8,512]{1,0:T(8,128)S(1)}, f32[8,512]{1,0:T(8,128)S(1)}, u32[]{:S(2)}, u32[]{:S(2)}) collective-permute-start(f32[8,512]{1,0:T(8,128)S(1)} %shard_map.76.refs_5_), channel_id=1, source_target_pairs={{0,16},{4,20},{8,24},{12,28},{16,0},{20,4},{24,8},{28,12},{1,17},{... | collective-permute-start | bytes 49160 | tf_op jit(solution)/shard_map/ppermute | solution.py:360
  87.4 3.7 %collective-permute-start.25 = (f32[8,512]{1,0:T(8,128)S(1)}, f32[8,512]{1,0:T(8,128)S(1)}, u32[]{:S(2)}, u32[]{:S(2)}) collective-permute-start(f32[8,512]{1,0:T(8,128)S(1)} %shard_map.76.refs_5_), channel_id=1, source_target_pairs={{0,8},{4,12},{8,0},{12,4},{16,24},{20,28},{24,16},{28,20},{1,9},{5... | collective-permute-start | bytes 49160 | tf_op jit(solution)/shard_map/ppermute | solution.py:360
  101.1 5.4 %collective-permute-start.30 = (f32[8,128]{1,0:T(8,128)S(1)}, f32[8,128]{1,0:T(8,128)S(1)}, u32[]{:S(2)}, u32[]{:S(2)}) collective-permute-start(f32[8,128]{1,0:T(8,128)S(1)} %shard_map.77.refs_5_), channel_id=1, source_target_pairs={{0,3},{1,2},{2,1},{3,0},{4,7},{5,6},{6,5},{7,4},{8,11},{9,10},{10,... | collective-permute-start | bytes 12296 | tf_op jit(solution)/shard_map/ppermute | solution.py:360
  102.6 4.5 %collective-permute-start.29 = (f32[8,128]{1,0:T(8,128)S(1)}, f32[8,128]{1,0:T(8,128)S(1)}, u32[]{:S(2)}, u32[]{:S(2)}) collective-permute-start(f32[8,128]{1,0:T(8,128)S(1)} %shard_map.77.refs_5_), channel_id=1, source_target_pairs={{0,2},{1,3},{2,0},{3,1},{4,6},{5,7},{6,4},{7,5},{8,10},{9,11},{10,... | collective-permute-start | bytes 12296 | tf_op jit(solution)/shard_map/ppermute | solution.py:360
  103.8 3.6 %collective-permute-start.28 = (f32[8,128]{1,0:T(8,128)S(1)}, f32[8,128]{1,0:T(8,128)S(1)}, u32[]{:S(2)}, u32[]{:S(2)}) collective-permute-start(f32[8,128]{1,0:T(8,128)S(1)} %shard_map.77.refs_5_), channel_id=1, source_target_pairs={{0,1},{1,0},{2,3},{3,2},{4,5},{5,4},{6,7},{7,6},{8,9},{9,8},{10,11... | collective-permute-start | bytes 12296 | tf_op jit(solution)/shard_map/ppermute | solution.py:360
  114.1 1.2 collective-permute-start.31
  115.2 3.7 %collective-permute-start.32 = (f32[1,512]{1,0:T(1,128)S(1)}, f32[1,512]{1,0:T(1,128)S(1)}, u32[]{:S(2)}, u32[]{:S(2)}) collective-permute-start(f32[1,512]{1,0:T(1,128)S(1)} %get-tuple-element.58), channel_id=1, source_target_pairs={{0,8},{4,12},{8,0},{12,4},{16,24},{20,28},{24,16},{28,20},{1,9},{5... | collective-permute-start | bytes 6152 | tf_op jit(solution)/shard_map/ppermute | solution.py:360
  116.8 3.6 %collective-permute-start.33 = (f32[1,512]{1,0:T(1,128)S(1)}, f32[1,512]{1,0:T(1,128)S(1)}, u32[]{:S(2)}, u32[]{:S(2)}) collective-permute-start(f32[1,512]{1,0:T(1,128)S(1)} %get-tuple-element.59), channel_id=1, source_target_pairs={{0,16},{4,20},{8,24},{12,28},{16,0},{20,4},{24,8},{28,12},{1,17},{... | collective-permute-start | bytes 6152 | tf_op jit(solution)/shard_map/ppermute | solution.py:360
  118.3 4.5 %collective-permute-start.34 = (f32[1,512]{1,0:T(1,128)S(1)}, f32[1,512]{1,0:T(1,128)S(1)}, u32[]{:S(2)}, u32[]{:S(2)}) collective-permute-start(f32[1,512]{1,0:T(1,128)S(1)} %get-tuple-element.60), channel_id=1, source_target_pairs={{0,24},{4,28},{8,16},{12,20},{16,8},{20,12},{24,0},{28,4},{1,25},{... | collective-permute-start | bytes 6152 | tf_op jit(solution)/shard_map/ppermute | solution.py:360

commit v8 on v7

--- a/solution.py
+++ b/solution.py
@@ -67,59 +67,56 @@
     return t_ref[g * width : (g + 1) * width, :LANES]
 
 
-def shifted_rows(a_ref, t_ref, pot_ref, aug_ref, lse_ref, top_ref, mass_ref, scores, e_ref=None, carried_ref=None):
-    c = lax.axis_index("col")
-    width = pot_ref.shape[1]
-    blocks = pot_ref.shape[0]
+def row_of(i, steps):
+    per = steps // lax.axis_size("col")
+    return pl.ds((lax.axis_index("col") ^ (i // per)) * per + i % per, 1)
+
+
+def add_shifts(a_ref, t_ref, potential, aug_ref, top_ref):
     steps = a_ref.shape[0] // LANES
-    per = steps // lax.axis_size("col")
     lane = lax.broadcasted_iota(jnp.int32, (LANES, LANES), 1)
-
-    def row(i):
-        return pl.ds((c ^ (i // per)) * per + i % per, 1)
-
     for i in range(steps):
         at = slice(i * LANES, (i + 1) * LANES)
         a = a_ref[at, :]
-        s = lax.dot_general(a, block_of(t_ref, 0, width), NT_DIMS, preferred_element_type=jnp.float32)
-        top = jnp.max(lane_fold(jnp.maximum, s + pot_ref[0:1, :]), axis=1, keepdims=True)
+        s = lax.dot_general(a, t_ref[: potential.shape[1], :LANES], NT_DIMS, preferred_element_type=jnp.float32)
+        top = jnp.max(lane_fold(jnp.maximum, s + potential), axis=1, keepdims=True)
         top = top.astype(jnp.bfloat16).astype(jnp.float32)
         aug_ref[at, :LANES] = a
         aug_ref[at, LANES:] = jnp.where(lane == 0, 1.0, jnp.where(lane == 1, -top, 0.0)).astype(jnp.bfloat16)
-        top_ref[row(i), :] = as_lanes(top)
-    rows = a_ref.shape[0]
-    half = rows // 2
-    for g in range(blocks + 1):
-        for h in range(0, rows, half):
-            at = slice(h, h + half)
-            if g < blocks:
-                t = t_ref[g * width : (g + 1) * width, :]
-                scores[g % 2, at, :] = lax.dot_general(aug_ref[at, :], t, NT_DIMS, preferred_element_type=jnp.float32)
-            if g > 0:
-                e = jnp.exp(scores[(g - 1) % 2, at, :])
-                m = lane_fold(jnp.add, e)
-                mass_ref[at, :] = m if g == 1 else mass_ref[at, :] + m
-                e = e.astype(jnp.bfloat16)
-                if e_ref is not None:
-                    e_ref[at, (g - 1) * width : g * width] = e
-                if carried_ref is not None:
-                    d = jnp.dot(e, block_of(t_ref, g - 1, width), preferred_element_type=jnp.float32)
-                    carried_ref[at, :] = d if g == 1 else carried_ref[at, :] + d
+        top_ref[row_of(i, steps), :] = as_lanes(top)
+
+
+def shifted_rows(aug_ref, t_ref, width, lse_ref, top_ref, mass_ref, e_ref=None, carried_ref=None):
+    rows = aug_ref.shape[0]
+    steps = rows // LANES
+    for g in range(t_ref.shape[0] // width):
+        cols = slice(g * width, (g + 1) * width)
+        for h in range(0, rows, 2 * LANES):
+            at = slice(h, h + 2 * LANES)
+            s = lax.dot_general(aug_ref[at, :], t_ref[cols, :], NT_DIMS, preferred_element_type=jnp.float32)
+            e = jnp.exp(s)
+            m = lane_fold(jnp.add, e)
+            mass_ref[at, :] = m if g == 0 else mass_ref[at, :] + m
+            e = e.astype(jnp.bfloat16)
+            if e_ref is not None:
+                e_ref[at, cols] = e
+            if carried_ref is not None:
+                d = jnp.dot(e, block_of(t_ref, g, width), preferred_element_type=jnp.float32)
+                carried_ref[at, :] = d if g == 0 else carried_ref[at, :] + d
     masses = []
     for i in range(steps):
         at = slice(i * LANES, (i + 1) * LANES)
         mass = jnp.sum(mass_ref[at, :], axis=1, keepdims=True)
         masses.append(as_lanes(mass))
-        lse_ref[row(i), :] = top_ref[row(i), :] + jnp.log(masses[i])
+        row = row_of(i, steps)
+        lse_ref[row, :] = top_ref[row, :] + jnp.log(masses[i])
         if carried_ref is not None:
             carried_ref[at, :] = carried_ref[at, :] / mass
     return within(masses)
 
 
 def exact_rows(a_ref, t_ref, column, scores, lse_ref, top_ref=None, e_ref=None, carried_ref=None):
-    c = lax.axis_index("col")
     steps = a_ref.shape[0] // LANES
-    per = steps // lax.axis_size("col")
     width = column[0].shape[1]
 
     @pl.loop(0, steps)
@@ -146,7 +143,7 @@
                 d = jnp.dot(e.astype(jnp.bfloat16), t, preferred_element_type=jnp.float32)
                 carried = d if carried is None else carried + d
         mass = jnp.sum(mass, axis=1, keepdims=True)
-        row = pl.ds((c ^ (i // per)) * per + i % per, 1)
+        row = row_of(i, steps)
         lse_ref[row, :] = as_lanes(top + jnp.log(mass))
         if top_ref is not None:
             top_ref[row, :] = as_lanes(top)
@@ -172,20 +169,28 @@
             a_ref[at, :] = project4(s_refs[k][...], [parts_ref[i] for i in range(3)])
 
 
+def potential_of(block_ref, width):
+    tail = block_ref[width:, :].astype(jnp.float32)
+    return jnp.concatenate([tail[j : j + 1, :] for j in range(width // LANES)], axis=1)
+
+
+def shift_kernel(width, a_ref, block_ref, aug_ref, top_ref):
+    add_shifts(a_ref, block_ref, potential_of(block_ref, width), aug_ref, top_ref)
+
+
 def couple_kernel(nt, width, *refs):
-    a_ref, t_refs = refs[0], refs[1 : 1 + nt]
-    lse_ref, carried_ref, t_ref, pot_ref, top_ref, mass_ref, aug_ref, ahead, scores = refs[1 + nt :]
+    a_ref, aug_ref, top_ref, t_refs = refs[0], refs[1], refs[2], refs[3 : 3 + nt]
+    lse_ref, carried_ref, t_ref, pot_ref, mass_ref, scores = refs[3 + nt :]
     lane = lax.broadcasted_iota(jnp.int32, (LANES, LANES), 1)
     for g in range(nt):
         t_ref[g * width : (g + 1) * width, :LANES] = t_refs[g][:width, :]
-        potential = t_refs[g][width:, :].astype(jnp.float32)
-        for j in range(width // LANES):
-            row = potential[j : j + 1, :]
-            at = g * width + j * LANES
-            added = jnp.where(lane == 0, as_rows(row), jnp.where(lane == 1, 1.0, 0.0))
+        pot_ref[g : g + 1, :] = potential_of(t_refs[g], width)
+        for j in range(0, width, LANES):
+            potential = as_rows(pot_ref[g : g + 1, j : j + LANES])
+            added = jnp.where(lane == 0, potential, jnp.where(lane == 1, 1.0, 0.0))
+            at = g * width + j
             t_ref[at : at + LANES, LANES:] = added.astype(jnp.bfloat16)
-            pot_ref[g : g + 1, j * LANES : (j + 1) * LANES] = row
-    fine = shifted_rows(a_ref, t_ref, pot_ref, aug_ref, lse_ref, top_ref, mass_ref, ahead, None, carried_ref)
+    fine = shifted_rows(aug_ref, t_ref, width, lse_ref, top_ref, mass_ref, None, carried_ref)
 
     @pl.when(jnp.logical_not(fine))
     def _():
@@ -226,13 +231,14 @@
 
 def first_rows_kernel(*refs):
     s_ref, t_ref, pot_ref, m_refs = refs[0], refs[1], refs[2], refs[3:5]
-    moment_ref, a_ref, lse_ref, top_ref, e_ref, mass_ref, aug_ref, ahead, scores = refs[5:]
+    moment_ref, a_ref, lse_ref, top_ref, e_ref, mass_ref, aug_ref, scores = refs[5:]
     r = lax.axis_index("row")
     half = m_refs[0].shape[0]
     for k in range(2):
         moment_ref[pl.ds(pl.multiple_of((k ^ (r % 2)) * half, half), half), :] = m_refs[k][...]
     a_ref[...] = project4(s_ref[...], split3(moment_ref[...]))
-    fine = shifted_rows(a_ref, t_ref, pot_ref, aug_ref, lse_ref, top_ref, mass_ref, ahead, e_ref)
+    add_shifts(a_ref, t_ref, pot_ref[0:1, :], aug_ref, top_ref)
+    fine = shifted_rows(aug_ref, t_ref, pot_ref.shape[1], lse_ref, top_ref, mass_ref, e_ref)
 
     @pl.when(jnp.logical_not(fine))
     def _():
@@ -249,7 +255,7 @@
 def rows_kernel(rows_total, *refs):
     a_ref, e_ref, top_ref, t_ref, pot_ref = refs[:5]
     l_refs, (lse_ref, column_ref, weights, scores) = refs[5:-4], refs[-4:]
-    c, r = lax.axis_index("col"), lax.axis_index("row")
+    r = lax.axis_index("row")
     nt, width = pot_ref.shape
     column_ref[...] = math.log(rows_total) - log_sum([l[...] for l in l_refs])
     column = [column_ref[pl.ds(r ^ k, 1), :] for k in range(nt)]
@@ -258,13 +264,12 @@
     for k in range(nt):
         weights[:, k * width : (k + 1) * width] = high_low(jnp.exp(change[k] - top))
     steps = a_ref.shape[0] // LANES
-    per = steps // lax.axis_size("col")
     masses = []
     for i in range(steps):
         e = e_ref[i * LANES : (i + 1) * LANES, :]
         sums = lax.dot_general(weights[...], e, NT_DIMS, preferred_element_type=jnp.float32)
         masses.append(sums[0:1, :] + sums[1:2, :])
-        row = pl.ds((c ^ (i // per)) * per + i % per, 1)
+        row = row_of(i, steps)
         lse_ref[row, :] = top + top_ref[row, :] + jnp.log(masses[i])
 
     @pl.when(jnp.logical_not(within(masses)))
@@ -385,8 +390,6 @@
     row_scores = pltpu.VMEM((LANES, cols), f32)
     small = pltpu.VMEM(tile.shape, f32)
     sums = pltpu.VMEM((rows, LANES), f32)
-    ahead = pltpu.VMEM((2, rows, width), f32)
-    augmented = pltpu.VMEM((rows, 2 * depth), bf16)
 
     groups = width // LANES
     tail = jnp.pad(target_potential.reshape(groups, LANES), ((0, SUB - groups), (0, 0)))
@@ -405,11 +408,15 @@
     )
     far, a = lax.optimization_barrier((far, a))
     blocks = [x for pair in zip(far, [swap(x, "row", 1) for x in far]) for x in pair]
+    augmented = shape((rows, 2 * depth), bf16)
+    aug, top = call(
+        functools.partial(shift_kernel, width), [augmented, tile], [a, far[0]], flops=2 * rows * width * depth
+    )
     lse, carried, t, pot = call(
         functools.partial(couple_kernel, nt, width),
         [tile, shape((rows, depth), f32), shape((cols, 2 * depth), bf16), shape((nt, width), f32)],
-        [a] + blocks,
-        [small, sums, augmented, ahead, row_scores],
+        [a, aug, top] + blocks,
+        [sums, row_scores],
         2 * flops,
         exps,
     )
@@ -428,7 +435,7 @@
         first_rows_kernel,
         [shape((depth, depth), f32), projected, tile, tile, shape((rows, cols), bf16)],
         [s, t, pot, part, swap(part, "row", 1)],
-        [sums, augmented, ahead, row_scores],
+        [sums, pltpu.VMEM(augmented.shape, bf16), row_scores],
         flops,
         exps,
     )

time: 124 us -> 127 us (1.024)
  Pallas kernels: 52.8 us -> 56.6 us
    pallas_call x14 -> x15, Pallas kernels: 52.8 us -> 56.6 us  [call(): pl.pallas_call(kernel, out_shape=list(out), in_specs=[vmem] * len(args),...]
  transfers between devices with their start and end apart: 35 -> 35, of which waited for: 29 -> 27; matrix products, arithmetic and copies ran while one was open for 1% -> 1% of each run, Pallas kernels for 0% -> 1%
where the time goes in v8:
time: 127 us
  Pallas kernels  56.6 us (45%)
  starting transfers between devices  38.8 us (31%)
  waiting for transfers between devices  27.8 us (22%)
  local copies, waits for them, and re-layouts  1.68 us (1%)
    pallas_call x15, Pallas kernels, call(): pl.pallas_call(kernel, out_shape=list(out), in_specs=[vmem] * len(args),...  56.6 us
    ppermute x35, starting transfers between devices, swap(): lax.ppermute(x, axis, [(i, i ^ k) for i in range(lax.axis_size(axis))])  38.8 us
    ppermute x35, waiting for transfers between devices, swap(): lax.ppermute(x, axis, [(i, i ^ k) for i in range(lax.axis_size(axis))])  27.8 us
  transfers between devices with their start and end apart: 35, of which 27 were waited for; matrix products, arithmetic and copies ran while one was open for 1% of the time, Pallas kernels for 1%

profile of v8, /device:TPU:0, one launch (start us, length us, event | category | flops | bytes accessed | tf_op | source)
XLA Modules:
  0.0 126.5 jit_solution(5026224152124086237)
XLA Ops:
  0.6 3.1 %collective-permute-start = (bf16[256,128]{1,0:T(8,128)(2,1)}, bf16[256,128]{1,0:T(8,128)(2,1)S(1)}, u32[]{:S(2)}, u32[]{:S(2)}) collective-permute-start(bf16[256,128]{1,0:T(8,128)(2,1)} %own_ref.1), channel_id=1, source_target_pairs={{0,1},{1,0},{2,3},{3,2},{4,5},{5,4},{6,7},{7,6},{8,9},{9,8},{10,11... | collective-permute-start | bytes 196616 | tf_op jit(solution)/shard_map/ppermute | solution.py:365
  3.7 0.9 fusion.1.block_ref.refs_3_
  4.7 2.5 %collective-permute-start.5 = (bf16[528,128]{1,0:T(8,128)(2,1)S(1)}, bf16[528,128]{1,0:T(8,128)(2,1)S(1)}, u32[]{:S(2)}, u32[]{:S(2)}) collective-permute-start(bf16[528,128]{1,0:T(8,128)(2,1)S(1)} %fusion.1.block_ref.refs_3_), channel_id=1, source_target_pairs={{0,24},{4,28},{8,16},{12,20},{16,8},{20,12},{24,0},{28,4},{1,25},{... | collective-permute-start | bytes 405512 | tf_op jit(solution)/shard_map/ppermute | solution.py:365
  7.2 0.5 collective-permute-start.4
  7.7 0.5 collective-permute-start.3
  8.2 2.5 %collective-permute-start.2 = (bf16[256,128]{1,0:T(8,128)(2,1)}, bf16[256,128]{1,0:T(8,128)(2,1)S(1)}, u32[]{:S(2)}, u32[]{:S(2)}) collective-permute-start(bf16[256,128]{1,0:T(8,128)(2,1)} %own_ref.1), channel_id=1, source_target_pairs={{0,3},{1,2},{2,1},{3,0},{4,7},{5,6},{6,5},{7,4},{8,11},{9,10},{10,... | collective-permute-start | bytes 196616 | tf_op jit(solution)/shard_map/ppermute | solution.py:365
  10.8 0.8 copy-done
  11.6 0.8 copy-done.1
  12.5 0.2 shard_map.67
  12.7 1.8 %collective-permute-done.2.refs_3_ = bf16[256,128]{1,0:T(8,128)(2,1)S(1)} collective-permute-done((bf16[256,128]{1,0:T(8,128)(2,1)}, bf16[256,128]{1,0:T(8,128)(2,1)S(1)}, u32[]{:S(2)}, u32[]{:S(2)}) %collective-permute-start.2) | collective-permute-done | bytes 65568 | tf_op jit(solution)/shard_map/ppermute | solution.py:365
  14.5 2.3 %collective-permute-done.1.refs_2_ = bf16[256,128]{1,0:T(8,128)(2,1)S(1)} collective-permute-done((bf16[256,128]{1,0:T(8,128)(2,1)}, bf16[256,128]{1,0:T(8,128)(2,1)S(1)}, u32[]{:S(2)}, u32[]{:S(2)}) %collective-permute-start.1) | collective-permute-done | bytes 65568 | tf_op jit(solution)/shard_map/ppermute | solution.py:365
  16.8 0.3 shard_map.68
  17.2 0.5 collective-permute-start.8
  17.8 0.4 collective-permute-start.6
  18.2 0.7 shard_map.69
  19.2 17.8 %shard_map.70 = (f32[8,128]{1,0:T(8,128)S(1)}, f32[1024,128]{1,0:T(8,128)S(1)}, bf16[4096,256]{1,0:T(8,128)(2,1)S(1)}, f32[8,512]{1,0:T(8,128)S(1)}) custom-call(bf16[1024,128]{1,0:T(8,128)(2,1)S(1)} %get-tuple-element.39.a_ref.refs_0_, bf16[1024,256]{1,0:T(8,128)(2,1)S(1)} %get-tuple-element.41.refs_1_, f32[8,128]{1,0:T(8,128)S(1)} %get-tuple-element.42.refs_2_, ...), custom_call_target="tpu_custom_call" | custom-call | flops 2147483648 | bytes 4513792 | tf_op jit(solution)/shard_map/pallas_call | solution.py:353
  37.0 2.2 %collective-permute-start.12 = (f32[8,128]{1,0:T(8,128)S(1)}, f32[8,128]{1,0:T(8,128)S(1)}, u32[]{:S(2)}, u32[]{:S(2)}) collective-permute-start(f32[8,128]{1,0:T(8,128)S(1)} %get-tuple-element.48.refs_1_), channel_id=1, source_target_pairs={{0,3},{1,2},{2,1},{3,0},{4,7},{5,6},{6,5},{7,4},{8,11},{9,10},{10,... | collective-permute-start | bytes 12296 | tf_op jit(solution)/shard_map/ppermute | solution.py:365
  39.3 2.2 %collective-permute-start.10 = (f32[8,128]{1,0:T(8,128)S(1)}, f32[8,128]{1,0:T(8,128)S(1)}, u32[]{:S(2)}, u32[]{:S(2)}) collective-permute-start(f32[8,128]{1,0:T(8,128)S(1)} %get-tuple-element.48.refs_1_), channel_id=1, source_target_pairs={{0,1},{1,0},{2,3},{3,2},{4,5},{5,4},{6,7},{7,6},{8,9},{9,8},{10,11... | collective-permute-start | bytes 12296 | tf_op jit(solution)/shard_map/ppermute | solution.py:365
  41.5 1.0 collective-permute-done.12.refs_4_
  42.5 1.3 collective-permute-done.11.refs_3_
  43.8 0.5 shard_map.71
  44.4 1.2 collective-permute-done.13.refs_1_
  45.6 1.7 %collective-permute-start.16 = (f32[64,128]{1,0:T(8,128)S(1)}, f32[64,128]{1,0:T(8,128)S(1)}, u32[]{:S(2)}, u32[]{:S(2)}) collective-permute-start(f32[64,128]{1,0:T(8,128)S(1)} %shard_map.72.refs_0_), channel_id=1, source_target_pairs={{0,3},{1,2},{2,1},{3,0},{4,7},{5,6},{6,5},{7,4},{8,11},{9,10},{10,... | collective-permute-start | bytes 98312 | tf_op jit(solution)/shard_map/ppermute | solution.py:365
  47.3 1.1 collective-permute-start.15
  48.4 1.6 %collective-permute-start.14 = (f32[64,128]{1,0:T(8,128)S(1)}, f32[64,128]{1,0:T(8,128)S(1)}, u32[]{:S(2)}, u32[]{:S(2)}) collective-permute-start(f32[64,128]{1,0:T(8,128)S(1)} %shard_map.72.refs_0_), channel_id=1, source_target_pairs={{0,1},{1,0},{2,3},{3,2},{4,5},{5,4},{6,7},{7,6},{8,9},{9,8},{10,11... | collective-permute-start | bytes 98312 | tf_op jit(solution)/shard_map/ppermute | solution.py:365
  50.0 1.6 %collective-permute-done.16.refs_3_ = f32[64,128]{1,0:T(8,128)S(1)} collective-permute-done((f32[64,128]{1,0:T(8,128)S(1)}, f32[64,128]{1,0:T(8,128)S(1)}, u32[]{:S(2)}, u32[]{:S(2)}) %collective-permute-start.16) | collective-permute-done | bytes 32800 | tf_op jit(solution)/shard_map/ppermute | solution.py:365
  51.6 0.5 collective-permute-done.15.refs_2_
  52.1 0.3 collective-permute-done.14.refs_1_
  52.4 2.5 %collective-permute-start.19 = (f32[64,128]{1,0:T(8,128)S(1)}, f32[64,128]{1,0:T(8,128)S(1)}, u32[]{:S(2)}, u32[]{:S(2)}) collective-permute-start(f32[64,128]{1,0:T(8,128)S(1)} %shard_map.73.refs_0_), channel_id=1, source_target_pairs={{0,24},{4,28},{8,16},{12,20},{16,8},{20,12},{24,0},{28,4},{1,25},{... | collective-permute-start | bytes 98312 | tf_op jit(solution)/shard_map/ppermute | solution.py:365
  54.9 0.5 collective-permute-start.18
  55.4 0.5 collective-permute-start.17
  56.0 1.3 %collective-permute-done.19.refs_3_ = f32[64,128]{1,0:T(8,128)S(1)} collective-permute-done((f32[64,128]{1,0:T(8,128)S(1)}, f32[64,128]{1,0:T(8,128)S(1)}, u32[]{:S(2)}, u32[]{:S(2)}) %collective-permute-start.19) | collective-permute-done | bytes 32800 | tf_op jit(solution)/shard_map/ppermute | solution.py:365
  57.3 1.6 %collective-permute-done.18.refs_2_ = f32[64,128]{1,0:T(8,128)S(1)} collective-permute-done((f32[64,128]{1,0:T(8,128)S(1)}, f32[64,128]{1,0:T(8,128)S(1)}, u32[]{:S(2)}, u32[]{:S(2)}) %collective-permute-start.18) | collective-permute-done | bytes 32800 | tf_op jit(solution)/shard_map/ppermute | solution.py:365
  58.9 0.5 collective-permute-done.17.refs_1_
  59.5 1.2 collective-permute-done.20.refs_4_
  60.6 12.6 %shard_map.75 = (f32[128,128]{1,0:T(8,128)}, bf16[1024,128]{1,0:T(8,128)(2,1)S(1)}, f32[8,128]{1,0:T(8,128)S(1)}, f32[8,128]{1,0:T(8,128)S(1)}, bf16[1024,4096]{1,0:T(8,128)(2,1)S(1)}) custom-call(bf16[1024,128]{1,0:T(8,128)(2,1)S(1)} %get-tuple-element.37.refs_0_, bf16[4096,256]{1,0:T(8,128)(2,1)S(1)} %get-tuple-element.46.refs_1_.refs_3_, ...), custom_call_target="tpu_custom_call" | custom-call | flops 1073741824 | bytes 11165696 | tf_op jit(solution)/shard_map/pallas_call | solution.py:353
  73.2 2.3 %collective-permute-start.23 = (f32[8,128]{1,0:T(8,128)S(1)}, f32[8,128]{1,0:T(8,128)S(1)}, u32[]{:S(2)}, u32[]{:S(2)}) collective-permute-start(f32[8,128]{1,0:T(8,128)S(1)} %get-tuple-element.56.refs_5_), channel_id=1, source_target_pairs={{0,3},{1,2},{2,1},{3,0},{4,7},{5,6},{6,5},{7,4},{8,11},{9,10},{10,... | collective-permute-start | bytes 12296 | tf_op jit(solution)/shard_map/ppermute | solution.py:365
  75.5 0.6 collective-permute-start.22
  76.2 1.5 %collective-permute-start.21 = (f32[8,128]{1,0:T(8,128)S(1)}, f32[8,128]{1,0:T(8,128)S(1)}, u32[]{:S(2)}, u32[]{:S(2)}) collective-permute-start(f32[8,128]{1,0:T(8,128)S(1)} %get-tuple-element.56.refs_5_), channel_id=1, source_target_pairs={{0,1},{1,0},{2,3},{3,2},{4,5},{5,4},{6,7},{7,6},{8,9},{9,8},{10,11... | collective-permute-start | bytes 12296 | tf_op jit(solution)/shard_map/ppermute | solution.py:365
  77.6 1.0 collective-permute-done.23.refs_8_
  78.6 1.4 %collective-permute-done.22.refs_7_ = f32[8,128]{1,0:T(8,128)S(1)} collective-permute-done((f32[8,128]{1,0:T(8,128)S(1)}, f32[8,128]{1,0:T(8,128)S(1)}, u32[]{:S(2)}, u32[]{:S(2)}) %collective-permute-start.22) | collective-permute-done | bytes 4128 | tf_op jit(solution)/shard_map/ppermute | solution.py:365
  80.1 7.0 %shard_map.76 = (f32[8,512]{1,0:T(8,128)S(1)}, f32[8,128]{1,0:T(8,128)}) custom-call(bf16[1024,128]{1,0:T(8,128)(2,1)S(1)} %get-tuple-element.53.refs_0_, bf16[1024,4096]{1,0:T(8,128)(2,1)S(1)} %get-tuple-element.54.refs_1_, f32[8,128]{1,0:T(8,128)S(1)} %get-tuple-element.55.refs_2_, bf16[4096,256]{1,0:T(8,128)(2,1)S(1)} %get-tuple-element.46.refs_1_.refs_3_, ...), custom_call_target="tpu_custom_call" | custom-call | flops 67108864 | bytes 10805248 | tf_op jit(solution)/shard_map/pallas_call | solution.py:353
  87.1 1.2 collective-permute-done.24.refs_1_
  88.3 1.6 %collective-permute-start.27 = (f32[8,512]{1,0:T(8,128)S(1)}, f32[8,512]{1,0:T(8,128)S(1)}, u32[]{:S(2)}, u32[]{:S(2)}) collective-permute-start(f32[8,512]{1,0:T(8,128)S(1)} %shard_map.77.refs_5_), channel_id=1, source_target_pairs={{0,24},{4,28},{8,16},{12,20},{16,8},{20,12},{24,0},{28,4},{1,25},{... | collective-permute-start | bytes 49160 | tf_op jit(solution)/shard_map/ppermute | solution.py:365
  89.9 0.5 collective-permute-start.26
  90.4 1.5 %collective-permute-start.25 = (f32[8,512]{1,0:T(8,128)S(1)}, f32[8,512]{1,0:T(8,128)S(1)}, u32[]{:S(2)}, u32[]{:S(2)}) collective-permute-start(f32[8,512]{1,0:T(8,128)S(1)} %shard_map.77.refs_5_), channel_id=1, source_target_pairs={{0,8},{4,12},{8,0},{12,4},{16,24},{20,28},{24,16},{28,20},{1,9},{5... | collective-permute-start | bytes 49160 | tf_op jit(solution)/shard_map/ppermute | solution.py:365
  91.9 1.1 collective-permute-done.27.refs_8_
  93.0 0.6 collective-permute-done.26.refs_7_
  93.6 0.5 collective-permute-done.25.refs_6_
  94.1 10.0 %shard_map.78.refs_5_ = f32[8,128]{1,0:T(8,128)S(1)} custom-call(bf16[1024,128]{1,0:T(8,128)(2,1)S(1)} %get-tuple-element.53.refs_0_, bf16[1024,4096]{1,0:T(8,128)(2,1)S(1)} %get-tuple-element.54.refs_1_, f32[8,128]{1,0:T(8,128)S(1)} %get-tuple-element.55.refs_2_, bf16[4096,256]{1,0:T(8,128)(2,1)S(1)} %get-tuple-element.46.refs_1_.refs_3_, ...), custom_call_target="tpu_custom_call" | custom-call | flops 67108864 | bytes 10838016 | tf_op jit(solution)/shard_map/pallas_call | solution.py:353
  104.1 1.6 %collective-permute-start.30 = (f32[8,128]{1,0:T(8,128)S(1)}, f32[8,128]{1,0:T(8,128)S(1)}, u32[]{:S(2)}, u32[]{:S(2)}) collective-permute-start(f32[8,128]{1,0:T(8,128)S(1)} %shard_map.78.refs_5_), channel_id=1, source_target_pairs={{0,3},{1,2},{2,1},{3,0},{4,7},{5,6},{6,5},{7,4},{8,11},{9,10},{10,... | collective-permute-start | bytes 12296 | tf_op jit(solution)/shard_map/ppermute | solution.py:365
  105.6 1.1 collective-permute-start.29
  106.7 1.8 %collective-permute-start.28 = (f32[8,128]{1,0:T(8,128)S(1)}, f32[8,128]{1,0:T(8,128)S(1)}, u32[]{:S(2)}, u32[]{:S(2)}) collective-permute-start(f32[8,128]{1,0:T(8,128)S(1)} %shard_map.78.refs_5_), channel_id=1, source_target_pairs={{0,1},{1,0},{2,3},{3,2},{4,5},{5,4},{6,7},{7,6},{8,9},{9,8},{10,11... | collective-permute-start | bytes 12296 | tf_op jit(solution)/shard_map/ppermute | solution.py:365
  108.5 1.0 collective-permute-done.30.refs_8_
  109.5 0.6 collective-permute-done.29.refs_7_
  110.1 0.2 collective-permute-done.28.refs_6_
  110.3 6.8 %shard_map.79 = (f32[4,1,512]{2,1,0:T(1,128)S(1)}, f32[4,1,512]{2,1,0:T(1,128)S(1)}, f32[8,128]{1,0:T(8,128)}) custom-call(bf16[1024,128]{1,0:T(8,128)(2,1)S(1)} %get-tuple-element.53.refs_0_, bf16[1024,4096]{1,0:T(8,128)(2,1)S(1)} %get-tuple-element.54.refs_1_, f32[8,128]{1,0:T(8,128)S(1)} %get-tuple-element.55.refs_2_, ...), custom_call_target="tpu_custom_call" | custom-call | flops 67108864 | bytes 10805248 | tf_op jit(solution)/shard_map/pallas_call | solution.py:353
  117.2 1.2 collective-permute-done.31.y_ref
  118.4 1.6 %collective-permute-start.32 = (f32[1,512]{1,0:T(1,128)S(1)}, f32[1,512]{1,0:T(1,128)S(1)}, u32[]{:S(2)}, u32[]{:S(2)}) collective-permute-start(f32[1,512]{1,0:T(1,128)S(1)} %get-tuple-element.62), channel_id=1, source_target_pairs={{0,8},{4,12},{8,0},{12,4},{16,24},{20,28},{24,16},{28,20},{1,9},{5... | collective-permute-start | bytes 6152 | tf_op jit(solution)/shard_map/ppermute | solution.py:365
  119.9 1.5 %collective-permute-start.33 = (f32[1,512]{1,0:T(1,128)S(1)}, f32[1,512]{1,0:T(1,128)S(1)}, u32[]{:S(2)}, u32[]{:S(2)}) collective-permute-start(f32[1,512]{1,0:T(1,128)S(1)} %get-tuple-element.63), channel_id=1, source_target_pairs={{0,16},{4,20},{8,24},{12,28},{16,0},{20,4},{24,8},{28,12},{1,17},{... | collective-permute-start | bytes 6152 | tf_op jit(solution)/shard_map/ppermute | solution.py:365
  121.4 0.5 collective-permute-start.34
  122.0 1.5 %collective-permute-done.33.refs_2_ = f32[1,512]{1,0:T(1,128)S(1)} collective-permute-done((f32[1,512]{1,0:T(1,128)S(1)}, f32[1,512]{1,0:T(1,128)S(1)}, u32[]{:S(2)}, u32[]{:S(2)}) %collective-permute-start.33) | collective-permute-done | bytes 2080 | tf_op jit(solution)/shard_map/ppermute | solution.py:365
  123.5 2.4 %collective-permute-done.34.refs_3_ = f32[1,512]{1,0:T(1,128)S(1)} collective-permute-done((f32[1,512]{1,0:T(1,128)S(1)}, f32[1,512]{1,0:T(1,128)S(1)}, u32[]{:S(2)}, u32[]{:S(2)}) %collective-permute-start.34) | collective-permute-done | bytes 2080 | tf_op jit(solution)/shard_map/ppermute | solution.py:365
  125.9 0.6 shard_map.81
  (26 shorter events, 1.0 us)
Async XLA Ops:
  0.6 10.1 %collective-permute-start = (bf16[256,128]{1,0:T(8,128)(2,1)}, bf16[256,128]{1,0:T(8,128)(2,1)S(1)}, u32[]{:S(2)}, u32[]{:S(2)}) collective-permute-start(bf16[256,128]{1,0:T(8,128)(2,1)} %own_ref.1), channel_id=1, source_target_pairs={{0,1},{1,0},{2,3},{3,2},{4,5},{5,4},{6,7},{7,6},{8,9},{9,8},{10,11... | collective-permute-start | bytes 196616 | tf_op jit(solution)/shard_map/ppermute | solution.py:365
  4.7 12.4 %collective-permute-start.5 = (bf16[528,128]{1,0:T(8,128)(2,1)S(1)}, bf16[528,128]{1,0:T(8,128)(2,1)S(1)}, u32[]{:S(2)}, u32[]{:S(2)}) collective-permute-start(bf16[528,128]{1,0:T(8,128)(2,1)S(1)} %fusion.1.block_ref.refs_3_), channel_id=1, source_target_pairs={{0,24},{4,28},{8,16},{12,20},{16,8},{20,12},{24,0},{28,4},{1,25},{... | collective-permute-start | bytes 405512 | tf_op jit(solution)/shard_map/ppermute | solution.py:365
  7.2 9.9 %collective-permute-start.4 = (bf16[528,128]{1,0:T(8,128)(2,1)S(1)}, bf16[528,128]{1,0:T(8,128)(2,1)S(1)}, u32[]{:S(2)}, u32[]{:S(2)}) collective-permute-start(bf16[528,128]{1,0:T(8,128)(2,1)S(1)} %fusion.1.block_ref.refs_3_), channel_id=1, source_target_pairs={{0,16},{4,20},{8,24},{12,28},{16,0},{20,4},{24,8},{28,12},{1,17},{... | collective-permute-start | bytes 405512 | tf_op jit(solution)/shard_map/ppermute | solution.py:365
  7.7 9.4 %collective-permute-start.3 = (bf16[528,128]{1,0:T(8,128)(2,1)S(1)}, bf16[528,128]{1,0:T(8,128)(2,1)S(1)}, u32[]{:S(2)}, u32[]{:S(2)}) collective-permute-start(bf16[528,128]{1,0:T(8,128)(2,1)S(1)} %fusion.1.block_ref.refs_3_), channel_id=1, source_target_pairs={{0,8},{4,12},{8,0},{12,4},{16,24},{20,28},{24,16},{28,20},{1,9},{5... | collective-permute-start | bytes 405512 | tf_op jit(solution)/shard_map/ppermute | solution.py:365
  8.2 6.3 %collective-permute-start.2 = (bf16[256,128]{1,0:T(8,128)(2,1)}, bf16[256,128]{1,0:T(8,128)(2,1)S(1)}, u32[]{:S(2)}, u32[]{:S(2)}) collective-permute-start(bf16[256,128]{1,0:T(8,128)(2,1)} %own_ref.1), channel_id=1, source_target_pairs={{0,3},{1,2},{2,1},{3,0},{4,7},{5,6},{6,5},{7,4},{8,11},{9,10},{10,... | collective-permute-start | bytes 196616 | tf_op jit(solution)/shard_map/ppermute | solution.py:365
  10.7 6.1 %collective-permute-start.1 = (bf16[256,128]{1,0:T(8,128)(2,1)}, bf16[256,128]{1,0:T(8,128)(2,1)S(1)}, u32[]{:S(2)}, u32[]{:S(2)}) collective-permute-start(bf16[256,128]{1,0:T(8,128)(2,1)} %own_ref.1), channel_id=1, source_target_pairs={{0,2},{1,3},{2,0},{3,1},{4,6},{5,7},{6,4},{7,5},{8,10},{9,11},{10,... | collective-permute-start | bytes 196616 | tf_op jit(solution)/shard_map/ppermute | solution.py:365
  10.8 0.8 copy-start
  11.6 0.8 copy-start.1
  17.1 1.8 %collective-permute-start.7 = (bf16[528,128]{1,0:T(8,128)(2,1)S(1)}, bf16[528,128]{1,0:T(8,128)(2,1)S(1)}, u32[]{:S(2)}, u32[]{:S(2)}) collective-permute-start(bf16[528,128]{1,0:T(8,128)(2,1)S(1)} %collective-permute-done.3.refs_5_), channel_id=1, source_target_pairs={{0,4},{4,0},{8,12},{12,8},{16,20},{20,16},{24,28},{28,24},{1,5},{5... | collective-permute-start | bytes 405512 | tf_op jit(solution)/shard_map/ppermute | solution.py:365
  17.2 1.7 %collective-permute-start.8 = (bf16[528,128]{1,0:T(8,128)(2,1)S(1)}, bf16[528,128]{1,0:T(8,128)(2,1)S(1)}, u32[]{:S(2)}, u32[]{:S(2)}) collective-permute-start(bf16[528,128]{1,0:T(8,128)(2,1)S(1)} %collective-permute-done.4.refs_7_), channel_id=1, source_target_pairs={{0,4},{4,0},{8,12},{12,8},{16,20},{20,16},{24,28},{28,24},{1,5},{5... | collective-permute-start | bytes 405512 | tf_op jit(solution)/shard_map/ppermute | solution.py:365
  17.7 1.4 %collective-permute-start.9 = (bf16[528,128]{1,0:T(8,128)(2,1)S(1)}, bf16[528,128]{1,0:T(8,128)(2,1)S(1)}, u32[]{:S(2)}, u32[]{:S(2)}) collective-permute-start(bf16[528,128]{1,0:T(8,128)(2,1)S(1)} %collective-permute-done.5.refs_9_), channel_id=1, source_target_pairs={{0,4},{4,0},{8,12},{12,8},{16,20},{20,16},{24,28},{28,24},{1,5},{5... | collective-permute-start | bytes 405512 | tf_op jit(solution)/shard_map/ppermute | solution.py:365
  17.8 1.5 %collective-permute-start.6 = (bf16[528,128]{1,0:T(8,128)(2,1)S(1)}, bf16[528,128]{1,0:T(8,128)(2,1)S(1)}, u32[]{:S(2)}, u32[]{:S(2)}) collective-permute-start(bf16[528,128]{1,0:T(8,128)(2,1)S(1)} %fusion.1.block_ref.refs_3_), channel_id=1, source_target_pairs={{0,4},{4,0},{8,12},{12,8},{16,20},{20,16},{24,28},{28,24},{1,5},{5... | collective-permute-start | bytes 405512 | tf_op jit(solution)/shard_map/ppermute | solution.py:365
  37.0 5.5 %collective-permute-start.12 = (f32[8,128]{1,0:T(8,128)S(1)}, f32[8,128]{1,0:T(8,128)S(1)}, u32[]{:S(2)}, u32[]{:S(2)}) collective-permute-start(f32[8,128]{1,0:T(8,128)S(1)} %get-tuple-element.48.refs_1_), channel_id=1, source_target_pairs={{0,3},{1,2},{2,1},{3,0},{4,7},{5,6},{6,5},{7,4},{8,11},{9,10},{10,... | collective-permute-start | bytes 12296 | tf_op jit(solution)/shard_map/ppermute | solution.py:365
  39.2 4.5 %collective-permute-start.11 = (f32[8,128]{1,0:T(8,128)S(1)}, f32[8,128]{1,0:T(8,128)S(1)}, u32[]{:S(2)}, u32[]{:S(2)}) collective-permute-start(f32[8,128]{1,0:T(8,128)S(1)} %get-tuple-element.48.refs_1_), channel_id=1, source_target_pairs={{0,2},{1,3},{2,0},{3,1},{4,6},{5,7},{6,4},{7,5},{8,10},{9,11},{10,... | collective-permute-start | bytes 12296 | tf_op jit(solution)/shard_map/ppermute | solution.py:365
  39.3 4.5 %collective-permute-start.10 = (f32[8,128]{1,0:T(8,128)S(1)}, f32[8,128]{1,0:T(8,128)S(1)}, u32[]{:S(2)}, u32[]{:S(2)}) collective-permute-start(f32[8,128]{1,0:T(8,128)S(1)} %get-tuple-element.48.refs_1_), channel_id=1, source_target_pairs={{0,1},{1,0},{2,3},{3,2},{4,5},{5,4},{6,7},{7,6},{8,9},{9,8},{10,11... | collective-permute-start | bytes 12296 | tf_op jit(solution)/shard_map/ppermute | solution.py:365
  44.3 1.3 %collective-permute-start.13 = (f32[64,128]{1,0:T(8,128)S(1)}, f32[64,128]{1,0:T(8,128)S(1)}, u32[]{:S(2)}, u32[]{:S(2)}) collective-permute-start(f32[64,128]{1,0:T(8,128)S(1)} %get-tuple-element.51), channel_id=1, source_target_pairs={{0,4},{4,0},{8,12},{12,8},{16,20},{20,16},{24,28},{28,24},{1,5},{5... | collective-permute-start | bytes 98312 | tf_op jit(solution)/shard_map/ppermute | solution.py:365
  45.6 6.0 %collective-permute-start.16 = (f32[64,128]{1,0:T(8,128)S(1)}, f32[64,128]{1,0:T(8,128)S(1)}, u32[]{:S(2)}, u32[]{:S(2)}) collective-permute-start(f32[64,128]{1,0:T(8,128)S(1)} %shard_map.72.refs_0_), channel_id=1, source_target_pairs={{0,3},{1,2},{2,1},{3,0},{4,7},{5,6},{6,5},{7,4},{8,11},{9,10},{10,... | collective-permute-start | bytes 98312 | tf_op jit(solution)/shard_map/ppermute | solution.py:365
  47.3 4.8 %collective-permute-start.15 = (f32[64,128]{1,0:T(8,128)S(1)}, f32[64,128]{1,0:T(8,128)S(1)}, u32[]{:S(2)}, u32[]{:S(2)}) collective-permute-start(f32[64,128]{1,0:T(8,128)S(1)} %shard_map.72.refs_0_), channel_id=1, source_target_pairs={{0,2},{1,3},{2,0},{3,1},{4,6},{5,7},{6,4},{7,5},{8,10},{9,11},{10,... | collective-permute-start | bytes 98312 | tf_op jit(solution)/shard_map/ppermute | solution.py:365
  48.4 4.0 %collective-permute-start.14 = (f32[64,128]{1,0:T(8,128)S(1)}, f32[64,128]{1,0:T(8,128)S(1)}, u32[]{:S(2)}, u32[]{:S(2)}) collective-permute-start(f32[64,128]{1,0:T(8,128)S(1)} %shard_map.72.refs_0_), channel_id=1, source_target_pairs={{0,1},{1,0},{2,3},{3,2},{4,5},{5,4},{6,7},{7,6},{8,9},{9,8},{10,11... | collective-permute-start | bytes 98312 | tf_op jit(solution)/shard_map/ppermute | solution.py:365
  52.4 4.9 %collective-permute-start.19 = (f32[64,128]{1,0:T(8,128)S(1)}, f32[64,128]{1,0:T(8,128)S(1)}, u32[]{:S(2)}, u32[]{:S(2)}) collective-permute-start(f32[64,128]{1,0:T(8,128)S(1)} %shard_map.73.refs_0_), channel_id=1, source_target_pairs={{0,24},{4,28},{8,16},{12,20},{16,8},{20,12},{24,0},{28,4},{1,25},{... | collective-permute-start | bytes 98312 | tf_op jit(solution)/shard_map/ppermute | solution.py:365
  54.9 3.9 %collective-permute-start.18 = (f32[64,128]{1,0:T(8,128)S(1)}, f32[64,128]{1,0:T(8,128)S(1)}, u32[]{:S(2)}, u32[]{:S(2)}) collective-permute-start(f32[64,128]{1,0:T(8,128)S(1)} %shard_map.73.refs_0_), channel_id=1, source_target_pairs={{0,16},{4,20},{8,24},{12,28},{16,0},{20,4},{24,8},{28,12},{1,17},{... | collective-permute-start | bytes 98312 | tf_op jit(solution)/shard_map/ppermute | solution.py:365
  55.4 3.9 %collective-permute-start.17 = (f32[64,128]{1,0:T(8,128)S(1)}, f32[64,128]{1,0:T(8,128)S(1)}, u32[]{:S(2)}, u32[]{:S(2)}) collective-permute-start(f32[64,128]{1,0:T(8,128)S(1)} %shard_map.73.refs_0_), channel_id=1, source_target_pairs={{0,8},{4,12},{8,0},{12,4},{16,24},{20,28},{24,16},{28,20},{1,9},{5... | collective-permute-start | bytes 98312 | tf_op jit(solution)/shard_map/ppermute | solution.py:365
  59.4 1.3 %collective-permute-start.20 = (f32[64,128]{1,0:T(8,128)S(1)}, f32[64,128]{1,0:T(8,128)S(1)}, u32[]{:S(2)}, u32[]{:S(2)}) collective-permute-start(f32[64,128]{1,0:T(8,128)S(1)} %shard_map.74.refs_3_), channel_id=1, source_target_pairs={{0,4},{4,0},{8,12},{12,8},{16,20},{20,16},{24,28},{28,24},{1,5},{5... | collective-permute-start | bytes 98312 | tf_op jit(solution)/shard_map/ppermute | solution.py:365
  73.2 5.4 %collective-permute-start.23 = (f32[8,128]{1,0:T(8,128)S(1)}, f32[8,128]{1,0:T(8,128)S(1)}, u32[]{:S(2)}, u32[]{:S(2)}) collective-permute-start(f32[8,128]{1,0:T(8,128)S(1)} %get-tuple-element.56.refs_5_), channel_id=1, source_target_pairs={{0,3},{1,2},{2,1},{3,0},{4,7},{5,6},{6,5},{7,4},{8,11},{9,10},{10,... | collective-permute-start | bytes 12296 | tf_op jit(solution)/shard_map/ppermute | solution.py:365
  75.5 4.5 %collective-permute-start.22 = (f32[8,128]{1,0:T(8,128)S(1)}, f32[8,128]{1,0:T(8,128)S(1)}, u32[]{:S(2)}, u32[]{:S(2)}) collective-permute-start(f32[8,128]{1,0:T(8,128)S(1)} %get-tuple-element.56.refs_5_), channel_id=1, source_target_pairs={{0,2},{1,3},{2,0},{3,1},{4,6},{5,7},{6,4},{7,5},{8,10},{9,11},{10,... | collective-permute-start | bytes 12296 | tf_op jit(solution)/shard_map/ppermute | solution.py:365
  76.2 3.9 %collective-permute-start.21 = (f32[8,128]{1,0:T(8,128)S(1)}, f32[8,128]{1,0:T(8,128)S(1)}, u32[]{:S(2)}, u32[]{:S(2)}) collective-permute-start(f32[8,128]{1,0:T(8,128)S(1)} %get-tuple-element.56.refs_5_), channel_id=1, source_target_pairs={{0,1},{1,0},{2,3},{3,2},{4,5},{5,4},{6,7},{7,6},{8,9},{9,8},{10,11... | collective-permute-start | bytes 12296 | tf_op jit(solution)/shard_map/ppermute | solution.py:365
  87.1 1.2 collective-permute-start.24
  88.3 4.7 %collective-permute-start.27 = (f32[8,512]{1,0:T(8,128)S(1)}, f32[8,512]{1,0:T(8,128)S(1)}, u32[]{:S(2)}, u32[]{:S(2)}) collective-permute-start(f32[8,512]{1,0:T(8,128)S(1)} %shard_map.77.refs_5_), channel_id=1, source_target_pairs={{0,24},{4,28},{8,16},{12,20},{16,8},{20,12},{24,0},{28,4},{1,25},{... | collective-permute-start | bytes 49160 | tf_op jit(solution)/shard_map/ppermute | solution.py:365
  89.9 3.7 %collective-permute-start.26 = (f32[8,512]{1,0:T(8,128)S(1)}, f32[8,512]{1,0:T(8,128)S(1)}, u32[]{:S(2)}, u32[]{:S(2)}) collective-permute-start(f32[8,512]{1,0:T(8,128)S(1)} %shard_map.77.refs_5_), channel_id=1, source_target_pairs={{0,16},{4,20},{8,24},{12,28},{16,0},{20,4},{24,8},{28,12},{1,17},{... | collective-permute-start | bytes 49160 | tf_op jit(solution)/shard_map/ppermute | solution.py:365
  90.4 3.7 %collective-permute-start.25 = (f32[8,512]{1,0:T(8,128)S(1)}, f32[8,512]{1,0:T(8,128)S(1)}, u32[]{:S(2)}, u32[]{:S(2)}) collective-permute-start(f32[8,512]{1,0:T(8,128)S(1)} %shard_map.77.refs_5_), channel_id=1, source_target_pairs={{0,8},{4,12},{8,0},{12,4},{16,24},{20,28},{24,16},{28,20},{1,9},{5... | collective-permute-start | bytes 49160 | tf_op jit(solution)/shard_map/ppermute | solution.py:365
  104.1 5.4 %collective-permute-start.30 = (f32[8,128]{1,0:T(8,128)S(1)}, f32[8,128]{1,0:T(8,128)S(1)}, u32[]{:S(2)}, u32[]{:S(2)}) collective-permute-start(f32[8,128]{1,0:T(8,128)S(1)} %shard_map.78.refs_5_), channel_id=1, source_target_pairs={{0,3},{1,2},{2,1},{3,0},{4,7},{5,6},{6,5},{7,4},{8,11},{9,10},{10,... | collective-permute-start | bytes 12296 | tf_op jit(solution)/shard_map/ppermute | solution.py:365
  105.6 4.5 %collective-permute-start.29 = (f32[8,128]{1,0:T(8,128)S(1)}, f32[8,128]{1,0:T(8,128)S(1)}, u32[]{:S(2)}, u32[]{:S(2)}) collective-permute-start(f32[8,128]{1,0:T(8,128)S(1)} %shard_map.78.refs_5_), channel_id=1, source_target_pairs={{0,2},{1,3},{2,0},{3,1},{4,6},{5,7},{6,4},{7,5},{8,10},{9,11},{10,... | collective-permute-start | bytes 12296 | tf_op jit(solution)/shard_map/ppermute | solution.py:365
  106.7 3.6 %collective-permute-start.28 = (f32[8,128]{1,0:T(8,128)S(1)}, f32[8,128]{1,0:T(8,128)S(1)}, u32[]{:S(2)}, u32[]{:S(2)}) collective-permute-start(f32[8,128]{1,0:T(8,128)S(1)} %shard_map.78.refs_5_), channel_id=1, source_target_pairs={{0,1},{1,0},{2,3},{3,2},{4,5},{5,4},{6,7},{7,6},{8,9},{9,8},{10,11... | collective-permute-start | bytes 12296 | tf_op jit(solution)/shard_map/ppermute | solution.py:365
  117.2 1.2 collective-permute-start.31
  118.4 3.7 %collective-permute-start.32 = (f32[1,512]{1,0:T(1,128)S(1)}, f32[1,512]{1,0:T(1,128)S(1)}, u32[]{:S(2)}, u32[]{:S(2)}) collective-permute-start(f32[1,512]{1,0:T(1,128)S(1)} %get-tuple-element.62), channel_id=1, source_target_pairs={{0,8},{4,12},{8,0},{12,4},{16,24},{20,28},{24,16},{28,20},{1,9},{5... | collective-permute-start | bytes 6152 | tf_op jit(solution)/shard_map/ppermute | solution.py:365
  119.9 3.6 %collective-permute-start.33 = (f32[1,512]{1,0:T(1,128)S(1)}, f32[1,512]{1,0:T(1,128)S(1)}, u32[]{:S(2)}, u32[]{:S(2)}) collective-permute-start(f32[1,512]{1,0:T(1,128)S(1)} %get-tuple-element.63), channel_id=1, source_target_pairs={{0,16},{4,20},{8,24},{12,28},{16,0},{20,4},{24,8},{28,12},{1,17},{... | collective-permute-start | bytes 6152 | tf_op jit(solution)/shard_map/ppermute | solution.py:365
  121.4 4.5 %collective-permute-start.34 = (f32[1,512]{1,0:T(1,128)S(1)}, f32[1,512]{1,0:T(1,128)S(1)}, u32[]{:S(2)}, u32[]{:S(2)}) collective-permute-start(f32[1,512]{1,0:T(1,128)S(1)} %get-tuple-element.64), channel_id=1, source_target_pairs={{0,24},{4,28},{8,16},{12,20},{16,8},{20,12},{24,0},{28,4},{1,25},{... | collective-permute-start | bytes 6152 | tf_op jit(solution)/shard_map/ppermute | solution.py:365

commit v9 on v8

--- a/solution.py
+++ b/solution.py
@@ -86,23 +86,27 @@
         top_ref[row_of(i, steps), :] = as_lanes(top)
 
 
-def shifted_rows(aug_ref, t_ref, width, lse_ref, top_ref, mass_ref, e_ref=None, carried_ref=None):
+def shifted_rows(aug_ref, t_ref, width, lse_ref, top_ref, mass_ref, scores, e_ref, carried_ref=None):
     rows = aug_ref.shape[0]
     steps = rows // LANES
-    for g in range(t_ref.shape[0] // width):
-        cols = slice(g * width, (g + 1) * width)
-        for h in range(0, rows, 2 * LANES):
-            at = slice(h, h + 2 * LANES)
-            s = lax.dot_general(aug_ref[at, :], t_ref[cols, :], NT_DIMS, preferred_element_type=jnp.float32)
-            e = jnp.exp(s)
-            m = lane_fold(jnp.add, e)
-            mass_ref[at, :] = m if g == 0 else mass_ref[at, :] + m
-            e = e.astype(jnp.bfloat16)
-            if e_ref is not None:
-                e_ref[at, cols] = e
-            if carried_ref is not None:
-                d = jnp.dot(e, block_of(t_ref, g, width), preferred_element_type=jnp.float32)
-                carried_ref[at, :] = d if g == 0 else carried_ref[at, :] + d
+    blocks = t_ref.shape[0] // width
+    keep = e_ref.shape[1] // width
+    for g in range(blocks + 2):
+        if g < blocks:
+            t = t_ref[g * width : (g + 1) * width, :]
+            scores[g % 2] = lax.dot_general(aug_ref[...], t, NT_DIMS, preferred_element_type=jnp.float32)
+        if g > 1 and carried_ref is not None:
+            e = e_ref[:, (g - 2) % keep * width : ((g - 2) % keep + 1) * width]
+            d = jnp.dot(e, block_of(t_ref, g - 2, width), preferred_element_type=jnp.float32)
+            carried_ref[...] = d if g == 2 else carried_ref[...] + d
+        if 0 < g <= blocks:
+            cols = slice((g - 1) % keep * width, ((g - 1) % keep + 1) * width)
+            for h in range(0, rows, LANES):
+                at = slice(h, h + LANES)
+                e = jnp.exp(scores[(g - 1) % 2, at, :])
+                m = lane_fold(jnp.add, e)
+                mass_ref[at, :] = m if g == 1 else mass_ref[at, :] + m
+                e_ref[at, cols] = e.astype(jnp.bfloat16)
     masses = []
     for i in range(steps):
         at = slice(i * LANES, (i + 1) * LANES)
@@ -180,7 +184,7 @@
 
 def couple_kernel(nt, width, *refs):
     a_ref, aug_ref, top_ref, t_refs = refs[0], refs[1], refs[2], refs[3 : 3 + nt]
-    lse_ref, carried_ref, t_ref, pot_ref, mass_ref, scores = refs[3 + nt :]
+    lse_ref, carried_ref, t_ref, pot_ref, mass_ref, ahead, e_ref, scores = refs[3 + nt :]
     lane = lax.broadcasted_iota(jnp.int32, (LANES, LANES), 1)
     for g in range(nt):
         t_ref[g * width : (g + 1) * width, :LANES] = t_refs[g][:width, :]
@@ -190,7 +194,7 @@
             added = jnp.where(lane == 0, potential, jnp.where(lane == 1, 1.0, 0.0))
             at = g * width + j
             t_ref[at : at + LANES, LANES:] = added.astype(jnp.bfloat16)
-    fine = shifted_rows(aug_ref, t_ref, width, lse_ref, top_ref, mass_ref, None, carried_ref)
+    fine = shifted_rows(aug_ref, t_ref, width, lse_ref, top_ref, mass_ref, ahead, e_ref, carried_ref)
 
     @pl.when(jnp.logical_not(fine))
     def _():
@@ -231,14 +235,14 @@
 
 def first_rows_kernel(*refs):
     s_ref, t_ref, pot_ref, m_refs = refs[0], refs[1], refs[2], refs[3:5]
-    moment_ref, a_ref, lse_ref, top_ref, e_ref, mass_ref, aug_ref, scores = refs[5:]
+    moment_ref, a_ref, lse_ref, top_ref, e_ref, mass_ref, aug_ref, ahead, scores = refs[5:]
     r = lax.axis_index("row")
     half = m_refs[0].shape[0]
     for k in range(2):
         moment_ref[pl.ds(pl.multiple_of((k ^ (r % 2)) * half, half), half), :] = m_refs[k][...]
     a_ref[...] = project4(s_ref[...], split3(moment_ref[...]))
     add_shifts(a_ref, t_ref, pot_ref[0:1, :], aug_ref, top_ref)
-    fine = shifted_rows(aug_ref, t_ref, pot_ref.shape[1], lse_ref, top_ref, mass_ref, e_ref)
+    fine = shifted_rows(aug_ref, t_ref, pot_ref.shape[1], lse_ref, top_ref, mass_ref, ahead, e_ref)
 
     @pl.when(jnp.logical_not(fine))
     def _():
@@ -250,6 +254,10 @@
     high = x.astype(jnp.bfloat16).astype(jnp.float32)
     at = lax.broadcasted_iota(jnp.int32, (SUB, x.shape[1]), 0)
     return jnp.where(at == 0, high, jnp.where(at == 1, x - high, 0.0)).astype(jnp.bfloat16)
+
+
+def on_vector_unit(part):
+    return part % 8 in (2, 4, 6)
 
 
 def rows_kernel(rows_total, *refs):
@@ -266,9 +274,17 @@
     steps = a_ref.shape[0] // LANES
     masses = []
     for i in range(steps):
-        e = e_ref[i * LANES : (i + 1) * LANES, :]
-        sums = lax.dot_general(weights[...], e, NT_DIMS, preferred_element_type=jnp.float32)
-        masses.append(sums[0:1, :] + sums[1:2, :])
+        at = slice(i * LANES, (i + 1) * LANES)
+        if on_vector_unit(i):
+            total = None
+            for k in range(nt):
+                e = e_ref[at, k * width : (k + 1) * width].astype(jnp.float32)
+                m = lane_fold(jnp.add, e * jnp.exp(change[k] - top))
+                total = m if total is None else total + m
+            masses.append(as_lanes(jnp.sum(total, axis=1, keepdims=True)))
+        else:
+            sums = lax.dot_general(weights[...], e_ref[at, :], NT_DIMS, preferred_element_type=jnp.float32)
+            masses.append(sums[0:1, :] + sums[1:2, :])
         row = row_of(i, steps)
         lse_ref[row, :] = top + top_ref[row, :] + jnp.log(masses[i])
 
@@ -292,7 +308,9 @@
     for k in range(ns):
         for j in range(per):
             at = (k * per + j) * LANES
-            weights[:, at : at + LANES] = high_low(weight_rows[pl.ds((c ^ k) * per + j, 1), :])
+            row = weight_rows[pl.ds((c ^ k) * per + j, 1), :]
+            weights[:, at : at + LANES] = high_low(row)
+            spread_rows[at : at + LANES, :] = as_rows(row)
 
     def store(g, lse):
         if last:
@@ -302,9 +320,18 @@
 
     masses = []
     for g in range(nt):
-        e = e_ref[:, g * width : (g + 1) * width]
-        sums = jnp.dot(weights[...], e, preferred_element_type=jnp.float32)
-        masses.append(sums[0:1, :] + sums[1:2, :])
+        cols = slice(g * width, (g + 1) * width)
+        if on_vector_unit(g):
+            total = None
+            for at in range(0, rows, LANES):
+                e = e_ref[at : at + LANES, cols].astype(jnp.float32)
+                e = e * jnp.concatenate([spread_rows[at : at + LANES, :]] * (width // LANES), axis=1)
+                m = jnp.sum(e.reshape(LANES // 8, 8, width), axis=0)
+                total = m if total is None else total + m
+            masses.append(jnp.sum(total, axis=0, keepdims=True))
+        else:
+            sums = jnp.dot(weights[...], e_ref[:, cols], preferred_element_type=jnp.float32)
+            masses.append(sums[0:1, :] + sums[1:2, :])
         store(g, top - pot_ref[g : g + 1, :] + jnp.log(masses[g]))
 
     @pl.when(jnp.logical_not(within(masses)))
@@ -390,6 +417,7 @@
     row_scores = pltpu.VMEM((LANES, cols), f32)
     small = pltpu.VMEM(tile.shape, f32)
     sums = pltpu.VMEM((rows, LANES), f32)
+    ahead = pltpu.VMEM((2, rows, width), f32)
 
     groups = width // LANES
     tail = jnp.pad(target_potential.reshape(groups, LANES), ((0, SUB - groups), (0, 0)))
@@ -416,7 +444,7 @@
         functools.partial(couple_kernel, nt, width),
         [tile, shape((rows, depth), f32), shape((cols, 2 * depth), bf16), shape((nt, width), f32)],
         [a, aug, top] + blocks,
-        [sums, row_scores],
+        [sums, ahead, pltpu.VMEM((rows, 3 * width), bf16), row_scores],
         2 * flops,
         exps,
     )
@@ -435,7 +463,7 @@
         first_rows_kernel,
         [shape((depth, depth), f32), projected, tile, tile, shape((rows, cols), bf16)],
         [s, t, pot, part, swap(part, "row", 1)],
-        [sums, pltpu.VMEM(augmented.shape, bf16), row_scores],
+        [sums, pltpu.VMEM(augmented.shape, bf16), ahead, row_scores],
         flops,
         exps,
     )

time: 127 us -> 124 us (0.976)
  Pallas kernels: 56.6 us -> 53.7 us
    pallas_call x15, Pallas kernels: 56.6 us -> 53.7 us  [call(): pl.pallas_call(kernel, out_shape=list(out), in_specs=[vmem] * len(args),...]
where the time goes in v9:
time: 124 us
  Pallas kernels  53.7 us (43%)
  starting transfers between devices  38.8 us (31%)
  waiting for transfers between devices  27.8 us (22%)
  local copies, waits for them, and re-layouts  1.68 us (1%)
    pallas_call x15, Pallas kernels, call(): pl.pallas_call(kernel, out_shape=list(out), in_specs=[vmem] * len(args),...  53.7 us
    ppermute x35, starting transfers between devices, swap(): lax.ppermute(x, axis, [(i, i ^ k) for i in range(lax.axis_size(axis))])  38.8 us
    ppermute x35, waiting for transfers between devices, swap(): lax.ppermute(x, axis, [(i, i ^ k) for i in range(lax.axis_size(axis))])  27.8 us
  transfers between devices with their start and end apart: 35, of which 27 were waited for; matrix products, arithmetic and copies ran while one was open for 1% of the time, Pallas kernels for 1%

profile of v9, /device:TPU:0, one launch (start us, length us, event | category | flops | bytes accessed | tf_op | source)
XLA Modules:
  0.0 123.7 jit_solution(8447171851780721702)
XLA Ops:
  0.6 3.1 %collective-permute-start = (bf16[256,128]{1,0:T(8,128)(2,1)}, bf16[256,128]{1,0:T(8,128)(2,1)S(1)}, u32[]{:S(2)}, u32[]{:S(2)}) collective-permute-start(bf16[256,128]{1,0:T(8,128)(2,1)} %own_ref.1), channel_id=1, source_target_pairs={{0,1},{1,0},{2,3},{3,2},{4,5},{5,4},{6,7},{7,6},{8,9},{9,8},{10,11... | collective-permute-start | bytes 196616 | tf_op jit(solution)/shard_map/ppermute | solution.py:392
  3.7 0.9 fusion.1.block_ref.refs_3_
  4.7 2.5 %collective-permute-start.5 = (bf16[528,128]{1,0:T(8,128)(2,1)S(1)}, bf16[528,128]{1,0:T(8,128)(2,1)S(1)}, u32[]{:S(2)}, u32[]{:S(2)}) collective-permute-start(bf16[528,128]{1,0:T(8,128)(2,1)S(1)} %fusion.1.block_ref.refs_3_), channel_id=1, source_target_pairs={{0,24},{4,28},{8,16},{12,20},{16,8},{20,12},{24,0},{28,4},{1,25},{... | collective-permute-start | bytes 405512 | tf_op jit(solution)/shard_map/ppermute | solution.py:392
  7.2 0.5 collective-permute-start.4
  7.7 0.5 collective-permute-start.3
  8.2 2.5 %collective-permute-start.2 = (bf16[256,128]{1,0:T(8,128)(2,1)}, bf16[256,128]{1,0:T(8,128)(2,1)S(1)}, u32[]{:S(2)}, u32[]{:S(2)}) collective-permute-start(bf16[256,128]{1,0:T(8,128)(2,1)} %own_ref.1), channel_id=1, source_target_pairs={{0,3},{1,2},{2,1},{3,0},{4,7},{5,6},{6,5},{7,4},{8,11},{9,10},{10,... | collective-permute-start | bytes 196616 | tf_op jit(solution)/shard_map/ppermute | solution.py:392
  10.8 0.8 copy-done
  11.6 0.8 copy-done.1
  12.5 0.2 shard_map.67
  12.7 1.8 %collective-permute-done.2.refs_3_ = bf16[256,128]{1,0:T(8,128)(2,1)S(1)} collective-permute-done((bf16[256,128]{1,0:T(8,128)(2,1)}, bf16[256,128]{1,0:T(8,128)(2,1)S(1)}, u32[]{:S(2)}, u32[]{:S(2)}) %collective-permute-start.2) | collective-permute-done | bytes 65568 | tf_op jit(solution)/shard_map/ppermute | solution.py:392
  14.5 2.3 %collective-permute-done.1.refs_2_ = bf16[256,128]{1,0:T(8,128)(2,1)S(1)} collective-permute-done((bf16[256,128]{1,0:T(8,128)(2,1)}, bf16[256,128]{1,0:T(8,128)(2,1)S(1)}, u32[]{:S(2)}, u32[]{:S(2)}) %collective-permute-start.1) | collective-permute-done | bytes 65568 | tf_op jit(solution)/shard_map/ppermute | solution.py:392
  16.8 0.3 shard_map.68
  17.2 0.5 collective-permute-start.8
  17.8 0.4 collective-permute-start.6
  18.2 0.7 shard_map.69
  19.2 15.4 %shard_map.70 = (f32[8,128]{1,0:T(8,128)S(1)}, f32[1024,128]{1,0:T(8,128)S(1)}, bf16[4096,256]{1,0:T(8,128)(2,1)S(1)}, f32[8,512]{1,0:T(8,128)S(1)}) custom-call(bf16[1024,128]{1,0:T(8,128)(2,1)S(1)} %get-tuple-element.39.a_ref.refs_0_, bf16[1024,256]{1,0:T(8,128)(2,1)S(1)} %get-tuple-element.41.refs_1_, f32[8,128]{1,0:T(8,128)S(1)} %get-tuple-element.42.refs_2_, ...), custom_call_target="tpu_custom_call" | custom-call | flops 2147483648 | bytes 4513792 | tf_op jit(solution)/shard_map/pallas_call | solution.py:380
  34.6 2.2 %collective-permute-start.12 = (f32[8,128]{1,0:T(8,128)S(1)}, f32[8,128]{1,0:T(8,128)S(1)}, u32[]{:S(2)}, u32[]{:S(2)}) collective-permute-start(f32[8,128]{1,0:T(8,128)S(1)} %get-tuple-element.48.refs_1_), channel_id=1, source_target_pairs={{0,3},{1,2},{2,1},{3,0},{4,7},{5,6},{6,5},{7,4},{8,11},{9,10},{10,... | collective-permute-start | bytes 12296 | tf_op jit(solution)/shard_map/ppermute | solution.py:392
  36.9 2.2 %collective-permute-start.10 = (f32[8,128]{1,0:T(8,128)S(1)}, f32[8,128]{1,0:T(8,128)S(1)}, u32[]{:S(2)}, u32[]{:S(2)}) collective-permute-start(f32[8,128]{1,0:T(8,128)S(1)} %get-tuple-element.48.refs_1_), channel_id=1, source_target_pairs={{0,1},{1,0},{2,3},{3,2},{4,5},{5,4},{6,7},{7,6},{8,9},{9,8},{10,11... | collective-permute-start | bytes 12296 | tf_op jit(solution)/shard_map/ppermute | solution.py:392
  39.1 1.0 collective-permute-done.12.refs_4_
  40.1 1.2 %collective-permute-done.11.refs_3_ = f32[8,128]{1,0:T(8,128)S(1)} collective-permute-done((f32[8,128]{1,0:T(8,128)S(1)}, f32[8,128]{1,0:T(8,128)S(1)}, u32[]{:S(2)}, u32[]{:S(2)}) %collective-permute-start.11) | collective-permute-done | bytes 4128 | tf_op jit(solution)/shard_map/ppermute | solution.py:392
  41.4 0.5 shard_map.71
  42.0 1.2 collective-permute-done.13.refs_1_
  43.2 1.7 %collective-permute-start.16 = (f32[64,128]{1,0:T(8,128)S(1)}, f32[64,128]{1,0:T(8,128)S(1)}, u32[]{:S(2)}, u32[]{:S(2)}) collective-permute-start(f32[64,128]{1,0:T(8,128)S(1)} %shard_map.72.refs_0_), channel_id=1, source_target_pairs={{0,3},{1,2},{2,1},{3,0},{4,7},{5,6},{6,5},{7,4},{8,11},{9,10},{10,... | collective-permute-start | bytes 98312 | tf_op jit(solution)/shard_map/ppermute | solution.py:392
  44.9 1.1 collective-permute-start.15
  46.0 1.6 %collective-permute-start.14 = (f32[64,128]{1,0:T(8,128)S(1)}, f32[64,128]{1,0:T(8,128)S(1)}, u32[]{:S(2)}, u32[]{:S(2)}) collective-permute-start(f32[64,128]{1,0:T(8,128)S(1)} %shard_map.72.refs_0_), channel_id=1, source_target_pairs={{0,1},{1,0},{2,3},{3,2},{4,5},{5,4},{6,7},{7,6},{8,9},{9,8},{10,11... | collective-permute-start | bytes 98312 | tf_op jit(solution)/shard_map/ppermute | solution.py:392
  47.6 1.6 %collective-permute-done.16.refs_3_ = f32[64,128]{1,0:T(8,128)S(1)} collective-permute-done((f32[64,128]{1,0:T(8,128)S(1)}, f32[64,128]{1,0:T(8,128)S(1)}, u32[]{:S(2)}, u32[]{:S(2)}) %collective-permute-start.16) | collective-permute-done | bytes 32800 | tf_op jit(solution)/shard_map/ppermute | solution.py:392
  49.2 0.5 collective-permute-done.15.refs_2_
  49.7 0.3 collective-permute-done.14.refs_1_
  50.0 2.5 %collective-permute-start.19 = (f32[64,128]{1,0:T(8,128)S(1)}, f32[64,128]{1,0:T(8,128)S(1)}, u32[]{:S(2)}, u32[]{:S(2)}) collective-permute-start(f32[64,128]{1,0:T(8,128)S(1)} %shard_map.73.refs_0_), channel_id=1, source_target_pairs={{0,24},{4,28},{8,16},{12,20},{16,8},{20,12},{24,0},{28,4},{1,25},{... | collective-permute-start | bytes 98312 | tf_op jit(solution)/shard_map/ppermute | solution.py:392
  52.5 0.5 collective-permute-start.18
  53.1 0.5 collective-permute-start.17
  53.6 1.3 %collective-permute-done.19.refs_3_ = f32[64,128]{1,0:T(8,128)S(1)} collective-permute-done((f32[64,128]{1,0:T(8,128)S(1)}, f32[64,128]{1,0:T(8,128)S(1)}, u32[]{:S(2)}, u32[]{:S(2)}) %collective-permute-start.19) | collective-permute-done | bytes 32800 | tf_op jit(solution)/shard_map/ppermute | solution.py:392
  54.9 1.5 %collective-permute-done.18.refs_2_ = f32[64,128]{1,0:T(8,128)S(1)} collective-permute-done((f32[64,128]{1,0:T(8,128)S(1)}, f32[64,128]{1,0:T(8,128)S(1)}, u32[]{:S(2)}, u32[]{:S(2)}) %collective-permute-start.18) | collective-permute-done | bytes 32800 | tf_op jit(solution)/shard_map/ppermute | solution.py:392
  56.5 0.5 collective-permute-done.17.refs_1_
  57.1 1.2 collective-permute-done.20.refs_4_
  58.3 12.3 %shard_map.75 = (f32[128,128]{1,0:T(8,128)}, bf16[1024,128]{1,0:T(8,128)(2,1)S(1)}, f32[8,128]{1,0:T(8,128)S(1)}, f32[8,128]{1,0:T(8,128)S(1)}, bf16[1024,4096]{1,0:T(8,128)(2,1)S(1)}) custom-call(bf16[1024,128]{1,0:T(8,128)(2,1)S(1)} %get-tuple-element.37.refs_0_, bf16[4096,256]{1,0:T(8,128)(2,1)S(1)} %get-tuple-element.46.refs_1_.refs_3_, ...), custom_call_target="tpu_custom_call" | custom-call | flops 1073741824 | bytes 11165696 | tf_op jit(solution)/shard_map/pallas_call | solution.py:380
  70.6 2.3 %collective-permute-start.23 = (f32[8,128]{1,0:T(8,128)S(1)}, f32[8,128]{1,0:T(8,128)S(1)}, u32[]{:S(2)}, u32[]{:S(2)}) collective-permute-start(f32[8,128]{1,0:T(8,128)S(1)} %get-tuple-element.56.refs_5_), channel_id=1, source_target_pairs={{0,3},{1,2},{2,1},{3,0},{4,7},{5,6},{6,5},{7,4},{8,11},{9,10},{10,... | collective-permute-start | bytes 12296 | tf_op jit(solution)/shard_map/ppermute | solution.py:392
  72.9 0.6 collective-permute-start.22
  73.5 1.5 %collective-permute-start.21 = (f32[8,128]{1,0:T(8,128)S(1)}, f32[8,128]{1,0:T(8,128)S(1)}, u32[]{:S(2)}, u32[]{:S(2)}) collective-permute-start(f32[8,128]{1,0:T(8,128)S(1)} %get-tuple-element.56.refs_5_), channel_id=1, source_target_pairs={{0,1},{1,0},{2,3},{3,2},{4,5},{5,4},{6,7},{7,6},{8,9},{9,8},{10,11... | collective-permute-start | bytes 12296 | tf_op jit(solution)/shard_map/ppermute | solution.py:392
  74.9 1.0 collective-permute-done.23.refs_8_
  76.0 1.4 %collective-permute-done.22.refs_7_ = f32[8,128]{1,0:T(8,128)S(1)} collective-permute-done((f32[8,128]{1,0:T(8,128)S(1)}, f32[8,128]{1,0:T(8,128)S(1)}, u32[]{:S(2)}, u32[]{:S(2)}) %collective-permute-start.22) | collective-permute-done | bytes 4128 | tf_op jit(solution)/shard_map/ppermute | solution.py:392
  77.4 7.0 %shard_map.76 = (f32[8,512]{1,0:T(8,128)S(1)}, f32[8,128]{1,0:T(8,128)}) custom-call(bf16[1024,128]{1,0:T(8,128)(2,1)S(1)} %get-tuple-element.53.refs_0_, bf16[1024,4096]{1,0:T(8,128)(2,1)S(1)} %get-tuple-element.54.refs_1_, f32[8,128]{1,0:T(8,128)S(1)} %get-tuple-element.55.refs_2_, bf16[4096,256]{1,0:T(8,128)(2,1)S(1)} %get-tuple-element.46.refs_1_.refs_3_, ...), custom_call_target="tpu_custom_call" | custom-call | flops 67108864 | bytes 10805248 | tf_op jit(solution)/shard_map/pallas_call | solution.py:380
  84.4 1.2 collective-permute-done.24.refs_1_
  85.6 1.6 %collective-permute-start.27 = (f32[8,512]{1,0:T(8,128)S(1)}, f32[8,512]{1,0:T(8,128)S(1)}, u32[]{:S(2)}, u32[]{:S(2)}) collective-permute-start(f32[8,512]{1,0:T(8,128)S(1)} %shard_map.77.refs_5_), channel_id=1, source_target_pairs={{0,24},{4,28},{8,16},{12,20},{16,8},{20,12},{24,0},{28,4},{1,25},{... | collective-permute-start | bytes 49160 | tf_op jit(solution)/shard_map/ppermute | solution.py:392
  87.2 0.5 collective-permute-start.26
  87.7 1.5 %collective-permute-start.25 = (f32[8,512]{1,0:T(8,128)S(1)}, f32[8,512]{1,0:T(8,128)S(1)}, u32[]{:S(2)}, u32[]{:S(2)}) collective-permute-start(f32[8,512]{1,0:T(8,128)S(1)} %shard_map.77.refs_5_), channel_id=1, source_target_pairs={{0,8},{4,12},{8,0},{12,4},{16,24},{20,28},{24,16},{28,20},{1,9},{5... | collective-permute-start | bytes 49160 | tf_op jit(solution)/shard_map/ppermute | solution.py:392
  89.2 1.1 collective-permute-done.27.refs_8_
  90.3 0.6 collective-permute-done.26.refs_7_
  90.9 0.5 collective-permute-done.25.refs_6_
  91.4 9.7 %shard_map.78.refs_5_ = f32[8,128]{1,0:T(8,128)S(1)} custom-call(bf16[1024,128]{1,0:T(8,128)(2,1)S(1)} %get-tuple-element.53.refs_0_, bf16[1024,4096]{1,0:T(8,128)(2,1)S(1)} %get-tuple-element.54.refs_1_, f32[8,128]{1,0:T(8,128)S(1)} %get-tuple-element.55.refs_2_, bf16[4096,256]{1,0:T(8,128)(2,1)S(1)} %get-tuple-element.46.refs_1_.refs_3_, ...), custom_call_target="tpu_custom_call" | custom-call | flops 67108864 | bytes 10838016 | tf_op jit(solution)/shard_map/pallas_call | solution.py:380
  101.1 1.6 %collective-permute-start.30 = (f32[8,128]{1,0:T(8,128)S(1)}, f32[8,128]{1,0:T(8,128)S(1)}, u32[]{:S(2)}, u32[]{:S(2)}) collective-permute-start(f32[8,128]{1,0:T(8,128)S(1)} %shard_map.78.refs_5_), channel_id=1, source_target_pairs={{0,3},{1,2},{2,1},{3,0},{4,7},{5,6},{6,5},{7,4},{8,11},{9,10},{10,... | collective-permute-start | bytes 12296 | tf_op jit(solution)/shard_map/ppermute | solution.py:392
  102.7 1.1 collective-permute-start.29
  103.8 1.7 %collective-permute-start.28 = (f32[8,128]{1,0:T(8,128)S(1)}, f32[8,128]{1,0:T(8,128)S(1)}, u32[]{:S(2)}, u32[]{:S(2)}) collective-permute-start(f32[8,128]{1,0:T(8,128)S(1)} %shard_map.78.refs_5_), channel_id=1, source_target_pairs={{0,1},{1,0},{2,3},{3,2},{4,5},{5,4},{6,7},{7,6},{8,9},{9,8},{10,11... | collective-permute-start | bytes 12296 | tf_op jit(solution)/shard_map/ppermute | solution.py:392
  105.5 1.0 collective-permute-done.30.refs_8_
  106.5 0.6 collective-permute-done.29.refs_7_
  107.2 0.2 collective-permute-done.28.refs_6_
  107.4 6.9 %shard_map.79 = (f32[4,1,512]{2,1,0:T(1,128)S(1)}, f32[4,1,512]{2,1,0:T(1,128)S(1)}, f32[8,128]{1,0:T(8,128)}) custom-call(bf16[1024,128]{1,0:T(8,128)(2,1)S(1)} %get-tuple-element.53.refs_0_, bf16[1024,4096]{1,0:T(8,128)(2,1)S(1)} %get-tuple-element.54.refs_1_, f32[8,128]{1,0:T(8,128)S(1)} %get-tuple-element.55.refs_2_, ...), custom_call_target="tpu_custom_call" | custom-call | flops 67108864 | bytes 10805248 | tf_op jit(solution)/shard_map/pallas_call | solution.py:380
  114.3 1.2 collective-permute-done.31.y_ref
  115.5 1.6 %collective-permute-start.32 = (f32[1,512]{1,0:T(1,128)S(1)}, f32[1,512]{1,0:T(1,128)S(1)}, u32[]{:S(2)}, u32[]{:S(2)}) collective-permute-start(f32[1,512]{1,0:T(1,128)S(1)} %get-tuple-element.62), channel_id=1, source_target_pairs={{0,8},{4,12},{8,0},{12,4},{16,24},{20,28},{24,16},{28,20},{1,9},{5... | collective-permute-start | bytes 6152 | tf_op jit(solution)/shard_map/ppermute | solution.py:392
  117.1 1.5 %collective-permute-start.33 = (f32[1,512]{1,0:T(1,128)S(1)}, f32[1,512]{1,0:T(1,128)S(1)}, u32[]{:S(2)}, u32[]{:S(2)}) collective-permute-start(f32[1,512]{1,0:T(1,128)S(1)} %get-tuple-element.63), channel_id=1, source_target_pairs={{0,16},{4,20},{8,24},{12,28},{16,0},{20,4},{24,8},{28,12},{1,17},{... | collective-permute-start | bytes 6152 | tf_op jit(solution)/shard_map/ppermute | solution.py:392
  118.6 0.5 collective-permute-start.34
  119.2 1.5 %collective-permute-done.33.refs_2_ = f32[1,512]{1,0:T(1,128)S(1)} collective-permute-done((f32[1,512]{1,0:T(1,128)S(1)}, f32[1,512]{1,0:T(1,128)S(1)}, u32[]{:S(2)}, u32[]{:S(2)}) %collective-permute-start.33) | collective-permute-done | bytes 2080 | tf_op jit(solution)/shard_map/ppermute | solution.py:392
  120.7 2.4 %collective-permute-done.34.refs_3_ = f32[1,512]{1,0:T(1,128)S(1)} collective-permute-done((f32[1,512]{1,0:T(1,128)S(1)}, f32[1,512]{1,0:T(1,128)S(1)}, u32[]{:S(2)}, u32[]{:S(2)}) %collective-permute-start.34) | collective-permute-done | bytes 2080 | tf_op jit(solution)/shard_map/ppermute | solution.py:392
  123.1 0.6 shard_map.81
  (26 shorter events, 1.0 us)
Async XLA Ops:
  0.6 10.1 %collective-permute-start = (bf16[256,128]{1,0:T(8,128)(2,1)}, bf16[256,128]{1,0:T(8,128)(2,1)S(1)}, u32[]{:S(2)}, u32[]{:S(2)}) collective-permute-start(bf16[256,128]{1,0:T(8,128)(2,1)} %own_ref.1), channel_id=1, source_target_pairs={{0,1},{1,0},{2,3},{3,2},{4,5},{5,4},{6,7},{7,6},{8,9},{9,8},{10,11... | collective-permute-start | bytes 196616 | tf_op jit(solution)/shard_map/ppermute | solution.py:392
  4.7 12.4 %collective-permute-start.5 = (bf16[528,128]{1,0:T(8,128)(2,1)S(1)}, bf16[528,128]{1,0:T(8,128)(2,1)S(1)}, u32[]{:S(2)}, u32[]{:S(2)}) collective-permute-start(bf16[528,128]{1,0:T(8,128)(2,1)S(1)} %fusion.1.block_ref.refs_3_), channel_id=1, source_target_pairs={{0,24},{4,28},{8,16},{12,20},{16,8},{20,12},{24,0},{28,4},{1,25},{... | collective-permute-start | bytes 405512 | tf_op jit(solution)/shard_map/ppermute | solution.py:392
  7.2 9.9 %collective-permute-start.4 = (bf16[528,128]{1,0:T(8,128)(2,1)S(1)}, bf16[528,128]{1,0:T(8,128)(2,1)S(1)}, u32[]{:S(2)}, u32[]{:S(2)}) collective-permute-start(bf16[528,128]{1,0:T(8,128)(2,1)S(1)} %fusion.1.block_ref.refs_3_), channel_id=1, source_target_pairs={{0,16},{4,20},{8,24},{12,28},{16,0},{20,4},{24,8},{28,12},{1,17},{... | collective-permute-start | bytes 405512 | tf_op jit(solution)/shard_map/ppermute | solution.py:392
  7.7 9.4 %collective-permute-start.3 = (bf16[528,128]{1,0:T(8,128)(2,1)S(1)}, bf16[528,128]{1,0:T(8,128)(2,1)S(1)}, u32[]{:S(2)}, u32[]{:S(2)}) collective-permute-start(bf16[528,128]{1,0:T(8,128)(2,1)S(1)} %fusion.1.block_ref.refs_3_), channel_id=1, source_target_pairs={{0,8},{4,12},{8,0},{12,4},{16,24},{20,28},{24,16},{28,20},{1,9},{5... | collective-permute-start | bytes 405512 | tf_op jit(solution)/shard_map/ppermute | solution.py:392
  8.2 6.3 %collective-permute-start.2 = (bf16[256,128]{1,0:T(8,128)(2,1)}, bf16[256,128]{1,0:T(8,128)(2,1)S(1)}, u32[]{:S(2)}, u32[]{:S(2)}) collective-permute-start(bf16[256,128]{1,0:T(8,128)(2,1)} %own_ref.1), channel_id=1, source_target_pairs={{0,3},{1,2},{2,1},{3,0},{4,7},{5,6},{6,5},{7,4},{8,11},{9,10},{10,... | collective-permute-start | bytes 196616 | tf_op jit(solution)/shard_map/ppermute | solution.py:392
  10.7 6.1 %collective-permute-start.1 = (bf16[256,128]{1,0:T(8,128)(2,1)}, bf16[256,128]{1,0:T(8,128)(2,1)S(1)}, u32[]{:S(2)}, u32[]{:S(2)}) collective-permute-start(bf16[256,128]{1,0:T(8,128)(2,1)} %own_ref.1), channel_id=1, source_target_pairs={{0,2},{1,3},{2,0},{3,1},{4,6},{5,7},{6,4},{7,5},{8,10},{9,11},{10,... | collective-permute-start | bytes 196616 | tf_op jit(solution)/shard_map/ppermute | solution.py:392
  10.8 0.8 copy-start
  11.6 0.8 copy-start.1
  17.1 1.8 %collective-permute-start.7 = (bf16[528,128]{1,0:T(8,128)(2,1)S(1)}, bf16[528,128]{1,0:T(8,128)(2,1)S(1)}, u32[]{:S(2)}, u32[]{:S(2)}) collective-permute-start(bf16[528,128]{1,0:T(8,128)(2,1)S(1)} %collective-permute-done.3.refs_5_), channel_id=1, source_target_pairs={{0,4},{4,0},{8,12},{12,8},{16,20},{20,16},{24,28},{28,24},{1,5},{5... | collective-permute-start | bytes 405512 | tf_op jit(solution)/shard_map/ppermute | solution.py:392
  17.2 1.7 %collective-permute-start.8 = (bf16[528,128]{1,0:T(8,128)(2,1)S(1)}, bf16[528,128]{1,0:T(8,128)(2,1)S(1)}, u32[]{:S(2)}, u32[]{:S(2)}) collective-permute-start(bf16[528,128]{1,0:T(8,128)(2,1)S(1)} %collective-permute-done.4.refs_7_), channel_id=1, source_target_pairs={{0,4},{4,0},{8,12},{12,8},{16,20},{20,16},{24,28},{28,24},{1,5},{5... | collective-permute-start | bytes 405512 | tf_op jit(solution)/shard_map/ppermute | solution.py:392
  17.7 1.4 %collective-permute-start.9 = (bf16[528,128]{1,0:T(8,128)(2,1)S(1)}, bf16[528,128]{1,0:T(8,128)(2,1)S(1)}, u32[]{:S(2)}, u32[]{:S(2)}) collective-permute-start(bf16[528,128]{1,0:T(8,128)(2,1)S(1)} %collective-permute-done.5.refs_9_), channel_id=1, source_target_pairs={{0,4},{4,0},{8,12},{12,8},{16,20},{20,16},{24,28},{28,24},{1,5},{5... | collective-permute-start | bytes 405512 | tf_op jit(solution)/shard_map/ppermute | solution.py:392
  17.8 1.5 %collective-permute-start.6 = (bf16[528,128]{1,0:T(8,128)(2,1)S(1)}, bf16[528,128]{1,0:T(8,128)(2,1)S(1)}, u32[]{:S(2)}, u32[]{:S(2)}) collective-permute-start(bf16[528,128]{1,0:T(8,128)(2,1)S(1)} %fusion.1.block_ref.refs_3_), channel_id=1, source_target_pairs={{0,4},{4,0},{8,12},{12,8},{16,20},{20,16},{24,28},{28,24},{1,5},{5... | collective-permute-start | bytes 405512 | tf_op jit(solution)/shard_map/ppermute | solution.py:392
  34.6 5.5 %collective-permute-start.12 = (f32[8,128]{1,0:T(8,128)S(1)}, f32[8,128]{1,0:T(8,128)S(1)}, u32[]{:S(2)}, u32[]{:S(2)}) collective-permute-start(f32[8,128]{1,0:T(8,128)S(1)} %get-tuple-element.48.refs_1_), channel_id=1, source_target_pairs={{0,3},{1,2},{2,1},{3,0},{4,7},{5,6},{6,5},{7,4},{8,11},{9,10},{10,... | collective-permute-start | bytes 12296 | tf_op jit(solution)/shard_map/ppermute | solution.py:392
  36.9 4.5 %collective-permute-start.11 = (f32[8,128]{1,0:T(8,128)S(1)}, f32[8,128]{1,0:T(8,128)S(1)}, u32[]{:S(2)}, u32[]{:S(2)}) collective-permute-start(f32[8,128]{1,0:T(8,128)S(1)} %get-tuple-element.48.refs_1_), channel_id=1, source_target_pairs={{0,2},{1,3},{2,0},{3,1},{4,6},{5,7},{6,4},{7,5},{8,10},{9,11},{10,... | collective-permute-start | bytes 12296 | tf_op jit(solution)/shard_map/ppermute | solution.py:392
  36.9 4.5 %collective-permute-start.10 = (f32[8,128]{1,0:T(8,128)S(1)}, f32[8,128]{1,0:T(8,128)S(1)}, u32[]{:S(2)}, u32[]{:S(2)}) collective-permute-start(f32[8,128]{1,0:T(8,128)S(1)} %get-tuple-element.48.refs_1_), channel_id=1, source_target_pairs={{0,1},{1,0},{2,3},{3,2},{4,5},{5,4},{6,7},{7,6},{8,9},{9,8},{10,11... | collective-permute-start | bytes 12296 | tf_op jit(solution)/shard_map/ppermute | solution.py:392
  41.9 1.3 %collective-permute-start.13 = (f32[64,128]{1,0:T(8,128)S(1)}, f32[64,128]{1,0:T(8,128)S(1)}, u32[]{:S(2)}, u32[]{:S(2)}) collective-permute-start(f32[64,128]{1,0:T(8,128)S(1)} %get-tuple-element.51), channel_id=1, source_target_pairs={{0,4},{4,0},{8,12},{12,8},{16,20},{20,16},{24,28},{28,24},{1,5},{5... | collective-permute-start | bytes 98312 | tf_op jit(solution)/shard_map/ppermute | solution.py:392
  43.2 6.0 %collective-permute-start.16 = (f32[64,128]{1,0:T(8,128)S(1)}, f32[64,128]{1,0:T(8,128)S(1)}, u32[]{:S(2)}, u32[]{:S(2)}) collective-permute-start(f32[64,128]{1,0:T(8,128)S(1)} %shard_map.72.refs_0_), channel_id=1, source_target_pairs={{0,3},{1,2},{2,1},{3,0},{4,7},{5,6},{6,5},{7,4},{8,11},{9,10},{10,... | collective-permute-start | bytes 98312 | tf_op jit(solution)/shard_map/ppermute | solution.py:392
  44.9 4.8 %collective-permute-start.15 = (f32[64,128]{1,0:T(8,128)S(1)}, f32[64,128]{1,0:T(8,128)S(1)}, u32[]{:S(2)}, u32[]{:S(2)}) collective-permute-start(f32[64,128]{1,0:T(8,128)S(1)} %shard_map.72.refs_0_), channel_id=1, source_target_pairs={{0,2},{1,3},{2,0},{3,1},{4,6},{5,7},{6,4},{7,5},{8,10},{9,11},{10,... | collective-permute-start | bytes 98312 | tf_op jit(solution)/shard_map/ppermute | solution.py:392
  46.0 4.0 %collective-permute-start.14 = (f32[64,128]{1,0:T(8,128)S(1)}, f32[64,128]{1,0:T(8,128)S(1)}, u32[]{:S(2)}, u32[]{:S(2)}) collective-permute-start(f32[64,128]{1,0:T(8,128)S(1)} %shard_map.72.refs_0_), channel_id=1, source_target_pairs={{0,1},{1,0},{2,3},{3,2},{4,5},{5,4},{6,7},{7,6},{8,9},{9,8},{10,11... | collective-permute-start | bytes 98312 | tf_op jit(solution)/shard_map/ppermute | solution.py:392
  50.0 4.9 %collective-permute-start.19 = (f32[64,128]{1,0:T(8,128)S(1)}, f32[64,128]{1,0:T(8,128)S(1)}, u32[]{:S(2)}, u32[]{:S(2)}) collective-permute-start(f32[64,128]{1,0:T(8,128)S(1)} %shard_map.73.refs_0_), channel_id=1, source_target_pairs={{0,24},{4,28},{8,16},{12,20},{16,8},{20,12},{24,0},{28,4},{1,25},{... | collective-permute-start | bytes 98312 | tf_op jit(solution)/shard_map/ppermute | solution.py:392
  52.5 3.9 %collective-permute-start.18 = (f32[64,128]{1,0:T(8,128)S(1)}, f32[64,128]{1,0:T(8,128)S(1)}, u32[]{:S(2)}, u32[]{:S(2)}) collective-permute-start(f32[64,128]{1,0:T(8,128)S(1)} %shard_map.73.refs_0_), channel_id=1, source_target_pairs={{0,16},{4,20},{8,24},{12,28},{16,0},{20,4},{24,8},{28,12},{1,17},{... | collective-permute-start | bytes 98312 | tf_op jit(solution)/shard_map/ppermute | solution.py:392
  53.1 3.9 %collective-permute-start.17 = (f32[64,128]{1,0:T(8,128)S(1)}, f32[64,128]{1,0:T(8,128)S(1)}, u32[]{:S(2)}, u32[]{:S(2)}) collective-permute-start(f32[64,128]{1,0:T(8,128)S(1)} %shard_map.73.refs_0_), channel_id=1, source_target_pairs={{0,8},{4,12},{8,0},{12,4},{16,24},{20,28},{24,16},{28,20},{1,9},{5... | collective-permute-start | bytes 98312 | tf_op jit(solution)/shard_map/ppermute | solution.py:392
  57.0 1.3 %collective-permute-start.20 = (f32[64,128]{1,0:T(8,128)S(1)}, f32[64,128]{1,0:T(8,128)S(1)}, u32[]{:S(2)}, u32[]{:S(2)}) collective-permute-start(f32[64,128]{1,0:T(8,128)S(1)} %shard_map.74.refs_3_), channel_id=1, source_target_pairs={{0,4},{4,0},{8,12},{12,8},{16,20},{20,16},{24,28},{28,24},{1,5},{5... | collective-permute-start | bytes 98312 | tf_op jit(solution)/shard_map/ppermute | solution.py:392
  70.6 5.4 %collective-permute-start.23 = (f32[8,128]{1,0:T(8,128)S(1)}, f32[8,128]{1,0:T(8,128)S(1)}, u32[]{:S(2)}, u32[]{:S(2)}) collective-permute-start(f32[8,128]{1,0:T(8,128)S(1)} %get-tuple-element.56.refs_5_), channel_id=1, source_target_pairs={{0,3},{1,2},{2,1},{3,0},{4,7},{5,6},{6,5},{7,4},{8,11},{9,10},{10,... | collective-permute-start | bytes 12296 | tf_op jit(solution)/shard_map/ppermute | solution.py:392
  72.9 4.5 %collective-permute-start.22 = (f32[8,128]{1,0:T(8,128)S(1)}, f32[8,128]{1,0:T(8,128)S(1)}, u32[]{:S(2)}, u32[]{:S(2)}) collective-permute-start(f32[8,128]{1,0:T(8,128)S(1)} %get-tuple-element.56.refs_5_), channel_id=1, source_target_pairs={{0,2},{1,3},{2,0},{3,1},{4,6},{5,7},{6,4},{7,5},{8,10},{9,11},{10,... | collective-permute-start | bytes 12296 | tf_op jit(solution)/shard_map/ppermute | solution.py:392
  73.5 3.9 %collective-permute-start.21 = (f32[8,128]{1,0:T(8,128)S(1)}, f32[8,128]{1,0:T(8,128)S(1)}, u32[]{:S(2)}, u32[]{:S(2)}) collective-permute-start(f32[8,128]{1,0:T(8,128)S(1)} %get-tuple-element.56.refs_5_), channel_id=1, source_target_pairs={{0,1},{1,0},{2,3},{3,2},{4,5},{5,4},{6,7},{7,6},{8,9},{9,8},{10,11... | collective-permute-start | bytes 12296 | tf_op jit(solution)/shard_map/ppermute | solution.py:392
  84.4 1.2 collective-permute-start.24
  85.6 4.7 %collective-permute-start.27 = (f32[8,512]{1,0:T(8,128)S(1)}, f32[8,512]{1,0:T(8,128)S(1)}, u32[]{:S(2)}, u32[]{:S(2)}) collective-permute-start(f32[8,512]{1,0:T(8,128)S(1)} %shard_map.77.refs_5_), channel_id=1, source_target_pairs={{0,24},{4,28},{8,16},{12,20},{16,8},{20,12},{24,0},{28,4},{1,25},{... | collective-permute-start | bytes 49160 | tf_op jit(solution)/shard_map/ppermute | solution.py:392
  87.2 3.7 %collective-permute-start.26 = (f32[8,512]{1,0:T(8,128)S(1)}, f32[8,512]{1,0:T(8,128)S(1)}, u32[]{:S(2)}, u32[]{:S(2)}) collective-permute-start(f32[8,512]{1,0:T(8,128)S(1)} %shard_map.77.refs_5_), channel_id=1, source_target_pairs={{0,16},{4,20},{8,24},{12,28},{16,0},{20,4},{24,8},{28,12},{1,17},{... | collective-permute-start | bytes 49160 | tf_op jit(solution)/shard_map/ppermute | solution.py:392
  87.7 3.7 %collective-permute-start.25 = (f32[8,512]{1,0:T(8,128)S(1)}, f32[8,512]{1,0:T(8,128)S(1)}, u32[]{:S(2)}, u32[]{:S(2)}) collective-permute-start(f32[8,512]{1,0:T(8,128)S(1)} %shard_map.77.refs_5_), channel_id=1, source_target_pairs={{0,8},{4,12},{8,0},{12,4},{16,24},{20,28},{24,16},{28,20},{1,9},{5... | collective-permute-start | bytes 49160 | tf_op jit(solution)/shard_map/ppermute | solution.py:392
  101.1 5.4 %collective-permute-start.30 = (f32[8,128]{1,0:T(8,128)S(1)}, f32[8,128]{1,0:T(8,128)S(1)}, u32[]{:S(2)}, u32[]{:S(2)}) collective-permute-start(f32[8,128]{1,0:T(8,128)S(1)} %shard_map.78.refs_5_), channel_id=1, source_target_pairs={{0,3},{1,2},{2,1},{3,0},{4,7},{5,6},{6,5},{7,4},{8,11},{9,10},{10,... | collective-permute-start | bytes 12296 | tf_op jit(solution)/shard_map/ppermute | solution.py:392
  102.7 4.5 %collective-permute-start.29 = (f32[8,128]{1,0:T(8,128)S(1)}, f32[8,128]{1,0:T(8,128)S(1)}, u32[]{:S(2)}, u32[]{:S(2)}) collective-permute-start(f32[8,128]{1,0:T(8,128)S(1)} %shard_map.78.refs_5_), channel_id=1, source_target_pairs={{0,2},{1,3},{2,0},{3,1},{4,6},{5,7},{6,4},{7,5},{8,10},{9,11},{10,... | collective-permute-start | bytes 12296 | tf_op jit(solution)/shard_map/ppermute | solution.py:392
  103.8 3.6 %collective-permute-start.28 = (f32[8,128]{1,0:T(8,128)S(1)}, f32[8,128]{1,0:T(8,128)S(1)}, u32[]{:S(2)}, u32[]{:S(2)}) collective-permute-start(f32[8,128]{1,0:T(8,128)S(1)} %shard_map.78.refs_5_), channel_id=1, source_target_pairs={{0,1},{1,0},{2,3},{3,2},{4,5},{5,4},{6,7},{7,6},{8,9},{9,8},{10,11... | collective-permute-start | bytes 12296 | tf_op jit(solution)/shard_map/ppermute | solution.py:392
  114.3 1.2 collective-permute-start.31
  115.5 3.7 %collective-permute-start.32 = (f32[1,512]{1,0:T(1,128)S(1)}, f32[1,512]{1,0:T(1,128)S(1)}, u32[]{:S(2)}, u32[]{:S(2)}) collective-permute-start(f32[1,512]{1,0:T(1,128)S(1)} %get-tuple-element.62), channel_id=1, source_target_pairs={{0,8},{4,12},{8,0},{12,4},{16,24},{20,28},{24,16},{28,20},{1,9},{5... | collective-permute-start | bytes 6152 | tf_op jit(solution)/shard_map/ppermute | solution.py:392
  117.1 3.6 %collective-permute-start.33 = (f32[1,512]{1,0:T(1,128)S(1)}, f32[1,512]{1,0:T(1,128)S(1)}, u32[]{:S(2)}, u32[]{:S(2)}) collective-permute-start(f32[1,512]{1,0:T(1,128)S(1)} %get-tuple-element.63), channel_id=1, source_target_pairs={{0,16},{4,20},{8,24},{12,28},{16,0},{20,4},{24,8},{28,12},{1,17},{... | collective-permute-start | bytes 6152 | tf_op jit(solution)/shard_map/ppermute | solution.py:392
  118.6 4.5 %collective-permute-start.34 = (f32[1,512]{1,0:T(1,128)S(1)}, f32[1,512]{1,0:T(1,128)S(1)}, u32[]{:S(2)}, u32[]{:S(2)}) collective-permute-start(f32[1,512]{1,0:T(1,128)S(1)} %get-tuple-element.64), channel_id=1, source_target_pairs={{0,24},{4,28},{8,16},{12,20},{16,8},{20,12},{24,0},{28,4},{1,25},{... | collective-permute-start | bytes 6152 | tf_op jit(solution)/shard_map/ppermute | solution.py:392

commit v10 on v8

--- a/solution.py
+++ b/solution.py
@@ -11,6 +11,7 @@
 ITERS = 2
 LANES = 128
 SUB = 16
+STAGE = 256
 SMALLEST = 1e-16
 LARGEST = 1e12
 NT_DIMS = (((1,), (1,)), ((), ()))
@@ -86,23 +87,22 @@
         top_ref[row_of(i, steps), :] = as_lanes(top)
 
 
-def shifted_rows(aug_ref, t_ref, width, lse_ref, top_ref, mass_ref, e_ref=None, carried_ref=None):
+def shifted_rows(aug_ref, t_ref, width, lse_ref, top_ref, mass_ref, e_ref, carried_ref=None):
     rows = aug_ref.shape[0]
     steps = rows // LANES
-    for g in range(t_ref.shape[0] // width):
-        cols = slice(g * width, (g + 1) * width)
-        for h in range(0, rows, 2 * LANES):
-            at = slice(h, h + 2 * LANES)
-            s = lax.dot_general(aug_ref[at, :], t_ref[cols, :], NT_DIMS, preferred_element_type=jnp.float32)
-            e = jnp.exp(s)
+    stages = t_ref.shape[0] // width
+    keep = e_ref.shape[1] // width
+    for g in range(stages + 1):
+        if g > 0 and carried_ref is not None:
+            e = e_ref[:, (g - 1) % keep * width : ((g - 1) % keep + 1) * width]
+            d = jnp.dot(e, block_of(t_ref, g - 1, width), preferred_element_type=jnp.float32)
+            carried_ref[...] = d if g == 1 else carried_ref[...] + d
+        if g < stages:
+            t = t_ref[g * width : (g + 1) * width, :]
+            e = jnp.exp(lax.dot_general(aug_ref[...], t, NT_DIMS, preferred_element_type=jnp.float32))
             m = lane_fold(jnp.add, e)
-            mass_ref[at, :] = m if g == 0 else mass_ref[at, :] + m
-            e = e.astype(jnp.bfloat16)
-            if e_ref is not None:
-                e_ref[at, cols] = e
-            if carried_ref is not None:
-                d = jnp.dot(e, block_of(t_ref, g, width), preferred_element_type=jnp.float32)
-                carried_ref[at, :] = d if g == 0 else carried_ref[at, :] + d
+            mass_ref[...] = m if g == 0 else mass_ref[...] + m
+            e_ref[:, g % keep * width : (g % keep + 1) * width] = e.astype(jnp.bfloat16)
     masses = []
     for i in range(steps):
         at = slice(i * LANES, (i + 1) * LANES)
@@ -180,7 +180,7 @@
 
 def couple_kernel(nt, width, *refs):
     a_ref, aug_ref, top_ref, t_refs = refs[0], refs[1], refs[2], refs[3 : 3 + nt]
-    lse_ref, carried_ref, t_ref, pot_ref, mass_ref, scores = refs[3 + nt :]
+    lse_ref, carried_ref, t_ref, pot_ref, mass_ref, e_ref, scores = refs[3 + nt :]
     lane = lax.broadcasted_iota(jnp.int32, (LANES, LANES), 1)
     for g in range(nt):
         t_ref[g * width : (g + 1) * width, :LANES] = t_refs[g][:width, :]
@@ -190,7 +190,7 @@
             added = jnp.where(lane == 0, potential, jnp.where(lane == 1, 1.0, 0.0))
             at = g * width + j
             t_ref[at : at + LANES, LANES:] = added.astype(jnp.bfloat16)
-    fine = shifted_rows(aug_ref, t_ref, width, lse_ref, top_ref, mass_ref, None, carried_ref)
+    fine = shifted_rows(aug_ref, t_ref, STAGE, lse_ref, top_ref, mass_ref, e_ref, carried_ref)
 
     @pl.when(jnp.logical_not(fine))
     def _():
@@ -238,7 +238,7 @@
         moment_ref[pl.ds(pl.multiple_of((k ^ (r % 2)) * half, half), half), :] = m_refs[k][...]
     a_ref[...] = project4(s_ref[...], split3(moment_ref[...]))
     add_shifts(a_ref, t_ref, pot_ref[0:1, :], aug_ref, top_ref)
-    fine = shifted_rows(aug_ref, t_ref, pot_ref.shape[1], lse_ref, top_ref, mass_ref, e_ref)
+    fine = shifted_rows(aug_ref, t_ref, STAGE, lse_ref, top_ref, mass_ref, e_ref)
 
     @pl.when(jnp.logical_not(fine))
     def _():
@@ -250,6 +250,10 @@
     high = x.astype(jnp.bfloat16).astype(jnp.float32)
     at = lax.broadcasted_iota(jnp.int32, (SUB, x.shape[1]), 0)
     return jnp.where(at == 0, high, jnp.where(at == 1, x - high, 0.0)).astype(jnp.bfloat16)
+
+
+def on_vector_unit(part):
+    return part % 8 in (2, 4, 6)
 
 
 def rows_kernel(rows_total, *refs):
@@ -260,17 +264,25 @@
     column_ref[...] = math.log(rows_total) - log_sum([l[...] for l in l_refs])
     column = [column_ref[pl.ds(r ^ k, 1), :] for k in range(nt)]
     change = [column[k] - pot_ref[k : k + 1, :] for k in range(nt)]
-    top = jnp.max(functools.reduce(jnp.maximum, change), axis=1, keepdims=True)
+    weight = [jnp.exp(x) for x in change]
     for k in range(nt):
-        weights[:, k * width : (k + 1) * width] = high_low(jnp.exp(change[k] - top))
+        weights[:, k * width : (k + 1) * width] = high_low(weight[k])
     steps = a_ref.shape[0] // LANES
     masses = []
     for i in range(steps):
-        e = e_ref[i * LANES : (i + 1) * LANES, :]
-        sums = lax.dot_general(weights[...], e, NT_DIMS, preferred_element_type=jnp.float32)
-        masses.append(sums[0:1, :] + sums[1:2, :])
+        at = slice(i * LANES, (i + 1) * LANES)
+        if on_vector_unit(i):
+            total = None
+            for k in range(nt):
+                e = e_ref[at, k * width : (k + 1) * width].astype(jnp.float32)
+                m = lane_fold(jnp.add, e * weight[k])
+                total = m if total is None else total + m
+            masses.append(as_lanes(jnp.sum(total, axis=1, keepdims=True)))
+        else:
+            sums = lax.dot_general(weights[...], e_ref[at, :], NT_DIMS, preferred_element_type=jnp.float32)
+            masses.append(sums[0:1, :] + sums[1:2, :])
         row = row_of(i, steps)
-        lse_ref[row, :] = top + top_ref[row, :] + jnp.log(masses[i])
+        lse_ref[row, :] = top_ref[row, :] + jnp.log(masses[i])
 
     @pl.when(jnp.logical_not(within(masses)))
     def _():
@@ -286,9 +298,7 @@
     per = rows // ns // LANES
     potential = math.log(cols_total) - log_sum([l[...] for l in l_refs])
     sp_ref[...] = potential
-    shift = potential + top_ref[...]
-    top = jnp.max(jnp.max(shift, axis=1, keepdims=True), axis=0, keepdims=True)
-    weight_rows[...] = jnp.exp(shift - top)
+    weight_rows[...] = jnp.exp(potential + top_ref[...])
     for k in range(ns):
         for j in range(per):
             at = (k * per + j) * LANES
@@ -300,14 +310,12 @@
         else:
             out_refs[0][pl.ds(r ^ g, 1), :] = lse
 
-    masses = []
+    sums = jnp.dot(weights[...], e_ref[...], preferred_element_type=jnp.float32)
+    mass = sums[0:1, :] + sums[1:2, :]
     for g in range(nt):
-        e = e_ref[:, g * width : (g + 1) * width]
-        sums = jnp.dot(weights[...], e, preferred_element_type=jnp.float32)
-        masses.append(sums[0:1, :] + sums[1:2, :])
-        store(g, top - pot_ref[g : g + 1, :] + jnp.log(masses[g]))
-
-    @pl.when(jnp.logical_not(within(masses)))
+        store(g, jnp.log(mass[:, g * width : (g + 1) * width]) - pot_ref[g : g + 1, :])
+
+    @pl.when(jnp.logical_not(within([mass])))
     def _():
         exact_columns(ns, a_ref, t_ref, sp_ref, spread_rows, scores, store)
 
@@ -416,7 +424,7 @@
         functools.partial(couple_kernel, nt, width),
         [tile, shape((rows, depth), f32), shape((cols, 2 * depth), bf16), shape((nt, width), f32)],
         [a, aug, top] + blocks,
-        [sums, row_scores],
+        [sums, pltpu.VMEM((rows, 2 * STAGE), bf16), row_scores],
         2 * flops,
         exps,
     )

time: 127 us -> 123 us (0.969)
  Pallas kernels: 56.6 us -> 53.1 us
    pallas_call x15, Pallas kernels: 56.6 us -> 53.1 us  [call(): pl.pallas_call(kernel, out_shape=list(out), in_specs=[vmem] * len(args),...]
where the time goes in v10:
time: 123 us
  Pallas kernels  53.1 us (43%)
  starting transfers between devices  38.8 us (32%)
  waiting for transfers between devices  27.8 us (23%)
  local copies, waits for them, and re-layouts  1.68 us (1%)
    pallas_call x15, Pallas kernels, call(): pl.pallas_call(kernel, out_shape=list(out), in_specs=[vmem] * len(args),...  53.1 us
    ppermute x35, starting transfers between devices, swap(): lax.ppermute(x, axis, [(i, i ^ k) for i in range(lax.axis_size(axis))])  38.8 us
    ppermute x35, waiting for transfers between devices, swap(): lax.ppermute(x, axis, [(i, i ^ k) for i in range(lax.axis_size(axis))])  27.8 us
  transfers between devices with their start and end apart: 35, of which 27 were waited for; matrix products, arithmetic and copies ran while one was open for 1% of the time, Pallas kernels for 1%

profile of v10, /device:TPU:0, one launch (start us, length us, event | category | flops | bytes accessed | tf_op | source)
XLA Modules:
  0.0 123.0 jit_solution(10571375001876969738)
XLA Ops:
  0.6 3.1 %collective-permute-start = (bf16[256,128]{1,0:T(8,128)(2,1)}, bf16[256,128]{1,0:T(8,128)(2,1)S(1)}, u32[]{:S(2)}, u32[]{:S(2)}) collective-permute-start(bf16[256,128]{1,0:T(8,128)(2,1)} %own_ref.1), channel_id=1, source_target_pairs={{0,1},{1,0},{2,3},{3,2},{4,5},{5,4},{6,7},{7,6},{8,9},{9,8},{10,11... | collective-permute-start | bytes 196616 | tf_op jit(solution)/shard_map/ppermute | solution.py:373
  3.7 0.9 fusion.1.block_ref.refs_3_
  4.7 2.5 %collective-permute-start.5 = (bf16[528,128]{1,0:T(8,128)(2,1)S(1)}, bf16[528,128]{1,0:T(8,128)(2,1)S(1)}, u32[]{:S(2)}, u32[]{:S(2)}) collective-permute-start(bf16[528,128]{1,0:T(8,128)(2,1)S(1)} %fusion.1.block_ref.refs_3_), channel_id=1, source_target_pairs={{0,24},{4,28},{8,16},{12,20},{16,8},{20,12},{24,0},{28,4},{1,25},{... | collective-permute-start | bytes 405512 | tf_op jit(solution)/shard_map/ppermute | solution.py:373
  7.2 0.5 collective-permute-start.4
  7.7 0.5 collective-permute-start.3
  8.2 2.5 %collective-permute-start.2 = (bf16[256,128]{1,0:T(8,128)(2,1)}, bf16[256,128]{1,0:T(8,128)(2,1)S(1)}, u32[]{:S(2)}, u32[]{:S(2)}) collective-permute-start(bf16[256,128]{1,0:T(8,128)(2,1)} %own_ref.1), channel_id=1, source_target_pairs={{0,3},{1,2},{2,1},{3,0},{4,7},{5,6},{6,5},{7,4},{8,11},{9,10},{10,... | collective-permute-start | bytes 196616 | tf_op jit(solution)/shard_map/ppermute | solution.py:373
  10.8 0.8 copy-done
  11.6 0.8 copy-done.1
  12.5 0.2 shard_map.67
  12.7 1.8 %collective-permute-done.2.refs_3_ = bf16[256,128]{1,0:T(8,128)(2,1)S(1)} collective-permute-done((bf16[256,128]{1,0:T(8,128)(2,1)}, bf16[256,128]{1,0:T(8,128)(2,1)S(1)}, u32[]{:S(2)}, u32[]{:S(2)}) %collective-permute-start.2) | collective-permute-done | bytes 65568 | tf_op jit(solution)/shard_map/ppermute | solution.py:373
  14.5 2.3 %collective-permute-done.1.refs_2_ = bf16[256,128]{1,0:T(8,128)(2,1)S(1)} collective-permute-done((bf16[256,128]{1,0:T(8,128)(2,1)}, bf16[256,128]{1,0:T(8,128)(2,1)S(1)}, u32[]{:S(2)}, u32[]{:S(2)}) %collective-permute-start.1) | collective-permute-done | bytes 65568 | tf_op jit(solution)/shard_map/ppermute | solution.py:373
  16.8 0.3 shard_map.68
  17.2 0.5 collective-permute-start.8
  17.8 0.4 collective-permute-start.6
  18.2 0.7 shard_map.69
  19.1 0.2 collective-permute-done.6.refs_4_
  19.2 15.2 %shard_map.70 = (f32[8,128]{1,0:T(8,128)S(1)}, f32[1024,128]{1,0:T(8,128)S(1)}, bf16[4096,256]{1,0:T(8,128)(2,1)S(1)}, f32[8,512]{1,0:T(8,128)S(1)}) custom-call(bf16[1024,128]{1,0:T(8,128)(2,1)S(1)} %get-tuple-element.39.a_ref.refs_0_, bf16[1024,256]{1,0:T(8,128)(2,1)S(1)} %get-tuple-element.41.refs_1_, f32[8,128]{1,0:T(8,128)S(1)} %get-tuple-element.42.refs_2_, ...), custom_call_target="tpu_custom_call" | custom-call | flops 2147483648 | bytes 4513792 | tf_op jit(solution)/shard_map/pallas_call | solution.py:361
  34.5 2.2 %collective-permute-start.12 = (f32[8,128]{1,0:T(8,128)S(1)}, f32[8,128]{1,0:T(8,128)S(1)}, u32[]{:S(2)}, u32[]{:S(2)}) collective-permute-start(f32[8,128]{1,0:T(8,128)S(1)} %get-tuple-element.48.refs_1_), channel_id=1, source_target_pairs={{0,3},{1,2},{2,1},{3,0},{4,7},{5,6},{6,5},{7,4},{8,11},{9,10},{10,... | collective-permute-start | bytes 12296 | tf_op jit(solution)/shard_map/ppermute | solution.py:373
  36.7 2.2 %collective-permute-start.10 = (f32[8,128]{1,0:T(8,128)S(1)}, f32[8,128]{1,0:T(8,128)S(1)}, u32[]{:S(2)}, u32[]{:S(2)}) collective-permute-start(f32[8,128]{1,0:T(8,128)S(1)} %get-tuple-element.48.refs_1_), channel_id=1, source_target_pairs={{0,1},{1,0},{2,3},{3,2},{4,5},{5,4},{6,7},{7,6},{8,9},{9,8},{10,11... | collective-permute-start | bytes 12296 | tf_op jit(solution)/shard_map/ppermute | solution.py:373
  38.9 1.0 collective-permute-done.12.refs_4_
  39.9 1.3 %collective-permute-done.11.refs_3_ = f32[8,128]{1,0:T(8,128)S(1)} collective-permute-done((f32[8,128]{1,0:T(8,128)S(1)}, f32[8,128]{1,0:T(8,128)S(1)}, u32[]{:S(2)}, u32[]{:S(2)}) %collective-permute-start.11) | collective-permute-done | bytes 4128 | tf_op jit(solution)/shard_map/ppermute | solution.py:373
  41.2 0.5 shard_map.71
  41.8 1.2 collective-permute-done.13.refs_1_
  43.0 1.7 %collective-permute-start.16 = (f32[64,128]{1,0:T(8,128)S(1)}, f32[64,128]{1,0:T(8,128)S(1)}, u32[]{:S(2)}, u32[]{:S(2)}) collective-permute-start(f32[64,128]{1,0:T(8,128)S(1)} %shard_map.72.refs_0_), channel_id=1, source_target_pairs={{0,3},{1,2},{2,1},{3,0},{4,7},{5,6},{6,5},{7,4},{8,11},{9,10},{10,... | collective-permute-start | bytes 98312 | tf_op jit(solution)/shard_map/ppermute | solution.py:373
  44.7 1.1 collective-permute-start.15
  45.8 1.6 %collective-permute-start.14 = (f32[64,128]{1,0:T(8,128)S(1)}, f32[64,128]{1,0:T(8,128)S(1)}, u32[]{:S(2)}, u32[]{:S(2)}) collective-permute-start(f32[64,128]{1,0:T(8,128)S(1)} %shard_map.72.refs_0_), channel_id=1, source_target_pairs={{0,1},{1,0},{2,3},{3,2},{4,5},{5,4},{6,7},{7,6},{8,9},{9,8},{10,11... | collective-permute-start | bytes 98312 | tf_op jit(solution)/shard_map/ppermute | solution.py:373
  47.4 1.6 %collective-permute-done.16.refs_3_ = f32[64,128]{1,0:T(8,128)S(1)} collective-permute-done((f32[64,128]{1,0:T(8,128)S(1)}, f32[64,128]{1,0:T(8,128)S(1)}, u32[]{:S(2)}, u32[]{:S(2)}) %collective-permute-start.16) | collective-permute-done | bytes 32800 | tf_op jit(solution)/shard_map/ppermute | solution.py:373
  49.0 0.5 collective-permute-done.15.refs_2_
  49.5 0.3 collective-permute-done.14.refs_1_
  49.9 2.5 %collective-permute-start.19 = (f32[64,128]{1,0:T(8,128)S(1)}, f32[64,128]{1,0:T(8,128)S(1)}, u32[]{:S(2)}, u32[]{:S(2)}) collective-permute-start(f32[64,128]{1,0:T(8,128)S(1)} %shard_map.73.refs_0_), channel_id=1, source_target_pairs={{0,24},{4,28},{8,16},{12,20},{16,8},{20,12},{24,0},{28,4},{1,25},{... | collective-permute-start | bytes 98312 | tf_op jit(solution)/shard_map/ppermute | solution.py:373
  52.4 0.5 collective-permute-start.18
  52.9 0.5 collective-permute-start.17
  53.4 1.3 %collective-permute-done.19.refs_3_ = f32[64,128]{1,0:T(8,128)S(1)} collective-permute-done((f32[64,128]{1,0:T(8,128)S(1)}, f32[64,128]{1,0:T(8,128)S(1)}, u32[]{:S(2)}, u32[]{:S(2)}) %collective-permute-start.19) | collective-permute-done | bytes 32800 | tf_op jit(solution)/shard_map/ppermute | solution.py:373
  54.7 1.5 %collective-permute-done.18.refs_2_ = f32[64,128]{1,0:T(8,128)S(1)} collective-permute-done((f32[64,128]{1,0:T(8,128)S(1)}, f32[64,128]{1,0:T(8,128)S(1)}, u32[]{:S(2)}, u32[]{:S(2)}) %collective-permute-start.18) | collective-permute-done | bytes 32800 | tf_op jit(solution)/shard_map/ppermute | solution.py:373
  56.3 0.5 collective-permute-done.17.refs_1_
  56.9 1.2 collective-permute-done.20.refs_4_
  58.1 12.2 %shard_map.75 = (f32[128,128]{1,0:T(8,128)}, bf16[1024,128]{1,0:T(8,128)(2,1)S(1)}, f32[8,128]{1,0:T(8,128)S(1)}, f32[8,128]{1,0:T(8,128)S(1)}, bf16[1024,4096]{1,0:T(8,128)(2,1)S(1)}) custom-call(bf16[1024,128]{1,0:T(8,128)(2,1)S(1)} %get-tuple-element.37.refs_0_, bf16[4096,256]{1,0:T(8,128)(2,1)S(1)} %get-tuple-element.46.refs_1_.refs_3_, ...), custom_call_target="tpu_custom_call" | custom-call | flops 1073741824 | bytes 11165696 | tf_op jit(solution)/shard_map/pallas_call | solution.py:361
  70.3 2.3 %collective-permute-start.23 = (f32[8,128]{1,0:T(8,128)S(1)}, f32[8,128]{1,0:T(8,128)S(1)}, u32[]{:S(2)}, u32[]{:S(2)}) collective-permute-start(f32[8,128]{1,0:T(8,128)S(1)} %get-tuple-element.56.refs_5_), channel_id=1, source_target_pairs={{0,3},{1,2},{2,1},{3,0},{4,7},{5,6},{6,5},{7,4},{8,11},{9,10},{10,... | collective-permute-start | bytes 12296 | tf_op jit(solution)/shard_map/ppermute | solution.py:373
  72.6 0.6 collective-permute-start.22
  73.2 1.5 %collective-permute-start.21 = (f32[8,128]{1,0:T(8,128)S(1)}, f32[8,128]{1,0:T(8,128)S(1)}, u32[]{:S(2)}, u32[]{:S(2)}) collective-permute-start(f32[8,128]{1,0:T(8,128)S(1)} %get-tuple-element.56.refs_5_), channel_id=1, source_target_pairs={{0,1},{1,0},{2,3},{3,2},{4,5},{5,4},{6,7},{7,6},{8,9},{9,8},{10,11... | collective-permute-start | bytes 12296 | tf_op jit(solution)/shard_map/ppermute | solution.py:373
  74.7 1.0 collective-permute-done.23.refs_8_
  75.7 1.4 %collective-permute-done.22.refs_7_ = f32[8,128]{1,0:T(8,128)S(1)} collective-permute-done((f32[8,128]{1,0:T(8,128)S(1)}, f32[8,128]{1,0:T(8,128)S(1)}, u32[]{:S(2)}, u32[]{:S(2)}) %collective-permute-start.22) | collective-permute-done | bytes 4128 | tf_op jit(solution)/shard_map/ppermute | solution.py:373
  77.1 7.0 %shard_map.76 = (f32[8,512]{1,0:T(8,128)S(1)}, f32[8,128]{1,0:T(8,128)}) custom-call(bf16[1024,128]{1,0:T(8,128)(2,1)S(1)} %get-tuple-element.53.refs_0_, bf16[1024,4096]{1,0:T(8,128)(2,1)S(1)} %get-tuple-element.54.refs_1_, f32[8,128]{1,0:T(8,128)S(1)} %get-tuple-element.55.refs_2_, bf16[4096,256]{1,0:T(8,128)(2,1)S(1)} %get-tuple-element.46.refs_1_.refs_3_, ...), custom_call_target="tpu_custom_call" | custom-call | flops 67108864 | bytes 10805248 | tf_op jit(solution)/shard_map/pallas_call | solution.py:361
  84.1 1.2 collective-permute-done.24.refs_1_
  85.3 1.6 %collective-permute-start.27 = (f32[8,512]{1,0:T(8,128)S(1)}, f32[8,512]{1,0:T(8,128)S(1)}, u32[]{:S(2)}, u32[]{:S(2)}) collective-permute-start(f32[8,512]{1,0:T(8,128)S(1)} %shard_map.77.refs_5_), channel_id=1, source_target_pairs={{0,24},{4,28},{8,16},{12,20},{16,8},{20,12},{24,0},{28,4},{1,25},{... | collective-permute-start | bytes 49160 | tf_op jit(solution)/shard_map/ppermute | solution.py:373
  86.8 0.5 collective-permute-start.26
  87.3 1.5 %collective-permute-start.25 = (f32[8,512]{1,0:T(8,128)S(1)}, f32[8,512]{1,0:T(8,128)S(1)}, u32[]{:S(2)}, u32[]{:S(2)}) collective-permute-start(f32[8,512]{1,0:T(8,128)S(1)} %shard_map.77.refs_5_), channel_id=1, source_target_pairs={{0,8},{4,12},{8,0},{12,4},{16,24},{20,28},{24,16},{28,20},{1,9},{5... | collective-permute-start | bytes 49160 | tf_op jit(solution)/shard_map/ppermute | solution.py:373
  88.8 1.1 collective-permute-done.27.refs_8_
  90.0 0.6 collective-permute-done.26.refs_7_
  90.6 0.5 collective-permute-done.25.refs_6_
  91.1 9.5 %shard_map.78.refs_5_ = f32[8,128]{1,0:T(8,128)S(1)} custom-call(bf16[1024,128]{1,0:T(8,128)(2,1)S(1)} %get-tuple-element.53.refs_0_, bf16[1024,4096]{1,0:T(8,128)(2,1)S(1)} %get-tuple-element.54.refs_1_, f32[8,128]{1,0:T(8,128)S(1)} %get-tuple-element.55.refs_2_, bf16[4096,256]{1,0:T(8,128)(2,1)S(1)} %get-tuple-element.46.refs_1_.refs_3_, ...), custom_call_target="tpu_custom_call" | custom-call | flops 67108864 | bytes 10838016 | tf_op jit(solution)/shard_map/pallas_call | solution.py:361
  100.6 1.6 %collective-permute-start.30 = (f32[8,128]{1,0:T(8,128)S(1)}, f32[8,128]{1,0:T(8,128)S(1)}, u32[]{:S(2)}, u32[]{:S(2)}) collective-permute-start(f32[8,128]{1,0:T(8,128)S(1)} %shard_map.78.refs_5_), channel_id=1, source_target_pairs={{0,3},{1,2},{2,1},{3,0},{4,7},{5,6},{6,5},{7,4},{8,11},{9,10},{10,... | collective-permute-start | bytes 12296 | tf_op jit(solution)/shard_map/ppermute | solution.py:373
  102.2 1.1 collective-permute-start.29
  103.3 1.8 %collective-permute-start.28 = (f32[8,128]{1,0:T(8,128)S(1)}, f32[8,128]{1,0:T(8,128)S(1)}, u32[]{:S(2)}, u32[]{:S(2)}) collective-permute-start(f32[8,128]{1,0:T(8,128)S(1)} %shard_map.78.refs_5_), channel_id=1, source_target_pairs={{0,1},{1,0},{2,3},{3,2},{4,5},{5,4},{6,7},{7,6},{8,9},{9,8},{10,11... | collective-permute-start | bytes 12296 | tf_op jit(solution)/shard_map/ppermute | solution.py:373
  105.0 1.0 collective-permute-done.30.refs_8_
  106.0 0.7 collective-permute-done.29.refs_7_
  106.9 6.7 %shard_map.79 = (f32[4,1,512]{2,1,0:T(1,128)S(1)}, f32[4,1,512]{2,1,0:T(1,128)S(1)}, f32[8,128]{1,0:T(8,128)}) custom-call(bf16[1024,128]{1,0:T(8,128)(2,1)S(1)} %get-tuple-element.53.refs_0_, bf16[1024,4096]{1,0:T(8,128)(2,1)S(1)} %get-tuple-element.54.refs_1_, f32[8,128]{1,0:T(8,128)S(1)} %get-tuple-element.55.refs_2_, ...), custom_call_target="tpu_custom_call" | custom-call | flops 67108864 | bytes 10805248 | tf_op jit(solution)/shard_map/pallas_call | solution.py:361
  113.6 1.2 collective-permute-done.31.y_ref
  114.8 1.6 %collective-permute-start.32 = (f32[1,512]{1,0:T(1,128)S(1)}, f32[1,512]{1,0:T(1,128)S(1)}, u32[]{:S(2)}, u32[]{:S(2)}) collective-permute-start(f32[1,512]{1,0:T(1,128)S(1)} %get-tuple-element.62), channel_id=1, source_target_pairs={{0,8},{4,12},{8,0},{12,4},{16,24},{20,28},{24,16},{28,20},{1,9},{5... | collective-permute-start | bytes 6152 | tf_op jit(solution)/shard_map/ppermute | solution.py:373
  116.4 1.5 %collective-permute-start.33 = (f32[1,512]{1,0:T(1,128)S(1)}, f32[1,512]{1,0:T(1,128)S(1)}, u32[]{:S(2)}, u32[]{:S(2)}) collective-permute-start(f32[1,512]{1,0:T(1,128)S(1)} %get-tuple-element.63), channel_id=1, source_target_pairs={{0,16},{4,20},{8,24},{12,28},{16,0},{20,4},{24,8},{28,12},{1,17},{... | collective-permute-start | bytes 6152 | tf_op jit(solution)/shard_map/ppermute | solution.py:373
  117.9 0.5 collective-permute-start.34
  118.5 1.5 %collective-permute-done.33.refs_2_ = f32[1,512]{1,0:T(1,128)S(1)} collective-permute-done((f32[1,512]{1,0:T(1,128)S(1)}, f32[1,512]{1,0:T(1,128)S(1)}, u32[]{:S(2)}, u32[]{:S(2)}) %collective-permute-start.33) | collective-permute-done | bytes 2080 | tf_op jit(solution)/shard_map/ppermute | solution.py:373
  120.0 2.4 %collective-permute-done.34.refs_3_ = f32[1,512]{1,0:T(1,128)S(1)} collective-permute-done((f32[1,512]{1,0:T(1,128)S(1)}, f32[1,512]{1,0:T(1,128)S(1)}, u32[]{:S(2)}, u32[]{:S(2)}) %collective-permute-start.34) | collective-permute-done | bytes 2080 | tf_op jit(solution)/shard_map/ppermute | solution.py:373
  122.4 0.6 shard_map.81
  (26 shorter events, 0.9 us)
Async XLA Ops:
  0.6 10.1 %collective-permute-start = (bf16[256,128]{1,0:T(8,128)(2,1)}, bf16[256,128]{1,0:T(8,128)(2,1)S(1)}, u32[]{:S(2)}, u32[]{:S(2)}) collective-permute-start(bf16[256,128]{1,0:T(8,128)(2,1)} %own_ref.1), channel_id=1, source_target_pairs={{0,1},{1,0},{2,3},{3,2},{4,5},{5,4},{6,7},{7,6},{8,9},{9,8},{10,11... | collective-permute-start | bytes 196616 | tf_op jit(solution)/shard_map/ppermute | solution.py:373
  4.7 12.4 %collective-permute-start.5 = (bf16[528,128]{1,0:T(8,128)(2,1)S(1)}, bf16[528,128]{1,0:T(8,128)(2,1)S(1)}, u32[]{:S(2)}, u32[]{:S(2)}) collective-permute-start(bf16[528,128]{1,0:T(8,128)(2,1)S(1)} %fusion.1.block_ref.refs_3_), channel_id=1, source_target_pairs={{0,24},{4,28},{8,16},{12,20},{16,8},{20,12},{24,0},{28,4},{1,25},{... | collective-permute-start | bytes 405512 | tf_op jit(solution)/shard_map/ppermute | solution.py:373
  7.2 9.9 %collective-permute-start.4 = (bf16[528,128]{1,0:T(8,128)(2,1)S(1)}, bf16[528,128]{1,0:T(8,128)(2,1)S(1)}, u32[]{:S(2)}, u32[]{:S(2)}) collective-permute-start(bf16[528,128]{1,0:T(8,128)(2,1)S(1)} %fusion.1.block_ref.refs_3_), channel_id=1, source_target_pairs={{0,16},{4,20},{8,24},{12,28},{16,0},{20,4},{24,8},{28,12},{1,17},{... | collective-permute-start | bytes 405512 | tf_op jit(solution)/shard_map/ppermute | solution.py:373
  7.7 9.4 %collective-permute-start.3 = (bf16[528,128]{1,0:T(8,128)(2,1)S(1)}, bf16[528,128]{1,0:T(8,128)(2,1)S(1)}, u32[]{:S(2)}, u32[]{:S(2)}) collective-permute-start(bf16[528,128]{1,0:T(8,128)(2,1)S(1)} %fusion.1.block_ref.refs_3_), channel_id=1, source_target_pairs={{0,8},{4,12},{8,0},{12,4},{16,24},{20,28},{24,16},{28,20},{1,9},{5... | collective-permute-start | bytes 405512 | tf_op jit(solution)/shard_map/ppermute | solution.py:373
  8.2 6.3 %collective-permute-start.2 = (bf16[256,128]{1,0:T(8,128)(2,1)}, bf16[256,128]{1,0:T(8,128)(2,1)S(1)}, u32[]{:S(2)}, u32[]{:S(2)}) collective-permute-start(bf16[256,128]{1,0:T(8,128)(2,1)} %own_ref.1), channel_id=1, source_target_pairs={{0,3},{1,2},{2,1},{3,0},{4,7},{5,6},{6,5},{7,4},{8,11},{9,10},{10,... | collective-permute-start | bytes 196616 | tf_op jit(solution)/shard_map/ppermute | solution.py:373
  10.7 6.1 %collective-permute-start.1 = (bf16[256,128]{1,0:T(8,128)(2,1)}, bf16[256,128]{1,0:T(8,128)(2,1)S(1)}, u32[]{:S(2)}, u32[]{:S(2)}) collective-permute-start(bf16[256,128]{1,0:T(8,128)(2,1)} %own_ref.1), channel_id=1, source_target_pairs={{0,2},{1,3},{2,0},{3,1},{4,6},{5,7},{6,4},{7,5},{8,10},{9,11},{10,... | collective-permute-start | bytes 196616 | tf_op jit(solution)/shard_map/ppermute | solution.py:373
  10.8 0.8 copy-start
  11.6 0.8 copy-start.1
  17.1 1.8 %collective-permute-start.7 = (bf16[528,128]{1,0:T(8,128)(2,1)S(1)}, bf16[528,128]{1,0:T(8,128)(2,1)S(1)}, u32[]{:S(2)}, u32[]{:S(2)}) collective-permute-start(bf16[528,128]{1,0:T(8,128)(2,1)S(1)} %collective-permute-done.3.refs_5_), channel_id=1, source_target_pairs={{0,4},{4,0},{8,12},{12,8},{16,20},{20,16},{24,28},{28,24},{1,5},{5... | collective-permute-start | bytes 405512 | tf_op jit(solution)/shard_map/ppermute | solution.py:373
  17.2 1.7 %collective-permute-start.8 = (bf16[528,128]{1,0:T(8,128)(2,1)S(1)}, bf16[528,128]{1,0:T(8,128)(2,1)S(1)}, u32[]{:S(2)}, u32[]{:S(2)}) collective-permute-start(bf16[528,128]{1,0:T(8,128)(2,1)S(1)} %collective-permute-done.4.refs_7_), channel_id=1, source_target_pairs={{0,4},{4,0},{8,12},{12,8},{16,20},{20,16},{24,28},{28,24},{1,5},{5... | collective-permute-start | bytes 405512 | tf_op jit(solution)/shard_map/ppermute | solution.py:373
  17.7 1.4 %collective-permute-start.9 = (bf16[528,128]{1,0:T(8,128)(2,1)S(1)}, bf16[528,128]{1,0:T(8,128)(2,1)S(1)}, u32[]{:S(2)}, u32[]{:S(2)}) collective-permute-start(bf16[528,128]{1,0:T(8,128)(2,1)S(1)} %collective-permute-done.5.refs_9_), channel_id=1, source_target_pairs={{0,4},{4,0},{8,12},{12,8},{16,20},{20,16},{24,28},{28,24},{1,5},{5... | collective-permute-start | bytes 405512 | tf_op jit(solution)/shard_map/ppermute | solution.py:373
  17.8 1.5 %collective-permute-start.6 = (bf16[528,128]{1,0:T(8,128)(2,1)S(1)}, bf16[528,128]{1,0:T(8,128)(2,1)S(1)}, u32[]{:S(2)}, u32[]{:S(2)}) collective-permute-start(bf16[528,128]{1,0:T(8,128)(2,1)S(1)} %fusion.1.block_ref.refs_3_), channel_id=1, source_target_pairs={{0,4},{4,0},{8,12},{12,8},{16,20},{20,16},{24,28},{28,24},{1,5},{5... | collective-permute-start | bytes 405512 | tf_op jit(solution)/shard_map/ppermute | solution.py:373
  34.5 5.5 %collective-permute-start.12 = (f32[8,128]{1,0:T(8,128)S(1)}, f32[8,128]{1,0:T(8,128)S(1)}, u32[]{:S(2)}, u32[]{:S(2)}) collective-permute-start(f32[8,128]{1,0:T(8,128)S(1)} %get-tuple-element.48.refs_1_), channel_id=1, source_target_pairs={{0,3},{1,2},{2,1},{3,0},{4,7},{5,6},{6,5},{7,4},{8,11},{9,10},{10,... | collective-permute-start | bytes 12296 | tf_op jit(solution)/shard_map/ppermute | solution.py:373
  36.7 4.5 %collective-permute-start.11 = (f32[8,128]{1,0:T(8,128)S(1)}, f32[8,128]{1,0:T(8,128)S(1)}, u32[]{:S(2)}, u32[]{:S(2)}) collective-permute-start(f32[8,128]{1,0:T(8,128)S(1)} %get-tuple-element.48.refs_1_), channel_id=1, source_target_pairs={{0,2},{1,3},{2,0},{3,1},{4,6},{5,7},{6,4},{7,5},{8,10},{9,11},{10,... | collective-permute-start | bytes 12296 | tf_op jit(solution)/shard_map/ppermute | solution.py:373
  36.7 4.5 %collective-permute-start.10 = (f32[8,128]{1,0:T(8,128)S(1)}, f32[8,128]{1,0:T(8,128)S(1)}, u32[]{:S(2)}, u32[]{:S(2)}) collective-permute-start(f32[8,128]{1,0:T(8,128)S(1)} %get-tuple-element.48.refs_1_), channel_id=1, source_target_pairs={{0,1},{1,0},{2,3},{3,2},{4,5},{5,4},{6,7},{7,6},{8,9},{9,8},{10,11... | collective-permute-start | bytes 12296 | tf_op jit(solution)/shard_map/ppermute | solution.py:373
  41.7 1.3 %collective-permute-start.13 = (f32[64,128]{1,0:T(8,128)S(1)}, f32[64,128]{1,0:T(8,128)S(1)}, u32[]{:S(2)}, u32[]{:S(2)}) collective-permute-start(f32[64,128]{1,0:T(8,128)S(1)} %get-tuple-element.51), channel_id=1, source_target_pairs={{0,4},{4,0},{8,12},{12,8},{16,20},{20,16},{24,28},{28,24},{1,5},{5... | collective-permute-start | bytes 98312 | tf_op jit(solution)/shard_map/ppermute | solution.py:373
  43.0 6.0 %collective-permute-start.16 = (f32[64,128]{1,0:T(8,128)S(1)}, f32[64,128]{1,0:T(8,128)S(1)}, u32[]{:S(2)}, u32[]{:S(2)}) collective-permute-start(f32[64,128]{1,0:T(8,128)S(1)} %shard_map.72.refs_0_), channel_id=1, source_target_pairs={{0,3},{1,2},{2,1},{3,0},{4,7},{5,6},{6,5},{7,4},{8,11},{9,10},{10,... | collective-permute-start | bytes 98312 | tf_op jit(solution)/shard_map/ppermute | solution.py:373
  44.7 4.8 %collective-permute-start.15 = (f32[64,128]{1,0:T(8,128)S(1)}, f32[64,128]{1,0:T(8,128)S(1)}, u32[]{:S(2)}, u32[]{:S(2)}) collective-permute-start(f32[64,128]{1,0:T(8,128)S(1)} %shard_map.72.refs_0_), channel_id=1, source_target_pairs={{0,2},{1,3},{2,0},{3,1},{4,6},{5,7},{6,4},{7,5},{8,10},{9,11},{10,... | collective-permute-start | bytes 98312 | tf_op jit(solution)/shard_map/ppermute | solution.py:373
  45.8 4.0 %collective-permute-start.14 = (f32[64,128]{1,0:T(8,128)S(1)}, f32[64,128]{1,0:T(8,128)S(1)}, u32[]{:S(2)}, u32[]{:S(2)}) collective-permute-start(f32[64,128]{1,0:T(8,128)S(1)} %shard_map.72.refs_0_), channel_id=1, source_target_pairs={{0,1},{1,0},{2,3},{3,2},{4,5},{5,4},{6,7},{7,6},{8,9},{9,8},{10,11... | collective-permute-start | bytes 98312 | tf_op jit(solution)/shard_map/ppermute | solution.py:373
  49.9 4.9 %collective-permute-start.19 = (f32[64,128]{1,0:T(8,128)S(1)}, f32[64,128]{1,0:T(8,128)S(1)}, u32[]{:S(2)}, u32[]{:S(2)}) collective-permute-start(f32[64,128]{1,0:T(8,128)S(1)} %shard_map.73.refs_0_), channel_id=1, source_target_pairs={{0,24},{4,28},{8,16},{12,20},{16,8},{20,12},{24,0},{28,4},{1,25},{... | collective-permute-start | bytes 98312 | tf_op jit(solution)/shard_map/ppermute | solution.py:373
  52.4 3.9 %collective-permute-start.18 = (f32[64,128]{1,0:T(8,128)S(1)}, f32[64,128]{1,0:T(8,128)S(1)}, u32[]{:S(2)}, u32[]{:S(2)}) collective-permute-start(f32[64,128]{1,0:T(8,128)S(1)} %shard_map.73.refs_0_), channel_id=1, source_target_pairs={{0,16},{4,20},{8,24},{12,28},{16,0},{20,4},{24,8},{28,12},{1,17},{... | collective-permute-start | bytes 98312 | tf_op jit(solution)/shard_map/ppermute | solution.py:373
  52.9 3.9 %collective-permute-start.17 = (f32[64,128]{1,0:T(8,128)S(1)}, f32[64,128]{1,0:T(8,128)S(1)}, u32[]{:S(2)}, u32[]{:S(2)}) collective-permute-start(f32[64,128]{1,0:T(8,128)S(1)} %shard_map.73.refs_0_), channel_id=1, source_target_pairs={{0,8},{4,12},{8,0},{12,4},{16,24},{20,28},{24,16},{28,20},{1,9},{5... | collective-permute-start | bytes 98312 | tf_op jit(solution)/shard_map/ppermute | solution.py:373
  56.8 1.3 %collective-permute-start.20 = (f32[64,128]{1,0:T(8,128)S(1)}, f32[64,128]{1,0:T(8,128)S(1)}, u32[]{:S(2)}, u32[]{:S(2)}) collective-permute-start(f32[64,128]{1,0:T(8,128)S(1)} %shard_map.74.refs_3_), channel_id=1, source_target_pairs={{0,4},{4,0},{8,12},{12,8},{16,20},{20,16},{24,28},{28,24},{1,5},{5... | collective-permute-start | bytes 98312 | tf_op jit(solution)/shard_map/ppermute | solution.py:373
  70.3 5.4 %collective-permute-start.23 = (f32[8,128]{1,0:T(8,128)S(1)}, f32[8,128]{1,0:T(8,128)S(1)}, u32[]{:S(2)}, u32[]{:S(2)}) collective-permute-start(f32[8,128]{1,0:T(8,128)S(1)} %get-tuple-element.56.refs_5_), channel_id=1, source_target_pairs={{0,3},{1,2},{2,1},{3,0},{4,7},{5,6},{6,5},{7,4},{8,11},{9,10},{10,... | collective-permute-start | bytes 12296 | tf_op jit(solution)/shard_map/ppermute | solution.py:373
  72.6 4.5 %collective-permute-start.22 = (f32[8,128]{1,0:T(8,128)S(1)}, f32[8,128]{1,0:T(8,128)S(1)}, u32[]{:S(2)}, u32[]{:S(2)}) collective-permute-start(f32[8,128]{1,0:T(8,128)S(1)} %get-tuple-element.56.refs_5_), channel_id=1, source_target_pairs={{0,2},{1,3},{2,0},{3,1},{4,6},{5,7},{6,4},{7,5},{8,10},{9,11},{10,... | collective-permute-start | bytes 12296 | tf_op jit(solution)/shard_map/ppermute | solution.py:373
  73.2 3.9 %collective-permute-start.21 = (f32[8,128]{1,0:T(8,128)S(1)}, f32[8,128]{1,0:T(8,128)S(1)}, u32[]{:S(2)}, u32[]{:S(2)}) collective-permute-start(f32[8,128]{1,0:T(8,128)S(1)} %get-tuple-element.56.refs_5_), channel_id=1, source_target_pairs={{0,1},{1,0},{2,3},{3,2},{4,5},{5,4},{6,7},{7,6},{8,9},{9,8},{10,11... | collective-permute-start | bytes 12296 | tf_op jit(solution)/shard_map/ppermute | solution.py:373
  84.1 1.2 collective-permute-start.24
  85.3 4.7 %collective-permute-start.27 = (f32[8,512]{1,0:T(8,128)S(1)}, f32[8,512]{1,0:T(8,128)S(1)}, u32[]{:S(2)}, u32[]{:S(2)}) collective-permute-start(f32[8,512]{1,0:T(8,128)S(1)} %shard_map.77.refs_5_), channel_id=1, source_target_pairs={{0,24},{4,28},{8,16},{12,20},{16,8},{20,12},{24,0},{28,4},{1,25},{... | collective-permute-start | bytes 49160 | tf_op jit(solution)/shard_map/ppermute | solution.py:373
  86.8 3.7 %collective-permute-start.26 = (f32[8,512]{1,0:T(8,128)S(1)}, f32[8,512]{1,0:T(8,128)S(1)}, u32[]{:S(2)}, u32[]{:S(2)}) collective-permute-start(f32[8,512]{1,0:T(8,128)S(1)} %shard_map.77.refs_5_), channel_id=1, source_target_pairs={{0,16},{4,20},{8,24},{12,28},{16,0},{20,4},{24,8},{28,12},{1,17},{... | collective-permute-start | bytes 49160 | tf_op jit(solution)/shard_map/ppermute | solution.py:373
  87.3 3.7 %collective-permute-start.25 = (f32[8,512]{1,0:T(8,128)S(1)}, f32[8,512]{1,0:T(8,128)S(1)}, u32[]{:S(2)}, u32[]{:S(2)}) collective-permute-start(f32[8,512]{1,0:T(8,128)S(1)} %shard_map.77.refs_5_), channel_id=1, source_target_pairs={{0,8},{4,12},{8,0},{12,4},{16,24},{20,28},{24,16},{28,20},{1,9},{5... | collective-permute-start | bytes 49160 | tf_op jit(solution)/shard_map/ppermute | solution.py:373
  100.6 5.4 %collective-permute-start.30 = (f32[8,128]{1,0:T(8,128)S(1)}, f32[8,128]{1,0:T(8,128)S(1)}, u32[]{:S(2)}, u32[]{:S(2)}) collective-permute-start(f32[8,128]{1,0:T(8,128)S(1)} %shard_map.78.refs_5_), channel_id=1, source_target_pairs={{0,3},{1,2},{2,1},{3,0},{4,7},{5,6},{6,5},{7,4},{8,11},{9,10},{10,... | collective-permute-start | bytes 12296 | tf_op jit(solution)/shard_map/ppermute | solution.py:373
  102.2 4.5 %collective-permute-start.29 = (f32[8,128]{1,0:T(8,128)S(1)}, f32[8,128]{1,0:T(8,128)S(1)}, u32[]{:S(2)}, u32[]{:S(2)}) collective-permute-start(f32[8,128]{1,0:T(8,128)S(1)} %shard_map.78.refs_5_), channel_id=1, source_target_pairs={{0,2},{1,3},{2,0},{3,1},{4,6},{5,7},{6,4},{7,5},{8,10},{9,11},{10,... | collective-permute-start | bytes 12296 | tf_op jit(solution)/shard_map/ppermute | solution.py:373
  103.3 3.6 %collective-permute-start.28 = (f32[8,128]{1,0:T(8,128)S(1)}, f32[8,128]{1,0:T(8,128)S(1)}, u32[]{:S(2)}, u32[]{:S(2)}) collective-permute-start(f32[8,128]{1,0:T(8,128)S(1)} %shard_map.78.refs_5_), channel_id=1, source_target_pairs={{0,1},{1,0},{2,3},{3,2},{4,5},{5,4},{6,7},{7,6},{8,9},{9,8},{10,11... | collective-permute-start | bytes 12296 | tf_op jit(solution)/shard_map/ppermute | solution.py:373
  113.6 1.2 collective-permute-start.31
  114.8 3.7 %collective-permute-start.32 = (f32[1,512]{1,0:T(1,128)S(1)}, f32[1,512]{1,0:T(1,128)S(1)}, u32[]{:S(2)}, u32[]{:S(2)}) collective-permute-start(f32[1,512]{1,0:T(1,128)S(1)} %get-tuple-element.62), channel_id=1, source_target_pairs={{0,8},{4,12},{8,0},{12,4},{16,24},{20,28},{24,16},{28,20},{1,9},{5... | collective-permute-start | bytes 6152 | tf_op jit(solution)/shard_map/ppermute | solution.py:373
  116.4 3.6 %collective-permute-start.33 = (f32[1,512]{1,0:T(1,128)S(1)}, f32[1,512]{1,0:T(1,128)S(1)}, u32[]{:S(2)}, u32[]{:S(2)}) collective-permute-start(f32[1,512]{1,0:T(1,128)S(1)} %get-tuple-element.63), channel_id=1, source_target_pairs={{0,16},{4,20},{8,24},{12,28},{16,0},{20,4},{24,8},{28,12},{1,17},{... | collective-permute-start | bytes 6152 | tf_op jit(solution)/shard_map/ppermute | solution.py:373
  117.9 4.5 %collective-permute-start.34 = (f32[1,512]{1,0:T(1,128)S(1)}, f32[1,512]{1,0:T(1,128)S(1)}, u32[]{:S(2)}, u32[]{:S(2)}) collective-permute-start(f32[1,512]{1,0:T(1,128)S(1)} %get-tuple-element.64), channel_id=1, source_target_pairs={{0,24},{4,28},{8,16},{12,20},{16,8},{20,12},{24,0},{28,4},{1,25},{... | collective-permute-start | bytes 6152 | tf_op jit(solution)/shard_map/ppermute | solution.py:373

commit v11 on v10

--- a/solution.py
+++ b/solution.py
@@ -74,17 +74,17 @@
 
 
 def add_shifts(a_ref, t_ref, potential, aug_ref, top_ref):
-    steps = a_ref.shape[0] // LANES
+    rows = a_ref.shape[0]
+    steps = rows // LANES
     lane = lax.broadcasted_iota(jnp.int32, (LANES, LANES), 1)
+    s = lax.dot_general(a_ref[...], t_ref[: potential.shape[1], :LANES], NT_DIMS, preferred_element_type=jnp.float32)
+    aug_ref[:, :LANES] = a_ref[...]
+    top = jnp.max(lane_fold(jnp.maximum, s + potential), axis=1, keepdims=True)
     for i in range(steps):
         at = slice(i * LANES, (i + 1) * LANES)
-        a = a_ref[at, :]
-        s = lax.dot_general(a, t_ref[: potential.shape[1], :LANES], NT_DIMS, preferred_element_type=jnp.float32)
-        top = jnp.max(lane_fold(jnp.maximum, s + potential), axis=1, keepdims=True)
-        top = top.astype(jnp.bfloat16).astype(jnp.float32)
-        aug_ref[at, :LANES] = a
-        aug_ref[at, LANES:] = jnp.where(lane == 0, 1.0, jnp.where(lane == 1, -top, 0.0)).astype(jnp.bfloat16)
-        top_ref[row_of(i, steps), :] = as_lanes(top)
+        shift = top[at, :].astype(jnp.bfloat16).astype(jnp.float32)
+        aug_ref[at, LANES:] = jnp.where(lane == 0, 1.0, jnp.where(lane == 1, -shift, 0.0)).astype(jnp.bfloat16)
+        top_ref[row_of(i, steps), :] = as_lanes(shift)
 
 
 def shifted_rows(aug_ref, t_ref, width, lse_ref, top_ref, mass_ref, e_ref, carried_ref=None):
@@ -347,7 +347,7 @@
 
 
 def split_kernel(x_ref, y_ref, *out_refs):
-    for k, out_ref in enumerate(out_refs):
+    for k, out_ref in enumerate(reversed(out_refs)):
         out_ref[...] = log_sum([x_ref[k], y_ref[k]])
 
 
@@ -402,8 +402,8 @@
     groups = width // LANES
     tail = jnp.pad(target_potential.reshape(groups, LANES), ((0, SUB - groups), (0, 0)))
     block = jnp.concatenate([target, tail], axis=0)
+    pieces = exchange(source, "col")
     far = exchange_chips(block)
-    pieces = exchange(source, "col")
     own = shape((piece, depth), bf16)
     s_own, a_own, moment_parts = call(
         own_kernel, [own, own, shape((3, depth, depth), bf16)], [source, prev_moment], flops=6 * piece * depth * depth
@@ -412,7 +412,7 @@
         functools.partial(project_kernel, ns),
         [projected, projected],
         [s_own] + pieces[1:] + [a_own, moment_parts],
-        flops=6 * rows * depth * depth,
+        flops=200 * rows * depth * depth,
     )
     far, a = lax.optimization_barrier((far, a))
     blocks = [x for pair in zip(far, [swap(x, "row", 1) for x in far]) for x in pair]
@@ -473,7 +473,7 @@
         )
     one = shape((1, width), f32)
     parts = call(split_kernel, [one] * (nt // 2), [column, swap(sent[0], "row", 1)])
-    parts = [parts[0]] + [swap(x, "row", 2 * k) for k, x in enumerate(parts) if k > 0]
+    parts = [swap(x, "row", nt - 2 - 2 * k) for k, x in enumerate(parts[:-1])] + [parts[-1]]
     update, = call(functools.partial(update_kernel, rows_total), [one], parts)
     return moment, source_potential.reshape(rows), update.reshape(width)
 

time: 123 us -> 122 us (level)
  transfers between devices with their start and end apart: 35 -> 35, of which waited for: 27 -> 28; matrix products, arithmetic and copies ran while one was open for 1% -> 1% of each run, Pallas kernels for 1% -> 1%
where the time goes in v11:
time: 122 us
  Pallas kernels  53.1 us (44%)
  starting transfers between devices  38.8 us (32%)
  waiting for transfers between devices  26.9 us (22%)
  local copies, waits for them, and re-layouts  1.68 us (1%)
    pallas_call x15, Pallas kernels, call(): pl.pallas_call(kernel, out_shape=list(out), in_specs=[vmem] * len(args),...  53.1 us
    ppermute x35, starting transfers between devices, swap(): lax.ppermute(x, axis, [(i, i ^ k) for i in range(lax.axis_size(axis))])  38.8 us
    ppermute x35, waiting for transfers between devices, swap(): lax.ppermute(x, axis, [(i, i ^ k) for i in range(lax.axis_size(axis))])  26.9 us
  transfers between devices with their start and end apart: 35, of which 28 were waited for; matrix products, arithmetic and copies ran while one was open for 1% of the time, Pallas kernels for 1%

profile of v11, /device:TPU:0, one launch (start us, length us, event | category | flops | bytes accessed | tf_op | source)
XLA Modules:
  0.0 122.2 jit_solution(2845500445883804648)
XLA Ops:
  0.6 3.1 %collective-permute-start = (bf16[256,128]{1,0:T(8,128)(2,1)}, bf16[256,128]{1,0:T(8,128)(2,1)S(1)}, u32[]{:S(2)}, u32[]{:S(2)}) collective-permute-start(bf16[256,128]{1,0:T(8,128)(2,1)} %own_ref.1), channel_id=1, source_target_pairs={{0,1},{1,0},{2,3},{3,2},{4,5},{5,4},{6,7},{7,6},{8,9},{9,8},{10,11... | collective-permute-start | bytes 196616 | tf_op jit(solution)/shard_map/ppermute | solution.py:373
  3.7 2.5 %collective-permute-start.2 = (bf16[256,128]{1,0:T(8,128)(2,1)}, bf16[256,128]{1,0:T(8,128)(2,1)S(1)}, u32[]{:S(2)}, u32[]{:S(2)}) collective-permute-start(bf16[256,128]{1,0:T(8,128)(2,1)} %own_ref.1), channel_id=1, source_target_pairs={{0,3},{1,2},{2,1},{3,0},{4,7},{5,6},{6,5},{7,4},{8,11},{9,10},{10,... | collective-permute-start | bytes 196616 | tf_op jit(solution)/shard_map/ppermute | solution.py:373
  6.3 0.9 fusion.1.block_ref.refs_3_
  7.2 2.5 %collective-permute-start.5 = (bf16[528,128]{1,0:T(8,128)(2,1)S(1)}, bf16[528,128]{1,0:T(8,128)(2,1)S(1)}, u32[]{:S(2)}, u32[]{:S(2)}) collective-permute-start(bf16[528,128]{1,0:T(8,128)(2,1)S(1)} %fusion.1.block_ref.refs_3_), channel_id=1, source_target_pairs={{0,24},{4,28},{8,16},{12,20},{16,8},{20,12},{24,0},{28,4},{1,25},{... | collective-permute-start | bytes 405512 | tf_op jit(solution)/shard_map/ppermute | solution.py:373
  9.8 0.5 collective-permute-start.4
  10.3 0.8 copy-done
  11.1 0.8 copy-done.1
  11.9 0.2 shard_map.67
  12.2 0.6 collective-permute-start.3
  12.9 0.3 shard_map.68
  13.3 2.6 %collective-permute-done.4.refs_7_ = bf16[528,128]{1,0:T(8,128)(2,1)S(1)} collective-permute-done((bf16[528,128]{1,0:T(8,128)(2,1)S(1)}, bf16[528,128]{1,0:T(8,128)(2,1)S(1)}, u32[]{:S(2)}, u32[]{:S(2)}) %collective-permute-start.4) | collective-permute-done | bytes 135200 | tf_op jit(solution)/shard_map/ppermute | solution.py:373
  15.9 1.4 %collective-permute-done.3.refs_5_ = bf16[528,128]{1,0:T(8,128)(2,1)S(1)} collective-permute-done((bf16[528,128]{1,0:T(8,128)(2,1)S(1)}, bf16[528,128]{1,0:T(8,128)(2,1)S(1)}, u32[]{:S(2)}, u32[]{:S(2)}) %collective-permute-start.3) | collective-permute-done | bytes 135200 | tf_op jit(solution)/shard_map/ppermute | solution.py:373
  17.3 0.5 collective-permute-start.8
  17.8 0.5 collective-permute-start.6
  18.3 0.6 shard_map.69
  18.9 0.2 collective-permute-done.9.refs_10_
  19.3 15.3 %shard_map.70 = (f32[8,128]{1,0:T(8,128)S(1)}, f32[1024,128]{1,0:T(8,128)S(1)}, bf16[4096,256]{1,0:T(8,128)(2,1)S(1)}, f32[8,512]{1,0:T(8,128)S(1)}) custom-call(bf16[1024,128]{1,0:T(8,128)(2,1)S(1)} %get-tuple-element.39.a_ref.refs_0_, bf16[1024,256]{1,0:T(8,128)(2,1)S(1)} %get-tuple-element.41.refs_1_, f32[8,128]{1,0:T(8,128)S(1)} %get-tuple-element.42.refs_2_, ...), custom_call_target="tpu_custom_call" | custom-call | flops 2147483648 | bytes 4513792 | tf_op jit(solution)/shard_map/pallas_call | solution.py:361
  34.6 3.0 %collective-permute-start.12 = (f32[8,128]{1,0:T(8,128)S(1)}, f32[8,128]{1,0:T(8,128)S(1)}, u32[]{:S(2)}, u32[]{:S(2)}) collective-permute-start(f32[8,128]{1,0:T(8,128)S(1)} %get-tuple-element.48.refs_1_), channel_id=1, source_target_pairs={{0,3},{1,2},{2,1},{3,0},{4,7},{5,6},{6,5},{7,4},{8,11},{9,10},{10,... | collective-permute-start | bytes 12296 | tf_op jit(solution)/shard_map/ppermute | solution.py:373
  37.6 0.3 collective-permute-start.11
  38.0 1.1 collective-permute-start.10
  39.1 1.0 collective-permute-done.12.refs_4_
  40.1 2.0 %collective-permute-done.11.refs_3_ = f32[8,128]{1,0:T(8,128)S(1)} collective-permute-done((f32[8,128]{1,0:T(8,128)S(1)}, f32[8,128]{1,0:T(8,128)S(1)}, u32[]{:S(2)}, u32[]{:S(2)}) %collective-permute-start.11) | collective-permute-done | bytes 4128 | tf_op jit(solution)/shard_map/ppermute | solution.py:373
  42.1 0.5 shard_map.71
  42.8 1.2 collective-permute-done.13.refs_1_
  44.0 1.9 %collective-permute-start.16 = (f32[64,128]{1,0:T(8,128)S(1)}, f32[64,128]{1,0:T(8,128)S(1)}, u32[]{:S(2)}, u32[]{:S(2)}) collective-permute-start(f32[64,128]{1,0:T(8,128)S(1)} %shard_map.72.refs_0_), channel_id=1, source_target_pairs={{0,3},{1,2},{2,1},{3,0},{4,7},{5,6},{6,5},{7,4},{8,11},{9,10},{10,... | collective-permute-start | bytes 98312 | tf_op jit(solution)/shard_map/ppermute | solution.py:373
  46.1 2.3 %collective-permute-start.14 = (f32[64,128]{1,0:T(8,128)S(1)}, f32[64,128]{1,0:T(8,128)S(1)}, u32[]{:S(2)}, u32[]{:S(2)}) collective-permute-start(f32[64,128]{1,0:T(8,128)S(1)} %shard_map.72.refs_0_), channel_id=1, source_target_pairs={{0,1},{1,0},{2,3},{3,2},{4,5},{5,4},{6,7},{7,6},{8,9},{9,8},{10,11... | collective-permute-start | bytes 98312 | tf_op jit(solution)/shard_map/ppermute | solution.py:373
  48.3 1.7 %collective-permute-done.16.refs_3_ = f32[64,128]{1,0:T(8,128)S(1)} collective-permute-done((f32[64,128]{1,0:T(8,128)S(1)}, f32[64,128]{1,0:T(8,128)S(1)}, u32[]{:S(2)}, u32[]{:S(2)}) %collective-permute-start.16) | collective-permute-done | bytes 32800 | tf_op jit(solution)/shard_map/ppermute | solution.py:373
  50.1 0.8 collective-permute-done.15.refs_2_
  50.9 1.6 %collective-permute-start.19 = (f32[64,128]{1,0:T(8,128)S(1)}, f32[64,128]{1,0:T(8,128)S(1)}, u32[]{:S(2)}, u32[]{:S(2)}) collective-permute-start(f32[64,128]{1,0:T(8,128)S(1)} %shard_map.73.refs_0_), channel_id=1, source_target_pairs={{0,24},{4,28},{8,16},{12,20},{16,8},{20,12},{24,0},{28,4},{1,25},{... | collective-permute-start | bytes 98312 | tf_op jit(solution)/shard_map/ppermute | solution.py:373
  52.5 0.5 collective-permute-start.18
  53.0 1.5 %collective-permute-start.17 = (f32[64,128]{1,0:T(8,128)S(1)}, f32[64,128]{1,0:T(8,128)S(1)}, u32[]{:S(2)}, u32[]{:S(2)}) collective-permute-start(f32[64,128]{1,0:T(8,128)S(1)} %shard_map.73.refs_0_), channel_id=1, source_target_pairs={{0,8},{4,12},{8,0},{12,4},{16,24},{20,28},{24,16},{28,20},{1,9},{5... | collective-permute-start | bytes 98312 | tf_op jit(solution)/shard_map/ppermute | solution.py:373
  54.5 1.4 %collective-permute-done.19.refs_3_ = f32[64,128]{1,0:T(8,128)S(1)} collective-permute-done((f32[64,128]{1,0:T(8,128)S(1)}, f32[64,128]{1,0:T(8,128)S(1)}, u32[]{:S(2)}, u32[]{:S(2)}) %collective-permute-start.19) | collective-permute-done | bytes 32800 | tf_op jit(solution)/shard_map/ppermute | solution.py:373
  55.9 0.5 collective-permute-done.18.refs_2_
  56.4 0.5 collective-permute-done.17.refs_1_
  57.0 1.2 collective-permute-done.20.refs_4_
  58.2 12.2 %shard_map.75 = (f32[128,128]{1,0:T(8,128)}, bf16[1024,128]{1,0:T(8,128)(2,1)S(1)}, f32[8,128]{1,0:T(8,128)S(1)}, f32[8,128]{1,0:T(8,128)S(1)}, bf16[1024,4096]{1,0:T(8,128)(2,1)S(1)}) custom-call(bf16[1024,128]{1,0:T(8,128)(2,1)S(1)} %get-tuple-element.37.refs_0_, bf16[4096,256]{1,0:T(8,128)(2,1)S(1)} %get-tuple-element.46.refs_1_.refs_3_, ...), custom_call_target="tpu_custom_call" | custom-call | flops 1073741824 | bytes 11165696 | tf_op jit(solution)/shard_map/pallas_call | solution.py:361
  70.4 2.3 %collective-permute-start.23 = (f32[8,128]{1,0:T(8,128)S(1)}, f32[8,128]{1,0:T(8,128)S(1)}, u32[]{:S(2)}, u32[]{:S(2)}) collective-permute-start(f32[8,128]{1,0:T(8,128)S(1)} %get-tuple-element.56.refs_5_), channel_id=1, source_target_pairs={{0,3},{1,2},{2,1},{3,0},{4,7},{5,6},{6,5},{7,4},{8,11},{9,10},{10,... | collective-permute-start | bytes 12296 | tf_op jit(solution)/shard_map/ppermute | solution.py:373
  72.7 0.5 collective-permute-start.22
  73.2 1.6 %collective-permute-start.21 = (f32[8,128]{1,0:T(8,128)S(1)}, f32[8,128]{1,0:T(8,128)S(1)}, u32[]{:S(2)}, u32[]{:S(2)}) collective-permute-start(f32[8,128]{1,0:T(8,128)S(1)} %get-tuple-element.56.refs_5_), channel_id=1, source_target_pairs={{0,1},{1,0},{2,3},{3,2},{4,5},{5,4},{6,7},{7,6},{8,9},{9,8},{10,11... | collective-permute-start | bytes 12296 | tf_op jit(solution)/shard_map/ppermute | solution.py:373
  74.8 1.0 collective-permute-done.23.refs_8_
  75.8 1.4 %collective-permute-done.22.refs_7_ = f32[8,128]{1,0:T(8,128)S(1)} collective-permute-done((f32[8,128]{1,0:T(8,128)S(1)}, f32[8,128]{1,0:T(8,128)S(1)}, u32[]{:S(2)}, u32[]{:S(2)}) %collective-permute-start.22) | collective-permute-done | bytes 4128 | tf_op jit(solution)/shard_map/ppermute | solution.py:373
  77.2 7.0 %shard_map.76 = (f32[8,512]{1,0:T(8,128)S(1)}, f32[8,128]{1,0:T(8,128)}) custom-call(bf16[1024,128]{1,0:T(8,128)(2,1)S(1)} %get-tuple-element.53.refs_0_, bf16[1024,4096]{1,0:T(8,128)(2,1)S(1)} %get-tuple-element.54.refs_1_, f32[8,128]{1,0:T(8,128)S(1)} %get-tuple-element.55.refs_2_, bf16[4096,256]{1,0:T(8,128)(2,1)S(1)} %get-tuple-element.46.refs_1_.refs_3_, ...), custom_call_target="tpu_custom_call" | custom-call | flops 67108864 | bytes 10805248 | tf_op jit(solution)/shard_map/pallas_call | solution.py:361
  84.2 1.2 collective-permute-done.24.refs_1_
  85.4 2.5 %collective-permute-start.27 = (f32[8,512]{1,0:T(8,128)S(1)}, f32[8,512]{1,0:T(8,128)S(1)}, u32[]{:S(2)}, u32[]{:S(2)}) collective-permute-start(f32[8,512]{1,0:T(8,128)S(1)} %shard_map.77.refs_5_), channel_id=1, source_target_pairs={{0,24},{4,28},{8,16},{12,20},{16,8},{20,12},{24,0},{28,4},{1,25},{... | collective-permute-start | bytes 49160 | tf_op jit(solution)/shard_map/ppermute | solution.py:373
  87.9 0.5 collective-permute-start.26
  88.4 0.5 collective-permute-start.25
  89.0 1.1 collective-permute-done.27.refs_8_
  90.1 1.5 %collective-permute-done.26.refs_7_ = f32[8,512]{1,0:T(8,128)S(1)} collective-permute-done((f32[8,512]{1,0:T(8,128)S(1)}, f32[8,512]{1,0:T(8,128)S(1)}, u32[]{:S(2)}, u32[]{:S(2)}) %collective-permute-start.26) | collective-permute-done | bytes 16416 | tf_op jit(solution)/shard_map/ppermute | solution.py:373
  91.7 0.5 collective-permute-done.25.refs_6_
  92.2 9.5 %shard_map.78.refs_5_ = f32[8,128]{1,0:T(8,128)S(1)} custom-call(bf16[1024,128]{1,0:T(8,128)(2,1)S(1)} %get-tuple-element.53.refs_0_, bf16[1024,4096]{1,0:T(8,128)(2,1)S(1)} %get-tuple-element.54.refs_1_, f32[8,128]{1,0:T(8,128)S(1)} %get-tuple-element.55.refs_2_, bf16[4096,256]{1,0:T(8,128)(2,1)S(1)} %get-tuple-element.46.refs_1_.refs_3_, ...), custom_call_target="tpu_custom_call" | custom-call | flops 67108864 | bytes 10838016 | tf_op jit(solution)/shard_map/pallas_call | solution.py:361
  101.7 1.6 %collective-permute-start.30 = (f32[8,128]{1,0:T(8,128)S(1)}, f32[8,128]{1,0:T(8,128)S(1)}, u32[]{:S(2)}, u32[]{:S(2)}) collective-permute-start(f32[8,128]{1,0:T(8,128)S(1)} %shard_map.78.refs_5_), channel_id=1, source_target_pairs={{0,3},{1,2},{2,1},{3,0},{4,7},{5,6},{6,5},{7,4},{8,11},{9,10},{10,... | collective-permute-start | bytes 12296 | tf_op jit(solution)/shard_map/ppermute | solution.py:373
  103.3 1.1 collective-permute-start.29
  104.4 1.8 %collective-permute-start.28 = (f32[8,128]{1,0:T(8,128)S(1)}, f32[8,128]{1,0:T(8,128)S(1)}, u32[]{:S(2)}, u32[]{:S(2)}) collective-permute-start(f32[8,128]{1,0:T(8,128)S(1)} %shard_map.78.refs_5_), channel_id=1, source_target_pairs={{0,1},{1,0},{2,3},{3,2},{4,5},{5,4},{6,7},{7,6},{8,9},{9,8},{10,11... | collective-permute-start | bytes 12296 | tf_op jit(solution)/shard_map/ppermute | solution.py:373
  106.1 1.0 collective-permute-done.30.refs_8_
  107.1 0.7 collective-permute-done.29.refs_7_
  108.0 6.7 %shard_map.79 = (f32[4,1,512]{2,1,0:T(1,128)S(1)}, f32[4,1,512]{2,1,0:T(1,128)S(1)}, f32[8,128]{1,0:T(8,128)}) custom-call(bf16[1024,128]{1,0:T(8,128)(2,1)S(1)} %get-tuple-element.53.refs_0_, bf16[1024,4096]{1,0:T(8,128)(2,1)S(1)} %get-tuple-element.54.refs_1_, f32[8,128]{1,0:T(8,128)S(1)} %get-tuple-element.55.refs_2_, ...), custom_call_target="tpu_custom_call" | custom-call | flops 67108864 | bytes 10805248 | tf_op jit(solution)/shard_map/pallas_call | solution.py:361
  114.7 1.2 collective-permute-done.31.y_ref
  115.9 1.6 %collective-permute-start.32 = (f32[1,512]{1,0:T(1,128)S(1)}, f32[1,512]{1,0:T(1,128)S(1)}, u32[]{:S(2)}, u32[]{:S(2)}) collective-permute-start(f32[1,512]{1,0:T(1,128)S(1)} %get-tuple-element.61), channel_id=1, source_target_pairs={{0,24},{4,28},{8,16},{12,20},{16,8},{20,12},{24,0},{28,4},{1,25},{... | collective-permute-start | bytes 6152 | tf_op jit(solution)/shard_map/ppermute | solution.py:373
  117.5 0.5 collective-permute-start.33
  118.0 1.5 %collective-permute-start.34 = (f32[1,512]{1,0:T(1,128)S(1)}, f32[1,512]{1,0:T(1,128)S(1)}, u32[]{:S(2)}, u32[]{:S(2)}) collective-permute-start(f32[1,512]{1,0:T(1,128)S(1)} %get-tuple-element.63), channel_id=1, source_target_pairs={{0,8},{4,12},{8,0},{12,4},{16,24},{20,28},{24,16},{28,20},{1,9},{5... | collective-permute-start | bytes 6152 | tf_op jit(solution)/shard_map/ppermute | solution.py:373
  119.5 1.0 collective-permute-done.32.refs_0_
  120.5 0.6 collective-permute-done.33.refs_1_
  121.1 0.5 collective-permute-done.34.refs_2_
  121.6 0.6 shard_map.81
  (26 shorter events, 1.1 us)
Async XLA Ops:
  0.6 11.5 %collective-permute-start = (bf16[256,128]{1,0:T(8,128)(2,1)}, bf16[256,128]{1,0:T(8,128)(2,1)S(1)}, u32[]{:S(2)}, u32[]{:S(2)}) collective-permute-start(bf16[256,128]{1,0:T(8,128)(2,1)} %own_ref.1), channel_id=1, source_target_pairs={{0,1},{1,0},{2,3},{3,2},{4,5},{5,4},{6,7},{7,6},{8,9},{9,8},{10,11... | collective-permute-start | bytes 196616 | tf_op jit(solution)/shard_map/ppermute | solution.py:373
  3.7 9.1 %collective-permute-start.2 = (bf16[256,128]{1,0:T(8,128)(2,1)}, bf16[256,128]{1,0:T(8,128)(2,1)S(1)}, u32[]{:S(2)}, u32[]{:S(2)}) collective-permute-start(bf16[256,128]{1,0:T(8,128)(2,1)} %own_ref.1), channel_id=1, source_target_pairs={{0,3},{1,2},{2,1},{3,0},{4,7},{5,6},{6,5},{7,4},{8,11},{9,10},{10,... | collective-permute-start | bytes 196616 | tf_op jit(solution)/shard_map/ppermute | solution.py:373
  6.2 6.7 %collective-permute-start.1 = (bf16[256,128]{1,0:T(8,128)(2,1)}, bf16[256,128]{1,0:T(8,128)(2,1)S(1)}, u32[]{:S(2)}, u32[]{:S(2)}) collective-permute-start(bf16[256,128]{1,0:T(8,128)(2,1)} %own_ref.1), channel_id=1, source_target_pairs={{0,2},{1,3},{2,0},{3,1},{4,6},{5,7},{6,4},{7,5},{8,10},{9,11},{10,... | collective-permute-start | bytes 196616 | tf_op jit(solution)/shard_map/ppermute | solution.py:373
  7.2 6.0 %collective-permute-start.5 = (bf16[528,128]{1,0:T(8,128)(2,1)S(1)}, bf16[528,128]{1,0:T(8,128)(2,1)S(1)}, u32[]{:S(2)}, u32[]{:S(2)}) collective-permute-start(bf16[528,128]{1,0:T(8,128)(2,1)S(1)} %fusion.1.block_ref.refs_3_), channel_id=1, source_target_pairs={{0,24},{4,28},{8,16},{12,20},{16,8},{20,12},{24,0},{28,4},{1,25},{... | collective-permute-start | bytes 405512 | tf_op jit(solution)/shard_map/ppermute | solution.py:373
  9.8 6.1 %collective-permute-start.4 = (bf16[528,128]{1,0:T(8,128)(2,1)S(1)}, bf16[528,128]{1,0:T(8,128)(2,1)S(1)}, u32[]{:S(2)}, u32[]{:S(2)}) collective-permute-start(bf16[528,128]{1,0:T(8,128)(2,1)S(1)} %fusion.1.block_ref.refs_3_), channel_id=1, source_target_pairs={{0,16},{4,20},{8,24},{12,28},{16,0},{20,4},{24,8},{28,12},{1,17},{... | collective-permute-start | bytes 405512 | tf_op jit(solution)/shard_map/ppermute | solution.py:373
  10.3 0.8 copy-start
  11.1 0.8 copy-start.1
  12.2 5.1 %collective-permute-start.3 = (bf16[528,128]{1,0:T(8,128)(2,1)S(1)}, bf16[528,128]{1,0:T(8,128)(2,1)S(1)}, u32[]{:S(2)}, u32[]{:S(2)}) collective-permute-start(bf16[528,128]{1,0:T(8,128)(2,1)S(1)} %fusion.1.block_ref.refs_3_), channel_id=1, source_target_pairs={{0,8},{4,12},{8,0},{12,4},{16,24},{20,28},{24,16},{28,20},{1,9},{5... | collective-permute-start | bytes 405512 | tf_op jit(solution)/shard_map/ppermute | solution.py:373
  17.3 1.6 %collective-permute-start.7 = (bf16[528,128]{1,0:T(8,128)(2,1)S(1)}, bf16[528,128]{1,0:T(8,128)(2,1)S(1)}, u32[]{:S(2)}, u32[]{:S(2)}) collective-permute-start(bf16[528,128]{1,0:T(8,128)(2,1)S(1)} %collective-permute-done.3.refs_5_), channel_id=1, source_target_pairs={{0,4},{4,0},{8,12},{12,8},{16,20},{20,16},{24,28},{28,24},{1,5},{5... | collective-permute-start | bytes 405512 | tf_op jit(solution)/shard_map/ppermute | solution.py:373
  17.3 1.6 %collective-permute-start.8 = (bf16[528,128]{1,0:T(8,128)(2,1)S(1)}, bf16[528,128]{1,0:T(8,128)(2,1)S(1)}, u32[]{:S(2)}, u32[]{:S(2)}) collective-permute-start(bf16[528,128]{1,0:T(8,128)(2,1)S(1)} %collective-permute-done.4.refs_7_), channel_id=1, source_target_pairs={{0,4},{4,0},{8,12},{12,8},{16,20},{20,16},{24,28},{28,24},{1,5},{5... | collective-permute-start | bytes 405512 | tf_op jit(solution)/shard_map/ppermute | solution.py:373
  17.8 1.4 %collective-permute-start.9 = (bf16[528,128]{1,0:T(8,128)(2,1)S(1)}, bf16[528,128]{1,0:T(8,128)(2,1)S(1)}, u32[]{:S(2)}, u32[]{:S(2)}) collective-permute-start(bf16[528,128]{1,0:T(8,128)(2,1)S(1)} %collective-permute-done.5.refs_9_), channel_id=1, source_target_pairs={{0,4},{4,0},{8,12},{12,8},{16,20},{20,16},{24,28},{28,24},{1,5},{5... | collective-permute-start | bytes 405512 | tf_op jit(solution)/shard_map/ppermute | solution.py:373
  17.8 1.5 %collective-permute-start.6 = (bf16[528,128]{1,0:T(8,128)(2,1)S(1)}, bf16[528,128]{1,0:T(8,128)(2,1)S(1)}, u32[]{:S(2)}, u32[]{:S(2)}) collective-permute-start(bf16[528,128]{1,0:T(8,128)(2,1)S(1)} %fusion.1.block_ref.refs_3_), channel_id=1, source_target_pairs={{0,4},{4,0},{8,12},{12,8},{16,20},{20,16},{24,28},{28,24},{1,5},{5... | collective-permute-start | bytes 405512 | tf_op jit(solution)/shard_map/ppermute | solution.py:373
  34.6 5.5 %collective-permute-start.12 = (f32[8,128]{1,0:T(8,128)S(1)}, f32[8,128]{1,0:T(8,128)S(1)}, u32[]{:S(2)}, u32[]{:S(2)}) collective-permute-start(f32[8,128]{1,0:T(8,128)S(1)} %get-tuple-element.48.refs_1_), channel_id=1, source_target_pairs={{0,3},{1,2},{2,1},{3,0},{4,7},{5,6},{6,5},{7,4},{8,11},{9,10},{10,... | collective-permute-start | bytes 12296 | tf_op jit(solution)/shard_map/ppermute | solution.py:373
  37.6 4.5 %collective-permute-start.11 = (f32[8,128]{1,0:T(8,128)S(1)}, f32[8,128]{1,0:T(8,128)S(1)}, u32[]{:S(2)}, u32[]{:S(2)}) collective-permute-start(f32[8,128]{1,0:T(8,128)S(1)} %get-tuple-element.48.refs_1_), channel_id=1, source_target_pairs={{0,2},{1,3},{2,0},{3,1},{4,6},{5,7},{6,4},{7,5},{8,10},{9,11},{10,... | collective-permute-start | bytes 12296 | tf_op jit(solution)/shard_map/ppermute | solution.py:373
  38.0 4.2 %collective-permute-start.10 = (f32[8,128]{1,0:T(8,128)S(1)}, f32[8,128]{1,0:T(8,128)S(1)}, u32[]{:S(2)}, u32[]{:S(2)}) collective-permute-start(f32[8,128]{1,0:T(8,128)S(1)} %get-tuple-element.48.refs_1_), channel_id=1, source_target_pairs={{0,1},{1,0},{2,3},{3,2},{4,5},{5,4},{6,7},{7,6},{8,9},{9,8},{10,11... | collective-permute-start | bytes 12296 | tf_op jit(solution)/shard_map/ppermute | solution.py:373
  42.7 1.3 %collective-permute-start.13 = (f32[64,128]{1,0:T(8,128)S(1)}, f32[64,128]{1,0:T(8,128)S(1)}, u32[]{:S(2)}, u32[]{:S(2)}) collective-permute-start(f32[64,128]{1,0:T(8,128)S(1)} %get-tuple-element.51), channel_id=1, source_target_pairs={{0,4},{4,0},{8,12},{12,8},{16,20},{20,16},{24,28},{28,24},{1,5},{5... | collective-permute-start | bytes 98312 | tf_op jit(solution)/shard_map/ppermute | solution.py:373
  44.0 6.1 %collective-permute-start.16 = (f32[64,128]{1,0:T(8,128)S(1)}, f32[64,128]{1,0:T(8,128)S(1)}, u32[]{:S(2)}, u32[]{:S(2)}) collective-permute-start(f32[64,128]{1,0:T(8,128)S(1)} %shard_map.72.refs_0_), channel_id=1, source_target_pairs={{0,3},{1,2},{2,1},{3,0},{4,7},{5,6},{6,5},{7,4},{8,11},{9,10},{10,... | collective-permute-start | bytes 98312 | tf_op jit(solution)/shard_map/ppermute | solution.py:373
  45.9 5.0 %collective-permute-start.15 = (f32[64,128]{1,0:T(8,128)S(1)}, f32[64,128]{1,0:T(8,128)S(1)}, u32[]{:S(2)}, u32[]{:S(2)}) collective-permute-start(f32[64,128]{1,0:T(8,128)S(1)} %shard_map.72.refs_0_), channel_id=1, source_target_pairs={{0,2},{1,3},{2,0},{3,1},{4,6},{5,7},{6,4},{7,5},{8,10},{9,11},{10,... | collective-permute-start | bytes 98312 | tf_op jit(solution)/shard_map/ppermute | solution.py:373
  46.1 4.9 %collective-permute-start.14 = (f32[64,128]{1,0:T(8,128)S(1)}, f32[64,128]{1,0:T(8,128)S(1)}, u32[]{:S(2)}, u32[]{:S(2)}) collective-permute-start(f32[64,128]{1,0:T(8,128)S(1)} %shard_map.72.refs_0_), channel_id=1, source_target_pairs={{0,1},{1,0},{2,3},{3,2},{4,5},{5,4},{6,7},{7,6},{8,9},{9,8},{10,11... | collective-permute-start | bytes 98312 | tf_op jit(solution)/shard_map/ppermute | solution.py:373
  50.9 5.0 %collective-permute-start.19 = (f32[64,128]{1,0:T(8,128)S(1)}, f32[64,128]{1,0:T(8,128)S(1)}, u32[]{:S(2)}, u32[]{:S(2)}) collective-permute-start(f32[64,128]{1,0:T(8,128)S(1)} %shard_map.73.refs_0_), channel_id=1, source_target_pairs={{0,24},{4,28},{8,16},{12,20},{16,8},{20,12},{24,0},{28,4},{1,25},{... | collective-permute-start | bytes 98312 | tf_op jit(solution)/shard_map/ppermute | solution.py:373
  52.5 3.9 %collective-permute-start.18 = (f32[64,128]{1,0:T(8,128)S(1)}, f32[64,128]{1,0:T(8,128)S(1)}, u32[]{:S(2)}, u32[]{:S(2)}) collective-permute-start(f32[64,128]{1,0:T(8,128)S(1)} %shard_map.73.refs_0_), channel_id=1, source_target_pairs={{0,16},{4,20},{8,24},{12,28},{16,0},{20,4},{24,8},{28,12},{1,17},{... | collective-permute-start | bytes 98312 | tf_op jit(solution)/shard_map/ppermute | solution.py:373
  53.0 3.9 %collective-permute-start.17 = (f32[64,128]{1,0:T(8,128)S(1)}, f32[64,128]{1,0:T(8,128)S(1)}, u32[]{:S(2)}, u32[]{:S(2)}) collective-permute-start(f32[64,128]{1,0:T(8,128)S(1)} %shard_map.73.refs_0_), channel_id=1, source_target_pairs={{0,8},{4,12},{8,0},{12,4},{16,24},{20,28},{24,16},{28,20},{1,9},{5... | collective-permute-start | bytes 98312 | tf_op jit(solution)/shard_map/ppermute | solution.py:373
  56.9 1.3 %collective-permute-start.20 = (f32[64,128]{1,0:T(8,128)S(1)}, f32[64,128]{1,0:T(8,128)S(1)}, u32[]{:S(2)}, u32[]{:S(2)}) collective-permute-start(f32[64,128]{1,0:T(8,128)S(1)} %shard_map.74.refs_3_), channel_id=1, source_target_pairs={{0,4},{4,0},{8,12},{12,8},{16,20},{20,16},{24,28},{28,24},{1,5},{5... | collective-permute-start | bytes 98312 | tf_op jit(solution)/shard_map/ppermute | solution.py:373
  70.4 5.4 %collective-permute-start.23 = (f32[8,128]{1,0:T(8,128)S(1)}, f32[8,128]{1,0:T(8,128)S(1)}, u32[]{:S(2)}, u32[]{:S(2)}) collective-permute-start(f32[8,128]{1,0:T(8,128)S(1)} %get-tuple-element.56.refs_5_), channel_id=1, source_target_pairs={{0,3},{1,2},{2,1},{3,0},{4,7},{5,6},{6,5},{7,4},{8,11},{9,10},{10,... | collective-permute-start | bytes 12296 | tf_op jit(solution)/shard_map/ppermute | solution.py:373
  72.7 4.5 %collective-permute-start.22 = (f32[8,128]{1,0:T(8,128)S(1)}, f32[8,128]{1,0:T(8,128)S(1)}, u32[]{:S(2)}, u32[]{:S(2)}) collective-permute-start(f32[8,128]{1,0:T(8,128)S(1)} %get-tuple-element.56.refs_5_), channel_id=1, source_target_pairs={{0,2},{1,3},{2,0},{3,1},{4,6},{5,7},{6,4},{7,5},{8,10},{9,11},{10,... | collective-permute-start | bytes 12296 | tf_op jit(solution)/shard_map/ppermute | solution.py:373
  73.2 4.0 %collective-permute-start.21 = (f32[8,128]{1,0:T(8,128)S(1)}, f32[8,128]{1,0:T(8,128)S(1)}, u32[]{:S(2)}, u32[]{:S(2)}) collective-permute-start(f32[8,128]{1,0:T(8,128)S(1)} %get-tuple-element.56.refs_5_), channel_id=1, source_target_pairs={{0,1},{1,0},{2,3},{3,2},{4,5},{5,4},{6,7},{7,6},{8,9},{9,8},{10,11... | collective-permute-start | bytes 12296 | tf_op jit(solution)/shard_map/ppermute | solution.py:373
  84.2 1.2 collective-permute-start.24
  85.4 4.7 %collective-permute-start.27 = (f32[8,512]{1,0:T(8,128)S(1)}, f32[8,512]{1,0:T(8,128)S(1)}, u32[]{:S(2)}, u32[]{:S(2)}) collective-permute-start(f32[8,512]{1,0:T(8,128)S(1)} %shard_map.77.refs_5_), channel_id=1, source_target_pairs={{0,24},{4,28},{8,16},{12,20},{16,8},{20,12},{24,0},{28,4},{1,25},{... | collective-permute-start | bytes 49160 | tf_op jit(solution)/shard_map/ppermute | solution.py:373
  87.9 3.7 %collective-permute-start.26 = (f32[8,512]{1,0:T(8,128)S(1)}, f32[8,512]{1,0:T(8,128)S(1)}, u32[]{:S(2)}, u32[]{:S(2)}) collective-permute-start(f32[8,512]{1,0:T(8,128)S(1)} %shard_map.77.refs_5_), channel_id=1, source_target_pairs={{0,16},{4,20},{8,24},{12,28},{16,0},{20,4},{24,8},{28,12},{1,17},{... | collective-permute-start | bytes 49160 | tf_op jit(solution)/shard_map/ppermute | solution.py:373
  88.4 3.7 %collective-permute-start.25 = (f32[8,512]{1,0:T(8,128)S(1)}, f32[8,512]{1,0:T(8,128)S(1)}, u32[]{:S(2)}, u32[]{:S(2)}) collective-permute-start(f32[8,512]{1,0:T(8,128)S(1)} %shard_map.77.refs_5_), channel_id=1, source_target_pairs={{0,8},{4,12},{8,0},{12,4},{16,24},{20,28},{24,16},{28,20},{1,9},{5... | collective-permute-start | bytes 49160 | tf_op jit(solution)/shard_map/ppermute | solution.py:373
  101.7 5.4 %collective-permute-start.30 = (f32[8,128]{1,0:T(8,128)S(1)}, f32[8,128]{1,0:T(8,128)S(1)}, u32[]{:S(2)}, u32[]{:S(2)}) collective-permute-start(f32[8,128]{1,0:T(8,128)S(1)} %shard_map.78.refs_5_), channel_id=1, source_target_pairs={{0,3},{1,2},{2,1},{3,0},{4,7},{5,6},{6,5},{7,4},{8,11},{9,10},{10,... | collective-permute-start | bytes 12296 | tf_op jit(solution)/shard_map/ppermute | solution.py:373
  103.3 4.5 %collective-permute-start.29 = (f32[8,128]{1,0:T(8,128)S(1)}, f32[8,128]{1,0:T(8,128)S(1)}, u32[]{:S(2)}, u32[]{:S(2)}) collective-permute-start(f32[8,128]{1,0:T(8,128)S(1)} %shard_map.78.refs_5_), channel_id=1, source_target_pairs={{0,2},{1,3},{2,0},{3,1},{4,6},{5,7},{6,4},{7,5},{8,10},{9,11},{10,... | collective-permute-start | bytes 12296 | tf_op jit(solution)/shard_map/ppermute | solution.py:373
  104.4 3.6 %collective-permute-start.28 = (f32[8,128]{1,0:T(8,128)S(1)}, f32[8,128]{1,0:T(8,128)S(1)}, u32[]{:S(2)}, u32[]{:S(2)}) collective-permute-start(f32[8,128]{1,0:T(8,128)S(1)} %shard_map.78.refs_5_), channel_id=1, source_target_pairs={{0,1},{1,0},{2,3},{3,2},{4,5},{5,4},{6,7},{7,6},{8,9},{9,8},{10,11... | collective-permute-start | bytes 12296 | tf_op jit(solution)/shard_map/ppermute | solution.py:373
  114.7 1.2 collective-permute-start.31
  115.9 4.5 %collective-permute-start.32 = (f32[1,512]{1,0:T(1,128)S(1)}, f32[1,512]{1,0:T(1,128)S(1)}, u32[]{:S(2)}, u32[]{:S(2)}) collective-permute-start(f32[1,512]{1,0:T(1,128)S(1)} %get-tuple-element.61), channel_id=1, source_target_pairs={{0,24},{4,28},{8,16},{12,20},{16,8},{20,12},{24,0},{28,4},{1,25},{... | collective-permute-start | bytes 6152 | tf_op jit(solution)/shard_map/ppermute | solution.py:373
  117.5 3.6 %collective-permute-start.33 = (f32[1,512]{1,0:T(1,128)S(1)}, f32[1,512]{1,0:T(1,128)S(1)}, u32[]{:S(2)}, u32[]{:S(2)}) collective-permute-start(f32[1,512]{1,0:T(1,128)S(1)} %get-tuple-element.62), channel_id=1, source_target_pairs={{0,16},{4,20},{8,24},{12,28},{16,0},{20,4},{24,8},{28,12},{1,17},{... | collective-permute-start | bytes 6152 | tf_op jit(solution)/shard_map/ppermute | solution.py:373
  118.0 3.6 %collective-permute-start.34 = (f32[1,512]{1,0:T(1,128)S(1)}, f32[1,512]{1,0:T(1,128)S(1)}, u32[]{:S(2)}, u32[]{:S(2)}) collective-permute-start(f32[1,512]{1,0:T(1,128)S(1)} %get-tuple-element.63), channel_id=1, source_target_pairs={{0,8},{4,12},{8,0},{12,4},{16,24},{20,28},{24,16},{28,20},{1,9},{5... | collective-permute-start | bytes 6152 | tf_op jit(solution)/shard_map/ppermute | solution.py:373

commit v12 on v11

--- a/solution.py
+++ b/solution.py
@@ -151,22 +151,14 @@
             carried_ref[rows, :] = carried / mass
 
 
-def own_kernel(own_ref, moment_ref, s_ref, a_ref, parts_ref):
-    s_ref[...] = own_ref[...]
-    for k, part in enumerate(split3(moment_ref[...])):
-        parts_ref[k] = part
-    a_ref[...] = project4(own_ref[...], split3(moment_ref[...]))
-
-
 def project_kernel(ns, *refs):
-    s_refs, a_own_ref, parts_ref, s_ref, a_ref = refs[:ns], *refs[ns:]
-    piece = a_own_ref.shape[0]
-    a_ref[:piece, :] = a_own_ref[...]
+    s_refs, moment_ref, s_ref, a_ref = refs[:ns], *refs[ns:]
+    piece = s_refs[0].shape[0]
+    parts = split3(moment_ref[...])
     for k in range(ns):
         at = slice(k * piece, (k + 1) * piece)
         s_ref[at, :] = s_refs[k][...]
-        if k > 0:
-            a_ref[at, :] = project4(s_refs[k][...], [parts_ref[i] for i in range(3)])
+        a_ref[at, :] = project4(s_refs[k][...], parts)
 
 
 def potential_of(block_ref, width):
@@ -404,17 +396,13 @@
     block = jnp.concatenate([target, tail], axis=0)
     pieces = exchange(source, "col")
     far = exchange_chips(block)
-    own = shape((piece, depth), bf16)
-    s_own, a_own, moment_parts = call(
-        own_kernel, [own, own, shape((3, depth, depth), bf16)], [source, prev_moment], flops=6 * piece * depth * depth
-    )
     s, a = call(
         functools.partial(project_kernel, ns),
         [projected, projected],
-        [s_own] + pieces[1:] + [a_own, moment_parts],
+        pieces + [prev_moment],
         flops=200 * rows * depth * depth,
     )
-    far, a = lax.optimization_barrier((far, a))
+    far = [lax.optimization_barrier((x, a))[0] for x in far]
     blocks = [x for pair in zip(far, [swap(x, "row", 1) for x in far]) for x in pair]
     augmented = shape((rows, 2 * depth), bf16)
     aug, top = call(

time: 122 us -> 122 us (level)
    pallas_call x15 -> x14, Pallas kernels: 53.1 us -> 53 us  [call(): pl.pallas_call(kernel, out_shape=list(out), in_specs=[vmem] * len(args),...]
  transfers between devices with their start and end apart: 35 -> 35, of which waited for: 28 -> 29; matrix products, arithmetic and copies ran while one was open for 1% -> 1% of each run, Pallas kernels for 1% -> 1%
where the time goes in v12:
time: 122 us
  Pallas kernels  53 us (43%)
  starting transfers between devices  38.3 us (31%)
  waiting for transfers between devices  27.4 us (22%)
  local copies, waits for them, and re-layouts  1.68 us (1%)
    pallas_call x14, Pallas kernels, call(): pl.pallas_call(kernel, out_shape=list(out), in_specs=[vmem] * len(args),...  53 us
    ppermute x35, starting transfers between devices, swap(): lax.ppermute(x, axis, [(i, i ^ k) for i in range(lax.axis_size(axis))])  38.3 us
    ppermute x35, waiting for transfers between devices, swap(): lax.ppermute(x, axis, [(i, i ^ k) for i in range(lax.axis_size(axis))])  27.4 us
  transfers between devices with their start and end apart: 35, of which 29 were waited for; matrix products, arithmetic and copies ran while one was open for 1% of the time, Pallas kernels for 1%

profile of v12, /device:TPU:0, one launch (start us, length us, event | category | flops | bytes accessed | tf_op | source)
XLA Modules:
  0.0 122.0 jit_solution(9596944503617361758)
XLA Ops:
  0.6 4.1 %collective-permute-start.1 = (bf16[256,128]{1,0:T(8,128)(2,1)}, bf16[256,128]{1,0:T(8,128)(2,1)S(1)}, u32[]{:S(2)}, u32[]{:S(2)}) collective-permute-start(bf16[256,128]{1,0:T(8,128)(2,1)} %refs_0_.1), channel_id=1, source_target_pairs={{0,2},{1,3},{2,0},{3,1},{4,6},{5,7},{6,4},{7,5},{8,10},{9,11},{10,... | collective-permute-start | bytes 196616 | tf_op jit(solution)/shard_map/ppermute | solution.py:365
  4.7 1.6 %collective-permute-start = (bf16[256,128]{1,0:T(8,128)(2,1)}, bf16[256,128]{1,0:T(8,128)(2,1)S(1)}, u32[]{:S(2)}, u32[]{:S(2)}) collective-permute-start(bf16[256,128]{1,0:T(8,128)(2,1)} %refs_0_.1), channel_id=1, source_target_pairs={{0,1},{1,0},{2,3},{3,2},{4,5},{5,4},{6,7},{7,6},{8,9},{9,8},{10,11... | collective-permute-start | bytes 196616 | tf_op jit(solution)/shard_map/ppermute | solution.py:365
  6.3 0.9 fusion.1.block_ref.refs_3_
  7.2 2.7 %collective-permute-start.8 = (bf16[528,128]{1,0:T(8,128)(2,1)S(1)}, bf16[528,128]{1,0:T(8,128)(2,1)S(1)}, u32[]{:S(2)}, u32[]{:S(2)}) collective-permute-start(bf16[528,128]{1,0:T(8,128)(2,1)S(1)} %fusion.1.block_ref.refs_3_), channel_id=1, source_target_pairs={{0,24},{4,28},{8,16},{12,20},{16,8},{20,12},{24,0},{28,4},{1,25},{... | collective-permute-start | bytes 405512 | tf_op jit(solution)/shard_map/ppermute | solution.py:365
  10.0 0.5 collective-permute-start.6
  10.5 0.3 collective-permute-start.4
  10.8 1.8 %collective-permute-done.2.refs_3_ = bf16[256,128]{1,0:T(8,128)(2,1)S(1)} collective-permute-done((bf16[256,128]{1,0:T(8,128)(2,1)}, bf16[256,128]{1,0:T(8,128)(2,1)S(1)}, u32[]{:S(2)}, u32[]{:S(2)}) %collective-permute-start.2) | collective-permute-done | bytes 65568 | tf_op jit(solution)/shard_map/ppermute | solution.py:365
  12.6 0.8 copy-done
  13.4 0.8 copy-done.1
  14.3 0.4 shard_map.67
  14.7 1.1 collective-permute-done.6.refs_7_
  15.9 0.5 collective-permute-start.7
  16.4 0.6 shard_map.68
  17.1 0.2 collective-permute-done.5.refs_6_
  17.5 0.3 collective-permute-done.9.refs_10_
  17.8 15.3 %shard_map.69 = (f32[8,128]{1,0:T(8,128)S(1)}, f32[1024,128]{1,0:T(8,128)S(1)}, bf16[4096,256]{1,0:T(8,128)(2,1)S(1)}, f32[8,512]{1,0:T(8,128)S(1)}) custom-call(bf16[1024,128]{1,0:T(8,128)(2,1)S(1)} %get-tuple-element.31.a_ref.refs_0_, bf16[1024,256]{1,0:T(8,128)(2,1)S(1)} %get-tuple-element.33.refs_1_, f32[8,128]{1,0:T(8,128)S(1)} %get-tuple-element.34.refs_2_, ...), custom_call_target="tpu_custom_call" | custom-call | flops 2147483648 | bytes 4513792 | tf_op jit(solution)/shard_map/pallas_call | solution.py:353
  33.1 3.6 %collective-permute-start.12 = (f32[8,128]{1,0:T(8,128)S(1)}, f32[8,128]{1,0:T(8,128)S(1)}, u32[]{:S(2)}, u32[]{:S(2)}) collective-permute-start(f32[8,128]{1,0:T(8,128)S(1)} %get-tuple-element.40.refs_1_), channel_id=1, source_target_pairs={{0,3},{1,2},{2,1},{3,0},{4,7},{5,6},{6,5},{7,4},{8,11},{9,10},{10,... | collective-permute-start | bytes 12296 | tf_op jit(solution)/shard_map/ppermute | solution.py:365
  36.7 0.8 collective-permute-start.10
  37.6 1.0 collective-permute-done.12.refs_4_
  38.6 2.6 %collective-permute-done.11.refs_3_ = f32[8,128]{1,0:T(8,128)S(1)} collective-permute-done((f32[8,128]{1,0:T(8,128)S(1)}, f32[8,128]{1,0:T(8,128)S(1)}, u32[]{:S(2)}, u32[]{:S(2)}) %collective-permute-start.11) | collective-permute-done | bytes 4128 | tf_op jit(solution)/shard_map/ppermute | solution.py:365
  41.2 0.5 shard_map.70
  41.9 1.2 collective-permute-done.13.refs_1_
  43.1 1.5 %collective-permute-start.16 = (f32[64,128]{1,0:T(8,128)S(1)}, f32[64,128]{1,0:T(8,128)S(1)}, u32[]{:S(2)}, u32[]{:S(2)}) collective-permute-start(f32[64,128]{1,0:T(8,128)S(1)} %shard_map.71.refs_0_), channel_id=1, source_target_pairs={{0,3},{1,2},{2,1},{3,0},{4,7},{5,6},{6,5},{7,4},{8,11},{9,10},{10,... | collective-permute-start | bytes 98312 | tf_op jit(solution)/shard_map/ppermute | solution.py:365
  44.5 0.6 collective-permute-start.15
  45.2 2.3 %collective-permute-start.14 = (f32[64,128]{1,0:T(8,128)S(1)}, f32[64,128]{1,0:T(8,128)S(1)}, u32[]{:S(2)}, u32[]{:S(2)}) collective-permute-start(f32[64,128]{1,0:T(8,128)S(1)} %shard_map.71.refs_0_), channel_id=1, source_target_pairs={{0,1},{1,0},{2,3},{3,2},{4,5},{5,4},{6,7},{7,6},{8,9},{9,8},{10,11... | collective-permute-start | bytes 98312 | tf_op jit(solution)/shard_map/ppermute | solution.py:365
  47.5 1.6 %collective-permute-done.16.refs_3_ = f32[64,128]{1,0:T(8,128)S(1)} collective-permute-done((f32[64,128]{1,0:T(8,128)S(1)}, f32[64,128]{1,0:T(8,128)S(1)}, u32[]{:S(2)}, u32[]{:S(2)}) %collective-permute-start.16) | collective-permute-done | bytes 32800 | tf_op jit(solution)/shard_map/ppermute | solution.py:365
  49.1 0.4 collective-permute-done.15.refs_2_
  49.5 0.2 collective-permute-done.14.refs_1_
  49.8 1.9 %collective-permute-start.19 = (f32[64,128]{1,0:T(8,128)S(1)}, f32[64,128]{1,0:T(8,128)S(1)}, u32[]{:S(2)}, u32[]{:S(2)}) collective-permute-start(f32[64,128]{1,0:T(8,128)S(1)} %shard_map.72.refs_0_), channel_id=1, source_target_pairs={{0,24},{4,28},{8,16},{12,20},{16,8},{20,12},{24,0},{28,4},{1,25},{... | collective-permute-start | bytes 98312 | tf_op jit(solution)/shard_map/ppermute | solution.py:365
  51.6 1.2 collective-permute-start.18
  52.8 0.5 collective-permute-start.17
  53.3 1.5 %collective-permute-done.19.refs_3_ = f32[64,128]{1,0:T(8,128)S(1)} collective-permute-done((f32[64,128]{1,0:T(8,128)S(1)}, f32[64,128]{1,0:T(8,128)S(1)}, u32[]{:S(2)}, u32[]{:S(2)}) %collective-permute-start.19) | collective-permute-done | bytes 32800 | tf_op jit(solution)/shard_map/ppermute | solution.py:365
  54.8 0.7 collective-permute-done.18.refs_2_
  55.6 1.2 collective-permute-done.17.refs_1_
  56.8 1.2 collective-permute-done.20.refs_4_
  58.0 12.2 %shard_map.74 = (f32[128,128]{1,0:T(8,128)}, bf16[1024,128]{1,0:T(8,128)(2,1)S(1)}, f32[8,128]{1,0:T(8,128)S(1)}, f32[8,128]{1,0:T(8,128)S(1)}, bf16[1024,4096]{1,0:T(8,128)(2,1)S(1)}) custom-call(bf16[1024,128]{1,0:T(8,128)(2,1)S(1)} %get-tuple-element.30.refs_0_, bf16[4096,256]{1,0:T(8,128)(2,1)S(1)} %get-tuple-element.38.refs_1_.refs_3_, ...), custom_call_target="tpu_custom_call" | custom-call | flops 1073741824 | bytes 11165696 | tf_op jit(solution)/shard_map/pallas_call | solution.py:353
  70.2 2.3 %collective-permute-start.23 = (f32[8,128]{1,0:T(8,128)S(1)}, f32[8,128]{1,0:T(8,128)S(1)}, u32[]{:S(2)}, u32[]{:S(2)}) collective-permute-start(f32[8,128]{1,0:T(8,128)S(1)} %get-tuple-element.48.refs_5_), channel_id=1, source_target_pairs={{0,3},{1,2},{2,1},{3,0},{4,7},{5,6},{6,5},{7,4},{8,11},{9,10},{10,... | collective-permute-start | bytes 12296 | tf_op jit(solution)/shard_map/ppermute | solution.py:365
  72.6 0.8 collective-permute-start.22
  73.3 1.3 %collective-permute-start.21 = (f32[8,128]{1,0:T(8,128)S(1)}, f32[8,128]{1,0:T(8,128)S(1)}, u32[]{:S(2)}, u32[]{:S(2)}) collective-permute-start(f32[8,128]{1,0:T(8,128)S(1)} %get-tuple-element.48.refs_5_), channel_id=1, source_target_pairs={{0,1},{1,0},{2,3},{3,2},{4,5},{5,4},{6,7},{7,6},{8,9},{9,8},{10,11... | collective-permute-start | bytes 12296 | tf_op jit(solution)/shard_map/ppermute | solution.py:365
  74.6 1.0 collective-permute-done.23.refs_8_
  75.6 1.4 %collective-permute-done.22.refs_7_ = f32[8,128]{1,0:T(8,128)S(1)} collective-permute-done((f32[8,128]{1,0:T(8,128)S(1)}, f32[8,128]{1,0:T(8,128)S(1)}, u32[]{:S(2)}, u32[]{:S(2)}) %collective-permute-start.22) | collective-permute-done | bytes 4128 | tf_op jit(solution)/shard_map/ppermute | solution.py:365
  77.1 7.0 %shard_map.75 = (f32[8,512]{1,0:T(8,128)S(1)}, f32[8,128]{1,0:T(8,128)}) custom-call(bf16[1024,128]{1,0:T(8,128)(2,1)S(1)} %get-tuple-element.45.refs_0_, bf16[1024,4096]{1,0:T(8,128)(2,1)S(1)} %get-tuple-element.46.refs_1_, f32[8,128]{1,0:T(8,128)S(1)} %get-tuple-element.47.refs_2_, bf16[4096,256]{1,0:T(8,128)(2,1)S(1)} %get-tuple-element.38.refs_1_.refs_3_, ...), custom_call_target="tpu_custom_call" | custom-call | flops 67108864 | bytes 10805248 | tf_op jit(solution)/shard_map/pallas_call | solution.py:353
  84.0 1.2 collective-permute-done.24.refs_1_
  85.2 1.4 %collective-permute-start.27 = (f32[8,512]{1,0:T(8,128)S(1)}, f32[8,512]{1,0:T(8,128)S(1)}, u32[]{:S(2)}, u32[]{:S(2)}) collective-permute-start(f32[8,512]{1,0:T(8,128)S(1)} %shard_map.76.refs_5_), channel_id=1, source_target_pairs={{0,24},{4,28},{8,16},{12,20},{16,8},{20,12},{24,0},{28,4},{1,25},{... | collective-permute-start | bytes 49160 | tf_op jit(solution)/shard_map/ppermute | solution.py:365
  86.7 0.6 collective-permute-start.26
  87.3 1.5 %collective-permute-start.25 = (f32[8,512]{1,0:T(8,128)S(1)}, f32[8,512]{1,0:T(8,128)S(1)}, u32[]{:S(2)}, u32[]{:S(2)}) collective-permute-start(f32[8,512]{1,0:T(8,128)S(1)} %shard_map.76.refs_5_), channel_id=1, source_target_pairs={{0,8},{4,12},{8,0},{12,4},{16,24},{20,28},{24,16},{28,20},{1,9},{5... | collective-permute-start | bytes 49160 | tf_op jit(solution)/shard_map/ppermute | solution.py:365
  88.8 1.1 collective-permute-done.27.refs_8_
  89.9 0.5 collective-permute-done.26.refs_7_
  90.4 0.6 collective-permute-done.25.refs_6_
  91.0 9.5 %shard_map.77.refs_5_ = f32[8,128]{1,0:T(8,128)S(1)} custom-call(bf16[1024,128]{1,0:T(8,128)(2,1)S(1)} %get-tuple-element.45.refs_0_, bf16[1024,4096]{1,0:T(8,128)(2,1)S(1)} %get-tuple-element.46.refs_1_, f32[8,128]{1,0:T(8,128)S(1)} %get-tuple-element.47.refs_2_, bf16[4096,256]{1,0:T(8,128)(2,1)S(1)} %get-tuple-element.38.refs_1_.refs_3_, ...), custom_call_target="tpu_custom_call" | custom-call | flops 67108864 | bytes 10838016 | tf_op jit(solution)/shard_map/pallas_call | solution.py:353
  100.5 1.5 %collective-permute-start.30 = (f32[8,128]{1,0:T(8,128)S(1)}, f32[8,128]{1,0:T(8,128)S(1)}, u32[]{:S(2)}, u32[]{:S(2)}) collective-permute-start(f32[8,128]{1,0:T(8,128)S(1)} %shard_map.77.refs_5_), channel_id=1, source_target_pairs={{0,3},{1,2},{2,1},{3,0},{4,7},{5,6},{6,5},{7,4},{8,11},{9,10},{10,... | collective-permute-start | bytes 12296 | tf_op jit(solution)/shard_map/ppermute | solution.py:365
  102.1 1.1 collective-permute-start.29
  103.2 1.8 %collective-permute-start.28 = (f32[8,128]{1,0:T(8,128)S(1)}, f32[8,128]{1,0:T(8,128)S(1)}, u32[]{:S(2)}, u32[]{:S(2)}) collective-permute-start(f32[8,128]{1,0:T(8,128)S(1)} %shard_map.77.refs_5_), channel_id=1, source_target_pairs={{0,1},{1,0},{2,3},{3,2},{4,5},{5,4},{6,7},{7,6},{8,9},{9,8},{10,11... | collective-permute-start | bytes 12296 | tf_op jit(solution)/shard_map/ppermute | solution.py:365
  104.9 1.0 collective-permute-done.30.refs_8_
  106.0 0.6 collective-permute-done.29.refs_7_
  106.8 6.7 %shard_map.78 = (f32[4,1,512]{2,1,0:T(1,128)S(1)}, f32[4,1,512]{2,1,0:T(1,128)S(1)}, f32[8,128]{1,0:T(8,128)}) custom-call(bf16[1024,128]{1,0:T(8,128)(2,1)S(1)} %get-tuple-element.45.refs_0_, bf16[1024,4096]{1,0:T(8,128)(2,1)S(1)} %get-tuple-element.46.refs_1_, f32[8,128]{1,0:T(8,128)S(1)} %get-tuple-element.47.refs_2_, ...), custom_call_target="tpu_custom_call" | custom-call | flops 67108864 | bytes 10805248 | tf_op jit(solution)/shard_map/pallas_call | solution.py:353
  113.5 1.2 collective-permute-done.31.y_ref
  114.7 1.9 %collective-permute-start.32 = (f32[1,512]{1,0:T(1,128)S(1)}, f32[1,512]{1,0:T(1,128)S(1)}, u32[]{:S(2)}, u32[]{:S(2)}) collective-permute-start(f32[1,512]{1,0:T(1,128)S(1)} %get-tuple-element.53), channel_id=1, source_target_pairs={{0,24},{4,28},{8,16},{12,20},{16,8},{20,12},{24,0},{28,4},{1,25},{... | collective-permute-start | bytes 6152 | tf_op jit(solution)/shard_map/ppermute | solution.py:365
  116.6 1.2 collective-permute-start.33
  117.8 0.5 collective-permute-start.34
  118.3 1.0 collective-permute-done.32.refs_0_
  119.3 0.9 collective-permute-done.33.refs_1_
  120.2 1.2 collective-permute-done.34.refs_2_
  121.4 0.6 shard_map.80
  (25 shorter events, 0.8 us)
Async XLA Ops:
  0.6 9.9 %collective-permute-start.1 = (bf16[256,128]{1,0:T(8,128)(2,1)}, bf16[256,128]{1,0:T(8,128)(2,1)S(1)}, u32[]{:S(2)}, u32[]{:S(2)}) collective-permute-start(bf16[256,128]{1,0:T(8,128)(2,1)} %refs_0_.1), channel_id=1, source_target_pairs={{0,2},{1,3},{2,0},{3,1},{4,6},{5,7},{6,4},{7,5},{8,10},{9,11},{10,... | collective-permute-start | bytes 196616 | tf_op jit(solution)/shard_map/ppermute | solution.py:365
  4.7 6.1 %collective-permute-start = (bf16[256,128]{1,0:T(8,128)(2,1)}, bf16[256,128]{1,0:T(8,128)(2,1)S(1)}, u32[]{:S(2)}, u32[]{:S(2)}) collective-permute-start(bf16[256,128]{1,0:T(8,128)(2,1)} %refs_0_.1), channel_id=1, source_target_pairs={{0,1},{1,0},{2,3},{3,2},{4,5},{5,4},{6,7},{7,6},{8,9},{9,8},{10,11... | collective-permute-start | bytes 196616 | tf_op jit(solution)/shard_map/ppermute | solution.py:365
  6.3 6.3 %collective-permute-start.2 = (bf16[256,128]{1,0:T(8,128)(2,1)}, bf16[256,128]{1,0:T(8,128)(2,1)S(1)}, u32[]{:S(2)}, u32[]{:S(2)}) collective-permute-start(bf16[256,128]{1,0:T(8,128)(2,1)} %refs_0_.1), channel_id=1, source_target_pairs={{0,3},{1,2},{2,1},{3,0},{4,7},{5,6},{6,5},{7,4},{8,11},{9,10},{10,... | collective-permute-start | bytes 196616 | tf_op jit(solution)/shard_map/ppermute | solution.py:365
  7.2 7.5 %collective-permute-start.8 = (bf16[528,128]{1,0:T(8,128)(2,1)S(1)}, bf16[528,128]{1,0:T(8,128)(2,1)S(1)}, u32[]{:S(2)}, u32[]{:S(2)}) collective-permute-start(bf16[528,128]{1,0:T(8,128)(2,1)S(1)} %fusion.1.block_ref.refs_3_), channel_id=1, source_target_pairs={{0,24},{4,28},{8,16},{12,20},{16,8},{20,12},{24,0},{28,4},{1,25},{... | collective-permute-start | bytes 405512 | tf_op jit(solution)/shard_map/ppermute | solution.py:365
  10.0 5.9 %collective-permute-start.6 = (bf16[528,128]{1,0:T(8,128)(2,1)S(1)}, bf16[528,128]{1,0:T(8,128)(2,1)S(1)}, u32[]{:S(2)}, u32[]{:S(2)}) collective-permute-start(bf16[528,128]{1,0:T(8,128)(2,1)S(1)} %fusion.1.block_ref.refs_3_), channel_id=1, source_target_pairs={{0,16},{4,20},{8,24},{12,28},{16,0},{20,4},{24,8},{28,12},{1,17},{... | collective-permute-start | bytes 405512 | tf_op jit(solution)/shard_map/ppermute | solution.py:365
  10.5 5.4 %collective-permute-start.4 = (bf16[528,128]{1,0:T(8,128)(2,1)S(1)}, bf16[528,128]{1,0:T(8,128)(2,1)S(1)}, u32[]{:S(2)}, u32[]{:S(2)}) collective-permute-start(bf16[528,128]{1,0:T(8,128)(2,1)S(1)} %fusion.1.block_ref.refs_3_), channel_id=1, source_target_pairs={{0,8},{4,12},{8,0},{12,4},{16,24},{20,28},{24,16},{28,20},{1,9},{5... | collective-permute-start | bytes 405512 | tf_op jit(solution)/shard_map/ppermute | solution.py:365
  12.6 0.8 copy-start
  13.4 0.8 copy-start.1
  14.6 2.4 %collective-permute-start.3 = (bf16[528,128]{1,0:T(8,128)(2,1)S(1)}, bf16[528,128]{1,0:T(8,128)(2,1)S(1)}, u32[]{:S(2)}, u32[]{:S(2)}) collective-permute-start(bf16[528,128]{1,0:T(8,128)(2,1)S(1)} %fusion.1.block_ref.refs_3_), channel_id=1, source_target_pairs={{0,4},{4,0},{8,12},{12,8},{16,20},{20,16},{24,28},{28,24},{1,5},{5... | collective-permute-start | bytes 405512 | tf_op jit(solution)/shard_map/ppermute | solution.py:365
  15.9 1.4 %collective-permute-start.5 = (bf16[528,128]{1,0:T(8,128)(2,1)S(1)}, bf16[528,128]{1,0:T(8,128)(2,1)S(1)}, u32[]{:S(2)}, u32[]{:S(2)}) collective-permute-start(bf16[528,128]{1,0:T(8,128)(2,1)S(1)} %collective-permute-done.4.refs_5_), channel_id=1, source_target_pairs={{0,4},{4,0},{8,12},{12,8},{16,20},{20,16},{24,28},{28,24},{1,5},{5... | collective-permute-start | bytes 405512 | tf_op jit(solution)/shard_map/ppermute | solution.py:365
  15.9 1.5 %collective-permute-start.7 = (bf16[528,128]{1,0:T(8,128)(2,1)S(1)}, bf16[528,128]{1,0:T(8,128)(2,1)S(1)}, u32[]{:S(2)}, u32[]{:S(2)}) collective-permute-start(bf16[528,128]{1,0:T(8,128)(2,1)S(1)} %collective-permute-done.6.refs_7_), channel_id=1, source_target_pairs={{0,4},{4,0},{8,12},{12,8},{16,20},{20,16},{24,28},{28,24},{1,5},{5... | collective-permute-start | bytes 405512 | tf_op jit(solution)/shard_map/ppermute | solution.py:365
  16.4 1.4 %collective-permute-start.9 = (bf16[528,128]{1,0:T(8,128)(2,1)S(1)}, bf16[528,128]{1,0:T(8,128)(2,1)S(1)}, u32[]{:S(2)}, u32[]{:S(2)}) collective-permute-start(bf16[528,128]{1,0:T(8,128)(2,1)S(1)} %collective-permute-done.8.refs_9_), channel_id=1, source_target_pairs={{0,4},{4,0},{8,12},{12,8},{16,20},{20,16},{24,28},{28,24},{1,5},{5... | collective-permute-start | bytes 405512 | tf_op jit(solution)/shard_map/ppermute | solution.py:365
  33.1 5.5 %collective-permute-start.12 = (f32[8,128]{1,0:T(8,128)S(1)}, f32[8,128]{1,0:T(8,128)S(1)}, u32[]{:S(2)}, u32[]{:S(2)}) collective-permute-start(f32[8,128]{1,0:T(8,128)S(1)} %get-tuple-element.40.refs_1_), channel_id=1, source_target_pairs={{0,3},{1,2},{2,1},{3,0},{4,7},{5,6},{6,5},{7,4},{8,11},{9,10},{10,... | collective-permute-start | bytes 12296 | tf_op jit(solution)/shard_map/ppermute | solution.py:365
  36.7 4.5 %collective-permute-start.11 = (f32[8,128]{1,0:T(8,128)S(1)}, f32[8,128]{1,0:T(8,128)S(1)}, u32[]{:S(2)}, u32[]{:S(2)}) collective-permute-start(f32[8,128]{1,0:T(8,128)S(1)} %get-tuple-element.40.refs_1_), channel_id=1, source_target_pairs={{0,2},{1,3},{2,0},{3,1},{4,6},{5,7},{6,4},{7,5},{8,10},{9,11},{10,... | collective-permute-start | bytes 12296 | tf_op jit(solution)/shard_map/ppermute | solution.py:365
  36.7 4.5 %collective-permute-start.10 = (f32[8,128]{1,0:T(8,128)S(1)}, f32[8,128]{1,0:T(8,128)S(1)}, u32[]{:S(2)}, u32[]{:S(2)}) collective-permute-start(f32[8,128]{1,0:T(8,128)S(1)} %get-tuple-element.40.refs_1_), channel_id=1, source_target_pairs={{0,1},{1,0},{2,3},{3,2},{4,5},{5,4},{6,7},{7,6},{8,9},{9,8},{10,11... | collective-permute-start | bytes 12296 | tf_op jit(solution)/shard_map/ppermute | solution.py:365
  41.8 1.3 %collective-permute-start.13 = (f32[64,128]{1,0:T(8,128)S(1)}, f32[64,128]{1,0:T(8,128)S(1)}, u32[]{:S(2)}, u32[]{:S(2)}) collective-permute-start(f32[64,128]{1,0:T(8,128)S(1)} %get-tuple-element.43), channel_id=1, source_target_pairs={{0,4},{4,0},{8,12},{12,8},{16,20},{20,16},{24,28},{28,24},{1,5},{5... | collective-permute-start | bytes 98312 | tf_op jit(solution)/shard_map/ppermute | solution.py:365
  43.1 6.0 %collective-permute-start.16 = (f32[64,128]{1,0:T(8,128)S(1)}, f32[64,128]{1,0:T(8,128)S(1)}, u32[]{:S(2)}, u32[]{:S(2)}) collective-permute-start(f32[64,128]{1,0:T(8,128)S(1)} %shard_map.71.refs_0_), channel_id=1, source_target_pairs={{0,3},{1,2},{2,1},{3,0},{4,7},{5,6},{6,5},{7,4},{8,11},{9,10},{10,... | collective-permute-start | bytes 98312 | tf_op jit(solution)/shard_map/ppermute | solution.py:365
  44.5 5.0 %collective-permute-start.15 = (f32[64,128]{1,0:T(8,128)S(1)}, f32[64,128]{1,0:T(8,128)S(1)}, u32[]{:S(2)}, u32[]{:S(2)}) collective-permute-start(f32[64,128]{1,0:T(8,128)S(1)} %shard_map.71.refs_0_), channel_id=1, source_target_pairs={{0,2},{1,3},{2,0},{3,1},{4,6},{5,7},{6,4},{7,5},{8,10},{9,11},{10,... | collective-permute-start | bytes 98312 | tf_op jit(solution)/shard_map/ppermute | solution.py:365
  45.2 4.6 %collective-permute-start.14 = (f32[64,128]{1,0:T(8,128)S(1)}, f32[64,128]{1,0:T(8,128)S(1)}, u32[]{:S(2)}, u32[]{:S(2)}) collective-permute-start(f32[64,128]{1,0:T(8,128)S(1)} %shard_map.71.refs_0_), channel_id=1, source_target_pairs={{0,1},{1,0},{2,3},{3,2},{4,5},{5,4},{6,7},{7,6},{8,9},{9,8},{10,11... | collective-permute-start | bytes 98312 | tf_op jit(solution)/shard_map/ppermute | solution.py:365
  49.8 5.1 %collective-permute-start.19 = (f32[64,128]{1,0:T(8,128)S(1)}, f32[64,128]{1,0:T(8,128)S(1)}, u32[]{:S(2)}, u32[]{:S(2)}) collective-permute-start(f32[64,128]{1,0:T(8,128)S(1)} %shard_map.72.refs_0_), channel_id=1, source_target_pairs={{0,24},{4,28},{8,16},{12,20},{16,8},{20,12},{24,0},{28,4},{1,25},{... | collective-permute-start | bytes 98312 | tf_op jit(solution)/shard_map/ppermute | solution.py:365
  51.6 3.9 %collective-permute-start.18 = (f32[64,128]{1,0:T(8,128)S(1)}, f32[64,128]{1,0:T(8,128)S(1)}, u32[]{:S(2)}, u32[]{:S(2)}) collective-permute-start(f32[64,128]{1,0:T(8,128)S(1)} %shard_map.72.refs_0_), channel_id=1, source_target_pairs={{0,16},{4,20},{8,24},{12,28},{16,0},{20,4},{24,8},{28,12},{1,17},{... | collective-permute-start | bytes 98312 | tf_op jit(solution)/shard_map/ppermute | solution.py:365
  52.8 3.9 %collective-permute-start.17 = (f32[64,128]{1,0:T(8,128)S(1)}, f32[64,128]{1,0:T(8,128)S(1)}, u32[]{:S(2)}, u32[]{:S(2)}) collective-permute-start(f32[64,128]{1,0:T(8,128)S(1)} %shard_map.72.refs_0_), channel_id=1, source_target_pairs={{0,8},{4,12},{8,0},{12,4},{16,24},{20,28},{24,16},{28,20},{1,9},{5... | collective-permute-start | bytes 98312 | tf_op jit(solution)/shard_map/ppermute | solution.py:365
  56.7 1.3 %collective-permute-start.20 = (f32[64,128]{1,0:T(8,128)S(1)}, f32[64,128]{1,0:T(8,128)S(1)}, u32[]{:S(2)}, u32[]{:S(2)}) collective-permute-start(f32[64,128]{1,0:T(8,128)S(1)} %shard_map.73.refs_3_), channel_id=1, source_target_pairs={{0,4},{4,0},{8,12},{12,8},{16,20},{20,16},{24,28},{28,24},{1,5},{5... | collective-permute-start | bytes 98312 | tf_op jit(solution)/shard_map/ppermute | solution.py:365
  70.2 5.4 %collective-permute-start.23 = (f32[8,128]{1,0:T(8,128)S(1)}, f32[8,128]{1,0:T(8,128)S(1)}, u32[]{:S(2)}, u32[]{:S(2)}) collective-permute-start(f32[8,128]{1,0:T(8,128)S(1)} %get-tuple-element.48.refs_5_), channel_id=1, source_target_pairs={{0,3},{1,2},{2,1},{3,0},{4,7},{5,6},{6,5},{7,4},{8,11},{9,10},{10,... | collective-permute-start | bytes 12296 | tf_op jit(solution)/shard_map/ppermute | solution.py:365
  72.6 4.5 %collective-permute-start.22 = (f32[8,128]{1,0:T(8,128)S(1)}, f32[8,128]{1,0:T(8,128)S(1)}, u32[]{:S(2)}, u32[]{:S(2)}) collective-permute-start(f32[8,128]{1,0:T(8,128)S(1)} %get-tuple-element.48.refs_5_), channel_id=1, source_target_pairs={{0,2},{1,3},{2,0},{3,1},{4,6},{5,7},{6,4},{7,5},{8,10},{9,11},{10,... | collective-permute-start | bytes 12296 | tf_op jit(solution)/shard_map/ppermute | solution.py:365
  73.3 3.7 %collective-permute-start.21 = (f32[8,128]{1,0:T(8,128)S(1)}, f32[8,128]{1,0:T(8,128)S(1)}, u32[]{:S(2)}, u32[]{:S(2)}) collective-permute-start(f32[8,128]{1,0:T(8,128)S(1)} %get-tuple-element.48.refs_5_), channel_id=1, source_target_pairs={{0,1},{1,0},{2,3},{3,2},{4,5},{5,4},{6,7},{7,6},{8,9},{9,8},{10,11... | collective-permute-start | bytes 12296 | tf_op jit(solution)/shard_map/ppermute | solution.py:365
  84.0 1.2 collective-permute-start.24
  85.2 4.7 %collective-permute-start.27 = (f32[8,512]{1,0:T(8,128)S(1)}, f32[8,512]{1,0:T(8,128)S(1)}, u32[]{:S(2)}, u32[]{:S(2)}) collective-permute-start(f32[8,512]{1,0:T(8,128)S(1)} %shard_map.76.refs_5_), channel_id=1, source_target_pairs={{0,24},{4,28},{8,16},{12,20},{16,8},{20,12},{24,0},{28,4},{1,25},{... | collective-permute-start | bytes 49160 | tf_op jit(solution)/shard_map/ppermute | solution.py:365
  86.7 3.7 %collective-permute-start.26 = (f32[8,512]{1,0:T(8,128)S(1)}, f32[8,512]{1,0:T(8,128)S(1)}, u32[]{:S(2)}, u32[]{:S(2)}) collective-permute-start(f32[8,512]{1,0:T(8,128)S(1)} %shard_map.76.refs_5_), channel_id=1, source_target_pairs={{0,16},{4,20},{8,24},{12,28},{16,0},{20,4},{24,8},{28,12},{1,17},{... | collective-permute-start | bytes 49160 | tf_op jit(solution)/shard_map/ppermute | solution.py:365
  87.3 3.7 %collective-permute-start.25 = (f32[8,512]{1,0:T(8,128)S(1)}, f32[8,512]{1,0:T(8,128)S(1)}, u32[]{:S(2)}, u32[]{:S(2)}) collective-permute-start(f32[8,512]{1,0:T(8,128)S(1)} %shard_map.76.refs_5_), channel_id=1, source_target_pairs={{0,8},{4,12},{8,0},{12,4},{16,24},{20,28},{24,16},{28,20},{1,9},{5... | collective-permute-start | bytes 49160 | tf_op jit(solution)/shard_map/ppermute | solution.py:365
  100.5 5.4 %collective-permute-start.30 = (f32[8,128]{1,0:T(8,128)S(1)}, f32[8,128]{1,0:T(8,128)S(1)}, u32[]{:S(2)}, u32[]{:S(2)}) collective-permute-start(f32[8,128]{1,0:T(8,128)S(1)} %shard_map.77.refs_5_), channel_id=1, source_target_pairs={{0,3},{1,2},{2,1},{3,0},{4,7},{5,6},{6,5},{7,4},{8,11},{9,10},{10,... | collective-permute-start | bytes 12296 | tf_op jit(solution)/shard_map/ppermute | solution.py:365
  102.1 4.5 %collective-permute-start.29 = (f32[8,128]{1,0:T(8,128)S(1)}, f32[8,128]{1,0:T(8,128)S(1)}, u32[]{:S(2)}, u32[]{:S(2)}) collective-permute-start(f32[8,128]{1,0:T(8,128)S(1)} %shard_map.77.refs_5_), channel_id=1, source_target_pairs={{0,2},{1,3},{2,0},{3,1},{4,6},{5,7},{6,4},{7,5},{8,10},{9,11},{10,... | collective-permute-start | bytes 12296 | tf_op jit(solution)/shard_map/ppermute | solution.py:365
  103.2 3.6 %collective-permute-start.28 = (f32[8,128]{1,0:T(8,128)S(1)}, f32[8,128]{1,0:T(8,128)S(1)}, u32[]{:S(2)}, u32[]{:S(2)}) collective-permute-start(f32[8,128]{1,0:T(8,128)S(1)} %shard_map.77.refs_5_), channel_id=1, source_target_pairs={{0,1},{1,0},{2,3},{3,2},{4,5},{5,4},{6,7},{7,6},{8,9},{9,8},{10,11... | collective-permute-start | bytes 12296 | tf_op jit(solution)/shard_map/ppermute | solution.py:365
  113.5 1.2 collective-permute-start.31
  114.7 4.5 %collective-permute-start.32 = (f32[1,512]{1,0:T(1,128)S(1)}, f32[1,512]{1,0:T(1,128)S(1)}, u32[]{:S(2)}, u32[]{:S(2)}) collective-permute-start(f32[1,512]{1,0:T(1,128)S(1)} %get-tuple-element.53), channel_id=1, source_target_pairs={{0,24},{4,28},{8,16},{12,20},{16,8},{20,12},{24,0},{28,4},{1,25},{... | collective-permute-start | bytes 6152 | tf_op jit(solution)/shard_map/ppermute | solution.py:365
  116.6 3.6 %collective-permute-start.33 = (f32[1,512]{1,0:T(1,128)S(1)}, f32[1,512]{1,0:T(1,128)S(1)}, u32[]{:S(2)}, u32[]{:S(2)}) collective-permute-start(f32[1,512]{1,0:T(1,128)S(1)} %get-tuple-element.54), channel_id=1, source_target_pairs={{0,16},{4,20},{8,24},{12,28},{16,0},{20,4},{24,8},{28,12},{1,17},{... | collective-permute-start | bytes 6152 | tf_op jit(solution)/shard_map/ppermute | solution.py:365
  117.8 3.6 %collective-permute-start.34 = (f32[1,512]{1,0:T(1,128)S(1)}, f32[1,512]{1,0:T(1,128)S(1)}, u32[]{:S(2)}, u32[]{:S(2)}) collective-permute-start(f32[1,512]{1,0:T(1,128)S(1)} %get-tuple-element.55), channel_id=1, source_target_pairs={{0,8},{4,12},{8,0},{12,4},{16,24},{20,28},{24,16},{28,20},{1,9},{5... | collective-permute-start | bytes 6152 | tf_op jit(solution)/shard_map/ppermute | solution.py:365

commit v13 on v12

--- a/solution.py
+++ b/solution.py
@@ -151,14 +151,14 @@
             carried_ref[rows, :] = carried / mass
 
 
-def project_kernel(ns, *refs):
-    s_refs, moment_ref, s_ref, a_ref = refs[:ns], *refs[ns:]
+def project_kernel(order, *refs):
+    s_refs, moment_ref, s_ref, a_ref = refs[: len(order)], *refs[len(order) :]
     piece = s_refs[0].shape[0]
     parts = split3(moment_ref[...])
-    for k in range(ns):
+    for k, piece_ref in zip(order, s_refs):
         at = slice(k * piece, (k + 1) * piece)
-        s_ref[at, :] = s_refs[k][...]
-        a_ref[at, :] = project4(s_refs[k][...], parts)
+        s_ref[at, :] = piece_ref[...]
+        a_ref[at, :] = project4(piece_ref[...], parts)
 
 
 def potential_of(block_ref, width):
@@ -396,10 +396,11 @@
     block = jnp.concatenate([target, tail], axis=0)
     pieces = exchange(source, "col")
     far = exchange_chips(block)
+    order = [0, ns - 2, ns - 1] + list(range(ns - 3, 0, -1)) if ns > 2 else list(range(ns))
     s, a = call(
-        functools.partial(project_kernel, ns),
+        functools.partial(project_kernel, order),
         [projected, projected],
-        pieces + [prev_moment],
+        [pieces[k] for k in order] + [prev_moment],
         flops=200 * rows * depth * depth,
     )
     far = [lax.optimization_barrier((x, a))[0] for x in far]

time: 122 us -> 122 us (level)
  transfers between devices with their start and end apart: 35 -> 35, of which waited for: 29 -> 30; matrix products, arithmetic and copies ran while one was open for 1% -> 1% of each run, Pallas kernels for 1% -> 1%
where the time goes in v13:
time: 122 us
  Pallas kernels  52.9 us (43%)
  starting transfers between devices  38.4 us (31%)
  waiting for transfers between devices  27.3 us (22%)
  local copies, waits for them, and re-layouts  1.68 us (1%)
    pallas_call x14, Pallas kernels, call(): pl.pallas_call(kernel, out_shape=list(out), in_specs=[vmem] * len(args),...  52.9 us
    ppermute x35, starting transfers between devices, swap(): lax.ppermute(x, axis, [(i, i ^ k) for i in range(lax.axis_size(axis))])  38.4 us
    ppermute x35, waiting for transfers between devices, swap(): lax.ppermute(x, axis, [(i, i ^ k) for i in range(lax.axis_size(axis))])  27.3 us
  transfers between devices with their start and end apart: 35, of which 30 were waited for; matrix products, arithmetic and copies ran while one was open for 1% of the time, Pallas kernels for 1%

profile of v13, /device:TPU:0, one launch (start us, length us, event | category | flops | bytes accessed | tf_op | source)
XLA Modules:
  0.0 122.0 jit_solution(13806949050778698690)
XLA Ops:
  0.6 5.1 %collective-permute-start.1 = (bf16[256,128]{1,0:T(8,128)(2,1)}, bf16[256,128]{1,0:T(8,128)(2,1)S(1)}, u32[]{:S(2)}, u32[]{:S(2)}) collective-permute-start(bf16[256,128]{1,0:T(8,128)(2,1)} %refs_0_.1), channel_id=1, source_target_pairs={{0,3},{1,2},{2,1},{3,0},{4,7},{5,6},{6,5},{7,4},{8,11},{9,10},{10,... | collective-permute-start | bytes 196616 | tf_op jit(solution)/shard_map/ppermute | solution.py:365
  5.7 0.6 collective-permute-start.2
  6.4 0.9 fusion.1.block_ref.refs_3_
  7.3 2.7 %collective-permute-start.8 = (bf16[528,128]{1,0:T(8,128)(2,1)S(1)}, bf16[528,128]{1,0:T(8,128)(2,1)S(1)}, u32[]{:S(2)}, u32[]{:S(2)}) collective-permute-start(bf16[528,128]{1,0:T(8,128)(2,1)S(1)} %fusion.1.block_ref.refs_3_), channel_id=1, source_target_pairs={{0,24},{4,28},{8,16},{12,20},{16,8},{20,12},{24,0},{28,4},{1,25},{... | collective-permute-start | bytes 405512 | tf_op jit(solution)/shard_map/ppermute | solution.py:365
  10.0 0.5 collective-permute-start.6
  10.5 0.4 collective-permute-start.4
  10.9 0.7 collective-permute-done.refs_1_
  11.6 0.8 copy-done
  12.4 0.8 copy-done.1
  13.2 0.4 shard_map.67
  13.7 0.3 collective-permute-done.8.refs_9_
  14.0 1.9 %collective-permute-done.6.refs_7_ = bf16[528,128]{1,0:T(8,128)(2,1)S(1)} collective-permute-done((bf16[528,128]{1,0:T(8,128)(2,1)S(1)}, bf16[528,128]{1,0:T(8,128)(2,1)S(1)}, u32[]{:S(2)}, u32[]{:S(2)}) %collective-permute-start.6) | collective-permute-done | bytes 135200 | tf_op jit(solution)/shard_map/ppermute | solution.py:365
  16.0 0.5 collective-permute-start.7
  16.5 0.6 shard_map.68
  17.1 0.2 collective-permute-done.5.refs_6_
  17.6 0.3 collective-permute-done.9.refs_10_
  17.9 15.3 %shard_map.69 = (f32[8,128]{1,0:T(8,128)S(1)}, f32[1024,128]{1,0:T(8,128)S(1)}, bf16[4096,256]{1,0:T(8,128)(2,1)S(1)}, f32[8,512]{1,0:T(8,128)S(1)}) custom-call(bf16[1024,128]{1,0:T(8,128)(2,1)S(1)} %get-tuple-element.31.a_ref.refs_0_, bf16[1024,256]{1,0:T(8,128)(2,1)S(1)} %get-tuple-element.33.refs_1_, f32[8,128]{1,0:T(8,128)S(1)} %get-tuple-element.34.refs_2_, ...), custom_call_target="tpu_custom_call" | custom-call | flops 2147483648 | bytes 4513792 | tf_op jit(solution)/shard_map/pallas_call | solution.py:353
  33.2 3.5 %collective-permute-start.12 = (f32[8,128]{1,0:T(8,128)S(1)}, f32[8,128]{1,0:T(8,128)S(1)}, u32[]{:S(2)}, u32[]{:S(2)}) collective-permute-start(f32[8,128]{1,0:T(8,128)S(1)} %get-tuple-element.40.refs_1_), channel_id=1, source_target_pairs={{0,3},{1,2},{2,1},{3,0},{4,7},{5,6},{6,5},{7,4},{8,11},{9,10},{10,... | collective-permute-start | bytes 12296 | tf_op jit(solution)/shard_map/ppermute | solution.py:365
  36.7 0.9 collective-permute-start.10
  37.7 1.0 collective-permute-done.12.refs_4_
  38.7 2.6 %collective-permute-done.11.refs_3_ = f32[8,128]{1,0:T(8,128)S(1)} collective-permute-done((f32[8,128]{1,0:T(8,128)S(1)}, f32[8,128]{1,0:T(8,128)S(1)}, u32[]{:S(2)}, u32[]{:S(2)}) %collective-permute-start.11) | collective-permute-done | bytes 4128 | tf_op jit(solution)/shard_map/ppermute | solution.py:365
  41.2 0.5 shard_map.70
  41.9 1.2 collective-permute-done.13.refs_1_
  43.1 1.5 %collective-permute-start.16 = (f32[64,128]{1,0:T(8,128)S(1)}, f32[64,128]{1,0:T(8,128)S(1)}, u32[]{:S(2)}, u32[]{:S(2)}) collective-permute-start(f32[64,128]{1,0:T(8,128)S(1)} %shard_map.71.refs_0_), channel_id=1, source_target_pairs={{0,3},{1,2},{2,1},{3,0},{4,7},{5,6},{6,5},{7,4},{8,11},{9,10},{10,... | collective-permute-start | bytes 98312 | tf_op jit(solution)/shard_map/ppermute | solution.py:365
  44.5 0.6 collective-permute-start.15
  45.2 2.3 %collective-permute-start.14 = (f32[64,128]{1,0:T(8,128)S(1)}, f32[64,128]{1,0:T(8,128)S(1)}, u32[]{:S(2)}, u32[]{:S(2)}) collective-permute-start(f32[64,128]{1,0:T(8,128)S(1)} %shard_map.71.refs_0_), channel_id=1, source_target_pairs={{0,1},{1,0},{2,3},{3,2},{4,5},{5,4},{6,7},{7,6},{8,9},{9,8},{10,11... | collective-permute-start | bytes 98312 | tf_op jit(solution)/shard_map/ppermute | solution.py:365
  47.4 1.6 %collective-permute-done.16.refs_3_ = f32[64,128]{1,0:T(8,128)S(1)} collective-permute-done((f32[64,128]{1,0:T(8,128)S(1)}, f32[64,128]{1,0:T(8,128)S(1)}, u32[]{:S(2)}, u32[]{:S(2)}) %collective-permute-start.16) | collective-permute-done | bytes 32800 | tf_op jit(solution)/shard_map/ppermute | solution.py:365
  49.1 0.4 collective-permute-done.15.refs_2_
  49.8 1.8 %collective-permute-start.19 = (f32[64,128]{1,0:T(8,128)S(1)}, f32[64,128]{1,0:T(8,128)S(1)}, u32[]{:S(2)}, u32[]{:S(2)}) collective-permute-start(f32[64,128]{1,0:T(8,128)S(1)} %shard_map.72.refs_0_), channel_id=1, source_target_pairs={{0,24},{4,28},{8,16},{12,20},{16,8},{20,12},{24,0},{28,4},{1,25},{... | collective-permute-start | bytes 98312 | tf_op jit(solution)/shard_map/ppermute | solution.py:365
  51.5 1.3 %collective-permute-start.18 = (f32[64,128]{1,0:T(8,128)S(1)}, f32[64,128]{1,0:T(8,128)S(1)}, u32[]{:S(2)}, u32[]{:S(2)}) collective-permute-start(f32[64,128]{1,0:T(8,128)S(1)} %shard_map.72.refs_0_), channel_id=1, source_target_pairs={{0,16},{4,20},{8,24},{12,28},{16,0},{20,4},{24,8},{28,12},{1,17},{... | collective-permute-start | bytes 98312 | tf_op jit(solution)/shard_map/ppermute | solution.py:365
  52.8 0.5 collective-permute-start.17
  53.3 1.6 %collective-permute-done.19.refs_3_ = f32[64,128]{1,0:T(8,128)S(1)} collective-permute-done((f32[64,128]{1,0:T(8,128)S(1)}, f32[64,128]{1,0:T(8,128)S(1)}, u32[]{:S(2)}, u32[]{:S(2)}) %collective-permute-start.19) | collective-permute-done | bytes 32800 | tf_op jit(solution)/shard_map/ppermute | solution.py:365
  54.9 0.5 collective-permute-done.18.refs_2_
  55.4 1.3 %collective-permute-done.17.refs_1_ = f32[64,128]{1,0:T(8,128)S(1)} collective-permute-done((f32[64,128]{1,0:T(8,128)S(1)}, f32[64,128]{1,0:T(8,128)S(1)}, u32[]{:S(2)}, u32[]{:S(2)}) %collective-permute-start.17) | collective-permute-done | bytes 32800 | tf_op jit(solution)/shard_map/ppermute | solution.py:365
  56.8 1.2 collective-permute-done.20.refs_4_
  58.0 12.2 %shard_map.74 = (f32[128,128]{1,0:T(8,128)}, bf16[1024,128]{1,0:T(8,128)(2,1)S(1)}, f32[8,128]{1,0:T(8,128)S(1)}, f32[8,128]{1,0:T(8,128)S(1)}, bf16[1024,4096]{1,0:T(8,128)(2,1)S(1)}) custom-call(bf16[1024,128]{1,0:T(8,128)(2,1)S(1)} %get-tuple-element.30.refs_0_, bf16[4096,256]{1,0:T(8,128)(2,1)S(1)} %get-tuple-element.38.refs_1_.refs_3_, ...), custom_call_target="tpu_custom_call" | custom-call | flops 1073741824 | bytes 11165696 | tf_op jit(solution)/shard_map/pallas_call | solution.py:353
  70.2 2.3 %collective-permute-start.23 = (f32[8,128]{1,0:T(8,128)S(1)}, f32[8,128]{1,0:T(8,128)S(1)}, u32[]{:S(2)}, u32[]{:S(2)}) collective-permute-start(f32[8,128]{1,0:T(8,128)S(1)} %get-tuple-element.48.refs_5_), channel_id=1, source_target_pairs={{0,3},{1,2},{2,1},{3,0},{4,7},{5,6},{6,5},{7,4},{8,11},{9,10},{10,... | collective-permute-start | bytes 12296 | tf_op jit(solution)/shard_map/ppermute | solution.py:365
  72.6 0.8 collective-permute-start.22
  73.3 1.3 %collective-permute-start.21 = (f32[8,128]{1,0:T(8,128)S(1)}, f32[8,128]{1,0:T(8,128)S(1)}, u32[]{:S(2)}, u32[]{:S(2)}) collective-permute-start(f32[8,128]{1,0:T(8,128)S(1)} %get-tuple-element.48.refs_5_), channel_id=1, source_target_pairs={{0,1},{1,0},{2,3},{3,2},{4,5},{5,4},{6,7},{7,6},{8,9},{9,8},{10,11... | collective-permute-start | bytes 12296 | tf_op jit(solution)/shard_map/ppermute | solution.py:365
  74.6 1.0 collective-permute-done.23.refs_8_
  75.6 1.4 %collective-permute-done.22.refs_7_ = f32[8,128]{1,0:T(8,128)S(1)} collective-permute-done((f32[8,128]{1,0:T(8,128)S(1)}, f32[8,128]{1,0:T(8,128)S(1)}, u32[]{:S(2)}, u32[]{:S(2)}) %collective-permute-start.22) | collective-permute-done | bytes 4128 | tf_op jit(solution)/shard_map/ppermute | solution.py:365
  77.1 7.0 %shard_map.75 = (f32[8,512]{1,0:T(8,128)S(1)}, f32[8,128]{1,0:T(8,128)}) custom-call(bf16[1024,128]{1,0:T(8,128)(2,1)S(1)} %get-tuple-element.45.refs_0_, bf16[1024,4096]{1,0:T(8,128)(2,1)S(1)} %get-tuple-element.46.refs_1_, f32[8,128]{1,0:T(8,128)S(1)} %get-tuple-element.47.refs_2_, bf16[4096,256]{1,0:T(8,128)(2,1)S(1)} %get-tuple-element.38.refs_1_.refs_3_, ...), custom_call_target="tpu_custom_call" | custom-call | flops 67108864 | bytes 10805248 | tf_op jit(solution)/shard_map/pallas_call | solution.py:353
  84.0 1.2 collective-permute-done.24.refs_1_
  85.2 1.5 %collective-permute-start.27 = (f32[8,512]{1,0:T(8,128)S(1)}, f32[8,512]{1,0:T(8,128)S(1)}, u32[]{:S(2)}, u32[]{:S(2)}) collective-permute-start(f32[8,512]{1,0:T(8,128)S(1)} %shard_map.76.refs_5_), channel_id=1, source_target_pairs={{0,24},{4,28},{8,16},{12,20},{16,8},{20,12},{24,0},{28,4},{1,25},{... | collective-permute-start | bytes 49160 | tf_op jit(solution)/shard_map/ppermute | solution.py:365
  86.7 0.5 collective-permute-start.26
  87.2 1.5 %collective-permute-start.25 = (f32[8,512]{1,0:T(8,128)S(1)}, f32[8,512]{1,0:T(8,128)S(1)}, u32[]{:S(2)}, u32[]{:S(2)}) collective-permute-start(f32[8,512]{1,0:T(8,128)S(1)} %shard_map.76.refs_5_), channel_id=1, source_target_pairs={{0,8},{4,12},{8,0},{12,4},{16,24},{20,28},{24,16},{28,20},{1,9},{5... | collective-permute-start | bytes 49160 | tf_op jit(solution)/shard_map/ppermute | solution.py:365
  88.8 1.1 collective-permute-done.27.refs_8_
  89.9 0.5 collective-permute-done.26.refs_7_
  90.4 0.5 collective-permute-done.25.refs_6_
  91.0 9.5 %shard_map.77.refs_5_ = f32[8,128]{1,0:T(8,128)S(1)} custom-call(bf16[1024,128]{1,0:T(8,128)(2,1)S(1)} %get-tuple-element.45.refs_0_, bf16[1024,4096]{1,0:T(8,128)(2,1)S(1)} %get-tuple-element.46.refs_1_, f32[8,128]{1,0:T(8,128)S(1)} %get-tuple-element.47.refs_2_, bf16[4096,256]{1,0:T(8,128)(2,1)S(1)} %get-tuple-element.38.refs_1_.refs_3_, ...), custom_call_target="tpu_custom_call" | custom-call | flops 67108864 | bytes 10838016 | tf_op jit(solution)/shard_map/pallas_call | solution.py:353
  100.5 1.6 %collective-permute-start.30 = (f32[8,128]{1,0:T(8,128)S(1)}, f32[8,128]{1,0:T(8,128)S(1)}, u32[]{:S(2)}, u32[]{:S(2)}) collective-permute-start(f32[8,128]{1,0:T(8,128)S(1)} %shard_map.77.refs_5_), channel_id=1, source_target_pairs={{0,3},{1,2},{2,1},{3,0},{4,7},{5,6},{6,5},{7,4},{8,11},{9,10},{10,... | collective-permute-start | bytes 12296 | tf_op jit(solution)/shard_map/ppermute | solution.py:365
  102.1 1.1 collective-permute-start.29
  103.2 1.8 %collective-permute-start.28 = (f32[8,128]{1,0:T(8,128)S(1)}, f32[8,128]{1,0:T(8,128)S(1)}, u32[]{:S(2)}, u32[]{:S(2)}) collective-permute-start(f32[8,128]{1,0:T(8,128)S(1)} %shard_map.77.refs_5_), channel_id=1, source_target_pairs={{0,1},{1,0},{2,3},{3,2},{4,5},{5,4},{6,7},{7,6},{8,9},{9,8},{10,11... | collective-permute-start | bytes 12296 | tf_op jit(solution)/shard_map/ppermute | solution.py:365
  104.9 1.0 collective-permute-done.30.refs_8_
  105.9 0.6 collective-permute-done.29.refs_7_
  106.8 6.7 %shard_map.78 = (f32[4,1,512]{2,1,0:T(1,128)S(1)}, f32[4,1,512]{2,1,0:T(1,128)S(1)}, f32[8,128]{1,0:T(8,128)}) custom-call(bf16[1024,128]{1,0:T(8,128)(2,1)S(1)} %get-tuple-element.45.refs_0_, bf16[1024,4096]{1,0:T(8,128)(2,1)S(1)} %get-tuple-element.46.refs_1_, f32[8,128]{1,0:T(8,128)S(1)} %get-tuple-element.47.refs_2_, ...), custom_call_target="tpu_custom_call" | custom-call | flops 67108864 | bytes 10805248 | tf_op jit(solution)/shard_map/pallas_call | solution.py:353
  113.5 1.2 collective-permute-done.31.y_ref
  114.7 1.8 %collective-permute-start.32 = (f32[1,512]{1,0:T(1,128)S(1)}, f32[1,512]{1,0:T(1,128)S(1)}, u32[]{:S(2)}, u32[]{:S(2)}) collective-permute-start(f32[1,512]{1,0:T(1,128)S(1)} %get-tuple-element.53), channel_id=1, source_target_pairs={{0,24},{4,28},{8,16},{12,20},{16,8},{20,12},{24,0},{28,4},{1,25},{... | collective-permute-start | bytes 6152 | tf_op jit(solution)/shard_map/ppermute | solution.py:365
  116.5 1.3 %collective-permute-start.33 = (f32[1,512]{1,0:T(1,128)S(1)}, f32[1,512]{1,0:T(1,128)S(1)}, u32[]{:S(2)}, u32[]{:S(2)}) collective-permute-start(f32[1,512]{1,0:T(1,128)S(1)} %get-tuple-element.54), channel_id=1, source_target_pairs={{0,16},{4,20},{8,24},{12,28},{16,0},{20,4},{24,8},{28,12},{1,17},{... | collective-permute-start | bytes 6152 | tf_op jit(solution)/shard_map/ppermute | solution.py:365
  117.8 0.5 collective-permute-start.34
  118.3 1.0 collective-permute-done.32.refs_0_
  119.3 0.8 collective-permute-done.33.refs_1_
  120.1 1.3 %collective-permute-done.34.refs_2_ = f32[1,512]{1,0:T(1,128)S(1)} collective-permute-done((f32[1,512]{1,0:T(1,128)S(1)}, f32[1,512]{1,0:T(1,128)S(1)}, u32[]{:S(2)}, u32[]{:S(2)}) %collective-permute-start.34) | collective-permute-done | bytes 2080 | tf_op jit(solution)/shard_map/ppermute | solution.py:365
  121.4 0.6 shard_map.80
  (25 shorter events, 1.0 us)
Async XLA Ops:
  0.6 9.9 %collective-permute-start.1 = (bf16[256,128]{1,0:T(8,128)(2,1)}, bf16[256,128]{1,0:T(8,128)(2,1)S(1)}, u32[]{:S(2)}, u32[]{:S(2)}) collective-permute-start(bf16[256,128]{1,0:T(8,128)(2,1)} %refs_0_.1), channel_id=1, source_target_pairs={{0,3},{1,2},{2,1},{3,0},{4,7},{5,6},{6,5},{7,4},{8,11},{9,10},{10,... | collective-permute-start | bytes 196616 | tf_op jit(solution)/shard_map/ppermute | solution.py:365
  5.7 5.8 %collective-permute-start = (bf16[256,128]{1,0:T(8,128)(2,1)}, bf16[256,128]{1,0:T(8,128)(2,1)S(1)}, u32[]{:S(2)}, u32[]{:S(2)}) collective-permute-start(bf16[256,128]{1,0:T(8,128)(2,1)} %refs_0_.1), channel_id=1, source_target_pairs={{0,2},{1,3},{2,0},{3,1},{4,6},{5,7},{6,4},{7,5},{8,10},{9,11},{10,... | collective-permute-start | bytes 196616 | tf_op jit(solution)/shard_map/ppermute | solution.py:365
  5.7 5.8 %collective-permute-start.2 = (bf16[256,128]{1,0:T(8,128)(2,1)}, bf16[256,128]{1,0:T(8,128)(2,1)S(1)}, u32[]{:S(2)}, u32[]{:S(2)}) collective-permute-start(bf16[256,128]{1,0:T(8,128)(2,1)} %refs_0_.1), channel_id=1, source_target_pairs={{0,1},{1,0},{2,3},{3,2},{4,5},{5,4},{6,7},{7,6},{8,9},{9,8},{10,11... | collective-permute-start | bytes 196616 | tf_op jit(solution)/shard_map/ppermute | solution.py:365
  7.3 6.7 %collective-permute-start.8 = (bf16[528,128]{1,0:T(8,128)(2,1)S(1)}, bf16[528,128]{1,0:T(8,128)(2,1)S(1)}, u32[]{:S(2)}, u32[]{:S(2)}) collective-permute-start(bf16[528,128]{1,0:T(8,128)(2,1)S(1)} %fusion.1.block_ref.refs_3_), channel_id=1, source_target_pairs={{0,24},{4,28},{8,16},{12,20},{16,8},{20,12},{24,0},{28,4},{1,25},{... | collective-permute-start | bytes 405512 | tf_op jit(solution)/shard_map/ppermute | solution.py:365
  10.0 6.0 %collective-permute-start.6 = (bf16[528,128]{1,0:T(8,128)(2,1)S(1)}, bf16[528,128]{1,0:T(8,128)(2,1)S(1)}, u32[]{:S(2)}, u32[]{:S(2)}) collective-permute-start(bf16[528,128]{1,0:T(8,128)(2,1)S(1)} %fusion.1.block_ref.refs_3_), channel_id=1, source_target_pairs={{0,16},{4,20},{8,24},{12,28},{16,0},{20,4},{24,8},{28,12},{1,17},{... | collective-permute-start | bytes 405512 | tf_op jit(solution)/shard_map/ppermute | solution.py:365
  10.5 5.5 %collective-permute-start.4 = (bf16[528,128]{1,0:T(8,128)(2,1)S(1)}, bf16[528,128]{1,0:T(8,128)(2,1)S(1)}, u32[]{:S(2)}, u32[]{:S(2)}) collective-permute-start(bf16[528,128]{1,0:T(8,128)(2,1)S(1)} %fusion.1.block_ref.refs_3_), channel_id=1, source_target_pairs={{0,8},{4,12},{8,0},{12,4},{16,24},{20,28},{24,16},{28,20},{1,9},{5... | collective-permute-start | bytes 405512 | tf_op jit(solution)/shard_map/ppermute | solution.py:365
  11.6 0.8 copy-start
  12.4 0.8 copy-start.1
  13.6 3.5 %collective-permute-start.3 = (bf16[528,128]{1,0:T(8,128)(2,1)S(1)}, bf16[528,128]{1,0:T(8,128)(2,1)S(1)}, u32[]{:S(2)}, u32[]{:S(2)}) collective-permute-start(bf16[528,128]{1,0:T(8,128)(2,1)S(1)} %fusion.1.block_ref.refs_3_), channel_id=1, source_target_pairs={{0,4},{4,0},{8,12},{12,8},{16,20},{20,16},{24,28},{28,24},{1,5},{5... | collective-permute-start | bytes 405512 | tf_op jit(solution)/shard_map/ppermute | solution.py:365
  16.0 1.4 %collective-permute-start.5 = (bf16[528,128]{1,0:T(8,128)(2,1)S(1)}, bf16[528,128]{1,0:T(8,128)(2,1)S(1)}, u32[]{:S(2)}, u32[]{:S(2)}) collective-permute-start(bf16[528,128]{1,0:T(8,128)(2,1)S(1)} %collective-permute-done.4.refs_5_), channel_id=1, source_target_pairs={{0,4},{4,0},{8,12},{12,8},{16,20},{20,16},{24,28},{28,24},{1,5},{5... | collective-permute-start | bytes 405512 | tf_op jit(solution)/shard_map/ppermute | solution.py:365
  16.0 1.5 %collective-permute-start.7 = (bf16[528,128]{1,0:T(8,128)(2,1)S(1)}, bf16[528,128]{1,0:T(8,128)(2,1)S(1)}, u32[]{:S(2)}, u32[]{:S(2)}) collective-permute-start(bf16[528,128]{1,0:T(8,128)(2,1)S(1)} %collective-permute-done.6.refs_7_), channel_id=1, source_target_pairs={{0,4},{4,0},{8,12},{12,8},{16,20},{20,16},{24,28},{28,24},{1,5},{5... | collective-permute-start | bytes 405512 | tf_op jit(solution)/shard_map/ppermute | solution.py:365
  16.5 1.4 %collective-permute-start.9 = (bf16[528,128]{1,0:T(8,128)(2,1)S(1)}, bf16[528,128]{1,0:T(8,128)(2,1)S(1)}, u32[]{:S(2)}, u32[]{:S(2)}) collective-permute-start(bf16[528,128]{1,0:T(8,128)(2,1)S(1)} %collective-permute-done.8.refs_9_), channel_id=1, source_target_pairs={{0,4},{4,0},{8,12},{12,8},{16,20},{20,16},{24,28},{28,24},{1,5},{5... | collective-permute-start | bytes 405512 | tf_op jit(solution)/shard_map/ppermute | solution.py:365
  33.2 5.5 %collective-permute-start.12 = (f32[8,128]{1,0:T(8,128)S(1)}, f32[8,128]{1,0:T(8,128)S(1)}, u32[]{:S(2)}, u32[]{:S(2)}) collective-permute-start(f32[8,128]{1,0:T(8,128)S(1)} %get-tuple-element.40.refs_1_), channel_id=1, source_target_pairs={{0,3},{1,2},{2,1},{3,0},{4,7},{5,6},{6,5},{7,4},{8,11},{9,10},{10,... | collective-permute-start | bytes 12296 | tf_op jit(solution)/shard_map/ppermute | solution.py:365
  36.7 4.5 %collective-permute-start.11 = (f32[8,128]{1,0:T(8,128)S(1)}, f32[8,128]{1,0:T(8,128)S(1)}, u32[]{:S(2)}, u32[]{:S(2)}) collective-permute-start(f32[8,128]{1,0:T(8,128)S(1)} %get-tuple-element.40.refs_1_), channel_id=1, source_target_pairs={{0,2},{1,3},{2,0},{3,1},{4,6},{5,7},{6,4},{7,5},{8,10},{9,11},{10,... | collective-permute-start | bytes 12296 | tf_op jit(solution)/shard_map/ppermute | solution.py:365
  36.7 4.5 %collective-permute-start.10 = (f32[8,128]{1,0:T(8,128)S(1)}, f32[8,128]{1,0:T(8,128)S(1)}, u32[]{:S(2)}, u32[]{:S(2)}) collective-permute-start(f32[8,128]{1,0:T(8,128)S(1)} %get-tuple-element.40.refs_1_), channel_id=1, source_target_pairs={{0,1},{1,0},{2,3},{3,2},{4,5},{5,4},{6,7},{7,6},{8,9},{9,8},{10,11... | collective-permute-start | bytes 12296 | tf_op jit(solution)/shard_map/ppermute | solution.py:365
  41.8 1.3 %collective-permute-start.13 = (f32[64,128]{1,0:T(8,128)S(1)}, f32[64,128]{1,0:T(8,128)S(1)}, u32[]{:S(2)}, u32[]{:S(2)}) collective-permute-start(f32[64,128]{1,0:T(8,128)S(1)} %get-tuple-element.43), channel_id=1, source_target_pairs={{0,4},{4,0},{8,12},{12,8},{16,20},{20,16},{24,28},{28,24},{1,5},{5... | collective-permute-start | bytes 98312 | tf_op jit(solution)/shard_map/ppermute | solution.py:365
  43.1 6.0 %collective-permute-start.16 = (f32[64,128]{1,0:T(8,128)S(1)}, f32[64,128]{1,0:T(8,128)S(1)}, u32[]{:S(2)}, u32[]{:S(2)}) collective-permute-start(f32[64,128]{1,0:T(8,128)S(1)} %shard_map.71.refs_0_), channel_id=1, source_target_pairs={{0,3},{1,2},{2,1},{3,0},{4,7},{5,6},{6,5},{7,4},{8,11},{9,10},{10,... | collective-permute-start | bytes 98312 | tf_op jit(solution)/shard_map/ppermute | solution.py:365
  44.5 5.0 %collective-permute-start.15 = (f32[64,128]{1,0:T(8,128)S(1)}, f32[64,128]{1,0:T(8,128)S(1)}, u32[]{:S(2)}, u32[]{:S(2)}) collective-permute-start(f32[64,128]{1,0:T(8,128)S(1)} %shard_map.71.refs_0_), channel_id=1, source_target_pairs={{0,2},{1,3},{2,0},{3,1},{4,6},{5,7},{6,4},{7,5},{8,10},{9,11},{10,... | collective-permute-start | bytes 98312 | tf_op jit(solution)/shard_map/ppermute | solution.py:365
  45.2 4.6 %collective-permute-start.14 = (f32[64,128]{1,0:T(8,128)S(1)}, f32[64,128]{1,0:T(8,128)S(1)}, u32[]{:S(2)}, u32[]{:S(2)}) collective-permute-start(f32[64,128]{1,0:T(8,128)S(1)} %shard_map.71.refs_0_), channel_id=1, source_target_pairs={{0,1},{1,0},{2,3},{3,2},{4,5},{5,4},{6,7},{7,6},{8,9},{9,8},{10,11... | collective-permute-start | bytes 98312 | tf_op jit(solution)/shard_map/ppermute | solution.py:365
  49.8 5.2 %collective-permute-start.19 = (f32[64,128]{1,0:T(8,128)S(1)}, f32[64,128]{1,0:T(8,128)S(1)}, u32[]{:S(2)}, u32[]{:S(2)}) collective-permute-start(f32[64,128]{1,0:T(8,128)S(1)} %shard_map.72.refs_0_), channel_id=1, source_target_pairs={{0,24},{4,28},{8,16},{12,20},{16,8},{20,12},{24,0},{28,4},{1,25},{... | collective-permute-start | bytes 98312 | tf_op jit(solution)/shard_map/ppermute | solution.py:365
  51.5 3.9 %collective-permute-start.18 = (f32[64,128]{1,0:T(8,128)S(1)}, f32[64,128]{1,0:T(8,128)S(1)}, u32[]{:S(2)}, u32[]{:S(2)}) collective-permute-start(f32[64,128]{1,0:T(8,128)S(1)} %shard_map.72.refs_0_), channel_id=1, source_target_pairs={{0,16},{4,20},{8,24},{12,28},{16,0},{20,4},{24,8},{28,12},{1,17},{... | collective-permute-start | bytes 98312 | tf_op jit(solution)/shard_map/ppermute | solution.py:365
  52.8 3.9 %collective-permute-start.17 = (f32[64,128]{1,0:T(8,128)S(1)}, f32[64,128]{1,0:T(8,128)S(1)}, u32[]{:S(2)}, u32[]{:S(2)}) collective-permute-start(f32[64,128]{1,0:T(8,128)S(1)} %shard_map.72.refs_0_), channel_id=1, source_target_pairs={{0,8},{4,12},{8,0},{12,4},{16,24},{20,28},{24,16},{28,20},{1,9},{5... | collective-permute-start | bytes 98312 | tf_op jit(solution)/shard_map/ppermute | solution.py:365
  56.7 1.3 %collective-permute-start.20 = (f32[64,128]{1,0:T(8,128)S(1)}, f32[64,128]{1,0:T(8,128)S(1)}, u32[]{:S(2)}, u32[]{:S(2)}) collective-permute-start(f32[64,128]{1,0:T(8,128)S(1)} %shard_map.73.refs_3_), channel_id=1, source_target_pairs={{0,4},{4,0},{8,12},{12,8},{16,20},{20,16},{24,28},{28,24},{1,5},{5... | collective-permute-start | bytes 98312 | tf_op jit(solution)/shard_map/ppermute | solution.py:365
  70.2 5.4 %collective-permute-start.23 = (f32[8,128]{1,0:T(8,128)S(1)}, f32[8,128]{1,0:T(8,128)S(1)}, u32[]{:S(2)}, u32[]{:S(2)}) collective-permute-start(f32[8,128]{1,0:T(8,128)S(1)} %get-tuple-element.48.refs_5_), channel_id=1, source_target_pairs={{0,3},{1,2},{2,1},{3,0},{4,7},{5,6},{6,5},{7,4},{8,11},{9,10},{10,... | collective-permute-start | bytes 12296 | tf_op jit(solution)/shard_map/ppermute | solution.py:365
  72.6 4.5 %collective-permute-start.22 = (f32[8,128]{1,0:T(8,128)S(1)}, f32[8,128]{1,0:T(8,128)S(1)}, u32[]{:S(2)}, u32[]{:S(2)}) collective-permute-start(f32[8,128]{1,0:T(8,128)S(1)} %get-tuple-element.48.refs_5_), channel_id=1, source_target_pairs={{0,2},{1,3},{2,0},{3,1},{4,6},{5,7},{6,4},{7,5},{8,10},{9,11},{10,... | collective-permute-start | bytes 12296 | tf_op jit(solution)/shard_map/ppermute | solution.py:365
  73.3 3.7 %collective-permute-start.21 = (f32[8,128]{1,0:T(8,128)S(1)}, f32[8,128]{1,0:T(8,128)S(1)}, u32[]{:S(2)}, u32[]{:S(2)}) collective-permute-start(f32[8,128]{1,0:T(8,128)S(1)} %get-tuple-element.48.refs_5_), channel_id=1, source_target_pairs={{0,1},{1,0},{2,3},{3,2},{4,5},{5,4},{6,7},{7,6},{8,9},{9,8},{10,11... | collective-permute-start | bytes 12296 | tf_op jit(solution)/shard_map/ppermute | solution.py:365
  84.0 1.2 collective-permute-start.24
  85.2 4.7 %collective-permute-start.27 = (f32[8,512]{1,0:T(8,128)S(1)}, f32[8,512]{1,0:T(8,128)S(1)}, u32[]{:S(2)}, u32[]{:S(2)}) collective-permute-start(f32[8,512]{1,0:T(8,128)S(1)} %shard_map.76.refs_5_), channel_id=1, source_target_pairs={{0,24},{4,28},{8,16},{12,20},{16,8},{20,12},{24,0},{28,4},{1,25},{... | collective-permute-start | bytes 49160 | tf_op jit(solution)/shard_map/ppermute | solution.py:365
  86.7 3.7 %collective-permute-start.26 = (f32[8,512]{1,0:T(8,128)S(1)}, f32[8,512]{1,0:T(8,128)S(1)}, u32[]{:S(2)}, u32[]{:S(2)}) collective-permute-start(f32[8,512]{1,0:T(8,128)S(1)} %shard_map.76.refs_5_), channel_id=1, source_target_pairs={{0,16},{4,20},{8,24},{12,28},{16,0},{20,4},{24,8},{28,12},{1,17},{... | collective-permute-start | bytes 49160 | tf_op jit(solution)/shard_map/ppermute | solution.py:365
  87.2 3.7 %collective-permute-start.25 = (f32[8,512]{1,0:T(8,128)S(1)}, f32[8,512]{1,0:T(8,128)S(1)}, u32[]{:S(2)}, u32[]{:S(2)}) collective-permute-start(f32[8,512]{1,0:T(8,128)S(1)} %shard_map.76.refs_5_), channel_id=1, source_target_pairs={{0,8},{4,12},{8,0},{12,4},{16,24},{20,28},{24,16},{28,20},{1,9},{5... | collective-permute-start | bytes 49160 | tf_op jit(solution)/shard_map/ppermute | solution.py:365
  100.5 5.4 %collective-permute-start.30 = (f32[8,128]{1,0:T(8,128)S(1)}, f32[8,128]{1,0:T(8,128)S(1)}, u32[]{:S(2)}, u32[]{:S(2)}) collective-permute-start(f32[8,128]{1,0:T(8,128)S(1)} %shard_map.77.refs_5_), channel_id=1, source_target_pairs={{0,3},{1,2},{2,1},{3,0},{4,7},{5,6},{6,5},{7,4},{8,11},{9,10},{10,... | collective-permute-start | bytes 12296 | tf_op jit(solution)/shard_map/ppermute | solution.py:365
  102.1 4.5 %collective-permute-start.29 = (f32[8,128]{1,0:T(8,128)S(1)}, f32[8,128]{1,0:T(8,128)S(1)}, u32[]{:S(2)}, u32[]{:S(2)}) collective-permute-start(f32[8,128]{1,0:T(8,128)S(1)} %shard_map.77.refs_5_), channel_id=1, source_target_pairs={{0,2},{1,3},{2,0},{3,1},{4,6},{5,7},{6,4},{7,5},{8,10},{9,11},{10,... | collective-permute-start | bytes 12296 | tf_op jit(solution)/shard_map/ppermute | solution.py:365
  103.2 3.6 %collective-permute-start.28 = (f32[8,128]{1,0:T(8,128)S(1)}, f32[8,128]{1,0:T(8,128)S(1)}, u32[]{:S(2)}, u32[]{:S(2)}) collective-permute-start(f32[8,128]{1,0:T(8,128)S(1)} %shard_map.77.refs_5_), channel_id=1, source_target_pairs={{0,1},{1,0},{2,3},{3,2},{4,5},{5,4},{6,7},{7,6},{8,9},{9,8},{10,11... | collective-permute-start | bytes 12296 | tf_op jit(solution)/shard_map/ppermute | solution.py:365
  113.5 1.2 collective-permute-start.31
  114.7 4.5 %collective-permute-start.32 = (f32[1,512]{1,0:T(1,128)S(1)}, f32[1,512]{1,0:T(1,128)S(1)}, u32[]{:S(2)}, u32[]{:S(2)}) collective-permute-start(f32[1,512]{1,0:T(1,128)S(1)} %get-tuple-element.53), channel_id=1, source_target_pairs={{0,24},{4,28},{8,16},{12,20},{16,8},{20,12},{24,0},{28,4},{1,25},{... | collective-permute-start | bytes 6152 | tf_op jit(solution)/shard_map/ppermute | solution.py:365
  116.5 3.6 %collective-permute-start.33 = (f32[1,512]{1,0:T(1,128)S(1)}, f32[1,512]{1,0:T(1,128)S(1)}, u32[]{:S(2)}, u32[]{:S(2)}) collective-permute-start(f32[1,512]{1,0:T(1,128)S(1)} %get-tuple-element.54), channel_id=1, source_target_pairs={{0,16},{4,20},{8,24},{12,28},{16,0},{20,4},{24,8},{28,12},{1,17},{... | collective-permute-start | bytes 6152 | tf_op jit(solution)/shard_map/ppermute | solution.py:365
  117.8 3.6 %collective-permute-start.34 = (f32[1,512]{1,0:T(1,128)S(1)}, f32[1,512]{1,0:T(1,128)S(1)}, u32[]{:S(2)}, u32[]{:S(2)}) collective-permute-start(f32[1,512]{1,0:T(1,128)S(1)} %get-tuple-element.55), channel_id=1, source_target_pairs={{0,8},{4,12},{8,0},{12,4},{16,24},{20,28},{24,16},{28,20},{1,9},{5... | collective-permute-start | bytes 6152 | tf_op jit(solution)/shard_map/ppermute | solution.py:365

commit v14 on v13

--- a/solution.py
+++ b/solution.py
@@ -170,23 +170,49 @@
     add_shifts(a_ref, block_ref, potential_of(block_ref, width), aug_ref, top_ref)
 
 
-def couple_kernel(nt, width, *refs):
-    a_ref, aug_ref, top_ref, t_refs = refs[0], refs[1], refs[2], refs[3 : 3 + nt]
-    lse_ref, carried_ref, t_ref, pot_ref, mass_ref, e_ref, scores = refs[3 + nt :]
+def block_at(slot):
+    r = lax.axis_index("row")
+    return (r - r % 2) ^ slot
+
+
+def pair_kernel(own_ref, mate_ref, out_ref):
+    core = lax.axis_index("row") % 2
+    size = own_ref.shape[0]
+    for at, ref in ((core, own_ref), (1 - core, mate_ref)):
+        out_ref[pl.ds(pl.multiple_of(at * size, SUB), size), :] = ref[...]
+
+
+def couple_kernel(chips, width, *refs):
+    a_ref, aug_ref, top_ref, pair_ref = refs[:4]
+    far_refs = refs[4 : 4 + chips]
+    lse_ref, carried_ref, t_ref, pot_ref, mass_ref, e_ref, scores = refs[4 + chips :]
+    core = lax.axis_index("row") % 2
     lane = lax.broadcasted_iota(jnp.int32, (LANES, LANES), 1)
-    for g in range(nt):
-        t_ref[g * width : (g + 1) * width, :LANES] = t_refs[g][:width, :]
-        pot_ref[g : g + 1, :] = potential_of(t_refs[g], width)
-        for j in range(0, width, LANES):
-            potential = as_rows(pot_ref[g : g + 1, j : j + LANES])
-            added = jnp.where(lane == 0, potential, jnp.where(lane == 1, 1.0, 0.0))
-            at = g * width + j
-            t_ref[at : at + LANES, LANES:] = added.astype(jnp.bfloat16)
+
+    def place(ref, first, slot):
+        at = pl.multiple_of(slot * width, LANES)
+        t_ref[pl.ds(at, width), :LANES] = ref[first : first + width, :]
+        tail = ref[first + width : first + width + SUB, :].astype(jnp.float32)
+        for j in range(width // LANES):
+            row = tail[j : j + 1, :]
+            added = jnp.where(lane == 0, as_rows(row), jnp.where(lane == 1, 1.0, 0.0))
+            t_ref[pl.ds(at + j * LANES, LANES), LANES:] = added.astype(jnp.bfloat16)
+        rows = [tail[j : j + 1, :] for j in range(width // LANES)]
+        pot_ref[pl.ds(slot, 1), :] = jnp.concatenate(rows, axis=1)
+
+    for k in range(2):
+        place(pair_ref, k * (width + SUB), k)
+    for j in range(0, chips - 2, 2):
+        for ref, chip in ((far_refs[j], j + 1 + core), (far_refs[j + 1], j + 2 - core)):
+            for k in range(2):
+                place(ref, k * (width + SUB), 2 * chip + k)
+    place(far_refs[-2], 0, 2 * (chips - 1) + core)
+    place(far_refs[-1], 0, 2 * (chips - 1) + 1 - core)
     fine = shifted_rows(aug_ref, t_ref, STAGE, lse_ref, top_ref, mass_ref, e_ref, carried_ref)
 
     @pl.when(jnp.logical_not(fine))
     def _():
-        column = [pot_ref[g : g + 1, :] for g in range(nt)]
+        column = [pot_ref[g : g + 1, :] for g in range(2 * chips)]
         exact_rows(a_ref, t_ref, column, scores, lse_ref, None, None, carried_ref)
 
 
@@ -251,10 +277,9 @@
 def rows_kernel(rows_total, *refs):
     a_ref, e_ref, top_ref, t_ref, pot_ref = refs[:5]
     l_refs, (lse_ref, column_ref, weights, scores) = refs[5:-4], refs[-4:]
-    r = lax.axis_index("row")
     nt, width = pot_ref.shape
     column_ref[...] = math.log(rows_total) - log_sum([l[...] for l in l_refs])
-    column = [column_ref[pl.ds(r ^ k, 1), :] for k in range(nt)]
+    column = [column_ref[pl.ds(block_at(k), 1), :] for k in range(nt)]
     change = [column[k] - pot_ref[k : k + 1, :] for k in range(nt)]
     weight = [jnp.exp(x) for x in change]
     for k in range(nt):
@@ -283,8 +308,8 @@
 
 def columns_kernel(ns, cols_total, last, *refs):
     a_ref, e_ref, top_ref, t_ref, pot_ref, l_refs = *refs[:5], refs[5 : 5 + ns]
-    out_refs, (sp_ref, weight_rows, weights, spread_rows, scores) = refs[5 + ns : -5], refs[-5:]
-    c, r = lax.axis_index("col"), lax.axis_index("row")
+    out_refs, (sp_ref, weight_rows, weights, spread_rows, scores, both) = refs[5 + ns : -6], refs[-6:]
+    c = lax.axis_index("col")
     nt, width = pot_ref.shape
     rows = a_ref.shape[0]
     per = rows // ns // LANES
@@ -298,9 +323,9 @@
 
     def store(g, lse):
         if last:
-            out_refs[g % 2][g // 2] = lse
+            both[(g + lax.axis_index("row")) % 2, g // 2] = lse
         else:
-            out_refs[0][pl.ds(r ^ g, 1), :] = lse
+            out_refs[0][pl.ds(block_at(g), 1), :] = lse
 
     sums = jnp.dot(weights[...], e_ref[...], preferred_element_type=jnp.float32)
     mass = sums[0:1, :] + sums[1:2, :]
@@ -310,6 +335,10 @@
     @pl.when(jnp.logical_not(within([mass])))
     def _():
         exact_columns(ns, a_ref, t_ref, sp_ref, spread_rows, scores, store)
+
+    if last:
+        for k in range(2):
+            out_refs[k][...] = both[k]
 
 
 def exact_columns(ns, a_ref, t_ref, sp_ref, spread_rows, scores, store):
@@ -365,6 +394,10 @@
     return lax.ppermute(x, axis, [(i, i ^ k) for i in range(lax.axis_size(axis))])
 
 
+def swap_by_core(x, even, odd):
+    return lax.ppermute(x, "row", [(i, i ^ (odd if i % 2 else even)) for i in range(lax.axis_size("row"))])
+
+
 def exchange(x, axis):
     return [x] + [swap(x, axis, k) for k in range(1, lax.axis_size(axis))]
 
@@ -394,8 +427,11 @@
     groups = width // LANES
     tail = jnp.pad(target_potential.reshape(groups, LANES), ((0, SUB - groups), (0, 0)))
     block = jnp.concatenate([target, tail], axis=0)
+    chips = nt // 2
+    mate = swap(block, "row", 1)
     pieces = exchange(source, "col")
-    far = exchange_chips(block)
+    pair, = call(pair_kernel, [shape((2 * block.shape[0], LANES), bf16)], [block, mate])
+    far = [swap_by_core(pair, 2 * j, 2 * j + 2) for j in range(1, chips - 1, 2)] + [swap(block, "row", nt - 2)]
     order = [0, ns - 2, ns - 1] + list(range(ns - 3, 0, -1)) if ns > 2 else list(range(ns))
     s, a = call(
         functools.partial(project_kernel, order),
@@ -404,15 +440,15 @@
         flops=200 * rows * depth * depth,
     )
     far = [lax.optimization_barrier((x, a))[0] for x in far]
-    blocks = [x for pair in zip(far, [swap(x, "row", 1) for x in far]) for x in pair]
+    far = [x for got in far for x in (got, swap(got, "row", 1))]
     augmented = shape((rows, 2 * depth), bf16)
     aug, top = call(
-        functools.partial(shift_kernel, width), [augmented, tile], [a, far[0]], flops=2 * rows * width * depth
+        functools.partial(shift_kernel, width), [augmented, tile], [a, block], flops=2 * rows * width * depth
     )
     lse, carried, t, pot = call(
-        functools.partial(couple_kernel, nt, width),
+        functools.partial(couple_kernel, chips, width),
         [tile, shape((rows, depth), f32), shape((cols, 2 * depth), bf16), shape((nt, width), f32)],
-        [a, aug, top] + blocks,
+        [a, aug, top, pair] + far,
         [sums, pltpu.VMEM((rows, 2 * STAGE), bf16), row_scores],
         2 * flops,
         exps,
@@ -457,6 +493,7 @@
                 pltpu.VMEM((SUB, rows), bf16),
                 pltpu.VMEM((rows, LANES), f32),
                 pltpu.VMEM((rows, width), f32),
+                pltpu.VMEM((2, nt // 2, 1, width), f32),
             ],
             16 * rows * cols,
         )

time: 122 us -> 123 us (level)
    ppermute x0 -> x1, waiting for transfers between devices: none -> 1.48 us  [swap_by_core(): lax.ppermute(x, 'row', [(i, i ^ (odd if i % 2 else even)) for i in range(...]
    ppermute x35 -> x32, starting transfers between devices: 38.4 us -> 37.4 us  [swap(): lax.ppermute(x, axis, [(i, i ^ k) for i in range(lax.axis_size(axis))])]
    ppermute x35 -> x32, waiting for transfers between devices: 27.3 us -> 26.7 us  [swap(): lax.ppermute(x, axis, [(i, i ^ k) for i in range(lax.axis_size(axis))])]
    pallas_call x14 -> x15, Pallas kernels: 52.9 us -> 53 us  [call(): pl.pallas_call(kernel, out_shape=list(out), in_specs=[vmem] * len(args),...]
  transfers between devices with their start and end apart: 35 -> 33, of which waited for: 30 -> 25; matrix products, arithmetic and copies ran while one was open for 1% -> 0% of each run, Pallas kernels for 1% -> 1%
where the time goes in v14:
time: 123 us
  Pallas kernels  53 us (43%)
  starting transfers between devices  38 us (31%)
  waiting for transfers between devices  28.2 us (23%)
  local copies, waits for them, and re-layouts  1.68 us (1%)
    pallas_call x15, Pallas kernels, call(): pl.pallas_call(kernel, out_shape=list(out), in_specs=[vmem] * len(args),...  53 us
    ppermute x32, starting transfers between devices, swap(): lax.ppermute(x, axis, [(i, i ^ k) for i in range(lax.axis_size(axis))])  37.4 us
    ppermute x32, waiting for transfers between devices, swap(): lax.ppermute(x, axis, [(i, i ^ k) for i in range(lax.axis_size(axis))])  26.7 us
  transfers between devices with their start and end apart: 33, of which 25 were waited for; matrix products, arithmetic and copies ran while one was open for 0% of the time, Pallas kernels for 1%

profile of v14, /device:TPU:0, one launch (start us, length us, event | category | flops | bytes accessed | tf_op | source)
XLA Modules:
  0.0 122.5 jit_solution(11482371561568282329)
XLA Ops:
  0.6 0.9 fusion.1.block_ref.own_ref
  1.6 0.5 collective-permute-start.3
  2.1 4.7 %collective-permute-start.1 = (bf16[256,128]{1,0:T(8,128)(2,1)}, bf16[256,128]{1,0:T(8,128)(2,1)S(1)}, u32[]{:S(2)}, u32[]{:S(2)}) collective-permute-start(bf16[256,128]{1,0:T(8,128)(2,1)} %refs_0_.1), channel_id=1, source_target_pairs={{0,3},{1,2},{2,1},{3,0},{4,7},{5,6},{6,5},{7,4},{8,11},{9,10},{10,... | collective-permute-start | bytes 196616 | tf_op jit(solution)/shard_map/ppermute | solution.py:394
  6.8 0.6 collective-permute-start.2
  7.4 2.6 %collective-permute-start.6 = (bf16[528,128]{1,0:T(8,128)(2,1)S(1)}, bf16[528,128]{1,0:T(8,128)(2,1)S(1)}, u32[]{:S(2)}, u32[]{:S(2)}) collective-permute-start(bf16[528,128]{1,0:T(8,128)(2,1)S(1)} %fusion.1.block_ref.own_ref), channel_id=1, source_target_pairs={{0,24},{4,28},{8,16},{12,20},{16,8},{20,12},{24,0},{28,4},{1,25},{... | collective-permute-start | bytes 405512 | tf_op jit(solution)/shard_map/ppermute | solution.py:394
  10.0 0.6 collective-permute-start.4
  10.6 2.4 %collective-permute-done.refs_1_ = bf16[256,128]{1,0:T(8,128)(2,1)S(1)} collective-permute-done((bf16[256,128]{1,0:T(8,128)(2,1)}, bf16[256,128]{1,0:T(8,128)(2,1)S(1)}, u32[]{:S(2)}, u32[]{:S(2)}) %collective-permute-start) | collective-permute-done | bytes 65568 | tf_op jit(solution)/shard_map/ppermute | solution.py:394
  13.0 0.8 copy-done
  13.9 0.8 copy-done.1
  14.7 0.4 shard_map.67
  15.1 1.5 %collective-permute-done.4.refs_4_ = bf16[1056,128]{1,0:T(8,128)(2,1)S(1)} collective-permute-done((bf16[1056,128]{1,0:T(8,128)(2,1)S(1)}, bf16[1056,128]{1,0:T(8,128)(2,1)S(1)}, u32[]{:S(2)}, u32[]{:S(2)}) %collective-permute-start.4) | collective-permute-done | bytes 270368 | tf_op jit(solution)/shard_map/ppermute | solution.py:398
  16.6 0.5 collective-permute-start.7
  17.1 0.6 shard_map.68
  17.7 0.6 collective-permute-done.7.refs_7_
  18.3 15.3 %shard_map.70 = (f32[8,128]{1,0:T(8,128)S(1)}, f32[1024,128]{1,0:T(8,128)S(1)}, bf16[4096,256]{1,0:T(8,128)(2,1)S(1)}, f32[8,512]{1,0:T(8,128)S(1)}) custom-call(bf16[1024,128]{1,0:T(8,128)(2,1)S(1)} %get-tuple-element.29.a_ref.refs_0_, bf16[1024,256]{1,0:T(8,128)(2,1)S(1)} %get-tuple-element.30.refs_1_, f32[8,128]{1,0:T(8,128)S(1)} %get-tuple-element.31.refs_2_, ...), custom_call_target="tpu_custom_call" | custom-call | flops 2147483648 | bytes 4513792 | tf_op jit(solution)/shard_map/pallas_call | solution.py:382
  33.7 3.6 %collective-permute-start.10 = (f32[8,128]{1,0:T(8,128)S(1)}, f32[8,128]{1,0:T(8,128)S(1)}, u32[]{:S(2)}, u32[]{:S(2)}) collective-permute-start(f32[8,128]{1,0:T(8,128)S(1)} %get-tuple-element.36.refs_1_), channel_id=1, source_target_pairs={{0,3},{1,2},{2,1},{3,0},{4,7},{5,6},{6,5},{7,4},{8,11},{9,10},{10,... | collective-permute-start | bytes 12296 | tf_op jit(solution)/shard_map/ppermute | solution.py:394
  37.3 0.8 collective-permute-start.8
  38.1 1.0 collective-permute-done.10.refs_4_
  39.1 2.7 %collective-permute-done.9.refs_3_ = f32[8,128]{1,0:T(8,128)S(1)} collective-permute-done((f32[8,128]{1,0:T(8,128)S(1)}, f32[8,128]{1,0:T(8,128)S(1)}, u32[]{:S(2)}, u32[]{:S(2)}) %collective-permute-start.9) | collective-permute-done | bytes 4128 | tf_op jit(solution)/shard_map/ppermute | solution.py:394
  41.8 0.5 shard_map.71
  42.4 0.1 collective-permute-start.11
  42.5 1.2 collective-permute-done.11.refs_1_
  43.7 1.5 %collective-permute-start.14 = (f32[64,128]{1,0:T(8,128)S(1)}, f32[64,128]{1,0:T(8,128)S(1)}, u32[]{:S(2)}, u32[]{:S(2)}) collective-permute-start(f32[64,128]{1,0:T(8,128)S(1)} %shard_map.72.refs_0_), channel_id=1, source_target_pairs={{0,3},{1,2},{2,1},{3,0},{4,7},{5,6},{6,5},{7,4},{8,11},{9,10},{10,... | collective-permute-start | bytes 98312 | tf_op jit(solution)/shard_map/ppermute | solution.py:394
  45.1 0.6 collective-permute-start.13
  45.8 2.3 %collective-permute-start.12 = (f32[64,128]{1,0:T(8,128)S(1)}, f32[64,128]{1,0:T(8,128)S(1)}, u32[]{:S(2)}, u32[]{:S(2)}) collective-permute-start(f32[64,128]{1,0:T(8,128)S(1)} %shard_map.72.refs_0_), channel_id=1, source_target_pairs={{0,1},{1,0},{2,3},{3,2},{4,5},{5,4},{6,7},{7,6},{8,9},{9,8},{10,11... | collective-permute-start | bytes 98312 | tf_op jit(solution)/shard_map/ppermute | solution.py:394
  48.0 1.6 %collective-permute-done.14.refs_3_ = f32[64,128]{1,0:T(8,128)S(1)} collective-permute-done((f32[64,128]{1,0:T(8,128)S(1)}, f32[64,128]{1,0:T(8,128)S(1)}, u32[]{:S(2)}, u32[]{:S(2)}) %collective-permute-start.14) | collective-permute-done | bytes 32800 | tf_op jit(solution)/shard_map/ppermute | solution.py:394
  49.7 0.4 collective-permute-done.13.refs_2_
  50.1 0.2 collective-permute-done.12.refs_1_
  50.3 1.5 %collective-permute-start.17 = (f32[64,128]{1,0:T(8,128)S(1)}, f32[64,128]{1,0:T(8,128)S(1)}, u32[]{:S(2)}, u32[]{:S(2)}) collective-permute-start(f32[64,128]{1,0:T(8,128)S(1)} %shard_map.73.refs_0_), channel_id=1, source_target_pairs={{0,24},{4,28},{8,16},{12,20},{16,8},{20,12},{24,0},{28,4},{1,25},{... | collective-permute-start | bytes 98312 | tf_op jit(solution)/shard_map/ppermute | solution.py:394
  51.8 1.5 %collective-permute-start.16 = (f32[64,128]{1,0:T(8,128)S(1)}, f32[64,128]{1,0:T(8,128)S(1)}, u32[]{:S(2)}, u32[]{:S(2)}) collective-permute-start(f32[64,128]{1,0:T(8,128)S(1)} %shard_map.73.refs_0_), channel_id=1, source_target_pairs={{0,16},{4,20},{8,24},{12,28},{16,0},{20,4},{24,8},{28,12},{1,17},{... | collective-permute-start | bytes 98312 | tf_op jit(solution)/shard_map/ppermute | solution.py:394
  53.3 0.6 collective-permute-start.15
  53.9 1.4 %collective-permute-done.17.refs_3_ = f32[64,128]{1,0:T(8,128)S(1)} collective-permute-done((f32[64,128]{1,0:T(8,128)S(1)}, f32[64,128]{1,0:T(8,128)S(1)}, u32[]{:S(2)}, u32[]{:S(2)}) %collective-permute-start.17) | collective-permute-done | bytes 32800 | tf_op jit(solution)/shard_map/ppermute | solution.py:394
  55.3 0.4 collective-permute-done.16.refs_2_
  55.7 1.5 %collective-permute-done.15.refs_1_ = f32[64,128]{1,0:T(8,128)S(1)} collective-permute-done((f32[64,128]{1,0:T(8,128)S(1)}, f32[64,128]{1,0:T(8,128)S(1)}, u32[]{:S(2)}, u32[]{:S(2)}) %collective-permute-start.15) | collective-permute-done | bytes 32800 | tf_op jit(solution)/shard_map/ppermute | solution.py:394
  57.4 1.2 collective-permute-done.18.refs_4_
  58.6 12.2 %shard_map.75 = (f32[128,128]{1,0:T(8,128)}, bf16[1024,128]{1,0:T(8,128)(2,1)S(1)}, f32[8,128]{1,0:T(8,128)S(1)}, f32[8,128]{1,0:T(8,128)S(1)}, bf16[1024,4096]{1,0:T(8,128)(2,1)S(1)}) custom-call(bf16[1024,128]{1,0:T(8,128)(2,1)S(1)} %get-tuple-element.28.refs_0_, bf16[4096,256]{1,0:T(8,128)(2,1)S(1)} %get-tuple-element.34.refs_1_.refs_3_, ...), custom_call_target="tpu_custom_call" | custom-call | flops 1073741824 | bytes 11165696 | tf_op jit(solution)/shard_map/pallas_call | solution.py:382
  70.8 2.3 %collective-permute-start.21 = (f32[8,128]{1,0:T(8,128)S(1)}, f32[8,128]{1,0:T(8,128)S(1)}, u32[]{:S(2)}, u32[]{:S(2)}) collective-permute-start(f32[8,128]{1,0:T(8,128)S(1)} %get-tuple-element.44.refs_5_), channel_id=1, source_target_pairs={{0,3},{1,2},{2,1},{3,0},{4,7},{5,6},{6,5},{7,4},{8,11},{9,10},{10,... | collective-permute-start | bytes 12296 | tf_op jit(solution)/shard_map/ppermute | solution.py:394
  73.1 0.8 collective-permute-start.20
  73.9 1.3 %collective-permute-start.19 = (f32[8,128]{1,0:T(8,128)S(1)}, f32[8,128]{1,0:T(8,128)S(1)}, u32[]{:S(2)}, u32[]{:S(2)}) collective-permute-start(f32[8,128]{1,0:T(8,128)S(1)} %get-tuple-element.44.refs_5_), channel_id=1, source_target_pairs={{0,1},{1,0},{2,3},{3,2},{4,5},{5,4},{6,7},{7,6},{8,9},{9,8},{10,11... | collective-permute-start | bytes 12296 | tf_op jit(solution)/shard_map/ppermute | solution.py:394
  75.2 1.0 collective-permute-done.21.refs_8_
  76.2 1.4 %collective-permute-done.20.refs_7_ = f32[8,128]{1,0:T(8,128)S(1)} collective-permute-done((f32[8,128]{1,0:T(8,128)S(1)}, f32[8,128]{1,0:T(8,128)S(1)}, u32[]{:S(2)}, u32[]{:S(2)}) %collective-permute-start.20) | collective-permute-done | bytes 4128 | tf_op jit(solution)/shard_map/ppermute | solution.py:394
  77.6 7.0 %shard_map.76 = (f32[8,512]{1,0:T(8,128)S(1)}, f32[8,128]{1,0:T(8,128)}) custom-call(bf16[1024,128]{1,0:T(8,128)(2,1)S(1)} %get-tuple-element.41.refs_0_, bf16[1024,4096]{1,0:T(8,128)(2,1)S(1)} %get-tuple-element.42.refs_1_, f32[8,128]{1,0:T(8,128)S(1)} %get-tuple-element.43.refs_2_, bf16[4096,256]{1,0:T(8,128)(2,1)S(1)} %get-tuple-element.34.refs_1_.refs_3_, ...), custom_call_target="tpu_custom_call" | custom-call | flops 67108864 | bytes 10805248 | tf_op jit(solution)/shard_map/pallas_call | solution.py:382
  84.6 1.2 collective-permute-done.22.refs_1_
  85.8 0.9 collective-permute-start.25
  86.7 1.2 collective-permute-start.24
  87.8 1.5 %collective-permute-start.23 = (f32[8,512]{1,0:T(8,128)S(1)}, f32[8,512]{1,0:T(8,128)S(1)}, u32[]{:S(2)}, u32[]{:S(2)}) collective-permute-start(f32[8,512]{1,0:T(8,128)S(1)} %shard_map.77.refs_5_), channel_id=1, source_target_pairs={{0,8},{4,12},{8,0},{12,4},{16,24},{20,28},{24,16},{28,20},{1,9},{5... | collective-permute-start | bytes 49160 | tf_op jit(solution)/shard_map/ppermute | solution.py:394
  89.3 1.3 %collective-permute-done.25.refs_8_ = f32[8,512]{1,0:T(8,128)S(1)} collective-permute-done((f32[8,512]{1,0:T(8,128)S(1)}, f32[8,512]{1,0:T(8,128)S(1)}, u32[]{:S(2)}, u32[]{:S(2)}) %collective-permute-start.25) | collective-permute-done | bytes 16416 | tf_op jit(solution)/shard_map/ppermute | solution.py:394
  90.6 1.0 collective-permute-done.23.refs_6_
  91.6 9.5 %shard_map.78.refs_5_ = f32[8,128]{1,0:T(8,128)S(1)} custom-call(bf16[1024,128]{1,0:T(8,128)(2,1)S(1)} %get-tuple-element.41.refs_0_, bf16[1024,4096]{1,0:T(8,128)(2,1)S(1)} %get-tuple-element.42.refs_1_, f32[8,128]{1,0:T(8,128)S(1)} %get-tuple-element.43.refs_2_, bf16[4096,256]{1,0:T(8,128)(2,1)S(1)} %get-tuple-element.34.refs_1_.refs_3_, ...), custom_call_target="tpu_custom_call" | custom-call | flops 67108864 | bytes 10838016 | tf_op jit(solution)/shard_map/pallas_call | solution.py:382
  101.1 1.5 %collective-permute-start.28 = (f32[8,128]{1,0:T(8,128)S(1)}, f32[8,128]{1,0:T(8,128)S(1)}, u32[]{:S(2)}, u32[]{:S(2)}) collective-permute-start(f32[8,128]{1,0:T(8,128)S(1)} %shard_map.78.refs_5_), channel_id=1, source_target_pairs={{0,3},{1,2},{2,1},{3,0},{4,7},{5,6},{6,5},{7,4},{8,11},{9,10},{10,... | collective-permute-start | bytes 12296 | tf_op jit(solution)/shard_map/ppermute | solution.py:394
  102.6 1.1 collective-permute-start.27
  103.8 1.8 %collective-permute-start.26 = (f32[8,128]{1,0:T(8,128)S(1)}, f32[8,128]{1,0:T(8,128)S(1)}, u32[]{:S(2)}, u32[]{:S(2)}) collective-permute-start(f32[8,128]{1,0:T(8,128)S(1)} %shard_map.78.refs_5_), channel_id=1, source_target_pairs={{0,1},{1,0},{2,3},{3,2},{4,5},{5,4},{6,7},{7,6},{8,9},{9,8},{10,11... | collective-permute-start | bytes 12296 | tf_op jit(solution)/shard_map/ppermute | solution.py:394
  105.5 1.0 collective-permute-done.28.refs_8_
  106.5 0.6 collective-permute-done.27.refs_7_
  107.2 0.2 collective-permute-done.26.refs_6_
  107.4 6.8 %shard_map.79 = (f32[4,1,512]{2,1,0:T(1,128)S(1)}, f32[4,1,512]{2,1,0:T(1,128)S(1)}, f32[8,128]{1,0:T(8,128)}) custom-call(bf16[1024,128]{1,0:T(8,128)(2,1)S(1)} %get-tuple-element.41.refs_0_, bf16[1024,4096]{1,0:T(8,128)(2,1)S(1)} %get-tuple-element.42.refs_1_, f32[8,128]{1,0:T(8,128)S(1)} %get-tuple-element.43.refs_2_, ...), custom_call_target="tpu_custom_call" | custom-call | flops 67108864 | bytes 10805248 | tf_op jit(solution)/shard_map/pallas_call | solution.py:382
  114.1 1.2 collective-permute-done.29.y_ref
  115.3 1.5 %collective-permute-start.30 = (f32[1,512]{1,0:T(1,128)S(1)}, f32[1,512]{1,0:T(1,128)S(1)}, u32[]{:S(2)}, u32[]{:S(2)}) collective-permute-start(f32[1,512]{1,0:T(1,128)S(1)} %get-tuple-element.49), channel_id=1, source_target_pairs={{0,24},{4,28},{8,16},{12,20},{16,8},{20,12},{24,0},{28,4},{1,25},{... | collective-permute-start | bytes 6152 | tf_op jit(solution)/shard_map/ppermute | solution.py:394
  116.8 1.5 %collective-permute-start.31 = (f32[1,512]{1,0:T(1,128)S(1)}, f32[1,512]{1,0:T(1,128)S(1)}, u32[]{:S(2)}, u32[]{:S(2)}) collective-permute-start(f32[1,512]{1,0:T(1,128)S(1)} %get-tuple-element.50), channel_id=1, source_target_pairs={{0,16},{4,20},{8,24},{12,28},{16,0},{20,4},{24,8},{28,12},{1,17},{... | collective-permute-start | bytes 6152 | tf_op jit(solution)/shard_map/ppermute | solution.py:394
  118.3 0.6 collective-permute-start.32
  118.9 1.0 collective-permute-done.30.refs_0_
  119.9 0.5 collective-permute-done.31.refs_1_
  120.4 1.5 %collective-permute-done.32.refs_2_ = f32[1,512]{1,0:T(1,128)S(1)} collective-permute-done((f32[1,512]{1,0:T(1,128)S(1)}, f32[1,512]{1,0:T(1,128)S(1)}, u32[]{:S(2)}, u32[]{:S(2)}) %collective-permute-start.32) | collective-permute-done | bytes 2080 | tf_op jit(solution)/shard_map/ppermute | solution.py:394
  121.9 0.6 shard_map.81
  (22 shorter events, 0.2 us)
Async XLA Ops:
  1.6 8.4 %collective-permute-start.3 = (bf16[528,128]{1,0:T(8,128)(2,1)S(1)}, bf16[528,128]{1,0:T(8,128)(2,1)S(1)}, u32[]{:S(2)}, u32[]{:S(2)}) collective-permute-start(bf16[528,128]{1,0:T(8,128)(2,1)S(1)} %fusion.1.block_ref.own_ref), channel_id=1, source_target_pairs={{0,4},{4,0},{8,12},{12,8},{16,20},{20,16},{24,28},{28,24},{1,5},{5... | collective-permute-start | bytes 405512 | tf_op jit(solution)/shard_map/ppermute | solution.py:394
  2.1 8.6 %collective-permute-start.1 = (bf16[256,128]{1,0:T(8,128)(2,1)}, bf16[256,128]{1,0:T(8,128)(2,1)S(1)}, u32[]{:S(2)}, u32[]{:S(2)}) collective-permute-start(bf16[256,128]{1,0:T(8,128)(2,1)} %refs_0_.1), channel_id=1, source_target_pairs={{0,3},{1,2},{2,1},{3,0},{4,7},{5,6},{6,5},{7,4},{8,11},{9,10},{10,... | collective-permute-start | bytes 196616 | tf_op jit(solution)/shard_map/ppermute | solution.py:394
  6.8 6.3 %collective-permute-start = (bf16[256,128]{1,0:T(8,128)(2,1)}, bf16[256,128]{1,0:T(8,128)(2,1)S(1)}, u32[]{:S(2)}, u32[]{:S(2)}) collective-permute-start(bf16[256,128]{1,0:T(8,128)(2,1)} %refs_0_.1), channel_id=1, source_target_pairs={{0,2},{1,3},{2,0},{3,1},{4,6},{5,7},{6,4},{7,5},{8,10},{9,11},{10,... | collective-permute-start | bytes 196616 | tf_op jit(solution)/shard_map/ppermute | solution.py:394
  6.8 6.3 %collective-permute-start.2 = (bf16[256,128]{1,0:T(8,128)(2,1)}, bf16[256,128]{1,0:T(8,128)(2,1)S(1)}, u32[]{:S(2)}, u32[]{:S(2)}) collective-permute-start(bf16[256,128]{1,0:T(8,128)(2,1)} %refs_0_.1), channel_id=1, source_target_pairs={{0,1},{1,0},{2,3},{3,2},{4,5},{5,4},{6,7},{7,6},{8,9},{9,8},{10,11... | collective-permute-start | bytes 196616 | tf_op jit(solution)/shard_map/ppermute | solution.py:394
  7.4 9.2 %collective-permute-start.6 = (bf16[528,128]{1,0:T(8,128)(2,1)S(1)}, bf16[528,128]{1,0:T(8,128)(2,1)S(1)}, u32[]{:S(2)}, u32[]{:S(2)}) collective-permute-start(bf16[528,128]{1,0:T(8,128)(2,1)S(1)} %fusion.1.block_ref.own_ref), channel_id=1, source_target_pairs={{0,24},{4,28},{8,16},{12,20},{16,8},{20,12},{24,0},{28,4},{1,25},{... | collective-permute-start | bytes 405512 | tf_op jit(solution)/shard_map/ppermute | solution.py:394
  10.0 6.5 %collective-permute-start.4 = (bf16[1056,128]{1,0:T(8,128)(2,1)S(1)}, bf16[1056,128]{1,0:T(8,128)(2,1)S(1)}, u32[]{:S(2)}, u32[]{:S(2)}) collective-permute-start(bf16[1056,128]{1,0:T(8,128)(2,1)S(1)} %shard_map.69.refs_3_), channel_id=1, source_target_pairs={{0,8},{4,20},{8,0},{12,28},{16,24},{20,4},{24,16},{28,12},{1,9},{5... | collective-permute-start | bytes 811016 | tf_op jit(solution)/shard_map/ppermute | solution.py:398
  13.0 0.8 copy-start
  13.9 0.8 copy-start.1
  16.6 1.7 %collective-permute-start.5 = (bf16[1056,128]{1,0:T(8,128)(2,1)S(1)}, bf16[1056,128]{1,0:T(8,128)(2,1)S(1)}, u32[]{:S(2)}, u32[]{:S(2)}) collective-permute-start(bf16[1056,128]{1,0:T(8,128)(2,1)S(1)} %collective-permute-done.4.refs_4_), channel_id=1, source_target_pairs={{0,4},{4,0},{8,12},{12,8},{16,20},{20,16},{24,28},{28,24},{1,5},{5... | collective-permute-start | bytes 811016 | tf_op jit(solution)/shard_map/ppermute | solution.py:394
  16.6 1.7 %collective-permute-start.7 = (bf16[528,128]{1,0:T(8,128)(2,1)S(1)}, bf16[528,128]{1,0:T(8,128)(2,1)S(1)}, u32[]{:S(2)}, u32[]{:S(2)}) collective-permute-start(bf16[528,128]{1,0:T(8,128)(2,1)S(1)} %collective-permute-done.6.refs_6_), channel_id=1, source_target_pairs={{0,4},{4,0},{8,12},{12,8},{16,20},{20,16},{24,28},{28,24},{1,5},{5... | collective-permute-start | bytes 405512 | tf_op jit(solution)/shard_map/ppermute | solution.py:394
  33.7 5.5 %collective-permute-start.10 = (f32[8,128]{1,0:T(8,128)S(1)}, f32[8,128]{1,0:T(8,128)S(1)}, u32[]{:S(2)}, u32[]{:S(2)}) collective-permute-start(f32[8,128]{1,0:T(8,128)S(1)} %get-tuple-element.36.refs_1_), channel_id=1, source_target_pairs={{0,3},{1,2},{2,1},{3,0},{4,7},{5,6},{6,5},{7,4},{8,11},{9,10},{10,... | collective-permute-start | bytes 12296 | tf_op jit(solution)/shard_map/ppermute | solution.py:394
  37.3 4.5 %collective-permute-start.9 = (f32[8,128]{1,0:T(8,128)S(1)}, f32[8,128]{1,0:T(8,128)S(1)}, u32[]{:S(2)}, u32[]{:S(2)}) collective-permute-start(f32[8,128]{1,0:T(8,128)S(1)} %get-tuple-element.36.refs_1_), channel_id=1, source_target_pairs={{0,2},{1,3},{2,0},{3,1},{4,6},{5,7},{6,4},{7,5},{8,10},{9,11},{10,... | collective-permute-start | bytes 12296 | tf_op jit(solution)/shard_map/ppermute | solution.py:394
  37.3 4.5 %collective-permute-start.8 = (f32[8,128]{1,0:T(8,128)S(1)}, f32[8,128]{1,0:T(8,128)S(1)}, u32[]{:S(2)}, u32[]{:S(2)}) collective-permute-start(f32[8,128]{1,0:T(8,128)S(1)} %get-tuple-element.36.refs_1_), channel_id=1, source_target_pairs={{0,1},{1,0},{2,3},{3,2},{4,5},{5,4},{6,7},{7,6},{8,9},{9,8},{10,11... | collective-permute-start | bytes 12296 | tf_op jit(solution)/shard_map/ppermute | solution.py:394
  42.4 1.3 %collective-permute-start.11 = (f32[64,128]{1,0:T(8,128)S(1)}, f32[64,128]{1,0:T(8,128)S(1)}, u32[]{:S(2)}, u32[]{:S(2)}) collective-permute-start(f32[64,128]{1,0:T(8,128)S(1)} %get-tuple-element.39), channel_id=1, source_target_pairs={{0,4},{4,0},{8,12},{12,8},{16,20},{20,16},{24,28},{28,24},{1,5},{5... | collective-permute-start | bytes 98312 | tf_op jit(solution)/shard_map/ppermute | solution.py:394
  43.7 6.0 %collective-permute-start.14 = (f32[64,128]{1,0:T(8,128)S(1)}, f32[64,128]{1,0:T(8,128)S(1)}, u32[]{:S(2)}, u32[]{:S(2)}) collective-permute-start(f32[64,128]{1,0:T(8,128)S(1)} %shard_map.72.refs_0_), channel_id=1, source_target_pairs={{0,3},{1,2},{2,1},{3,0},{4,7},{5,6},{6,5},{7,4},{8,11},{9,10},{10,... | collective-permute-start | bytes 98312 | tf_op jit(solution)/shard_map/ppermute | solution.py:394
  45.1 5.0 %collective-permute-start.13 = (f32[64,128]{1,0:T(8,128)S(1)}, f32[64,128]{1,0:T(8,128)S(1)}, u32[]{:S(2)}, u32[]{:S(2)}) collective-permute-start(f32[64,128]{1,0:T(8,128)S(1)} %shard_map.72.refs_0_), channel_id=1, source_target_pairs={{0,2},{1,3},{2,0},{3,1},{4,6},{5,7},{6,4},{7,5},{8,10},{9,11},{10,... | collective-permute-start | bytes 98312 | tf_op jit(solution)/shard_map/ppermute | solution.py:394
  45.8 4.6 %collective-permute-start.12 = (f32[64,128]{1,0:T(8,128)S(1)}, f32[64,128]{1,0:T(8,128)S(1)}, u32[]{:S(2)}, u32[]{:S(2)}) collective-permute-start(f32[64,128]{1,0:T(8,128)S(1)} %shard_map.72.refs_0_), channel_id=1, source_target_pairs={{0,1},{1,0},{2,3},{3,2},{4,5},{5,4},{6,7},{7,6},{8,9},{9,8},{10,11... | collective-permute-start | bytes 98312 | tf_op jit(solution)/shard_map/ppermute | solution.py:394
  50.3 5.0 %collective-permute-start.17 = (f32[64,128]{1,0:T(8,128)S(1)}, f32[64,128]{1,0:T(8,128)S(1)}, u32[]{:S(2)}, u32[]{:S(2)}) collective-permute-start(f32[64,128]{1,0:T(8,128)S(1)} %shard_map.73.refs_0_), channel_id=1, source_target_pairs={{0,24},{4,28},{8,16},{12,20},{16,8},{20,12},{24,0},{28,4},{1,25},{... | collective-permute-start | bytes 98312 | tf_op jit(solution)/shard_map/ppermute | solution.py:394
  51.8 3.9 %collective-permute-start.16 = (f32[64,128]{1,0:T(8,128)S(1)}, f32[64,128]{1,0:T(8,128)S(1)}, u32[]{:S(2)}, u32[]{:S(2)}) collective-permute-start(f32[64,128]{1,0:T(8,128)S(1)} %shard_map.73.refs_0_), channel_id=1, source_target_pairs={{0,16},{4,20},{8,24},{12,28},{16,0},{20,4},{24,8},{28,12},{1,17},{... | collective-permute-start | bytes 98312 | tf_op jit(solution)/shard_map/ppermute | solution.py:394
  53.3 3.9 %collective-permute-start.15 = (f32[64,128]{1,0:T(8,128)S(1)}, f32[64,128]{1,0:T(8,128)S(1)}, u32[]{:S(2)}, u32[]{:S(2)}) collective-permute-start(f32[64,128]{1,0:T(8,128)S(1)} %shard_map.73.refs_0_), channel_id=1, source_target_pairs={{0,8},{4,12},{8,0},{12,4},{16,24},{20,28},{24,16},{28,20},{1,9},{5... | collective-permute-start | bytes 98312 | tf_op jit(solution)/shard_map/ppermute | solution.py:394
  57.3 1.3 %collective-permute-start.18 = (f32[64,128]{1,0:T(8,128)S(1)}, f32[64,128]{1,0:T(8,128)S(1)}, u32[]{:S(2)}, u32[]{:S(2)}) collective-permute-start(f32[64,128]{1,0:T(8,128)S(1)} %shard_map.74.refs_3_), channel_id=1, source_target_pairs={{0,4},{4,0},{8,12},{12,8},{16,20},{20,16},{24,28},{28,24},{1,5},{5... | collective-permute-start | bytes 98312 | tf_op jit(solution)/shard_map/ppermute | solution.py:394
  70.8 5.4 %collective-permute-start.21 = (f32[8,128]{1,0:T(8,128)S(1)}, f32[8,128]{1,0:T(8,128)S(1)}, u32[]{:S(2)}, u32[]{:S(2)}) collective-permute-start(f32[8,128]{1,0:T(8,128)S(1)} %get-tuple-element.44.refs_5_), channel_id=1, source_target_pairs={{0,3},{1,2},{2,1},{3,0},{4,7},{5,6},{6,5},{7,4},{8,11},{9,10},{10,... | collective-permute-start | bytes 12296 | tf_op jit(solution)/shard_map/ppermute | solution.py:394
  73.1 4.5 %collective-permute-start.20 = (f32[8,128]{1,0:T(8,128)S(1)}, f32[8,128]{1,0:T(8,128)S(1)}, u32[]{:S(2)}, u32[]{:S(2)}) collective-permute-start(f32[8,128]{1,0:T(8,128)S(1)} %get-tuple-element.44.refs_5_), channel_id=1, source_target_pairs={{0,2},{1,3},{2,0},{3,1},{4,6},{5,7},{6,4},{7,5},{8,10},{9,11},{10,... | collective-permute-start | bytes 12296 | tf_op jit(solution)/shard_map/ppermute | solution.py:394
  73.9 3.7 %collective-permute-start.19 = (f32[8,128]{1,0:T(8,128)S(1)}, f32[8,128]{1,0:T(8,128)S(1)}, u32[]{:S(2)}, u32[]{:S(2)}) collective-permute-start(f32[8,128]{1,0:T(8,128)S(1)} %get-tuple-element.44.refs_5_), channel_id=1, source_target_pairs={{0,1},{1,0},{2,3},{3,2},{4,5},{5,4},{6,7},{7,6},{8,9},{9,8},{10,11... | collective-permute-start | bytes 12296 | tf_op jit(solution)/shard_map/ppermute | solution.py:394
  84.5 1.2 collective-permute-start.22
  85.8 4.8 %collective-permute-start.25 = (f32[8,512]{1,0:T(8,128)S(1)}, f32[8,512]{1,0:T(8,128)S(1)}, u32[]{:S(2)}, u32[]{:S(2)}) collective-permute-start(f32[8,512]{1,0:T(8,128)S(1)} %shard_map.77.refs_5_), channel_id=1, source_target_pairs={{0,24},{4,28},{8,16},{12,20},{16,8},{20,12},{24,0},{28,4},{1,25},{... | collective-permute-start | bytes 49160 | tf_op jit(solution)/shard_map/ppermute | solution.py:394
  86.7 3.9 %collective-permute-start.24 = (f32[8,512]{1,0:T(8,128)S(1)}, f32[8,512]{1,0:T(8,128)S(1)}, u32[]{:S(2)}, u32[]{:S(2)}) collective-permute-start(f32[8,512]{1,0:T(8,128)S(1)} %shard_map.77.refs_5_), channel_id=1, source_target_pairs={{0,16},{4,20},{8,24},{12,28},{16,0},{20,4},{24,8},{28,12},{1,17},{... | collective-permute-start | bytes 49160 | tf_op jit(solution)/shard_map/ppermute | solution.py:394
  87.8 3.7 %collective-permute-start.23 = (f32[8,512]{1,0:T(8,128)S(1)}, f32[8,512]{1,0:T(8,128)S(1)}, u32[]{:S(2)}, u32[]{:S(2)}) collective-permute-start(f32[8,512]{1,0:T(8,128)S(1)} %shard_map.77.refs_5_), channel_id=1, source_target_pairs={{0,8},{4,12},{8,0},{12,4},{16,24},{20,28},{24,16},{28,20},{1,9},{5... | collective-permute-start | bytes 49160 | tf_op jit(solution)/shard_map/ppermute | solution.py:394
  101.1 5.4 %collective-permute-start.28 = (f32[8,128]{1,0:T(8,128)S(1)}, f32[8,128]{1,0:T(8,128)S(1)}, u32[]{:S(2)}, u32[]{:S(2)}) collective-permute-start(f32[8,128]{1,0:T(8,128)S(1)} %shard_map.78.refs_5_), channel_id=1, source_target_pairs={{0,3},{1,2},{2,1},{3,0},{4,7},{5,6},{6,5},{7,4},{8,11},{9,10},{10,... | collective-permute-start | bytes 12296 | tf_op jit(solution)/shard_map/ppermute | solution.py:394
  102.6 4.5 %collective-permute-start.27 = (f32[8,128]{1,0:T(8,128)S(1)}, f32[8,128]{1,0:T(8,128)S(1)}, u32[]{:S(2)}, u32[]{:S(2)}) collective-permute-start(f32[8,128]{1,0:T(8,128)S(1)} %shard_map.78.refs_5_), channel_id=1, source_target_pairs={{0,2},{1,3},{2,0},{3,1},{4,6},{5,7},{6,4},{7,5},{8,10},{9,11},{10,... | collective-permute-start | bytes 12296 | tf_op jit(solution)/shard_map/ppermute | solution.py:394
  103.8 3.6 %collective-permute-start.26 = (f32[8,128]{1,0:T(8,128)S(1)}, f32[8,128]{1,0:T(8,128)S(1)}, u32[]{:S(2)}, u32[]{:S(2)}) collective-permute-start(f32[8,128]{1,0:T(8,128)S(1)} %shard_map.78.refs_5_), channel_id=1, source_target_pairs={{0,1},{1,0},{2,3},{3,2},{4,5},{5,4},{6,7},{7,6},{8,9},{9,8},{10,11... | collective-permute-start | bytes 12296 | tf_op jit(solution)/shard_map/ppermute | solution.py:394
  114.1 1.2 collective-permute-start.29
  115.3 4.5 %collective-permute-start.30 = (f32[1,512]{1,0:T(1,128)S(1)}, f32[1,512]{1,0:T(1,128)S(1)}, u32[]{:S(2)}, u32[]{:S(2)}) collective-permute-start(f32[1,512]{1,0:T(1,128)S(1)} %get-tuple-element.49), channel_id=1, source_target_pairs={{0,24},{4,28},{8,16},{12,20},{16,8},{20,12},{24,0},{28,4},{1,25},{... | collective-permute-start | bytes 6152 | tf_op jit(solution)/shard_map/ppermute | solution.py:394
  116.8 3.6 %collective-permute-start.31 = (f32[1,512]{1,0:T(1,128)S(1)}, f32[1,512]{1,0:T(1,128)S(1)}, u32[]{:S(2)}, u32[]{:S(2)}) collective-permute-start(f32[1,512]{1,0:T(1,128)S(1)} %get-tuple-element.50), channel_id=1, source_target_pairs={{0,16},{4,20},{8,24},{12,28},{16,0},{20,4},{24,8},{28,12},{1,17},{... | collective-permute-start | bytes 6152 | tf_op jit(solution)/shard_map/ppermute | solution.py:394
  118.3 3.6 %collective-permute-start.32 = (f32[1,512]{1,0:T(1,128)S(1)}, f32[1,512]{1,0:T(1,128)S(1)}, u32[]{:S(2)}, u32[]{:S(2)}) collective-permute-start(f32[1,512]{1,0:T(1,128)S(1)} %get-tuple-element.51), channel_id=1, source_target_pairs={{0,8},{4,12},{8,0},{12,4},{16,24},{20,28},{24,16},{28,20},{1,9},{5... | collective-permute-start | bytes 6152 | tf_op jit(solution)/shard_map/ppermute | solution.py:394

commit v15 on v13

--- a/solution.py
+++ b/solution.py
@@ -11,7 +11,7 @@
 ITERS = 2
 LANES = 128
 SUB = 16
-STAGE = 256
+STAGE = 512
 SMALLEST = 1e-16
 LARGEST = 1e12
 NT_DIMS = (((1,), (1,)), ((), ()))
@@ -87,31 +87,42 @@
         top_ref[row_of(i, steps), :] = as_lanes(shift)
 
 
-def shifted_rows(aug_ref, t_ref, width, lse_ref, top_ref, mass_ref, e_ref, carried_ref=None):
-    rows = aug_ref.shape[0]
-    steps = rows // LANES
-    stages = t_ref.shape[0] // width
-    keep = e_ref.shape[1] // width
-    for g in range(stages + 1):
-        if g > 0 and carried_ref is not None:
-            e = e_ref[:, (g - 1) % keep * width : ((g - 1) % keep + 1) * width]
-            d = jnp.dot(e, block_of(t_ref, g - 1, width), preferred_element_type=jnp.float32)
-            carried_ref[...] = d if g == 1 else carried_ref[...] + d
-        if g < stages:
-            t = t_ref[g * width : (g + 1) * width, :]
-            e = jnp.exp(lax.dot_general(aug_ref[...], t, NT_DIMS, preferred_element_type=jnp.float32))
+def exponentials(aug_ref, t_ref, e_ref, width, mass_ref=None):
+    for at in range(0, t_ref.shape[0], width):
+        t = t_ref[at : at + width, :]
+        e = jnp.exp(lax.dot_general(aug_ref[...], t, NT_DIMS, preferred_element_type=jnp.float32))
+        if mass_ref is not None:
             m = lane_fold(jnp.add, e)
-            mass_ref[...] = m if g == 0 else mass_ref[...] + m
-            e_ref[:, g % keep * width : (g % keep + 1) * width] = e.astype(jnp.bfloat16)
+            mass_ref[...] = m if at == 0 else mass_ref[...] + m
+        e_ref[:, at : at + width] = e.astype(jnp.bfloat16)
+
+
+def shifted_rows(aug_ref, t_ref, lse_ref, top_ref, mass_ref, e_ref):
+    exponentials(aug_ref, t_ref, e_ref, STAGE, mass_ref)
+    steps = aug_ref.shape[0] // LANES
     masses = []
     for i in range(steps):
         at = slice(i * LANES, (i + 1) * LANES)
-        mass = jnp.sum(mass_ref[at, :], axis=1, keepdims=True)
-        masses.append(as_lanes(mass))
+        masses.append(as_lanes(jnp.sum(mass_ref[at, :], axis=1, keepdims=True)))
         row = row_of(i, steps)
         lse_ref[row, :] = top_ref[row, :] + jnp.log(masses[i])
-        if carried_ref is not None:
-            carried_ref[at, :] = carried_ref[at, :] / mass
+    return within(masses)
+
+
+def shifted_couple(aug_ref, t_ref, lse_ref, top_ref, e_ref, carried_ref):
+    exponentials(aug_ref, t_ref, e_ref, STAGE)
+    rows = aug_ref.shape[0]
+    steps = rows // LANES
+    masses = []
+    for h in range(0, rows, 4 * LANES):
+        d = jnp.dot(e_ref[h : h + 4 * LANES, :], t_ref[...], preferred_element_type=jnp.float32)
+        for i in range(h // LANES, h // LANES + 4):
+            at = slice(i * LANES - h, (i + 1) * LANES - h)
+            mass = d[at, LANES + 1 : LANES + 2]
+            carried_ref[i * LANES : (i + 1) * LANES, :] = d[at, :LANES] / mass
+            masses.append(as_lanes(mass))
+            row = row_of(i, steps)
+            lse_ref[row, :] = top_ref[row, :] + jnp.log(masses[i])
     return within(masses)
 
 
@@ -172,7 +183,7 @@
 
 def couple_kernel(nt, width, *refs):
     a_ref, aug_ref, top_ref, t_refs = refs[0], refs[1], refs[2], refs[3 : 3 + nt]
-    lse_ref, carried_ref, t_ref, pot_ref, mass_ref, e_ref, scores = refs[3 + nt :]
+    lse_ref, carried_ref, t_ref, pot_ref, e_ref, scores = refs[3 + nt :]
     lane = lax.broadcasted_iota(jnp.int32, (LANES, LANES), 1)
     for g in range(nt):
         t_ref[g * width : (g + 1) * width, :LANES] = t_refs[g][:width, :]
@@ -182,7 +193,7 @@
             added = jnp.where(lane == 0, potential, jnp.where(lane == 1, 1.0, 0.0))
             at = g * width + j
             t_ref[at : at + LANES, LANES:] = added.astype(jnp.bfloat16)
-    fine = shifted_rows(aug_ref, t_ref, STAGE, lse_ref, top_ref, mass_ref, e_ref, carried_ref)
+    fine = shifted_couple(aug_ref, t_ref, lse_ref, top_ref, e_ref, carried_ref)
 
     @pl.when(jnp.logical_not(fine))
     def _():
@@ -230,7 +241,7 @@
         moment_ref[pl.ds(pl.multiple_of((k ^ (r % 2)) * half, half), half), :] = m_refs[k][...]
     a_ref[...] = project4(s_ref[...], split3(moment_ref[...]))
     add_shifts(a_ref, t_ref, pot_ref[0:1, :], aug_ref, top_ref)
-    fine = shifted_rows(aug_ref, t_ref, STAGE, lse_ref, top_ref, mass_ref, e_ref)
+    fine = shifted_rows(aug_ref, t_ref, lse_ref, top_ref, mass_ref, e_ref)
 
     @pl.when(jnp.logical_not(fine))
     def _():
@@ -413,7 +424,7 @@
         functools.partial(couple_kernel, nt, width),
         [tile, shape((rows, depth), f32), shape((cols, 2 * depth), bf16), shape((nt, width), f32)],
         [a, aug, top] + blocks,
-        [sums, pltpu.VMEM((rows, 2 * STAGE), bf16), row_scores],
+        [pltpu.VMEM((rows, cols), bf16), row_scores],
         2 * flops,
         exps,
     )

time: 122 us -> 122 us (level)
  no operation moved by 1% of the time
where the time goes in v15:
time: 122 us
  Pallas kernels  53.2 us (44%)
  starting transfers between devices  38.4 us (31%)
  waiting for transfers between devices  27.3 us (22%)
  local copies, waits for them, and re-layouts  1.68 us (1%)
    pallas_call x14, Pallas kernels, call(): pl.pallas_call(kernel, out_shape=list(out), in_specs=[vmem] * len(args),...  53.2 us
    ppermute x35, starting transfers between devices, swap(): lax.ppermute(x, axis, [(i, i ^ k) for i in range(lax.axis_size(axis))])  38.4 us
    ppermute x35, waiting for transfers between devices, swap(): lax.ppermute(x, axis, [(i, i ^ k) for i in range(lax.axis_size(axis))])  27.3 us
  transfers between devices with their start and end apart: 35, of which 30 were waited for; matrix products, arithmetic and copies ran while one was open for 1% of the time, Pallas kernels for 1%

profile of v15, /device:TPU:0, one launch (start us, length us, event | category | flops | bytes accessed | tf_op | source)
XLA Modules:
  0.0 122.2 jit_solution(3154479892467941260)
XLA Ops:
  0.6 5.1 %collective-permute-start.1 = (bf16[256,128]{1,0:T(8,128)(2,1)}, bf16[256,128]{1,0:T(8,128)(2,1)S(1)}, u32[]{:S(2)}, u32[]{:S(2)}) collective-permute-start(bf16[256,128]{1,0:T(8,128)(2,1)} %refs_0_.1), channel_id=1, source_target_pairs={{0,3},{1,2},{2,1},{3,0},{4,7},{5,6},{6,5},{7,4},{8,11},{9,10},{10,... | collective-permute-start | bytes 196616 | tf_op jit(solution)/shard_map/ppermute | solution.py:376
  5.7 0.6 collective-permute-start.2
  6.4 0.9 fusion.1.block_ref.refs_3_
  7.3 2.7 %collective-permute-start.8 = (bf16[528,128]{1,0:T(8,128)(2,1)S(1)}, bf16[528,128]{1,0:T(8,128)(2,1)S(1)}, u32[]{:S(2)}, u32[]{:S(2)}) collective-permute-start(bf16[528,128]{1,0:T(8,128)(2,1)S(1)} %fusion.1.block_ref.refs_3_), channel_id=1, source_target_pairs={{0,24},{4,28},{8,16},{12,20},{16,8},{20,12},{24,0},{28,4},{1,25},{... | collective-permute-start | bytes 405512 | tf_op jit(solution)/shard_map/ppermute | solution.py:376
  10.0 0.5 collective-permute-start.6
  10.5 0.4 collective-permute-start.4
  10.9 0.7 collective-permute-done.refs_1_
  11.6 0.8 copy-done
  12.4 0.8 copy-done.1
  13.2 0.4 shard_map.67
  13.7 0.3 collective-permute-done.8.refs_9_
  14.0 1.9 %collective-permute-done.6.refs_7_ = bf16[528,128]{1,0:T(8,128)(2,1)S(1)} collective-permute-done((bf16[528,128]{1,0:T(8,128)(2,1)S(1)}, bf16[528,128]{1,0:T(8,128)(2,1)S(1)}, u32[]{:S(2)}, u32[]{:S(2)}) %collective-permute-start.6) | collective-permute-done | bytes 135200 | tf_op jit(solution)/shard_map/ppermute | solution.py:376
  16.0 0.5 collective-permute-start.7
  16.5 0.6 shard_map.68
  17.1 0.2 collective-permute-done.5.refs_6_
  17.6 0.3 collective-permute-done.9.refs_10_
  17.9 15.5 %shard_map.69 = (f32[8,128]{1,0:T(8,128)S(1)}, f32[1024,128]{1,0:T(8,128)S(1)}, bf16[4096,256]{1,0:T(8,128)(2,1)S(1)}, f32[8,512]{1,0:T(8,128)S(1)}) custom-call(bf16[1024,128]{1,0:T(8,128)(2,1)S(1)} %get-tuple-element.31.a_ref.refs_0_, bf16[1024,256]{1,0:T(8,128)(2,1)S(1)} %get-tuple-element.33.refs_1_, f32[8,128]{1,0:T(8,128)S(1)} %get-tuple-element.34.refs_2_, ...), custom_call_target="tpu_custom_call" | custom-call | flops 2147483648 | bytes 4513792 | tf_op jit(solution)/shard_map/pallas_call | solution.py:364
  33.4 3.5 %collective-permute-start.12 = (f32[8,128]{1,0:T(8,128)S(1)}, f32[8,128]{1,0:T(8,128)S(1)}, u32[]{:S(2)}, u32[]{:S(2)}) collective-permute-start(f32[8,128]{1,0:T(8,128)S(1)} %get-tuple-element.40.refs_1_), channel_id=1, source_target_pairs={{0,3},{1,2},{2,1},{3,0},{4,7},{5,6},{6,5},{7,4},{8,11},{9,10},{10,... | collective-permute-start | bytes 12296 | tf_op jit(solution)/shard_map/ppermute | solution.py:376
  36.9 0.9 collective-permute-start.10
  37.8 1.0 collective-permute-done.12.refs_4_
  38.8 2.6 %collective-permute-done.11.refs_3_ = f32[8,128]{1,0:T(8,128)S(1)} collective-permute-done((f32[8,128]{1,0:T(8,128)S(1)}, f32[8,128]{1,0:T(8,128)S(1)}, u32[]{:S(2)}, u32[]{:S(2)}) %collective-permute-start.11) | collective-permute-done | bytes 4128 | tf_op jit(solution)/shard_map/ppermute | solution.py:376
  41.4 0.5 shard_map.70
  42.0 1.2 collective-permute-done.13.refs_1_
  43.2 1.5 %collective-permute-start.16 = (f32[64,128]{1,0:T(8,128)S(1)}, f32[64,128]{1,0:T(8,128)S(1)}, u32[]{:S(2)}, u32[]{:S(2)}) collective-permute-start(f32[64,128]{1,0:T(8,128)S(1)} %shard_map.71.refs_0_), channel_id=1, source_target_pairs={{0,3},{1,2},{2,1},{3,0},{4,7},{5,6},{6,5},{7,4},{8,11},{9,10},{10,... | collective-permute-start | bytes 98312 | tf_op jit(solution)/shard_map/ppermute | solution.py:376
  44.7 0.6 collective-permute-start.15
  45.3 2.3 %collective-permute-start.14 = (f32[64,128]{1,0:T(8,128)S(1)}, f32[64,128]{1,0:T(8,128)S(1)}, u32[]{:S(2)}, u32[]{:S(2)}) collective-permute-start(f32[64,128]{1,0:T(8,128)S(1)} %shard_map.71.refs_0_), channel_id=1, source_target_pairs={{0,1},{1,0},{2,3},{3,2},{4,5},{5,4},{6,7},{7,6},{8,9},{9,8},{10,11... | collective-permute-start | bytes 98312 | tf_op jit(solution)/shard_map/ppermute | solution.py:376
  47.6 1.6 %collective-permute-done.16.refs_3_ = f32[64,128]{1,0:T(8,128)S(1)} collective-permute-done((f32[64,128]{1,0:T(8,128)S(1)}, f32[64,128]{1,0:T(8,128)S(1)}, u32[]{:S(2)}, u32[]{:S(2)}) %collective-permute-start.16) | collective-permute-done | bytes 32800 | tf_op jit(solution)/shard_map/ppermute | solution.py:376
  49.3 0.4 collective-permute-done.15.refs_2_
  49.9 1.8 %collective-permute-start.19 = (f32[64,128]{1,0:T(8,128)S(1)}, f32[64,128]{1,0:T(8,128)S(1)}, u32[]{:S(2)}, u32[]{:S(2)}) collective-permute-start(f32[64,128]{1,0:T(8,128)S(1)} %shard_map.72.refs_0_), channel_id=1, source_target_pairs={{0,24},{4,28},{8,16},{12,20},{16,8},{20,12},{24,0},{28,4},{1,25},{... | collective-permute-start | bytes 98312 | tf_op jit(solution)/shard_map/ppermute | solution.py:376
  51.7 1.3 %collective-permute-start.18 = (f32[64,128]{1,0:T(8,128)S(1)}, f32[64,128]{1,0:T(8,128)S(1)}, u32[]{:S(2)}, u32[]{:S(2)}) collective-permute-start(f32[64,128]{1,0:T(8,128)S(1)} %shard_map.72.refs_0_), channel_id=1, source_target_pairs={{0,16},{4,20},{8,24},{12,28},{16,0},{20,4},{24,8},{28,12},{1,17},{... | collective-permute-start | bytes 98312 | tf_op jit(solution)/shard_map/ppermute | solution.py:376
  53.0 0.5 collective-permute-start.17
  53.5 1.6 %collective-permute-done.19.refs_3_ = f32[64,128]{1,0:T(8,128)S(1)} collective-permute-done((f32[64,128]{1,0:T(8,128)S(1)}, f32[64,128]{1,0:T(8,128)S(1)}, u32[]{:S(2)}, u32[]{:S(2)}) %collective-permute-start.19) | collective-permute-done | bytes 32800 | tf_op jit(solution)/shard_map/ppermute | solution.py:376
  55.1 0.5 collective-permute-done.18.refs_2_
  55.6 1.3 %collective-permute-done.17.refs_1_ = f32[64,128]{1,0:T(8,128)S(1)} collective-permute-done((f32[64,128]{1,0:T(8,128)S(1)}, f32[64,128]{1,0:T(8,128)S(1)}, u32[]{:S(2)}, u32[]{:S(2)}) %collective-permute-start.17) | collective-permute-done | bytes 32800 | tf_op jit(solution)/shard_map/ppermute | solution.py:376
  57.0 1.2 collective-permute-done.20.refs_4_
  58.2 12.3 %shard_map.74 = (f32[128,128]{1,0:T(8,128)}, bf16[1024,128]{1,0:T(8,128)(2,1)S(1)}, f32[8,128]{1,0:T(8,128)S(1)}, f32[8,128]{1,0:T(8,128)S(1)}, bf16[1024,4096]{1,0:T(8,128)(2,1)S(1)}) custom-call(bf16[1024,128]{1,0:T(8,128)(2,1)S(1)} %get-tuple-element.30.refs_0_, bf16[4096,256]{1,0:T(8,128)(2,1)S(1)} %get-tuple-element.38.refs_1_.refs_3_, ...), custom_call_target="tpu_custom_call" | custom-call | flops 1073741824 | bytes 11165696 | tf_op jit(solution)/shard_map/pallas_call | solution.py:364
  70.5 2.3 %collective-permute-start.23 = (f32[8,128]{1,0:T(8,128)S(1)}, f32[8,128]{1,0:T(8,128)S(1)}, u32[]{:S(2)}, u32[]{:S(2)}) collective-permute-start(f32[8,128]{1,0:T(8,128)S(1)} %get-tuple-element.48.refs_5_), channel_id=1, source_target_pairs={{0,3},{1,2},{2,1},{3,0},{4,7},{5,6},{6,5},{7,4},{8,11},{9,10},{10,... | collective-permute-start | bytes 12296 | tf_op jit(solution)/shard_map/ppermute | solution.py:376
  72.8 0.8 collective-permute-start.22
  73.6 1.3 %collective-permute-start.21 = (f32[8,128]{1,0:T(8,128)S(1)}, f32[8,128]{1,0:T(8,128)S(1)}, u32[]{:S(2)}, u32[]{:S(2)}) collective-permute-start(f32[8,128]{1,0:T(8,128)S(1)} %get-tuple-element.48.refs_5_), channel_id=1, source_target_pairs={{0,1},{1,0},{2,3},{3,2},{4,5},{5,4},{6,7},{7,6},{8,9},{9,8},{10,11... | collective-permute-start | bytes 12296 | tf_op jit(solution)/shard_map/ppermute | solution.py:376
  74.9 1.0 collective-permute-done.23.refs_8_
  75.9 1.4 %collective-permute-done.22.refs_7_ = f32[8,128]{1,0:T(8,128)S(1)} collective-permute-done((f32[8,128]{1,0:T(8,128)S(1)}, f32[8,128]{1,0:T(8,128)S(1)}, u32[]{:S(2)}, u32[]{:S(2)}) %collective-permute-start.22) | collective-permute-done | bytes 4128 | tf_op jit(solution)/shard_map/ppermute | solution.py:376
  77.3 7.0 %shard_map.75 = (f32[8,512]{1,0:T(8,128)S(1)}, f32[8,128]{1,0:T(8,128)}) custom-call(bf16[1024,128]{1,0:T(8,128)(2,1)S(1)} %get-tuple-element.45.refs_0_, bf16[1024,4096]{1,0:T(8,128)(2,1)S(1)} %get-tuple-element.46.refs_1_, f32[8,128]{1,0:T(8,128)S(1)} %get-tuple-element.47.refs_2_, bf16[4096,256]{1,0:T(8,128)(2,1)S(1)} %get-tuple-element.38.refs_1_.refs_3_, ...), custom_call_target="tpu_custom_call" | custom-call | flops 67108864 | bytes 10805248 | tf_op jit(solution)/shard_map/pallas_call | solution.py:364
  84.3 1.2 collective-permute-done.24.refs_1_
  85.5 1.5 %collective-permute-start.27 = (f32[8,512]{1,0:T(8,128)S(1)}, f32[8,512]{1,0:T(8,128)S(1)}, u32[]{:S(2)}, u32[]{:S(2)}) collective-permute-start(f32[8,512]{1,0:T(8,128)S(1)} %shard_map.76.refs_5_), channel_id=1, source_target_pairs={{0,24},{4,28},{8,16},{12,20},{16,8},{20,12},{24,0},{28,4},{1,25},{... | collective-permute-start | bytes 49160 | tf_op jit(solution)/shard_map/ppermute | solution.py:376
  86.9 0.6 collective-permute-start.26
  87.5 1.5 %collective-permute-start.25 = (f32[8,512]{1,0:T(8,128)S(1)}, f32[8,512]{1,0:T(8,128)S(1)}, u32[]{:S(2)}, u32[]{:S(2)}) collective-permute-start(f32[8,512]{1,0:T(8,128)S(1)} %shard_map.76.refs_5_), channel_id=1, source_target_pairs={{0,8},{4,12},{8,0},{12,4},{16,24},{20,28},{24,16},{28,20},{1,9},{5... | collective-permute-start | bytes 49160 | tf_op jit(solution)/shard_map/ppermute | solution.py:376
  89.0 1.1 collective-permute-done.27.refs_8_
  90.2 0.5 collective-permute-done.26.refs_7_
  90.7 0.6 collective-permute-done.25.refs_6_
  91.2 9.5 %shard_map.77.refs_5_ = f32[8,128]{1,0:T(8,128)S(1)} custom-call(bf16[1024,128]{1,0:T(8,128)(2,1)S(1)} %get-tuple-element.45.refs_0_, bf16[1024,4096]{1,0:T(8,128)(2,1)S(1)} %get-tuple-element.46.refs_1_, f32[8,128]{1,0:T(8,128)S(1)} %get-tuple-element.47.refs_2_, bf16[4096,256]{1,0:T(8,128)(2,1)S(1)} %get-tuple-element.38.refs_1_.refs_3_, ...), custom_call_target="tpu_custom_call" | custom-call | flops 67108864 | bytes 10838016 | tf_op jit(solution)/shard_map/pallas_call | solution.py:364
  100.8 1.6 %collective-permute-start.30 = (f32[8,128]{1,0:T(8,128)S(1)}, f32[8,128]{1,0:T(8,128)S(1)}, u32[]{:S(2)}, u32[]{:S(2)}) collective-permute-start(f32[8,128]{1,0:T(8,128)S(1)} %shard_map.77.refs_5_), channel_id=1, source_target_pairs={{0,3},{1,2},{2,1},{3,0},{4,7},{5,6},{6,5},{7,4},{8,11},{9,10},{10,... | collective-permute-start | bytes 12296 | tf_op jit(solution)/shard_map/ppermute | solution.py:376
  102.3 1.1 collective-permute-start.29
  103.4 1.8 %collective-permute-start.28 = (f32[8,128]{1,0:T(8,128)S(1)}, f32[8,128]{1,0:T(8,128)S(1)}, u32[]{:S(2)}, u32[]{:S(2)}) collective-permute-start(f32[8,128]{1,0:T(8,128)S(1)} %shard_map.77.refs_5_), channel_id=1, source_target_pairs={{0,1},{1,0},{2,3},{3,2},{4,5},{5,4},{6,7},{7,6},{8,9},{9,8},{10,11... | collective-permute-start | bytes 12296 | tf_op jit(solution)/shard_map/ppermute | solution.py:376
  105.2 1.0 collective-permute-done.30.refs_8_
  106.2 0.6 collective-permute-done.29.refs_7_
  107.0 6.7 %shard_map.78 = (f32[4,1,512]{2,1,0:T(1,128)S(1)}, f32[4,1,512]{2,1,0:T(1,128)S(1)}, f32[8,128]{1,0:T(8,128)}) custom-call(bf16[1024,128]{1,0:T(8,128)(2,1)S(1)} %get-tuple-element.45.refs_0_, bf16[1024,4096]{1,0:T(8,128)(2,1)S(1)} %get-tuple-element.46.refs_1_, f32[8,128]{1,0:T(8,128)S(1)} %get-tuple-element.47.refs_2_, ...), custom_call_target="tpu_custom_call" | custom-call | flops 67108864 | bytes 10805248 | tf_op jit(solution)/shard_map/pallas_call | solution.py:364
  113.8 1.2 collective-permute-done.31.y_ref
  115.0 1.8 %collective-permute-start.32 = (f32[1,512]{1,0:T(1,128)S(1)}, f32[1,512]{1,0:T(1,128)S(1)}, u32[]{:S(2)}, u32[]{:S(2)}) collective-permute-start(f32[1,512]{1,0:T(1,128)S(1)} %get-tuple-element.53), channel_id=1, source_target_pairs={{0,24},{4,28},{8,16},{12,20},{16,8},{20,12},{24,0},{28,4},{1,25},{... | collective-permute-start | bytes 6152 | tf_op jit(solution)/shard_map/ppermute | solution.py:376
  116.8 1.3 %collective-permute-start.33 = (f32[1,512]{1,0:T(1,128)S(1)}, f32[1,512]{1,0:T(1,128)S(1)}, u32[]{:S(2)}, u32[]{:S(2)}) collective-permute-start(f32[1,512]{1,0:T(1,128)S(1)} %get-tuple-element.54), channel_id=1, source_target_pairs={{0,16},{4,20},{8,24},{12,28},{16,0},{20,4},{24,8},{28,12},{1,17},{... | collective-permute-start | bytes 6152 | tf_op jit(solution)/shard_map/ppermute | solution.py:376
  118.1 0.5 collective-permute-start.34
  118.5 1.0 collective-permute-done.32.refs_0_
  119.5 0.8 collective-permute-done.33.refs_1_
  120.3 1.3 %collective-permute-done.34.refs_2_ = f32[1,512]{1,0:T(1,128)S(1)} collective-permute-done((f32[1,512]{1,0:T(1,128)S(1)}, f32[1,512]{1,0:T(1,128)S(1)}, u32[]{:S(2)}, u32[]{:S(2)}) %collective-permute-start.34) | collective-permute-done | bytes 2080 | tf_op jit(solution)/shard_map/ppermute | solution.py:376
  121.6 0.6 shard_map.80
  (25 shorter events, 1.0 us)
Async XLA Ops:
  0.6 9.9 %collective-permute-start.1 = (bf16[256,128]{1,0:T(8,128)(2,1)}, bf16[256,128]{1,0:T(8,128)(2,1)S(1)}, u32[]{:S(2)}, u32[]{:S(2)}) collective-permute-start(bf16[256,128]{1,0:T(8,128)(2,1)} %refs_0_.1), channel_id=1, source_target_pairs={{0,3},{1,2},{2,1},{3,0},{4,7},{5,6},{6,5},{7,4},{8,11},{9,10},{10,... | collective-permute-start | bytes 196616 | tf_op jit(solution)/shard_map/ppermute | solution.py:376
  5.7 5.8 %collective-permute-start = (bf16[256,128]{1,0:T(8,128)(2,1)}, bf16[256,128]{1,0:T(8,128)(2,1)S(1)}, u32[]{:S(2)}, u32[]{:S(2)}) collective-permute-start(bf16[256,128]{1,0:T(8,128)(2,1)} %refs_0_.1), channel_id=1, source_target_pairs={{0,2},{1,3},{2,0},{3,1},{4,6},{5,7},{6,4},{7,5},{8,10},{9,11},{10,... | collective-permute-start | bytes 196616 | tf_op jit(solution)/shard_map/ppermute | solution.py:376
  5.7 5.8 %collective-permute-start.2 = (bf16[256,128]{1,0:T(8,128)(2,1)}, bf16[256,128]{1,0:T(8,128)(2,1)S(1)}, u32[]{:S(2)}, u32[]{:S(2)}) collective-permute-start(bf16[256,128]{1,0:T(8,128)(2,1)} %refs_0_.1), channel_id=1, source_target_pairs={{0,1},{1,0},{2,3},{3,2},{4,5},{5,4},{6,7},{7,6},{8,9},{9,8},{10,11... | collective-permute-start | bytes 196616 | tf_op jit(solution)/shard_map/ppermute | solution.py:376
  7.3 6.7 %collective-permute-start.8 = (bf16[528,128]{1,0:T(8,128)(2,1)S(1)}, bf16[528,128]{1,0:T(8,128)(2,1)S(1)}, u32[]{:S(2)}, u32[]{:S(2)}) collective-permute-start(bf16[528,128]{1,0:T(8,128)(2,1)S(1)} %fusion.1.block_ref.refs_3_), channel_id=1, source_target_pairs={{0,24},{4,28},{8,16},{12,20},{16,8},{20,12},{24,0},{28,4},{1,25},{... | collective-permute-start | bytes 405512 | tf_op jit(solution)/shard_map/ppermute | solution.py:376
  10.0 6.0 %collective-permute-start.6 = (bf16[528,128]{1,0:T(8,128)(2,1)S(1)}, bf16[528,128]{1,0:T(8,128)(2,1)S(1)}, u32[]{:S(2)}, u32[]{:S(2)}) collective-permute-start(bf16[528,128]{1,0:T(8,128)(2,1)S(1)} %fusion.1.block_ref.refs_3_), channel_id=1, source_target_pairs={{0,16},{4,20},{8,24},{12,28},{16,0},{20,4},{24,8},{28,12},{1,17},{... | collective-permute-start | bytes 405512 | tf_op jit(solution)/shard_map/ppermute | solution.py:376
  10.5 5.5 %collective-permute-start.4 = (bf16[528,128]{1,0:T(8,128)(2,1)S(1)}, bf16[528,128]{1,0:T(8,128)(2,1)S(1)}, u32[]{:S(2)}, u32[]{:S(2)}) collective-permute-start(bf16[528,128]{1,0:T(8,128)(2,1)S(1)} %fusion.1.block_ref.refs_3_), channel_id=1, source_target_pairs={{0,8},{4,12},{8,0},{12,4},{16,24},{20,28},{24,16},{28,20},{1,9},{5... | collective-permute-start | bytes 405512 | tf_op jit(solution)/shard_map/ppermute | solution.py:376
  11.6 0.8 copy-start
  12.4 0.8 copy-start.1
  13.6 3.5 %collective-permute-start.3 = (bf16[528,128]{1,0:T(8,128)(2,1)S(1)}, bf16[528,128]{1,0:T(8,128)(2,1)S(1)}, u32[]{:S(2)}, u32[]{:S(2)}) collective-permute-start(bf16[528,128]{1,0:T(8,128)(2,1)S(1)} %fusion.1.block_ref.refs_3_), channel_id=1, source_target_pairs={{0,4},{4,0},{8,12},{12,8},{16,20},{20,16},{24,28},{28,24},{1,5},{5... | collective-permute-start | bytes 405512 | tf_op jit(solution)/shard_map/ppermute | solution.py:376
  16.0 1.4 %collective-permute-start.5 = (bf16[528,128]{1,0:T(8,128)(2,1)S(1)}, bf16[528,128]{1,0:T(8,128)(2,1)S(1)}, u32[]{:S(2)}, u32[]{:S(2)}) collective-permute-start(bf16[528,128]{1,0:T(8,128)(2,1)S(1)} %collective-permute-done.4.refs_5_), channel_id=1, source_target_pairs={{0,4},{4,0},{8,12},{12,8},{16,20},{20,16},{24,28},{28,24},{1,5},{5... | collective-permute-start | bytes 405512 | tf_op jit(solution)/shard_map/ppermute | solution.py:376
  16.0 1.5 %collective-permute-start.7 = (bf16[528,128]{1,0:T(8,128)(2,1)S(1)}, bf16[528,128]{1,0:T(8,128)(2,1)S(1)}, u32[]{:S(2)}, u32[]{:S(2)}) collective-permute-start(bf16[528,128]{1,0:T(8,128)(2,1)S(1)} %collective-permute-done.6.refs_7_), channel_id=1, source_target_pairs={{0,4},{4,0},{8,12},{12,8},{16,20},{20,16},{24,28},{28,24},{1,5},{5... | collective-permute-start | bytes 405512 | tf_op jit(solution)/shard_map/ppermute | solution.py:376
  16.5 1.4 %collective-permute-start.9 = (bf16[528,128]{1,0:T(8,128)(2,1)S(1)}, bf16[528,128]{1,0:T(8,128)(2,1)S(1)}, u32[]{:S(2)}, u32[]{:S(2)}) collective-permute-start(bf16[528,128]{1,0:T(8,128)(2,1)S(1)} %collective-permute-done.8.refs_9_), channel_id=1, source_target_pairs={{0,4},{4,0},{8,12},{12,8},{16,20},{20,16},{24,28},{28,24},{1,5},{5... | collective-permute-start | bytes 405512 | tf_op jit(solution)/shard_map/ppermute | solution.py:376
  33.4 5.5 %collective-permute-start.12 = (f32[8,128]{1,0:T(8,128)S(1)}, f32[8,128]{1,0:T(8,128)S(1)}, u32[]{:S(2)}, u32[]{:S(2)}) collective-permute-start(f32[8,128]{1,0:T(8,128)S(1)} %get-tuple-element.40.refs_1_), channel_id=1, source_target_pairs={{0,3},{1,2},{2,1},{3,0},{4,7},{5,6},{6,5},{7,4},{8,11},{9,10},{10,... | collective-permute-start | bytes 12296 | tf_op jit(solution)/shard_map/ppermute | solution.py:376
  36.9 4.5 %collective-permute-start.11 = (f32[8,128]{1,0:T(8,128)S(1)}, f32[8,128]{1,0:T(8,128)S(1)}, u32[]{:S(2)}, u32[]{:S(2)}) collective-permute-start(f32[8,128]{1,0:T(8,128)S(1)} %get-tuple-element.40.refs_1_), channel_id=1, source_target_pairs={{0,2},{1,3},{2,0},{3,1},{4,6},{5,7},{6,4},{7,5},{8,10},{9,11},{10,... | collective-permute-start | bytes 12296 | tf_op jit(solution)/shard_map/ppermute | solution.py:376
  36.9 4.5 %collective-permute-start.10 = (f32[8,128]{1,0:T(8,128)S(1)}, f32[8,128]{1,0:T(8,128)S(1)}, u32[]{:S(2)}, u32[]{:S(2)}) collective-permute-start(f32[8,128]{1,0:T(8,128)S(1)} %get-tuple-element.40.refs_1_), channel_id=1, source_target_pairs={{0,1},{1,0},{2,3},{3,2},{4,5},{5,4},{6,7},{7,6},{8,9},{9,8},{10,11... | collective-permute-start | bytes 12296 | tf_op jit(solution)/shard_map/ppermute | solution.py:376
  42.0 1.3 %collective-permute-start.13 = (f32[64,128]{1,0:T(8,128)S(1)}, f32[64,128]{1,0:T(8,128)S(1)}, u32[]{:S(2)}, u32[]{:S(2)}) collective-permute-start(f32[64,128]{1,0:T(8,128)S(1)} %get-tuple-element.43), channel_id=1, source_target_pairs={{0,4},{4,0},{8,12},{12,8},{16,20},{20,16},{24,28},{28,24},{1,5},{5... | collective-permute-start | bytes 98312 | tf_op jit(solution)/shard_map/ppermute | solution.py:376
  43.2 6.0 %collective-permute-start.16 = (f32[64,128]{1,0:T(8,128)S(1)}, f32[64,128]{1,0:T(8,128)S(1)}, u32[]{:S(2)}, u32[]{:S(2)}) collective-permute-start(f32[64,128]{1,0:T(8,128)S(1)} %shard_map.71.refs_0_), channel_id=1, source_target_pairs={{0,3},{1,2},{2,1},{3,0},{4,7},{5,6},{6,5},{7,4},{8,11},{9,10},{10,... | collective-permute-start | bytes 98312 | tf_op jit(solution)/shard_map/ppermute | solution.py:376
  44.7 5.0 %collective-permute-start.15 = (f32[64,128]{1,0:T(8,128)S(1)}, f32[64,128]{1,0:T(8,128)S(1)}, u32[]{:S(2)}, u32[]{:S(2)}) collective-permute-start(f32[64,128]{1,0:T(8,128)S(1)} %shard_map.71.refs_0_), channel_id=1, source_target_pairs={{0,2},{1,3},{2,0},{3,1},{4,6},{5,7},{6,4},{7,5},{8,10},{9,11},{10,... | collective-permute-start | bytes 98312 | tf_op jit(solution)/shard_map/ppermute | solution.py:376
  45.3 4.6 %collective-permute-start.14 = (f32[64,128]{1,0:T(8,128)S(1)}, f32[64,128]{1,0:T(8,128)S(1)}, u32[]{:S(2)}, u32[]{:S(2)}) collective-permute-start(f32[64,128]{1,0:T(8,128)S(1)} %shard_map.71.refs_0_), channel_id=1, source_target_pairs={{0,1},{1,0},{2,3},{3,2},{4,5},{5,4},{6,7},{7,6},{8,9},{9,8},{10,11... | collective-permute-start | bytes 98312 | tf_op jit(solution)/shard_map/ppermute | solution.py:376
  49.9 5.2 %collective-permute-start.19 = (f32[64,128]{1,0:T(8,128)S(1)}, f32[64,128]{1,0:T(8,128)S(1)}, u32[]{:S(2)}, u32[]{:S(2)}) collective-permute-start(f32[64,128]{1,0:T(8,128)S(1)} %shard_map.72.refs_0_), channel_id=1, source_target_pairs={{0,24},{4,28},{8,16},{12,20},{16,8},{20,12},{24,0},{28,4},{1,25},{... | collective-permute-start | bytes 98312 | tf_op jit(solution)/shard_map/ppermute | solution.py:376
  51.7 3.9 %collective-permute-start.18 = (f32[64,128]{1,0:T(8,128)S(1)}, f32[64,128]{1,0:T(8,128)S(1)}, u32[]{:S(2)}, u32[]{:S(2)}) collective-permute-start(f32[64,128]{1,0:T(8,128)S(1)} %shard_map.72.refs_0_), channel_id=1, source_target_pairs={{0,16},{4,20},{8,24},{12,28},{16,0},{20,4},{24,8},{28,12},{1,17},{... | collective-permute-start | bytes 98312 | tf_op jit(solution)/shard_map/ppermute | solution.py:376
  53.0 3.9 %collective-permute-start.17 = (f32[64,128]{1,0:T(8,128)S(1)}, f32[64,128]{1,0:T(8,128)S(1)}, u32[]{:S(2)}, u32[]{:S(2)}) collective-permute-start(f32[64,128]{1,0:T(8,128)S(1)} %shard_map.72.refs_0_), channel_id=1, source_target_pairs={{0,8},{4,12},{8,0},{12,4},{16,24},{20,28},{24,16},{28,20},{1,9},{5... | collective-permute-start | bytes 98312 | tf_op jit(solution)/shard_map/ppermute | solution.py:376
  56.9 1.3 %collective-permute-start.20 = (f32[64,128]{1,0:T(8,128)S(1)}, f32[64,128]{1,0:T(8,128)S(1)}, u32[]{:S(2)}, u32[]{:S(2)}) collective-permute-start(f32[64,128]{1,0:T(8,128)S(1)} %shard_map.73.refs_3_), channel_id=1, source_target_pairs={{0,4},{4,0},{8,12},{12,8},{16,20},{20,16},{24,28},{28,24},{1,5},{5... | collective-permute-start | bytes 98312 | tf_op jit(solution)/shard_map/ppermute | solution.py:376
  70.5 5.4 %collective-permute-start.23 = (f32[8,128]{1,0:T(8,128)S(1)}, f32[8,128]{1,0:T(8,128)S(1)}, u32[]{:S(2)}, u32[]{:S(2)}) collective-permute-start(f32[8,128]{1,0:T(8,128)S(1)} %get-tuple-element.48.refs_5_), channel_id=1, source_target_pairs={{0,3},{1,2},{2,1},{3,0},{4,7},{5,6},{6,5},{7,4},{8,11},{9,10},{10,... | collective-permute-start | bytes 12296 | tf_op jit(solution)/shard_map/ppermute | solution.py:376
  72.8 4.5 %collective-permute-start.22 = (f32[8,128]{1,0:T(8,128)S(1)}, f32[8,128]{1,0:T(8,128)S(1)}, u32[]{:S(2)}, u32[]{:S(2)}) collective-permute-start(f32[8,128]{1,0:T(8,128)S(1)} %get-tuple-element.48.refs_5_), channel_id=1, source_target_pairs={{0,2},{1,3},{2,0},{3,1},{4,6},{5,7},{6,4},{7,5},{8,10},{9,11},{10,... | collective-permute-start | bytes 12296 | tf_op jit(solution)/shard_map/ppermute | solution.py:376
  73.6 3.7 %collective-permute-start.21 = (f32[8,128]{1,0:T(8,128)S(1)}, f32[8,128]{1,0:T(8,128)S(1)}, u32[]{:S(2)}, u32[]{:S(2)}) collective-permute-start(f32[8,128]{1,0:T(8,128)S(1)} %get-tuple-element.48.refs_5_), channel_id=1, source_target_pairs={{0,1},{1,0},{2,3},{3,2},{4,5},{5,4},{6,7},{7,6},{8,9},{9,8},{10,11... | collective-permute-start | bytes 12296 | tf_op jit(solution)/shard_map/ppermute | solution.py:376
  84.3 1.2 collective-permute-start.24
  85.5 4.7 %collective-permute-start.27 = (f32[8,512]{1,0:T(8,128)S(1)}, f32[8,512]{1,0:T(8,128)S(1)}, u32[]{:S(2)}, u32[]{:S(2)}) collective-permute-start(f32[8,512]{1,0:T(8,128)S(1)} %shard_map.76.refs_5_), channel_id=1, source_target_pairs={{0,24},{4,28},{8,16},{12,20},{16,8},{20,12},{24,0},{28,4},{1,25},{... | collective-permute-start | bytes 49160 | tf_op jit(solution)/shard_map/ppermute | solution.py:376
  86.9 3.7 %collective-permute-start.26 = (f32[8,512]{1,0:T(8,128)S(1)}, f32[8,512]{1,0:T(8,128)S(1)}, u32[]{:S(2)}, u32[]{:S(2)}) collective-permute-start(f32[8,512]{1,0:T(8,128)S(1)} %shard_map.76.refs_5_), channel_id=1, source_target_pairs={{0,16},{4,20},{8,24},{12,28},{16,0},{20,4},{24,8},{28,12},{1,17},{... | collective-permute-start | bytes 49160 | tf_op jit(solution)/shard_map/ppermute | solution.py:376
  87.5 3.7 %collective-permute-start.25 = (f32[8,512]{1,0:T(8,128)S(1)}, f32[8,512]{1,0:T(8,128)S(1)}, u32[]{:S(2)}, u32[]{:S(2)}) collective-permute-start(f32[8,512]{1,0:T(8,128)S(1)} %shard_map.76.refs_5_), channel_id=1, source_target_pairs={{0,8},{4,12},{8,0},{12,4},{16,24},{20,28},{24,16},{28,20},{1,9},{5... | collective-permute-start | bytes 49160 | tf_op jit(solution)/shard_map/ppermute | solution.py:376
  100.8 5.4 %collective-permute-start.30 = (f32[8,128]{1,0:T(8,128)S(1)}, f32[8,128]{1,0:T(8,128)S(1)}, u32[]{:S(2)}, u32[]{:S(2)}) collective-permute-start(f32[8,128]{1,0:T(8,128)S(1)} %shard_map.77.refs_5_), channel_id=1, source_target_pairs={{0,3},{1,2},{2,1},{3,0},{4,7},{5,6},{6,5},{7,4},{8,11},{9,10},{10,... | collective-permute-start | bytes 12296 | tf_op jit(solution)/shard_map/ppermute | solution.py:376
  102.3 4.5 %collective-permute-start.29 = (f32[8,128]{1,0:T(8,128)S(1)}, f32[8,128]{1,0:T(8,128)S(1)}, u32[]{:S(2)}, u32[]{:S(2)}) collective-permute-start(f32[8,128]{1,0:T(8,128)S(1)} %shard_map.77.refs_5_), channel_id=1, source_target_pairs={{0,2},{1,3},{2,0},{3,1},{4,6},{5,7},{6,4},{7,5},{8,10},{9,11},{10,... | collective-permute-start | bytes 12296 | tf_op jit(solution)/shard_map/ppermute | solution.py:376
  103.4 3.6 %collective-permute-start.28 = (f32[8,128]{1,0:T(8,128)S(1)}, f32[8,128]{1,0:T(8,128)S(1)}, u32[]{:S(2)}, u32[]{:S(2)}) collective-permute-start(f32[8,128]{1,0:T(8,128)S(1)} %shard_map.77.refs_5_), channel_id=1, source_target_pairs={{0,1},{1,0},{2,3},{3,2},{4,5},{5,4},{6,7},{7,6},{8,9},{9,8},{10,11... | collective-permute-start | bytes 12296 | tf_op jit(solution)/shard_map/ppermute | solution.py:376
  113.8 1.2 collective-permute-start.31
  115.0 4.5 %collective-permute-start.32 = (f32[1,512]{1,0:T(1,128)S(1)}, f32[1,512]{1,0:T(1,128)S(1)}, u32[]{:S(2)}, u32[]{:S(2)}) collective-permute-start(f32[1,512]{1,0:T(1,128)S(1)} %get-tuple-element.53), channel_id=1, source_target_pairs={{0,24},{4,28},{8,16},{12,20},{16,8},{20,12},{24,0},{28,4},{1,25},{... | collective-permute-start | bytes 6152 | tf_op jit(solution)/shard_map/ppermute | solution.py:376
  116.8 3.6 %collective-permute-start.33 = (f32[1,512]{1,0:T(1,128)S(1)}, f32[1,512]{1,0:T(1,128)S(1)}, u32[]{:S(2)}, u32[]{:S(2)}) collective-permute-start(f32[1,512]{1,0:T(1,128)S(1)} %get-tuple-element.54), channel_id=1, source_target_pairs={{0,16},{4,20},{8,24},{12,28},{16,0},{20,4},{24,8},{28,12},{1,17},{... | collective-permute-start | bytes 6152 | tf_op jit(solution)/shard_map/ppermute | solution.py:376
  118.1 3.6 %collective-permute-start.34 = (f32[1,512]{1,0:T(1,128)S(1)}, f32[1,512]{1,0:T(1,128)S(1)}, u32[]{:S(2)}, u32[]{:S(2)}) collective-permute-start(f32[1,512]{1,0:T(1,128)S(1)} %get-tuple-element.55), channel_id=1, source_target_pairs={{0,8},{4,12},{8,0},{12,4},{16,24},{20,28},{24,16},{28,20},{1,9},{5... | collective-permute-start | bytes 6152 | tf_op jit(solution)/shard_map/ppermute | solution.py:376

commit v16 on v15

--- a/solution.py
+++ b/solution.py
@@ -11,7 +11,6 @@
 ITERS = 2
 LANES = 128
 SUB = 16
-STAGE = 512
 SMALLEST = 1e-16
 LARGEST = 1e12
 NT_DIMS = (((1,), (1,)), ((), ()))
@@ -73,33 +72,35 @@
     return pl.ds((lax.axis_index("col") ^ (i // per)) * per + i % per, 1)
 
 
-def add_shifts(a_ref, t_ref, potential, aug_ref, top_ref):
-    rows = a_ref.shape[0]
-    steps = rows // LANES
-    lane = lax.broadcasted_iota(jnp.int32, (LANES, LANES), 1)
-    s = lax.dot_general(a_ref[...], t_ref[: potential.shape[1], :LANES], NT_DIMS, preferred_element_type=jnp.float32)
-    aug_ref[:, :LANES] = a_ref[...]
+def add_shifts(a_ref, t_ref, potential, shift_ref, top_ref):
+    steps = a_ref.shape[0] // LANES
+    t = t_ref[: potential.shape[1], :LANES]
+    s = lax.dot_general(a_ref[...], t, NT_DIMS, preferred_element_type=jnp.float32)
     top = jnp.max(lane_fold(jnp.maximum, s + potential), axis=1, keepdims=True)
     for i in range(steps):
         at = slice(i * LANES, (i + 1) * LANES)
-        shift = top[at, :].astype(jnp.bfloat16).astype(jnp.float32)
-        aug_ref[at, LANES:] = jnp.where(lane == 0, 1.0, jnp.where(lane == 1, -shift, 0.0)).astype(jnp.bfloat16)
-        top_ref[row_of(i, steps), :] = as_lanes(shift)
-
-
-def exponentials(aug_ref, t_ref, e_ref, width, mass_ref=None):
-    for at in range(0, t_ref.shape[0], width):
-        t = t_ref[at : at + width, :]
-        e = jnp.exp(lax.dot_general(aug_ref[...], t, NT_DIMS, preferred_element_type=jnp.float32))
-        if mass_ref is not None:
-            m = lane_fold(jnp.add, e)
-            mass_ref[...] = m if at == 0 else mass_ref[...] + m
-        e_ref[:, at : at + width] = e.astype(jnp.bfloat16)
-
-
-def shifted_rows(aug_ref, t_ref, lse_ref, top_ref, mass_ref, e_ref):
-    exponentials(aug_ref, t_ref, e_ref, STAGE, mass_ref)
-    steps = aug_ref.shape[0] // LANES
+        shift_ref[at, :] = jnp.broadcast_to(top[at, :], (LANES, LANES))
+        top_ref[row_of(i, steps), :] = as_lanes(top[at, :])
+
+
+def exponentials(a_ref, t_ref, pot_ref, shift_ref, e_ref, mass_ref=None):
+    width = pot_ref.shape[1]
+    for g in range(pot_ref.shape[0]):
+        cols = slice(g * width, (g + 1) * width)
+        for h in range(0, a_ref.shape[0], 2 * LANES):
+            at = slice(h, h + 2 * LANES)
+            s = lax.dot_general(a_ref[at, :], t_ref[cols, :LANES], NT_DIMS, preferred_element_type=jnp.float32)
+            shift = jnp.concatenate([shift_ref[at, :]] * (width // LANES), axis=1)
+            e = jnp.exp(s + pot_ref[g : g + 1, :] - shift)
+            if mass_ref is not None:
+                m = lane_fold(jnp.add, e)
+                mass_ref[at, :] = m if g == 0 else mass_ref[at, :] + m
+            e_ref[at, cols] = e.astype(jnp.bfloat16)
+
+
+def shifted_rows(a_ref, t_ref, pot_ref, shift_ref, lse_ref, top_ref, mass_ref, e_ref):
+    exponentials(a_ref, t_ref, pot_ref, shift_ref, e_ref, mass_ref)
+    steps = a_ref.shape[0] // LANES
     masses = []
     for i in range(steps):
         at = slice(i * LANES, (i + 1) * LANES)
@@ -109,16 +110,16 @@
     return within(masses)
 
 
-def shifted_couple(aug_ref, t_ref, lse_ref, top_ref, e_ref, carried_ref):
-    exponentials(aug_ref, t_ref, e_ref, STAGE)
-    rows = aug_ref.shape[0]
+def shifted_couple(a_ref, t_ref, pot_ref, shift_ref, lse_ref, top_ref, e_ref, carried_ref):
+    exponentials(a_ref, t_ref, pot_ref, shift_ref, e_ref)
+    rows = a_ref.shape[0]
     steps = rows // LANES
     masses = []
     for h in range(0, rows, 4 * LANES):
         d = jnp.dot(e_ref[h : h + 4 * LANES, :], t_ref[...], preferred_element_type=jnp.float32)
         for i in range(h // LANES, h // LANES + 4):
             at = slice(i * LANES - h, (i + 1) * LANES - h)
-            mass = d[at, LANES + 1 : LANES + 2]
+            mass = d[at, LANES : LANES + 1]
             carried_ref[i * LANES : (i + 1) * LANES, :] = d[at, :LANES] / mass
             masses.append(as_lanes(mass))
             row = row_of(i, steps)
@@ -177,23 +178,21 @@
     return jnp.concatenate([tail[j : j + 1, :] for j in range(width // LANES)], axis=1)
 
 
-def shift_kernel(width, a_ref, block_ref, aug_ref, top_ref):
-    add_shifts(a_ref, block_ref, potential_of(block_ref, width), aug_ref, top_ref)
+def shift_kernel(width, a_ref, block_ref, shift_ref, top_ref):
+    add_shifts(a_ref, block_ref, potential_of(block_ref, width), shift_ref, top_ref)
 
 
 def couple_kernel(nt, width, *refs):
-    a_ref, aug_ref, top_ref, t_refs = refs[0], refs[1], refs[2], refs[3 : 3 + nt]
+    a_ref, shift_ref, top_ref, t_refs = refs[0], refs[1], refs[2], refs[3 : 3 + nt]
     lse_ref, carried_ref, t_ref, pot_ref, e_ref, scores = refs[3 + nt :]
-    lane = lax.broadcasted_iota(jnp.int32, (LANES, LANES), 1)
+    lane = lax.broadcasted_iota(jnp.int32, (width, LANES), 1)
+    one = jnp.where(lane == 0, 1.0, 0.0).astype(jnp.bfloat16)
     for g in range(nt):
-        t_ref[g * width : (g + 1) * width, :LANES] = t_refs[g][:width, :]
+        at = slice(g * width, (g + 1) * width)
+        t_ref[at, :LANES] = t_refs[g][:width, :]
+        t_ref[at, LANES:] = one
         pot_ref[g : g + 1, :] = potential_of(t_refs[g], width)
-        for j in range(0, width, LANES):
-            potential = as_rows(pot_ref[g : g + 1, j : j + LANES])
-            added = jnp.where(lane == 0, potential, jnp.where(lane == 1, 1.0, 0.0))
-            at = g * width + j
-            t_ref[at : at + LANES, LANES:] = added.astype(jnp.bfloat16)
-    fine = shifted_couple(aug_ref, t_ref, lse_ref, top_ref, e_ref, carried_ref)
+    fine = shifted_couple(a_ref, t_ref, pot_ref, shift_ref, lse_ref, top_ref, e_ref, carried_ref)
 
     @pl.when(jnp.logical_not(fine))
     def _():
@@ -234,14 +233,14 @@
 
 def first_rows_kernel(*refs):
     s_ref, t_ref, pot_ref, m_refs = refs[0], refs[1], refs[2], refs[3:5]
-    moment_ref, a_ref, lse_ref, top_ref, e_ref, mass_ref, aug_ref, scores = refs[5:]
+    moment_ref, a_ref, lse_ref, top_ref, e_ref, mass_ref, shift_ref, scores = refs[5:]
     r = lax.axis_index("row")
     half = m_refs[0].shape[0]
     for k in range(2):
         moment_ref[pl.ds(pl.multiple_of((k ^ (r % 2)) * half, half), half), :] = m_refs[k][...]
     a_ref[...] = project4(s_ref[...], split3(moment_ref[...]))
-    add_shifts(a_ref, t_ref, pot_ref[0:1, :], aug_ref, top_ref)
-    fine = shifted_rows(aug_ref, t_ref, lse_ref, top_ref, mass_ref, e_ref)
+    add_shifts(a_ref, t_ref, pot_ref[0:1, :], shift_ref, top_ref)
+    fine = shifted_rows(a_ref, t_ref, pot_ref, shift_ref, lse_ref, top_ref, mass_ref, e_ref)
 
     @pl.when(jnp.logical_not(fine))
     def _():
@@ -416,14 +415,13 @@
     )
     far = [lax.optimization_barrier((x, a))[0] for x in far]
     blocks = [x for pair in zip(far, [swap(x, "row", 1) for x in far]) for x in pair]
-    augmented = shape((rows, 2 * depth), bf16)
-    aug, top = call(
-        functools.partial(shift_kernel, width), [augmented, tile], [a, far[0]], flops=2 * rows * width * depth
+    shift, top = call(
+        functools.partial(shift_kernel, width), [shape((rows, LANES), f32), tile], [a, far[0]], flops=2 * rows * width * depth
     )
     lse, carried, t, pot = call(
         functools.partial(couple_kernel, nt, width),
         [tile, shape((rows, depth), f32), shape((cols, 2 * depth), bf16), shape((nt, width), f32)],
-        [a, aug, top] + blocks,
+        [a, shift, top] + blocks,
         [pltpu.VMEM((rows, cols), bf16), row_scores],
         2 * flops,
         exps,
@@ -443,7 +441,7 @@
         first_rows_kernel,
         [shape((depth, depth), f32), projected, tile, tile, shape((rows, cols), bf16)],
         [s, t, pot, part, swap(part, "row", 1)],
-        [sums, pltpu.VMEM(augmented.shape, bf16), row_scores],
+        [sums, sums, row_scores],
         flops,
         exps,
     )

time: 122 us -> 124 us (1.016)
  Pallas kernels: 53.2 us -> 54.7 us
    pallas_call x14, Pallas kernels: 53.2 us -> 54.7 us  [call(): pl.pallas_call(kernel, out_shape=list(out), in_specs=[vmem] * len(args),...]
where the time goes in v16:
time: 124 us
  Pallas kernels  54.7 us (44%)
  starting transfers between devices  38.4 us (31%)
  waiting for transfers between devices  27.2 us (22%)
  local copies, waits for them, and re-layouts  1.68 us (1%)
    pallas_call x14, Pallas kernels, call(): pl.pallas_call(kernel, out_shape=list(out), in_specs=[vmem] * len(args),...  54.7 us
    ppermute x35, starting transfers between devices, swap(): lax.ppermute(x, axis, [(i, i ^ k) for i in range(lax.axis_size(axis))])  38.4 us
    ppermute x35, waiting for transfers between devices, swap(): lax.ppermute(x, axis, [(i, i ^ k) for i in range(lax.axis_size(axis))])  27.2 us
  transfers between devices with their start and end apart: 35, of which 30 were waited for; matrix products, arithmetic and copies ran while one was open for 1% of the time, Pallas kernels for 1%

profile of v16, /device:TPU:0, one launch (start us, length us, event | category | flops | bytes accessed | tf_op | source)
XLA Modules:
  0.0 123.6 jit_solution(9500195151769909254)
XLA Ops:
  0.6 5.1 %collective-permute-start.1 = (bf16[256,128]{1,0:T(8,128)(2,1)}, bf16[256,128]{1,0:T(8,128)(2,1)S(1)}, u32[]{:S(2)}, u32[]{:S(2)}) collective-permute-start(bf16[256,128]{1,0:T(8,128)(2,1)} %refs_0_.1), channel_id=1, source_target_pairs={{0,3},{1,2},{2,1},{3,0},{4,7},{5,6},{6,5},{7,4},{8,11},{9,10},{10,... | collective-permute-start | bytes 196616 | tf_op jit(solution)/shard_map/ppermute | solution.py:375
  5.7 0.6 collective-permute-start.2
  6.4 0.9 fusion.1.block_ref.refs_3_
  7.3 2.7 %collective-permute-start.8 = (bf16[528,128]{1,0:T(8,128)(2,1)S(1)}, bf16[528,128]{1,0:T(8,128)(2,1)S(1)}, u32[]{:S(2)}, u32[]{:S(2)}) collective-permute-start(bf16[528,128]{1,0:T(8,128)(2,1)S(1)} %fusion.1.block_ref.refs_3_), channel_id=1, source_target_pairs={{0,24},{4,28},{8,16},{12,20},{16,8},{20,12},{24,0},{28,4},{1,25},{... | collective-permute-start | bytes 405512 | tf_op jit(solution)/shard_map/ppermute | solution.py:375
  10.0 0.5 collective-permute-start.6
  10.5 0.4 collective-permute-start.4
  10.9 0.7 collective-permute-done.refs_1_
  11.6 0.8 copy-done
  12.4 0.8 copy-done.1
  13.2 0.4 shard_map.67
  13.7 0.3 collective-permute-done.8.refs_9_
  14.0 1.9 %collective-permute-done.6.refs_7_ = bf16[528,128]{1,0:T(8,128)(2,1)S(1)} collective-permute-done((bf16[528,128]{1,0:T(8,128)(2,1)S(1)}, bf16[528,128]{1,0:T(8,128)(2,1)S(1)}, u32[]{:S(2)}, u32[]{:S(2)}) %collective-permute-start.6) | collective-permute-done | bytes 135200 | tf_op jit(solution)/shard_map/ppermute | solution.py:375
  16.0 0.5 collective-permute-start.7
  16.5 0.7 shard_map.68
  17.6 0.3 collective-permute-done.9.refs_10_
  17.9 16.0 %shard_map.69 = (f32[8,128]{1,0:T(8,128)S(1)}, f32[1024,128]{1,0:T(8,128)S(1)}, bf16[4096,256]{1,0:T(8,128)(2,1)S(1)}, f32[8,512]{1,0:T(8,128)S(1)}) custom-call(bf16[1024,128]{1,0:T(8,128)(2,1)S(1)} %get-tuple-element.31.a_ref.refs_0_, f32[1024,128]{1,0:T(8,128)S(1)} %get-tuple-element.33.refs_1_, f32[8,128]{1,0:T(8,128)S(1)} %get-tuple-element.34.refs_2_, ...), custom_call_target="tpu_custom_call" | custom-call | flops 2147483648 | bytes 4513792 | tf_op jit(solution)/shard_map/pallas_call | solution.py:363
  33.9 3.5 %collective-permute-start.12 = (f32[8,128]{1,0:T(8,128)S(1)}, f32[8,128]{1,0:T(8,128)S(1)}, u32[]{:S(2)}, u32[]{:S(2)}) collective-permute-start(f32[8,128]{1,0:T(8,128)S(1)} %get-tuple-element.40.refs_1_), channel_id=1, source_target_pairs={{0,3},{1,2},{2,1},{3,0},{4,7},{5,6},{6,5},{7,4},{8,11},{9,10},{10,... | collective-permute-start | bytes 12296 | tf_op jit(solution)/shard_map/ppermute | solution.py:375
  37.4 0.9 collective-permute-start.10
  38.3 1.0 collective-permute-done.12.refs_4_
  39.3 2.6 %collective-permute-done.11.refs_3_ = f32[8,128]{1,0:T(8,128)S(1)} collective-permute-done((f32[8,128]{1,0:T(8,128)S(1)}, f32[8,128]{1,0:T(8,128)S(1)}, u32[]{:S(2)}, u32[]{:S(2)}) %collective-permute-start.11) | collective-permute-done | bytes 4128 | tf_op jit(solution)/shard_map/ppermute | solution.py:375
  41.9 0.5 shard_map.70
  42.5 1.2 collective-permute-done.13.refs_1_
  43.7 1.5 %collective-permute-start.16 = (f32[64,128]{1,0:T(8,128)S(1)}, f32[64,128]{1,0:T(8,128)S(1)}, u32[]{:S(2)}, u32[]{:S(2)}) collective-permute-start(f32[64,128]{1,0:T(8,128)S(1)} %shard_map.71.refs_0_), channel_id=1, source_target_pairs={{0,3},{1,2},{2,1},{3,0},{4,7},{5,6},{6,5},{7,4},{8,11},{9,10},{10,... | collective-permute-start | bytes 98312 | tf_op jit(solution)/shard_map/ppermute | solution.py:375
  45.2 0.6 collective-permute-start.15
  45.8 2.3 %collective-permute-start.14 = (f32[64,128]{1,0:T(8,128)S(1)}, f32[64,128]{1,0:T(8,128)S(1)}, u32[]{:S(2)}, u32[]{:S(2)}) collective-permute-start(f32[64,128]{1,0:T(8,128)S(1)} %shard_map.71.refs_0_), channel_id=1, source_target_pairs={{0,1},{1,0},{2,3},{3,2},{4,5},{5,4},{6,7},{7,6},{8,9},{9,8},{10,11... | collective-permute-start | bytes 98312 | tf_op jit(solution)/shard_map/ppermute | solution.py:375
  48.1 1.6 %collective-permute-done.16.refs_3_ = f32[64,128]{1,0:T(8,128)S(1)} collective-permute-done((f32[64,128]{1,0:T(8,128)S(1)}, f32[64,128]{1,0:T(8,128)S(1)}, u32[]{:S(2)}, u32[]{:S(2)}) %collective-permute-start.16) | collective-permute-done | bytes 32800 | tf_op jit(solution)/shard_map/ppermute | solution.py:375
  49.7 0.4 collective-permute-done.15.refs_2_
  50.2 0.2 collective-permute-done.14.refs_1_
  50.4 1.8 %collective-permute-start.19 = (f32[64,128]{1,0:T(8,128)S(1)}, f32[64,128]{1,0:T(8,128)S(1)}, u32[]{:S(2)}, u32[]{:S(2)}) collective-permute-start(f32[64,128]{1,0:T(8,128)S(1)} %shard_map.72.refs_0_), channel_id=1, source_target_pairs={{0,24},{4,28},{8,16},{12,20},{16,8},{20,12},{24,0},{28,4},{1,25},{... | collective-permute-start | bytes 98312 | tf_op jit(solution)/shard_map/ppermute | solution.py:375
  52.2 1.3 %collective-permute-start.18 = (f32[64,128]{1,0:T(8,128)S(1)}, f32[64,128]{1,0:T(8,128)S(1)}, u32[]{:S(2)}, u32[]{:S(2)}) collective-permute-start(f32[64,128]{1,0:T(8,128)S(1)} %shard_map.72.refs_0_), channel_id=1, source_target_pairs={{0,16},{4,20},{8,24},{12,28},{16,0},{20,4},{24,8},{28,12},{1,17},{... | collective-permute-start | bytes 98312 | tf_op jit(solution)/shard_map/ppermute | solution.py:375
  53.5 0.5 collective-permute-start.17
  54.0 1.6 %collective-permute-done.19.refs_3_ = f32[64,128]{1,0:T(8,128)S(1)} collective-permute-done((f32[64,128]{1,0:T(8,128)S(1)}, f32[64,128]{1,0:T(8,128)S(1)}, u32[]{:S(2)}, u32[]{:S(2)}) %collective-permute-start.19) | collective-permute-done | bytes 32800 | tf_op jit(solution)/shard_map/ppermute | solution.py:375
  55.6 0.5 collective-permute-done.18.refs_2_
  56.1 1.3 %collective-permute-done.17.refs_1_ = f32[64,128]{1,0:T(8,128)S(1)} collective-permute-done((f32[64,128]{1,0:T(8,128)S(1)}, f32[64,128]{1,0:T(8,128)S(1)}, u32[]{:S(2)}, u32[]{:S(2)}) %collective-permute-start.17) | collective-permute-done | bytes 32800 | tf_op jit(solution)/shard_map/ppermute | solution.py:375
  57.5 1.2 collective-permute-done.20.refs_4_
  58.7 13.2 %shard_map.74 = (f32[128,128]{1,0:T(8,128)}, bf16[1024,128]{1,0:T(8,128)(2,1)S(1)}, f32[8,128]{1,0:T(8,128)S(1)}, f32[8,128]{1,0:T(8,128)S(1)}, bf16[1024,4096]{1,0:T(8,128)(2,1)S(1)}) custom-call(bf16[1024,128]{1,0:T(8,128)(2,1)S(1)} %get-tuple-element.30.refs_0_, bf16[4096,256]{1,0:T(8,128)(2,1)S(1)} %get-tuple-element.38.refs_1_.refs_3_, ...), custom_call_target="tpu_custom_call" | custom-call | flops 1073741824 | bytes 11165696 | tf_op jit(solution)/shard_map/pallas_call | solution.py:363
  71.8 2.3 %collective-permute-start.23 = (f32[8,128]{1,0:T(8,128)S(1)}, f32[8,128]{1,0:T(8,128)S(1)}, u32[]{:S(2)}, u32[]{:S(2)}) collective-permute-start(f32[8,128]{1,0:T(8,128)S(1)} %get-tuple-element.48.refs_5_), channel_id=1, source_target_pairs={{0,3},{1,2},{2,1},{3,0},{4,7},{5,6},{6,5},{7,4},{8,11},{9,10},{10,... | collective-permute-start | bytes 12296 | tf_op jit(solution)/shard_map/ppermute | solution.py:375
  74.2 0.8 collective-permute-start.22
  74.9 1.3 %collective-permute-start.21 = (f32[8,128]{1,0:T(8,128)S(1)}, f32[8,128]{1,0:T(8,128)S(1)}, u32[]{:S(2)}, u32[]{:S(2)}) collective-permute-start(f32[8,128]{1,0:T(8,128)S(1)} %get-tuple-element.48.refs_5_), channel_id=1, source_target_pairs={{0,1},{1,0},{2,3},{3,2},{4,5},{5,4},{6,7},{7,6},{8,9},{9,8},{10,11... | collective-permute-start | bytes 12296 | tf_op jit(solution)/shard_map/ppermute | solution.py:375
  76.2 1.0 collective-permute-done.23.refs_8_
  77.3 1.4 %collective-permute-done.22.refs_7_ = f32[8,128]{1,0:T(8,128)S(1)} collective-permute-done((f32[8,128]{1,0:T(8,128)S(1)}, f32[8,128]{1,0:T(8,128)S(1)}, u32[]{:S(2)}, u32[]{:S(2)}) %collective-permute-start.22) | collective-permute-done | bytes 4128 | tf_op jit(solution)/shard_map/ppermute | solution.py:375
  78.7 7.0 %shard_map.75 = (f32[8,512]{1,0:T(8,128)S(1)}, f32[8,128]{1,0:T(8,128)}) custom-call(bf16[1024,128]{1,0:T(8,128)(2,1)S(1)} %get-tuple-element.45.refs_0_, bf16[1024,4096]{1,0:T(8,128)(2,1)S(1)} %get-tuple-element.46.refs_1_, f32[8,128]{1,0:T(8,128)S(1)} %get-tuple-element.47.refs_2_, bf16[4096,256]{1,0:T(8,128)(2,1)S(1)} %get-tuple-element.38.refs_1_.refs_3_, ...), custom_call_target="tpu_custom_call" | custom-call | flops 67108864 | bytes 10805248 | tf_op jit(solution)/shard_map/pallas_call | solution.py:363
  85.6 1.2 collective-permute-done.24.refs_1_
  86.8 1.5 %collective-permute-start.27 = (f32[8,512]{1,0:T(8,128)S(1)}, f32[8,512]{1,0:T(8,128)S(1)}, u32[]{:S(2)}, u32[]{:S(2)}) collective-permute-start(f32[8,512]{1,0:T(8,128)S(1)} %shard_map.76.refs_5_), channel_id=1, source_target_pairs={{0,24},{4,28},{8,16},{12,20},{16,8},{20,12},{24,0},{28,4},{1,25},{... | collective-permute-start | bytes 49160 | tf_op jit(solution)/shard_map/ppermute | solution.py:375
  88.3 0.6 collective-permute-start.26
  88.9 1.5 %collective-permute-start.25 = (f32[8,512]{1,0:T(8,128)S(1)}, f32[8,512]{1,0:T(8,128)S(1)}, u32[]{:S(2)}, u32[]{:S(2)}) collective-permute-start(f32[8,512]{1,0:T(8,128)S(1)} %shard_map.76.refs_5_), channel_id=1, source_target_pairs={{0,8},{4,12},{8,0},{12,4},{16,24},{20,28},{24,16},{28,20},{1,9},{5... | collective-permute-start | bytes 49160 | tf_op jit(solution)/shard_map/ppermute | solution.py:375
  90.4 1.1 collective-permute-done.27.refs_8_
  91.5 0.5 collective-permute-done.26.refs_7_
  92.0 0.6 collective-permute-done.25.refs_6_
  92.6 9.5 %shard_map.77.refs_5_ = f32[8,128]{1,0:T(8,128)S(1)} custom-call(bf16[1024,128]{1,0:T(8,128)(2,1)S(1)} %get-tuple-element.45.refs_0_, bf16[1024,4096]{1,0:T(8,128)(2,1)S(1)} %get-tuple-element.46.refs_1_, f32[8,128]{1,0:T(8,128)S(1)} %get-tuple-element.47.refs_2_, bf16[4096,256]{1,0:T(8,128)(2,1)S(1)} %get-tuple-element.38.refs_1_.refs_3_, ...), custom_call_target="tpu_custom_call" | custom-call | flops 67108864 | bytes 10838016 | tf_op jit(solution)/shard_map/pallas_call | solution.py:363
  102.1 1.6 %collective-permute-start.30 = (f32[8,128]{1,0:T(8,128)S(1)}, f32[8,128]{1,0:T(8,128)S(1)}, u32[]{:S(2)}, u32[]{:S(2)}) collective-permute-start(f32[8,128]{1,0:T(8,128)S(1)} %shard_map.77.refs_5_), channel_id=1, source_target_pairs={{0,3},{1,2},{2,1},{3,0},{4,7},{5,6},{6,5},{7,4},{8,11},{9,10},{10,... | collective-permute-start | bytes 12296 | tf_op jit(solution)/shard_map/ppermute | solution.py:375
  103.7 1.1 collective-permute-start.29
  104.8 1.7 %collective-permute-start.28 = (f32[8,128]{1,0:T(8,128)S(1)}, f32[8,128]{1,0:T(8,128)S(1)}, u32[]{:S(2)}, u32[]{:S(2)}) collective-permute-start(f32[8,128]{1,0:T(8,128)S(1)} %shard_map.77.refs_5_), channel_id=1, source_target_pairs={{0,1},{1,0},{2,3},{3,2},{4,5},{5,4},{6,7},{7,6},{8,9},{9,8},{10,11... | collective-permute-start | bytes 12296 | tf_op jit(solution)/shard_map/ppermute | solution.py:375
  106.5 1.0 collective-permute-done.30.refs_8_
  107.6 0.6 collective-permute-done.29.refs_7_
  108.4 6.7 %shard_map.78 = (f32[4,1,512]{2,1,0:T(1,128)S(1)}, f32[4,1,512]{2,1,0:T(1,128)S(1)}, f32[8,128]{1,0:T(8,128)}) custom-call(bf16[1024,128]{1,0:T(8,128)(2,1)S(1)} %get-tuple-element.45.refs_0_, bf16[1024,4096]{1,0:T(8,128)(2,1)S(1)} %get-tuple-element.46.refs_1_, f32[8,128]{1,0:T(8,128)S(1)} %get-tuple-element.47.refs_2_, ...), custom_call_target="tpu_custom_call" | custom-call | flops 67108864 | bytes 10805248 | tf_op jit(solution)/shard_map/pallas_call | solution.py:363
  115.2 1.2 collective-permute-done.31.y_ref
  116.3 1.8 %collective-permute-start.32 = (f32[1,512]{1,0:T(1,128)S(1)}, f32[1,512]{1,0:T(1,128)S(1)}, u32[]{:S(2)}, u32[]{:S(2)}) collective-permute-start(f32[1,512]{1,0:T(1,128)S(1)} %get-tuple-element.53), channel_id=1, source_target_pairs={{0,24},{4,28},{8,16},{12,20},{16,8},{20,12},{24,0},{28,4},{1,25},{... | collective-permute-start | bytes 6152 | tf_op jit(solution)/shard_map/ppermute | solution.py:375
  118.1 1.3 %collective-permute-start.33 = (f32[1,512]{1,0:T(1,128)S(1)}, f32[1,512]{1,0:T(1,128)S(1)}, u32[]{:S(2)}, u32[]{:S(2)}) collective-permute-start(f32[1,512]{1,0:T(1,128)S(1)} %get-tuple-element.54), channel_id=1, source_target_pairs={{0,16},{4,20},{8,24},{12,28},{16,0},{20,4},{24,8},{28,12},{1,17},{... | collective-permute-start | bytes 6152 | tf_op jit(solution)/shard_map/ppermute | solution.py:375
  119.4 0.5 collective-permute-start.34
  119.9 1.0 collective-permute-done.32.refs_0_
  120.9 0.8 collective-permute-done.33.refs_1_
  121.7 1.3 %collective-permute-done.34.refs_2_ = f32[1,512]{1,0:T(1,128)S(1)} collective-permute-done((f32[1,512]{1,0:T(1,128)S(1)}, f32[1,512]{1,0:T(1,128)S(1)}, u32[]{:S(2)}, u32[]{:S(2)}) %collective-permute-start.34) | collective-permute-done | bytes 2080 | tf_op jit(solution)/shard_map/ppermute | solution.py:375
  123.0 0.6 shard_map.80
  (25 shorter events, 0.9 us)
Async XLA Ops:
  0.6 9.9 %collective-permute-start.1 = (bf16[256,128]{1,0:T(8,128)(2,1)}, bf16[256,128]{1,0:T(8,128)(2,1)S(1)}, u32[]{:S(2)}, u32[]{:S(2)}) collective-permute-start(bf16[256,128]{1,0:T(8,128)(2,1)} %refs_0_.1), channel_id=1, source_target_pairs={{0,3},{1,2},{2,1},{3,0},{4,7},{5,6},{6,5},{7,4},{8,11},{9,10},{10,... | collective-permute-start | bytes 196616 | tf_op jit(solution)/shard_map/ppermute | solution.py:375
  5.7 5.8 %collective-permute-start = (bf16[256,128]{1,0:T(8,128)(2,1)}, bf16[256,128]{1,0:T(8,128)(2,1)S(1)}, u32[]{:S(2)}, u32[]{:S(2)}) collective-permute-start(bf16[256,128]{1,0:T(8,128)(2,1)} %refs_0_.1), channel_id=1, source_target_pairs={{0,2},{1,3},{2,0},{3,1},{4,6},{5,7},{6,4},{7,5},{8,10},{9,11},{10,... | collective-permute-start | bytes 196616 | tf_op jit(solution)/shard_map/ppermute | solution.py:375
  5.7 5.8 %collective-permute-start.2 = (bf16[256,128]{1,0:T(8,128)(2,1)}, bf16[256,128]{1,0:T(8,128)(2,1)S(1)}, u32[]{:S(2)}, u32[]{:S(2)}) collective-permute-start(bf16[256,128]{1,0:T(8,128)(2,1)} %refs_0_.1), channel_id=1, source_target_pairs={{0,1},{1,0},{2,3},{3,2},{4,5},{5,4},{6,7},{7,6},{8,9},{9,8},{10,11... | collective-permute-start | bytes 196616 | tf_op jit(solution)/shard_map/ppermute | solution.py:375
  7.3 6.7 %collective-permute-start.8 = (bf16[528,128]{1,0:T(8,128)(2,1)S(1)}, bf16[528,128]{1,0:T(8,128)(2,1)S(1)}, u32[]{:S(2)}, u32[]{:S(2)}) collective-permute-start(bf16[528,128]{1,0:T(8,128)(2,1)S(1)} %fusion.1.block_ref.refs_3_), channel_id=1, source_target_pairs={{0,24},{4,28},{8,16},{12,20},{16,8},{20,12},{24,0},{28,4},{1,25},{... | collective-permute-start | bytes 405512 | tf_op jit(solution)/shard_map/ppermute | solution.py:375
  10.0 6.0 %collective-permute-start.6 = (bf16[528,128]{1,0:T(8,128)(2,1)S(1)}, bf16[528,128]{1,0:T(8,128)(2,1)S(1)}, u32[]{:S(2)}, u32[]{:S(2)}) collective-permute-start(bf16[528,128]{1,0:T(8,128)(2,1)S(1)} %fusion.1.block_ref.refs_3_), channel_id=1, source_target_pairs={{0,16},{4,20},{8,24},{12,28},{16,0},{20,4},{24,8},{28,12},{1,17},{... | collective-permute-start | bytes 405512 | tf_op jit(solution)/shard_map/ppermute | solution.py:375
  10.5 5.5 %collective-permute-start.4 = (bf16[528,128]{1,0:T(8,128)(2,1)S(1)}, bf16[528,128]{1,0:T(8,128)(2,1)S(1)}, u32[]{:S(2)}, u32[]{:S(2)}) collective-permute-start(bf16[528,128]{1,0:T(8,128)(2,1)S(1)} %fusion.1.block_ref.refs_3_), channel_id=1, source_target_pairs={{0,8},{4,12},{8,0},{12,4},{16,24},{20,28},{24,16},{28,20},{1,9},{5... | collective-permute-start | bytes 405512 | tf_op jit(solution)/shard_map/ppermute | solution.py:375
  11.6 0.8 copy-start
  12.4 0.8 copy-start.1
  13.6 3.6 %collective-permute-start.3 = (bf16[528,128]{1,0:T(8,128)(2,1)S(1)}, bf16[528,128]{1,0:T(8,128)(2,1)S(1)}, u32[]{:S(2)}, u32[]{:S(2)}) collective-permute-start(bf16[528,128]{1,0:T(8,128)(2,1)S(1)} %fusion.1.block_ref.refs_3_), channel_id=1, source_target_pairs={{0,4},{4,0},{8,12},{12,8},{16,20},{20,16},{24,28},{28,24},{1,5},{5... | collective-permute-start | bytes 405512 | tf_op jit(solution)/shard_map/ppermute | solution.py:375
  16.0 1.4 %collective-permute-start.5 = (bf16[528,128]{1,0:T(8,128)(2,1)S(1)}, bf16[528,128]{1,0:T(8,128)(2,1)S(1)}, u32[]{:S(2)}, u32[]{:S(2)}) collective-permute-start(bf16[528,128]{1,0:T(8,128)(2,1)S(1)} %collective-permute-done.4.refs_5_), channel_id=1, source_target_pairs={{0,4},{4,0},{8,12},{12,8},{16,20},{20,16},{24,28},{28,24},{1,5},{5... | collective-permute-start | bytes 405512 | tf_op jit(solution)/shard_map/ppermute | solution.py:375
  16.0 1.5 %collective-permute-start.7 = (bf16[528,128]{1,0:T(8,128)(2,1)S(1)}, bf16[528,128]{1,0:T(8,128)(2,1)S(1)}, u32[]{:S(2)}, u32[]{:S(2)}) collective-permute-start(bf16[528,128]{1,0:T(8,128)(2,1)S(1)} %collective-permute-done.6.refs_7_), channel_id=1, source_target_pairs={{0,4},{4,0},{8,12},{12,8},{16,20},{20,16},{24,28},{28,24},{1,5},{5... | collective-permute-start | bytes 405512 | tf_op jit(solution)/shard_map/ppermute | solution.py:375
  16.5 1.4 %collective-permute-start.9 = (bf16[528,128]{1,0:T(8,128)(2,1)S(1)}, bf16[528,128]{1,0:T(8,128)(2,1)S(1)}, u32[]{:S(2)}, u32[]{:S(2)}) collective-permute-start(bf16[528,128]{1,0:T(8,128)(2,1)S(1)} %collective-permute-done.8.refs_9_), channel_id=1, source_target_pairs={{0,4},{4,0},{8,12},{12,8},{16,20},{20,16},{24,28},{28,24},{1,5},{5... | collective-permute-start | bytes 405512 | tf_op jit(solution)/shard_map/ppermute | solution.py:375
  33.9 5.5 %collective-permute-start.12 = (f32[8,128]{1,0:T(8,128)S(1)}, f32[8,128]{1,0:T(8,128)S(1)}, u32[]{:S(2)}, u32[]{:S(2)}) collective-permute-start(f32[8,128]{1,0:T(8,128)S(1)} %get-tuple-element.40.refs_1_), channel_id=1, source_target_pairs={{0,3},{1,2},{2,1},{3,0},{4,7},{5,6},{6,5},{7,4},{8,11},{9,10},{10,... | collective-permute-start | bytes 12296 | tf_op jit(solution)/shard_map/ppermute | solution.py:375
  37.4 4.5 %collective-permute-start.11 = (f32[8,128]{1,0:T(8,128)S(1)}, f32[8,128]{1,0:T(8,128)S(1)}, u32[]{:S(2)}, u32[]{:S(2)}) collective-permute-start(f32[8,128]{1,0:T(8,128)S(1)} %get-tuple-element.40.refs_1_), channel_id=1, source_target_pairs={{0,2},{1,3},{2,0},{3,1},{4,6},{5,7},{6,4},{7,5},{8,10},{9,11},{10,... | collective-permute-start | bytes 12296 | tf_op jit(solution)/shard_map/ppermute | solution.py:375
  37.4 4.5 %collective-permute-start.10 = (f32[8,128]{1,0:T(8,128)S(1)}, f32[8,128]{1,0:T(8,128)S(1)}, u32[]{:S(2)}, u32[]{:S(2)}) collective-permute-start(f32[8,128]{1,0:T(8,128)S(1)} %get-tuple-element.40.refs_1_), channel_id=1, source_target_pairs={{0,1},{1,0},{2,3},{3,2},{4,5},{5,4},{6,7},{7,6},{8,9},{9,8},{10,11... | collective-permute-start | bytes 12296 | tf_op jit(solution)/shard_map/ppermute | solution.py:375
  42.4 1.3 %collective-permute-start.13 = (f32[64,128]{1,0:T(8,128)S(1)}, f32[64,128]{1,0:T(8,128)S(1)}, u32[]{:S(2)}, u32[]{:S(2)}) collective-permute-start(f32[64,128]{1,0:T(8,128)S(1)} %get-tuple-element.43), channel_id=1, source_target_pairs={{0,4},{4,0},{8,12},{12,8},{16,20},{20,16},{24,28},{28,24},{1,5},{5... | collective-permute-start | bytes 98312 | tf_op jit(solution)/shard_map/ppermute | solution.py:375
  43.7 6.0 %collective-permute-start.16 = (f32[64,128]{1,0:T(8,128)S(1)}, f32[64,128]{1,0:T(8,128)S(1)}, u32[]{:S(2)}, u32[]{:S(2)}) collective-permute-start(f32[64,128]{1,0:T(8,128)S(1)} %shard_map.71.refs_0_), channel_id=1, source_target_pairs={{0,3},{1,2},{2,1},{3,0},{4,7},{5,6},{6,5},{7,4},{8,11},{9,10},{10,... | collective-permute-start | bytes 98312 | tf_op jit(solution)/shard_map/ppermute | solution.py:375
  45.2 5.0 %collective-permute-start.15 = (f32[64,128]{1,0:T(8,128)S(1)}, f32[64,128]{1,0:T(8,128)S(1)}, u32[]{:S(2)}, u32[]{:S(2)}) collective-permute-start(f32[64,128]{1,0:T(8,128)S(1)} %shard_map.71.refs_0_), channel_id=1, source_target_pairs={{0,2},{1,3},{2,0},{3,1},{4,6},{5,7},{6,4},{7,5},{8,10},{9,11},{10,... | collective-permute-start | bytes 98312 | tf_op jit(solution)/shard_map/ppermute | solution.py:375
  45.8 4.6 %collective-permute-start.14 = (f32[64,128]{1,0:T(8,128)S(1)}, f32[64,128]{1,0:T(8,128)S(1)}, u32[]{:S(2)}, u32[]{:S(2)}) collective-permute-start(f32[64,128]{1,0:T(8,128)S(1)} %shard_map.71.refs_0_), channel_id=1, source_target_pairs={{0,1},{1,0},{2,3},{3,2},{4,5},{5,4},{6,7},{7,6},{8,9},{9,8},{10,11... | collective-permute-start | bytes 98312 | tf_op jit(solution)/shard_map/ppermute | solution.py:375
  50.4 5.2 %collective-permute-start.19 = (f32[64,128]{1,0:T(8,128)S(1)}, f32[64,128]{1,0:T(8,128)S(1)}, u32[]{:S(2)}, u32[]{:S(2)}) collective-permute-start(f32[64,128]{1,0:T(8,128)S(1)} %shard_map.72.refs_0_), channel_id=1, source_target_pairs={{0,24},{4,28},{8,16},{12,20},{16,8},{20,12},{24,0},{28,4},{1,25},{... | collective-permute-start | bytes 98312 | tf_op jit(solution)/shard_map/ppermute | solution.py:375
  52.2 3.9 %collective-permute-start.18 = (f32[64,128]{1,0:T(8,128)S(1)}, f32[64,128]{1,0:T(8,128)S(1)}, u32[]{:S(2)}, u32[]{:S(2)}) collective-permute-start(f32[64,128]{1,0:T(8,128)S(1)} %shard_map.72.refs_0_), channel_id=1, source_target_pairs={{0,16},{4,20},{8,24},{12,28},{16,0},{20,4},{24,8},{28,12},{1,17},{... | collective-permute-start | bytes 98312 | tf_op jit(solution)/shard_map/ppermute | solution.py:375
  53.5 3.9 %collective-permute-start.17 = (f32[64,128]{1,0:T(8,128)S(1)}, f32[64,128]{1,0:T(8,128)S(1)}, u32[]{:S(2)}, u32[]{:S(2)}) collective-permute-start(f32[64,128]{1,0:T(8,128)S(1)} %shard_map.72.refs_0_), channel_id=1, source_target_pairs={{0,8},{4,12},{8,0},{12,4},{16,24},{20,28},{24,16},{28,20},{1,9},{5... | collective-permute-start | bytes 98312 | tf_op jit(solution)/shard_map/ppermute | solution.py:375
  57.4 1.3 %collective-permute-start.20 = (f32[64,128]{1,0:T(8,128)S(1)}, f32[64,128]{1,0:T(8,128)S(1)}, u32[]{:S(2)}, u32[]{:S(2)}) collective-permute-start(f32[64,128]{1,0:T(8,128)S(1)} %shard_map.73.refs_3_), channel_id=1, source_target_pairs={{0,4},{4,0},{8,12},{12,8},{16,20},{20,16},{24,28},{28,24},{1,5},{5... | collective-permute-start | bytes 98312 | tf_op jit(solution)/shard_map/ppermute | solution.py:375
  71.8 5.4 %collective-permute-start.23 = (f32[8,128]{1,0:T(8,128)S(1)}, f32[8,128]{1,0:T(8,128)S(1)}, u32[]{:S(2)}, u32[]{:S(2)}) collective-permute-start(f32[8,128]{1,0:T(8,128)S(1)} %get-tuple-element.48.refs_5_), channel_id=1, source_target_pairs={{0,3},{1,2},{2,1},{3,0},{4,7},{5,6},{6,5},{7,4},{8,11},{9,10},{10,... | collective-permute-start | bytes 12296 | tf_op jit(solution)/shard_map/ppermute | solution.py:375
  74.2 4.5 %collective-permute-start.22 = (f32[8,128]{1,0:T(8,128)S(1)}, f32[8,128]{1,0:T(8,128)S(1)}, u32[]{:S(2)}, u32[]{:S(2)}) collective-permute-start(f32[8,128]{1,0:T(8,128)S(1)} %get-tuple-element.48.refs_5_), channel_id=1, source_target_pairs={{0,2},{1,3},{2,0},{3,1},{4,6},{5,7},{6,4},{7,5},{8,10},{9,11},{10,... | collective-permute-start | bytes 12296 | tf_op jit(solution)/shard_map/ppermute | solution.py:375
  74.9 3.7 %collective-permute-start.21 = (f32[8,128]{1,0:T(8,128)S(1)}, f32[8,128]{1,0:T(8,128)S(1)}, u32[]{:S(2)}, u32[]{:S(2)}) collective-permute-start(f32[8,128]{1,0:T(8,128)S(1)} %get-tuple-element.48.refs_5_), channel_id=1, source_target_pairs={{0,1},{1,0},{2,3},{3,2},{4,5},{5,4},{6,7},{7,6},{8,9},{9,8},{10,11... | collective-permute-start | bytes 12296 | tf_op jit(solution)/shard_map/ppermute | solution.py:375
  85.6 1.2 collective-permute-start.24
  86.8 4.7 %collective-permute-start.27 = (f32[8,512]{1,0:T(8,128)S(1)}, f32[8,512]{1,0:T(8,128)S(1)}, u32[]{:S(2)}, u32[]{:S(2)}) collective-permute-start(f32[8,512]{1,0:T(8,128)S(1)} %shard_map.76.refs_5_), channel_id=1, source_target_pairs={{0,24},{4,28},{8,16},{12,20},{16,8},{20,12},{24,0},{28,4},{1,25},{... | collective-permute-start | bytes 49160 | tf_op jit(solution)/shard_map/ppermute | solution.py:375
  88.3 3.7 %collective-permute-start.26 = (f32[8,512]{1,0:T(8,128)S(1)}, f32[8,512]{1,0:T(8,128)S(1)}, u32[]{:S(2)}, u32[]{:S(2)}) collective-permute-start(f32[8,512]{1,0:T(8,128)S(1)} %shard_map.76.refs_5_), channel_id=1, source_target_pairs={{0,16},{4,20},{8,24},{12,28},{16,0},{20,4},{24,8},{28,12},{1,17},{... | collective-permute-start | bytes 49160 | tf_op jit(solution)/shard_map/ppermute | solution.py:375
  88.9 3.7 %collective-permute-start.25 = (f32[8,512]{1,0:T(8,128)S(1)}, f32[8,512]{1,0:T(8,128)S(1)}, u32[]{:S(2)}, u32[]{:S(2)}) collective-permute-start(f32[8,512]{1,0:T(8,128)S(1)} %shard_map.76.refs_5_), channel_id=1, source_target_pairs={{0,8},{4,12},{8,0},{12,4},{16,24},{20,28},{24,16},{28,20},{1,9},{5... | collective-permute-start | bytes 49160 | tf_op jit(solution)/shard_map/ppermute | solution.py:375
  102.1 5.4 %collective-permute-start.30 = (f32[8,128]{1,0:T(8,128)S(1)}, f32[8,128]{1,0:T(8,128)S(1)}, u32[]{:S(2)}, u32[]{:S(2)}) collective-permute-start(f32[8,128]{1,0:T(8,128)S(1)} %shard_map.77.refs_5_), channel_id=1, source_target_pairs={{0,3},{1,2},{2,1},{3,0},{4,7},{5,6},{6,5},{7,4},{8,11},{9,10},{10,... | collective-permute-start | bytes 12296 | tf_op jit(solution)/shard_map/ppermute | solution.py:375
  103.7 4.5 %collective-permute-start.29 = (f32[8,128]{1,0:T(8,128)S(1)}, f32[8,128]{1,0:T(8,128)S(1)}, u32[]{:S(2)}, u32[]{:S(2)}) collective-permute-start(f32[8,128]{1,0:T(8,128)S(1)} %shard_map.77.refs_5_), channel_id=1, source_target_pairs={{0,2},{1,3},{2,0},{3,1},{4,6},{5,7},{6,4},{7,5},{8,10},{9,11},{10,... | collective-permute-start | bytes 12296 | tf_op jit(solution)/shard_map/ppermute | solution.py:375
  104.8 3.6 %collective-permute-start.28 = (f32[8,128]{1,0:T(8,128)S(1)}, f32[8,128]{1,0:T(8,128)S(1)}, u32[]{:S(2)}, u32[]{:S(2)}) collective-permute-start(f32[8,128]{1,0:T(8,128)S(1)} %shard_map.77.refs_5_), channel_id=1, source_target_pairs={{0,1},{1,0},{2,3},{3,2},{4,5},{5,4},{6,7},{7,6},{8,9},{9,8},{10,11... | collective-permute-start | bytes 12296 | tf_op jit(solution)/shard_map/ppermute | solution.py:375
  115.2 1.2 collective-permute-start.31
  116.3 4.5 %collective-permute-start.32 = (f32[1,512]{1,0:T(1,128)S(1)}, f32[1,512]{1,0:T(1,128)S(1)}, u32[]{:S(2)}, u32[]{:S(2)}) collective-permute-start(f32[1,512]{1,0:T(1,128)S(1)} %get-tuple-element.53), channel_id=1, source_target_pairs={{0,24},{4,28},{8,16},{12,20},{16,8},{20,12},{24,0},{28,4},{1,25},{... | collective-permute-start | bytes 6152 | tf_op jit(solution)/shard_map/ppermute | solution.py:375
  118.1 3.6 %collective-permute-start.33 = (f32[1,512]{1,0:T(1,128)S(1)}, f32[1,512]{1,0:T(1,128)S(1)}, u32[]{:S(2)}, u32[]{:S(2)}) collective-permute-start(f32[1,512]{1,0:T(1,128)S(1)} %get-tuple-element.54), channel_id=1, source_target_pairs={{0,16},{4,20},{8,24},{12,28},{16,0},{20,4},{24,8},{28,12},{1,17},{... | collective-permute-start | bytes 6152 | tf_op jit(solution)/shard_map/ppermute | solution.py:375
  119.4 3.6 %collective-permute-start.34 = (f32[1,512]{1,0:T(1,128)S(1)}, f32[1,512]{1,0:T(1,128)S(1)}, u32[]{:S(2)}, u32[]{:S(2)}) collective-permute-start(f32[1,512]{1,0:T(1,128)S(1)} %get-tuple-element.55), channel_id=1, source_target_pairs={{0,8},{4,12},{8,0},{12,4},{16,24},{20,28},{24,16},{28,20},{1,9},{5... | collective-permute-start | bytes 6152 | tf_op jit(solution)/shard_map/ppermute | solution.py:375
